TPU v7x, 32 devices: a whole 2x2x4 slice. The times are simulated.
32 devices in a mesh: grp: 2 (over x), row: 8 (over z, y), node: 2 (over core).
Axes of the slice: x: 2, y: 2, z: 4, core: 2. Of those that a mesh axis runs over, the one named last changes fastest.
Arguments:
- pair_rep: bfloat16 [384, 192, 128], P(('grp', 'row', 'node')), parts along dimension 0, may hold values from -6 to 6
- length: int32 [2], P('grp'), parts along dimension 0, may hold values from 96 to 192
- ln_pair: float32 [128], replicated, may hold values from 0.1 to 1.9
- tri_in: bfloat16 [4, 128, 128], replicated, may hold values from -0.5 to 0.5
- tri_gate: bfloat16 [128, 128], replicated, may hold values from -0.5 to 0.5
- ln_hidden: float32 [128], replicated, may hold values from 0.1 to 1.9
- tri_out: bfloat16 [128, 128], replicated, may hold values from -0.5 to 0.5
- ln_att: float32 [128], replicated, may hold values from 0.1 to 1.9
- att_q: bfloat16 [128, 128], replicated, may hold values from -3 to 3
- att_k: bfloat16 [128, 128], replicated, may hold values from -3 to 3
- att_v: bfloat16 [128, 128], replicated, may hold values from -0.5 to 0.5
- att_bias: bfloat16 [128, 4], replicated, may hold values from -0.5 to 0.5
- att_gate: bfloat16 [128, 128], replicated, may hold values from -0.5 to 0.5
- att_out: bfloat16 [128, 128], replicated, may hold values from -0.5 to 0.5
Outputs:
- attended: bfloat16 [384, 192, 128], P('grp', ('row', 'node')), parts along dimension 0
There are 2 independent parts, one for each index of `grp`. A program takes and returns all parts, laid end to end along the dimension named above; an argument that names none is the same for every part. Nothing has to cross between parts.
All inputs are finite; a program needn't handle non-finite values.
Results may differ from a plain program's by a relative error of at most 0.0081.
Values may be sent and summed in bfloat16 or wider, within the bound.
No kernel may reach another device: no remote copies, remote signals or barrier semaphores. Data moves between devices by JAX's collectives and lax.ppermute only.
A program may use at most 128 MiB of HBM per device.

v0:
```python
import jax
import jax.numpy as jnp
from jax import lax
from jax.sharding import PartitionSpec as P

eps = 1e-05


def layer_norm(values, gain_vec, reduce_axis):
    average = jnp.mean(values, axis=reduce_axis, keepdims=True)
    centred = values - average
    variance = jnp.mean(centred * centred, axis=reduce_axis, keepdims=True)
    return centred * lax.rsqrt(variance + eps) * gain_vec


def shards(
    pair_rep,
    length,
    ln_pair,
    tri_in,
    tri_gate,
    ln_hidden,
    tri_out,
    ln_att,
    att_q,
    att_k,
    att_v,
    att_bias,
    att_gate,
    att_out,
):
    f32 = jnp.float32
    bf16 = jnp.bfloat16
    rows_here = pair_rep.shape[0]
    crop_len = pair_rep.shape[1]
    first_row = lax.axis_index(("row", "node")) * rows_here
    key_live = jnp.arange(crop_len, dtype=jnp.int32) < length[0]
    row_live = first_row + jnp.arange(rows_here, dtype=jnp.int32) < length[0]
    pair_mask = (row_live[:, None] & key_live[None, :]).astype(f32)
    normed = layer_norm(pair_rep.astype(f32), ln_pair, 2).astype(bf16)
    projected = jnp.einsum("rnc,pce->pern", normed, tri_in, preferred_element_type=f32)
    left_edge = (jax.nn.sigmoid(projected[0]) * projected[1] * pair_mask).astype(bf16)
    right_edge = (jax.nn.sigmoid(projected[2]) * projected[3] * pair_mask).astype(bf16)
    gating = jax.nn.sigmoid(jnp.einsum("rnc,cd->rnd", normed, tri_gate, preferred_element_type=f32))
    outer_sum = jnp.einsum(
        "erk,ejk->erj",
        left_edge,
        lax.all_gather(right_edge, ("row", "node"), axis=1, tiled=True),
        preferred_element_type=f32,
    )
    hidden_norm = layer_norm(outer_sum, ln_hidden[:, None, None], 0).astype(bf16)
    update = jnp.einsum("ern,ed->rnd", hidden_norm, tri_out, preferred_element_type=f32)
    first_out = (pair_rep.astype(f32) + gating * update).astype(bf16)
    columns = lax.all_to_all(first_out, ("row", "node"), split_axis=1, concat_axis=0, tiled=True)
    col_norm = layer_norm(columns.astype(f32), ln_att, 2).astype(bf16)
    joined_w = jnp.concatenate([att_q, att_k, att_v, att_gate], axis=1)
    joined_proj = jnp.einsum("ijc,ce->ije", col_norm, joined_w, preferred_element_type=f32)
    proj_width = att_q.shape[1]
    head_count = att_bias.shape[1]
    head_dim = proj_width // head_count
    query_proj = joined_proj[..., :proj_width].astype(bf16)
    key_proj = joined_proj[..., proj_width : 2 * proj_width].astype(bf16)
    value_proj = joined_proj[..., 2 * proj_width : 3 * proj_width].astype(bf16)
    att_gating = jax.nn.sigmoid(joined_proj[..., 3 * proj_width :])
    bias_local = jnp.einsum("kic,ch->hki", col_norm, att_bias, preferred_element_type=f32).astype(
        bf16
    )
    full_bias = lax.all_gather(bias_local, ("row", "node"), axis=2, tiled=True).astype(f32)
    score_scale = head_dim ** (-0.5)

    def one_column(column):
        query_col = lax.dynamic_index_in_dim(query_proj, column, 1, keepdims=False).reshape(
            crop_len, head_count, head_dim
        )
        key_col = lax.dynamic_index_in_dim(key_proj, column, 1, keepdims=False).reshape(
            crop_len, head_count, head_dim
        )
        value_col = lax.dynamic_index_in_dim(value_proj, column, 1, keepdims=False).reshape(
            crop_len, head_count, head_dim
        )
        scores = (
            jnp.einsum("khd,ihd->hki", key_col, query_col, preferred_element_type=f32) * score_scale
            + full_bias
        )
        scores = jnp.where(key_live[None, :, None], scores, -1000000000.0)
        row_max = jnp.max(scores, axis=1, keepdims=True)
        exp_scores = jnp.exp(scores - row_max)
        attn_probs = (exp_scores / jnp.sum(exp_scores, axis=1, keepdims=True)).astype(bf16)
        return jnp.einsum(
            "hki,khd->ihd", attn_probs, value_col, preferred_element_type=f32
        ).reshape(crop_len, proj_width)

    attended = jnp.swapaxes(lax.map(one_column, jnp.arange(rows_here, dtype=jnp.int32)), 0, 1)
    gated = (attended * att_gating).astype(bf16)
    return (
        columns.astype(f32) + jnp.einsum("ije,ed->ijd", gated, att_out, preferred_element_type=f32)
    ).astype(bf16)


def solution(mesh):
    placed = (
        P(("grp", "row", "node"), None, None),
        P("grp"),
        P(),
        P(),
        P(),
        P(),
        P(),
        P(),
        P(),
        P(),
        P(),
        P(),
        P(),
        P(),
    )
    return jax.shard_map(
        shards,
        mesh=mesh,
        in_specs=placed,
        out_specs=P("grp", ("row", "node"), None),
        check_vma=False,
    )
```

profile of v0, /device:TPU:0, one launch (start us, length us, event | category | flops | bytes accessed | tf_op | source)
XLA Modules:
  0.0 269.4 jit_solution(12650610805624951265)
XLA Ops:
  6.6 1.4 convert_reduce_fusion
  8.0 1.9 fusion.16
  10.7 0.8 convolution_bitcast_fusion
  11.5 1.5 fusion.25
  13.0 1.1 copy.76
  14.1 1.6 fusion.13
  15.7 81.5 %all-gather.2.cloned.1.call-done = bf16[128,192,192]{0,2,1:T(8,128)(2,1)} async-done(((bf16[128,12,192]{0,2,1:T(8,128)(2,1)}), bf16[128,192,192]{0,2,1:T(8,128)(2,1)}) %all-gather.2.cloned.1.call-update) | async-done | bytes 9437200 | tf_op jit(solution)/shard_map/all_gather | solution.py:48
  97.3 17.4 %copy.77 = bf16[128,192,192]{2,1,0:T(8,128)(2,1)} copy(bf16[128,192,192]{0,2,1:T(8,128)(2,1)} %all-gather.2.cloned.1.call-done) | data formatting | bytes 18874368 | tf_op jit(solution)/shard_map/all_gather | solution.py:48
  114.7 7.9 %fusion.63 = (f32[12,192]{1,0:T(8,128)S(1)}, f32[128,12,192]{2,1,0:T(8,128)S(1)}) fusion(bf16[128,12,192]{2,1,0:T(8,128)(2,1)S(1)} %copy.76, bf16[128,192,192]{2,1,0:T(8,128)(2,1)} %copy.77), kind=kOutput, calls=%fused_computation.95 | convolution fusion | flops 113538816 | bytes 11215872 | tf_op jit(solution)/shard_map/erk,ejk->erj/dot_general | solution.py:45
  124.6 1.3 copy.79
  125.8 3.6 %all-to-all-start = ((bf16[12,192,128]{2,0,1:T(8,128)(2,1)}), bf16[12,192,128]{2,0,1:T(8,128)(2,1)S(1)}, u32[]{:S(2)}, u32[]{:S(2)}) async-start(bf16[12,192,128]{2,0,1:T(8,128)(2,1)} %copy.79), calls=%async_computation | async-start | bytes 1572864 | tf_op jit(solution)/shard_map/all_to_all | solution.py:54
  129.5 18.7 %all-to-all-done = bf16[12,192,128]{2,0,1:T(8,128)(2,1)S(1)} async-done(((bf16[12,192,128]{2,0,1:T(8,128)(2,1)}), bf16[12,192,128]{2,0,1:T(8,128)(2,1)S(1)}, u32[]{:S(2)}, u32[]{:S(2)}) %all-to-all-start) | async-done | bytes 589856 | tf_op jit(solution)/shard_map/all_to_all | solution.py:54
  148.9 0.9 multiply_reduce_fusion.1
  151.8 1.0 fusion.40
  152.8 22.4 %all_gather.7 = bf16[4,192,192]{1,0,2:T(4,128)(2,1)S(1)} all-gather(bf16[4,192,12]{1,0,2:T(4,128)(2,1)S(1)} %fusion.40), channel_id=1, replica_groups=mesh['grp'=2,'row'=8,'node'=2] {'row','node'}, dimensions={2}, use_global_device_ids=true | all-gather | bytes 313344 | tf_op jit(solution)/shard_map/all_gather | solution.py:68
  175.5 2.7 %fusion.64 = (bf16[192,12,512]{2,0,1:T(8,128)(2,1)S(1)}, f32[192,12,512]{2,0,1:T(8,128)}) fusion(bf16[128,128]{1,0:T(8,128)(2,1)S(1)} %copy-done.4, bf16[128,128]{1,0:T(8,128)(2,1)S(1)} %copy-done.5, bf16[128,128]{1,0:T(8,128)(2,1)S(1)} %copy-done.6, bf16[128,128]{1,0:T(8,128)(2,1)S(1)} %copy-done.7, f32[192,12,128]{2,0,1:T(8,128)S(1)} %reshape.130, ...), kind=kOutput, calls=%fused_computation.96 | convolution fusion | flops 304873472 | bytes 8407552 | tf_op jit(solution)/shard_map/ijc,ce->ije/dot_general | solution.py:57
  178.3 1.5 fusion.62
  179.7 79.9 %while.11 = (s32[]{:T(128)}, f32[12,192,128]{2,1,0:T(8,128)}, s32[12]{0:T(128)S(1)}, bf16[192,12,128]{2,0,1:T(8,128)(2,1)}, bf16[192,12,128]{2,0,1:T(8,128)(2,1)...) while((s32[]{:T(128)}, f32[12,192,128]{2,1,0:T(8,128)}, ...), condition=%wide.region_9.10_spmd.clone, body=%wide.region_6.9_spmd.clone.sunk | while | flops 20055364 | bytes 3595303 | solution.py:93
  182.2 0.8 constant_dynamic-slice_fusion.6
  184.4 0.8 constant_dynamic-slice_fusion.5
  188.8 0.8 constant_dynamic-slice_fusion.6
  195.5 0.8 constant_dynamic-slice_fusion.6
  202.1 0.8 constant_dynamic-slice_fusion.6
  208.8 0.8 constant_dynamic-slice_fusion.6
  215.4 0.8 constant_dynamic-slice_fusion.6
  222.1 0.8 constant_dynamic-slice_fusion.6
  228.8 0.8 constant_dynamic-slice_fusion.6
  235.4 0.8 constant_dynamic-slice_fusion.6
  242.1 0.8 constant_dynamic-slice_fusion.6
  248.7 0.8 constant_dynamic-slice_fusion.6
  255.4 0.8 constant_dynamic-slice_fusion.6
  259.6 2.9 %fusion.14 = bf16[192,12,128]{2,0,1:T(8,128)(2,1)} fusion(f32[192,12,128]{2,0,1:T(8,128)S(1)} %reshape.130, f32[192,12,512]{2,0,1:T(8,128)} %get-tuple-element.133, f32[12,192,128]{2,1,0:T(8,128)} %get-tuple-element.47, bf16[128,128]{1,0:T(8,128)(2,1)S(1)} %copy-done.12), kind=kOutput, calls=%fused_computation.30 | convolution fusion | flops 77561856 | bytes 4161536 | tf_op jit(solution)/shard_map/ije,ed->ijd/dot_general | solution.py:96
  (183 shorter events, 51.5 us)
Async XLA Ops:
  6.5 4.1 %copy-start = (bf16[4,128,128]{2,1,0:T(8,128)(2,1)S(1)}, bf16[4,128,128]{2,1,0:T(8,128)(2,1)}, u32[]{:S(2)}) copy-start(bf16[4,128,128]{2,1,0:T(8,128)(2,1)} %param.19) | copy-start | bytes 393220
  6.5 4.1 %copy-start.1 = (bf16[12,192,128]{2,1,0:T(8,128)(2,1)S(1)}, bf16[12,192,128]{2,1,0:T(8,128)(2,1)}, u32[]{:S(2)}) copy-start(bf16[12,192,128]{2,1,0:T(8,128)(2,1)} %param.16) | copy-start | bytes 1769476
  6.5 4.1 %copy-start.10 = (f32[128]{0:T(128)S(1)}, f32[128]{0:T(128)}, u32[]{:S(2)}) copy-start(f32[128]{0:T(128)} %param.18) | copy-start | bytes 1540
  6.5 90.8 %all-gather.2.cloned.1.call-start = ((), (), s32[]{:S(2)}) async-start(), calls=%async_computation.1 | async-start | bytes 10027008 | tf_op jit(solution)/shard_map/all_gather | solution.py:48
  9.9 0.8 copy-start.2
  122.6 0.7 copy-start.11
  123.3 0.8 copy-start.3
  125.8 22.3 %all-to-all-start = ((bf16[12,192,128]{2,0,1:T(8,128)(2,1)}), bf16[12,192,128]{2,0,1:T(8,128)(2,1)S(1)}, u32[]{:S(2)}, u32[]{:S(2)}) async-start(bf16[12,192,128]{2,0,1:T(8,128)(2,1)} %copy.79), calls=%async_computation | async-start | bytes 1572864 | tf_op jit(solution)/shard_map/all_to_all | solution.py:54
  151.1 0.7 copy-start.8
  151.1 0.7 copy-start.9
  151.8 23.7 %copy-start.4 = (bf16[128,128]{1,0:T(8,128)(2,1)S(1)}, bf16[128,128]{1,0:T(8,128)(2,1)}, u32[]{:S(2)}) copy-start(bf16[128,128]{1,0:T(8,128)(2,1)} %param.28) | copy-start | bytes 98308
  151.8 23.7 %copy-start.5 = (bf16[128,128]{1,0:T(8,128)(2,1)S(1)}, bf16[128,128]{1,0:T(8,128)(2,1)}, u32[]{:S(2)}) copy-start(bf16[128,128]{1,0:T(8,128)(2,1)} %param.26) | copy-start | bytes 98308
  151.8 23.7 %copy-start.6 = (bf16[128,128]{1,0:T(8,128)(2,1)S(1)}, bf16[128,128]{1,0:T(8,128)(2,1)}, u32[]{:S(2)}) copy-start(bf16[128,128]{1,0:T(8,128)(2,1)} %param.25) | copy-start | bytes 98308
  151.8 23.8 %copy-start.7 = (bf16[128,128]{1,0:T(8,128)(2,1)S(1)}, bf16[128,128]{1,0:T(8,128)(2,1)}, u32[]{:S(2)}) copy-start(bf16[128,128]{1,0:T(8,128)(2,1)} %param.24) | copy-start | bytes 98308
  179.7 79.9 %copy-start.12 = (bf16[128,128]{1,0:T(8,128)(2,1)S(1)}, bf16[128,128]{1,0:T(8,128)(2,1)}, u32[]{:S(2)}) copy-start(bf16[128,128]{1,0:T(8,128)(2,1)} %param.29) | copy-start | bytes 98308
Sparse Core Ops, SparseCore 0:
  13.1 84.1 all-gather.1
where the time goes:
time: 272 us; the launch traced here: 269 us
  waiting for transfers between devices  100 us (37%)
  local copies, waits for them, and re-layouts  64.1 us (24%)
  matrix products  24.9 us (9%)
  loops' own time  22.5 us (8%)
  blocking collectives  22.4 us (8%)
  other arithmetic  17.2 us (6%)
  between operations  14.3 us (5%)
  starting transfers between devices  3.61 us (1%)
    all_gather x1, waiting for transfers between devices, shards(): lax.all_gather(right_edge, ('row', 'node'), axis=1, tiled=True)  81.5 us
    another operation x1, loops' own time, shards(): lax.map(one_column, jnp.arange(rows_here, dtype=jnp.int32))  22.5 us
    all_gather x1, blocking collectives, shards(): lax.all_gather(bias_local, ('row', 'node'), axis=2, tiled=True).astype(f32)  22.4 us
    all_to_all x1, waiting for transfers between devices, shards(): lax.all_to_all(first_out, ('row', 'node'), split_axis=1, concat_axis=0, t...  18.7 us
    all_gather x1, local copies, waits for them, and re-layouts, shards(): lax.all_gather(right_edge, ('row', 'node'), axis=1, tiled=True)  17.4 us
    dynamic_slice x24, local copies, waits for them, and re-layouts, one_column(): lax.dynamic_index_in_dim(query_proj, column, 1, keepdims=False)  11.3 us
    dynamic_slice x24, local copies, waits for them, and re-layouts, one_column(): lax.dynamic_index_in_dim(value_proj, column, 1, keepdims=False)  10.9 us
    dynamic_update_slice x24, local copies, waits for them, and re-layouts, shards(): lax.map(one_column, jnp.arange(rows_here, dtype=jnp.int32))  8.91 us
  transfers between devices with their start and end apart: 2, of which 2 were waited for; matrix products, arithmetic and copies ran while one was open for 1% of the time, Pallas kernels for 0%

commit v1 on v0

v1 whole, which is shorter than its diff:
```python
import jax
import jax.numpy as jnp
from jax import lax
from jax.experimental import pallas as pl
from jax.experimental.pallas import tpu as pltpu
from jax.sharding import PartitionSpec as P

EPS = 1e-05
LANES = 128
LOG2E = 1.4426950408889634
F32 = jnp.float32
BF16 = jnp.bfloat16
AXES = ("row", "node")
VMEM_BYTES = 48 * 1024 * 1024


def norm_last(values, gain):
    average = jnp.mean(values, axis=-1, keepdims=True)
    centred = values - average
    variance = jnp.mean(centred * centred, axis=-1, keepdims=True)
    return centred * lax.rsqrt(variance + EPS) * gain


def sigmoid(values):
    return 0.5 * jnp.tanh(0.5 * values) + 0.5


def dot(a, b, a_dim, b_dim):
    return lax.dot_general(a, b, (((a_dim,), (b_dim,)), ((), ())), preferred_element_type=F32)


def call(kernel, out_shape, args, scratch=(), smem=(), name=None):
    specs = [
        pl.BlockSpec(memory_space=pltpu.SMEM if n in smem else pltpu.VMEM) for n in range(len(args))
    ]
    single = not isinstance(out_shape, (list, tuple))
    vmem = pl.BlockSpec(memory_space=pltpu.VMEM)
    return pl.pallas_call(
        kernel,
        out_shape=out_shape,
        in_specs=specs,
        out_specs=vmem if single else [vmem] * len(out_shape),
        scratch_shapes=list(scratch),
        compiler_params=pltpu.CompilerParams(vmem_limit_bytes=VMEM_BYTES),
        name=name,
    )(*args)


class Sizes:
    def __init__(self, rows, crop, devices, channels):
        self.rows, self.crop, self.devices = rows, crop, devices
        self.half = rows // 2
        self.whole = crop // LANES
        self.rest = crop % LANES
        self.tiles = rows * crop // LANES
        self.chans = channels // devices
        self.fold = max(1, 16 // self.chans)
        while self.tiles % self.fold:
            self.fold //= 2
        self.fold_tiles = self.tiles // self.fold
        self.channels = channels

    def place(self, source, local):
        h, q = divmod(local, self.half)
        return h * (self.crop // 2) + source * self.half + q


def residue_of(sz, place):
    h = (place >= sz.crop // 2).astype(jnp.int32)
    rem = place - h * (sz.crop // 2)
    source = rem // sz.half
    return source * sz.rows + h * sz.half + (rem - source * sz.half)


def edges_kernel(sz, len_ref, x_ref, ln_ref, w_ref, out_ref, norm_ref):
    length, first = len_ref[0], len_ref[1]
    cd, two = sz.chans, 2 * sz.chans
    ch = sz.channels
    r = lax.broadcasted_iota(jnp.int32, (2 * ch, 2 * ch), 0)
    e = lax.broadcasted_iota(jnp.int32, (2 * ch, 2 * ch), 1)
    target = ((r // cd) % 2) * ch + (r // two) * cd + r % cd
    pick = (target == e).astype(BF16)
    gate_w = dot(pick, jnp.concatenate([w_ref[0], w_ref[2]], axis=1), 1, 1).astype(BF16)
    value_w = dot(pick, jnp.concatenate([w_ref[1], w_ref[3]], axis=1), 1, 1).astype(BF16)
    gain = ln_ref[...]
    main = sz.whole * LANES
    for row in range(sz.rows):
        normed = norm_last(x_ref[row].astype(F32), gain).astype(BF16)
        norm_ref[pl.ds(row * main, main), :] = normed[:main]
        if sz.rest:
            h, q = divmod(row, sz.half)
            norm_ref[pl.ds(sz.rows * main + q * LANES + h * sz.rest, sz.rest), :] = normed[main:]
    lane = lax.broadcasted_iota(jnp.int32, (1, LANES), 1)

    def live(tile):
        if tile < sz.rows * sz.whole:
            row, m = divmod(tile, sz.whole)
            return ((first + row < length) & (m * LANES + lane < length)).astype(F32)
        q = tile - sz.rows * sz.whole
        second = lane >= sz.rest
        row = first + q + jnp.where(second, sz.half, 0)
        k = main + lane - jnp.where(second, sz.rest, 0)
        return ((row < length) & (k < length)).astype(F32)

    step = 2 if sz.tiles % 2 == 0 else 1
    for tile in range(0, sz.tiles, step):
        n = norm_ref[pl.ds(tile * LANES, step * LANES), :]
        mask = jnp.concatenate([live(tile + s) for s in range(step)], axis=1)
        edge = sigmoid(dot(gate_w, n, 1, 1)) * dot(value_w, n, 1, 1) * mask
        out_ref[:, :, tile * LANES : (tile + step) * LANES] = edge.reshape(
            sz.devices, two, step * LANES
        ).astype(BF16)


def outer_kernel(sz, e_ref, out_ref, main_ref, rest_ref, omain_ref, orest_ref):
    cd, two = sz.chans, 2 * sz.chans
    n, w, half = sz.crop, sz.whole, sz.half
    for s in range(sz.devices):
        for tile in range(sz.tiles):
            block = e_ref[s, :, tile * LANES : (tile + 1) * LANES].astype(F32)
            if tile < sz.rows * w:
                row, m = divmod(tile, w)
                main_ref[m, pl.ds(sz.place(s, row) * two, two), :] = block
            else:
                q = tile - sz.rows * w
                rest_ref[pl.ds((s * half + q) * two, two), :] = block

    def matrix(index):
        parts = [main_ref[m, pl.ds(index, n, stride=two), :].astype(BF16) for m in range(w)]
        if sz.rest:
            t = rest_ref[pl.ds(index, n // 2, stride=two), :].astype(BF16)
            parts.append(jnp.concatenate([t[:, : sz.rest], t[:, sz.rest :]], axis=0))
        return jnp.concatenate(parts, axis=1) if len(parts) > 1 else parts[0]

    for c in range(cd):
        outer = dot(matrix(cd + c), matrix(c), 1, 1)
        for m in range(w):
            omain_ref[m, pl.ds(c, n, stride=cd), :] = outer[:, m * LANES : (m + 1) * LANES]
        if sz.rest:
            orest_ref[pl.ds(c, n // 2, stride=cd), :] = jnp.concatenate(
                [outer[: n // 2, w * LANES :], outer[n // 2 :, w * LANES :]], axis=1
            )
    for s in range(sz.devices):
        for t in range(sz.fold_tiles):
            blocks = []
            for f in range(sz.fold):
                tile = f * sz.fold_tiles + t
                if tile < sz.rows * w:
                    row, m = divmod(tile, w)
                    blocks.append(omain_ref[m, pl.ds(sz.place(s, row) * cd, cd), :])
                else:
                    q = tile - sz.rows * w
                    blocks.append(orest_ref[pl.ds((s * half + q) * cd, cd), :])
            block = jnp.concatenate(blocks, axis=0) if len(blocks) > 1 else blocks[0]
            out_ref[s, :, t * LANES : (t + 1) * LANES] = block.astype(BF16)


def update_kernel(
    sz, o_ref, x_ref, lnp_ref, gate_ref, lnh_ref, tri_ref, lna_ref, biasw_ref,
    first_ref, col_ref, bias_ref, cols_ref,
):
    n, w, half, ch = sz.crop, sz.whole, sz.half, sz.channels
    for s in range(sz.devices):
        for row in range(sz.rows):
            cols_ref[pl.ds(sz.place(s, row) * 16, sz.rows), :] = x_ref[s * sz.rows + row].astype(F32)
    gain_h = jnp.transpose(jnp.broadcast_to(lnh_ref[...], (ch, ch)))
    tri = tri_ref[...]

    def update(tile):
        f, t = divmod(tile, sz.fold_tiles)
        block = o_ref[:, :, t * LANES : (t + 1) * LANES].astype(F32)
        block = block[:, f * sz.chans : (f + 1) * sz.chans, :].reshape(ch, LANES)
        average = jnp.mean(block, axis=0, keepdims=True)
        centred = block - average
        variance = jnp.mean(centred * centred, axis=0, keepdims=True)
        hidden = (centred * lax.rsqrt(variance + EPS) * gain_h).astype(BF16)
        return dot(hidden, tri, 0, 0)

    rest = [update(sz.rows * w + q) for q in range(half)] if sz.rest else None
    for j in range(sz.rows):
        parts = [update(j * w + m) for m in range(w)]
        if sz.rest:
            h, q = divmod(j, half)
            parts.append(rest[q][h * sz.rest : (h + 1) * sz.rest])
        change = jnp.concatenate(parts, axis=0) if len(parts) > 1 else parts[0]
        x = cols_ref[pl.ds(j, n, stride=16), :]
        normed = norm_last(x, lnp_ref[...]).astype(BF16)
        gating = sigmoid(dot(normed, gate_ref[...], 1, 0))
        first = (x + gating * change).astype(BF16)
        first_ref[j] = first
        col = norm_last(first.astype(F32), lna_ref[...]).astype(BF16)
        col_ref[j] = col
        heads = biasw_ref.shape[1]
        bias_ref[pl.ds(j * heads, heads), :] = dot(biasw_ref[...], col, 0, 1)


def project_kernel(sz, col_ref, q_ref, k_ref, v_ref, g_ref, qo_ref, ko_ref, vo_ref, go_ref):
    n, ch = sz.crop, sz.channels
    qk = jnp.concatenate([q_ref[...], k_ref[...]], axis=1)
    vg = jnp.transpose(jnp.concatenate([v_ref[...], g_ref[...]], axis=1).astype(F32)).astype(BF16)
    width = q_ref.shape[1]
    for j in range(sz.rows):
        col = col_ref[j]
        both = dot(col, qk, 1, 0)
        qo_ref[j] = both[:, :width].astype(BF16)
        ko_ref[j] = both[:, width:].astype(BF16)
        other = dot(vg, col, 1, 1)
        vo_ref[j] = other[:width].astype(BF16)
        go_ref[j] = sigmoid(other[width:])


def attend_kernel(
    sz, heads, len_ref, q_ref, k_ref, v_ref, g_ref, first_ref, bias_ref, aout_ref,
    out_ref, rows_ref, biasT_ref, sum_ref,
):
    n, w, ch = sz.crop, sz.whole, sz.channels
    length = len_ref[0]
    width = q_ref.shape[2]
    hd = width // heads
    per = sz.half * heads
    for s in range(sz.devices):
        block = bias_ref[s].astype(F32) * LOG2E
        for h in range(2):
            part = block[h * per : (h + 1) * per]
            at = pl.ds((h * sz.devices + s) * per, per)
            for m in range(w):
                rows_ref[m, at, :] = part[:, m * LANES : (m + 1) * LANES]
            if sz.rest:
                rows_ref[w, at, : sz.rest] = part[:, w * LANES :]
    key = residue_of(sz, lax.broadcasted_iota(jnp.int32, (n, LANES), 0))
    dead = jnp.where(key < length, 0.0, -1e9 * LOG2E).astype(F32)
    halves = []
    for head in range(heads):
        b = [
            jnp.transpose(rows_ref[m, pl.ds(head, n, stride=heads), :])
            for m in range(w + (sz.rest > 0))
        ]
        if sz.rest:
            b[w] = b[w][: sz.rest]
        b = jnp.concatenate(b, axis=0) if len(b) > 1 else b[0]
        for m in range(w):
            biasT_ref[:, (head * w + m) * LANES : (head * w + m + 1) * LANES] = (
                b[:, m * LANES : (m + 1) * LANES] + dead
            )
        if sz.rest:
            halves.append(b[:, w * LANES :])
    per_tile = LANES // sz.rest if sz.rest else 1
    base = heads * w
    if sz.rest:
        for t in range(heads // per_tile):
            biasT_ref[:, (base + t) * LANES : (base + t + 1) * LANES] = (
                jnp.concatenate(halves[t * per_tile : (t + 1) * per_tile], axis=1) + dead
            )
    lane = lax.broadcasted_iota(jnp.int32, (1, width), 1)
    head_masks = [((lane >= h * hd) & (lane < (h + 1) * hd)).astype(BF16) for h in range(heads)]
    scale = (hd ** (-0.5)) * LOG2E
    for j in range(sz.rows):
        q = q_ref[j]
        masked = [q * head_masks[h] for h in range(heads)]
        pieces = [masked[h][: w * LANES] for h in range(heads)]
        if sz.rest:
            pieces += [masked[h][w * LANES :] for h in range(heads)]
        stacked = jnp.concatenate(pieces, axis=0)
        scores = dot(k_ref[j], stacked, 1, 1) * scale + biasT_ref[...]
        top = jnp.max(scores, axis=0, keepdims=True)
        weights = jnp.exp2(scores - top)
        total = jnp.sum(weights, axis=0, keepdims=True)
        mixed = dot(v_ref[j], weights.astype(BF16), 1, 0)
        inverse = 1.0 / total
        mains, rests = [], []
        for h in range(heads):
            sl = slice(h * w * LANES, (h + 1) * w * LANES)
            mains.append(mixed[h * hd : (h + 1) * hd, sl] * inverse[:, sl])
            if sz.rest:
                t, part = divmod(h, per_tile)
                sl = slice((base + t) * LANES, (base + t + 1) * LANES)
                piece = mixed[h * hd : (h + 1) * hd, sl] * inverse[:, sl]
                rests.append(piece[:, part * sz.rest : (part + 1) * sz.rest])
        attended = jnp.concatenate(mains, axis=0)
        if sz.rest:
            attended = jnp.concatenate([attended, jnp.concatenate(rests, axis=0)], axis=1)
        gated = (attended * g_ref[j]).astype(BF16)
        total_out = first_ref[j].astype(F32) + dot(gated, aout_ref[...], 0, 0)
        sum_ref[pl.ds(j, n, stride=16), :] = total_out
    for s in range(sz.devices):
        for row in range(sz.rows):
            out_ref[s * sz.rows + row] = sum_ref[pl.ds(sz.place(s, row) * 16, sz.rows), :].astype(
                BF16
            )


def shards(
    devices,
    pair_rep, length, ln_pair, tri_in, tri_gate, ln_hidden, tri_out, ln_att,
    att_q, att_k, att_v, att_bias, att_gate, att_out,
):
    rows, crop, ch = pair_rep.shape
    heads = att_bias.shape[1]
    sz = Sizes(rows, crop, devices, ch)
    n, cd = crop, sz.chans
    first_row = lax.axis_index(AXES) * rows
    info = jnp.stack([length[0], first_row.astype(jnp.int32)])
    columns = lax.all_to_all(pair_rep, AXES, split_axis=1, concat_axis=0, tiled=True)

    def bound(kernel, *extra):
        def run(*refs):
            return kernel(sz, *extra, *refs)

        return run

    shape = jax.ShapeDtypeStruct
    edges = call(
        bound(edges_kernel),
        shape((devices, 2 * cd, rows * crop), BF16),
        (info, pair_rep, ln_pair[None], tri_in),
        scratch=[pltpu.VMEM((rows * crop, ch), BF16)],
        smem=(0,),
        name="edges",
    )
    edges = lax.all_to_all(edges, AXES, split_axis=0, concat_axis=0, tiled=True)
    rest_rows = max(n // 2, 8)
    outer = call(
        bound(outer_kernel),
        shape((devices, sz.fold * cd, rows * crop // sz.fold), BF16),
        (edges,),
        scratch=[
            pltpu.VMEM((sz.whole, n * 2 * cd, LANES), F32),
            pltpu.VMEM((rest_rows * 2 * cd, LANES), F32),
            pltpu.VMEM((sz.whole, n * cd, LANES), F32),
            pltpu.VMEM((rest_rows * cd, LANES), F32),
        ],
        name="outer",
    )
    outer = lax.all_to_all(outer, AXES, split_axis=0, concat_axis=0, tiled=True)
    first, col, bias = call(
        bound(update_kernel),
        [
            shape((rows, n, ch), BF16),
            shape((rows, n, ch), BF16),
            shape((rows * heads, n), F32),
        ],
        (outer, columns, ln_pair[None], tri_gate, ln_hidden[None], tri_out, ln_att[None], att_bias),
        scratch=[pltpu.VMEM((n * 16, ch), F32)],
        name="update",
    )
    bias_all = lax.all_gather(bias.astype(BF16), AXES, axis=0, tiled=False)
    query, key, value, gate = call(
        bound(project_kernel),
        [
            shape((rows, n, att_q.shape[1]), BF16),
            shape((rows, n, att_q.shape[1]), BF16),
            shape((rows, att_q.shape[1], n), BF16),
            shape((rows, att_q.shape[1], n), F32),
        ],
        (col, att_q, att_k, att_v, att_gate),
        name="project",
    )
    return call(
        bound(attend_kernel, heads),
        shape((n, rows, ch), BF16),
        (info, query, key, value, gate, first, bias_all, att_out),
        scratch=[
            pltpu.VMEM((-(-n // LANES), n * heads, LANES), F32),
            pltpu.VMEM((n, heads * n), F32),
            pltpu.VMEM((n * 16, ch), F32),
        ],
        smem=(0,),
        name="attend",
    )


def solution(mesh):
    devices = mesh.shape["row"] * mesh.shape["node"]

    def body(*args):
        return shards(devices, *args)

    return jax.shard_map(
        body,
        mesh=mesh,
        in_specs=(P(("grp", "row", "node"), None, None), P("grp")) + (P(),) * 12,
        out_specs=P("grp", AXES, None),
        check_vma=False,
    )
```

time: 272 us -> 120 us (0.44)
  local copies, waits for them, and re-layouts: 64.1 us -> 5.27 us
  waiting for transfers between devices: 100 us -> 55.8 us
  matrix products: 24.9 us -> 0 us
  loops' own time: 22.5 us -> 0 us
  other arithmetic: 17.2 us -> 0.08 us
  starting transfers between devices: 3.61 us -> 20.5 us
  Pallas kernels: 0 us -> 15.9 us
  between operations: 14.3 us -> 0.82 us
    all_gather x1 -> x0, waiting for transfers between devices: 81.5 us -> none  [shards(): lax.all_gather(right_edge, ('row', 'node'), axis=1, tiled=True)]
    all_to_all x1 -> x3, waiting for transfers between devices: 18.7 us -> 55.8 us  [the longest x1 23.8 us: shards(): edges = lax.all_to_all(edges, AXES, split_axis=0, concat_axis=0, tiled=True)]
    dynamic_slice x72 -> x0, local copies, waits for them, and re-layouts: 30.8 us -> none  [the longest x24 11.3 us: one_column(): lax.dynamic_index_in_dim(query_proj, column, 1, keepdims=False)]
    dot_general x31 -> x0, matrix products: 24.9 us -> none  [the longest x1 7.92 us: shards(): jnp.einsum('erk,ejk->erj', left_edge, lax.all_gather(right_edge, ('row',...]
    another operation x1 -> x0, loops' own time: 22.5 us -> none  [shards(): lax.map(one_column, jnp.arange(rows_here, dtype=jnp.int32))]
    all_gather x1 -> x0, local copies, waits for them, and re-layouts: 17.4 us -> none  [shards(): lax.all_gather(right_edge, ('row', 'node'), axis=1, tiled=True)]
    all_to_all x1 -> x3, starting transfers between devices: 3.61 us -> 20.5 us  [the longest x1 7.53 us: shards(): edges = lax.all_to_all(edges, AXES, split_axis=0, concat_axis=0, tiled=True)]
    pallas_call x0 -> x5, Pallas kernels: none -> 15.9 us  [call(): pl.pallas_call(kernel, out_shape=out_shape, in_specs=specs, out_specs=vme...]
  transfers between devices with their start and end apart: 2 -> 3, of which waited for: 2 -> 3; matrix products, arithmetic and copies ran while one was open for 1% -> 1% of each run, Pallas kernels for 0% -> 2%
where the time goes in v1:
time: 120 us
  waiting for transfers between devices  55.8 us (46%)
  blocking collectives  21.4 us (18%)
  starting transfers between devices  20.5 us (17%)
  Pallas kernels  15.9 us (13%)
  local copies, waits for them, and re-layouts  5.27 us (4%)
    all_to_all x1, waiting for transfers between devices, shards(): edges = lax.all_to_all(edges, AXES, split_axis=0, concat_axis=0, tiled=True)  23.8 us
    all_gather x1, blocking collectives, shards(): bias_all = lax.all_gather(bias.astype(BF16), AXES, axis=0, tiled=False)  21.4 us
    all_to_all x1, waiting for transfers between devices, shards(): lax.all_to_all(pair_rep, AXES, split_axis=1, concat_axis=0, tiled=True)  16.8 us
    pallas_call x5, Pallas kernels, call(): pl.pallas_call(kernel, out_shape=out_shape, in_specs=specs, out_specs=vme...  15.9 us
    all_to_all x1, waiting for transfers between devices, shards(): outer = lax.all_to_all(outer, AXES, split_axis=0, concat_axis=0, tiled=True)  15.2 us
    all_to_all x1, starting transfers between devices, shards(): edges = lax.all_to_all(edges, AXES, split_axis=0, concat_axis=0, tiled=True)  7.53 us
    all_to_all x1, starting transfers between devices, shards(): lax.all_to_all(pair_rep, AXES, split_axis=1, concat_axis=0, tiled=True)  7.48 us
    all_to_all x1, starting transfers between devices, shards(): outer = lax.all_to_all(outer, AXES, split_axis=0, concat_axis=0, tiled=True)  5.48 us
  transfers between devices with their start and end apart: 3, of which 3 were waited for; matrix products, arithmetic and copies ran while one was open for 1% of the time, Pallas kernels for 2%

profile of v1, /device:TPU:0, one launch (start us, length us, event | category | flops | bytes accessed | tf_op | source)
XLA Modules:
  0.0 119.7 jit_solution(7726376422870999003)
XLA Ops:
  0.7 0.1 pad_add_fusion.refs_0_
  0.7 1.1 copy-done
  1.8 0.9 copy-done.2
  2.7 0.7 copy-done.10
  3.4 3.3 %edges.1 = bf16[16,16,2304]{2,1,0:T(8,128)(2,1)} custom-call(s32[2]{0:T(128)S(1)} %pad_add_fusion.refs_0_, bf16[12,192,128]{2,1,0:T(8,128)(2,1)S(1)} %copy-done, f32[1,128]{1,0:T(1,128)S(1)} %bitcast.12, bf16[4,128,128]{2,1,0:T(8,128)(2,1)S(1)} %copy-done.2), custom_call_target="tpu_custom_call" | custom-call | tf_op jit(solution)/shard_map/edges/pallas_call | solution.py:38
  6.7 7.5 %all-to-all-start = ((bf16[16,16,2304]{2,1,0:T(8,128)(2,1)}), bf16[16,16,2304]{2,1,0:T(8,128)(2,1)S(1)}, u32[]{:S(2)}, u32[]{:S(2)}) async-start(bf16[16,16,2304]{2,1,0:T(8,128)(2,1)} %edges.1), calls=%async_computation | async-start | bytes 2359296 | tf_op jit(solution)/shard_map/all_to_all | solution.py:320
  14.2 1.3 %copy.21 = bf16[12,192,128]{2,0,1:T(8,128)(2,1)} copy(bf16[12,192,128]{2,1,0:T(8,128)(2,1)S(1)} %copy-done.1) | data formatting | bytes 1179648 | tf_op args[0]
  15.5 23.8 %all-to-all-done.refs_0_ = bf16[16,16,2304]{2,1,0:T(8,128)(2,1)S(1)} async-done(((bf16[16,16,2304]{2,1,0:T(8,128)(2,1)}), bf16[16,16,2304]{2,1,0:T(8,128)(2,1)S(1)}, u32[]{:S(2)}, u32[]{:S(2)}) %all-to-all-start) | async-done | bytes 1179680 | tf_op jit(solution)/shard_map/all_to_all | solution.py:320
  39.4 7.5 %all-to-all-start.2 = ((bf16[12,192,128]{2,0,1:T(8,128)(2,1)}), bf16[12,192,128]{2,0,1:T(8,128)(2,1)S(1)}, u32[]{:S(2)}, u32[]{:S(2)}) async-start(bf16[12,192,128]{2,0,1:T(8,128)(2,1)} %copy.21), calls=%async_computation.2 | async-start | bytes 1572864 | tf_op jit(solution)/shard_map/all_to_all | solution.py:303
  46.8 0.0 copy-start.14
  46.9 1.9 %outer.1 = bf16[16,16,1152]{2,1,0:T(8,128)(2,1)} custom-call(bf16[16,16,2304]{2,1,0:T(8,128)(2,1)S(1)} %all-to-all-done.refs_0_), custom_call_target="tpu_custom_call" | custom-call | tf_op jit(solution)/shard_map/outer/pallas_call | solution.py:38
  48.8 0.0 copy-start.13
  48.8 16.8 %all-to-all-done.2 = bf16[12,192,128]{2,0,1:T(8,128)(2,1)S(1)} async-done(((bf16[12,192,128]{2,0,1:T(8,128)(2,1)}), bf16[12,192,128]{2,0,1:T(8,128)(2,1)S(1)}, u32[]{:S(2)}, u32[]{:S(2)}) %all-to-all-start.2) | async-done | bytes 589856 | tf_op jit(solution)/shard_map/all_to_all | solution.py:303
  65.6 5.5 %all-to-all-start.1 = ((bf16[16,16,1152]{2,1,0:T(8,128)(2,1)}), bf16[16,16,1152]{2,1,0:T(8,128)(2,1)S(1)}, u32[]{:S(2)}, u32[]{:S(2)}) async-start(bf16[16,16,1152]{2,1,0:T(8,128)(2,1)} %outer.1), calls=%async_computation.1 | async-start | bytes 1179648 | tf_op jit(solution)/shard_map/all_to_all | solution.py:334
  71.0 0.1 copy.24.refs_7_
  71.2 0.2 copy.23
  71.4 0.0 copy-start.6
  71.4 0.0 copy-start.7
  71.4 0.0 copy-start.8
  71.4 0.0 copy-start.9
  71.4 15.2 %all-to-all-done.1.refs_0_ = bf16[16,16,1152]{2,1,0:T(8,128)(2,1)S(1)} async-done(((bf16[16,16,1152]{2,1,0:T(8,128)(2,1)}), bf16[16,16,1152]{2,1,0:T(8,128)(2,1)S(1)}, u32[]{:S(2)}, u32[]{:S(2)}) %all-to-all-start.1) | async-done | bytes 589856 | tf_op jit(solution)/shard_map/all_to_all | solution.py:334
  86.6 0.0 copy-done.11
  86.6 0.0 copy-done.12
  86.6 0.0 copy-done.13
  86.6 0.0 copy-start.3
  86.6 3.2 %update.1 = (bf16[12,192,128]{2,1,0:T(8,128)(2,1)S(1)}, bf16[12,192,128]{2,1,0:T(8,128)(2,1)S(1)}, f32[48,192]{1,0:T(8,128)S(1)}) custom-call(bf16[16,16,1152]{2,1,0:T(8,128)(2,1)S(1)} %all-to-all-done.1.refs_0_, bf16[192,12,128]{2,1,0:T(8,128)(2,1)S(1)} %bitcast.10, f32[1,128]{1,0:T(1,128)S(1)} %bitcast.13, bf16[128,128]{1,0:T(8,128)(2,1)S(1)} %copy-done.4, ...), custom_call_target="tpu_custom_call" | custom-call | tf_op jit(solution)/shard_map/update/pallas_call | solution.py:38
  89.9 21.4 %all-gather = bf16[768,192]{1,0:T(8,128)(2,1)S(1)} all-gather(bf16[48,192]{1,0:T(8,128)(2,1)S(1)} %convert_element_type.3), channel_id=2, replica_groups=mesh['grp'=2,'row'=8,'node'=2] {'row','node'}, dimensions={0}, use_global_device_ids=true | all-gather | bytes 313344 | tf_op jit(solution)/shard_map/all_gather | solution.py:346
  111.3 0.0 copy-done.6
  111.3 0.0 copy-done.8
  111.3 0.9 project.1
  112.2 6.6 %attend.1 = bf16[192,12,128]{2,1,0:T(8,128)(2,1)S(1)} custom-call(s32[2]{0:T(128)S(1)} %pad_add_fusion.refs_0_, bf16[12,192,128]{2,1,0:T(8,128)(2,1)S(1)} %get-tuple-element.13.refs_1_, bf16[12,192,128]{2,1,0:T(8,128)(2,1)S(1)} %get-tuple-element.14.refs_2_, bf16[12,128,192]{2,1,0:T(8,128)(2,1)S(1)} %get-tuple-element.15.refs_3_, ...), custom_call_target="tpu_custom_call" | custom-call | tf_op jit(solution)/shard_map/attend/pallas_call | solution.py:38
  118.8 1.0 copy.25
  (16 shorter events, 0.0 us)
Async XLA Ops:
  0.7 1.1 copy-start
  1.8 0.9 copy-start.2
  2.7 0.7 copy-start.10
  6.7 7.5 %copy-start.1 = (bf16[12,192,128]{2,1,0:T(8,128)(2,1)S(1)}, bf16[12,192,128]{2,1,0:T(8,128)(2,1)}, u32[]{:S(2)}) copy-start(bf16[12,192,128]{2,1,0:T(8,128)(2,1)} %refs_1_.2) | copy-start | bytes 1769476
  6.7 32.7 %all-to-all-start = ((bf16[16,16,2304]{2,1,0:T(8,128)(2,1)}), bf16[16,16,2304]{2,1,0:T(8,128)(2,1)S(1)}, u32[]{:S(2)}, u32[]{:S(2)}) async-start(bf16[16,16,2304]{2,1,0:T(8,128)(2,1)} %edges.1), calls=%async_computation | async-start | bytes 2359296 | tf_op jit(solution)/shard_map/all_to_all | solution.py:320
  39.4 26.2 %all-to-all-start.2 = ((bf16[12,192,128]{2,0,1:T(8,128)(2,1)}), bf16[12,192,128]{2,0,1:T(8,128)(2,1)S(1)}, u32[]{:S(2)}, u32[]{:S(2)}) async-start(bf16[12,192,128]{2,0,1:T(8,128)(2,1)} %copy.21), calls=%async_computation.2 | async-start | bytes 1572864 | tf_op jit(solution)/shard_map/all_to_all | solution.py:303
  46.8 24.2 %copy-start.14 = (bf16[128,4]{0,1:T(4,128)(2,1)S(1)}, bf16[128,4]{0,1:T(4,128)(2,1)}, u32[]{:S(2)}) copy-start(bf16[128,4]{0,1:T(4,128)(2,1)} %param.25) | copy-start | bytes 3076
  48.8 37.8 %copy-start.4 = (bf16[128,128]{1,0:T(8,128)(2,1)S(1)}, bf16[128,128]{1,0:T(8,128)(2,1)}, u32[]{:S(2)}) copy-start(bf16[128,128]{1,0:T(8,128)(2,1)} %refs_3_.4) | copy-start | bytes 98308
  48.8 37.8 %copy-start.5 = (bf16[128,128]{1,0:T(8,128)(2,1)S(1)}, bf16[128,128]{1,0:T(8,128)(2,1)}, u32[]{:S(2)}) copy-start(bf16[128,128]{1,0:T(8,128)(2,1)} %refs_5_.1) | copy-start | bytes 98308
  48.8 37.8 %copy-start.11 = (f32[128]{0:T(128)S(1)}, f32[128]{0:T(128)}, u32[]{:S(2)}) copy-start(f32[128]{0:T(128)} %param.16) | copy-start | bytes 1540
  48.8 37.8 %copy-start.12 = (f32[128]{0:T(128)S(1)}, f32[128]{0:T(128)}, u32[]{:S(2)}) copy-start(f32[128]{0:T(128)} %param.19) | copy-start | bytes 1540
  48.8 37.8 %copy-start.13 = (f32[128]{0:T(128)S(1)}, f32[128]{0:T(128)}, u32[]{:S(2)}) copy-start(f32[128]{0:T(128)} %param.21) | copy-start | bytes 1540
  65.6 21.0 %all-to-all-start.1 = ((bf16[16,16,1152]{2,1,0:T(8,128)(2,1)}), bf16[16,16,1152]{2,1,0:T(8,128)(2,1)S(1)}, u32[]{:S(2)}, u32[]{:S(2)}) async-start(bf16[16,16,1152]{2,1,0:T(8,128)(2,1)} %outer.1), calls=%async_computation.1 | async-start | bytes 1179648 | tf_op jit(solution)/shard_map/all_to_all | solution.py:334
  71.4 39.9 %copy-start.6 = (bf16[128,128]{1,0:T(8,128)(2,1)S(1)}, bf16[128,128]{1,0:T(8,128)(2,1)}, u32[]{:S(2)}) copy-start(bf16[128,128]{1,0:T(8,128)(2,1)} %refs_1_.3) | copy-start | bytes 98308
  71.4 39.9 %copy-start.7 = (bf16[128,128]{1,0:T(8,128)(2,1)S(1)}, bf16[128,128]{1,0:T(8,128)(2,1)}, u32[]{:S(2)}) copy-start(bf16[128,128]{1,0:T(8,128)(2,1)} %refs_2_.1) | copy-start | bytes 98308
  71.4 39.9 %copy-start.8 = (bf16[128,128]{1,0:T(8,128)(2,1)S(1)}, bf16[128,128]{1,0:T(8,128)(2,1)}, u32[]{:S(2)}) copy-start(bf16[128,128]{1,0:T(8,128)(2,1)} %refs_3_.5) | copy-start | bytes 98308
  71.4 39.9 %copy-start.9 = (bf16[128,128]{1,0:T(8,128)(2,1)S(1)}, bf16[128,128]{1,0:T(8,128)(2,1)}, u32[]{:S(2)}) copy-start(bf16[128,128]{1,0:T(8,128)(2,1)} %refs_4_.1) | copy-start | bytes 98308
  86.6 25.6 %copy-start.3 = (bf16[128,128]{1,0:T(8,128)(2,1)S(1)}, bf16[128,128]{1,0:T(8,128)(2,1)}, u32[]{:S(2)}) copy-start(bf16[128,128]{1,0:T(8,128)(2,1)} %refs_7_.2) | copy-start | bytes 98308

commit v2 on v1

--- a/solution.py
+++ b/solution.py
@@ -60,19 +60,11 @@
         self.fold_tiles = self.tiles // self.fold
         self.channels = channels
 
-    def place(self, source, local):
-        h, q = divmod(local, self.half)
-        return h * (self.crop // 2) + source * self.half + q
-
-
-def residue_of(sz, place):
-    h = (place >= sz.crop // 2).astype(jnp.int32)
-    rem = place - h * (sz.crop // 2)
-    source = rem // sz.half
-    return source * sz.rows + h * sz.half + (rem - source * sz.half)
-
-
-def edges_kernel(sz, len_ref, x_ref, ln_ref, w_ref, out_ref, norm_ref):
+        self.block = rows * rows
+        self.block_tiles = -(-self.block // (2 * self.chans))
+
+
+def edges_kernel(sz, len_ref, x_ref, ln_ref, w_ref, out_ref, norm_ref, pair_ref):
     length, first = len_ref[0], len_ref[1]
     cd, two = sz.chans, 2 * sz.chans
     ch = sz.channels
@@ -85,11 +77,18 @@
     gain = ln_ref[...]
     main = sz.whole * LANES
     for row in range(sz.rows):
-        normed = norm_last(x_ref[row].astype(F32), gain).astype(BF16)
+        x = x_ref[row].astype(F32)
+        for d in range(sz.devices):
+            pair_ref[d, row * sz.rows : (row + 1) * sz.rows, :] = x[d * sz.rows : (d + 1) * sz.rows]
+        normed = norm_last(x, gain).astype(BF16)
         norm_ref[pl.ds(row * main, main), :] = normed[:main]
         if sz.rest:
             h, q = divmod(row, sz.half)
             norm_ref[pl.ds(sz.rows * main + q * LANES + h * sz.rest, sz.rest), :] = normed[main:]
+    for d in range(sz.devices):
+        for t in range(sz.block_tiles):
+            at = (sz.tiles + t) * LANES
+            out_ref[d, :, at : at + LANES] = pair_ref[d, t * two : (t + 1) * two, :].astype(BF16)
     lane = lax.broadcasted_iota(jnp.int32, (1, LANES), 1)
 
     def live(tile):
@@ -120,16 +119,16 @@
             block = e_ref[s, :, tile * LANES : (tile + 1) * LANES].astype(F32)
             if tile < sz.rows * w:
                 row, m = divmod(tile, w)
-                main_ref[m, pl.ds(sz.place(s, row) * two, two), :] = block
+                main_ref[m, pl.ds((s * sz.rows + row) * two, two), :] = block
             else:
-                q = tile - sz.rows * w
-                rest_ref[pl.ds((s * half + q) * two, two), :] = block
+                at = s * sz.rows + tile - sz.rows * w
+                rest_ref[pl.ds(at * two, two), :] = block
+                rest_ref[pl.ds((at + half) * two, two), :] = pltpu.roll(block, sz.rest, 1)
 
     def matrix(index):
         parts = [main_ref[m, pl.ds(index, n, stride=two), :].astype(BF16) for m in range(w)]
         if sz.rest:
-            t = rest_ref[pl.ds(index, n // 2, stride=two), :].astype(BF16)
-            parts.append(jnp.concatenate([t[:, : sz.rest], t[:, sz.rest :]], axis=0))
+            parts.append(rest_ref[pl.ds(index, n, stride=two), :].astype(BF16)[:, : sz.rest])
         return jnp.concatenate(parts, axis=1) if len(parts) > 1 else parts[0]
 
     for c in range(cd):
@@ -137,9 +136,9 @@
         for m in range(w):
             omain_ref[m, pl.ds(c, n, stride=cd), :] = outer[:, m * LANES : (m + 1) * LANES]
         if sz.rest:
-            orest_ref[pl.ds(c, n // 2, stride=cd), :] = jnp.concatenate(
-                [outer[: n // 2, w * LANES :], outer[n // 2 :, w * LANES :]], axis=1
-            )
+            part = outer[:, w * LANES :]
+            orest_ref[pl.ds(c, n, stride=cd), :] = jnp.concatenate([part, part], axis=1)
+    low = lax.broadcasted_iota(jnp.int32, (cd, LANES), 1) < sz.rest
     for s in range(sz.devices):
         for t in range(sz.fold_tiles):
             blocks = []
@@ -147,22 +146,25 @@
                 tile = f * sz.fold_tiles + t
                 if tile < sz.rows * w:
                     row, m = divmod(tile, w)
-                    blocks.append(omain_ref[m, pl.ds(sz.place(s, row) * cd, cd), :])
+                    blocks.append(omain_ref[m, pl.ds((s * sz.rows + row) * cd, cd), :])
                 else:
-                    q = tile - sz.rows * w
-                    blocks.append(orest_ref[pl.ds((s * half + q) * cd, cd), :])
+                    at = s * sz.rows + tile - sz.rows * w
+                    one = orest_ref[pl.ds(at * cd, cd), :]
+                    blocks.append(jnp.where(low, one, orest_ref[pl.ds((at + half) * cd, cd), :]))
             block = jnp.concatenate(blocks, axis=0) if len(blocks) > 1 else blocks[0]
             out_ref[s, :, t * LANES : (t + 1) * LANES] = block.astype(BF16)
 
 
 def update_kernel(
     sz, o_ref, x_ref, lnp_ref, gate_ref, lnh_ref, tri_ref, lna_ref, biasw_ref,
-    first_ref, col_ref, bias_ref, cols_ref,
+    first_ref, col_ref, bias_ref, cols_ref, brow_ref,
 ):
     n, w, half, ch = sz.crop, sz.whole, sz.half, sz.channels
+    two = 2 * sz.chans
     for s in range(sz.devices):
-        for row in range(sz.rows):
-            cols_ref[pl.ds(sz.place(s, row) * 16, sz.rows), :] = x_ref[s * sz.rows + row].astype(F32)
+        for t in range(sz.block_tiles):
+            at = (sz.tiles + t) * LANES
+            cols_ref[pl.ds(s * sz.block + t * two, two), :] = x_ref[s, :, at : at + LANES].astype(F32)
     gain_h = jnp.transpose(jnp.broadcast_to(lnh_ref[...], (ch, ch)))
     tri = tri_ref[...]
 
@@ -183,7 +185,7 @@
             h, q = divmod(j, half)
             parts.append(rest[q][h * sz.rest : (h + 1) * sz.rest])
         change = jnp.concatenate(parts, axis=0) if len(parts) > 1 else parts[0]
-        x = cols_ref[pl.ds(j, n, stride=16), :]
+        x = cols_ref[pl.ds(j, n, stride=sz.rows), :]
         normed = norm_last(x, lnp_ref[...]).astype(BF16)
         gating = sigmoid(dot(normed, gate_ref[...], 1, 0))
         first = (x + gating * change).astype(BF16)
@@ -191,7 +193,8 @@
         col = norm_last(first.astype(F32), lna_ref[...]).astype(BF16)
         col_ref[j] = col
         heads = biasw_ref.shape[1]
-        bias_ref[pl.ds(j * heads, heads), :] = dot(biasw_ref[...], col, 0, 1)
+        brow_ref[pl.ds(j * heads, heads), :] = dot(biasw_ref[...], col, 0, 1)
+    bias_ref[...] = brow_ref[...].astype(BF16)
 
 
 def project_kernel(sz, col_ref, q_ref, k_ref, v_ref, g_ref, qo_ref, ko_ref, vo_ref, go_ref):
@@ -210,24 +213,23 @@
 
 
 def attend_kernel(
-    sz, heads, len_ref, q_ref, k_ref, v_ref, g_ref, first_ref, bias_ref, aout_ref,
-    out_ref, rows_ref, biasT_ref, sum_ref,
+    sz, heads, steps, len_ref, q_ref, k_ref, v_ref, g_ref, first_ref, aout_ref, *refs
 ):
+    bias_refs, (out_ref, rows_ref, biasT_ref) = refs[:-3], refs[-3:]
     n, w, ch = sz.crop, sz.whole, sz.channels
-    length = len_ref[0]
+    length, me = len_ref[0], len_ref[2]
     width = q_ref.shape[2]
     hd = width // heads
-    per = sz.half * heads
-    for s in range(sz.devices):
-        block = bias_ref[s].astype(F32) * LOG2E
-        for h in range(2):
-            part = block[h * per : (h + 1) * per]
-            at = pl.ds((h * sz.devices + s) * per, per)
+    per = sz.rows * heads
+    for ref, offsets in zip(bias_refs, steps):
+        for place, offset in enumerate(offsets):
+            at = pl.ds(pl.multiple_of((me ^ offset) * per, 8), per)
+            part = ref[place].astype(F32) * LOG2E
             for m in range(w):
                 rows_ref[m, at, :] = part[:, m * LANES : (m + 1) * LANES]
             if sz.rest:
                 rows_ref[w, at, : sz.rest] = part[:, w * LANES :]
-    key = residue_of(sz, lax.broadcasted_iota(jnp.int32, (n, LANES), 0))
+    key = lax.broadcasted_iota(jnp.int32, (n, LANES), 0)
     dead = jnp.where(key < length, 0.0, -1e9 * LOG2E).astype(F32)
     halves = []
     for head in range(heads):
@@ -281,12 +283,20 @@
             attended = jnp.concatenate([attended, jnp.concatenate(rests, axis=0)], axis=1)
         gated = (attended * g_ref[j]).astype(BF16)
         total_out = first_ref[j].astype(F32) + dot(gated, aout_ref[...], 0, 0)
-        sum_ref[pl.ds(j, n, stride=16), :] = total_out
-    for s in range(sz.devices):
-        for row in range(sz.rows):
-            out_ref[s * sz.rows + row] = sum_ref[pl.ds(sz.place(s, row) * 16, sz.rows), :].astype(
-                BF16
-            )
+        out_ref[j] = total_out.astype(BF16)
+
+
+def spread(block, devices):
+    pieces, offsets = [block[None]], [[0]]
+    bit = devices // 2
+    while bit:
+        held = jnp.concatenate(pieces, axis=0) if len(pieces) > 1 else pieces[0]
+        got = lax.ppermute(held, AXES, [(d, d ^ bit) for d in range(devices)])
+        known = [o for part in offsets for o in part]
+        pieces.append(got)
+        offsets.append([o ^ bit for o in known])
+        bit //= 2
+    return pieces, offsets
 
 
 def shards(
@@ -298,9 +308,8 @@
     heads = att_bias.shape[1]
     sz = Sizes(rows, crop, devices, ch)
     n, cd = crop, sz.chans
-    first_row = lax.axis_index(AXES) * rows
-    info = jnp.stack([length[0], first_row.astype(jnp.int32)])
-    columns = lax.all_to_all(pair_rep, AXES, split_axis=1, concat_axis=0, tiled=True)
+    me = lax.axis_index(AXES).astype(jnp.int32)
+    info = jnp.stack([length[0], me * rows, me])
 
     def bound(kernel, *extra):
         def run(*refs):
@@ -311,14 +320,17 @@
     shape = jax.ShapeDtypeStruct
     edges = call(
         bound(edges_kernel),
-        shape((devices, 2 * cd, rows * crop), BF16),
+        shape((devices, 2 * cd, (sz.tiles + sz.block_tiles) * LANES), BF16),
         (info, pair_rep, ln_pair[None], tri_in),
-        scratch=[pltpu.VMEM((rows * crop, ch), BF16)],
+        scratch=[
+            pltpu.VMEM((rows * crop, ch), BF16),
+            pltpu.VMEM((devices, sz.block_tiles * 2 * cd, ch), F32),
+        ],
         smem=(0,),
         name="edges",
     )
     edges = lax.all_to_all(edges, AXES, split_axis=0, concat_axis=0, tiled=True)
-    rest_rows = max(n // 2, 8)
+    rest_rows = n if sz.rest else 8
     outer = call(
         bound(outer_kernel),
         shape((devices, sz.fold * cd, rows * crop // sz.fold), BF16),
@@ -337,13 +349,16 @@
         [
             shape((rows, n, ch), BF16),
             shape((rows, n, ch), BF16),
-            shape((rows * heads, n), F32),
-        ],
-        (outer, columns, ln_pair[None], tri_gate, ln_hidden[None], tri_out, ln_att[None], att_bias),
-        scratch=[pltpu.VMEM((n * 16, ch), F32)],
+            shape((rows * heads, n), BF16),
+        ],
+        (outer, edges, ln_pair[None], tri_gate, ln_hidden[None], tri_out, ln_att[None], att_bias),
+        scratch=[
+            pltpu.VMEM((devices * sz.block + 2 * cd, ch), F32),
+            pltpu.VMEM((rows * heads, n), F32),
+        ],
         name="update",
     )
-    bias_all = lax.all_gather(bias.astype(BF16), AXES, axis=0, tiled=False)
+    pieces, steps = spread(bias, devices)
     query, key, value, gate = call(
         bound(project_kernel),
         [
@@ -355,18 +370,18 @@
         (col, att_q, att_k, att_v, att_gate),
         name="project",
     )
-    return call(
-        bound(attend_kernel, heads),
-        shape((n, rows, ch), BF16),
-        (info, query, key, value, gate, first, bias_all, att_out),
+    out = call(
+        bound(attend_kernel, heads, steps),
+        shape((rows, n, ch), BF16),
+        (info, query, key, value, gate, first, att_out, *pieces),
         scratch=[
             pltpu.VMEM((-(-n // LANES), n * heads, LANES), F32),
             pltpu.VMEM((n, heads * n), F32),
-            pltpu.VMEM((n * 16, ch), F32),
         ],
         smem=(0,),
         name="attend",
     )
+    return jnp.swapaxes(out, 0, 1)
 
 
 def solution(mesh):

time: 120 us -> 102 us (0.85)
  waiting for transfers between devices: 55.8 us -> 24.6 us
  blocking collectives: 21.4 us -> 48.8 us
  starting transfers between devices: 20.5 us -> 8.66 us
  local copies, waits for them, and re-layouts: 5.27 us -> 2.82 us
    all_to_all x0 -> x1, blocking collectives: none -> 48.8 us  [shards(): edges = lax.all_to_all(edges, AXES, split_axis=0, concat_axis=0, tiled=True)]
    all_to_all x2 -> x0, waiting for transfers between devices: 40.6 us -> none  [the longest x1 23.8 us: shards(): edges = lax.all_to_all(edges, AXES, split_axis=0, concat_axis=0, tiled=True)]
    all_gather x1 -> x0, blocking collectives: 21.4 us -> none  [shards(): bias_all = lax.all_gather(bias.astype(BF16), AXES, axis=0, tiled=False)]
    all_to_all x2 -> x0, starting transfers between devices: 15 us -> none  [the longest x1 7.53 us: shards(): edges = lax.all_to_all(edges, AXES, split_axis=0, concat_axis=0, tiled=True)]
    ppermute x0 -> x4, waiting for transfers between devices: none -> 9.28 us  [spread(): got = lax.ppermute(held, AXES, [(d, d ^ bit) for d in range(devices)])]
    ppermute x0 -> x4, starting transfers between devices: none -> 4.86 us  [spread(): got = lax.ppermute(held, AXES, [(d, d ^ bit) for d in range(devices)])]
    all_to_all x1, starting transfers between devices: 5.48 us -> 3.8 us  [shards(): outer = lax.all_to_all(outer, AXES, split_axis=0, concat_axis=0, tiled=True)]
    unnamed x32 -> x29, local copies, waits for them, and re-layouts: 4.11 us -> 2.82 us
  transfers between devices with their start and end apart: 3 -> 5, of which waited for: 3 -> 5; matrix products, arithmetic and copies ran while one was open for 1% -> 0% of each run, Pallas kernels for 2% -> 1%
where the time goes in v2:
time: 102 us
  blocking collectives  48.8 us (48%)
  waiting for transfers between devices  24.6 us (24%)
  Pallas kernels  15.7 us (15%)
  starting transfers between devices  8.66 us (8%)
  local copies, waits for them, and re-layouts  2.82 us (3%)
    all_to_all x1, blocking collectives, shards(): edges = lax.all_to_all(edges, AXES, split_axis=0, concat_axis=0, tiled=True)  48.8 us
    pallas_call x5, Pallas kernels, call(): pl.pallas_call(kernel, out_shape=out_shape, in_specs=specs, out_specs=vme...  15.7 us
    all_to_all x1, waiting for transfers between devices, shards(): outer = lax.all_to_all(outer, AXES, split_axis=0, concat_axis=0, tiled=True)  15.3 us
    ppermute x4, waiting for transfers between devices, spread(): got = lax.ppermute(held, AXES, [(d, d ^ bit) for d in range(devices)])  9.28 us
    ppermute x4, starting transfers between devices, spread(): got = lax.ppermute(held, AXES, [(d, d ^ bit) for d in range(devices)])  4.86 us
    all_to_all x1, starting transfers between devices, shards(): outer = lax.all_to_all(outer, AXES, split_axis=0, concat_axis=0, tiled=True)  3.8 us
    unnamed x29, local copies, waits for them, and re-layouts  2.82 us
  transfers between devices with their start and end apart: 5, of which 5 were waited for; matrix products, arithmetic and copies ran while one was open for 0% of the time, Pallas kernels for 1%

profile of v2, /device:TPU:0, one launch (start us, length us, event | category | flops | bytes accessed | tf_op | source)
XLA Modules:
  0.0 101.5 jit_solution(3083543567745478497)
XLA Ops:
  0.7 0.1 pad_add_fusion.refs_0_
  0.7 1.1 %copy-done = bf16[12,192,128]{2,1,0:T(8,128)(2,1)S(1)} copy-done((bf16[12,192,128]{2,1,0:T(8,128)(2,1)S(1)}, bf16[12,192,128]{2,1,0:T(8,128)(2,1)}, u32[]{:S(2)}) %copy-start) | copy-done | bytes 589848
  1.8 0.9 copy-done.1
  2.7 0.7 copy-done.9
  3.4 2.3 %edges.1 = bf16[16,16,3456]{2,1,0:T(8,128)(2,1)S(1)} custom-call(s32[3]{0:T(128)S(1)} %pad_add_fusion.refs_0_, bf16[12,192,128]{2,1,0:T(8,128)(2,1)S(1)} %copy-done, f32[1,128]{1,0:T(1,128)S(1)} %bitcast.12, bf16[4,128,128]{2,1,0:T(8,128)(2,1)S(1)} %copy-done.1), custom_call_target="tpu_custom_call" | custom-call | tf_op jit(solution)/shard_map/edges/pallas_call | solution.py:38
  5.7 48.8 %all_to_all.10.refs_0_.refs_1_ = bf16[16,16,3456]{2,1,0:T(8,128)(2,1)S(1)} all-to-all(bf16[16,16,3456]{2,1,0:T(8,128)(2,1)S(1)} %edges.1), channel_id=1, replica_groups=mesh['grp'=2,'row'=8,'node'=2] {'row','node'}, dimensions={0} | all-to-all | bytes 3538944 | tf_op jit(solution)/shard_map/all_to_all | solution.py:332
  54.5 0.0 copy-start.11
  54.5 0.0 copy-start.12
  54.5 2.2 %outer.1 = bf16[16,16,1152]{2,1,0:T(8,128)(2,1)} custom-call(bf16[16,16,3456]{2,1,0:T(8,128)(2,1)S(1)} %all_to_all.10.refs_0_.refs_1_), custom_call_target="tpu_custom_call" | custom-call | tf_op jit(solution)/shard_map/outer/pallas_call | solution.py:38
  56.7 3.8 %all-to-all-start.1 = ((bf16[16,16,1152]{2,1,0:T(8,128)(2,1)}), bf16[16,16,1152]{2,1,0:T(8,128)(2,1)S(1)}, u32[]{:S(2)}, u32[]{:S(2)}) async-start(bf16[16,16,1152]{2,1,0:T(8,128)(2,1)} %outer.1), calls=%async_computation.1 | async-start | bytes 1179648 | tf_op jit(solution)/shard_map/all_to_all | solution.py:346
  60.5 0.0 copy-done.13
  60.5 0.0 copy-start.5
  60.6 0.0 copy-start.6
  60.6 0.0 copy-start.7
  60.6 0.0 copy-start.8
  60.6 0.1 copy.15.refs_7_
  60.7 15.3 %all-to-all-done.1.refs_0_ = bf16[16,16,1152]{2,1,0:T(8,128)(2,1)S(1)} async-done(((bf16[16,16,1152]{2,1,0:T(8,128)(2,1)}), bf16[16,16,1152]{2,1,0:T(8,128)(2,1)S(1)}, u32[]{:S(2)}, u32[]{:S(2)}) %all-to-all-start.1) | async-done | bytes 589856 | tf_op jit(solution)/shard_map/all_to_all | solution.py:346
  76.0 0.0 copy-done.2
  76.0 0.0 copy-done.11
  76.0 0.0 copy-done.12
  76.1 0.0 copy-start.4
  76.1 3.2 %update.1 = (bf16[12,192,128]{2,1,0:T(8,128)(2,1)S(1)}, bf16[12,192,128]{2,1,0:T(8,128)(2,1)S(1)}, bf16[48,192]{1,0:T(8,128)(2,1)S(1)}) custom-call(bf16[16,16,1152]{2,1,0:T(8,128)(2,1)S(1)} %all-to-all-done.1.refs_0_, bf16[16,16,3456]{2,1,0:T(8,128)(2,1)S(1)} %all_to_all.10.refs_0_.refs_1_, f32[1,128]{1,0:T(1,128)S(1)} %bitcast.13, ...), custom_call_target="tpu_custom_call" | custom-call | tf_op jit(solution)/shard_map/update/pallas_call | solution.py:38
  79.3 2.6 %collective-permute-start = (bf16[1,48,192]{2,1,0:T(8,128)(2,1)S(1)}, bf16[1,48,192]{2,1,0:T(8,128)(2,1)S(1)}, u32[]{:S(2)}, u32[]{:S(2)}) collective-permute-start(bf16[1,48,192]{2,1,0:T(8,128)(2,1)S(1)} %bitcast.7), channel_id=1, source_target_pairs={{0,8},{1,9},{2,10},{3,11},{4,12},{5,13},{6,14},{7,15},{8,0},{9,1},... | collective-permute-start | bytes 55304 | tf_op jit(solution)/shard_map/ppermute | solution.py:294
  81.9 2.1 %collective-permute-done.refs_8_ = bf16[1,48,192]{2,1,0:T(8,128)(2,1)S(1)} collective-permute-done((bf16[1,48,192]{2,1,0:T(8,128)(2,1)S(1)}, bf16[1,48,192]{2,1,0:T(8,128)(2,1)S(1)}, u32[]{:S(2)}, u32[]{:S(2)}) %collective-permute-start) | collective-permute-done | bytes 18464 | tf_op jit(solution)/shard_map/ppermute | solution.py:294
  84.0 1.4 %collective-permute-start.1 = (bf16[2,48,192]{2,1,0:T(8,128)(2,1)S(1)}, bf16[2,48,192]{2,1,0:T(8,128)(2,1)S(1)}, u32[]{:S(2)}, u32[]{:S(2)}) collective-permute-start(bf16[2,48,192]{2,1,0:T(8,128)(2,1)S(1)} %pad_maximum_fusion.2), channel_id=1, source_target_pairs={{0,4},{1,5},{2,6},{3,7},{4,0},{5,1},{6,2},{7,3},{8,12},{9,13},{10,... | collective-permute-start | bytes 110600 | tf_op jit(solution)/shard_map/ppermute | solution.py:294
  85.5 2.7 %collective-permute-done.1.refs_9_ = bf16[2,48,192]{2,1,0:T(8,128)(2,1)S(1)} collective-permute-done((bf16[2,48,192]{2,1,0:T(8,128)(2,1)S(1)}, bf16[2,48,192]{2,1,0:T(8,128)(2,1)S(1)}, u32[]{:S(2)}, u32[]{:S(2)}) %collective-permute-start.1) | collective-permute-done | bytes 36896 | tf_op jit(solution)/shard_map/ppermute | solution.py:294
  88.2 0.8 collective-permute-start.2
  89.0 3.9 %collective-permute-done.2.refs_10_ = bf16[4,48,192]{2,1,0:T(8,128)(2,1)S(1)} collective-permute-done((bf16[4,48,192]{2,1,0:T(8,128)(2,1)S(1)}, bf16[4,48,192]{2,1,0:T(8,128)(2,1)S(1)}, u32[]{:S(2)}, u32[]{:S(2)}) %collective-permute-start.2) | collective-permute-done | bytes 73760 | tf_op jit(solution)/shard_map/ppermute | solution.py:294
  92.9 0.1 collective-permute-start.3
  93.1 0.9 project.1
  94.0 0.5 collective-permute-done.3.refs_11_
  94.5 7.1 %attend.1 = bf16[12,192,128]{2,1,0:T(8,128)(2,1)} custom-call(s32[3]{0:T(128)S(1)} %pad_add_fusion.refs_0_, bf16[12,192,128]{2,1,0:T(8,128)(2,1)S(1)} %get-tuple-element.13.refs_1_, bf16[12,192,128]{2,1,0:T(8,128)(2,1)S(1)} %get-tuple-element.14.refs_2_, bf16[12,128,192]{2,1,0:T(8,128)(2,1)S(1)} %get-tuple-element.15.refs_3_, ...), custom_call_target="tpu_custom_call" | custom-call | tf_op jit(solution)/shard_map/attend/pallas_call | solution.py:38
  (17 shorter events, 0.1 us)
Async XLA Ops:
  0.7 1.1 %copy-start = (bf16[12,192,128]{2,1,0:T(8,128)(2,1)S(1)}, bf16[12,192,128]{2,1,0:T(8,128)(2,1)}, u32[]{:S(2)}) copy-start(bf16[12,192,128]{2,1,0:T(8,128)(2,1)} %refs_1_.2) | copy-start | bytes 1769476
  1.8 0.9 copy-start.1
  2.7 0.7 copy-start.9
  54.5 6.1 %copy-start.13 = (bf16[128,4]{0,1:T(4,128)(2,1)S(1)}, bf16[128,4]{0,1:T(4,128)(2,1)}, u32[]{:S(2)}) copy-start(bf16[128,4]{0,1:T(4,128)(2,1)} %param.25) | copy-start | bytes 3076
  54.5 21.5 %copy-start.2 = (bf16[128,128]{1,0:T(8,128)(2,1)S(1)}, bf16[128,128]{1,0:T(8,128)(2,1)}, u32[]{:S(2)}) copy-start(bf16[128,128]{1,0:T(8,128)(2,1)} %refs_3_.4) | copy-start | bytes 98308
  54.5 21.5 %copy-start.3 = (bf16[128,128]{1,0:T(8,128)(2,1)S(1)}, bf16[128,128]{1,0:T(8,128)(2,1)}, u32[]{:S(2)}) copy-start(bf16[128,128]{1,0:T(8,128)(2,1)} %refs_5_.1) | copy-start | bytes 98308
  54.5 21.5 %copy-start.10 = (f32[128]{0:T(128)S(1)}, f32[128]{0:T(128)}, u32[]{:S(2)}) copy-start(f32[128]{0:T(128)} %param.16) | copy-start | bytes 1540
  54.5 21.6 %copy-start.11 = (f32[128]{0:T(128)S(1)}, f32[128]{0:T(128)}, u32[]{:S(2)}) copy-start(f32[128]{0:T(128)} %param.19) | copy-start | bytes 1540
  54.5 21.5 %copy-start.12 = (f32[128]{0:T(128)S(1)}, f32[128]{0:T(128)}, u32[]{:S(2)}) copy-start(f32[128]{0:T(128)} %param.21) | copy-start | bytes 1540
  56.7 19.3 %all-to-all-start.1 = ((bf16[16,16,1152]{2,1,0:T(8,128)(2,1)}), bf16[16,16,1152]{2,1,0:T(8,128)(2,1)S(1)}, u32[]{:S(2)}, u32[]{:S(2)}) async-start(bf16[16,16,1152]{2,1,0:T(8,128)(2,1)} %outer.1), calls=%async_computation.1 | async-start | bytes 1179648 | tf_op jit(solution)/shard_map/all_to_all | solution.py:346
  60.5 32.5 %copy-start.5 = (bf16[128,128]{1,0:T(8,128)(2,1)S(1)}, bf16[128,128]{1,0:T(8,128)(2,1)}, u32[]{:S(2)}) copy-start(bf16[128,128]{1,0:T(8,128)(2,1)} %refs_1_.3) | copy-start | bytes 98308
  60.6 32.5 %copy-start.6 = (bf16[128,128]{1,0:T(8,128)(2,1)S(1)}, bf16[128,128]{1,0:T(8,128)(2,1)}, u32[]{:S(2)}) copy-start(bf16[128,128]{1,0:T(8,128)(2,1)} %refs_2_.1) | copy-start | bytes 98308
  60.6 32.5 %copy-start.7 = (bf16[128,128]{1,0:T(8,128)(2,1)S(1)}, bf16[128,128]{1,0:T(8,128)(2,1)}, u32[]{:S(2)}) copy-start(bf16[128,128]{1,0:T(8,128)(2,1)} %refs_3_.5) | copy-start | bytes 98308
  60.6 32.5 %copy-start.8 = (bf16[128,128]{1,0:T(8,128)(2,1)S(1)}, bf16[128,128]{1,0:T(8,128)(2,1)}, u32[]{:S(2)}) copy-start(bf16[128,128]{1,0:T(8,128)(2,1)} %refs_4_.1) | copy-start | bytes 98308
  76.1 18.4 %copy-start.4 = (bf16[128,128]{1,0:T(8,128)(2,1)S(1)}, bf16[128,128]{1,0:T(8,128)(2,1)}, u32[]{:S(2)}) copy-start(bf16[128,128]{1,0:T(8,128)(2,1)} %refs_6_.1) | copy-start | bytes 98308
  79.3 4.7 %collective-permute-start = (bf16[1,48,192]{2,1,0:T(8,128)(2,1)S(1)}, bf16[1,48,192]{2,1,0:T(8,128)(2,1)S(1)}, u32[]{:S(2)}, u32[]{:S(2)}) collective-permute-start(bf16[1,48,192]{2,1,0:T(8,128)(2,1)S(1)} %bitcast.7), channel_id=1, source_target_pairs={{0,8},{1,9},{2,10},{3,11},{4,12},{5,13},{6,14},{7,15},{8,0},{9,1},... | collective-permute-start | bytes 55304 | tf_op jit(solution)/shard_map/ppermute | solution.py:294
  84.0 4.2 %collective-permute-start.1 = (bf16[2,48,192]{2,1,0:T(8,128)(2,1)S(1)}, bf16[2,48,192]{2,1,0:T(8,128)(2,1)S(1)}, u32[]{:S(2)}, u32[]{:S(2)}) collective-permute-start(bf16[2,48,192]{2,1,0:T(8,128)(2,1)S(1)} %pad_maximum_fusion.2), channel_id=1, source_target_pairs={{0,4},{1,5},{2,6},{3,7},{4,0},{5,1},{6,2},{7,3},{8,12},{9,13},{10,... | collective-permute-start | bytes 110600 | tf_op jit(solution)/shard_map/ppermute | solution.py:294
  88.2 4.7 %collective-permute-start.2 = (bf16[4,48,192]{2,1,0:T(8,128)(2,1)S(1)}, bf16[4,48,192]{2,1,0:T(8,128)(2,1)S(1)}, u32[]{:S(2)}, u32[]{:S(2)}) collective-permute-start(bf16[4,48,192]{2,1,0:T(8,128)(2,1)S(1)} %pad_maximum_fusion.1), channel_id=1, source_target_pairs={{0,2},{1,3},{2,0},{3,1},{4,6},{5,7},{6,4},{7,5},{8,10},{9,11},{10,... | collective-permute-start | bytes 221192 | tf_op jit(solution)/shard_map/ppermute | solution.py:294
  92.9 1.5 %collective-permute-start.3 = (bf16[8,48,192]{2,1,0:T(8,128)(2,1)S(1)}, bf16[8,48,192]{2,1,0:T(8,128)(2,1)S(1)}, u32[]{:S(2)}, u32[]{:S(2)}) collective-permute-start(bf16[8,48,192]{2,1,0:T(8,128)(2,1)S(1)} %pad_maximum_fusion), channel_id=1, source_target_pairs={{0,1},{1,0},{2,3},{3,2},{4,5},{5,4},{6,7},{7,6},{8,9},{9,8},{10,11... | collective-permute-start | bytes 442376 | tf_op jit(solution)/shard_map/ppermute | solution.py:294

commit v3 on v2

--- a/solution.py
+++ b/solution.py
@@ -48,32 +48,30 @@
 
 class Sizes:
     def __init__(self, rows, crop, devices, channels):
-        self.rows, self.crop, self.devices = rows, crop, devices
+        self.rows, self.crop, self.devices, self.channels = rows, crop, devices, channels
         self.half = rows // 2
+        self.group = devices // 2
+        self.columns = rows * self.group
         self.whole = crop // LANES
         self.rest = crop % LANES
         self.tiles = rows * crop // LANES
-        self.chans = channels // devices
-        self.fold = max(1, 16 // self.chans)
-        while self.tiles % self.fold:
-            self.fold //= 2
-        self.fold_tiles = self.tiles // self.fold
-        self.channels = channels
-
+        self.chans = channels // self.group
         self.block = rows * rows
-        self.block_tiles = -(-self.block // (2 * self.chans))
-
-
-def edges_kernel(sz, len_ref, x_ref, ln_ref, w_ref, out_ref, norm_ref, pair_ref):
-    length, first = len_ref[0], len_ref[1]
-    cd, two = sz.chans, 2 * sz.chans
-    ch = sz.channels
-    r = lax.broadcasted_iota(jnp.int32, (2 * ch, 2 * ch), 0)
-    e = lax.broadcasted_iota(jnp.int32, (2 * ch, 2 * ch), 1)
-    target = ((r // cd) % 2) * ch + (r // two) * cd + r % cd
-    pick = (target == e).astype(BF16)
-    gate_w = dot(pick, jnp.concatenate([w_ref[0], w_ref[2]], axis=1), 1, 1).astype(BF16)
-    value_w = dot(pick, jnp.concatenate([w_ref[1], w_ref[3]], axis=1), 1, 1).astype(BF16)
+        self.block_tiles = -(-self.block // self.chans)
+
+
+def edges_kernel(sz, len_ref, x_ref, ln_ref, w_ref, *refs):
+    near, far, pair = refs[: sz.group], refs[sz.group : 2 * sz.group], refs[2 * sz.group : -2]
+    norm_ref, pair_ref = refs[-2:]
+    length, first, me = len_ref[0], len_ref[1], len_ref[2]
+    cd, ch = sz.chans, sz.channels
+    mine = me & (sz.group - 1)
+    r = lax.broadcasted_iota(jnp.int32, (ch, ch), 0)
+    e = lax.broadcasted_iota(jnp.int32, (ch, ch), 1)
+    pick = (((r // cd) ^ mine) * cd + r % cd == e).astype(BF16)
+    weights = [dot(pick, w_ref[p], 1, 1).astype(BF16) for p in range(4)]
+    gate_w = jnp.concatenate([weights[0], weights[2]], axis=0)
+    value_w = jnp.concatenate([weights[1], weights[3]], axis=0)
     gain = ln_ref[...]
     main = sz.whole * LANES
     for row in range(sz.rows):
@@ -85,10 +83,14 @@
         if sz.rest:
             h, q = divmod(row, sz.half)
             norm_ref[pl.ds(sz.rows * main + q * LANES + h * sz.rest, sz.rest), :] = normed[main:]
-    for d in range(sz.devices):
+    for r in range(sz.group):
         for t in range(sz.block_tiles):
-            at = (sz.tiles + t) * LANES
-            out_ref[d, :, at : at + LANES] = pair_ref[d, t * two : (t + 1) * two, :].astype(BF16)
+            at = (2 * sz.tiles + t) * LANES
+            rows = slice(t * cd, (t + 1) * cd)
+            near[r][:, at : at + LANES] = pair_ref[me ^ r, rows, :].astype(BF16)
+            pair[r][:, t * LANES : (t + 1) * LANES] = pair_ref[me ^ (sz.group + r), rows, :].astype(
+                BF16
+            )
     lane = lax.broadcasted_iota(jnp.int32, (1, LANES), 1)
 
     def live(tile):
@@ -106,72 +108,96 @@
         n = norm_ref[pl.ds(tile * LANES, step * LANES), :]
         mask = jnp.concatenate([live(tile + s) for s in range(step)], axis=1)
         edge = sigmoid(dot(gate_w, n, 1, 1)) * dot(value_w, n, 1, 1) * mask
-        out_ref[:, :, tile * LANES : (tile + step) * LANES] = edge.reshape(
-            sz.devices, two, step * LANES
-        ).astype(BF16)
-
-
-def outer_kernel(sz, e_ref, out_ref, main_ref, rest_ref, omain_ref, orest_ref):
-    cd, two = sz.chans, 2 * sz.chans
-    n, w, half = sz.crop, sz.whole, sz.half
-    for s in range(sz.devices):
+        edge = edge.astype(BF16)
+        to = slice(tile * LANES, (tile + step) * LANES)
+        right_to = slice((sz.tiles + tile) * LANES, (sz.tiles + tile + step) * LANES)
+        for r in range(sz.group):
+            left = edge[r * cd : (r + 1) * cd]
+            near[r][:, to] = left
+            far[r][:, to] = left
+            near[r][:, right_to] = edge[ch + r * cd : ch + (r + 1) * cd]
+
+
+def outer_kernel(sz, len_ref, *refs):
+    near, far = refs[: sz.group], refs[sz.group : 2 * sz.group]
+    outs = refs[2 * sz.group : 3 * sz.group]
+    lmain_ref, lrest_ref, rmain_ref, rrest_ref, omain_ref, orest_ref = refs[3 * sz.group :]
+    me = len_ref[2]
+    mine = me & (sz.group - 1)
+    cd, n, w, half = sz.chans, sz.crop, sz.whole, sz.half
+
+    def unpack(ref, base, owner, main_ref, rest_ref):
         for tile in range(sz.tiles):
-            block = e_ref[s, :, tile * LANES : (tile + 1) * LANES].astype(F32)
+            at = (base + tile) * LANES
+            block = ref[:, at : at + LANES].astype(F32)
             if tile < sz.rows * w:
                 row, m = divmod(tile, w)
-                main_ref[m, pl.ds((s * sz.rows + row) * two, two), :] = block
+                main_ref[m, pl.ds(pl.multiple_of((owner * sz.rows + row) * cd, 8), cd), :] = block
             else:
-                at = s * sz.rows + tile - sz.rows * w
-                rest_ref[pl.ds(at * two, two), :] = block
-                rest_ref[pl.ds((at + half) * two, two), :] = pltpu.roll(block, sz.rest, 1)
-
-    def matrix(index):
-        parts = [main_ref[m, pl.ds(index, n, stride=two), :].astype(BF16) for m in range(w)]
-        if sz.rest:
-            parts.append(rest_ref[pl.ds(index, n, stride=two), :].astype(BF16)[:, : sz.rest])
+                row = owner * sz.rows + tile - sz.rows * w
+                rest_ref[pl.ds(pl.multiple_of(row * cd, 8), cd), :] = block
+                rest_ref[pl.ds(pl.multiple_of((row + half) * cd, 8), cd), :] = pltpu.roll(
+                    block, sz.rest, 1
+                )
+
+    for r in range(sz.group):
+        unpack(near[r], 0, me ^ r, lmain_ref, lrest_ref)
+        unpack(near[r], sz.tiles, mine ^ r, rmain_ref, rrest_ref)
+        unpack(far[r], 0, me ^ (sz.group + r), lmain_ref, lrest_ref)
+
+    def matrix(c, size, main_ref, rest_ref):
+        parts = [main_ref[m, pl.ds(c, size, stride=cd), :].astype(BF16) for m in range(w)]
+        if sz.rest:
+            parts.append(rest_ref[pl.ds(c, size, stride=cd), :].astype(BF16)[:, : sz.rest])
         return jnp.concatenate(parts, axis=1) if len(parts) > 1 else parts[0]
 
     for c in range(cd):
-        outer = dot(matrix(cd + c), matrix(c), 1, 1)
+        outer = dot(
+            matrix(c, sz.columns, rmain_ref, rrest_ref), matrix(c, n, lmain_ref, lrest_ref), 1, 1
+        )
         for m in range(w):
-            omain_ref[m, pl.ds(c, n, stride=cd), :] = outer[:, m * LANES : (m + 1) * LANES]
+            omain_ref[m, pl.ds(c, sz.columns, stride=cd), :] = outer[:, m * LANES : (m + 1) * LANES]
         if sz.rest:
             part = outer[:, w * LANES :]
-            orest_ref[pl.ds(c, n, stride=cd), :] = jnp.concatenate([part, part], axis=1)
+            orest_ref[pl.ds(c, sz.columns, stride=cd), :] = jnp.concatenate([part, part], axis=1)
     low = lax.broadcasted_iota(jnp.int32, (cd, LANES), 1) < sz.rest
-    for s in range(sz.devices):
-        for t in range(sz.fold_tiles):
-            blocks = []
-            for f in range(sz.fold):
-                tile = f * sz.fold_tiles + t
-                if tile < sz.rows * w:
-                    row, m = divmod(tile, w)
-                    blocks.append(omain_ref[m, pl.ds((s * sz.rows + row) * cd, cd), :])
-                else:
-                    at = s * sz.rows + tile - sz.rows * w
-                    one = orest_ref[pl.ds(at * cd, cd), :]
-                    blocks.append(jnp.where(low, one, orest_ref[pl.ds((at + half) * cd, cd), :]))
-            block = jnp.concatenate(blocks, axis=0) if len(blocks) > 1 else blocks[0]
-            out_ref[s, :, t * LANES : (t + 1) * LANES] = block.astype(BF16)
-
-
-def update_kernel(
-    sz, o_ref, x_ref, lnp_ref, gate_ref, lnh_ref, tri_ref, lna_ref, biasw_ref,
-    first_ref, col_ref, bias_ref, cols_ref, brow_ref,
-):
-    n, w, half, ch = sz.crop, sz.whole, sz.half, sz.channels
-    two = 2 * sz.chans
-    for s in range(sz.devices):
-        for t in range(sz.block_tiles):
-            at = (sz.tiles + t) * LANES
-            cols_ref[pl.ds(s * sz.block + t * two, two), :] = x_ref[s, :, at : at + LANES].astype(F32)
+    for r in range(sz.group):
+        start = (mine ^ r) * sz.rows
+        for tile in range(sz.tiles):
+            if tile < sz.rows * w:
+                row, m = divmod(tile, w)
+                block = omain_ref[m, pl.ds(pl.multiple_of((start + row) * cd, 8), cd), :]
+            else:
+                at = start + tile - sz.rows * w
+                block = jnp.where(
+                    low,
+                    orest_ref[pl.ds(pl.multiple_of(at * cd, 8), cd), :],
+                    orest_ref[pl.ds(pl.multiple_of((at + half) * cd, 8), cd), :],
+                )
+            outs[r][:, tile * LANES : (tile + 1) * LANES] = block.astype(BF16)
+
+
+def update_kernel(sz, len_ref, lnp_ref, gate_ref, lnh_ref, tri_ref, lna_ref, biasw_ref, *refs):
+    sums, near, pair = refs[: sz.group], refs[sz.group : 2 * sz.group], refs[2 * sz.group : -6]
+    first_ref, col_ref, bias_ref, cols_ref, brow_ref, sums_ref = refs[-6:]
+    n, w, half, ch, cd = sz.crop, sz.whole, sz.half, sz.channels, sz.chans
+    me = len_ref[2]
+    mine = me & (sz.group - 1)
+    for r in range(sz.group):
+        sums_ref[pl.ds(pl.multiple_of((mine ^ r) * cd, 8), cd), :] = sums[r][...].astype(F32)
+        for ref, base, owner in (
+            (near[r], 2 * sz.tiles, me ^ r),
+            (pair[r], 0, me ^ (sz.group + r)),
+        ):
+            for t in range(sz.block_tiles):
+                at = (base + t) * LANES
+                row = pl.multiple_of(owner * sz.block + t * cd, 8)
+                cols_ref[pl.ds(row, cd), :] = ref[:, at : at + LANES].astype(F32)
     gain_h = jnp.transpose(jnp.broadcast_to(lnh_ref[...], (ch, ch)))
     tri = tri_ref[...]
 
     def update(tile):
-        f, t = divmod(tile, sz.fold_tiles)
-        block = o_ref[:, :, t * LANES : (t + 1) * LANES].astype(F32)
-        block = block[:, f * sz.chans : (f + 1) * sz.chans, :].reshape(ch, LANES)
+        block = sums_ref[:, tile * LANES : (tile + 1) * LANES]
         average = jnp.mean(block, axis=0, keepdims=True)
         centred = block - average
         variance = jnp.mean(centred * centred, axis=0, keepdims=True)
@@ -318,32 +344,51 @@
         return run
 
     shape = jax.ShapeDtypeStruct
-    edges = call(
+    g, t, bt = sz.group, sz.tiles, sz.block_tiles
+
+    def slab(tiles):
+        return shape((cd, tiles * LANES), BF16)
+
+    def send(blocks, offset):
+        return [
+            block
+            if not (offset ^ r)
+            else lax.ppermute(block, AXES, [(d, d ^ offset ^ r) for d in range(devices)])
+            for r, block in enumerate(blocks)
+        ]
+
+    made = call(
         bound(edges_kernel),
-        shape((devices, 2 * cd, (sz.tiles + sz.block_tiles) * LANES), BF16),
+        [slab(2 * t + bt)] * g + [slab(t)] * g + [slab(bt)] * g,
         (info, pair_rep, ln_pair[None], tri_in),
         scratch=[
             pltpu.VMEM((rows * crop, ch), BF16),
-            pltpu.VMEM((devices, sz.block_tiles * 2 * cd, ch), F32),
+            pltpu.VMEM((devices, bt * cd, ch), F32),
         ],
         smem=(0,),
         name="edges",
     )
-    edges = lax.all_to_all(edges, AXES, split_axis=0, concat_axis=0, tiled=True)
-    rest_rows = n if sz.rest else 8
+    far = send(made[g : 2 * g], g)
+    near = send(made[:g], 0)
+    late, far, near = lax.optimization_barrier((made[2 * g :], far, near))
+    pair = send(late, g)
+    rest = sz.rest > 0
     outer = call(
         bound(outer_kernel),
-        shape((devices, sz.fold * cd, rows * crop // sz.fold), BF16),
-        (edges,),
+        [slab(t)] * g,
+        (info, *near, *far),
         scratch=[
-            pltpu.VMEM((sz.whole, n * 2 * cd, LANES), F32),
-            pltpu.VMEM((rest_rows * 2 * cd, LANES), F32),
             pltpu.VMEM((sz.whole, n * cd, LANES), F32),
-            pltpu.VMEM((rest_rows * cd, LANES), F32),
-        ],
+            pltpu.VMEM((n * cd if rest else 8, LANES), F32),
+            pltpu.VMEM((sz.whole, sz.columns * cd, LANES), F32),
+            pltpu.VMEM((sz.columns * cd if rest else 8, LANES), F32),
+            pltpu.VMEM((sz.whole, sz.columns * cd, LANES), F32),
+            pltpu.VMEM((sz.columns * cd if rest else 8, LANES), F32),
+        ],
+        smem=(0,),
         name="outer",
     )
-    outer = lax.all_to_all(outer, AXES, split_axis=0, concat_axis=0, tiled=True)
+    sums = send(outer, 0)
     first, col, bias = call(
         bound(update_kernel),
         [
@@ -351,11 +396,16 @@
             shape((rows, n, ch), BF16),
             shape((rows * heads, n), BF16),
         ],
-        (outer, edges, ln_pair[None], tri_gate, ln_hidden[None], tri_out, ln_att[None], att_bias),
+        (
+            info, ln_pair[None], tri_gate, ln_hidden[None], tri_out, ln_att[None], att_bias,
+            *sums, *near, *pair,
+        ),
         scratch=[
-            pltpu.VMEM((devices * sz.block + 2 * cd, ch), F32),
+            pltpu.VMEM((devices * sz.block + cd, ch), F32),
             pltpu.VMEM((rows * heads, n), F32),
-        ],
+            pltpu.VMEM((ch, rows * n), F32),
+        ],
+        smem=(0,),
         name="update",
     )
     pieces, steps = spread(bias, devices)

time: 102 us -> 110 us (1.078)
  blocking collectives: 48.8 us -> 0 us
  starting transfers between devices: 8.66 us -> 49.7 us
  waiting for transfers between devices: 24.6 us -> 39.5 us
  Pallas kernels: 15.7 us -> 17.1 us
    all_to_all x1 -> x0, blocking collectives: 48.8 us -> none  [shards(): edges = lax.all_to_all(edges, AXES, split_axis=0, concat_axis=0, tiled=True)]
    ppermute x0 -> x30, starting transfers between devices: none -> 48.2 us  [send(): lax.ppermute(block, AXES, [(d, d ^ offset ^ r) for d in range(devices)])]
    ppermute x0 -> x30, waiting for transfers between devices: none -> 26.9 us  [send(): lax.ppermute(block, AXES, [(d, d ^ offset ^ r) for d in range(devices)])]
    all_to_all x1 -> x0, waiting for transfers between devices: 15.3 us -> none  [shards(): outer = lax.all_to_all(outer, AXES, split_axis=0, concat_axis=0, tiled=True)]
    all_to_all x1 -> x0, starting transfers between devices: 3.8 us -> none  [shards(): outer = lax.all_to_all(outer, AXES, split_axis=0, concat_axis=0, tiled=True)]
    ppermute x4, starting transfers between devices: 4.86 us -> 1.52 us  [spread(): got = lax.ppermute(held, AXES, [(d, d ^ bit) for d in range(devices)])]
    ppermute x4, waiting for transfers between devices: 9.28 us -> 12.6 us  [spread(): got = lax.ppermute(held, AXES, [(d, d ^ bit) for d in range(devices)])]
    pallas_call x5, Pallas kernels: 15.7 us -> 17.1 us  [call(): pl.pallas_call(kernel, out_shape=out_shape, in_specs=specs, out_specs=vme...]
  transfers between devices with their start and end apart: 5 -> 34, of which waited for: 5 -> 15; matrix products, arithmetic and copies ran while one was open for 0% -> 0% of each run, Pallas kernels for 1% -> 3%
where the time goes in v3:
time: 110 us
  starting transfers between devices  49.7 us (45%)
  waiting for transfers between devices  39.5 us (36%)
  Pallas kernels  17.1 us (16%)
  local copies, waits for them, and re-layouts  2.81 us (3%)
    ppermute x30, starting transfers between devices, send(): lax.ppermute(block, AXES, [(d, d ^ offset ^ r) for d in range(devices)])  48.2 us
    ppermute x30, waiting for transfers between devices, send(): lax.ppermute(block, AXES, [(d, d ^ offset ^ r) for d in range(devices)])  26.9 us
    pallas_call x5, Pallas kernels, call(): pl.pallas_call(kernel, out_shape=out_shape, in_specs=specs, out_specs=vme...  17.1 us
    ppermute x4, waiting for transfers between devices, spread(): got = lax.ppermute(held, AXES, [(d, d ^ bit) for d in range(devices)])  12.6 us
    unnamed x29, local copies, waits for them, and re-layouts  2.81 us
  transfers between devices with their start and end apart: 34, of which 15 were waited for; matrix products, arithmetic and copies ran while one was open for 0% of the time, Pallas kernels for 3%

profile of v3, /device:TPU:0, one launch (start us, length us, event | category | flops | bytes accessed | tf_op | source)
XLA Modules:
  0.0 110.2 jit_solution(1122281488930456739)
XLA Ops:
  3.4 2.3 %edges.1 = (bf16[16,5760]{1,0:T(8,128)(2,1)S(1)}, bf16[16,5760]{1,0:T(8,128)(2,1)S(1)}, bf16[16,5760]{1,0:T(8,128)(2,1)S(1)}, bf16[16,5760]{1,0:T(8,128)(2,1)S(1...) custom-call(s32[3]{0:T(128)S(1)} %pad_add_fusion.refs_0_, ...), custom_call_target="tpu_custom_call" | custom-call | tf_op jit(solution)/shard_map/edges/pallas_call | solution.py:38
  5.7 4.1 %collective-permute-start = (bf16[16,2304]{1,0:T(8,128)(2,1)S(1)}, bf16[16,2304]{1,0:T(8,128)(2,1)S(1)}, u32[]{:S(2)}, u32[]{:S(2)}) collective-permute-start(bf16[16,2304]{1,0:T(8,128)(2,1)S(1)} %get-tuple-element.76), channel_id=1, source_target_pairs={{0,8},{1,9},{2,10},{3,11},{4,12},{5,13},{6,14},{7,15},{8,0},{9,1},... | collective-permute-start | bytes 221192 | tf_op jit(solution)/shard_map/ppermute | solution.py:356
  10.0 1.8 %collective-permute-start.9 = (bf16[16,5760]{1,0:T(8,128)(2,1)S(1)}, bf16[16,5760]{1,0:T(8,128)(2,1)S(1)}, u32[]{:S(2)}, u32[]{:S(2)}) collective-permute-start(bf16[16,5760]{1,0:T(8,128)(2,1)S(1)} %get-tuple-element.86), channel_id=1, source_target_pairs={{0,2},{1,3},{2,0},{3,1},{4,6},{5,7},{6,4},{7,5},{8,10},{9,11},{10,... | collective-permute-start | bytes 552968 | tf_op jit(solution)/shard_map/ppermute | solution.py:356
  11.8 2.5 %collective-permute-start.2 = (bf16[16,2304]{1,0:T(8,128)(2,1)S(1)}, bf16[16,2304]{1,0:T(8,128)(2,1)S(1)}, u32[]{:S(2)}, u32[]{:S(2)}) collective-permute-start(bf16[16,2304]{1,0:T(8,128)(2,1)S(1)} %get-tuple-element.78), channel_id=1, source_target_pairs={{0,10},{1,11},{2,8},{3,9},{4,14},{5,15},{6,12},{7,13},{8,2},{9,3},... | collective-permute-start | bytes 221192 | tf_op jit(solution)/shard_map/ppermute | solution.py:356
  14.7 3.8 %collective-permute-done.1.refs_10_ = bf16[16,2304]{1,0:T(8,128)(2,1)S(1)} collective-permute-done((bf16[16,2304]{1,0:T(8,128)(2,1)S(1)}, bf16[16,2304]{1,0:T(8,128)(2,1)S(1)}, u32[]{:S(2)}, u32[]{:S(2)}) %collective-permute-start.1) | collective-permute-done | bytes 73760 | tf_op jit(solution)/shard_map/ppermute | solution.py:356
  18.5 4.9 %collective-permute-start.4 = (bf16[16,2304]{1,0:T(8,128)(2,1)S(1)}, bf16[16,2304]{1,0:T(8,128)(2,1)S(1)}, u32[]{:S(2)}, u32[]{:S(2)}) collective-permute-start(bf16[16,2304]{1,0:T(8,128)(2,1)S(1)} %get-tuple-element.80), channel_id=1, source_target_pairs={{0,12},{1,13},{2,14},{3,15},{4,8},{5,9},{6,10},{7,11},{8,4},{9,5},... | collective-permute-start | bytes 221192 | tf_op jit(solution)/shard_map/ppermute | solution.py:356
  23.4 2.2 %collective-permute-start.5 = (bf16[16,2304]{1,0:T(8,128)(2,1)S(1)}, bf16[16,2304]{1,0:T(8,128)(2,1)S(1)}, u32[]{:S(2)}, u32[]{:S(2)}) collective-permute-start(bf16[16,2304]{1,0:T(8,128)(2,1)S(1)} %get-tuple-element.81), channel_id=1, source_target_pairs={{0,13},{1,12},{2,15},{3,14},{4,9},{5,8},{6,11},{7,10},{8,5},{9,4},... | collective-permute-start | bytes 221192 | tf_op jit(solution)/shard_map/ppermute | solution.py:356
  25.7 2.2 %collective-permute-start.6 = (bf16[16,2304]{1,0:T(8,128)(2,1)S(1)}, bf16[16,2304]{1,0:T(8,128)(2,1)S(1)}, u32[]{:S(2)}, u32[]{:S(2)}) collective-permute-start(bf16[16,2304]{1,0:T(8,128)(2,1)S(1)} %get-tuple-element.82), channel_id=1, source_target_pairs={{0,14},{1,15},{2,12},{3,13},{4,10},{5,11},{6,8},{7,9},{8,6},{9,7},... | collective-permute-start | bytes 221192 | tf_op jit(solution)/shard_map/ppermute | solution.py:356
  27.9 2.5 %collective-permute-start.7 = (bf16[16,2304]{1,0:T(8,128)(2,1)S(1)}, bf16[16,2304]{1,0:T(8,128)(2,1)S(1)}, u32[]{:S(2)}, u32[]{:S(2)}) collective-permute-start(bf16[16,2304]{1,0:T(8,128)(2,1)S(1)} %get-tuple-element.83), channel_id=1, source_target_pairs={{0,15},{1,14},{2,13},{3,12},{4,11},{5,10},{6,9},{7,8},{8,7},{9,6},... | collective-permute-start | bytes 221192 | tf_op jit(solution)/shard_map/ppermute | solution.py:356
  30.8 2.4 %collective-permute-done.6.refs_15_ = bf16[16,2304]{1,0:T(8,128)(2,1)S(1)} collective-permute-done((bf16[16,2304]{1,0:T(8,128)(2,1)S(1)}, bf16[16,2304]{1,0:T(8,128)(2,1)S(1)}, u32[]{:S(2)}, u32[]{:S(2)}) %collective-permute-start.6) | collective-permute-done | bytes 73760 | tf_op jit(solution)/shard_map/ppermute | solution.py:356
  33.3 3.1 %collective-permute-start.11 = (bf16[16,5760]{1,0:T(8,128)(2,1)S(1)}, bf16[16,5760]{1,0:T(8,128)(2,1)S(1)}, u32[]{:S(2)}, u32[]{:S(2)}) collective-permute-start(bf16[16,5760]{1,0:T(8,128)(2,1)S(1)} %get-tuple-element.88), channel_id=1, source_target_pairs={{0,4},{1,5},{2,6},{3,7},{4,0},{5,1},{6,2},{7,3},{8,12},{9,13},{10,... | collective-permute-start | bytes 552968 | tf_op jit(solution)/shard_map/ppermute | solution.py:356
  37.5 2.3 %collective-permute-start.14 = (bf16[16,5760]{1,0:T(8,128)(2,1)S(1)}, bf16[16,5760]{1,0:T(8,128)(2,1)S(1)}, u32[]{:S(2)}, u32[]{:S(2)}) collective-permute-start(bf16[16,5760]{1,0:T(8,128)(2,1)S(1)} %get-tuple-element.91), channel_id=1, source_target_pairs={{0,7},{1,6},{2,5},{3,4},{4,3},{5,2},{6,1},{7,0},{8,15},{9,14},{10,... | collective-permute-start | bytes 552968 | tf_op jit(solution)/shard_map/ppermute | solution.py:356
  39.8 1.4 %collective-permute-done.11.refs_5_.refs_19_ = bf16[16,5760]{1,0:T(8,128)(2,1)S(1)} collective-permute-done((bf16[16,5760]{1,0:T(8,128)(2,1)S(1)}, bf16[16,5760]{1,0:T(8,128)(2,1)S(1)}, u32[]{:S(2)}, u32[]{:S(2)}) %collective-permute-start.11) | collective-permute-done | bytes 184352 | tf_op jit(solution)/shard_map/ppermute | solution.py:356
  41.1 3.9 %collective-permute-done.12.refs_6_.refs_20_ = bf16[16,5760]{1,0:T(8,128)(2,1)S(1)} collective-permute-done((bf16[16,5760]{1,0:T(8,128)(2,1)S(1)}, bf16[16,5760]{1,0:T(8,128)(2,1)S(1)}, u32[]{:S(2)}, u32[]{:S(2)}) %collective-permute-start.12) | collective-permute-done | bytes 184352 | tf_op jit(solution)/shard_map/ppermute | solution.py:356
  45.1 4.3 %collective-permute-done.13.refs_7_.refs_21_ = bf16[16,5760]{1,0:T(8,128)(2,1)S(1)} collective-permute-done((bf16[16,5760]{1,0:T(8,128)(2,1)S(1)}, bf16[16,5760]{1,0:T(8,128)(2,1)S(1)}, u32[]{:S(2)}, u32[]{:S(2)}) %collective-permute-start.13) | collective-permute-done | bytes 184352 | tf_op jit(solution)/shard_map/ppermute | solution.py:356
  49.3 2.4 %collective-permute-done.14.refs_8_.refs_22_ = bf16[16,5760]{1,0:T(8,128)(2,1)S(1)} collective-permute-done((bf16[16,5760]{1,0:T(8,128)(2,1)S(1)}, bf16[16,5760]{1,0:T(8,128)(2,1)S(1)}, u32[]{:S(2)}, u32[]{:S(2)}) %collective-permute-start.14) | collective-permute-done | bytes 184352 | tf_op jit(solution)/shard_map/ppermute | solution.py:356
  51.8 3.3 %collective-permute-start.22 = (bf16[16,1152]{1,0:T(8,128)(2,1)S(1)}, bf16[16,1152]{1,0:T(8,128)(2,1)S(1)}, u32[]{:S(2)}, u32[]{:S(2)}) collective-permute-start(bf16[16,1152]{1,0:T(8,128)(2,1)S(1)} %get-tuple-element.116), channel_id=1, source_target_pairs={{0,8},{1,9},{2,10},{3,11},{4,12},{5,13},{6,14},{7,15},{8,0},{9,1},... | collective-permute-start | bytes 110600 | tf_op jit(solution)/shard_map/ppermute | solution.py:356
  55.6 3.6 %collective-permute-start.24 = (bf16[16,1152]{1,0:T(8,128)(2,1)S(1)}, bf16[16,1152]{1,0:T(8,128)(2,1)S(1)}, u32[]{:S(2)}, u32[]{:S(2)}) collective-permute-start(bf16[16,1152]{1,0:T(8,128)(2,1)S(1)} %get-tuple-element.118), channel_id=1, source_target_pairs={{0,10},{1,11},{2,8},{3,9},{4,14},{5,15},{6,12},{7,13},{8,2},{9,3},... | collective-permute-start | bytes 110600 | tf_op jit(solution)/shard_map/ppermute | solution.py:356
  59.2 2.2 %collective-permute-start.26 = (bf16[16,1152]{1,0:T(8,128)(2,1)S(1)}, bf16[16,1152]{1,0:T(8,128)(2,1)S(1)}, u32[]{:S(2)}, u32[]{:S(2)}) collective-permute-start(bf16[16,1152]{1,0:T(8,128)(2,1)S(1)} %get-tuple-element.120), channel_id=1, source_target_pairs={{0,12},{1,13},{2,14},{3,15},{4,8},{5,9},{6,10},{7,11},{8,4},{9,5},... | collective-permute-start | bytes 110600 | tf_op jit(solution)/shard_map/ppermute | solution.py:356
  61.4 2.7 %outer.1 = (bf16[16,2304]{1,0:T(8,128)(2,1)S(1)}, bf16[16,2304]{1,0:T(8,128)(2,1)S(1)}, bf16[16,2304]{1,0:T(8,128)(2,1)S(1)}, bf16[16,2304]{1,0:T(8,128)(2,1)S(1...) custom-call(s32[3]{0:T(128)S(1)} %pad_add_fusion.refs_0_, ...), custom_call_target="tpu_custom_call" | custom-call | tf_op jit(solution)/shard_map/outer/pallas_call | solution.py:38
  64.4 1.5 %collective-permute-start.16 = (bf16[16,2304]{1,0:T(8,128)(2,1)S(1)}, bf16[16,2304]{1,0:T(8,128)(2,1)S(1)}, u32[]{:S(2)}, u32[]{:S(2)}) collective-permute-start(bf16[16,2304]{1,0:T(8,128)(2,1)S(1)} %get-tuple-element.110), channel_id=1, source_target_pairs={{0,2},{1,3},{2,0},{3,1},{4,6},{5,7},{6,4},{7,5},{8,10},{9,11},{10,... | collective-permute-start | bytes 221192 | tf_op jit(solution)/shard_map/ppermute | solution.py:356
  66.8 2.5 %collective-permute-start.28 = (bf16[16,1152]{1,0:T(8,128)(2,1)S(1)}, bf16[16,1152]{1,0:T(8,128)(2,1)S(1)}, u32[]{:S(2)}, u32[]{:S(2)}) collective-permute-start(bf16[16,1152]{1,0:T(8,128)(2,1)S(1)} %get-tuple-element.122), channel_id=1, source_target_pairs={{0,14},{1,15},{2,12},{3,13},{4,10},{5,11},{6,8},{7,9},{8,6},{9,7},... | collective-permute-start | bytes 110600 | tf_op jit(solution)/shard_map/ppermute | solution.py:356
  69.3 2.3 %collective-permute-start.29 = (bf16[16,1152]{1,0:T(8,128)(2,1)S(1)}, bf16[16,1152]{1,0:T(8,128)(2,1)S(1)}, u32[]{:S(2)}, u32[]{:S(2)}) collective-permute-start(bf16[16,1152]{1,0:T(8,128)(2,1)S(1)} %get-tuple-element.123), channel_id=1, source_target_pairs={{0,15},{1,14},{2,13},{3,12},{4,11},{5,10},{6,9},{7,8},{8,7},{9,6},... | collective-permute-start | bytes 110600 | tf_op jit(solution)/shard_map/ppermute | solution.py:356
  72.2 1.5 %collective-permute-done.28.refs_29_ = bf16[16,1152]{1,0:T(8,128)(2,1)S(1)} collective-permute-done((bf16[16,1152]{1,0:T(8,128)(2,1)S(1)}, bf16[16,1152]{1,0:T(8,128)(2,1)S(1)}, u32[]{:S(2)}, u32[]{:S(2)}) %collective-permute-start.28) | collective-permute-done | bytes 36896 | tf_op jit(solution)/shard_map/ppermute | solution.py:356
  73.6 1.9 %collective-permute-done.29.refs_30_ = bf16[16,1152]{1,0:T(8,128)(2,1)S(1)} collective-permute-done((bf16[16,1152]{1,0:T(8,128)(2,1)S(1)}, bf16[16,1152]{1,0:T(8,128)(2,1)S(1)}, u32[]{:S(2)}, u32[]{:S(2)}) %collective-permute-start.29) | collective-permute-done | bytes 36896 | tf_op jit(solution)/shard_map/ppermute | solution.py:356
  75.5 2.8 %collective-permute-start.20 = (bf16[16,2304]{1,0:T(8,128)(2,1)S(1)}, bf16[16,2304]{1,0:T(8,128)(2,1)S(1)}, u32[]{:S(2)}, u32[]{:S(2)}) collective-permute-start(bf16[16,2304]{1,0:T(8,128)(2,1)S(1)} %get-tuple-element.114), channel_id=1, source_target_pairs={{0,6},{1,7},{2,4},{3,5},{4,2},{5,3},{6,0},{7,1},{8,14},{9,15},{10,... | collective-permute-start | bytes 221192 | tf_op jit(solution)/shard_map/ppermute | solution.py:356
  79.8 3.1 %collective-permute-done.20.refs_13_ = bf16[16,2304]{1,0:T(8,128)(2,1)S(1)} collective-permute-done((bf16[16,2304]{1,0:T(8,128)(2,1)S(1)}, bf16[16,2304]{1,0:T(8,128)(2,1)S(1)}, u32[]{:S(2)}, u32[]{:S(2)}) %collective-permute-start.20) | collective-permute-done | bytes 73760 | tf_op jit(solution)/shard_map/ppermute | solution.py:356
  83.8 3.9 %update.1 = (bf16[12,192,128]{2,1,0:T(8,128)(2,1)S(1)}, bf16[12,192,128]{2,1,0:T(8,128)(2,1)S(1)}, bf16[48,192]{1,0:T(8,128)(2,1)S(1)}) custom-call(s32[3]{0:T(128)S(1)} %pad_add_fusion.refs_0_, f32[1,128]{1,0:T(1,128)S(1)} %bitcast.13, bf16[128,128]{1,0:T(8,128)(2,1)S(1)} %copy-done.2, f32[1,128]{1,0:T(1,128)S(1)} %bitcast.14, ...), custom_call_target="tpu_custom_call" | custom-call | tf_op jit(solution)/shard_map/update/pallas_call | solution.py:38
  88.1 4.4 %collective-permute-done.30.refs_8_ = bf16[1,48,192]{2,1,0:T(8,128)(2,1)S(1)} collective-permute-done((bf16[1,48,192]{2,1,0:T(8,128)(2,1)S(1)}, bf16[1,48,192]{2,1,0:T(8,128)(2,1)S(1)}, u32[]{:S(2)}, u32[]{:S(2)}) %collective-permute-start.30) | collective-permute-done | bytes 18464 | tf_op jit(solution)/shard_map/ppermute | solution.py:320
  92.6 4.0 %collective-permute-done.31.refs_9_ = bf16[2,48,192]{2,1,0:T(8,128)(2,1)S(1)} collective-permute-done((bf16[2,48,192]{2,1,0:T(8,128)(2,1)S(1)}, bf16[2,48,192]{2,1,0:T(8,128)(2,1)S(1)}, u32[]{:S(2)}, u32[]{:S(2)}) %collective-permute-start.31) | collective-permute-done | bytes 36896 | tf_op jit(solution)/shard_map/ppermute | solution.py:320
  97.6 3.7 %collective-permute-done.32.refs_10_ = bf16[4,48,192]{2,1,0:T(8,128)(2,1)S(1)} collective-permute-done((bf16[4,48,192]{2,1,0:T(8,128)(2,1)S(1)}, bf16[4,48,192]{2,1,0:T(8,128)(2,1)S(1)}, u32[]{:S(2)}, u32[]{:S(2)}) %collective-permute-start.32) | collective-permute-done | bytes 73760 | tf_op jit(solution)/shard_map/ppermute | solution.py:320
  102.9 7.3 %attend.1 = bf16[12,192,128]{2,1,0:T(8,128)(2,1)} custom-call(s32[3]{0:T(128)S(1)} %pad_add_fusion.refs_0_, bf16[12,192,128]{2,1,0:T(8,128)(2,1)S(1)} %get-tuple-element.125.refs_1_, bf16[12,192,128]{2,1,0:T(8,128)(2,1)S(1)} %get-tuple-element.126.refs_2_, bf16[12,128,192]{2,1,0:T(8,128)(2,1)S(1)} %get-tuple-element.127.refs_3_, ...), custom_call_target="tpu_custom_call" | custom-call | tf_op jit(solution)/shard_map/attend/pallas_call | solution.py:38
  (74 shorter events, 12.5 us)
Async XLA Ops:
  5.7 8.6 %collective-permute-start = (bf16[16,2304]{1,0:T(8,128)(2,1)S(1)}, bf16[16,2304]{1,0:T(8,128)(2,1)S(1)}, u32[]{:S(2)}, u32[]{:S(2)}) collective-permute-start(bf16[16,2304]{1,0:T(8,128)(2,1)S(1)} %get-tuple-element.76), channel_id=1, source_target_pairs={{0,8},{1,9},{2,10},{3,11},{4,12},{5,13},{6,14},{7,15},{8,0},{9,1},... | collective-permute-start | bytes 221192 | tf_op jit(solution)/shard_map/ppermute | solution.py:356
  9.8 8.7 %collective-permute-start.1 = (bf16[16,2304]{1,0:T(8,128)(2,1)S(1)}, bf16[16,2304]{1,0:T(8,128)(2,1)S(1)}, u32[]{:S(2)}, u32[]{:S(2)}) collective-permute-start(bf16[16,2304]{1,0:T(8,128)(2,1)S(1)} %get-tuple-element.77), channel_id=1, source_target_pairs={{0,9},{1,8},{2,11},{3,10},{4,13},{5,12},{6,15},{7,14},{8,1},{9,0},... | collective-permute-start | bytes 221192 | tf_op jit(solution)/shard_map/ppermute | solution.py:356
  9.8 27.3 %collective-permute-start.8 = (bf16[16,5760]{1,0:T(8,128)(2,1)S(1)}, bf16[16,5760]{1,0:T(8,128)(2,1)S(1)}, u32[]{:S(2)}, u32[]{:S(2)}) collective-permute-start(bf16[16,5760]{1,0:T(8,128)(2,1)S(1)} %get-tuple-element.85), channel_id=1, source_target_pairs={{0,1},{1,0},{2,3},{3,2},{4,5},{5,4},{6,7},{7,6},{8,9},{9,8},{10,11... | collective-permute-start | bytes 552968 | tf_op jit(solution)/shard_map/ppermute | solution.py:356
  10.0 27.5 %collective-permute-start.9 = (bf16[16,5760]{1,0:T(8,128)(2,1)S(1)}, bf16[16,5760]{1,0:T(8,128)(2,1)S(1)}, u32[]{:S(2)}, u32[]{:S(2)}) collective-permute-start(bf16[16,5760]{1,0:T(8,128)(2,1)S(1)} %get-tuple-element.86), channel_id=1, source_target_pairs={{0,2},{1,3},{2,0},{3,1},{4,6},{5,7},{6,4},{7,5},{8,10},{9,11},{10,... | collective-permute-start | bytes 552968 | tf_op jit(solution)/shard_map/ppermute | solution.py:356
  11.8 11.6 %collective-permute-start.2 = (bf16[16,2304]{1,0:T(8,128)(2,1)S(1)}, bf16[16,2304]{1,0:T(8,128)(2,1)S(1)}, u32[]{:S(2)}, u32[]{:S(2)}) collective-permute-start(bf16[16,2304]{1,0:T(8,128)(2,1)S(1)} %get-tuple-element.78), channel_id=1, source_target_pairs={{0,10},{1,11},{2,8},{3,9},{4,14},{5,15},{6,12},{7,13},{8,2},{9,3},... | collective-permute-start | bytes 221192 | tf_op jit(solution)/shard_map/ppermute | solution.py:356
  14.3 11.3 %collective-permute-start.3 = (bf16[16,2304]{1,0:T(8,128)(2,1)S(1)}, bf16[16,2304]{1,0:T(8,128)(2,1)S(1)}, u32[]{:S(2)}, u32[]{:S(2)}) collective-permute-start(bf16[16,2304]{1,0:T(8,128)(2,1)S(1)} %get-tuple-element.79), channel_id=1, source_target_pairs={{0,11},{1,10},{2,9},{3,8},{4,15},{5,14},{6,13},{7,12},{8,3},{9,2},... | collective-permute-start | bytes 221192 | tf_op jit(solution)/shard_map/ppermute | solution.py:356
  18.5 9.4 %collective-permute-start.4 = (bf16[16,2304]{1,0:T(8,128)(2,1)S(1)}, bf16[16,2304]{1,0:T(8,128)(2,1)S(1)}, u32[]{:S(2)}, u32[]{:S(2)}) collective-permute-start(bf16[16,2304]{1,0:T(8,128)(2,1)S(1)} %get-tuple-element.80), channel_id=1, source_target_pairs={{0,12},{1,13},{2,14},{3,15},{4,8},{5,9},{6,10},{7,11},{8,4},{9,5},... | collective-permute-start | bytes 221192 | tf_op jit(solution)/shard_map/ppermute | solution.py:356
  23.4 6.9 %collective-permute-start.5 = (bf16[16,2304]{1,0:T(8,128)(2,1)S(1)}, bf16[16,2304]{1,0:T(8,128)(2,1)S(1)}, u32[]{:S(2)}, u32[]{:S(2)}) collective-permute-start(bf16[16,2304]{1,0:T(8,128)(2,1)S(1)} %get-tuple-element.81), channel_id=1, source_target_pairs={{0,13},{1,12},{2,15},{3,14},{4,9},{5,8},{6,11},{7,10},{8,5},{9,4},... | collective-permute-start | bytes 221192 | tf_op jit(solution)/shard_map/ppermute | solution.py:356
  25.7 7.6 %collective-permute-start.6 = (bf16[16,2304]{1,0:T(8,128)(2,1)S(1)}, bf16[16,2304]{1,0:T(8,128)(2,1)S(1)}, u32[]{:S(2)}, u32[]{:S(2)}) collective-permute-start(bf16[16,2304]{1,0:T(8,128)(2,1)S(1)} %get-tuple-element.82), channel_id=1, source_target_pairs={{0,14},{1,15},{2,12},{3,13},{4,10},{5,11},{6,8},{7,9},{8,6},{9,7},... | collective-permute-start | bytes 221192 | tf_op jit(solution)/shard_map/ppermute | solution.py:356
  27.9 8.5 %collective-permute-start.7 = (bf16[16,2304]{1,0:T(8,128)(2,1)S(1)}, bf16[16,2304]{1,0:T(8,128)(2,1)S(1)}, u32[]{:S(2)}, u32[]{:S(2)}) collective-permute-start(bf16[16,2304]{1,0:T(8,128)(2,1)S(1)} %get-tuple-element.83), channel_id=1, source_target_pairs={{0,15},{1,14},{2,13},{3,12},{4,11},{5,10},{6,9},{7,8},{8,7},{9,6},... | collective-permute-start | bytes 221192 | tf_op jit(solution)/shard_map/ppermute | solution.py:356
  30.3 9.4 %collective-permute-start.10 = (bf16[16,5760]{1,0:T(8,128)(2,1)S(1)}, bf16[16,5760]{1,0:T(8,128)(2,1)S(1)}, u32[]{:S(2)}, u32[]{:S(2)}) collective-permute-start(bf16[16,5760]{1,0:T(8,128)(2,1)S(1)} %get-tuple-element.87), channel_id=1, source_target_pairs={{0,3},{1,2},{2,1},{3,0},{4,7},{5,6},{6,5},{7,4},{8,11},{9,10},{10,... | collective-permute-start | bytes 552968 | tf_op jit(solution)/shard_map/ppermute | solution.py:356
  33.3 7.8 %collective-permute-start.11 = (bf16[16,5760]{1,0:T(8,128)(2,1)S(1)}, bf16[16,5760]{1,0:T(8,128)(2,1)S(1)}, u32[]{:S(2)}, u32[]{:S(2)}) collective-permute-start(bf16[16,5760]{1,0:T(8,128)(2,1)S(1)} %get-tuple-element.88), channel_id=1, source_target_pairs={{0,4},{1,5},{2,6},{3,7},{4,0},{5,1},{6,2},{7,3},{8,12},{9,13},{10,... | collective-permute-start | bytes 552968 | tf_op jit(solution)/shard_map/ppermute | solution.py:356
  36.4 8.7 %collective-permute-start.12 = (bf16[16,5760]{1,0:T(8,128)(2,1)S(1)}, bf16[16,5760]{1,0:T(8,128)(2,1)S(1)}, u32[]{:S(2)}, u32[]{:S(2)}) collective-permute-start(bf16[16,5760]{1,0:T(8,128)(2,1)S(1)} %get-tuple-element.89), channel_id=1, source_target_pairs={{0,5},{1,4},{2,7},{3,6},{4,1},{5,0},{6,3},{7,2},{8,13},{9,12},{10,... | collective-permute-start | bytes 552968 | tf_op jit(solution)/shard_map/ppermute | solution.py:356
  37.1 12.2 %collective-permute-start.13 = (bf16[16,5760]{1,0:T(8,128)(2,1)S(1)}, bf16[16,5760]{1,0:T(8,128)(2,1)S(1)}, u32[]{:S(2)}, u32[]{:S(2)}) collective-permute-start(bf16[16,5760]{1,0:T(8,128)(2,1)S(1)} %get-tuple-element.90), channel_id=1, source_target_pairs={{0,6},{1,7},{2,4},{3,5},{4,2},{5,3},{6,0},{7,1},{8,14},{9,15},{10,... | collective-permute-start | bytes 552968 | tf_op jit(solution)/shard_map/ppermute | solution.py:356
  37.5 14.3 %collective-permute-start.14 = (bf16[16,5760]{1,0:T(8,128)(2,1)S(1)}, bf16[16,5760]{1,0:T(8,128)(2,1)S(1)}, u32[]{:S(2)}, u32[]{:S(2)}) collective-permute-start(bf16[16,5760]{1,0:T(8,128)(2,1)S(1)} %get-tuple-element.91), channel_id=1, source_target_pairs={{0,7},{1,6},{2,5},{3,4},{4,3},{5,2},{6,1},{7,0},{8,15},{9,14},{10,... | collective-permute-start | bytes 552968 | tf_op jit(solution)/shard_map/ppermute | solution.py:356
  51.8 12.3 %collective-permute-start.22 = (bf16[16,1152]{1,0:T(8,128)(2,1)S(1)}, bf16[16,1152]{1,0:T(8,128)(2,1)S(1)}, u32[]{:S(2)}, u32[]{:S(2)}) collective-permute-start(bf16[16,1152]{1,0:T(8,128)(2,1)S(1)} %get-tuple-element.116), channel_id=1, source_target_pairs={{0,8},{1,9},{2,10},{3,11},{4,12},{5,13},{6,14},{7,15},{8,0},{9,1},... | collective-permute-start | bytes 110600 | tf_op jit(solution)/shard_map/ppermute | solution.py:356
  55.1 9.3 %collective-permute-start.23 = (bf16[16,1152]{1,0:T(8,128)(2,1)S(1)}, bf16[16,1152]{1,0:T(8,128)(2,1)S(1)}, u32[]{:S(2)}, u32[]{:S(2)}) collective-permute-start(bf16[16,1152]{1,0:T(8,128)(2,1)S(1)} %get-tuple-element.117), channel_id=1, source_target_pairs={{0,9},{1,8},{2,11},{3,10},{4,13},{5,12},{6,15},{7,14},{8,1},{9,0},... | collective-permute-start | bytes 110600 | tf_op jit(solution)/shard_map/ppermute | solution.py:356
  55.6 10.3 %collective-permute-start.24 = (bf16[16,1152]{1,0:T(8,128)(2,1)S(1)}, bf16[16,1152]{1,0:T(8,128)(2,1)S(1)}, u32[]{:S(2)}, u32[]{:S(2)}) collective-permute-start(bf16[16,1152]{1,0:T(8,128)(2,1)S(1)} %get-tuple-element.118), channel_id=1, source_target_pairs={{0,10},{1,11},{2,8},{3,9},{4,14},{5,15},{6,12},{7,13},{8,2},{9,3},... | collective-permute-start | bytes 110600 | tf_op jit(solution)/shard_map/ppermute | solution.py:356
  59.2 7.7 %collective-permute-start.25 = (bf16[16,1152]{1,0:T(8,128)(2,1)S(1)}, bf16[16,1152]{1,0:T(8,128)(2,1)S(1)}, u32[]{:S(2)}, u32[]{:S(2)}) collective-permute-start(bf16[16,1152]{1,0:T(8,128)(2,1)S(1)} %get-tuple-element.119), channel_id=1, source_target_pairs={{0,11},{1,10},{2,9},{3,8},{4,15},{5,14},{6,13},{7,12},{8,3},{9,2},... | collective-permute-start | bytes 110600 | tf_op jit(solution)/shard_map/ppermute | solution.py:356
  59.2 10.1 %collective-permute-start.26 = (bf16[16,1152]{1,0:T(8,128)(2,1)S(1)}, bf16[16,1152]{1,0:T(8,128)(2,1)S(1)}, u32[]{:S(2)}, u32[]{:S(2)}) collective-permute-start(bf16[16,1152]{1,0:T(8,128)(2,1)S(1)} %get-tuple-element.120), channel_id=1, source_target_pairs={{0,12},{1,13},{2,14},{3,15},{4,8},{5,9},{6,10},{7,11},{8,4},{9,5},... | collective-permute-start | bytes 110600 | tf_op jit(solution)/shard_map/ppermute | solution.py:356
  64.1 11.4 %collective-permute-start.15 = (bf16[16,2304]{1,0:T(8,128)(2,1)S(1)}, bf16[16,2304]{1,0:T(8,128)(2,1)S(1)}, u32[]{:S(2)}, u32[]{:S(2)}) collective-permute-start(bf16[16,2304]{1,0:T(8,128)(2,1)S(1)} %get-tuple-element.109), channel_id=1, source_target_pairs={{0,1},{1,0},{2,3},{3,2},{4,5},{5,4},{6,7},{7,6},{8,9},{9,8},{10,11... | collective-permute-start | bytes 221192 | tf_op jit(solution)/shard_map/ppermute | solution.py:356
  64.4 13.9 %collective-permute-start.16 = (bf16[16,2304]{1,0:T(8,128)(2,1)S(1)}, bf16[16,2304]{1,0:T(8,128)(2,1)S(1)}, u32[]{:S(2)}, u32[]{:S(2)}) collective-permute-start(bf16[16,2304]{1,0:T(8,128)(2,1)S(1)} %get-tuple-element.110), channel_id=1, source_target_pairs={{0,2},{1,3},{2,0},{3,1},{4,6},{5,7},{6,4},{7,5},{8,10},{9,11},{10,... | collective-permute-start | bytes 221192 | tf_op jit(solution)/shard_map/ppermute | solution.py:356
  65.9 5.7 %collective-permute-start.27 = (bf16[16,1152]{1,0:T(8,128)(2,1)S(1)}, bf16[16,1152]{1,0:T(8,128)(2,1)S(1)}, u32[]{:S(2)}, u32[]{:S(2)}) collective-permute-start(bf16[16,1152]{1,0:T(8,128)(2,1)S(1)} %get-tuple-element.121), channel_id=1, source_target_pairs={{0,13},{1,12},{2,15},{3,14},{4,9},{5,8},{6,11},{7,10},{8,5},{9,4},... | collective-permute-start | bytes 110600 | tf_op jit(solution)/shard_map/ppermute | solution.py:356
  66.8 6.8 %collective-permute-start.28 = (bf16[16,1152]{1,0:T(8,128)(2,1)S(1)}, bf16[16,1152]{1,0:T(8,128)(2,1)S(1)}, u32[]{:S(2)}, u32[]{:S(2)}) collective-permute-start(bf16[16,1152]{1,0:T(8,128)(2,1)S(1)} %get-tuple-element.122), channel_id=1, source_target_pairs={{0,14},{1,15},{2,12},{3,13},{4,10},{5,11},{6,8},{7,9},{8,6},{9,7},... | collective-permute-start | bytes 110600 | tf_op jit(solution)/shard_map/ppermute | solution.py:356
  69.3 6.2 %collective-permute-start.29 = (bf16[16,1152]{1,0:T(8,128)(2,1)S(1)}, bf16[16,1152]{1,0:T(8,128)(2,1)S(1)}, u32[]{:S(2)}, u32[]{:S(2)}) collective-permute-start(bf16[16,1152]{1,0:T(8,128)(2,1)S(1)} %get-tuple-element.123), channel_id=1, source_target_pairs={{0,15},{1,14},{2,13},{3,12},{4,11},{5,10},{6,9},{7,8},{8,7},{9,6},... | collective-permute-start | bytes 110600 | tf_op jit(solution)/shard_map/ppermute | solution.py:356
  71.6 6.8 %collective-permute-start.17 = (bf16[16,2304]{1,0:T(8,128)(2,1)S(1)}, bf16[16,2304]{1,0:T(8,128)(2,1)S(1)}, u32[]{:S(2)}, u32[]{:S(2)}) collective-permute-start(bf16[16,2304]{1,0:T(8,128)(2,1)S(1)} %get-tuple-element.111), channel_id=1, source_target_pairs={{0,3},{1,2},{2,1},{3,0},{4,7},{5,6},{6,5},{7,4},{8,11},{9,10},{10,... | collective-permute-start | bytes 221192 | tf_op jit(solution)/shard_map/ppermute | solution.py:356
  73.6 4.8 %collective-permute-start.18 = (bf16[16,2304]{1,0:T(8,128)(2,1)S(1)}, bf16[16,2304]{1,0:T(8,128)(2,1)S(1)}, u32[]{:S(2)}, u32[]{:S(2)}) collective-permute-start(bf16[16,2304]{1,0:T(8,128)(2,1)S(1)} %get-tuple-element.112), channel_id=1, source_target_pairs={{0,4},{1,5},{2,6},{3,7},{4,0},{5,1},{6,2},{7,3},{8,12},{9,13},{10,... | collective-permute-start | bytes 221192 | tf_op jit(solution)/shard_map/ppermute | solution.py:356
  75.5 4.3 %collective-permute-start.19 = (bf16[16,2304]{1,0:T(8,128)(2,1)S(1)}, bf16[16,2304]{1,0:T(8,128)(2,1)S(1)}, u32[]{:S(2)}, u32[]{:S(2)}) collective-permute-start(bf16[16,2304]{1,0:T(8,128)(2,1)S(1)} %get-tuple-element.113), channel_id=1, source_target_pairs={{0,5},{1,4},{2,7},{3,6},{4,1},{5,0},{6,3},{7,2},{8,13},{9,12},{10,... | collective-permute-start | bytes 221192 | tf_op jit(solution)/shard_map/ppermute | solution.py:356
  75.5 7.4 %collective-permute-start.20 = (bf16[16,2304]{1,0:T(8,128)(2,1)S(1)}, bf16[16,2304]{1,0:T(8,128)(2,1)S(1)}, u32[]{:S(2)}, u32[]{:S(2)}) collective-permute-start(bf16[16,2304]{1,0:T(8,128)(2,1)S(1)} %get-tuple-element.114), channel_id=1, source_target_pairs={{0,6},{1,7},{2,4},{3,5},{4,2},{5,3},{6,0},{7,1},{8,14},{9,15},{10,... | collective-permute-start | bytes 221192 | tf_op jit(solution)/shard_map/ppermute | solution.py:356
  78.3 5.5 %collective-permute-start.21 = (bf16[16,2304]{1,0:T(8,128)(2,1)S(1)}, bf16[16,2304]{1,0:T(8,128)(2,1)S(1)}, u32[]{:S(2)}, u32[]{:S(2)}) collective-permute-start(bf16[16,2304]{1,0:T(8,128)(2,1)S(1)} %get-tuple-element.115), channel_id=1, source_target_pairs={{0,7},{1,6},{2,5},{3,4},{4,3},{5,2},{6,1},{7,0},{8,15},{9,14},{10,... | collective-permute-start | bytes 221192 | tf_op jit(solution)/shard_map/ppermute | solution.py:356
  87.7 4.7 %collective-permute-start.30 = (bf16[1,48,192]{2,1,0:T(8,128)(2,1)S(1)}, bf16[1,48,192]{2,1,0:T(8,128)(2,1)S(1)}, u32[]{:S(2)}, u32[]{:S(2)}) collective-permute-start(bf16[1,48,192]{2,1,0:T(8,128)(2,1)S(1)} %bitcast.7), channel_id=1, source_target_pairs={{0,8},{1,9},{2,10},{3,11},{4,12},{5,13},{6,14},{7,15},{8,0},{9,1},... | collective-permute-start | bytes 55304 | tf_op jit(solution)/shard_map/ppermute | solution.py:320
  96.7 4.7 %collective-permute-start.32 = (bf16[4,48,192]{2,1,0:T(8,128)(2,1)S(1)}, bf16[4,48,192]{2,1,0:T(8,128)(2,1)S(1)}, u32[]{:S(2)}, u32[]{:S(2)}) collective-permute-start(bf16[4,48,192]{2,1,0:T(8,128)(2,1)S(1)} %pad_maximum_fusion.1), channel_id=1, source_target_pairs={{0,2},{1,3},{2,0},{3,1},{4,6},{5,7},{6,4},{7,5},{8,10},{9,11},{10,... | collective-permute-start | bytes 221192 | tf_op jit(solution)/shard_map/ppermute | solution.py:320
  (16 other events, 588.5 us)

commit v4 on v3

--- a/solution.py
+++ b/solution.py
@@ -60,37 +60,9 @@
         self.block_tiles = -(-self.block // self.chans)
 
 
-def edges_kernel(sz, len_ref, x_ref, ln_ref, w_ref, *refs):
-    near, far, pair = refs[: sz.group], refs[sz.group : 2 * sz.group], refs[2 * sz.group : -2]
-    norm_ref, pair_ref = refs[-2:]
-    length, first, me = len_ref[0], len_ref[1], len_ref[2]
-    cd, ch = sz.chans, sz.channels
-    mine = me & (sz.group - 1)
-    r = lax.broadcasted_iota(jnp.int32, (ch, ch), 0)
-    e = lax.broadcasted_iota(jnp.int32, (ch, ch), 1)
-    pick = (((r // cd) ^ mine) * cd + r % cd == e).astype(BF16)
-    weights = [dot(pick, w_ref[p], 1, 1).astype(BF16) for p in range(4)]
-    gate_w = jnp.concatenate([weights[0], weights[2]], axis=0)
-    value_w = jnp.concatenate([weights[1], weights[3]], axis=0)
-    gain = ln_ref[...]
+def project_edges(sz, info, norm_ref, gate_w, value_w, store):
+    length, first = info[0], info[1]
     main = sz.whole * LANES
-    for row in range(sz.rows):
-        x = x_ref[row].astype(F32)
-        for d in range(sz.devices):
-            pair_ref[d, row * sz.rows : (row + 1) * sz.rows, :] = x[d * sz.rows : (d + 1) * sz.rows]
-        normed = norm_last(x, gain).astype(BF16)
-        norm_ref[pl.ds(row * main, main), :] = normed[:main]
-        if sz.rest:
-            h, q = divmod(row, sz.half)
-            norm_ref[pl.ds(sz.rows * main + q * LANES + h * sz.rest, sz.rest), :] = normed[main:]
-    for r in range(sz.group):
-        for t in range(sz.block_tiles):
-            at = (2 * sz.tiles + t) * LANES
-            rows = slice(t * cd, (t + 1) * cd)
-            near[r][:, at : at + LANES] = pair_ref[me ^ r, rows, :].astype(BF16)
-            pair[r][:, t * LANES : (t + 1) * LANES] = pair_ref[me ^ (sz.group + r), rows, :].astype(
-                BF16
-            )
     lane = lax.broadcasted_iota(jnp.int32, (1, LANES), 1)
 
     def live(tile):
@@ -109,27 +81,69 @@
         mask = jnp.concatenate([live(tile + s) for s in range(step)], axis=1)
         edge = sigmoid(dot(gate_w, n, 1, 1)) * dot(value_w, n, 1, 1) * mask
         edge = edge.astype(BF16)
-        to = slice(tile * LANES, (tile + step) * LANES)
-        right_to = slice((sz.tiles + tile) * LANES, (sz.tiles + tile + step) * LANES)
-        for r in range(sz.group):
-            left = edge[r * cd : (r + 1) * cd]
-            near[r][:, to] = left
-            far[r][:, to] = left
-            near[r][:, right_to] = edge[ch + r * cd : ch + (r + 1) * cd]
-
-
-def outer_kernel(sz, len_ref, *refs):
-    near, far = refs[: sz.group], refs[sz.group : 2 * sz.group]
-    outs = refs[2 * sz.group : 3 * sz.group]
-    lmain_ref, lrest_ref, rmain_ref, rrest_ref, omain_ref, orest_ref = refs[3 * sz.group :]
-    me = len_ref[2]
-    mine = me & (sz.group - 1)
+        for g in range(sz.group):
+            store(g, tile, step, edge[g * sz.chans : (g + 1) * sz.chans])
+
+
+def turned(w):
+    return jnp.transpose(w.astype(F32)).astype(BF16)
+
+
+def left_kernel(sz, len_ref, x_ref, ln_ref, w_ref, out_ref, norm_ref):
+    gain = ln_ref[...]
+    main = sz.whole * LANES
+    for row in range(sz.rows):
+        normed = norm_last(x_ref[row].astype(F32), gain).astype(BF16)
+        norm_ref[pl.ds(row * main, main), :] = normed[:main]
+        if sz.rest:
+            h, q = divmod(row, sz.half)
+            norm_ref[pl.ds(sz.rows * main + q * LANES + h * sz.rest, sz.rest), :] = normed[main:]
+
+    def store(g, tile, step, edge):
+        out_ref[g, :, tile * LANES : (tile + step) * LANES] = edge
+
+    project_edges(sz, len_ref, norm_ref, turned(w_ref[0]), turned(w_ref[1]), store)
+
+
+def right_kernel(sz, len_ref, x_ref, far_ref, norm_ref, w_ref, out_ref, pair_ref):
+    cd = sz.chans
+    upper = len_ref[3]
+    for row in range(sz.rows):
+        for h in range(2):
+            x = x_ref[row, h * sz.columns : (h + 1) * sz.columns, :].astype(F32)
+            if h:
+                x = jnp.where(upper > 0, x, own)
+            else:
+                own = x
+        for base, values in ((0, x), (1, far_ref[row].astype(F32))):
+            for g in range(sz.group):
+                pair_ref[base, g, row * sz.rows : (row + 1) * sz.rows, :] = values[
+                    g * sz.rows : (g + 1) * sz.rows
+                ]
+    for base in range(2):
+        for g in range(sz.group):
+            for t in range(sz.block_tiles):
+                at = (sz.tiles + base * sz.block_tiles + t) * LANES
+                out_ref[g, :, at : at + LANES] = pair_ref[
+                    base, g, t * cd : (t + 1) * cd, :
+                ].astype(BF16)
+
+    def store(g, tile, step, edge):
+        out_ref[g, :, tile * LANES : (tile + step) * LANES] = edge
+
+    project_edges(sz, len_ref, norm_ref, turned(w_ref[2]), turned(w_ref[3]), store)
+
+
+def outer_kernel(
+    sz, len_ref, own_ref, far_ref, right_ref, out_ref,
+    lmain_ref, lrest_ref, rmain_ref, rrest_ref, omain_ref, orest_ref,
+):
+    upper = len_ref[3]
     cd, n, w, half = sz.chans, sz.crop, sz.whole, sz.half
 
-    def unpack(ref, base, owner, main_ref, rest_ref):
+    def unpack(ref, g, owner, main_ref, rest_ref):
         for tile in range(sz.tiles):
-            at = (base + tile) * LANES
-            block = ref[:, at : at + LANES].astype(F32)
+            block = ref[g, :, tile * LANES : (tile + 1) * LANES].astype(F32)
             if tile < sz.rows * w:
                 row, m = divmod(tile, w)
                 main_ref[m, pl.ds(pl.multiple_of((owner * sz.rows + row) * cd, 8), cd), :] = block
@@ -140,10 +154,10 @@
                     block, sz.rest, 1
                 )
 
-    for r in range(sz.group):
-        unpack(near[r], 0, me ^ r, lmain_ref, lrest_ref)
-        unpack(near[r], sz.tiles, mine ^ r, rmain_ref, rrest_ref)
-        unpack(far[r], 0, me ^ (sz.group + r), lmain_ref, lrest_ref)
+    for g in range(sz.group):
+        unpack(own_ref, g, upper * sz.group + g, lmain_ref, lrest_ref)
+        unpack(right_ref, g, g, rmain_ref, rrest_ref)
+        unpack(far_ref, g, (1 - upper) * sz.group + g, lmain_ref, lrest_ref)
 
     def matrix(c, size, main_ref, rest_ref):
         parts = [main_ref[m, pl.ds(c, size, stride=cd), :].astype(BF16) for m in range(w)]
@@ -161,43 +175,39 @@
             part = outer[:, w * LANES :]
             orest_ref[pl.ds(c, sz.columns, stride=cd), :] = jnp.concatenate([part, part], axis=1)
     low = lax.broadcasted_iota(jnp.int32, (cd, LANES), 1) < sz.rest
-    for r in range(sz.group):
-        start = (mine ^ r) * sz.rows
+    for g in range(sz.group):
+        start = g * sz.rows
         for tile in range(sz.tiles):
             if tile < sz.rows * w:
                 row, m = divmod(tile, w)
-                block = omain_ref[m, pl.ds(pl.multiple_of((start + row) * cd, 8), cd), :]
+                block = omain_ref[m, pl.ds((start + row) * cd, cd), :]
             else:
                 at = start + tile - sz.rows * w
                 block = jnp.where(
                     low,
-                    orest_ref[pl.ds(pl.multiple_of(at * cd, 8), cd), :],
-                    orest_ref[pl.ds(pl.multiple_of((at + half) * cd, 8), cd), :],
+                    orest_ref[pl.ds(at * cd, cd), :],
+                    orest_ref[pl.ds((at + half) * cd, cd), :],
                 )
-            outs[r][:, tile * LANES : (tile + 1) * LANES] = block.astype(BF16)
-
-
-def update_kernel(sz, len_ref, lnp_ref, gate_ref, lnh_ref, tri_ref, lna_ref, biasw_ref, *refs):
-    sums, near, pair = refs[: sz.group], refs[sz.group : 2 * sz.group], refs[2 * sz.group : -6]
-    first_ref, col_ref, bias_ref, cols_ref, brow_ref, sums_ref = refs[-6:]
+            out_ref[g, :, tile * LANES : (tile + 1) * LANES] = block.astype(BF16)
+
+
+def update_kernel(
+    sz, len_ref, lnp_ref, gate_ref, lnh_ref, tri_ref, lna_ref, biasw_ref, sums_ref, pair_ref,
+    first_ref, col_ref, bias_ref, cols_ref, brow_ref,
+):
     n, w, half, ch, cd = sz.crop, sz.whole, sz.half, sz.channels, sz.chans
-    me = len_ref[2]
-    mine = me & (sz.group - 1)
-    for r in range(sz.group):
-        sums_ref[pl.ds(pl.multiple_of((mine ^ r) * cd, 8), cd), :] = sums[r][...].astype(F32)
-        for ref, base, owner in (
-            (near[r], 2 * sz.tiles, me ^ r),
-            (pair[r], 0, me ^ (sz.group + r)),
-        ):
+    upper = len_ref[3]
+    for base, side in ((0, upper), (1, 1 - upper)):
+        for g in range(sz.group):
             for t in range(sz.block_tiles):
-                at = (base + t) * LANES
-                row = pl.multiple_of(owner * sz.block + t * cd, 8)
-                cols_ref[pl.ds(row, cd), :] = ref[:, at : at + LANES].astype(F32)
+                at = (sz.tiles + base * sz.block_tiles + t) * LANES
+                row = pl.multiple_of((side * sz.group + g) * sz.block + t * cd, 8)
+                cols_ref[pl.ds(row, cd), :] = pair_ref[g, :, at : at + LANES].astype(F32)
     gain_h = jnp.transpose(jnp.broadcast_to(lnh_ref[...], (ch, ch)))
     tri = tri_ref[...]
 
     def update(tile):
-        block = sums_ref[:, tile * LANES : (tile + 1) * LANES]
+        block = sums_ref[:, :, tile * LANES : (tile + 1) * LANES].astype(F32).reshape(ch, LANES)
         average = jnp.mean(block, axis=0, keepdims=True)
         centred = block - average
         variance = jnp.mean(centred * centred, axis=0, keepdims=True)
@@ -335,8 +345,8 @@
     sz = Sizes(rows, crop, devices, ch)
     n, cd = crop, sz.chans
     me = lax.axis_index(AXES).astype(jnp.int32)
-    info = jnp.stack([length[0], me * rows, me])
-
+    upper = me // sz.group
+    info = jnp.stack([length[0], me * rows, me, upper])
     def bound(kernel, *extra):
         def run(*refs):
             return kernel(sz, *extra, *refs)
@@ -347,36 +357,42 @@
     g, t, bt = sz.group, sz.tiles, sz.block_tiles
 
     def slab(tiles):
-        return shape((cd, tiles * LANES), BF16)
-
-    def send(blocks, offset):
-        return [
-            block
-            if not (offset ^ r)
-            else lax.ppermute(block, AXES, [(d, d ^ offset ^ r) for d in range(devices)])
-            for r, block in enumerate(blocks)
-        ]
-
-    made = call(
-        bound(edges_kernel),
-        [slab(2 * t + bt)] * g + [slab(t)] * g + [slab(bt)] * g,
+        return shape((g, cd, tiles * LANES), BF16)
+
+    def mirror(block):
+        return lax.ppermute(block, AXES, [(d, d ^ g) for d in range(devices)])
+
+    def within(blocks):
+        return lax.all_to_all(
+            blocks, AXES, split_axis=0, concat_axis=0, tiled=True,
+            axis_index_groups=[list(range(g)), list(range(g, devices))],
+        )
+
+    far_pair = mirror(lax.dynamic_slice_in_dim(pair_rep, (1 - upper) * sz.columns, sz.columns, 1))
+    left, normed = call(
+        bound(left_kernel),
+        [slab(t), shape((rows * crop, ch), BF16)],
         (info, pair_rep, ln_pair[None], tri_in),
-        scratch=[
-            pltpu.VMEM((rows * crop, ch), BF16),
-            pltpu.VMEM((devices, bt * cd, ch), F32),
-        ],
         smem=(0,),
-        name="edges",
-    )
-    far = send(made[g : 2 * g], g)
-    near = send(made[:g], 0)
-    late, far, near = lax.optimization_barrier((made[2 * g :], far, near))
-    pair = send(late, g)
+        name="left",
+    )
+    left = within(left)
+    far_left = mirror(left)
+    right = within(
+        call(
+            bound(right_kernel),
+            slab(t + 2 * bt),
+            (info, pair_rep, far_pair, normed, tri_in),
+            scratch=[pltpu.VMEM((2, g, bt * cd, ch), F32)],
+            smem=(0,),
+            name="right",
+        )
+    )
     rest = sz.rest > 0
     outer = call(
         bound(outer_kernel),
-        [slab(t)] * g,
-        (info, *near, *far),
+        slab(t),
+        (info, left, far_left, right),
         scratch=[
             pltpu.VMEM((sz.whole, n * cd, LANES), F32),
             pltpu.VMEM((n * cd if rest else 8, LANES), F32),
@@ -388,7 +404,7 @@
         smem=(0,),
         name="outer",
     )
-    sums = send(outer, 0)
+    sums = within(outer)
     first, col, bias = call(
         bound(update_kernel),
         [
@@ -398,12 +414,11 @@
         ],
         (
             info, ln_pair[None], tri_gate, ln_hidden[None], tri_out, ln_att[None], att_bias,
-            *sums, *near, *pair,
+            sums, right,
         ),
         scratch=[
             pltpu.VMEM((devices * sz.block + cd, ch), F32),
             pltpu.VMEM((rows * heads, n), F32),
-            pltpu.VMEM((ch, rows * n), F32),
         ],
         smem=(0,),
         name="update",

time: 110 us -> 108 us (0.982); the launches traced: 110 us -> 107 us
  starting transfers between devices: 49.7 us -> 28.1 us
  waiting for transfers between devices: 39.5 us -> 54.7 us
  Pallas kernels: 17.1 us -> 20.4 us
    ppermute x30 -> x2, starting transfers between devices: 48.2 us -> 5.23 us  [mirror(): return lax.ppermute(block, AXES, [(d, d ^ g) for d in range(devices)])]
    all_to_all x0 -> x3, starting transfers between devices: none -> 16.9 us  [within(): lax.all_to_all(blocks, AXES, split_axis=0, concat_axis=0, tiled=True, axi...]
    all_to_all x0 -> x3, waiting for transfers between devices: none -> 11.4 us  [within(): lax.all_to_all(blocks, AXES, split_axis=0, concat_axis=0, tiled=True, axi...]
    ppermute x30 -> x2, waiting for transfers between devices: 26.9 us -> 35 us  [mirror(): return lax.ppermute(block, AXES, [(d, d ^ g) for d in range(devices)])]
    ppermute x4, starting transfers between devices: 1.52 us -> 5.92 us  [spread(): got = lax.ppermute(held, AXES, [(d, d ^ bit) for d in range(devices)])]
    ppermute x4, waiting for transfers between devices: 12.6 us -> 8.25 us  [spread(): got = lax.ppermute(held, AXES, [(d, d ^ bit) for d in range(devices)])]
    pallas_call x5 -> x6, Pallas kernels: 17.1 us -> 20.4 us  [call(): pl.pallas_call(kernel, out_shape=out_shape, in_specs=specs, out_specs=vme...]
    unnamed x29 -> x33, local copies, waits for them, and re-layouts: 2.81 us -> 2.82 us
  transfers between devices with their start and end apart: 34 -> 9, of which waited for: 15 -> 8; matrix products, arithmetic and copies ran while one was open for 0% -> 0% of each run, Pallas kernels for 3% -> 3%
where the time goes in v4:
time: 108 us; the launch traced here: 107 us
  waiting for transfers between devices  54.7 us (51%)
  starting transfers between devices  28.1 us (26%)
  Pallas kernels  20.4 us (19%)
  local copies, waits for them, and re-layouts  2.85 us (3%)
    ppermute x2, waiting for transfers between devices, mirror(): return lax.ppermute(block, AXES, [(d, d ^ g) for d in range(devices)])  35 us
    pallas_call x6, Pallas kernels, call(): pl.pallas_call(kernel, out_shape=out_shape, in_specs=specs, out_specs=vme...  20.4 us
    all_to_all x3, starting transfers between devices, within(): lax.all_to_all(blocks, AXES, split_axis=0, concat_axis=0, tiled=True, axi...  16.9 us
    all_to_all x3, waiting for transfers between devices, within(): lax.all_to_all(blocks, AXES, split_axis=0, concat_axis=0, tiled=True, axi...  11.4 us
    ppermute x4, waiting for transfers between devices, spread(): got = lax.ppermute(held, AXES, [(d, d ^ bit) for d in range(devices)])  8.25 us
    ppermute x4, starting transfers between devices, spread(): got = lax.ppermute(held, AXES, [(d, d ^ bit) for d in range(devices)])  5.92 us
    ppermute x2, starting transfers between devices, mirror(): return lax.ppermute(block, AXES, [(d, d ^ g) for d in range(devices)])  5.23 us
    unnamed x33, local copies, waits for them, and re-layouts  2.82 us
  transfers between devices with their start and end apart: 9, of which 8 were waited for; matrix products, arithmetic and copies ran while one was open for 0% of the time, Pallas kernels for 3%

profile of v4, /device:TPU:0, one launch (start us, length us, event | category | flops | bytes accessed | tf_op | source)
XLA Modules:
  0.0 107.1 jit_solution(15865299975142490124)
XLA Ops:
  0.7 0.1 pad_add_fusion.refs_0_
  0.7 1.1 copy-done
  1.8 0.9 copy-done.2
  2.7 0.7 copy-done.11
  3.4 2.9 %left.1 = (bf16[8,16,2304]{2,1,0:T(8,128)(2,1)}, bf16[2304,128]{1,0:T(8,128)(2,1)S(1)}) custom-call(s32[4]{0:T(128)S(1)} %pad_add_fusion.refs_0_, bf16[12,192,128]{2,1,0:T(8,128)(2,1)S(1)} %copy-done, f32[1,128]{1,0:T(1,128)S(1)} %bitcast.13, bf16[4,128,128]{2,1,0:T(8,128)(2,1)S(1)} %copy-done.2), custom_call_target="tpu_custom_call" | custom-call | tf_op jit(solution)/shard_map/left/pallas_call | solution.py:38
  6.2 5.2 %all-to-all-start = ((bf16[8,16,2304]{2,1,0:T(8,128)(2,1)}), bf16[8,16,2304]{2,1,0:T(8,128)(2,1)S(1)}, u32[]{:S(2)}, u32[]{:S(2)}) async-start(bf16[8,16,2304]{2,1,0:T(8,128)(2,1)} %get-tuple-element.14), calls=%async_computation | async-start | bytes 1179648 | tf_op jit(solution)/shard_map/all_to_all | solution.py:366
  11.5 2.7 %collective-permute-start.1 = (bf16[12,96,128]{2,1,0:T(8,128)(2,1)S(1)}, bf16[12,96,128]{2,1,0:T(8,128)(2,1)S(1)}, u32[]{:S(2)}, u32[]{:S(2)}) collective-permute-start(bf16[12,96,128]{2,1,0:T(8,128)(2,1)S(1)} %constant_dynamic-slice_fusion), channel_id=1, source_target_pairs={{0,8},{1,9},{2,10},{3,11},{4,12},{5,13},{6,14},{7,15},{8,0},{9,1},... | collective-permute-start | bytes 884744 | tf_op jit(solution)/shard_map/ppermute | solution.py:363
  14.2 11.1 %collective-permute-done.1.refs_2_ = bf16[12,96,128]{2,1,0:T(8,128)(2,1)S(1)} collective-permute-done((bf16[12,96,128]{2,1,0:T(8,128)(2,1)S(1)}, bf16[12,96,128]{2,1,0:T(8,128)(2,1)S(1)}, u32[]{:S(2)}, u32[]{:S(2)}) %collective-permute-start.1) | collective-permute-done | bytes 294944 | tf_op jit(solution)/shard_map/ppermute | solution.py:363
  25.3 2.2 %right.1 = bf16[8,16,4608]{2,1,0:T(8,128)(2,1)} custom-call(s32[4]{0:T(128)S(1)} %pad_add_fusion.refs_0_, bf16[12,192,128]{2,1,0:T(8,128)(2,1)S(1)} %copy-done.1, bf16[12,96,128]{2,1,0:T(8,128)(2,1)S(1)} %collective-permute-done.1.refs_2_, bf16[2304,128]{1,0:T(8,128)(2,1)S(1)} %get-tuple-element.15.refs_3_, bf16[4,128,128]{2,1,0:T(8,128)(2,1)S(1)} %copy-done.3), custom_call_target="tpu_custom_call" | custom-call | tf_op jit(solution)/shard_map/right/pallas_call | solution.py:38
  27.6 6.8 %all-to-all-start.1 = ((bf16[8,16,4608]{2,1,0:T(8,128)(2,1)}), bf16[8,16,4608]{2,1,0:T(8,128)(2,1)S(1)}, u32[]{:S(2)}, u32[]{:S(2)}) async-start(bf16[8,16,4608]{2,1,0:T(8,128)(2,1)} %right.1), calls=%async_computation.1 | async-start | bytes 2359296 | tf_op jit(solution)/shard_map/all_to_all | solution.py:366
  34.4 2.6 %collective-permute-start = (bf16[8,16,2304]{2,1,0:T(8,128)(2,1)S(1)}, bf16[8,16,2304]{2,1,0:T(8,128)(2,1)S(1)}, u32[]{:S(2)}, u32[]{:S(2)}) collective-permute-start(bf16[8,16,2304]{2,1,0:T(8,128)(2,1)S(1)} %all-to-all-done.refs_1_), channel_id=1, source_target_pairs={{0,8},{1,9},{2,10},{3,11},{4,12},{5,13},{6,14},{7,15},{8,0},{9,1},... | collective-permute-start | bytes 1769480 | tf_op jit(solution)/shard_map/ppermute | solution.py:363
  36.9 23.9 %collective-permute-done.refs_2_ = bf16[8,16,2304]{2,1,0:T(8,128)(2,1)S(1)} collective-permute-done((bf16[8,16,2304]{2,1,0:T(8,128)(2,1)S(1)}, bf16[8,16,2304]{2,1,0:T(8,128)(2,1)S(1)}, u32[]{:S(2)}, u32[]{:S(2)}) %collective-permute-start) | collective-permute-done | bytes 589856 | tf_op jit(solution)/shard_map/ppermute | solution.py:363
  60.8 2.0 %all-to-all-done.1.refs_3_.refs_8_ = bf16[8,16,4608]{2,1,0:T(8,128)(2,1)S(1)} async-done(((bf16[8,16,4608]{2,1,0:T(8,128)(2,1)}), bf16[8,16,4608]{2,1,0:T(8,128)(2,1)S(1)}, u32[]{:S(2)}, u32[]{:S(2)}) %all-to-all-start.1) | async-done | bytes 1179680 | tf_op jit(solution)/shard_map/all_to_all | solution.py:366
  62.9 3.5 %outer.1 = bf16[8,16,2304]{2,1,0:T(8,128)(2,1)} custom-call(s32[4]{0:T(128)S(1)} %pad_add_fusion.refs_0_, bf16[8,16,2304]{2,1,0:T(8,128)(2,1)S(1)} %all-to-all-done.refs_1_, bf16[8,16,2304]{2,1,0:T(8,128)(2,1)S(1)} %collective-permute-done.refs_2_, bf16[8,16,4608]{2,1,0:T(8,128)(2,1)S(1)} %all-to-all-done.1.refs_3_.refs_8_), custom_call_target="tpu_custom_call" | custom-call | tf_op jit(solution)/shard_map/outer/pallas_call | solution.py:38
  66.4 0.0 copy-start.13
  66.4 0.0 copy-start.14
  66.4 4.9 %all-to-all-start.2 = ((bf16[8,16,2304]{2,1,0:T(8,128)(2,1)}), bf16[8,16,2304]{2,1,0:T(8,128)(2,1)S(1)}, u32[]{:S(2)}, u32[]{:S(2)}) async-start(bf16[8,16,2304]{2,1,0:T(8,128)(2,1)} %outer.1), calls=%async_computation.2 | async-start | bytes 1179648 | tf_op jit(solution)/shard_map/all_to_all | solution.py:366
  71.3 0.1 copy.15.refs_6_
  71.5 9.4 %all-to-all-done.2.refs_7_ = bf16[8,16,2304]{2,1,0:T(8,128)(2,1)S(1)} async-done(((bf16[8,16,2304]{2,1,0:T(8,128)(2,1)}), bf16[8,16,2304]{2,1,0:T(8,128)(2,1)S(1)}, u32[]{:S(2)}, u32[]{:S(2)}) %all-to-all-start.2) | async-done | bytes 589856 | tf_op jit(solution)/shard_map/all_to_all | solution.py:366
  80.9 0.0 copy-start.8
  80.9 0.0 copy-start.9
  81.0 3.8 %update.1 = (bf16[12,192,128]{2,1,0:T(8,128)(2,1)S(1)}, bf16[12,192,128]{2,1,0:T(8,128)(2,1)S(1)}, bf16[48,192]{1,0:T(8,128)(2,1)S(1)}) custom-call(s32[4]{0:T(128)S(1)} %pad_add_fusion.refs_0_, f32[1,128]{1,0:T(1,128)S(1)} %bitcast.14, bf16[128,128]{1,0:T(8,128)(2,1)S(1)} %copy-done.4, f32[1,128]{1,0:T(1,128)S(1)} %bitcast.15, ...), custom_call_target="tpu_custom_call" | custom-call | tf_op jit(solution)/shard_map/update/pallas_call | solution.py:38
  84.8 2.5 %collective-permute-start.2 = (bf16[1,48,192]{2,1,0:T(8,128)(2,1)S(1)}, bf16[1,48,192]{2,1,0:T(8,128)(2,1)S(1)}, u32[]{:S(2)}, u32[]{:S(2)}) collective-permute-start(bf16[1,48,192]{2,1,0:T(8,128)(2,1)S(1)} %bitcast.8), channel_id=1, source_target_pairs={{0,8},{1,9},{2,10},{3,11},{4,12},{5,13},{6,14},{7,15},{8,0},{9,1},... | collective-permute-start | bytes 55304 | tf_op jit(solution)/shard_map/ppermute | solution.py:330
  87.3 2.2 %collective-permute-done.2.refs_8_ = bf16[1,48,192]{2,1,0:T(8,128)(2,1)S(1)} collective-permute-done((bf16[1,48,192]{2,1,0:T(8,128)(2,1)S(1)}, bf16[1,48,192]{2,1,0:T(8,128)(2,1)S(1)}, u32[]{:S(2)}, u32[]{:S(2)}) %collective-permute-start.2) | collective-permute-done | bytes 18464 | tf_op jit(solution)/shard_map/ppermute | solution.py:330
  89.6 1.5 %collective-permute-start.3 = (bf16[2,48,192]{2,1,0:T(8,128)(2,1)S(1)}, bf16[2,48,192]{2,1,0:T(8,128)(2,1)S(1)}, u32[]{:S(2)}, u32[]{:S(2)}) collective-permute-start(bf16[2,48,192]{2,1,0:T(8,128)(2,1)S(1)} %pad_maximum_fusion.2), channel_id=1, source_target_pairs={{0,4},{1,5},{2,6},{3,7},{4,0},{5,1},{6,2},{7,3},{8,12},{9,13},{10,... | collective-permute-start | bytes 110600 | tf_op jit(solution)/shard_map/ppermute | solution.py:330
  91.1 2.6 %collective-permute-done.3.refs_9_ = bf16[2,48,192]{2,1,0:T(8,128)(2,1)S(1)} collective-permute-done((bf16[2,48,192]{2,1,0:T(8,128)(2,1)S(1)}, bf16[2,48,192]{2,1,0:T(8,128)(2,1)S(1)}, u32[]{:S(2)}, u32[]{:S(2)}) %collective-permute-start.3) | collective-permute-done | bytes 36896 | tf_op jit(solution)/shard_map/ppermute | solution.py:330
  93.7 1.8 %collective-permute-start.4 = (bf16[4,48,192]{2,1,0:T(8,128)(2,1)S(1)}, bf16[4,48,192]{2,1,0:T(8,128)(2,1)S(1)}, u32[]{:S(2)}, u32[]{:S(2)}) collective-permute-start(bf16[4,48,192]{2,1,0:T(8,128)(2,1)S(1)} %pad_maximum_fusion.1), channel_id=1, source_target_pairs={{0,2},{1,3},{2,0},{3,1},{4,6},{5,7},{6,4},{7,5},{8,10},{9,11},{10,... | collective-permute-start | bytes 221192 | tf_op jit(solution)/shard_map/ppermute | solution.py:330
  95.5 2.9 %collective-permute-done.4.refs_10_ = bf16[4,48,192]{2,1,0:T(8,128)(2,1)S(1)} collective-permute-done((bf16[4,48,192]{2,1,0:T(8,128)(2,1)S(1)}, bf16[4,48,192]{2,1,0:T(8,128)(2,1)S(1)}, u32[]{:S(2)}, u32[]{:S(2)}) %collective-permute-start.4) | collective-permute-done | bytes 73760 | tf_op jit(solution)/shard_map/ppermute | solution.py:330
  98.5 0.1 collective-permute-start.5
  98.6 0.9 project.1
  99.5 0.5 collective-permute-done.5.refs_11_
  100.0 7.1 %attend.1 = bf16[12,192,128]{2,1,0:T(8,128)(2,1)} custom-call(s32[4]{0:T(128)S(1)} %pad_add_fusion.refs_0_, bf16[12,192,128]{2,1,0:T(8,128)(2,1)S(1)} %get-tuple-element.17.refs_1_, bf16[12,192,128]{2,1,0:T(8,128)(2,1)S(1)} %get-tuple-element.18.refs_2_, bf16[12,128,192]{2,1,0:T(8,128)(2,1)S(1)} %get-tuple-element.19.refs_3_, ...), custom_call_target="tpu_custom_call" | custom-call | tf_op jit(solution)/shard_map/attend/pallas_call | solution.py:38
  (30 shorter events, 0.2 us)
Async XLA Ops:
  0.7 1.1 copy-start
  1.8 0.9 copy-start.2
  2.7 0.7 copy-start.11
  3.4 8.1 %copy-start.1 = (bf16[12,192,128]{2,1,0:T(8,128)(2,1)S(1)}, bf16[12,192,128]{2,1,0:T(8,128)(2,1)}, u32[]{:S(2)}) copy-start(bf16[12,192,128]{2,1,0:T(8,128)(2,1)} %refs_1_.4) | copy-start | bytes 1769476
  3.4 22.0 %copy-start.3 = (bf16[4,128,128]{2,1,0:T(8,128)(2,1)S(1)}, bf16[4,128,128]{2,1,0:T(8,128)(2,1)}, u32[]{:S(2)}) copy-start(bf16[4,128,128]{2,1,0:T(8,128)(2,1)} %refs_4_.3) | copy-start | bytes 393220
  6.2 21.3 %all-to-all-start = ((bf16[8,16,2304]{2,1,0:T(8,128)(2,1)}), bf16[8,16,2304]{2,1,0:T(8,128)(2,1)S(1)}, u32[]{:S(2)}, u32[]{:S(2)}) async-start(bf16[8,16,2304]{2,1,0:T(8,128)(2,1)} %get-tuple-element.14), calls=%async_computation | async-start | bytes 1179648 | tf_op jit(solution)/shard_map/all_to_all | solution.py:366
  11.5 13.8 %collective-permute-start.1 = (bf16[12,96,128]{2,1,0:T(8,128)(2,1)S(1)}, bf16[12,96,128]{2,1,0:T(8,128)(2,1)S(1)}, u32[]{:S(2)}, u32[]{:S(2)}) collective-permute-start(bf16[12,96,128]{2,1,0:T(8,128)(2,1)S(1)} %constant_dynamic-slice_fusion), channel_id=1, source_target_pairs={{0,8},{1,9},{2,10},{3,11},{4,12},{5,13},{6,14},{7,15},{8,0},{9,1},... | collective-permute-start | bytes 884744 | tf_op jit(solution)/shard_map/ppermute | solution.py:363
  27.6 35.3 %all-to-all-start.1 = ((bf16[8,16,4608]{2,1,0:T(8,128)(2,1)}), bf16[8,16,4608]{2,1,0:T(8,128)(2,1)S(1)}, u32[]{:S(2)}, u32[]{:S(2)}) async-start(bf16[8,16,4608]{2,1,0:T(8,128)(2,1)} %right.1), calls=%async_computation.1 | async-start | bytes 2359296 | tf_op jit(solution)/shard_map/all_to_all | solution.py:366
  34.4 26.5 %collective-permute-start = (bf16[8,16,2304]{2,1,0:T(8,128)(2,1)S(1)}, bf16[8,16,2304]{2,1,0:T(8,128)(2,1)S(1)}, u32[]{:S(2)}, u32[]{:S(2)}) collective-permute-start(bf16[8,16,2304]{2,1,0:T(8,128)(2,1)S(1)} %all-to-all-done.refs_1_), channel_id=1, source_target_pairs={{0,8},{1,9},{2,10},{3,11},{4,12},{5,13},{6,14},{7,15},{8,0},{9,1},... | collective-permute-start | bytes 1769480 | tf_op jit(solution)/shard_map/ppermute | solution.py:363
  66.4 4.9 %copy-start.15 = (bf16[128,4]{0,1:T(4,128)(2,1)S(1)}, bf16[128,4]{0,1:T(4,128)(2,1)}, u32[]{:S(2)}) copy-start(bf16[128,4]{0,1:T(4,128)(2,1)} %param.25) | copy-start | bytes 3076
  66.4 14.5 %copy-start.4 = (bf16[128,128]{1,0:T(8,128)(2,1)S(1)}, bf16[128,128]{1,0:T(8,128)(2,1)}, u32[]{:S(2)}) copy-start(bf16[128,128]{1,0:T(8,128)(2,1)} %refs_2_.2) | copy-start | bytes 98308
  66.4 14.5 %copy-start.5 = (bf16[128,128]{1,0:T(8,128)(2,1)S(1)}, bf16[128,128]{1,0:T(8,128)(2,1)}, u32[]{:S(2)}) copy-start(bf16[128,128]{1,0:T(8,128)(2,1)} %refs_4_.4) | copy-start | bytes 98308
  66.4 14.5 %copy-start.12 = (f32[128]{0:T(128)S(1)}, f32[128]{0:T(128)}, u32[]{:S(2)}) copy-start(f32[128]{0:T(128)} %param.16) | copy-start | bytes 1540
  66.4 14.5 %copy-start.13 = (f32[128]{0:T(128)S(1)}, f32[128]{0:T(128)}, u32[]{:S(2)}) copy-start(f32[128]{0:T(128)} %param.19) | copy-start | bytes 1540
  66.4 14.5 %copy-start.14 = (f32[128]{0:T(128)S(1)}, f32[128]{0:T(128)}, u32[]{:S(2)}) copy-start(f32[128]{0:T(128)} %param.21) | copy-start | bytes 1540
  66.4 14.4 %all-to-all-start.2 = ((bf16[8,16,2304]{2,1,0:T(8,128)(2,1)}), bf16[8,16,2304]{2,1,0:T(8,128)(2,1)S(1)}, u32[]{:S(2)}, u32[]{:S(2)}) async-start(bf16[8,16,2304]{2,1,0:T(8,128)(2,1)} %outer.1), calls=%async_computation.2 | async-start | bytes 1179648 | tf_op jit(solution)/shard_map/all_to_all | solution.py:366
  80.9 17.6 %copy-start.7 = (bf16[128,128]{1,0:T(8,128)(2,1)S(1)}, bf16[128,128]{1,0:T(8,128)(2,1)}, u32[]{:S(2)}) copy-start(bf16[128,128]{1,0:T(8,128)(2,1)} %refs_1_.5) | copy-start | bytes 98308
  80.9 17.6 %copy-start.8 = (bf16[128,128]{1,0:T(8,128)(2,1)S(1)}, bf16[128,128]{1,0:T(8,128)(2,1)}, u32[]{:S(2)}) copy-start(bf16[128,128]{1,0:T(8,128)(2,1)} %refs_2_.3) | copy-start | bytes 98308
  80.9 17.6 %copy-start.9 = (bf16[128,128]{1,0:T(8,128)(2,1)S(1)}, bf16[128,128]{1,0:T(8,128)(2,1)}, u32[]{:S(2)}) copy-start(bf16[128,128]{1,0:T(8,128)(2,1)} %refs_3_.3) | copy-start | bytes 98308
  80.9 17.6 %copy-start.10 = (bf16[128,128]{1,0:T(8,128)(2,1)S(1)}, bf16[128,128]{1,0:T(8,128)(2,1)}, u32[]{:S(2)}) copy-start(bf16[128,128]{1,0:T(8,128)(2,1)} %refs_4_.5) | copy-start | bytes 98308
  84.8 15.2 %copy-start.6 = (bf16[128,128]{1,0:T(8,128)(2,1)S(1)}, bf16[128,128]{1,0:T(8,128)(2,1)}, u32[]{:S(2)}) copy-start(bf16[128,128]{1,0:T(8,128)(2,1)} %refs_6_.2) | copy-start | bytes 98308
  84.8 4.8 %collective-permute-start.2 = (bf16[1,48,192]{2,1,0:T(8,128)(2,1)S(1)}, bf16[1,48,192]{2,1,0:T(8,128)(2,1)S(1)}, u32[]{:S(2)}, u32[]{:S(2)}) collective-permute-start(bf16[1,48,192]{2,1,0:T(8,128)(2,1)S(1)} %bitcast.8), channel_id=1, source_target_pairs={{0,8},{1,9},{2,10},{3,11},{4,12},{5,13},{6,14},{7,15},{8,0},{9,1},... | collective-permute-start | bytes 55304 | tf_op jit(solution)/shard_map/ppermute | solution.py:330
  89.6 4.2 %collective-permute-start.3 = (bf16[2,48,192]{2,1,0:T(8,128)(2,1)S(1)}, bf16[2,48,192]{2,1,0:T(8,128)(2,1)S(1)}, u32[]{:S(2)}, u32[]{:S(2)}) collective-permute-start(bf16[2,48,192]{2,1,0:T(8,128)(2,1)S(1)} %pad_maximum_fusion.2), channel_id=1, source_target_pairs={{0,4},{1,5},{2,6},{3,7},{4,0},{5,1},{6,2},{7,3},{8,12},{9,13},{10,... | collective-permute-start | bytes 110600 | tf_op jit(solution)/shard_map/ppermute | solution.py:330
  93.7 4.7 %collective-permute-start.4 = (bf16[4,48,192]{2,1,0:T(8,128)(2,1)S(1)}, bf16[4,48,192]{2,1,0:T(8,128)(2,1)S(1)}, u32[]{:S(2)}, u32[]{:S(2)}) collective-permute-start(bf16[4,48,192]{2,1,0:T(8,128)(2,1)S(1)} %pad_maximum_fusion.1), channel_id=1, source_target_pairs={{0,2},{1,3},{2,0},{3,1},{4,6},{5,7},{6,4},{7,5},{8,10},{9,11},{10,... | collective-permute-start | bytes 221192 | tf_op jit(solution)/shard_map/ppermute | solution.py:330
  98.5 1.5 %collective-permute-start.5 = (bf16[8,48,192]{2,1,0:T(8,128)(2,1)S(1)}, bf16[8,48,192]{2,1,0:T(8,128)(2,1)S(1)}, u32[]{:S(2)}, u32[]{:S(2)}) collective-permute-start(bf16[8,48,192]{2,1,0:T(8,128)(2,1)S(1)} %pad_maximum_fusion), channel_id=1, source_target_pairs={{0,1},{1,0},{2,3},{3,2},{4,5},{5,4},{6,7},{7,6},{8,9},{9,8},{10,11... | collective-permute-start | bytes 442376 | tf_op jit(solution)/shard_map/ppermute | solution.py:330

commit v5 on v3

--- a/solution.py
+++ b/solution.py
@@ -60,16 +60,18 @@
         self.block_tiles = -(-self.block // self.chans)
 
 
-def edges_kernel(sz, len_ref, x_ref, ln_ref, w_ref, *refs):
-    near, far, pair = refs[: sz.group], refs[sz.group : 2 * sz.group], refs[2 * sz.group : -2]
-    norm_ref, pair_ref = refs[-2:]
+def edges_kernel(sz, len_ref, x_ref, ln_ref, w_ref, out_ref, *refs):
+    near, pair = refs[: sz.group], refs[sz.group : 2 * sz.group]
+    norm_ref, pair_ref = refs[2 * sz.group :]
     length, first, me = len_ref[0], len_ref[1], len_ref[2]
     cd, ch = sz.chans, sz.channels
     mine = me & (sz.group - 1)
     r = lax.broadcasted_iota(jnp.int32, (ch, ch), 0)
     e = lax.broadcasted_iota(jnp.int32, (ch, ch), 1)
-    pick = (((r // cd) ^ mine) * cd + r % cd == e).astype(BF16)
-    weights = [dot(pick, w_ref[p], 1, 1).astype(BF16) for p in range(4)]
+    plain = (r == e).astype(BF16)
+    slots = (((r // cd) ^ mine) * cd + r % cd == e).astype(BF16)
+    picks = (plain, plain, slots, slots)
+    weights = [dot(pick, w_ref[p], 1, 1).astype(BF16) for p, pick in enumerate(picks)]
     gate_w = jnp.concatenate([weights[0], weights[2]], axis=0)
     value_w = jnp.concatenate([weights[1], weights[3]], axis=0)
     gain = ln_ref[...]
@@ -85,7 +87,7 @@
             norm_ref[pl.ds(sz.rows * main + q * LANES + h * sz.rest, sz.rest), :] = normed[main:]
     for r in range(sz.group):
         for t in range(sz.block_tiles):
-            at = (2 * sz.tiles + t) * LANES
+            at = (sz.tiles + t) * LANES
             rows = slice(t * cd, (t + 1) * cd)
             near[r][:, at : at + LANES] = pair_ref[me ^ r, rows, :].astype(BF16)
             pair[r][:, t * LANES : (t + 1) * LANES] = pair_ref[me ^ (sz.group + r), rows, :].astype(
@@ -110,26 +112,22 @@
         edge = sigmoid(dot(gate_w, n, 1, 1)) * dot(value_w, n, 1, 1) * mask
         edge = edge.astype(BF16)
         to = slice(tile * LANES, (tile + step) * LANES)
-        right_to = slice((sz.tiles + tile) * LANES, (sz.tiles + tile + step) * LANES)
-        for r in range(sz.group):
-            left = edge[r * cd : (r + 1) * cd]
-            near[r][:, to] = left
-            far[r][:, to] = left
-            near[r][:, right_to] = edge[ch + r * cd : ch + (r + 1) * cd]
-
-
-def outer_kernel(sz, len_ref, *refs):
-    near, far = refs[: sz.group], refs[sz.group : 2 * sz.group]
-    outs = refs[2 * sz.group : 3 * sz.group]
-    lmain_ref, lrest_ref, rmain_ref, rrest_ref, omain_ref, orest_ref = refs[3 * sz.group :]
-    me = len_ref[2]
-    mine = me & (sz.group - 1)
+        for g in range(sz.group):
+            left = edge[g * cd : (g + 1) * cd]
+            out_ref[g, :, to] = left
+            out_ref[sz.group + g, :, to] = left
+            near[g][:, to] = edge[ch + g * cd : ch + (g + 1) * cd]
+
+
+def outer_kernel(sz, len_ref, left_ref, *refs):
+    near, out_ref = refs[: sz.group], refs[sz.group]
+    lmain_ref, lrest_ref, rmain_ref, rrest_ref, omain_ref, orest_ref = refs[sz.group + 1 :]
+    mine = len_ref[2] & (sz.group - 1)
     cd, n, w, half = sz.chans, sz.crop, sz.whole, sz.half
 
-    def unpack(ref, base, owner, main_ref, rest_ref):
+    def unpack(ref, owner, main_ref, rest_ref):
         for tile in range(sz.tiles):
-            at = (base + tile) * LANES
-            block = ref[:, at : at + LANES].astype(F32)
+            block = ref[:, tile * LANES : (tile + 1) * LANES].astype(F32)
             if tile < sz.rows * w:
                 row, m = divmod(tile, w)
                 main_ref[m, pl.ds(pl.multiple_of((owner * sz.rows + row) * cd, 8), cd), :] = block
@@ -140,10 +138,10 @@
                     block, sz.rest, 1
                 )
 
+    for d in range(sz.devices):
+        unpack(left_ref.at[d], jnp.int32(d), lmain_ref, lrest_ref)
     for r in range(sz.group):
-        unpack(near[r], 0, me ^ r, lmain_ref, lrest_ref)
-        unpack(near[r], sz.tiles, mine ^ r, rmain_ref, rrest_ref)
-        unpack(far[r], 0, me ^ (sz.group + r), lmain_ref, lrest_ref)
+        unpack(near[r], mine ^ r, rmain_ref, rrest_ref)
 
     def matrix(c, size, main_ref, rest_ref):
         parts = [main_ref[m, pl.ds(c, size, stride=cd), :].astype(BF16) for m in range(w)]
@@ -161,32 +159,32 @@
             part = outer[:, w * LANES :]
             orest_ref[pl.ds(c, sz.columns, stride=cd), :] = jnp.concatenate([part, part], axis=1)
     low = lax.broadcasted_iota(jnp.int32, (cd, LANES), 1) < sz.rest
-    for r in range(sz.group):
-        start = (mine ^ r) * sz.rows
+    for g in range(sz.group):
+        start = g * sz.rows
         for tile in range(sz.tiles):
             if tile < sz.rows * w:
                 row, m = divmod(tile, w)
-                block = omain_ref[m, pl.ds(pl.multiple_of((start + row) * cd, 8), cd), :]
+                block = omain_ref[m, pl.ds((start + row) * cd, cd), :]
             else:
                 at = start + tile - sz.rows * w
                 block = jnp.where(
                     low,
-                    orest_ref[pl.ds(pl.multiple_of(at * cd, 8), cd), :],
-                    orest_ref[pl.ds(pl.multiple_of((at + half) * cd, 8), cd), :],
+                    orest_ref[pl.ds(at * cd, cd), :],
+                    orest_ref[pl.ds((at + half) * cd, cd), :],
                 )
-            outs[r][:, tile * LANES : (tile + 1) * LANES] = block.astype(BF16)
-
-
-def update_kernel(sz, len_ref, lnp_ref, gate_ref, lnh_ref, tri_ref, lna_ref, biasw_ref, *refs):
-    sums, near, pair = refs[: sz.group], refs[sz.group : 2 * sz.group], refs[2 * sz.group : -6]
-    first_ref, col_ref, bias_ref, cols_ref, brow_ref, sums_ref = refs[-6:]
+            out_ref[g, :, tile * LANES : (tile + 1) * LANES] = block.astype(BF16)
+
+
+def update_kernel(
+    sz, len_ref, lnp_ref, gate_ref, lnh_ref, tri_ref, lna_ref, biasw_ref, sums_ref, *refs
+):
+    near, pair = refs[: sz.group], refs[sz.group : 2 * sz.group]
+    first_ref, col_ref, bias_ref, cols_ref, brow_ref = refs[2 * sz.group :]
     n, w, half, ch, cd = sz.crop, sz.whole, sz.half, sz.channels, sz.chans
     me = len_ref[2]
-    mine = me & (sz.group - 1)
     for r in range(sz.group):
-        sums_ref[pl.ds(pl.multiple_of((mine ^ r) * cd, 8), cd), :] = sums[r][...].astype(F32)
         for ref, base, owner in (
-            (near[r], 2 * sz.tiles, me ^ r),
+            (near[r], sz.tiles, me ^ r),
             (pair[r], 0, me ^ (sz.group + r)),
         ):
             for t in range(sz.block_tiles):
@@ -197,7 +195,7 @@
     tri = tri_ref[...]
 
     def update(tile):
-        block = sums_ref[:, tile * LANES : (tile + 1) * LANES]
+        block = sums_ref[:, :, tile * LANES : (tile + 1) * LANES].astype(F32).reshape(ch, LANES)
         average = jnp.mean(block, axis=0, keepdims=True)
         centred = block - average
         variance = jnp.mean(centred * centred, axis=0, keepdims=True)
@@ -336,7 +334,6 @@
     n, cd = crop, sz.chans
     me = lax.axis_index(AXES).astype(jnp.int32)
     info = jnp.stack([length[0], me * rows, me])
-
     def bound(kernel, *extra):
         def run(*refs):
             return kernel(sz, *extra, *refs)
@@ -346,8 +343,8 @@
     shape = jax.ShapeDtypeStruct
     g, t, bt = sz.group, sz.tiles, sz.block_tiles
 
-    def slab(tiles):
-        return shape((cd, tiles * LANES), BF16)
+    def slab(tiles, *lead):
+        return shape((*lead, cd, tiles * LANES), BF16)
 
     def send(blocks, offset):
         return [
@@ -357,9 +354,9 @@
             for r, block in enumerate(blocks)
         ]
 
-    made = call(
+    left, *others = call(
         bound(edges_kernel),
-        [slab(2 * t + bt)] * g + [slab(t)] * g + [slab(bt)] * g,
+        [slab(t, devices)] + [slab(t + bt)] * g + [slab(bt)] * g,
         (info, pair_rep, ln_pair[None], tri_in),
         scratch=[
             pltpu.VMEM((rows * crop, ch), BF16),
@@ -368,15 +365,13 @@
         smem=(0,),
         name="edges",
     )
-    far = send(made[g : 2 * g], g)
-    near = send(made[:g], 0)
-    late, far, near = lax.optimization_barrier((made[2 * g :], far, near))
-    pair = send(late, g)
+    left = lax.all_to_all(left, AXES, split_axis=0, concat_axis=0, tiled=True)
+    near = send(others[:g], 0)
     rest = sz.rest > 0
     outer = call(
         bound(outer_kernel),
-        [slab(t)] * g,
-        (info, *near, *far),
+        slab(t, g),
+        (info, left, *near),
         scratch=[
             pltpu.VMEM((sz.whole, n * cd, LANES), F32),
             pltpu.VMEM((n * cd if rest else 8, LANES), F32),
@@ -388,7 +383,12 @@
         smem=(0,),
         name="outer",
     )
-    sums = send(outer, 0)
+    late, outer = lax.optimization_barrier((others[g:], outer))
+    sums = lax.all_to_all(
+        outer, AXES, split_axis=0, concat_axis=0, tiled=True,
+        axis_index_groups=[list(range(g)), list(range(g, devices))],
+    )
+    pair = send(late, g)
     first, col, bias = call(
         bound(update_kernel),
         [
@@ -398,12 +398,11 @@
         ],
         (
             info, ln_pair[None], tri_gate, ln_hidden[None], tri_out, ln_att[None], att_bias,
-            *sums, *near, *pair,
+            sums, *near, *pair,
         ),
         scratch=[
             pltpu.VMEM((devices * sz.block + cd, ch), F32),
             pltpu.VMEM((rows * heads, n), F32),
-            pltpu.VMEM((ch, rows * n), F32),
         ],
         smem=(0,),
         name="update",

time: 110 us -> 101 us (0.918)
  starting transfers between devices: 49.7 us -> 36.4 us
  waiting for transfers between devices: 39.5 us -> 41.9 us
  Pallas kernels: 17.1 us -> 18.6 us
    ppermute x30 -> x15, starting transfers between devices: 48.2 us -> 23.3 us  [send(): lax.ppermute(block, AXES, [(d, d ^ offset ^ r) for d in range(devices)])]
    all_to_all x0 -> x2, starting transfers between devices: none -> 11.3 us  [the longest x1 7.38 us: shards(): left = lax.all_to_all(left, AXES, split_axis=0, concat_axis=0, tiled=True)]
    ppermute x30 -> x15, waiting for transfers between devices: 26.9 us -> 29.5 us  [send(): lax.ppermute(block, AXES, [(d, d ^ offset ^ r) for d in range(devices)])]
    pallas_call x5, Pallas kernels: 17.1 us -> 18.6 us  [call(): pl.pallas_call(kernel, out_shape=out_shape, in_specs=specs, out_specs=vme...]
  transfers between devices with their start and end apart: 34 -> 21, of which waited for: 15 -> 12; matrix products, arithmetic and copies ran while one was open for 0% -> 0% of each run, Pallas kernels for 3% -> 1%
where the time goes in v5:
time: 101 us
  waiting for transfers between devices  41.9 us (41%)
  starting transfers between devices  36.4 us (36%)
  Pallas kernels  18.6 us (18%)
  local copies, waits for them, and re-layouts  2.82 us (3%)
    ppermute x15, waiting for transfers between devices, send(): lax.ppermute(block, AXES, [(d, d ^ offset ^ r) for d in range(devices)])  29.5 us
    ppermute x15, starting transfers between devices, send(): lax.ppermute(block, AXES, [(d, d ^ offset ^ r) for d in range(devices)])  23.3 us
    pallas_call x5, Pallas kernels, call(): pl.pallas_call(kernel, out_shape=out_shape, in_specs=specs, out_specs=vme...  18.6 us
    ppermute x4, waiting for transfers between devices, spread(): got = lax.ppermute(held, AXES, [(d, d ^ bit) for d in range(devices)])  12.3 us
    all_to_all x1, starting transfers between devices, shards(): left = lax.all_to_all(left, AXES, split_axis=0, concat_axis=0, tiled=True)  7.38 us
    all_to_all x1, starting transfers between devices, shards(): lax.all_to_all(outer, AXES, split_axis=0, concat_axis=0, tiled=True, axis...  3.87 us
    unnamed x29, local copies, waits for them, and re-layouts  2.82 us
  transfers between devices with their start and end apart: 21, of which 12 were waited for; matrix products, arithmetic and copies ran while one was open for 0% of the time, Pallas kernels for 1%

profile of v5, /device:TPU:0, one launch (start us, length us, event | category | flops | bytes accessed | tf_op | source)
XLA Modules:
  0.0 100.7 jit_solution(17103455900291302183)
XLA Ops:
  0.7 1.1 %copy-done = bf16[12,192,128]{2,1,0:T(8,128)(2,1)S(1)} copy-done((bf16[12,192,128]{2,1,0:T(8,128)(2,1)S(1)}, bf16[12,192,128]{2,1,0:T(8,128)(2,1)}, u32[]{:S(2)}) %copy-start) | copy-done | bytes 589848
  1.8 0.9 copy-done.1
  2.7 0.7 copy-done.9
  3.4 3.3 %edges.1 = (bf16[16,16,2304]{2,1,0:T(8,128)(2,1)}, bf16[16,3456]{1,0:T(8,128)(2,1)S(1)}, bf16[16,3456]{1,0:T(8,128)(2,1)S(1)}, bf16[16,3456]{1,0:T(8,128)(2,1)S(...) custom-call(s32[3]{0:T(128)S(1)} %pad_add_fusion.refs_0_, ...), custom_call_target="tpu_custom_call" | custom-call | tf_op jit(solution)/shard_map/edges/pallas_call | solution.py:38
  6.7 7.4 %all-to-all-start = ((bf16[16,16,2304]{2,1,0:T(8,128)(2,1)}), bf16[16,16,2304]{2,1,0:T(8,128)(2,1)S(1)}, u32[]{:S(2)}, u32[]{:S(2)}) async-start(bf16[16,16,2304]{2,1,0:T(8,128)(2,1)} %get-tuple-element.46), calls=%async_computation | async-start | bytes 2359296 | tf_op jit(solution)/shard_map/all_to_all | solution.py:368
  14.5 1.7 %collective-permute-start.1 = (bf16[16,3456]{1,0:T(8,128)(2,1)S(1)}, bf16[16,3456]{1,0:T(8,128)(2,1)S(1)}, u32[]{:S(2)}, u32[]{:S(2)}) collective-permute-start(bf16[16,3456]{1,0:T(8,128)(2,1)S(1)} %get-tuple-element.49), channel_id=1, source_target_pairs={{0,2},{1,3},{2,0},{3,1},{4,6},{5,7},{6,4},{7,5},{8,10},{9,11},{10,... | collective-permute-start | bytes 331784 | tf_op jit(solution)/shard_map/ppermute | solution.py:353
  16.2 1.7 %collective-permute-start.3 = (bf16[16,3456]{1,0:T(8,128)(2,1)S(1)}, bf16[16,3456]{1,0:T(8,128)(2,1)S(1)}, u32[]{:S(2)}, u32[]{:S(2)}) collective-permute-start(bf16[16,3456]{1,0:T(8,128)(2,1)S(1)} %get-tuple-element.51), channel_id=1, source_target_pairs={{0,4},{1,5},{2,6},{3,7},{4,0},{5,1},{6,2},{7,3},{8,12},{9,13},{10,... | collective-permute-start | bytes 331784 | tf_op jit(solution)/shard_map/ppermute | solution.py:353
  18.0 2.6 %collective-permute-start.5 = (bf16[16,3456]{1,0:T(8,128)(2,1)S(1)}, bf16[16,3456]{1,0:T(8,128)(2,1)S(1)}, u32[]{:S(2)}, u32[]{:S(2)}) collective-permute-start(bf16[16,3456]{1,0:T(8,128)(2,1)S(1)} %get-tuple-element.53), channel_id=1, source_target_pairs={{0,6},{1,7},{2,4},{3,5},{4,2},{5,3},{6,0},{7,1},{8,14},{9,15},{10,... | collective-permute-start | bytes 331784 | tf_op jit(solution)/shard_map/ppermute | solution.py:353
  20.6 7.5 %collective-permute-done.1.refs_4_.refs_10_ = bf16[16,3456]{1,0:T(8,128)(2,1)S(1)} collective-permute-done((bf16[16,3456]{1,0:T(8,128)(2,1)S(1)}, bf16[16,3456]{1,0:T(8,128)(2,1)S(1)}, u32[]{:S(2)}, u32[]{:S(2)}) %collective-permute-start.1) | collective-permute-done | bytes 110624 | tf_op jit(solution)/shard_map/ppermute | solution.py:353
  28.1 2.9 %collective-permute-done.2.refs_5_.refs_11_ = bf16[16,3456]{1,0:T(8,128)(2,1)S(1)} collective-permute-done((bf16[16,3456]{1,0:T(8,128)(2,1)S(1)}, bf16[16,3456]{1,0:T(8,128)(2,1)S(1)}, u32[]{:S(2)}, u32[]{:S(2)}) %collective-permute-start.2) | collective-permute-done | bytes 110624 | tf_op jit(solution)/shard_map/ppermute | solution.py:353
  31.0 5.9 %collective-permute-done.3.refs_6_.refs_12_ = bf16[16,3456]{1,0:T(8,128)(2,1)S(1)} collective-permute-done((bf16[16,3456]{1,0:T(8,128)(2,1)S(1)}, bf16[16,3456]{1,0:T(8,128)(2,1)S(1)}, u32[]{:S(2)}, u32[]{:S(2)}) %collective-permute-start.3) | collective-permute-done | bytes 110624 | tf_op jit(solution)/shard_map/ppermute | solution.py:353
  36.9 3.1 %collective-permute-done.4.refs_7_.refs_13_ = bf16[16,3456]{1,0:T(8,128)(2,1)S(1)} collective-permute-done((bf16[16,3456]{1,0:T(8,128)(2,1)S(1)}, bf16[16,3456]{1,0:T(8,128)(2,1)S(1)}, u32[]{:S(2)}, u32[]{:S(2)}) %collective-permute-start.4) | collective-permute-done | bytes 110624 | tf_op jit(solution)/shard_map/ppermute | solution.py:353
  40.0 4.7 %collective-permute-done.5.refs_8_.refs_14_ = bf16[16,3456]{1,0:T(8,128)(2,1)S(1)} collective-permute-done((bf16[16,3456]{1,0:T(8,128)(2,1)S(1)}, bf16[16,3456]{1,0:T(8,128)(2,1)S(1)}, u32[]{:S(2)}, u32[]{:S(2)}) %collective-permute-start.5) | collective-permute-done | bytes 110624 | tf_op jit(solution)/shard_map/ppermute | solution.py:353
  44.7 1.4 %collective-permute-done.6.refs_9_.refs_15_ = bf16[16,3456]{1,0:T(8,128)(2,1)S(1)} collective-permute-done((bf16[16,3456]{1,0:T(8,128)(2,1)S(1)}, bf16[16,3456]{1,0:T(8,128)(2,1)S(1)}, u32[]{:S(2)}, u32[]{:S(2)}) %collective-permute-start.6) | collective-permute-done | bytes 110624 | tf_op jit(solution)/shard_map/ppermute | solution.py:353
  46.1 3.5 %outer.1 = bf16[8,16,2304]{2,1,0:T(8,128)(2,1)} custom-call(s32[3]{0:T(128)S(1)} %pad_add_fusion.refs_0_, bf16[16,16,2304]{2,1,0:T(8,128)(2,1)S(1)} %all-to-all-done.refs_1_, bf16[16,3456]{1,0:T(8,128)(2,1)S(1)} %get-tuple-element.47.refs_2_.refs_8_, bf16[16,3456]{1,0:T(8,128)(2,1)S(1)} %collective-permute-done.refs_3_.refs_9_, ...), custom_call_target="tpu_custom_call" | custom-call | tf_op jit(solution)/shard_map/outer/pallas_call | solution.py:38
  49.6 3.9 %all-to-all-start.1 = ((bf16[8,16,2304]{2,1,0:T(8,128)(2,1)}), bf16[8,16,2304]{2,1,0:T(8,128)(2,1)S(1)}, u32[]{:S(2)}, u32[]{:S(2)}) async-start(bf16[8,16,2304]{2,1,0:T(8,128)(2,1)} %outer.1), calls=%async_computation.1 | async-start | bytes 1179648 | tf_op jit(solution)/shard_map/all_to_all | solution.py:387
  53.5 3.2 %collective-permute-start.7 = (bf16[16,1152]{1,0:T(8,128)(2,1)S(1)}, bf16[16,1152]{1,0:T(8,128)(2,1)S(1)}, u32[]{:S(2)}, u32[]{:S(2)}) collective-permute-start(bf16[16,1152]{1,0:T(8,128)(2,1)S(1)} %get-tuple-element.56), channel_id=1, source_target_pairs={{0,8},{1,9},{2,10},{3,11},{4,12},{5,13},{6,14},{7,15},{8,0},{9,1},... | collective-permute-start | bytes 110600 | tf_op jit(solution)/shard_map/ppermute | solution.py:353
  56.7 3.5 %collective-permute-start.9 = (bf16[16,1152]{1,0:T(8,128)(2,1)S(1)}, bf16[16,1152]{1,0:T(8,128)(2,1)S(1)}, u32[]{:S(2)}, u32[]{:S(2)}) collective-permute-start(bf16[16,1152]{1,0:T(8,128)(2,1)S(1)} %get-tuple-element.58), channel_id=1, source_target_pairs={{0,10},{1,11},{2,8},{3,9},{4,14},{5,15},{6,12},{7,13},{8,2},{9,3},... | collective-permute-start | bytes 110600 | tf_op jit(solution)/shard_map/ppermute | solution.py:353
  60.5 3.5 %collective-permute-start.11 = (bf16[16,1152]{1,0:T(8,128)(2,1)S(1)}, bf16[16,1152]{1,0:T(8,128)(2,1)S(1)}, u32[]{:S(2)}, u32[]{:S(2)}) collective-permute-start(bf16[16,1152]{1,0:T(8,128)(2,1)S(1)} %get-tuple-element.60), channel_id=1, source_target_pairs={{0,12},{1,13},{2,14},{3,15},{4,8},{5,9},{6,10},{7,11},{8,4},{9,5},... | collective-permute-start | bytes 110600 | tf_op jit(solution)/shard_map/ppermute | solution.py:353
  64.0 0.9 collective-permute-start.12
  64.9 3.3 %collective-permute-start.13 = (bf16[16,1152]{1,0:T(8,128)(2,1)S(1)}, bf16[16,1152]{1,0:T(8,128)(2,1)S(1)}, u32[]{:S(2)}, u32[]{:S(2)}) collective-permute-start(bf16[16,1152]{1,0:T(8,128)(2,1)S(1)} %get-tuple-element.62), channel_id=1, source_target_pairs={{0,14},{1,15},{2,12},{3,13},{4,10},{5,11},{6,8},{7,9},{8,6},{9,7},... | collective-permute-start | bytes 110600 | tf_op jit(solution)/shard_map/ppermute | solution.py:353
  68.2 2.1 %collective-permute-start.14 = (bf16[16,1152]{1,0:T(8,128)(2,1)S(1)}, bf16[16,1152]{1,0:T(8,128)(2,1)S(1)}, u32[]{:S(2)}, u32[]{:S(2)}) collective-permute-start(bf16[16,1152]{1,0:T(8,128)(2,1)S(1)} %get-tuple-element.63), channel_id=1, source_target_pairs={{0,15},{1,14},{2,13},{3,12},{4,11},{5,10},{6,9},{7,8},{8,7},{9,6},... | collective-permute-start | bytes 110600 | tf_op jit(solution)/shard_map/ppermute | solution.py:353
  70.5 1.3 %collective-permute-done.13.refs_22_ = bf16[16,1152]{1,0:T(8,128)(2,1)S(1)} collective-permute-done((bf16[16,1152]{1,0:T(8,128)(2,1)S(1)}, bf16[16,1152]{1,0:T(8,128)(2,1)S(1)}, u32[]{:S(2)}, u32[]{:S(2)}) %collective-permute-start.13) | collective-permute-done | bytes 36896 | tf_op jit(solution)/shard_map/ppermute | solution.py:353
  71.7 2.7 %collective-permute-done.14.refs_23_ = bf16[16,1152]{1,0:T(8,128)(2,1)S(1)} collective-permute-done((bf16[16,1152]{1,0:T(8,128)(2,1)S(1)}, bf16[16,1152]{1,0:T(8,128)(2,1)S(1)}, u32[]{:S(2)}, u32[]{:S(2)}) %collective-permute-start.14) | collective-permute-done | bytes 36896 | tf_op jit(solution)/shard_map/ppermute | solution.py:353
  74.5 3.8 %update.1 = (bf16[12,192,128]{2,1,0:T(8,128)(2,1)S(1)}, bf16[12,192,128]{2,1,0:T(8,128)(2,1)S(1)}, bf16[48,192]{1,0:T(8,128)(2,1)S(1)}) custom-call(s32[3]{0:T(128)S(1)} %pad_add_fusion.refs_0_, f32[1,128]{1,0:T(1,128)S(1)} %bitcast.13, bf16[128,128]{1,0:T(8,128)(2,1)S(1)} %copy-done.2, f32[1,128]{1,0:T(1,128)S(1)} %bitcast.14, ...), custom_call_target="tpu_custom_call" | custom-call | tf_op jit(solution)/shard_map/update/pallas_call | solution.py:38
  78.4 4.8 %collective-permute-done.15.refs_8_ = bf16[1,48,192]{2,1,0:T(8,128)(2,1)S(1)} collective-permute-done((bf16[1,48,192]{2,1,0:T(8,128)(2,1)S(1)}, bf16[1,48,192]{2,1,0:T(8,128)(2,1)S(1)}, u32[]{:S(2)}, u32[]{:S(2)}) %collective-permute-start.15) | collective-permute-done | bytes 18464 | tf_op jit(solution)/shard_map/ppermute | solution.py:318
  83.2 1.2 %collective-permute-start.16 = (bf16[2,48,192]{2,1,0:T(8,128)(2,1)S(1)}, bf16[2,48,192]{2,1,0:T(8,128)(2,1)S(1)}, u32[]{:S(2)}, u32[]{:S(2)}) collective-permute-start(bf16[2,48,192]{2,1,0:T(8,128)(2,1)S(1)} %pad_maximum_fusion.2), channel_id=1, source_target_pairs={{0,4},{1,5},{2,6},{3,7},{4,0},{5,1},{6,2},{7,3},{8,12},{9,13},{10,... | collective-permute-start | bytes 110600 | tf_op jit(solution)/shard_map/ppermute | solution.py:318
  84.4 2.9 %collective-permute-done.16.refs_9_ = bf16[2,48,192]{2,1,0:T(8,128)(2,1)S(1)} collective-permute-done((bf16[2,48,192]{2,1,0:T(8,128)(2,1)S(1)}, bf16[2,48,192]{2,1,0:T(8,128)(2,1)S(1)}, u32[]{:S(2)}, u32[]{:S(2)}) %collective-permute-start.16) | collective-permute-done | bytes 36896 | tf_op jit(solution)/shard_map/ppermute | solution.py:318
  87.4 0.6 collective-permute-start.17
  88.0 4.1 %collective-permute-done.17.refs_10_ = bf16[4,48,192]{2,1,0:T(8,128)(2,1)S(1)} collective-permute-done((bf16[4,48,192]{2,1,0:T(8,128)(2,1)S(1)}, bf16[4,48,192]{2,1,0:T(8,128)(2,1)S(1)}, u32[]{:S(2)}, u32[]{:S(2)}) %collective-permute-start.17) | collective-permute-done | bytes 73760 | tf_op jit(solution)/shard_map/ppermute | solution.py:318
  92.2 0.9 project.1
  93.6 7.1 %attend.1 = bf16[12,192,128]{2,1,0:T(8,128)(2,1)} custom-call(s32[3]{0:T(128)S(1)} %pad_add_fusion.refs_0_, bf16[12,192,128]{2,1,0:T(8,128)(2,1)S(1)} %get-tuple-element.65.refs_1_, bf16[12,192,128]{2,1,0:T(8,128)(2,1)S(1)} %get-tuple-element.66.refs_2_, bf16[12,128,192]{2,1,0:T(8,128)(2,1)S(1)} %get-tuple-element.67.refs_3_, ...), custom_call_target="tpu_custom_call" | custom-call | tf_op jit(solution)/shard_map/attend/pallas_call | solution.py:38
  (48 shorter events, 1.8 us)
Async XLA Ops:
  6.7 39.4 %all-to-all-start = ((bf16[16,16,2304]{2,1,0:T(8,128)(2,1)}), bf16[16,16,2304]{2,1,0:T(8,128)(2,1)S(1)}, u32[]{:S(2)}, u32[]{:S(2)}) async-start(bf16[16,16,2304]{2,1,0:T(8,128)(2,1)} %get-tuple-element.46), calls=%async_computation | async-start | bytes 2359296 | tf_op jit(solution)/shard_map/all_to_all | solution.py:368
  14.1 3.9 %collective-permute-start = (bf16[16,3456]{1,0:T(8,128)(2,1)S(1)}, bf16[16,3456]{1,0:T(8,128)(2,1)S(1)}, u32[]{:S(2)}, u32[]{:S(2)}) collective-permute-start(bf16[16,3456]{1,0:T(8,128)(2,1)S(1)} %get-tuple-element.48), channel_id=1, source_target_pairs={{0,1},{1,0},{2,3},{3,2},{4,5},{5,4},{6,7},{7,6},{8,9},{9,8},{10,11... | collective-permute-start | bytes 331784 | tf_op jit(solution)/shard_map/ppermute | solution.py:353
  14.5 13.6 %collective-permute-start.1 = (bf16[16,3456]{1,0:T(8,128)(2,1)S(1)}, bf16[16,3456]{1,0:T(8,128)(2,1)S(1)}, u32[]{:S(2)}, u32[]{:S(2)}) collective-permute-start(bf16[16,3456]{1,0:T(8,128)(2,1)S(1)} %get-tuple-element.49), channel_id=1, source_target_pairs={{0,2},{1,3},{2,0},{3,1},{4,6},{5,7},{6,4},{7,5},{8,10},{9,11},{10,... | collective-permute-start | bytes 331784 | tf_op jit(solution)/shard_map/ppermute | solution.py:353
  16.2 14.8 %collective-permute-start.2 = (bf16[16,3456]{1,0:T(8,128)(2,1)S(1)}, bf16[16,3456]{1,0:T(8,128)(2,1)S(1)}, u32[]{:S(2)}, u32[]{:S(2)}) collective-permute-start(bf16[16,3456]{1,0:T(8,128)(2,1)S(1)} %get-tuple-element.50), channel_id=1, source_target_pairs={{0,3},{1,2},{2,1},{3,0},{4,7},{5,6},{6,5},{7,4},{8,11},{9,10},{10,... | collective-permute-start | bytes 331784 | tf_op jit(solution)/shard_map/ppermute | solution.py:353
  16.2 20.7 %collective-permute-start.3 = (bf16[16,3456]{1,0:T(8,128)(2,1)S(1)}, bf16[16,3456]{1,0:T(8,128)(2,1)S(1)}, u32[]{:S(2)}, u32[]{:S(2)}) collective-permute-start(bf16[16,3456]{1,0:T(8,128)(2,1)S(1)} %get-tuple-element.51), channel_id=1, source_target_pairs={{0,4},{1,5},{2,6},{3,7},{4,0},{5,1},{6,2},{7,3},{8,12},{9,13},{10,... | collective-permute-start | bytes 331784 | tf_op jit(solution)/shard_map/ppermute | solution.py:353
  17.9 22.1 %collective-permute-start.4 = (bf16[16,3456]{1,0:T(8,128)(2,1)S(1)}, bf16[16,3456]{1,0:T(8,128)(2,1)S(1)}, u32[]{:S(2)}, u32[]{:S(2)}) collective-permute-start(bf16[16,3456]{1,0:T(8,128)(2,1)S(1)} %get-tuple-element.52), channel_id=1, source_target_pairs={{0,5},{1,4},{2,7},{3,6},{4,1},{5,0},{6,3},{7,2},{8,13},{9,12},{10,... | collective-permute-start | bytes 331784 | tf_op jit(solution)/shard_map/ppermute | solution.py:353
  18.0 26.7 %collective-permute-start.5 = (bf16[16,3456]{1,0:T(8,128)(2,1)S(1)}, bf16[16,3456]{1,0:T(8,128)(2,1)S(1)}, u32[]{:S(2)}, u32[]{:S(2)}) collective-permute-start(bf16[16,3456]{1,0:T(8,128)(2,1)S(1)} %get-tuple-element.53), channel_id=1, source_target_pairs={{0,6},{1,7},{2,4},{3,5},{4,2},{5,3},{6,0},{7,1},{8,14},{9,15},{10,... | collective-permute-start | bytes 331784 | tf_op jit(solution)/shard_map/ppermute | solution.py:353
  28.1 18.0 %collective-permute-start.6 = (bf16[16,3456]{1,0:T(8,128)(2,1)S(1)}, bf16[16,3456]{1,0:T(8,128)(2,1)S(1)}, u32[]{:S(2)}, u32[]{:S(2)}) collective-permute-start(bf16[16,3456]{1,0:T(8,128)(2,1)S(1)} %get-tuple-element.54), channel_id=1, source_target_pairs={{0,7},{1,6},{2,5},{3,4},{4,3},{5,2},{6,1},{7,0},{8,15},{9,14},{10,... | collective-permute-start | bytes 331784 | tf_op jit(solution)/shard_map/ppermute | solution.py:353
  49.6 20.7 %copy-start.13 = (bf16[128,4]{0,1:T(4,128)(2,1)S(1)}, bf16[128,4]{0,1:T(4,128)(2,1)}, u32[]{:S(2)}) copy-start(bf16[128,4]{0,1:T(4,128)(2,1)} %param.25) | copy-start | bytes 3076
  49.6 24.8 %copy-start.2 = (bf16[128,128]{1,0:T(8,128)(2,1)S(1)}, bf16[128,128]{1,0:T(8,128)(2,1)}, u32[]{:S(2)}) copy-start(bf16[128,128]{1,0:T(8,128)(2,1)} %refs_2_.2) | copy-start | bytes 98308
  49.6 24.8 %copy-start.3 = (bf16[128,128]{1,0:T(8,128)(2,1)S(1)}, bf16[128,128]{1,0:T(8,128)(2,1)}, u32[]{:S(2)}) copy-start(bf16[128,128]{1,0:T(8,128)(2,1)} %refs_4_.2) | copy-start | bytes 98308
  49.6 24.8 %copy-start.10 = (f32[128]{0:T(128)S(1)}, f32[128]{0:T(128)}, u32[]{:S(2)}) copy-start(f32[128]{0:T(128)} %param.16) | copy-start | bytes 1540
  49.6 24.8 %copy-start.11 = (f32[128]{0:T(128)S(1)}, f32[128]{0:T(128)}, u32[]{:S(2)}) copy-start(f32[128]{0:T(128)} %param.19) | copy-start | bytes 1540
  49.6 24.8 %copy-start.12 = (f32[128]{0:T(128)S(1)}, f32[128]{0:T(128)}, u32[]{:S(2)}) copy-start(f32[128]{0:T(128)} %param.21) | copy-start | bytes 1540
  49.6 24.8 %all-to-all-start.1 = ((bf16[8,16,2304]{2,1,0:T(8,128)(2,1)}), bf16[8,16,2304]{2,1,0:T(8,128)(2,1)S(1)}, u32[]{:S(2)}, u32[]{:S(2)}) async-start(bf16[8,16,2304]{2,1,0:T(8,128)(2,1)} %outer.1), calls=%async_computation.1 | async-start | bytes 1179648 | tf_op jit(solution)/shard_map/all_to_all | solution.py:387
  53.5 10.5 %collective-permute-start.7 = (bf16[16,1152]{1,0:T(8,128)(2,1)S(1)}, bf16[16,1152]{1,0:T(8,128)(2,1)S(1)}, u32[]{:S(2)}, u32[]{:S(2)}) collective-permute-start(bf16[16,1152]{1,0:T(8,128)(2,1)S(1)} %get-tuple-element.56), channel_id=1, source_target_pairs={{0,8},{1,9},{2,10},{3,11},{4,12},{5,13},{6,14},{7,15},{8,0},{9,1},... | collective-permute-start | bytes 110600 | tf_op jit(solution)/shard_map/ppermute | solution.py:353
  56.7 8.2 %collective-permute-start.8 = (bf16[16,1152]{1,0:T(8,128)(2,1)S(1)}, bf16[16,1152]{1,0:T(8,128)(2,1)S(1)}, u32[]{:S(2)}, u32[]{:S(2)}) collective-permute-start(bf16[16,1152]{1,0:T(8,128)(2,1)S(1)} %get-tuple-element.57), channel_id=1, source_target_pairs={{0,9},{1,8},{2,11},{3,10},{4,13},{5,12},{6,15},{7,14},{8,1},{9,0},... | collective-permute-start | bytes 110600 | tf_op jit(solution)/shard_map/ppermute | solution.py:353
  56.7 11.6 %collective-permute-start.9 = (bf16[16,1152]{1,0:T(8,128)(2,1)S(1)}, bf16[16,1152]{1,0:T(8,128)(2,1)S(1)}, u32[]{:S(2)}, u32[]{:S(2)}) collective-permute-start(bf16[16,1152]{1,0:T(8,128)(2,1)S(1)} %get-tuple-element.58), channel_id=1, source_target_pairs={{0,10},{1,11},{2,8},{3,9},{4,14},{5,15},{6,12},{7,13},{8,2},{9,3},... | collective-permute-start | bytes 110600 | tf_op jit(solution)/shard_map/ppermute | solution.py:353
  60.2 10.3 %collective-permute-start.10 = (bf16[16,1152]{1,0:T(8,128)(2,1)S(1)}, bf16[16,1152]{1,0:T(8,128)(2,1)S(1)}, u32[]{:S(2)}, u32[]{:S(2)}) collective-permute-start(bf16[16,1152]{1,0:T(8,128)(2,1)S(1)} %get-tuple-element.59), channel_id=1, source_target_pairs={{0,11},{1,10},{2,9},{3,8},{4,15},{5,14},{6,13},{7,12},{8,3},{9,2},... | collective-permute-start | bytes 110600 | tf_op jit(solution)/shard_map/ppermute | solution.py:353
  60.5 10.0 %collective-permute-start.11 = (bf16[16,1152]{1,0:T(8,128)(2,1)S(1)}, bf16[16,1152]{1,0:T(8,128)(2,1)S(1)}, u32[]{:S(2)}, u32[]{:S(2)}) collective-permute-start(bf16[16,1152]{1,0:T(8,128)(2,1)S(1)} %get-tuple-element.60), channel_id=1, source_target_pairs={{0,12},{1,13},{2,14},{3,15},{4,8},{5,9},{6,10},{7,11},{8,4},{9,5},... | collective-permute-start | bytes 110600 | tf_op jit(solution)/shard_map/ppermute | solution.py:353
  64.0 6.5 %collective-permute-start.12 = (bf16[16,1152]{1,0:T(8,128)(2,1)S(1)}, bf16[16,1152]{1,0:T(8,128)(2,1)S(1)}, u32[]{:S(2)}, u32[]{:S(2)}) collective-permute-start(bf16[16,1152]{1,0:T(8,128)(2,1)S(1)} %get-tuple-element.61), channel_id=1, source_target_pairs={{0,13},{1,12},{2,15},{3,14},{4,9},{5,8},{6,11},{7,10},{8,5},{9,4},... | collective-permute-start | bytes 110600 | tf_op jit(solution)/shard_map/ppermute | solution.py:353
  64.9 6.8 %collective-permute-start.13 = (bf16[16,1152]{1,0:T(8,128)(2,1)S(1)}, bf16[16,1152]{1,0:T(8,128)(2,1)S(1)}, u32[]{:S(2)}, u32[]{:S(2)}) collective-permute-start(bf16[16,1152]{1,0:T(8,128)(2,1)S(1)} %get-tuple-element.62), channel_id=1, source_target_pairs={{0,14},{1,15},{2,12},{3,13},{4,10},{5,11},{6,8},{7,9},{8,6},{9,7},... | collective-permute-start | bytes 110600 | tf_op jit(solution)/shard_map/ppermute | solution.py:353
  68.2 6.2 %collective-permute-start.14 = (bf16[16,1152]{1,0:T(8,128)(2,1)S(1)}, bf16[16,1152]{1,0:T(8,128)(2,1)S(1)}, u32[]{:S(2)}, u32[]{:S(2)}) collective-permute-start(bf16[16,1152]{1,0:T(8,128)(2,1)S(1)} %get-tuple-element.63), channel_id=1, source_target_pairs={{0,15},{1,14},{2,13},{3,12},{4,11},{5,10},{6,9},{7,8},{8,7},{9,6},... | collective-permute-start | bytes 110600 | tf_op jit(solution)/shard_map/ppermute | solution.py:353
  74.5 17.7 %copy-start.5 = (bf16[128,128]{1,0:T(8,128)(2,1)S(1)}, bf16[128,128]{1,0:T(8,128)(2,1)}, u32[]{:S(2)}) copy-start(bf16[128,128]{1,0:T(8,128)(2,1)} %refs_1_.3) | copy-start | bytes 98308
  74.5 17.7 %copy-start.6 = (bf16[128,128]{1,0:T(8,128)(2,1)S(1)}, bf16[128,128]{1,0:T(8,128)(2,1)}, u32[]{:S(2)}) copy-start(bf16[128,128]{1,0:T(8,128)(2,1)} %refs_2_.3) | copy-start | bytes 98308
  74.5 17.7 %copy-start.7 = (bf16[128,128]{1,0:T(8,128)(2,1)S(1)}, bf16[128,128]{1,0:T(8,128)(2,1)}, u32[]{:S(2)}) copy-start(bf16[128,128]{1,0:T(8,128)(2,1)} %refs_3_.3) | copy-start | bytes 98308
  74.5 17.7 %copy-start.8 = (bf16[128,128]{1,0:T(8,128)(2,1)S(1)}, bf16[128,128]{1,0:T(8,128)(2,1)}, u32[]{:S(2)}) copy-start(bf16[128,128]{1,0:T(8,128)(2,1)} %refs_4_.3) | copy-start | bytes 98308
  78.3 15.3 %copy-start.4 = (bf16[128,128]{1,0:T(8,128)(2,1)S(1)}, bf16[128,128]{1,0:T(8,128)(2,1)}, u32[]{:S(2)}) copy-start(bf16[128,128]{1,0:T(8,128)(2,1)} %refs_6_.2) | copy-start | bytes 98308
  78.3 4.8 %collective-permute-start.15 = (bf16[1,48,192]{2,1,0:T(8,128)(2,1)S(1)}, bf16[1,48,192]{2,1,0:T(8,128)(2,1)S(1)}, u32[]{:S(2)}, u32[]{:S(2)}) collective-permute-start(bf16[1,48,192]{2,1,0:T(8,128)(2,1)S(1)} %bitcast.7), channel_id=1, source_target_pairs={{0,8},{1,9},{2,10},{3,11},{4,12},{5,13},{6,14},{7,15},{8,0},{9,1},... | collective-permute-start | bytes 55304 | tf_op jit(solution)/shard_map/ppermute | solution.py:318
  83.2 4.2 %collective-permute-start.16 = (bf16[2,48,192]{2,1,0:T(8,128)(2,1)S(1)}, bf16[2,48,192]{2,1,0:T(8,128)(2,1)S(1)}, u32[]{:S(2)}, u32[]{:S(2)}) collective-permute-start(bf16[2,48,192]{2,1,0:T(8,128)(2,1)S(1)} %pad_maximum_fusion.2), channel_id=1, source_target_pairs={{0,4},{1,5},{2,6},{3,7},{4,0},{5,1},{6,2},{7,3},{8,12},{9,13},{10,... | collective-permute-start | bytes 110600 | tf_op jit(solution)/shard_map/ppermute | solution.py:318
  87.4 4.7 %collective-permute-start.17 = (bf16[4,48,192]{2,1,0:T(8,128)(2,1)S(1)}, bf16[4,48,192]{2,1,0:T(8,128)(2,1)S(1)}, u32[]{:S(2)}, u32[]{:S(2)}) collective-permute-start(bf16[4,48,192]{2,1,0:T(8,128)(2,1)S(1)} %pad_maximum_fusion.1), channel_id=1, source_target_pairs={{0,2},{1,3},{2,0},{3,1},{4,6},{5,7},{6,4},{7,5},{8,10},{9,11},{10,... | collective-permute-start | bytes 221192 | tf_op jit(solution)/shard_map/ppermute | solution.py:318
  92.1 1.5 %collective-permute-start.18 = (bf16[8,48,192]{2,1,0:T(8,128)(2,1)S(1)}, bf16[8,48,192]{2,1,0:T(8,128)(2,1)S(1)}, u32[]{:S(2)}, u32[]{:S(2)}) collective-permute-start(bf16[8,48,192]{2,1,0:T(8,128)(2,1)S(1)} %pad_maximum_fusion), channel_id=1, source_target_pairs={{0,1},{1,0},{2,3},{3,2},{4,5},{5,4},{6,7},{7,6},{8,9},{9,8},{10,11... | collective-permute-start | bytes 442376 | tf_op jit(solution)/shard_map/ppermute | solution.py:318
  (3 other events, 2.6 us)

commit v6 on v2

--- a/solution.py
+++ b/solution.py
@@ -61,10 +61,11 @@
         self.channels = channels
 
         self.block = rows * rows
-        self.block_tiles = -(-self.block // (2 * self.chans))
-
-
-def edges_kernel(sz, len_ref, x_ref, ln_ref, w_ref, out_ref, norm_ref, pair_ref):
+        self.packed = self.fold * self.chans
+        self.block_tiles = -(-self.block // self.packed)
+
+
+def edges_kernel(sz, len_ref, x_ref, ln_ref, w_ref, out_ref, norm_ref):
     length, first = len_ref[0], len_ref[1]
     cd, two = sz.chans, 2 * sz.chans
     ch = sz.channels
@@ -78,17 +79,11 @@
     main = sz.whole * LANES
     for row in range(sz.rows):
         x = x_ref[row].astype(F32)
-        for d in range(sz.devices):
-            pair_ref[d, row * sz.rows : (row + 1) * sz.rows, :] = x[d * sz.rows : (d + 1) * sz.rows]
         normed = norm_last(x, gain).astype(BF16)
         norm_ref[pl.ds(row * main, main), :] = normed[:main]
         if sz.rest:
             h, q = divmod(row, sz.half)
             norm_ref[pl.ds(sz.rows * main + q * LANES + h * sz.rest, sz.rest), :] = normed[main:]
-    for d in range(sz.devices):
-        for t in range(sz.block_tiles):
-            at = (sz.tiles + t) * LANES
-            out_ref[d, :, at : at + LANES] = pair_ref[d, t * two : (t + 1) * two, :].astype(BF16)
     lane = lax.broadcasted_iota(jnp.int32, (1, LANES), 1)
 
     def live(tile):
@@ -111,7 +106,7 @@
         ).astype(BF16)
 
 
-def outer_kernel(sz, e_ref, out_ref, main_ref, rest_ref, omain_ref, orest_ref):
+def outer_kernel(sz, e_ref, x_ref, out_ref, main_ref, rest_ref, omain_ref, orest_ref, pair_ref):
     cd, two = sz.chans, 2 * sz.chans
     n, w, half = sz.crop, sz.whole, sz.half
     for s in range(sz.devices):
@@ -153,18 +148,28 @@
                     blocks.append(jnp.where(low, one, orest_ref[pl.ds((at + half) * cd, cd), :]))
             block = jnp.concatenate(blocks, axis=0) if len(blocks) > 1 else blocks[0]
             out_ref[s, :, t * LANES : (t + 1) * LANES] = block.astype(BF16)
+    for row in range(sz.rows):
+        x = x_ref[row].astype(F32)
+        for d in range(sz.devices):
+            pair_ref[d, row * sz.rows : (row + 1) * sz.rows, :] = x[d * sz.rows : (d + 1) * sz.rows]
+    high = sz.packed
+    for d in range(sz.devices):
+        for t in range(sz.block_tiles):
+            at = (sz.fold_tiles + t) * LANES
+            out_ref[d, :, at : at + LANES] = pair_ref[d, t * high : (t + 1) * high, :].astype(BF16)
 
 
 def update_kernel(
-    sz, o_ref, x_ref, lnp_ref, gate_ref, lnh_ref, tri_ref, lna_ref, biasw_ref,
+    sz, o_ref, lnp_ref, gate_ref, lnh_ref, tri_ref, lna_ref, biasw_ref,
     first_ref, col_ref, bias_ref, cols_ref, brow_ref,
 ):
     n, w, half, ch = sz.crop, sz.whole, sz.half, sz.channels
-    two = 2 * sz.chans
+    high = sz.packed
     for s in range(sz.devices):
         for t in range(sz.block_tiles):
-            at = (sz.tiles + t) * LANES
-            cols_ref[pl.ds(s * sz.block + t * two, two), :] = x_ref[s, :, at : at + LANES].astype(F32)
+            at = (sz.fold_tiles + t) * LANES
+            rows = pl.ds(s * sz.block + t * high, high)
+            cols_ref[rows, :] = o_ref[s, :, at : at + LANES].astype(F32)
     gain_h = jnp.transpose(jnp.broadcast_to(lnh_ref[...], (ch, ch)))
     tri = tri_ref[...]
 
@@ -320,11 +325,10 @@
     shape = jax.ShapeDtypeStruct
     edges = call(
         bound(edges_kernel),
-        shape((devices, 2 * cd, (sz.tiles + sz.block_tiles) * LANES), BF16),
+        shape((devices, 2 * cd, sz.tiles * LANES), BF16),
         (info, pair_rep, ln_pair[None], tri_in),
         scratch=[
             pltpu.VMEM((rows * crop, ch), BF16),
-            pltpu.VMEM((devices, sz.block_tiles * 2 * cd, ch), F32),
         ],
         smem=(0,),
         name="edges",
@@ -333,13 +337,14 @@
     rest_rows = n if sz.rest else 8
     outer = call(
         bound(outer_kernel),
-        shape((devices, sz.fold * cd, rows * crop // sz.fold), BF16),
-        (edges,),
+        shape((devices, sz.packed, (sz.fold_tiles + sz.block_tiles) * LANES), BF16),
+        (edges, pair_rep),
         scratch=[
             pltpu.VMEM((sz.whole, n * 2 * cd, LANES), F32),
             pltpu.VMEM((rest_rows * 2 * cd, LANES), F32),
             pltpu.VMEM((sz.whole, n * cd, LANES), F32),
             pltpu.VMEM((rest_rows * cd, LANES), F32),
+            pltpu.VMEM((devices, sz.block_tiles * sz.packed, ch), F32),
         ],
         name="outer",
     )
@@ -351,9 +356,9 @@
             shape((rows, n, ch), BF16),
             shape((rows * heads, n), BF16),
         ],
-        (outer, edges, ln_pair[None], tri_gate, ln_hidden[None], tri_out, ln_att[None], att_bias),
+        (outer, ln_pair[None], tri_gate, ln_hidden[None], tri_out, ln_att[None], att_bias),
         scratch=[
-            pltpu.VMEM((devices * sz.block + 2 * cd, ch), F32),
+            pltpu.VMEM((devices * sz.block + sz.packed, ch), F32),
             pltpu.VMEM((rows * heads, n), F32),
         ],
         name="update",

time: 102 us -> 102 us (level)
  blocking collectives: 48.8 us -> 36.7 us
  waiting for transfers between devices: 24.6 us -> 33.5 us
  starting transfers between devices: 8.66 us -> 12.1 us
    all_to_all x1, blocking collectives: 48.8 us -> 36.7 us  [shards(): edges = lax.all_to_all(edges, AXES, split_axis=0, concat_axis=0, tiled=True)]
    all_to_all x1, waiting for transfers between devices: 15.3 us -> 24.7 us  [shards(): outer = lax.all_to_all(outer, AXES, split_axis=0, concat_axis=0, tiled=True)]
    ppermute x4, starting transfers between devices: 4.86 us -> 8.05 us  [spread(): got = lax.ppermute(held, AXES, [(d, d ^ bit) for d in range(devices)])]
where the time goes in v6:
time: 102 us
  blocking collectives  36.7 us (36%)
  waiting for transfers between devices  33.5 us (33%)
  Pallas kernels  16 us (16%)
  starting transfers between devices  12.1 us (12%)
  local copies, waits for them, and re-layouts  2.82 us (3%)
    all_to_all x1, blocking collectives, shards(): edges = lax.all_to_all(edges, AXES, split_axis=0, concat_axis=0, tiled=True)  36.7 us
    all_to_all x1, waiting for transfers between devices, shards(): outer = lax.all_to_all(outer, AXES, split_axis=0, concat_axis=0, tiled=True)  24.7 us
    pallas_call x5, Pallas kernels, call(): pl.pallas_call(kernel, out_shape=out_shape, in_specs=specs, out_specs=vme...  16 us
    ppermute x4, waiting for transfers between devices, spread(): got = lax.ppermute(held, AXES, [(d, d ^ bit) for d in range(devices)])  8.84 us
    ppermute x4, starting transfers between devices, spread(): got = lax.ppermute(held, AXES, [(d, d ^ bit) for d in range(devices)])  8.05 us
    all_to_all x1, starting transfers between devices, shards(): outer = lax.all_to_all(outer, AXES, split_axis=0, concat_axis=0, tiled=True)  4.02 us
    unnamed x29, local copies, waits for them, and re-layouts  2.82 us
  transfers between devices with their start and end apart: 5, of which 5 were waited for; matrix products, arithmetic and copies ran while one was open for 0% of the time, Pallas kernels for 1%

profile of v6, /device:TPU:0, one launch (start us, length us, event | category | flops | bytes accessed | tf_op | source)
XLA Modules:
  0.0 102.1 jit_solution(8779051497553069895)
XLA Ops:
  0.7 0.1 pad_add_fusion.refs_0_
  0.7 1.1 %copy-done = bf16[12,192,128]{2,1,0:T(8,128)(2,1)S(1)} copy-done((bf16[12,192,128]{2,1,0:T(8,128)(2,1)S(1)}, bf16[12,192,128]{2,1,0:T(8,128)(2,1)}, u32[]{:S(2)}) %copy-start) | copy-done | bytes 589848
  1.8 0.9 copy-done.1
  2.7 0.7 copy-done.9
  3.4 2.3 %edges.1 = bf16[16,16,2304]{2,1,0:T(8,128)(2,1)S(1)} custom-call(s32[3]{0:T(128)S(1)} %pad_add_fusion.refs_0_, bf16[12,192,128]{2,1,0:T(8,128)(2,1)S(1)} %copy-done, f32[1,128]{1,0:T(1,128)S(1)} %bitcast.12, bf16[4,128,128]{2,1,0:T(8,128)(2,1)S(1)} %copy-done.1), custom_call_target="tpu_custom_call" | custom-call | tf_op jit(solution)/shard_map/edges/pallas_call | solution.py:38
  5.6 36.7 %all_to_all.10.refs_0_ = bf16[16,16,2304]{2,1,0:T(8,128)(2,1)S(1)} all-to-all(bf16[16,16,2304]{2,1,0:T(8,128)(2,1)S(1)} %edges.1), channel_id=1, replica_groups=mesh['grp'=2,'row'=8,'node'=2] {'row','node'}, dimensions={0} | all-to-all | bytes 2359296 | tf_op jit(solution)/shard_map/all_to_all | solution.py:336
  42.3 2.6 %outer.1 = bf16[16,16,2304]{2,1,0:T(8,128)(2,1)} custom-call(bf16[16,16,2304]{2,1,0:T(8,128)(2,1)S(1)} %all_to_all.10.refs_0_, bf16[12,192,128]{2,1,0:T(8,128)(2,1)S(1)} %copy-done), custom_call_target="tpu_custom_call" | custom-call | tf_op jit(solution)/shard_map/outer/pallas_call | solution.py:38
  44.9 0.0 copy-start.11
  44.9 0.0 copy-start.12
  44.9 4.0 %all-to-all-start.1 = ((bf16[16,16,2304]{2,1,0:T(8,128)(2,1)}), bf16[16,16,2304]{2,1,0:T(8,128)(2,1)S(1)}, u32[]{:S(2)}, u32[]{:S(2)}) async-start(bf16[16,16,2304]{2,1,0:T(8,128)(2,1)} %outer.1), calls=%async_computation.1 | async-start | bytes 2359296 | tf_op jit(solution)/shard_map/all_to_all | solution.py:351
  49.0 0.0 copy-done.13
  49.0 0.0 copy-start.5
  49.0 0.0 copy-start.6
  49.0 0.0 copy-start.7
  49.0 0.0 copy-start.8
  49.0 0.1 copy.15.refs_6_
  49.1 24.7 %all-to-all-done.1.refs_0_ = bf16[16,16,2304]{2,1,0:T(8,128)(2,1)S(1)} async-done(((bf16[16,16,2304]{2,1,0:T(8,128)(2,1)}), bf16[16,16,2304]{2,1,0:T(8,128)(2,1)S(1)}, u32[]{:S(2)}, u32[]{:S(2)}) %all-to-all-start.1) | async-done | bytes 1179680 | tf_op jit(solution)/shard_map/all_to_all | solution.py:351
  73.8 0.0 copy-done.3
  73.8 0.0 copy-done.4
  73.8 0.0 copy-done.10
  73.9 0.0 copy-start.2
  73.9 3.2 %update.1 = (bf16[12,192,128]{2,1,0:T(8,128)(2,1)S(1)}, bf16[12,192,128]{2,1,0:T(8,128)(2,1)S(1)}, bf16[48,192]{1,0:T(8,128)(2,1)S(1)}) custom-call(bf16[16,16,2304]{2,1,0:T(8,128)(2,1)S(1)} %all-to-all-done.1.refs_0_, f32[1,128]{1,0:T(1,128)S(1)} %bitcast.13, bf16[128,128]{1,0:T(8,128)(2,1)S(1)} %copy-done.3, f32[1,128]{1,0:T(1,128)S(1)} %bitcast.14, ...), custom_call_target="tpu_custom_call" | custom-call | tf_op jit(solution)/shard_map/update/pallas_call | solution.py:38
  77.1 5.7 %collective-permute-start = (bf16[1,48,192]{2,1,0:T(8,128)(2,1)S(1)}, bf16[1,48,192]{2,1,0:T(8,128)(2,1)S(1)}, u32[]{:S(2)}, u32[]{:S(2)}) collective-permute-start(bf16[1,48,192]{2,1,0:T(8,128)(2,1)S(1)} %bitcast.7), channel_id=1, source_target_pairs={{0,8},{1,9},{2,10},{3,11},{4,12},{5,13},{6,14},{7,15},{8,0},{9,1},... | collective-permute-start | bytes 55304 | tf_op jit(solution)/shard_map/ppermute | solution.py:299
  82.8 1.8 %collective-permute-done.refs_8_ = bf16[1,48,192]{2,1,0:T(8,128)(2,1)S(1)} collective-permute-done((bf16[1,48,192]{2,1,0:T(8,128)(2,1)S(1)}, bf16[1,48,192]{2,1,0:T(8,128)(2,1)S(1)}, u32[]{:S(2)}, u32[]{:S(2)}) %collective-permute-start) | collective-permute-done | bytes 18464 | tf_op jit(solution)/shard_map/ppermute | solution.py:299
  84.6 1.1 %collective-permute-start.1 = (bf16[2,48,192]{2,1,0:T(8,128)(2,1)S(1)}, bf16[2,48,192]{2,1,0:T(8,128)(2,1)S(1)}, u32[]{:S(2)}, u32[]{:S(2)}) collective-permute-start(bf16[2,48,192]{2,1,0:T(8,128)(2,1)S(1)} %pad_maximum_fusion.2), channel_id=1, source_target_pairs={{0,4},{1,5},{2,6},{3,7},{4,0},{5,1},{6,2},{7,3},{8,12},{9,13},{10,... | collective-permute-start | bytes 110600 | tf_op jit(solution)/shard_map/ppermute | solution.py:299
  85.7 3.0 %collective-permute-done.1.refs_9_ = bf16[2,48,192]{2,1,0:T(8,128)(2,1)S(1)} collective-permute-done((bf16[2,48,192]{2,1,0:T(8,128)(2,1)S(1)}, bf16[2,48,192]{2,1,0:T(8,128)(2,1)S(1)}, u32[]{:S(2)}, u32[]{:S(2)}) %collective-permute-start.1) | collective-permute-done | bytes 36896 | tf_op jit(solution)/shard_map/ppermute | solution.py:299
  88.8 1.2 %collective-permute-start.2 = (bf16[4,48,192]{2,1,0:T(8,128)(2,1)S(1)}, bf16[4,48,192]{2,1,0:T(8,128)(2,1)S(1)}, u32[]{:S(2)}, u32[]{:S(2)}) collective-permute-start(bf16[4,48,192]{2,1,0:T(8,128)(2,1)S(1)} %pad_maximum_fusion.1), channel_id=1, source_target_pairs={{0,2},{1,3},{2,0},{3,1},{4,6},{5,7},{6,4},{7,5},{8,10},{9,11},{10,... | collective-permute-start | bytes 221192 | tf_op jit(solution)/shard_map/ppermute | solution.py:299
  89.9 3.5 %collective-permute-done.2.refs_10_ = bf16[4,48,192]{2,1,0:T(8,128)(2,1)S(1)} collective-permute-done((bf16[4,48,192]{2,1,0:T(8,128)(2,1)S(1)}, bf16[4,48,192]{2,1,0:T(8,128)(2,1)S(1)}, u32[]{:S(2)}, u32[]{:S(2)}) %collective-permute-start.2) | collective-permute-done | bytes 73760 | tf_op jit(solution)/shard_map/ppermute | solution.py:299
  93.5 0.1 collective-permute-start.3
  93.6 0.9 project.1
  94.5 0.5 collective-permute-done.3.refs_11_
  95.0 7.1 %attend.1 = bf16[12,192,128]{2,1,0:T(8,128)(2,1)} custom-call(s32[3]{0:T(128)S(1)} %pad_add_fusion.refs_0_, bf16[12,192,128]{2,1,0:T(8,128)(2,1)S(1)} %get-tuple-element.13.refs_1_, bf16[12,192,128]{2,1,0:T(8,128)(2,1)S(1)} %get-tuple-element.14.refs_2_, bf16[12,128,192]{2,1,0:T(8,128)(2,1)S(1)} %get-tuple-element.15.refs_3_, ...), custom_call_target="tpu_custom_call" | custom-call | tf_op jit(solution)/shard_map/attend/pallas_call | solution.py:38
  (17 shorter events, 0.1 us)
Async XLA Ops:
  0.7 1.1 %copy-start = (bf16[12,192,128]{2,1,0:T(8,128)(2,1)S(1)}, bf16[12,192,128]{2,1,0:T(8,128)(2,1)}, u32[]{:S(2)}) copy-start(bf16[12,192,128]{2,1,0:T(8,128)(2,1)} %refs_1_.4) | copy-start | bytes 1769476
  1.8 0.9 copy-start.1
  2.7 0.7 copy-start.9
  44.9 4.1 %copy-start.13 = (bf16[128,4]{0,1:T(4,128)(2,1)S(1)}, bf16[128,4]{0,1:T(4,128)(2,1)}, u32[]{:S(2)}) copy-start(bf16[128,4]{0,1:T(4,128)(2,1)} %param.25) | copy-start | bytes 3076
  44.9 28.9 %copy-start.3 = (bf16[128,128]{1,0:T(8,128)(2,1)S(1)}, bf16[128,128]{1,0:T(8,128)(2,1)}, u32[]{:S(2)}) copy-start(bf16[128,128]{1,0:T(8,128)(2,1)} %refs_2_.2) | copy-start | bytes 98308
  44.9 28.9 %copy-start.4 = (bf16[128,128]{1,0:T(8,128)(2,1)S(1)}, bf16[128,128]{1,0:T(8,128)(2,1)}, u32[]{:S(2)}) copy-start(bf16[128,128]{1,0:T(8,128)(2,1)} %refs_4_.2) | copy-start | bytes 98308
  44.9 28.9 %copy-start.10 = (f32[128]{0:T(128)S(1)}, f32[128]{0:T(128)}, u32[]{:S(2)}) copy-start(f32[128]{0:T(128)} %param.16) | copy-start | bytes 1540
  44.9 28.9 %copy-start.11 = (f32[128]{0:T(128)S(1)}, f32[128]{0:T(128)}, u32[]{:S(2)}) copy-start(f32[128]{0:T(128)} %param.19) | copy-start | bytes 1540
  44.9 28.9 %copy-start.12 = (f32[128]{0:T(128)S(1)}, f32[128]{0:T(128)}, u32[]{:S(2)}) copy-start(f32[128]{0:T(128)} %param.21) | copy-start | bytes 1540
  44.9 28.9 %all-to-all-start.1 = ((bf16[16,16,2304]{2,1,0:T(8,128)(2,1)}), bf16[16,16,2304]{2,1,0:T(8,128)(2,1)S(1)}, u32[]{:S(2)}, u32[]{:S(2)}) async-start(bf16[16,16,2304]{2,1,0:T(8,128)(2,1)} %outer.1), calls=%async_computation.1 | async-start | bytes 2359296 | tf_op jit(solution)/shard_map/all_to_all | solution.py:351
  49.0 44.6 %copy-start.5 = (bf16[128,128]{1,0:T(8,128)(2,1)S(1)}, bf16[128,128]{1,0:T(8,128)(2,1)}, u32[]{:S(2)}) copy-start(bf16[128,128]{1,0:T(8,128)(2,1)} %refs_1_.5) | copy-start | bytes 98308
  49.0 44.6 %copy-start.6 = (bf16[128,128]{1,0:T(8,128)(2,1)S(1)}, bf16[128,128]{1,0:T(8,128)(2,1)}, u32[]{:S(2)}) copy-start(bf16[128,128]{1,0:T(8,128)(2,1)} %refs_2_.3) | copy-start | bytes 98308
  49.0 44.6 %copy-start.7 = (bf16[128,128]{1,0:T(8,128)(2,1)S(1)}, bf16[128,128]{1,0:T(8,128)(2,1)}, u32[]{:S(2)}) copy-start(bf16[128,128]{1,0:T(8,128)(2,1)} %refs_3_.3) | copy-start | bytes 98308
  49.0 44.6 %copy-start.8 = (bf16[128,128]{1,0:T(8,128)(2,1)S(1)}, bf16[128,128]{1,0:T(8,128)(2,1)}, u32[]{:S(2)}) copy-start(bf16[128,128]{1,0:T(8,128)(2,1)} %refs_4_.3) | copy-start | bytes 98308
  73.9 21.2 %copy-start.2 = (bf16[128,128]{1,0:T(8,128)(2,1)S(1)}, bf16[128,128]{1,0:T(8,128)(2,1)}, u32[]{:S(2)}) copy-start(bf16[128,128]{1,0:T(8,128)(2,1)} %refs_6_.2) | copy-start | bytes 98308
  77.1 7.5 %collective-permute-start = (bf16[1,48,192]{2,1,0:T(8,128)(2,1)S(1)}, bf16[1,48,192]{2,1,0:T(8,128)(2,1)S(1)}, u32[]{:S(2)}, u32[]{:S(2)}) collective-permute-start(bf16[1,48,192]{2,1,0:T(8,128)(2,1)S(1)} %bitcast.7), channel_id=1, source_target_pairs={{0,8},{1,9},{2,10},{3,11},{4,12},{5,13},{6,14},{7,15},{8,0},{9,1},... | collective-permute-start | bytes 55304 | tf_op jit(solution)/shard_map/ppermute | solution.py:299
  84.6 4.2 %collective-permute-start.1 = (bf16[2,48,192]{2,1,0:T(8,128)(2,1)S(1)}, bf16[2,48,192]{2,1,0:T(8,128)(2,1)S(1)}, u32[]{:S(2)}, u32[]{:S(2)}) collective-permute-start(bf16[2,48,192]{2,1,0:T(8,128)(2,1)S(1)} %pad_maximum_fusion.2), channel_id=1, source_target_pairs={{0,4},{1,5},{2,6},{3,7},{4,0},{5,1},{6,2},{7,3},{8,12},{9,13},{10,... | collective-permute-start | bytes 110600 | tf_op jit(solution)/shard_map/ppermute | solution.py:299
  88.8 4.7 %collective-permute-start.2 = (bf16[4,48,192]{2,1,0:T(8,128)(2,1)S(1)}, bf16[4,48,192]{2,1,0:T(8,128)(2,1)S(1)}, u32[]{:S(2)}, u32[]{:S(2)}) collective-permute-start(bf16[4,48,192]{2,1,0:T(8,128)(2,1)S(1)} %pad_maximum_fusion.1), channel_id=1, source_target_pairs={{0,2},{1,3},{2,0},{3,1},{4,6},{5,7},{6,4},{7,5},{8,10},{9,11},{10,... | collective-permute-start | bytes 221192 | tf_op jit(solution)/shard_map/ppermute | solution.py:299
  93.5 1.5 %collective-permute-start.3 = (bf16[8,48,192]{2,1,0:T(8,128)(2,1)S(1)}, bf16[8,48,192]{2,1,0:T(8,128)(2,1)S(1)}, u32[]{:S(2)}, u32[]{:S(2)}) collective-permute-start(bf16[8,48,192]{2,1,0:T(8,128)(2,1)S(1)} %pad_maximum_fusion), channel_id=1, source_target_pairs={{0,1},{1,0},{2,3},{3,2},{4,5},{5,4},{6,7},{7,6},{8,9},{9,8},{10,11... | collective-permute-start | bytes 442376 | tf_op jit(solution)/shard_map/ppermute | solution.py:299

commit v7 on v6

--- a/solution.py
+++ b/solution.py
@@ -12,6 +12,7 @@
 BF16 = jnp.bfloat16
 AXES = ("row", "node")
 VMEM_BYTES = 48 * 1024 * 1024
+VMEM_MOST = 60 * 1024 * 1024
 
 
 def norm_last(values, gain):
@@ -29,19 +30,19 @@
     return lax.dot_general(a, b, (((a_dim,), (b_dim,)), ((), ())), preferred_element_type=F32)
 
 
-def call(kernel, out_shape, args, scratch=(), smem=(), name=None):
+def call(kernel, out_shape, args, scratch=(), smem=(), name=None, vmem=VMEM_BYTES):
     specs = [
         pl.BlockSpec(memory_space=pltpu.SMEM if n in smem else pltpu.VMEM) for n in range(len(args))
     ]
     single = not isinstance(out_shape, (list, tuple))
-    vmem = pl.BlockSpec(memory_space=pltpu.VMEM)
+    inside = pl.BlockSpec(memory_space=pltpu.VMEM)
     return pl.pallas_call(
         kernel,
         out_shape=out_shape,
         in_specs=specs,
-        out_specs=vmem if single else [vmem] * len(out_shape),
+        out_specs=inside if single else [inside] * len(out_shape),
         scratch_shapes=list(scratch),
-        compiler_params=pltpu.CompilerParams(vmem_limit_bytes=VMEM_BYTES),
+        compiler_params=pltpu.CompilerParams(vmem_limit_bytes=vmem),
         name=name,
     )(*args)
 
@@ -106,7 +107,19 @@
         ).astype(BF16)
 
 
-def outer_kernel(sz, e_ref, x_ref, out_ref, main_ref, rest_ref, omain_ref, orest_ref, pair_ref):
+def pack_kernel(sz, x_ref, out_ref, pair_ref):
+    for row in range(sz.rows):
+        x = x_ref[row].astype(F32)
+        for d in range(sz.devices):
+            pair_ref[d, row * sz.rows : (row + 1) * sz.rows, :] = x[d * sz.rows : (d + 1) * sz.rows]
+    high = sz.packed
+    for d in range(sz.devices):
+        for t in range(sz.block_tiles):
+            at = t * LANES
+            out_ref[d, :, at : at + LANES] = pair_ref[d, t * high : (t + 1) * high, :].astype(BF16)
+
+
+def outer_kernel(sz, e_ref, pair_ref, out_ref, main_ref, rest_ref, omain_ref, orest_ref):
     cd, two = sz.chans, 2 * sz.chans
     n, w, half = sz.crop, sz.whole, sz.half
     for s in range(sz.devices):
@@ -148,15 +161,7 @@
                     blocks.append(jnp.where(low, one, orest_ref[pl.ds((at + half) * cd, cd), :]))
             block = jnp.concatenate(blocks, axis=0) if len(blocks) > 1 else blocks[0]
             out_ref[s, :, t * LANES : (t + 1) * LANES] = block.astype(BF16)
-    for row in range(sz.rows):
-        x = x_ref[row].astype(F32)
-        for d in range(sz.devices):
-            pair_ref[d, row * sz.rows : (row + 1) * sz.rows, :] = x[d * sz.rows : (d + 1) * sz.rows]
-    high = sz.packed
-    for d in range(sz.devices):
-        for t in range(sz.block_tiles):
-            at = (sz.fold_tiles + t) * LANES
-            out_ref[d, :, at : at + LANES] = pair_ref[d, t * high : (t + 1) * high, :].astype(BF16)
+        out_ref[s, :, sz.fold_tiles * LANES :] = pair_ref[s]
 
 
 def update_kernel(
@@ -199,7 +204,15 @@
         col_ref[j] = col
         heads = biasw_ref.shape[1]
         brow_ref[pl.ds(j * heads, heads), :] = dot(biasw_ref[...], col, 0, 1)
-    bias_ref[...] = brow_ref[...].astype(BF16)
+    rows = brow_ref[...]
+    part = rows.shape[0] // 2
+    one, two = rows[:part], rows[part:]
+    message = [one[:, : w * LANES], two[:, : w * LANES]]
+    if sz.rest:
+        message += [one[:, w * LANES :], two[:, w * LANES :]]
+    message = jnp.concatenate(message, axis=1).astype(BF16)
+    for d in range(sz.devices):
+        bias_ref[d] = message
 
 
 def project_kernel(sz, col_ref, q_ref, k_ref, v_ref, g_ref, qo_ref, ko_ref, vo_ref, go_ref):
@@ -218,22 +231,23 @@
 
 
 def attend_kernel(
-    sz, heads, steps, len_ref, q_ref, k_ref, v_ref, g_ref, first_ref, aout_ref, *refs
+    sz, heads, len_ref, q_ref, k_ref, v_ref, g_ref, first_ref, aout_ref, bias_ref,
+    out_ref, rows_ref, biasT_ref,
 ):
-    bias_refs, (out_ref, rows_ref, biasT_ref) = refs[:-3], refs[-3:]
     n, w, ch = sz.crop, sz.whole, sz.channels
-    length, me = len_ref[0], len_ref[2]
+    length = len_ref[0]
     width = q_ref.shape[2]
     hd = width // heads
-    per = sz.rows * heads
-    for ref, offsets in zip(bias_refs, steps):
-        for place, offset in enumerate(offsets):
-            at = pl.ds(pl.multiple_of((me ^ offset) * per, 8), per)
-            part = ref[place].astype(F32) * LOG2E
+    per = sz.rows * heads // 2
+    for s in range(sz.devices):
+        block = bias_ref[s].astype(F32) * LOG2E
+        for p in range(2):
+            at = pl.ds((2 * s + p) * per, per)
             for m in range(w):
-                rows_ref[m, at, :] = part[:, m * LANES : (m + 1) * LANES]
+                rows_ref[m, at, :] = block[:, (p * w + m) * LANES : (p * w + m + 1) * LANES]
             if sz.rest:
-                rows_ref[w, at, : sz.rest] = part[:, w * LANES :]
+                tail = block[:, 2 * w * LANES :]
+                rows_ref[w, at, :] = pltpu.roll(tail, sz.rest, 1) if p else tail
     key = lax.broadcasted_iota(jnp.int32, (n, LANES), 0)
     dead = jnp.where(key < length, 0.0, -1e9 * LOG2E).astype(F32)
     halves = []
@@ -291,19 +305,6 @@
         out_ref[j] = total_out.astype(BF16)
 
 
-def spread(block, devices):
-    pieces, offsets = [block[None]], [[0]]
-    bit = devices // 2
-    while bit:
-        held = jnp.concatenate(pieces, axis=0) if len(pieces) > 1 else pieces[0]
-        got = lax.ppermute(held, AXES, [(d, d ^ bit) for d in range(devices)])
-        known = [o for part in offsets for o in part]
-        pieces.append(got)
-        offsets.append([o ^ bit for o in known])
-        bit //= 2
-    return pieces, offsets
-
-
 def shards(
     devices,
     pair_rep, length, ln_pair, tri_in, tri_gate, ln_hidden, tri_out, ln_att,
@@ -314,7 +315,7 @@
     sz = Sizes(rows, crop, devices, ch)
     n, cd = crop, sz.chans
     me = lax.axis_index(AXES).astype(jnp.int32)
-    info = jnp.stack([length[0], me * rows, me])
+    info = jnp.stack([length[0], me * rows])
 
     def bound(kernel, *extra):
         def run(*refs):
@@ -332,19 +333,26 @@
         ],
         smem=(0,),
         name="edges",
+        vmem=VMEM_MOST,
+    )
+    packed = call(
+        bound(pack_kernel),
+        shape((devices, sz.packed, sz.block_tiles * LANES), BF16),
+        (pair_rep,),
+        scratch=[pltpu.VMEM((devices, sz.block_tiles * sz.packed, ch), F32)],
+        name="pack",
     )
     edges = lax.all_to_all(edges, AXES, split_axis=0, concat_axis=0, tiled=True)
     rest_rows = n if sz.rest else 8
     outer = call(
         bound(outer_kernel),
         shape((devices, sz.packed, (sz.fold_tiles + sz.block_tiles) * LANES), BF16),
-        (edges, pair_rep),
+        (edges, packed),
         scratch=[
             pltpu.VMEM((sz.whole, n * 2 * cd, LANES), F32),
             pltpu.VMEM((rest_rows * 2 * cd, LANES), F32),
             pltpu.VMEM((sz.whole, n * cd, LANES), F32),
             pltpu.VMEM((rest_rows * cd, LANES), F32),
-            pltpu.VMEM((devices, sz.block_tiles * sz.packed, ch), F32),
         ],
         name="outer",
     )
@@ -354,7 +362,7 @@
         [
             shape((rows, n, ch), BF16),
             shape((rows, n, ch), BF16),
-            shape((rows * heads, n), BF16),
+            shape((devices, rows * heads // 2, 2 * n), BF16),
         ],
         (outer, ln_pair[None], tri_gate, ln_hidden[None], tri_out, ln_att[None], att_bias),
         scratch=[
@@ -363,7 +371,7 @@
         ],
         name="update",
     )
-    pieces, steps = spread(bias, devices)
+    bias = lax.all_to_all(bias, AXES, split_axis=0, concat_axis=0, tiled=True)
     query, key, value, gate = call(
         bound(project_kernel),
         [
@@ -376,9 +384,9 @@
         name="project",
     )
     out = call(
-        bound(attend_kernel, heads, steps),
+        bound(attend_kernel, heads),
         shape((rows, n, ch), BF16),
-        (info, query, key, value, gate, first, att_out, *pieces),
+        (info, query, key, value, gate, first, att_out, bias),
         scratch=[
             pltpu.VMEM((-(-n // LANES), n * heads, LANES), F32),
             pltpu.VMEM((n, heads * n), F32),

time: 102 us -> 107 us (1.049)
  blocking collectives: 36.7 us -> 0 us
  waiting for transfers between devices: 33.5 us -> 57.9 us
  starting transfers between devices: 12.1 us -> 22.6 us
  local copies, waits for them, and re-layouts: 2.82 us -> 5.88 us
  Pallas kernels: 16 us -> 18.5 us
    all_to_all x1 -> x0, blocking collectives: 36.7 us -> none  [shards(): edges = lax.all_to_all(edges, AXES, split_axis=0, concat_axis=0, tiled=True)]
    all_to_all x0 -> x2, waiting for transfers between devices: none -> 32.9 us  [the longest x1 25 us: shards(): edges = lax.all_to_all(edges, AXES, split_axis=0, concat_axis=0, tiled=True)]
    all_to_all x0 -> x2, starting transfers between devices: none -> 15 us  [the longest x1 7.5 us: shards(): edges = lax.all_to_all(edges, AXES, split_axis=0, concat_axis=0, tiled=True)]
    ppermute x4 -> x0, waiting for transfers between devices: 8.84 us -> none  [spread(): got = lax.ppermute(held, AXES, [(d, d ^ bit) for d in range(devices)])]
    ppermute x4 -> x0, starting transfers between devices: 8.05 us -> none  [spread(): got = lax.ppermute(held, AXES, [(d, d ^ bit) for d in range(devices)])]
    all_to_all x1, starting transfers between devices: 4.02 us -> 7.63 us  [shards(): outer = lax.all_to_all(outer, AXES, split_axis=0, concat_axis=0, tiled=True)]
    unnamed x29 -> x39, local copies, waits for them, and re-layouts: 2.82 us -> 5.88 us
    pallas_call x5 -> x6, Pallas kernels: 16 us -> 18.5 us  [call(): pl.pallas_call(kernel, out_shape=out_shape, in_specs=specs, out_specs=ins...]
  transfers between devices with their start and end apart: 5 -> 3, of which waited for: 5 -> 3; matrix products, arithmetic and copies ran while one was open for 0% -> 0% of each run, Pallas kernels for 1% -> 1%
where the time goes in v7:
time: 107 us; the launch traced here: 106 us
  waiting for transfers between devices  57.9 us (54%)
  starting transfers between devices  22.6 us (21%)
  Pallas kernels  18.5 us (17%)
  local copies, waits for them, and re-layouts  5.88 us (5%)
    all_to_all x1, waiting for transfers between devices, shards(): edges = lax.all_to_all(edges, AXES, split_axis=0, concat_axis=0, tiled=True)  25 us
    all_to_all x1, waiting for transfers between devices, shards(): outer = lax.all_to_all(outer, AXES, split_axis=0, concat_axis=0, tiled=True)  24.9 us
    pallas_call x6, Pallas kernels, call(): pl.pallas_call(kernel, out_shape=out_shape, in_specs=specs, out_specs=ins...  18.5 us
    all_to_all x1, waiting for transfers between devices, shards(): bias = lax.all_to_all(bias, AXES, split_axis=0, concat_axis=0, tiled=True)  7.96 us
    all_to_all x1, starting transfers between devices, shards(): outer = lax.all_to_all(outer, AXES, split_axis=0, concat_axis=0, tiled=True)  7.63 us
    all_to_all x1, starting transfers between devices, shards(): edges = lax.all_to_all(edges, AXES, split_axis=0, concat_axis=0, tiled=True)  7.5 us
    all_to_all x1, starting transfers between devices, shards(): bias = lax.all_to_all(bias, AXES, split_axis=0, concat_axis=0, tiled=True)  7.49 us
    unnamed x39, local copies, waits for them, and re-layouts  5.88 us
  transfers between devices with their start and end apart: 3, of which 3 were waited for; matrix products, arithmetic and copies ran while one was open for 0% of the time, Pallas kernels for 1%

profile of v7, /device:TPU:0, one launch (start us, length us, event | category | flops | bytes accessed | tf_op | source)
XLA Modules:
  0.0 106.3 jit_solution(17535222911259938633)
XLA Ops:
  0.7 0.6 pad_add_fusion.refs_0_
  1.2 3.9 %edges.1 = bf16[16,16,2304]{2,1,0:T(8,128)(2,1)} custom-call(s32[2]{0:T(128)} %pad_add_fusion.refs_0_, bf16[12,192,128]{2,1,0:T(8,128)(2,1)} %refs_0_.1, f32[1,128]{1,0:T(1,128)} %bitcast.5, bf16[4,128,128]{2,1,0:T(8,128)(2,1)} %refs_3_.2), custom_call_target="tpu_custom_call" | custom-call | tf_op jit(solution)/shard_map/edges/pallas_call | solution.py:39
  5.1 7.5 %all-to-all-start = ((bf16[16,16,2304]{2,1,0:T(8,128)(2,1)}), bf16[16,16,2304]{2,1,0:T(8,128)(2,1)S(1)}, u32[]{:S(2)}, u32[]{:S(2)}) async-start(bf16[16,16,2304]{2,1,0:T(8,128)(2,1)} %edges.1), calls=%async_computation | async-start | bytes 2359296 | tf_op jit(solution)/shard_map/all_to_all | solution.py:345
  12.6 0.0 copy-done
  12.7 0.2 pack.1.refs_1_
  12.8 25.0 %all-to-all-done.refs_0_ = bf16[16,16,2304]{2,1,0:T(8,128)(2,1)S(1)} async-done(((bf16[16,16,2304]{2,1,0:T(8,128)(2,1)}), bf16[16,16,2304]{2,1,0:T(8,128)(2,1)S(1)}, u32[]{:S(2)}, u32[]{:S(2)}) %all-to-all-start) | async-done | bytes 1179680 | tf_op jit(solution)/shard_map/all_to_all | solution.py:345
  37.8 2.5 %outer.1 = bf16[16,16,2304]{2,1,0:T(8,128)(2,1)} custom-call(bf16[16,16,2304]{2,1,0:T(8,128)(2,1)S(1)} %all-to-all-done.refs_0_, bf16[16,16,1152]{2,1,0:T(8,128)(2,1)S(1)} %pack.1.refs_1_), custom_call_target="tpu_custom_call" | custom-call | tf_op jit(solution)/shard_map/outer/pallas_call | solution.py:39
  40.3 0.0 copy-start.16
  40.3 0.0 copy-start.17
  40.3 7.6 %all-to-all-start.1 = ((bf16[16,16,2304]{2,1,0:T(8,128)(2,1)}), bf16[16,16,2304]{2,1,0:T(8,128)(2,1)S(1)}, u32[]{:S(2)}, u32[]{:S(2)}) async-start(bf16[16,16,2304]{2,1,0:T(8,128)(2,1)} %outer.1), calls=%async_computation.1 | async-start | bytes 2359296 | tf_op jit(solution)/shard_map/all_to_all | solution.py:359
  47.9 0.0 copy-start.10
  47.9 0.0 copy-start.11
  47.9 0.0 copy-start.12
  48.0 0.0 copy-start.13
  48.0 0.1 copy.15.refs_6_
  48.1 24.9 %all-to-all-done.1.refs_0_ = bf16[16,16,2304]{2,1,0:T(8,128)(2,1)S(1)} async-done(((bf16[16,16,2304]{2,1,0:T(8,128)(2,1)}), bf16[16,16,2304]{2,1,0:T(8,128)(2,1)S(1)}, u32[]{:S(2)}, u32[]{:S(2)}) %all-to-all-start.1) | async-done | bytes 1179680 | tf_op jit(solution)/shard_map/all_to_all | solution.py:359
  73.0 0.0 copy-done.9
  73.1 0.0 copy-start.7
  73.1 0.0 copy-start.15
  73.1 4.0 %update.1 = (bf16[12,192,128]{2,1,0:T(8,128)(2,1)S(1)}, bf16[12,192,128]{2,1,0:T(8,128)(2,1)S(1)}, bf16[16,24,384]{2,1,0:T(8,128)(2,1)}) custom-call(bf16[16,16,2304]{2,1,0:T(8,128)(2,1)S(1)} %all-to-all-done.1.refs_0_, f32[1,128]{1,0:T(1,128)S(1)} %bitcast.6, bf16[128,128]{1,0:T(8,128)(2,1)S(1)} %copy-done.8, f32[1,128]{1,0:T(1,128)S(1)} %bitcast.7, ...), custom_call_target="tpu_custom_call" | custom-call | tf_op jit(solution)/shard_map/update/pallas_call | solution.py:39
  77.1 0.8 copy-done.1
  77.9 7.5 %all-to-all-start.2 = ((bf16[16,24,384]{2,1,0:T(8,128)(2,1)}), bf16[16,24,384]{2,1,0:T(8,128)(2,1)S(1)}, u32[]{:S(2)}, u32[]{:S(2)}) async-start(bf16[16,24,384]{2,1,0:T(8,128)(2,1)} %get-tuple-element.18), calls=%async_computation.2 | async-start | bytes 589824 | tf_op jit(solution)/shard_map/all_to_all | solution.py:374
  85.5 0.9 project.1
  86.4 0.0 copy-start.3
  86.4 0.8 copy-done.3
  87.2 0.9 copy-done.5
  88.0 8.0 %all-to-all-done.2.refs_7_ = bf16[16,24,384]{2,1,0:T(8,128)(2,1)S(1)} async-done(((bf16[16,24,384]{2,1,0:T(8,128)(2,1)}), bf16[16,24,384]{2,1,0:T(8,128)(2,1)S(1)}, u32[]{:S(2)}, u32[]{:S(2)}) %all-to-all-start.2) | async-done | bytes 294944 | tf_op jit(solution)/shard_map/all_to_all | solution.py:374
  96.0 0.0 copy-done.15
  96.0 1.1 %copy-done.2 = bf16[12,192,128]{2,1,0:T(8,128)(2,1)S(1)} copy-done((bf16[12,192,128]{2,1,0:T(8,128)(2,1)S(1)}, bf16[12,192,128]{2,1,0:T(8,128)(2,1)}, u32[]{:S(2)}) %copy-start.2) | copy-done | bytes 589848
  97.1 1.1 copy-done.4
  98.1 1.1 copy-done.6
  99.2 7.1 %attend.1 = bf16[12,192,128]{2,1,0:T(8,128)(2,1)} custom-call(s32[2]{0:T(128)S(1)} %copy-done.15, bf16[12,192,128]{2,1,0:T(8,128)(2,1)S(1)} %copy-done.4, bf16[12,192,128]{2,1,0:T(8,128)(2,1)S(1)} %copy-done.6, bf16[12,128,192]{2,1,0:T(8,128)(2,1)S(1)} %get-tuple-element.15.refs_3_, f32[12,128,192]{2,1,0:T(8,128)S(1)} %get-tuple-element.16.refs_4_, ...), custom_call_target="tpu_custom_call" | custom-call | tf_op jit(solution)/shard_map/attend/pallas_call | solution.py:39
  (20 shorter events, 0.0 us)
Async XLA Ops:
  5.1 7.5 %copy-start = (bf16[12,192,128]{2,1,0:T(8,128)(2,1)S(1)}, bf16[12,192,128]{2,1,0:T(8,128)(2,1)}, u32[]{:S(2)}) copy-start(bf16[12,192,128]{2,1,0:T(8,128)(2,1)} %refs_0_.1) | copy-start | bytes 1769476
  5.1 32.6 %all-to-all-start = ((bf16[16,16,2304]{2,1,0:T(8,128)(2,1)}), bf16[16,16,2304]{2,1,0:T(8,128)(2,1)S(1)}, u32[]{:S(2)}, u32[]{:S(2)}) async-start(bf16[16,16,2304]{2,1,0:T(8,128)(2,1)} %edges.1), calls=%async_computation | async-start | bytes 2359296 | tf_op jit(solution)/shard_map/all_to_all | solution.py:345
  40.2 7.7 %copy-start.18 = (bf16[128,4]{0,1:T(4,128)(2,1)S(1)}, bf16[128,4]{0,1:T(4,128)(2,1)}, u32[]{:S(2)}) copy-start(bf16[128,4]{0,1:T(4,128)(2,1)} %param.25) | copy-start | bytes 3076
  40.2 32.8 %copy-start.8 = (bf16[128,128]{1,0:T(8,128)(2,1)S(1)}, bf16[128,128]{1,0:T(8,128)(2,1)}, u32[]{:S(2)}) copy-start(bf16[128,128]{1,0:T(8,128)(2,1)} %refs_2_.2) | copy-start | bytes 98308
  40.2 32.8 %copy-start.9 = (bf16[128,128]{1,0:T(8,128)(2,1)S(1)}, bf16[128,128]{1,0:T(8,128)(2,1)}, u32[]{:S(2)}) copy-start(bf16[128,128]{1,0:T(8,128)(2,1)} %refs_4_.2) | copy-start | bytes 98308
  40.2 32.8 %copy-start.14 = (f32[128]{0:T(128)S(1)}, f32[128]{0:T(128)}, u32[]{:S(2)}) copy-start(f32[128]{0:T(128)} %param.16) | copy-start | bytes 1540
  40.3 32.8 %copy-start.16 = (f32[128]{0:T(128)S(1)}, f32[128]{0:T(128)}, u32[]{:S(2)}) copy-start(f32[128]{0:T(128)} %param.19) | copy-start | bytes 1540
  40.3 32.8 %copy-start.17 = (f32[128]{0:T(128)S(1)}, f32[128]{0:T(128)}, u32[]{:S(2)}) copy-start(f32[128]{0:T(128)} %param.21) | copy-start | bytes 1540
  40.3 32.8 %all-to-all-start.1 = ((bf16[16,16,2304]{2,1,0:T(8,128)(2,1)}), bf16[16,16,2304]{2,1,0:T(8,128)(2,1)S(1)}, u32[]{:S(2)}, u32[]{:S(2)}) async-start(bf16[16,16,2304]{2,1,0:T(8,128)(2,1)} %outer.1), calls=%async_computation.1 | async-start | bytes 2359296 | tf_op jit(solution)/shard_map/all_to_all | solution.py:359
  47.9 37.5 %copy-start.10 = (bf16[128,128]{1,0:T(8,128)(2,1)S(1)}, bf16[128,128]{1,0:T(8,128)(2,1)}, u32[]{:S(2)}) copy-start(bf16[128,128]{1,0:T(8,128)(2,1)} %refs_1_.3) | copy-start | bytes 98308
  47.9 37.5 %copy-start.11 = (bf16[128,128]{1,0:T(8,128)(2,1)S(1)}, bf16[128,128]{1,0:T(8,128)(2,1)}, u32[]{:S(2)}) copy-start(bf16[128,128]{1,0:T(8,128)(2,1)} %refs_2_.3) | copy-start | bytes 98308
  47.9 37.5 %copy-start.12 = (bf16[128,128]{1,0:T(8,128)(2,1)S(1)}, bf16[128,128]{1,0:T(8,128)(2,1)}, u32[]{:S(2)}) copy-start(bf16[128,128]{1,0:T(8,128)(2,1)} %refs_3_.3) | copy-start | bytes 98308
  48.0 37.5 %copy-start.13 = (bf16[128,128]{1,0:T(8,128)(2,1)S(1)}, bf16[128,128]{1,0:T(8,128)(2,1)}, u32[]{:S(2)}) copy-start(bf16[128,128]{1,0:T(8,128)(2,1)} %refs_4_.3) | copy-start | bytes 98308
  73.1 22.9 %copy-start.7 = (bf16[128,128]{1,0:T(8,128)(2,1)S(1)}, bf16[128,128]{1,0:T(8,128)(2,1)}, u32[]{:S(2)}) copy-start(bf16[128,128]{1,0:T(8,128)(2,1)} %refs_6_.2) | copy-start | bytes 98308
  73.1 22.9 %copy-start.15 = (s32[2]{0:T(128)S(1)}, s32[2]{0:T(128)}, u32[]{:S(2)}) copy-start(s32[2]{0:T(128)} %pad_add_fusion.refs_0_) | copy-start | bytes 28
  77.1 0.8 copy-start.1
  77.9 18.1 %all-to-all-start.2 = ((bf16[16,24,384]{2,1,0:T(8,128)(2,1)}), bf16[16,24,384]{2,1,0:T(8,128)(2,1)S(1)}, u32[]{:S(2)}, u32[]{:S(2)}) async-start(bf16[16,24,384]{2,1,0:T(8,128)(2,1)} %get-tuple-element.18), calls=%async_computation.2 | async-start | bytes 589824 | tf_op jit(solution)/shard_map/all_to_all | solution.py:374
  86.4 0.8 copy-start.3
  87.2 0.9 copy-start.5
  96.0 1.1 %copy-start.2 = (bf16[12,192,128]{2,1,0:T(8,128)(2,1)S(1)}, bf16[12,192,128]{2,1,0:T(8,128)(2,1)}, u32[]{:S(2)}) copy-start(bf16[12,192,128]{2,1,0:T(8,128)(2,1)} %copy-done.1) | copy-start | bytes 1769476
  97.1 1.1 %copy-start.4 = (bf16[12,192,128]{2,1,0:T(8,128)(2,1)S(1)}, bf16[12,192,128]{2,1,0:T(8,128)(2,1)}, u32[]{:S(2)}) copy-start(bf16[12,192,128]{2,1,0:T(8,128)(2,1)} %copy-done.3) | copy-start | bytes 1769476
  98.1 1.1 %copy-start.6 = (bf16[12,192,128]{2,1,0:T(8,128)(2,1)S(1)}, bf16[12,192,128]{2,1,0:T(8,128)(2,1)}, u32[]{:S(2)}) copy-start(bf16[12,192,128]{2,1,0:T(8,128)(2,1)} %copy-done.5) | copy-start | bytes 1769476

commit v8 on v5

--- a/solution.py
+++ b/solution.py
@@ -12,6 +12,7 @@
 BF16 = jnp.bfloat16
 AXES = ("row", "node")
 VMEM_BYTES = 48 * 1024 * 1024
+VMEM_MOST = 60 * 1024 * 1024
 
 
 def norm_last(values, gain):
@@ -29,19 +30,19 @@
     return lax.dot_general(a, b, (((a_dim,), (b_dim,)), ((), ())), preferred_element_type=F32)
 
 
-def call(kernel, out_shape, args, scratch=(), smem=(), name=None):
+def call(kernel, out_shape, args, scratch=(), smem=(), name=None, vmem=VMEM_BYTES):
     specs = [
         pl.BlockSpec(memory_space=pltpu.SMEM if n in smem else pltpu.VMEM) for n in range(len(args))
     ]
     single = not isinstance(out_shape, (list, tuple))
-    vmem = pl.BlockSpec(memory_space=pltpu.VMEM)
+    inside = pl.BlockSpec(memory_space=pltpu.VMEM)
     return pl.pallas_call(
         kernel,
         out_shape=out_shape,
         in_specs=specs,
-        out_specs=vmem if single else [vmem] * len(out_shape),
+        out_specs=inside if single else [inside] * len(out_shape),
         scratch_shapes=list(scratch),
-        compiler_params=pltpu.CompilerParams(vmem_limit_bytes=VMEM_BYTES),
+        compiler_params=pltpu.CompilerParams(vmem_limit_bytes=vmem),
         name=name,
     )(*args)
 
@@ -61,8 +62,8 @@
 
 
 def edges_kernel(sz, len_ref, x_ref, ln_ref, w_ref, out_ref, *refs):
-    near, pair = refs[: sz.group], refs[sz.group : 2 * sz.group]
-    norm_ref, pair_ref = refs[2 * sz.group :]
+    near = refs[: sz.group]
+    norm_ref, pair_ref = refs[sz.group :]
     length, first, me = len_ref[0], len_ref[1], len_ref[2]
     cd, ch = sz.chans, sz.channels
     mine = me & (sz.group - 1)
@@ -85,14 +86,10 @@
         if sz.rest:
             h, q = divmod(row, sz.half)
             norm_ref[pl.ds(sz.rows * main + q * LANES + h * sz.rest, sz.rest), :] = normed[main:]
-    for r in range(sz.group):
+    for d in range(sz.devices):
         for t in range(sz.block_tiles):
             at = (sz.tiles + t) * LANES
-            rows = slice(t * cd, (t + 1) * cd)
-            near[r][:, at : at + LANES] = pair_ref[me ^ r, rows, :].astype(BF16)
-            pair[r][:, t * LANES : (t + 1) * LANES] = pair_ref[me ^ (sz.group + r), rows, :].astype(
-                BF16
-            )
+            out_ref[d, :, at : at + LANES] = pair_ref[d, t * cd : (t + 1) * cd, :].astype(BF16)
     lane = lax.broadcasted_iota(jnp.int32, (1, LANES), 1)
 
     def live(tile):
@@ -176,21 +173,15 @@
 
 
 def update_kernel(
-    sz, len_ref, lnp_ref, gate_ref, lnh_ref, tri_ref, lna_ref, biasw_ref, sums_ref, *refs
+    sz, lnp_ref, gate_ref, lnh_ref, tri_ref, lna_ref, biasw_ref, sums_ref, pair_ref,
+    first_ref, col_ref, bias_ref, cols_ref, brow_ref,
 ):
-    near, pair = refs[: sz.group], refs[sz.group : 2 * sz.group]
-    first_ref, col_ref, bias_ref, cols_ref, brow_ref = refs[2 * sz.group :]
     n, w, half, ch, cd = sz.crop, sz.whole, sz.half, sz.channels, sz.chans
-    me = len_ref[2]
-    for r in range(sz.group):
-        for ref, base, owner in (
-            (near[r], sz.tiles, me ^ r),
-            (pair[r], 0, me ^ (sz.group + r)),
-        ):
-            for t in range(sz.block_tiles):
-                at = (base + t) * LANES
-                row = pl.multiple_of(owner * sz.block + t * cd, 8)
-                cols_ref[pl.ds(row, cd), :] = ref[:, at : at + LANES].astype(F32)
+    for s in range(sz.devices):
+        for t in range(sz.block_tiles):
+            at = (sz.tiles + t) * LANES
+            rows = pl.ds(s * sz.block + t * cd, cd)
+            cols_ref[rows, :] = pair_ref[s, :, at : at + LANES].astype(F32)
     gain_h = jnp.transpose(jnp.broadcast_to(lnh_ref[...], (ch, ch)))
     tri = tri_ref[...]
 
@@ -356,7 +347,7 @@
 
     left, *others = call(
         bound(edges_kernel),
-        [slab(t, devices)] + [slab(t + bt)] * g + [slab(bt)] * g,
+        [slab(t + bt, devices)] + [slab(t)] * g,
         (info, pair_rep, ln_pair[None], tri_in),
         scratch=[
             pltpu.VMEM((rows * crop, ch), BF16),
@@ -364,9 +355,10 @@
         ],
         smem=(0,),
         name="edges",
+        vmem=VMEM_MOST,
     )
     left = lax.all_to_all(left, AXES, split_axis=0, concat_axis=0, tiled=True)
-    near = send(others[:g], 0)
+    near = send(others, 0)
     rest = sz.rest > 0
     outer = call(
         bound(outer_kernel),
@@ -383,12 +375,10 @@
         smem=(0,),
         name="outer",
     )
-    late, outer = lax.optimization_barrier((others[g:], outer))
     sums = lax.all_to_all(
         outer, AXES, split_axis=0, concat_axis=0, tiled=True,
         axis_index_groups=[list(range(g)), list(range(g, devices))],
     )
-    pair = send(late, g)
     first, col, bias = call(
         bound(update_kernel),
         [
@@ -397,14 +387,13 @@
             shape((rows * heads, n), BF16),
         ],
         (
-            info, ln_pair[None], tri_gate, ln_hidden[None], tri_out, ln_att[None], att_bias,
-            sums, *near, *pair,
+            ln_pair[None], tri_gate, ln_hidden[None], tri_out, ln_att[None], att_bias,
+            sums, left,
         ),
         scratch=[
             pltpu.VMEM((devices * sz.block + cd, ch), F32),
             pltpu.VMEM((rows * heads, n), F32),
         ],
-        smem=(0,),
         name="update",
     )
     pieces, steps = spread(bias, devices)

time: 101 us -> 97.2 us (0.962)
  starting transfers between devices: 36.4 us -> 26.8 us
  waiting for transfers between devices: 41.9 us -> 49.3 us
  local copies, waits for them, and re-layouts: 2.82 us -> 0.24 us
    ppermute x15 -> x7, starting transfers between devices: 23.3 us -> 6.55 us  [send(): lax.ppermute(block, AXES, [(d, d ^ offset ^ r) for d in range(devices)])]
    all_to_all x1, waiting for transfers between devices: 0.01 us -> 9.36 us  [shards(): lax.all_to_all(outer, AXES, split_axis=0, concat_axis=0, tiled=True, axis...]
    ppermute x4, waiting for transfers between devices: 12.3 us -> 8.56 us  [spread(): got = lax.ppermute(held, AXES, [(d, d ^ bit) for d in range(devices)])]
    ppermute x4, starting transfers between devices: 1.89 us -> 5.58 us  [spread(): got = lax.ppermute(held, AXES, [(d, d ^ bit) for d in range(devices)])]
    all_to_all x1, starting transfers between devices: 3.87 us -> 7.16 us  [shards(): lax.all_to_all(outer, AXES, split_axis=0, concat_axis=0, tiled=True, axis...]
    unnamed x29 -> x41, local copies, waits for them, and re-layouts: 2.82 us -> 0.24 us
    ppermute x15 -> x7, waiting for transfers between devices: 29.5 us -> 31.4 us  [send(): lax.ppermute(block, AXES, [(d, d ^ offset ^ r) for d in range(devices)])]
  transfers between devices with their start and end apart: 21 -> 13, of which waited for: 12 -> 11; matrix products, arithmetic and copies ran while one was open for 0% -> 0% of each run, Pallas kernels for 1% -> 1%
where the time goes in v8:
time: 97.2 us; the launch traced here: 96.9 us
  waiting for transfers between devices  49.3 us (51%)
  starting transfers between devices  26.8 us (28%)
  Pallas kernels  18.9 us (19%)
    ppermute x7, waiting for transfers between devices, send(): lax.ppermute(block, AXES, [(d, d ^ offset ^ r) for d in range(devices)])  31.4 us
    pallas_call x5, Pallas kernels, call(): pl.pallas_call(kernel, out_shape=out_shape, in_specs=specs, out_specs=ins...  18.9 us
    all_to_all x1, waiting for transfers between devices, shards(): lax.all_to_all(outer, AXES, split_axis=0, concat_axis=0, tiled=True, axis...  9.36 us
    ppermute x4, waiting for transfers between devices, spread(): got = lax.ppermute(held, AXES, [(d, d ^ bit) for d in range(devices)])  8.56 us
    all_to_all x1, starting transfers between devices, shards(): left = lax.all_to_all(left, AXES, split_axis=0, concat_axis=0, tiled=True)  7.53 us
    all_to_all x1, starting transfers between devices, shards(): lax.all_to_all(outer, AXES, split_axis=0, concat_axis=0, tiled=True, axis...  7.16 us
    ppermute x7, starting transfers between devices, send(): lax.ppermute(block, AXES, [(d, d ^ offset ^ r) for d in range(devices)])  6.55 us
    ppermute x4, starting transfers between devices, spread(): got = lax.ppermute(held, AXES, [(d, d ^ bit) for d in range(devices)])  5.58 us
  transfers between devices with their start and end apart: 13, of which 11 were waited for; matrix products, arithmetic and copies ran while one was open for 0% of the time, Pallas kernels for 1%

profile of v8, /device:TPU:0, one launch (start us, length us, event | category | flops | bytes accessed | tf_op | source)
XLA Modules:
  0.0 96.9 jit_solution(7020114333392356819)
XLA Ops:
  0.7 0.6 pad_add_fusion.refs_0_
  1.3 4.2 %edges.1 = (bf16[16,16,3456]{2,1,0:T(8,128)(2,1)}, bf16[16,2304]{1,0:T(8,128)(2,1)}, bf16[16,2304]{1,0:T(8,128)(2,1)}, bf16[16,2304]{1,0:T(8,128)(2,1)}, bf16[16...) custom-call(s32[3]{0:T(128)} %pad_add_fusion.refs_0_, ...), custom_call_target="tpu_custom_call" | custom-call | tf_op jit(solution)/shard_map/edges/pallas_call | solution.py:39
  5.6 7.5 %all-to-all-start = ((bf16[16,16,3456]{2,1,0:T(8,128)(2,1)}), bf16[16,16,3456]{2,1,0:T(8,128)(2,1)S(1)}, u32[]{:S(2)}, u32[]{:S(2)}) async-start(bf16[16,16,3456]{2,1,0:T(8,128)(2,1)} %get-tuple-element.21), calls=%async_computation | async-start | bytes 3538944 | tf_op jit(solution)/shard_map/all_to_all | solution.py:360
  13.1 0.5 collective-permute-start
  13.6 1.7 %collective-permute-start.1 = (bf16[16,2304]{1,0:T(8,128)(2,1)S(1)}, bf16[16,2304]{1,0:T(8,128)(2,1)S(1)}, u32[]{:S(2)}, u32[]{:S(2)}) collective-permute-start(bf16[16,2304]{1,0:T(8,128)(2,1)S(1)} %copy-done.18), channel_id=1, source_target_pairs={{0,2},{1,3},{2,0},{3,1},{4,6},{5,7},{6,4},{7,5},{8,10},{9,11},{10,... | collective-permute-start | bytes 221192 | tf_op jit(solution)/shard_map/ppermute | solution.py:344
  15.3 0.0 collective-permute-start.2
  15.3 1.7 %collective-permute-start.3 = (bf16[16,2304]{1,0:T(8,128)(2,1)S(1)}, bf16[16,2304]{1,0:T(8,128)(2,1)S(1)}, u32[]{:S(2)}, u32[]{:S(2)}) collective-permute-start(bf16[16,2304]{1,0:T(8,128)(2,1)S(1)} %copy-done.16), channel_id=1, source_target_pairs={{0,4},{1,5},{2,6},{3,7},{4,0},{5,1},{6,2},{7,3},{8,12},{9,13},{10,... | collective-permute-start | bytes 221192 | tf_op jit(solution)/shard_map/ppermute | solution.py:344
  17.0 0.1 collective-permute-start.4
  17.1 2.6 %collective-permute-start.5 = (bf16[16,2304]{1,0:T(8,128)(2,1)S(1)}, bf16[16,2304]{1,0:T(8,128)(2,1)S(1)}, u32[]{:S(2)}, u32[]{:S(2)}) collective-permute-start(bf16[16,2304]{1,0:T(8,128)(2,1)S(1)} %copy-done.14), channel_id=1, source_target_pairs={{0,6},{1,7},{2,4},{3,5},{4,2},{5,3},{6,0},{7,1},{8,14},{9,15},{10,... | collective-permute-start | bytes 221192 | tf_op jit(solution)/shard_map/ppermute | solution.py:344
  19.7 9.1 %collective-permute-done.1.refs_4_ = bf16[16,2304]{1,0:T(8,128)(2,1)S(1)} collective-permute-done((bf16[16,2304]{1,0:T(8,128)(2,1)S(1)}, bf16[16,2304]{1,0:T(8,128)(2,1)S(1)}, u32[]{:S(2)}, u32[]{:S(2)}) %collective-permute-start.1) | collective-permute-done | bytes 73760 | tf_op jit(solution)/shard_map/ppermute | solution.py:344
  28.8 0.6 collective-permute-done.2.refs_5_
  29.5 15.1 %collective-permute-done.3.refs_6_ = bf16[16,2304]{1,0:T(8,128)(2,1)S(1)} collective-permute-done((bf16[16,2304]{1,0:T(8,128)(2,1)S(1)}, bf16[16,2304]{1,0:T(8,128)(2,1)S(1)}, u32[]{:S(2)}, u32[]{:S(2)}) %collective-permute-start.3) | collective-permute-done | bytes 73760 | tf_op jit(solution)/shard_map/ppermute | solution.py:344
  44.6 1.6 %collective-permute-done.4.refs_7_ = bf16[16,2304]{1,0:T(8,128)(2,1)S(1)} collective-permute-done((bf16[16,2304]{1,0:T(8,128)(2,1)S(1)}, bf16[16,2304]{1,0:T(8,128)(2,1)S(1)}, u32[]{:S(2)}, u32[]{:S(2)}) %collective-permute-start.4) | collective-permute-done | bytes 73760 | tf_op jit(solution)/shard_map/ppermute | solution.py:344
  46.2 1.6 %collective-permute-done.5.refs_8_ = bf16[16,2304]{1,0:T(8,128)(2,1)S(1)} collective-permute-done((bf16[16,2304]{1,0:T(8,128)(2,1)S(1)}, bf16[16,2304]{1,0:T(8,128)(2,1)S(1)}, u32[]{:S(2)}, u32[]{:S(2)}) %collective-permute-start.5) | collective-permute-done | bytes 73760 | tf_op jit(solution)/shard_map/ppermute | solution.py:344
  47.8 3.4 %collective-permute-done.6.refs_9_ = bf16[16,2304]{1,0:T(8,128)(2,1)S(1)} collective-permute-done((bf16[16,2304]{1,0:T(8,128)(2,1)S(1)}, bf16[16,2304]{1,0:T(8,128)(2,1)S(1)}, u32[]{:S(2)}, u32[]{:S(2)}) %collective-permute-start.6) | collective-permute-done | bytes 73760 | tf_op jit(solution)/shard_map/ppermute | solution.py:344
  51.1 0.0 copy-start.12
  51.1 0.0 copy-start.1
  51.2 3.5 %outer.1 = bf16[8,16,2304]{2,1,0:T(8,128)(2,1)} custom-call(s32[3]{0:T(128)S(1)} %copy-done.8, bf16[16,16,3456]{2,1,0:T(8,128)(2,1)S(1)} %all-to-all-done.refs_1_.refs_7_, bf16[16,2304]{1,0:T(8,128)(2,1)S(1)} %copy-done, bf16[16,2304]{1,0:T(8,128)(2,1)S(1)} %collective-permute-done.refs_3_, bf16[16,2304]{1,0:T(8,128)(2,1)S(1)} %collective-permute-done.1.refs_4_, ...), custom_call_target="tpu_custom_call" | custom-call | tf_op jit(solution)/shard_map/outer/pallas_call | solution.py:39
  54.7 7.2 %all-to-all-start.1 = ((bf16[8,16,2304]{2,1,0:T(8,128)(2,1)}), bf16[8,16,2304]{2,1,0:T(8,128)(2,1)S(1)}, u32[]{:S(2)}, u32[]{:S(2)}) async-start(bf16[8,16,2304]{2,1,0:T(8,128)(2,1)} %outer.1), calls=%async_computation.1 | async-start | bytes 1179648 | tf_op jit(solution)/shard_map/all_to_all | solution.py:378
  61.9 0.1 copy.15.refs_5_
  62.0 9.4 %all-to-all-done.1.refs_6_ = bf16[8,16,2304]{2,1,0:T(8,128)(2,1)S(1)} async-done(((bf16[8,16,2304]{2,1,0:T(8,128)(2,1)}), bf16[8,16,2304]{2,1,0:T(8,128)(2,1)S(1)}, u32[]{:S(2)}, u32[]{:S(2)}) %all-to-all-start.1) | async-done | bytes 589856 | tf_op jit(solution)/shard_map/all_to_all | solution.py:378
  71.4 3.2 %update.1 = (bf16[12,192,128]{2,1,0:T(8,128)(2,1)S(1)}, bf16[12,192,128]{2,1,0:T(8,128)(2,1)S(1)}, bf16[48,192]{1,0:T(8,128)(2,1)S(1)}) custom-call(f32[1,128]{1,0:T(1,128)S(1)} %bitcast.13, bf16[128,128]{1,0:T(8,128)(2,1)S(1)} %copy-done.1, f32[1,128]{1,0:T(1,128)S(1)} %bitcast.14, bf16[128,128]{1,0:T(8,128)(2,1)S(1)} %copy-done.2, f32[1,128]{1,0:T(1,128)S(1)} %bitcast.15, ...), custom_call_target="tpu_custom_call" | custom-call | tf_op jit(solution)/shard_map/update/pallas_call | solution.py:39
  74.7 2.2 %collective-permute-start.7 = (bf16[1,48,192]{2,1,0:T(8,128)(2,1)S(1)}, bf16[1,48,192]{2,1,0:T(8,128)(2,1)S(1)}, u32[]{:S(2)}, u32[]{:S(2)}) collective-permute-start(bf16[1,48,192]{2,1,0:T(8,128)(2,1)S(1)} %bitcast.7), channel_id=1, source_target_pairs={{0,8},{1,9},{2,10},{3,11},{4,12},{5,13},{6,14},{7,15},{8,0},{9,1},... | collective-permute-start | bytes 55304 | tf_op jit(solution)/shard_map/ppermute | solution.py:309
  76.8 2.6 %collective-permute-done.7.refs_8_ = bf16[1,48,192]{2,1,0:T(8,128)(2,1)S(1)} collective-permute-done((bf16[1,48,192]{2,1,0:T(8,128)(2,1)S(1)}, bf16[1,48,192]{2,1,0:T(8,128)(2,1)S(1)}, u32[]{:S(2)}, u32[]{:S(2)}) %collective-permute-start.7) | collective-permute-done | bytes 18464 | tf_op jit(solution)/shard_map/ppermute | solution.py:309
  79.4 1.5 %collective-permute-start.8 = (bf16[2,48,192]{2,1,0:T(8,128)(2,1)S(1)}, bf16[2,48,192]{2,1,0:T(8,128)(2,1)S(1)}, u32[]{:S(2)}, u32[]{:S(2)}) collective-permute-start(bf16[2,48,192]{2,1,0:T(8,128)(2,1)S(1)} %pad_maximum_fusion.2), channel_id=1, source_target_pairs={{0,4},{1,5},{2,6},{3,7},{4,0},{5,1},{6,2},{7,3},{8,12},{9,13},{10,... | collective-permute-start | bytes 110600 | tf_op jit(solution)/shard_map/ppermute | solution.py:309
  80.9 2.6 %collective-permute-done.8.refs_9_ = bf16[2,48,192]{2,1,0:T(8,128)(2,1)S(1)} collective-permute-done((bf16[2,48,192]{2,1,0:T(8,128)(2,1)S(1)}, bf16[2,48,192]{2,1,0:T(8,128)(2,1)S(1)}, u32[]{:S(2)}, u32[]{:S(2)}) %collective-permute-start.8) | collective-permute-done | bytes 36896 | tf_op jit(solution)/shard_map/ppermute | solution.py:309
  83.6 1.8 %collective-permute-start.9 = (bf16[4,48,192]{2,1,0:T(8,128)(2,1)S(1)}, bf16[4,48,192]{2,1,0:T(8,128)(2,1)S(1)}, u32[]{:S(2)}, u32[]{:S(2)}) collective-permute-start(bf16[4,48,192]{2,1,0:T(8,128)(2,1)S(1)} %pad_maximum_fusion.1), channel_id=1, source_target_pairs={{0,2},{1,3},{2,0},{3,1},{4,6},{5,7},{6,4},{7,5},{8,10},{9,11},{10,... | collective-permute-start | bytes 221192 | tf_op jit(solution)/shard_map/ppermute | solution.py:309
  85.4 2.9 %collective-permute-done.9.refs_10_ = bf16[4,48,192]{2,1,0:T(8,128)(2,1)S(1)} collective-permute-done((bf16[4,48,192]{2,1,0:T(8,128)(2,1)S(1)}, bf16[4,48,192]{2,1,0:T(8,128)(2,1)S(1)}, u32[]{:S(2)}, u32[]{:S(2)}) %collective-permute-start.9) | collective-permute-done | bytes 73760 | tf_op jit(solution)/shard_map/ppermute | solution.py:309
  88.3 0.1 collective-permute-start.10
  88.4 0.9 project.1
  89.3 0.5 collective-permute-done.10.refs_11_
  89.8 7.1 %attend.1 = bf16[12,192,128]{2,1,0:T(8,128)(2,1)} custom-call(s32[3]{0:T(128)S(1)} %copy-done.8, bf16[12,192,128]{2,1,0:T(8,128)(2,1)S(1)} %get-tuple-element.31.refs_1_, bf16[12,192,128]{2,1,0:T(8,128)(2,1)S(1)} %get-tuple-element.32.refs_2_, bf16[12,128,192]{2,1,0:T(8,128)(2,1)S(1)} %get-tuple-element.33.refs_3_, ...), custom_call_target="tpu_custom_call" | custom-call | tf_op jit(solution)/shard_map/attend/pallas_call | solution.py:39
  (44 shorter events, 0.2 us)
Async XLA Ops:
  5.5 8.1 %copy-start.18 = (bf16[16,2304]{1,0:T(8,128)(2,1)S(1)}, bf16[16,2304]{1,0:T(8,128)(2,1)}, u32[]{:S(2)}) copy-start(bf16[16,2304]{1,0:T(8,128)(2,1)} %get-tuple-element.24) | copy-start | bytes 221188
  5.5 9.8 %copy-start.17 = (bf16[16,2304]{1,0:T(8,128)(2,1)S(1)}, bf16[16,2304]{1,0:T(8,128)(2,1)}, u32[]{:S(2)}) copy-start(bf16[16,2304]{1,0:T(8,128)(2,1)} %get-tuple-element.25) | copy-start | bytes 221188
  5.5 9.8 %copy-start.16 = (bf16[16,2304]{1,0:T(8,128)(2,1)S(1)}, bf16[16,2304]{1,0:T(8,128)(2,1)}, u32[]{:S(2)}) copy-start(bf16[16,2304]{1,0:T(8,128)(2,1)} %get-tuple-element.26) | copy-start | bytes 221188
  5.5 11.5 %copy-start.15 = (bf16[16,2304]{1,0:T(8,128)(2,1)S(1)}, bf16[16,2304]{1,0:T(8,128)(2,1)}, u32[]{:S(2)}) copy-start(bf16[16,2304]{1,0:T(8,128)(2,1)} %get-tuple-element.27) | copy-start | bytes 221188
  5.5 11.6 %copy-start.14 = (bf16[16,2304]{1,0:T(8,128)(2,1)S(1)}, bf16[16,2304]{1,0:T(8,128)(2,1)}, u32[]{:S(2)}) copy-start(bf16[16,2304]{1,0:T(8,128)(2,1)} %get-tuple-element.28) | copy-start | bytes 221188
  5.6 23.3 %copy-start.13 = (bf16[16,2304]{1,0:T(8,128)(2,1)S(1)}, bf16[16,2304]{1,0:T(8,128)(2,1)}, u32[]{:S(2)}) copy-start(bf16[16,2304]{1,0:T(8,128)(2,1)} %get-tuple-element.29) | copy-start | bytes 221188
  5.6 45.6 %copy-start = (bf16[16,2304]{1,0:T(8,128)(2,1)S(1)}, bf16[16,2304]{1,0:T(8,128)(2,1)}, u32[]{:S(2)}) copy-start(bf16[16,2304]{1,0:T(8,128)(2,1)} %get-tuple-element.22.refs_2_) | copy-start | bytes 221188
  5.6 45.5 %copy-start.8 = (s32[3]{0:T(128)S(1)}, s32[3]{0:T(128)}, u32[]{:S(2)}) copy-start(s32[3]{0:T(128)} %pad_add_fusion.refs_0_) | copy-start | bytes 40
  5.6 45.5 %all-to-all-start = ((bf16[16,16,3456]{2,1,0:T(8,128)(2,1)}), bf16[16,16,3456]{2,1,0:T(8,128)(2,1)S(1)}, u32[]{:S(2)}, u32[]{:S(2)}) async-start(bf16[16,16,3456]{2,1,0:T(8,128)(2,1)} %get-tuple-element.21), calls=%async_computation | async-start | bytes 3538944 | tf_op jit(solution)/shard_map/all_to_all | solution.py:360
  13.1 4.0 %collective-permute-start = (bf16[16,2304]{1,0:T(8,128)(2,1)S(1)}, bf16[16,2304]{1,0:T(8,128)(2,1)S(1)}, u32[]{:S(2)}, u32[]{:S(2)}) collective-permute-start(bf16[16,2304]{1,0:T(8,128)(2,1)S(1)} %copy-done.19), channel_id=1, source_target_pairs={{0,1},{1,0},{2,3},{3,2},{4,5},{5,4},{6,7},{7,6},{8,9},{9,8},{10,11... | collective-permute-start | bytes 221192 | tf_op jit(solution)/shard_map/ppermute | solution.py:344
  13.6 15.2 %collective-permute-start.1 = (bf16[16,2304]{1,0:T(8,128)(2,1)S(1)}, bf16[16,2304]{1,0:T(8,128)(2,1)S(1)}, u32[]{:S(2)}, u32[]{:S(2)}) collective-permute-start(bf16[16,2304]{1,0:T(8,128)(2,1)S(1)} %copy-done.18), channel_id=1, source_target_pairs={{0,2},{1,3},{2,0},{3,1},{4,6},{5,7},{6,4},{7,5},{8,10},{9,11},{10,... | collective-permute-start | bytes 221192 | tf_op jit(solution)/shard_map/ppermute | solution.py:344
  15.3 14.2 %collective-permute-start.2 = (bf16[16,2304]{1,0:T(8,128)(2,1)S(1)}, bf16[16,2304]{1,0:T(8,128)(2,1)S(1)}, u32[]{:S(2)}, u32[]{:S(2)}) collective-permute-start(bf16[16,2304]{1,0:T(8,128)(2,1)S(1)} %copy-done.17), channel_id=1, source_target_pairs={{0,3},{1,2},{2,1},{3,0},{4,7},{5,6},{6,5},{7,4},{8,11},{9,10},{10,... | collective-permute-start | bytes 221192 | tf_op jit(solution)/shard_map/ppermute | solution.py:344
  15.3 29.3 %collective-permute-start.3 = (bf16[16,2304]{1,0:T(8,128)(2,1)S(1)}, bf16[16,2304]{1,0:T(8,128)(2,1)S(1)}, u32[]{:S(2)}, u32[]{:S(2)}) collective-permute-start(bf16[16,2304]{1,0:T(8,128)(2,1)S(1)} %copy-done.16), channel_id=1, source_target_pairs={{0,4},{1,5},{2,6},{3,7},{4,0},{5,1},{6,2},{7,3},{8,12},{9,13},{10,... | collective-permute-start | bytes 221192 | tf_op jit(solution)/shard_map/ppermute | solution.py:344
  17.0 29.2 %collective-permute-start.4 = (bf16[16,2304]{1,0:T(8,128)(2,1)S(1)}, bf16[16,2304]{1,0:T(8,128)(2,1)S(1)}, u32[]{:S(2)}, u32[]{:S(2)}) collective-permute-start(bf16[16,2304]{1,0:T(8,128)(2,1)S(1)} %copy-done.15), channel_id=1, source_target_pairs={{0,5},{1,4},{2,7},{3,6},{4,1},{5,0},{6,3},{7,2},{8,13},{9,12},{10,... | collective-permute-start | bytes 221192 | tf_op jit(solution)/shard_map/ppermute | solution.py:344
  17.1 30.6 %collective-permute-start.5 = (bf16[16,2304]{1,0:T(8,128)(2,1)S(1)}, bf16[16,2304]{1,0:T(8,128)(2,1)S(1)}, u32[]{:S(2)}, u32[]{:S(2)}) collective-permute-start(bf16[16,2304]{1,0:T(8,128)(2,1)S(1)} %copy-done.14), channel_id=1, source_target_pairs={{0,6},{1,7},{2,4},{3,5},{4,2},{5,3},{6,0},{7,1},{8,14},{9,15},{10,... | collective-permute-start | bytes 221192 | tf_op jit(solution)/shard_map/ppermute | solution.py:344
  28.8 22.3 %collective-permute-start.6 = (bf16[16,2304]{1,0:T(8,128)(2,1)S(1)}, bf16[16,2304]{1,0:T(8,128)(2,1)S(1)}, u32[]{:S(2)}, u32[]{:S(2)}) collective-permute-start(bf16[16,2304]{1,0:T(8,128)(2,1)S(1)} %copy-done.13), channel_id=1, source_target_pairs={{0,7},{1,6},{2,5},{3,4},{4,3},{5,2},{6,1},{7,0},{8,15},{9,14},{10,... | collective-permute-start | bytes 221192 | tf_op jit(solution)/shard_map/ppermute | solution.py:344
  51.1 10.7 %copy-start.12 = (bf16[128,4]{0,1:T(4,128)(2,1)S(1)}, bf16[128,4]{0,1:T(4,128)(2,1)}, u32[]{:S(2)}) copy-start(bf16[128,4]{0,1:T(4,128)(2,1)} %param.25) | copy-start | bytes 3076
  51.1 20.3 %copy-start.1 = (bf16[128,128]{1,0:T(8,128)(2,1)S(1)}, bf16[128,128]{1,0:T(8,128)(2,1)}, u32[]{:S(2)}) copy-start(bf16[128,128]{1,0:T(8,128)(2,1)} %refs_1_.4) | copy-start | bytes 98308
  51.1 20.3 %copy-start.2 = (bf16[128,128]{1,0:T(8,128)(2,1)S(1)}, bf16[128,128]{1,0:T(8,128)(2,1)}, u32[]{:S(2)}) copy-start(bf16[128,128]{1,0:T(8,128)(2,1)} %refs_3_.4) | copy-start | bytes 98308
  51.2 20.2 %copy-start.9 = (f32[128]{0:T(128)S(1)}, f32[128]{0:T(128)}, u32[]{:S(2)}) copy-start(f32[128]{0:T(128)} %param.16) | copy-start | bytes 1540
  51.2 20.2 %copy-start.10 = (f32[128]{0:T(128)S(1)}, f32[128]{0:T(128)}, u32[]{:S(2)}) copy-start(f32[128]{0:T(128)} %param.19) | copy-start | bytes 1540
  51.2 20.2 %copy-start.11 = (f32[128]{0:T(128)S(1)}, f32[128]{0:T(128)}, u32[]{:S(2)}) copy-start(f32[128]{0:T(128)} %param.21) | copy-start | bytes 1540
  54.7 16.7 %all-to-all-start.1 = ((bf16[8,16,2304]{2,1,0:T(8,128)(2,1)}), bf16[8,16,2304]{2,1,0:T(8,128)(2,1)S(1)}, u32[]{:S(2)}, u32[]{:S(2)}) async-start(bf16[8,16,2304]{2,1,0:T(8,128)(2,1)} %outer.1), calls=%async_computation.1 | async-start | bytes 1179648 | tf_op jit(solution)/shard_map/all_to_all | solution.py:378
  61.9 26.5 %copy-start.4 = (bf16[128,128]{1,0:T(8,128)(2,1)S(1)}, bf16[128,128]{1,0:T(8,128)(2,1)}, u32[]{:S(2)}) copy-start(bf16[128,128]{1,0:T(8,128)(2,1)} %refs_1_.5) | copy-start | bytes 98308
  61.9 26.5 %copy-start.5 = (bf16[128,128]{1,0:T(8,128)(2,1)S(1)}, bf16[128,128]{1,0:T(8,128)(2,1)}, u32[]{:S(2)}) copy-start(bf16[128,128]{1,0:T(8,128)(2,1)} %refs_2_.1) | copy-start | bytes 98308
  61.9 26.5 %copy-start.6 = (bf16[128,128]{1,0:T(8,128)(2,1)S(1)}, bf16[128,128]{1,0:T(8,128)(2,1)}, u32[]{:S(2)}) copy-start(bf16[128,128]{1,0:T(8,128)(2,1)} %refs_3_.5) | copy-start | bytes 98308
  61.9 26.5 %copy-start.7 = (bf16[128,128]{1,0:T(8,128)(2,1)S(1)}, bf16[128,128]{1,0:T(8,128)(2,1)}, u32[]{:S(2)}) copy-start(bf16[128,128]{1,0:T(8,128)(2,1)} %refs_4_.1) | copy-start | bytes 98308
  71.4 18.4 %copy-start.3 = (bf16[128,128]{1,0:T(8,128)(2,1)S(1)}, bf16[128,128]{1,0:T(8,128)(2,1)}, u32[]{:S(2)}) copy-start(bf16[128,128]{1,0:T(8,128)(2,1)} %refs_6_.1) | copy-start | bytes 98308
  74.7 4.7 %collective-permute-start.7 = (bf16[1,48,192]{2,1,0:T(8,128)(2,1)S(1)}, bf16[1,48,192]{2,1,0:T(8,128)(2,1)S(1)}, u32[]{:S(2)}, u32[]{:S(2)}) collective-permute-start(bf16[1,48,192]{2,1,0:T(8,128)(2,1)S(1)} %bitcast.7), channel_id=1, source_target_pairs={{0,8},{1,9},{2,10},{3,11},{4,12},{5,13},{6,14},{7,15},{8,0},{9,1},... | collective-permute-start | bytes 55304 | tf_op jit(solution)/shard_map/ppermute | solution.py:309
  79.4 4.2 %collective-permute-start.8 = (bf16[2,48,192]{2,1,0:T(8,128)(2,1)S(1)}, bf16[2,48,192]{2,1,0:T(8,128)(2,1)S(1)}, u32[]{:S(2)}, u32[]{:S(2)}) collective-permute-start(bf16[2,48,192]{2,1,0:T(8,128)(2,1)S(1)} %pad_maximum_fusion.2), channel_id=1, source_target_pairs={{0,4},{1,5},{2,6},{3,7},{4,0},{5,1},{6,2},{7,3},{8,12},{9,13},{10,... | collective-permute-start | bytes 110600 | tf_op jit(solution)/shard_map/ppermute | solution.py:309
  83.6 4.7 %collective-permute-start.9 = (bf16[4,48,192]{2,1,0:T(8,128)(2,1)S(1)}, bf16[4,48,192]{2,1,0:T(8,128)(2,1)S(1)}, u32[]{:S(2)}, u32[]{:S(2)}) collective-permute-start(bf16[4,48,192]{2,1,0:T(8,128)(2,1)S(1)} %pad_maximum_fusion.1), channel_id=1, source_target_pairs={{0,2},{1,3},{2,0},{3,1},{4,6},{5,7},{6,4},{7,5},{8,10},{9,11},{10,... | collective-permute-start | bytes 221192 | tf_op jit(solution)/shard_map/ppermute | solution.py:309
  88.3 1.5 %collective-permute-start.10 = (bf16[8,48,192]{2,1,0:T(8,128)(2,1)S(1)}, bf16[8,48,192]{2,1,0:T(8,128)(2,1)S(1)}, u32[]{:S(2)}, u32[]{:S(2)}) collective-permute-start(bf16[8,48,192]{2,1,0:T(8,128)(2,1)S(1)} %pad_maximum_fusion), channel_id=1, source_target_pairs={{0,1},{1,0},{2,3},{3,2},{4,5},{5,4},{6,7},{7,6},{8,9},{9,8},{10,11... | collective-permute-start | bytes 442376 | tf_op jit(solution)/shard_map/ppermute | solution.py:309
  (1 other events, 7.6 us)

commit v9 on v8

--- a/solution.py
+++ b/solution.py
@@ -30,17 +30,25 @@
     return lax.dot_general(a, b, (((a_dim,), (b_dim,)), ((), ())), preferred_element_type=F32)
 
 
-def call(kernel, out_shape, args, scratch=(), smem=(), name=None, vmem=VMEM_BYTES):
+def position():
+    return lax.axis_index("row") * lax.axis_size("node") + lax.axis_index("node")
+
+
+def call(kernel, out_shape, args, scratch=(), smem=(), name=None, vmem=VMEM_BYTES, away=0):
     specs = [
         pl.BlockSpec(memory_space=pltpu.SMEM if n in smem else pltpu.VMEM) for n in range(len(args))
     ]
     single = not isinstance(out_shape, (list, tuple))
     inside = pl.BlockSpec(memory_space=pltpu.VMEM)
+    if away:
+        outs = [pl.BlockSpec(memory_space=pl.ANY)] * away + [inside] * (len(out_shape) - away)
+    else:
+        outs = inside if single else [inside] * len(out_shape)
     return pl.pallas_call(
         kernel,
         out_shape=out_shape,
         in_specs=specs,
-        out_specs=inside if single else [inside] * len(out_shape),
+        out_specs=outs,
         scratch_shapes=list(scratch),
         compiler_params=pltpu.CompilerParams(vmem_limit_bytes=vmem),
         name=name,
@@ -61,10 +69,21 @@
         self.block_tiles = -(-self.block // self.chans)
 
 
-def edges_kernel(sz, len_ref, x_ref, ln_ref, w_ref, out_ref, *refs):
+def edges_kernel(sz, len_ref, x_ref, ln_ref, w_ref, away_ref, *refs):
     near = refs[: sz.group]
-    norm_ref, pair_ref = refs[sz.group :]
-    length, first, me = len_ref[0], len_ref[1], len_ref[2]
+    norm_ref, pair_ref, out_ref, sems = refs[sz.group :]
+    length, me = len_ref[0], position()
+    first = me * sz.rows
+    copies = []
+
+    def leave(start, stop):
+        lanes = pl.ds(start * LANES, (stop - start) * LANES)
+        copy = pltpu.make_async_copy(
+            out_ref.at[:, :, lanes], away_ref.at[:, :, lanes], sems.at[len(copies)]
+        )
+        copy.start()
+        copies.append(copy)
+
     cd, ch = sz.chans, sz.channels
     mine = me & (sz.group - 1)
     r = lax.broadcasted_iota(jnp.int32, (ch, ch), 0)
@@ -90,6 +109,7 @@
         for t in range(sz.block_tiles):
             at = (sz.tiles + t) * LANES
             out_ref[d, :, at : at + LANES] = pair_ref[d, t * cd : (t + 1) * cd, :].astype(BF16)
+    leave(sz.tiles, sz.tiles + sz.block_tiles)
     lane = lax.broadcasted_iota(jnp.int32, (1, LANES), 1)
 
     def live(tile):
@@ -114,42 +134,51 @@
             out_ref[g, :, to] = left
             out_ref[sz.group + g, :, to] = left
             near[g][:, to] = edge[ch + g * cd : ch + (g + 1) * cd]
-
-
-def outer_kernel(sz, len_ref, left_ref, *refs):
-    near, out_ref = refs[: sz.group], refs[sz.group]
-    lmain_ref, lrest_ref, rmain_ref, rrest_ref, omain_ref, orest_ref = refs[sz.group + 1 :]
-    mine = len_ref[2] & (sz.group - 1)
+        leave(tile, tile + step)
+    for copy in copies:
+        copy.wait()
+
+
+def unpack(sz, ref, owner, main_ref, rest_ref):
+    cd, w = sz.chans, sz.whole
+    for tile in range(sz.tiles):
+        block = ref[:, tile * LANES : (tile + 1) * LANES].astype(F32)
+        if tile < sz.rows * w:
+            row, m = divmod(tile, w)
+            main_ref[m, pl.ds(pl.multiple_of((owner * sz.rows + row) * cd, 8), cd), :] = block
+        else:
+            row = owner * sz.rows + tile - sz.rows * w
+            rest_ref[pl.ds(pl.multiple_of(row * cd, 8), cd), :] = block
+            rest_ref[pl.ds(pl.multiple_of((row + sz.half) * cd, 8), cd), :] = pltpu.roll(
+                block, sz.rest, 1
+            )
+
+
+def matrix(sz, c, size, main_ref, rest_ref):
+    cd, w = sz.chans, sz.whole
+    parts = [main_ref[m, pl.ds(c, size, stride=cd), :].astype(BF16) for m in range(w)]
+    if sz.rest:
+        parts.append(rest_ref[pl.ds(c, size, stride=cd), :].astype(BF16)[:, : sz.rest])
+    return jnp.concatenate(parts, axis=1) if len(parts) > 1 else parts[0]
+
+
+def right_kernel(sz, *refs):
+    near, (out_ref, main_ref, rest_ref) = refs[: sz.group], refs[sz.group :]
+    mine = position() & (sz.group - 1)
+    for r in range(sz.group):
+        unpack(sz, near[r], mine ^ r, main_ref, rest_ref)
+    for c in range(sz.chans):
+        out_ref[c] = matrix(sz, c, sz.columns, main_ref, rest_ref)
+
+
+def outer_kernel(
+    sz, left_ref, right_ref, out_ref, lmain_ref, lrest_ref, omain_ref, orest_ref
+):
     cd, n, w, half = sz.chans, sz.crop, sz.whole, sz.half
-
-    def unpack(ref, owner, main_ref, rest_ref):
-        for tile in range(sz.tiles):
-            block = ref[:, tile * LANES : (tile + 1) * LANES].astype(F32)
-            if tile < sz.rows * w:
-                row, m = divmod(tile, w)
-                main_ref[m, pl.ds(pl.multiple_of((owner * sz.rows + row) * cd, 8), cd), :] = block
-            else:
-                row = owner * sz.rows + tile - sz.rows * w
-                rest_ref[pl.ds(pl.multiple_of(row * cd, 8), cd), :] = block
-                rest_ref[pl.ds(pl.multiple_of((row + half) * cd, 8), cd), :] = pltpu.roll(
-                    block, sz.rest, 1
-                )
-
     for d in range(sz.devices):
-        unpack(left_ref.at[d], jnp.int32(d), lmain_ref, lrest_ref)
-    for r in range(sz.group):
-        unpack(near[r], mine ^ r, rmain_ref, rrest_ref)
-
-    def matrix(c, size, main_ref, rest_ref):
-        parts = [main_ref[m, pl.ds(c, size, stride=cd), :].astype(BF16) for m in range(w)]
-        if sz.rest:
-            parts.append(rest_ref[pl.ds(c, size, stride=cd), :].astype(BF16)[:, : sz.rest])
-        return jnp.concatenate(parts, axis=1) if len(parts) > 1 else parts[0]
-
+        unpack(sz, left_ref.at[d], jnp.int32(d), lmain_ref, lrest_ref)
     for c in range(cd):
-        outer = dot(
-            matrix(c, sz.columns, rmain_ref, rrest_ref), matrix(c, n, lmain_ref, lrest_ref), 1, 1
-        )
+        outer = dot(right_ref[c], matrix(sz, c, n, lmain_ref, lrest_ref), 1, 1)
         for m in range(w):
             omain_ref[m, pl.ds(c, sz.columns, stride=cd), :] = outer[:, m * LANES : (m + 1) * LANES]
         if sz.rest:
@@ -172,16 +201,25 @@
             out_ref[g, :, tile * LANES : (tile + 1) * LANES] = block.astype(BF16)
 
 
-def update_kernel(
-    sz, lnp_ref, gate_ref, lnh_ref, tri_ref, lna_ref, biasw_ref, sums_ref, pair_ref,
-    first_ref, col_ref, bias_ref, cols_ref, brow_ref,
-):
-    n, w, half, ch, cd = sz.crop, sz.whole, sz.half, sz.channels, sz.chans
+def columns_kernel(sz, pair_ref, lnp_ref, gate_ref, x_ref, gating_ref, cols_ref):
+    cd = sz.chans
     for s in range(sz.devices):
         for t in range(sz.block_tiles):
             at = (sz.tiles + t) * LANES
             rows = pl.ds(s * sz.block + t * cd, cd)
             cols_ref[rows, :] = pair_ref[s, :, at : at + LANES].astype(F32)
+    for j in range(sz.rows):
+        x = cols_ref[pl.ds(j, sz.crop, stride=sz.rows), :]
+        x_ref[j] = x.astype(BF16)
+        normed = norm_last(x, lnp_ref[...]).astype(BF16)
+        gating_ref[j] = sigmoid(dot(normed, gate_ref[...], 1, 0))
+
+
+def update_kernel(
+    sz, x_ref, gating_ref, lnh_ref, tri_ref, lna_ref, biasw_ref, sums_ref,
+    first_ref, col_ref, bias_ref, brow_ref,
+):
+    n, w, half, ch = sz.crop, sz.whole, sz.half, sz.channels
     gain_h = jnp.transpose(jnp.broadcast_to(lnh_ref[...], (ch, ch)))
     tri = tri_ref[...]
 
@@ -200,16 +238,19 @@
             h, q = divmod(j, half)
             parts.append(rest[q][h * sz.rest : (h + 1) * sz.rest])
         change = jnp.concatenate(parts, axis=0) if len(parts) > 1 else parts[0]
-        x = cols_ref[pl.ds(j, n, stride=sz.rows), :]
-        normed = norm_last(x, lnp_ref[...]).astype(BF16)
-        gating = sigmoid(dot(normed, gate_ref[...], 1, 0))
-        first = (x + gating * change).astype(BF16)
+        first = (x_ref[j].astype(F32) + gating_ref[j] * change).astype(BF16)
         first_ref[j] = first
         col = norm_last(first.astype(F32), lna_ref[...]).astype(BF16)
         col_ref[j] = col
         heads = biasw_ref.shape[1]
         brow_ref[pl.ds(j * heads, heads), :] = dot(biasw_ref[...], col, 0, 1)
-    bias_ref[...] = brow_ref[...].astype(BF16)
+    rows = brow_ref[...]
+    part = rows.shape[0] // 2
+    one, two = rows[:part], rows[part:]
+    message = [one[:, : w * LANES], two[:, : w * LANES]]
+    if sz.rest:
+        message += [one[:, w * LANES :], two[:, w * LANES :]]
+    bias_ref[...] = jnp.concatenate(message, axis=1).astype(BF16)
 
 
 def project_kernel(sz, col_ref, q_ref, k_ref, v_ref, g_ref, qo_ref, ko_ref, vo_ref, go_ref):
@@ -232,18 +273,20 @@
 ):
     bias_refs, (out_ref, rows_ref, biasT_ref) = refs[:-3], refs[-3:]
     n, w, ch = sz.crop, sz.whole, sz.channels
-    length, me = len_ref[0], len_ref[2]
+    length, me = len_ref[0], position()
     width = q_ref.shape[2]
     hd = width // heads
-    per = sz.rows * heads
+    per = sz.rows * heads // 2
     for ref, offsets in zip(bias_refs, steps):
         for place, offset in enumerate(offsets):
-            at = pl.ds(pl.multiple_of((me ^ offset) * per, 8), per)
-            part = ref[place].astype(F32) * LOG2E
-            for m in range(w):
-                rows_ref[m, at, :] = part[:, m * LANES : (m + 1) * LANES]
-            if sz.rest:
-                rows_ref[w, at, : sz.rest] = part[:, w * LANES :]
+            block = ref[place].astype(F32) * LOG2E
+            for p in range(2):
+                at = pl.ds(pl.multiple_of(((me ^ offset) * 2 + p) * per, 8), per)
+                for m in range(w):
+                    rows_ref[m, at, :] = block[:, (p * w + m) * LANES : (p * w + m + 1) * LANES]
+                if sz.rest:
+                    tail = block[:, 2 * w * LANES :]
+                    rows_ref[w, at, :] = pltpu.roll(tail, sz.rest, 1) if p else tail
     key = lax.broadcasted_iota(jnp.int32, (n, LANES), 0)
     dead = jnp.where(key < length, 0.0, -1e9 * LOG2E).astype(F32)
     halves = []
@@ -303,14 +346,13 @@
 
 def spread(block, devices):
     pieces, offsets = [block[None]], [[0]]
-    bit = devices // 2
-    while bit:
+    first = [devices // 2, devices // 4, devices // 2 + devices // 4]
+    for partners in [first] + [[devices >> s] for s in range(3, devices.bit_length())]:
         held = jnp.concatenate(pieces, axis=0) if len(pieces) > 1 else pieces[0]
-        got = lax.ppermute(held, AXES, [(d, d ^ bit) for d in range(devices)])
         known = [o for part in offsets for o in part]
-        pieces.append(got)
-        offsets.append([o ^ bit for o in known])
-        bit //= 2
+        for bit in partners:
+            pieces.append(lax.ppermute(held, AXES, [(d, d ^ bit) for d in range(devices)]))
+            offsets.append([o ^ bit for o in known])
     return pieces, offsets
 
 
@@ -323,8 +365,6 @@
     heads = att_bias.shape[1]
     sz = Sizes(rows, crop, devices, ch)
     n, cd = crop, sz.chans
-    me = lax.axis_index(AXES).astype(jnp.int32)
-    info = jnp.stack([length[0], me * rows, me])
     def bound(kernel, *extra):
         def run(*refs):
             return kernel(sz, *extra, *refs)
@@ -348,52 +388,64 @@
     left, *others = call(
         bound(edges_kernel),
         [slab(t + bt, devices)] + [slab(t)] * g,
-        (info, pair_rep, ln_pair[None], tri_in),
+        (length, pair_rep, ln_pair[None], tri_in),
         scratch=[
             pltpu.VMEM((rows * crop, ch), BF16),
             pltpu.VMEM((devices, bt * cd, ch), F32),
+            pltpu.VMEM((devices, cd, (t + bt) * LANES), BF16),
+            pltpu.SemaphoreType.DMA((t + 1,)),
         ],
         smem=(0,),
+        away=1,
         name="edges",
         vmem=VMEM_MOST,
     )
     left = lax.all_to_all(left, AXES, split_axis=0, concat_axis=0, tiled=True)
     near = send(others, 0)
     rest = sz.rest > 0
+    column_rows = sz.columns * cd
+    right = call(
+        bound(right_kernel),
+        shape((cd, sz.columns, n), BF16),
+        tuple(near),
+        scratch=[
+            pltpu.VMEM((sz.whole, column_rows, LANES), F32),
+            pltpu.VMEM((column_rows if rest else 8, LANES), F32),
+        ],
+        name="right",
+    )
     outer = call(
         bound(outer_kernel),
         slab(t, g),
-        (info, left, *near),
+        (left, right),
         scratch=[
             pltpu.VMEM((sz.whole, n * cd, LANES), F32),
             pltpu.VMEM((n * cd if rest else 8, LANES), F32),
-            pltpu.VMEM((sz.whole, sz.columns * cd, LANES), F32),
-            pltpu.VMEM((sz.columns * cd if rest else 8, LANES), F32),
-            pltpu.VMEM((sz.whole, sz.columns * cd, LANES), F32),
-            pltpu.VMEM((sz.columns * cd if rest else 8, LANES), F32),
-        ],
-        smem=(0,),
+            pltpu.VMEM((sz.whole, column_rows, LANES), F32),
+            pltpu.VMEM((column_rows if rest else 8, LANES), F32),
+        ],
         name="outer",
     )
     sums = lax.all_to_all(
         outer, AXES, split_axis=0, concat_axis=0, tiled=True,
         axis_index_groups=[list(range(g)), list(range(g, devices))],
+    )
+    columns, gating = call(
+        bound(columns_kernel),
+        [shape((rows, n, ch), BF16), shape((rows, n, ch), F32)],
+        (left, ln_pair[None], tri_gate),
+        scratch=[pltpu.VMEM((devices * sz.block + cd, ch), F32)],
+        name="columns",
     )
     first, col, bias = call(
         bound(update_kernel),
         [
             shape((rows, n, ch), BF16),
             shape((rows, n, ch), BF16),
-            shape((rows * heads, n), BF16),
-        ],
-        (
-            ln_pair[None], tri_gate, ln_hidden[None], tri_out, ln_att[None], att_bias,
-            sums, left,
-        ),
-        scratch=[
-            pltpu.VMEM((devices * sz.block + cd, ch), F32),
-            pltpu.VMEM((rows * heads, n), F32),
-        ],
+            shape((rows * heads // 2, 2 * n), BF16),
+        ],
+        (columns, gating, ln_hidden[None], tri_out, ln_att[None], att_bias, sums),
+        scratch=[pltpu.VMEM((rows * heads, n), F32)],
         name="update",
     )
     pieces, steps = spread(bias, devices)
@@ -411,7 +463,7 @@
     out = call(
         bound(attend_kernel, heads, steps),
         shape((rows, n, ch), BF16),
-        (info, query, key, value, gate, first, att_out, *pieces),
+        (length, query, key, value, gate, first, att_out, *pieces),
         scratch=[
             pltpu.VMEM((-(-n // LANES), n * heads, LANES), F32),
             pltpu.VMEM((n, heads * n), F32),

time: 97.2 us -> 101 us (1.039); the launches traced: 96.9 us -> 99.6 us
  local copies, waits for them, and re-layouts: 0.24 us -> 8 us
  waiting for transfers between devices: 49.3 us -> 46.1 us
  starting transfers between devices: 26.8 us -> 25.7 us
    unnamed x41 -> x49, local copies, waits for them, and re-layouts: 0.24 us -> 7.99 us
    all_to_all x1, waiting for transfers between devices: 9.36 us -> 6.08 us  [shards(): lax.all_to_all(outer, AXES, split_axis=0, concat_axis=0, tiled=True, axis...]
    ppermute x4 -> x5, starting transfers between devices: 5.58 us -> 5.08 us  [spread(): lax.ppermute(held, AXES, [(d, d ^ bit) for d in range(devices)])]
    ppermute x4 -> x5, waiting for transfers between devices: 8.56 us -> 8.59 us  [spread(): lax.ppermute(held, AXES, [(d, d ^ bit) for d in range(devices)])]
    pallas_call x5 -> x7, Pallas kernels: 18.9 us -> 19 us  [call(): pl.pallas_call(kernel, out_shape=out_shape, in_specs=specs, out_specs=out...]
  transfers between devices with their start and end apart: 13 -> 14, of which waited for: 11 -> 11; matrix products, arithmetic and copies ran while one was open for 0% -> 1% of each run, Pallas kernels for 1% -> 3%
where the time goes in v9:
time: 101 us; the launch traced here: 99.6 us
  waiting for transfers between devices  46.1 us (46%)
  starting transfers between devices  25.7 us (25%)
  Pallas kernels  19 us (19%)
  local copies, waits for them, and re-layouts  8 us (8%)
    ppermute x7, waiting for transfers between devices, send(): lax.ppermute(block, AXES, [(d, d ^ offset ^ r) for d in range(devices)])  31.4 us
    pallas_call x7, Pallas kernels, call(): pl.pallas_call(kernel, out_shape=out_shape, in_specs=specs, out_specs=out...  19 us
    ppermute x5, waiting for transfers between devices, spread(): lax.ppermute(held, AXES, [(d, d ^ bit) for d in range(devices)])  8.59 us
    unnamed x49, local copies, waits for them, and re-layouts  7.99 us
    all_to_all x1, starting transfers between devices, shards(): left = lax.all_to_all(left, AXES, split_axis=0, concat_axis=0, tiled=True)  7.53 us
    ppermute x7, starting transfers between devices, send(): lax.ppermute(block, AXES, [(d, d ^ offset ^ r) for d in range(devices)])  6.55 us
    all_to_all x1, starting transfers between devices, shards(): lax.all_to_all(outer, AXES, split_axis=0, concat_axis=0, tiled=True, axis...  6.54 us
    all_to_all x1, waiting for transfers between devices, shards(): lax.all_to_all(outer, AXES, split_axis=0, concat_axis=0, tiled=True, axis...  6.08 us
  transfers between devices with their start and end apart: 14, of which 11 were waited for; matrix products, arithmetic and copies ran while one was open for 1% of the time, Pallas kernels for 3%

profile of v9, /device:TPU:0, one launch (start us, length us, event | category | flops | bytes accessed | tf_op | source)
XLA Modules:
  0.0 99.6 jit_solution(1662589531622055067)
XLA Ops:
  0.7 4.5 %edges.1 = (bf16[16,16,3456]{2,1,0:T(8,128)(2,1)}, bf16[16,2304]{1,0:T(8,128)(2,1)}, bf16[16,2304]{1,0:T(8,128)(2,1)}, bf16[16,2304]{1,0:T(8,128)(2,1)}, bf16[16...) custom-call(s32[1]{0:T(128)S(6)} %copy.20.refs_0_, ...), custom_call_target="tpu_custom_call" | custom-call | tf_op jit(solution)/shard_map/edges/pallas_call | solution.py:47
  5.3 7.5 %all-to-all-start = ((bf16[16,16,3456]{2,1,0:T(8,128)(2,1)}), bf16[16,16,3456]{2,1,0:T(8,128)(2,1)S(1)}, u32[]{:S(2)}, u32[]{:S(2)}) async-start(bf16[16,16,3456]{2,1,0:T(8,128)(2,1)} %get-tuple-element.23), calls=%async_computation | async-start | bytes 3538944 | tf_op jit(solution)/shard_map/all_to_all | solution.py:403
  13.3 1.7 %collective-permute-start.1 = (bf16[16,2304]{1,0:T(8,128)(2,1)S(1)}, bf16[16,2304]{1,0:T(8,128)(2,1)S(1)}, u32[]{:S(2)}, u32[]{:S(2)}) collective-permute-start(bf16[16,2304]{1,0:T(8,128)(2,1)S(1)} %copy-done.20), channel_id=1, source_target_pairs={{0,2},{1,3},{2,0},{3,1},{4,6},{5,7},{6,4},{7,5},{8,10},{9,11},{10,... | collective-permute-start | bytes 221192 | tf_op jit(solution)/shard_map/ppermute | solution.py:384
  15.0 1.7 %collective-permute-start.3 = (bf16[16,2304]{1,0:T(8,128)(2,1)S(1)}, bf16[16,2304]{1,0:T(8,128)(2,1)S(1)}, u32[]{:S(2)}, u32[]{:S(2)}) collective-permute-start(bf16[16,2304]{1,0:T(8,128)(2,1)S(1)} %copy-done.18), channel_id=1, source_target_pairs={{0,4},{1,5},{2,6},{3,7},{4,0},{5,1},{6,2},{7,3},{8,12},{9,13},{10,... | collective-permute-start | bytes 221192 | tf_op jit(solution)/shard_map/ppermute | solution.py:384
  16.8 2.6 %collective-permute-start.5 = (bf16[16,2304]{1,0:T(8,128)(2,1)S(1)}, bf16[16,2304]{1,0:T(8,128)(2,1)S(1)}, u32[]{:S(2)}, u32[]{:S(2)}) collective-permute-start(bf16[16,2304]{1,0:T(8,128)(2,1)S(1)} %copy-done.16), channel_id=1, source_target_pairs={{0,6},{1,7},{2,4},{3,5},{4,2},{5,3},{6,0},{7,1},{8,14},{9,15},{10,... | collective-permute-start | bytes 221192 | tf_op jit(solution)/shard_map/ppermute | solution.py:384
  19.4 9.1 %collective-permute-done.1.refs_2_ = bf16[16,2304]{1,0:T(8,128)(2,1)S(1)} collective-permute-done((bf16[16,2304]{1,0:T(8,128)(2,1)S(1)}, bf16[16,2304]{1,0:T(8,128)(2,1)S(1)}, u32[]{:S(2)}, u32[]{:S(2)}) %collective-permute-start.1) | collective-permute-done | bytes 73760 | tf_op jit(solution)/shard_map/ppermute | solution.py:384
  29.1 15.1 %collective-permute-done.3.refs_4_ = bf16[16,2304]{1,0:T(8,128)(2,1)S(1)} collective-permute-done((bf16[16,2304]{1,0:T(8,128)(2,1)S(1)}, bf16[16,2304]{1,0:T(8,128)(2,1)S(1)}, u32[]{:S(2)}, u32[]{:S(2)}) %collective-permute-start.3) | collective-permute-done | bytes 73760 | tf_op jit(solution)/shard_map/ppermute | solution.py:384
  44.3 1.6 %collective-permute-done.4.refs_5_ = bf16[16,2304]{1,0:T(8,128)(2,1)S(1)} collective-permute-done((bf16[16,2304]{1,0:T(8,128)(2,1)S(1)}, bf16[16,2304]{1,0:T(8,128)(2,1)S(1)}, u32[]{:S(2)}, u32[]{:S(2)}) %collective-permute-start.4) | collective-permute-done | bytes 73760 | tf_op jit(solution)/shard_map/ppermute | solution.py:384
  45.9 1.6 %collective-permute-done.5.refs_6_ = bf16[16,2304]{1,0:T(8,128)(2,1)S(1)} collective-permute-done((bf16[16,2304]{1,0:T(8,128)(2,1)S(1)}, bf16[16,2304]{1,0:T(8,128)(2,1)S(1)}, u32[]{:S(2)}, u32[]{:S(2)}) %collective-permute-start.5) | collective-permute-done | bytes 73760 | tf_op jit(solution)/shard_map/ppermute | solution.py:384
  47.4 3.4 %collective-permute-done.6.refs_7_ = bf16[16,2304]{1,0:T(8,128)(2,1)S(1)} collective-permute-done((bf16[16,2304]{1,0:T(8,128)(2,1)S(1)}, bf16[16,2304]{1,0:T(8,128)(2,1)S(1)}, u32[]{:S(2)}, u32[]{:S(2)}) %collective-permute-start.6) | collective-permute-done | bytes 73760 | tf_op jit(solution)/shard_map/ppermute | solution.py:384
  51.6 2.4 %outer.1 = bf16[8,16,2304]{2,1,0:T(8,128)(2,1)} custom-call(bf16[16,16,3456]{2,1,0:T(8,128)(2,1)S(1)} %all-to-all-done.refs_0_, bf16[16,96,192]{2,1,0:T(8,128)(2,1)S(1)} %right.1.refs_1_), custom_call_target="tpu_custom_call" | custom-call | tf_op jit(solution)/shard_map/outer/pallas_call | solution.py:47
  54.0 6.5 %all-to-all-start.1 = ((bf16[8,16,2304]{2,1,0:T(8,128)(2,1)}), bf16[8,16,2304]{2,1,0:T(8,128)(2,1)S(1)}, u32[]{:S(2)}, u32[]{:S(2)}) async-start(bf16[8,16,2304]{2,1,0:T(8,128)(2,1)} %outer.1), calls=%async_computation.1 | async-start | bytes 1179648 | tf_op jit(solution)/shard_map/all_to_all | solution.py:429
  61.3 0.8 copy-done.4
  62.0 1.1 %columns.1 = (bf16[12,192,128]{2,1,0:T(8,128)(2,1)S(1)}, f32[12,192,128]{2,1,0:T(8,128)S(1)}) custom-call(bf16[16,16,3456]{2,1,0:T(8,128)(2,1)S(1)} %all-to-all-done.refs_0_, f32[1,128]{1,0:T(1,128)S(1)} %bitcast.12, bf16[128,128]{1,0:T(8,128)(2,1)S(1)} %copy-done.4), custom_call_target="tpu_custom_call" | custom-call | tf_op jit(solution)/shard_map/columns/pallas_call | solution.py:47
  63.2 0.8 copy-done
  64.0 6.1 %all-to-all-done.1.refs_6_ = bf16[8,16,2304]{2,1,0:T(8,128)(2,1)S(1)} async-done(((bf16[8,16,2304]{2,1,0:T(8,128)(2,1)}), bf16[8,16,2304]{2,1,0:T(8,128)(2,1)S(1)}, u32[]{:S(2)}, u32[]{:S(2)}) %all-to-all-start.1) | async-done | bytes 589856 | tf_op jit(solution)/shard_map/all_to_all | solution.py:429
  70.1 1.1 %copy-done.1 = bf16[12,192,128]{2,1,0:T(8,128)(2,1)S(1)} copy-done((bf16[12,192,128]{2,1,0:T(8,128)(2,1)S(1)}, bf16[12,192,128]{2,1,0:T(8,128)(2,1)}, u32[]{:S(2)}) %copy-start.1) | copy-done | bytes 589848
  71.2 0.8 copy-done.2
  71.9 0.8 copy-done.5
  72.7 2.7 %update.1 = (bf16[12,192,128]{2,1,0:T(8,128)(2,1)S(1)}, bf16[12,192,128]{2,1,0:T(8,128)(2,1)S(1)}, bf16[24,384]{1,0:T(8,128)(2,1)S(1)}) custom-call(bf16[12,192,128]{2,1,0:T(8,128)(2,1)S(1)} %copy-done.1, f32[12,192,128]{2,1,0:T(8,128)S(1)} %get-tuple-element.25.refs_1_, f32[1,128]{1,0:T(1,128)S(1)} %bitcast.13, bf16[128,128]{1,0:T(8,128)(2,1)S(1)} %copy-done.5, ...), custom_call_target="tpu_custom_call" | custom-call | tf_op jit(solution)/shard_map/update/pallas_call | solution.py:47
  75.3 2.2 %collective-permute-start.7 = (bf16[1,24,384]{2,1,0:T(8,128)(2,1)S(1)}, bf16[1,24,384]{2,1,0:T(8,128)(2,1)S(1)}, u32[]{:S(2)}, u32[]{:S(2)}) collective-permute-start(bf16[1,24,384]{2,1,0:T(8,128)(2,1)S(1)} %bitcast.6), channel_id=1, source_target_pairs={{0,8},{1,9},{2,10},{3,11},{4,12},{5,13},{6,14},{7,15},{8,0},{9,1},... | collective-permute-start | bytes 55304 | tf_op jit(solution)/shard_map/ppermute | solution.py:354
  77.5 1.5 %collective-permute-start.8 = (bf16[1,24,384]{2,1,0:T(8,128)(2,1)S(1)}, bf16[1,24,384]{2,1,0:T(8,128)(2,1)S(1)}, u32[]{:S(2)}, u32[]{:S(2)}) collective-permute-start(bf16[1,24,384]{2,1,0:T(8,128)(2,1)S(1)} %bitcast.7), channel_id=1, source_target_pairs={{0,4},{1,5},{2,6},{3,7},{4,0},{5,1},{6,2},{7,3},{8,12},{9,13},{10,... | collective-permute-start | bytes 55304 | tf_op jit(solution)/shard_map/ppermute | solution.py:354
  79.0 0.7 collective-permute-start.9
  80.0 1.3 %collective-permute-done.8.refs_9_ = bf16[1,24,384]{2,1,0:T(8,128)(2,1)S(1)} collective-permute-done((bf16[1,24,384]{2,1,0:T(8,128)(2,1)S(1)}, bf16[1,24,384]{2,1,0:T(8,128)(2,1)S(1)}, u32[]{:S(2)}, u32[]{:S(2)}) %collective-permute-start.8) | collective-permute-done | bytes 18464 | tf_op jit(solution)/shard_map/ppermute | solution.py:354
  81.3 3.3 %collective-permute-done.9.refs_10_ = bf16[1,24,384]{2,1,0:T(8,128)(2,1)S(1)} collective-permute-done((bf16[1,24,384]{2,1,0:T(8,128)(2,1)S(1)}, bf16[1,24,384]{2,1,0:T(8,128)(2,1)S(1)}, u32[]{:S(2)}, u32[]{:S(2)}) %collective-permute-start.9) | collective-permute-done | bytes 18464 | tf_op jit(solution)/shard_map/ppermute | solution.py:354
  85.2 3.8 %collective-permute-done.10.refs_11_ = bf16[4,24,384]{2,1,0:T(8,128)(2,1)S(1)} collective-permute-done((bf16[4,24,384]{2,1,0:T(8,128)(2,1)S(1)}, bf16[4,24,384]{2,1,0:T(8,128)(2,1)S(1)}, u32[]{:S(2)}, u32[]{:S(2)}) %collective-permute-start.10) | collective-permute-done | bytes 73760 | tf_op jit(solution)/shard_map/ppermute | solution.py:354
  89.1 0.7 copy-done.7
  89.9 0.8 copy-done.8
  90.6 0.8 copy-done.9
  91.4 0.8 copy-done.10
  92.1 0.9 project.1
  93.0 6.6 %attend.1 = bf16[12,192,128]{2,1,0:T(8,128)(2,1)} custom-call(s32[1]{0:T(128)S(6)} %copy.20.refs_0_, bf16[12,192,128]{2,1,0:T(8,128)(2,1)S(1)} %get-tuple-element.35.refs_1_, bf16[12,192,128]{2,1,0:T(8,128)(2,1)S(1)} %get-tuple-element.36.refs_2_, bf16[12,128,192]{2,1,0:T(8,128)(2,1)S(1)} %get-tuple-element.37.refs_3_, ...), custom_call_target="tpu_custom_call" | custom-call | tf_op jit(solution)/shard_map/attend/pallas_call | solution.py:47
  (54 shorter events, 3.8 us)
Async XLA Ops:
  5.2 7.6 %copy-start.21 = (bf16[16,2304]{1,0:T(8,128)(2,1)S(1)}, bf16[16,2304]{1,0:T(8,128)(2,1)}, u32[]{:S(2)}) copy-start(bf16[16,2304]{1,0:T(8,128)(2,1)} %get-tuple-element.27) | copy-start | bytes 221188
  5.2 8.1 %copy-start.20 = (bf16[16,2304]{1,0:T(8,128)(2,1)S(1)}, bf16[16,2304]{1,0:T(8,128)(2,1)}, u32[]{:S(2)}) copy-start(bf16[16,2304]{1,0:T(8,128)(2,1)} %get-tuple-element.28) | copy-start | bytes 221188
  5.2 9.8 %copy-start.19 = (bf16[16,2304]{1,0:T(8,128)(2,1)S(1)}, bf16[16,2304]{1,0:T(8,128)(2,1)}, u32[]{:S(2)}) copy-start(bf16[16,2304]{1,0:T(8,128)(2,1)} %get-tuple-element.29) | copy-start | bytes 221188
  5.2 9.8 %copy-start.18 = (bf16[16,2304]{1,0:T(8,128)(2,1)S(1)}, bf16[16,2304]{1,0:T(8,128)(2,1)}, u32[]{:S(2)}) copy-start(bf16[16,2304]{1,0:T(8,128)(2,1)} %get-tuple-element.30) | copy-start | bytes 221188
  5.2 11.5 %copy-start.17 = (bf16[16,2304]{1,0:T(8,128)(2,1)S(1)}, bf16[16,2304]{1,0:T(8,128)(2,1)}, u32[]{:S(2)}) copy-start(bf16[16,2304]{1,0:T(8,128)(2,1)} %get-tuple-element.31) | copy-start | bytes 221188
  5.2 11.6 %copy-start.16 = (bf16[16,2304]{1,0:T(8,128)(2,1)S(1)}, bf16[16,2304]{1,0:T(8,128)(2,1)}, u32[]{:S(2)}) copy-start(bf16[16,2304]{1,0:T(8,128)(2,1)} %get-tuple-element.32) | copy-start | bytes 221188
  5.2 23.3 %copy-start.15 = (bf16[16,2304]{1,0:T(8,128)(2,1)S(1)}, bf16[16,2304]{1,0:T(8,128)(2,1)}, u32[]{:S(2)}) copy-start(bf16[16,2304]{1,0:T(8,128)(2,1)} %get-tuple-element.33) | copy-start | bytes 221188
  5.3 45.5 %copy-start.3 = (bf16[16,2304]{1,0:T(8,128)(2,1)S(1)}, bf16[16,2304]{1,0:T(8,128)(2,1)}, u32[]{:S(2)}) copy-start(bf16[16,2304]{1,0:T(8,128)(2,1)} %get-tuple-element.26.refs_0_) | copy-start | bytes 221188
  5.3 46.3 %all-to-all-start = ((bf16[16,16,3456]{2,1,0:T(8,128)(2,1)}), bf16[16,16,3456]{2,1,0:T(8,128)(2,1)S(1)}, u32[]{:S(2)}, u32[]{:S(2)}) async-start(bf16[16,16,3456]{2,1,0:T(8,128)(2,1)} %get-tuple-element.23), calls=%async_computation | async-start | bytes 3538944 | tf_op jit(solution)/shard_map/all_to_all | solution.py:403
  12.8 4.0 %collective-permute-start = (bf16[16,2304]{1,0:T(8,128)(2,1)S(1)}, bf16[16,2304]{1,0:T(8,128)(2,1)S(1)}, u32[]{:S(2)}, u32[]{:S(2)}) collective-permute-start(bf16[16,2304]{1,0:T(8,128)(2,1)S(1)} %copy-done.21), channel_id=1, source_target_pairs={{0,1},{1,0},{2,3},{3,2},{4,5},{5,4},{6,7},{7,6},{8,9},{9,8},{10,11... | collective-permute-start | bytes 221192 | tf_op jit(solution)/shard_map/ppermute | solution.py:384
  13.3 15.2 %collective-permute-start.1 = (bf16[16,2304]{1,0:T(8,128)(2,1)S(1)}, bf16[16,2304]{1,0:T(8,128)(2,1)S(1)}, u32[]{:S(2)}, u32[]{:S(2)}) collective-permute-start(bf16[16,2304]{1,0:T(8,128)(2,1)S(1)} %copy-done.20), channel_id=1, source_target_pairs={{0,2},{1,3},{2,0},{3,1},{4,6},{5,7},{6,4},{7,5},{8,10},{9,11},{10,... | collective-permute-start | bytes 221192 | tf_op jit(solution)/shard_map/ppermute | solution.py:384
  15.0 14.2 %collective-permute-start.2 = (bf16[16,2304]{1,0:T(8,128)(2,1)S(1)}, bf16[16,2304]{1,0:T(8,128)(2,1)S(1)}, u32[]{:S(2)}, u32[]{:S(2)}) collective-permute-start(bf16[16,2304]{1,0:T(8,128)(2,1)S(1)} %copy-done.19), channel_id=1, source_target_pairs={{0,3},{1,2},{2,1},{3,0},{4,7},{5,6},{6,5},{7,4},{8,11},{9,10},{10,... | collective-permute-start | bytes 221192 | tf_op jit(solution)/shard_map/ppermute | solution.py:384
  15.0 29.3 %collective-permute-start.3 = (bf16[16,2304]{1,0:T(8,128)(2,1)S(1)}, bf16[16,2304]{1,0:T(8,128)(2,1)S(1)}, u32[]{:S(2)}, u32[]{:S(2)}) collective-permute-start(bf16[16,2304]{1,0:T(8,128)(2,1)S(1)} %copy-done.18), channel_id=1, source_target_pairs={{0,4},{1,5},{2,6},{3,7},{4,0},{5,1},{6,2},{7,3},{8,12},{9,13},{10,... | collective-permute-start | bytes 221192 | tf_op jit(solution)/shard_map/ppermute | solution.py:384
  16.7 29.2 %collective-permute-start.4 = (bf16[16,2304]{1,0:T(8,128)(2,1)S(1)}, bf16[16,2304]{1,0:T(8,128)(2,1)S(1)}, u32[]{:S(2)}, u32[]{:S(2)}) collective-permute-start(bf16[16,2304]{1,0:T(8,128)(2,1)S(1)} %copy-done.17), channel_id=1, source_target_pairs={{0,5},{1,4},{2,7},{3,6},{4,1},{5,0},{6,3},{7,2},{8,13},{9,12},{10,... | collective-permute-start | bytes 221192 | tf_op jit(solution)/shard_map/ppermute | solution.py:384
  16.8 30.6 %collective-permute-start.5 = (bf16[16,2304]{1,0:T(8,128)(2,1)S(1)}, bf16[16,2304]{1,0:T(8,128)(2,1)S(1)}, u32[]{:S(2)}, u32[]{:S(2)}) collective-permute-start(bf16[16,2304]{1,0:T(8,128)(2,1)S(1)} %copy-done.16), channel_id=1, source_target_pairs={{0,6},{1,7},{2,4},{3,5},{4,2},{5,3},{6,0},{7,1},{8,14},{9,15},{10,... | collective-permute-start | bytes 221192 | tf_op jit(solution)/shard_map/ppermute | solution.py:384
  28.5 22.3 %collective-permute-start.6 = (bf16[16,2304]{1,0:T(8,128)(2,1)S(1)}, bf16[16,2304]{1,0:T(8,128)(2,1)S(1)}, u32[]{:S(2)}, u32[]{:S(2)}) collective-permute-start(bf16[16,2304]{1,0:T(8,128)(2,1)S(1)} %copy-done.15), channel_id=1, source_target_pairs={{0,7},{1,6},{2,5},{3,4},{4,3},{5,2},{6,1},{7,0},{8,15},{9,14},{10,... | collective-permute-start | bytes 221192 | tf_op jit(solution)/shard_map/ppermute | solution.py:384
  51.5 9.0 %copy-start.14 = (bf16[128,4]{0,1:T(4,128)(2,1)S(1)}, bf16[128,4]{0,1:T(4,128)(2,1)}, u32[]{:S(2)}) copy-start(bf16[128,4]{0,1:T(4,128)(2,1)} %param.25) | copy-start | bytes 3076
  51.5 9.7 %copy-start.11 = (f32[128]{0:T(128)S(1)}, f32[128]{0:T(128)}, u32[]{:S(2)}) copy-start(f32[128]{0:T(128)} %param.16) | copy-start | bytes 1540
  54.0 16.1 %copy-start.12 = (f32[128]{0:T(128)S(1)}, f32[128]{0:T(128)}, u32[]{:S(2)}) copy-start(f32[128]{0:T(128)} %param.19) | copy-start | bytes 1540
  54.0 16.1 %copy-start.13 = (f32[128]{0:T(128)S(1)}, f32[128]{0:T(128)}, u32[]{:S(2)}) copy-start(f32[128]{0:T(128)} %param.21) | copy-start | bytes 1540
  54.0 16.1 %all-to-all-start.1 = ((bf16[8,16,2304]{2,1,0:T(8,128)(2,1)}), bf16[8,16,2304]{2,1,0:T(8,128)(2,1)S(1)}, u32[]{:S(2)}, u32[]{:S(2)}) async-start(bf16[8,16,2304]{2,1,0:T(8,128)(2,1)} %outer.1), calls=%async_computation.1 | async-start | bytes 1179648 | tf_op jit(solution)/shard_map/all_to_all | solution.py:429
  61.3 0.8 copy-start.4
  63.2 0.8 copy-start
  70.1 1.1 %copy-start.1 = (bf16[12,192,128]{2,1,0:T(8,128)(2,1)S(1)}, bf16[12,192,128]{2,1,0:T(8,128)(2,1)}, u32[]{:S(2)}) copy-start(bf16[12,192,128]{2,1,0:T(8,128)(2,1)} %copy-done) | copy-start | bytes 1769476
  71.2 0.8 copy-start.2
  72.7 20.4 %copy-start.6 = (bf16[128,128]{1,0:T(8,128)(2,1)S(1)}, bf16[128,128]{1,0:T(8,128)(2,1)}, u32[]{:S(2)}) copy-start(bf16[128,128]{1,0:T(8,128)(2,1)} %refs_6_.1) | copy-start | bytes 98308
  75.3 4.7 %collective-permute-start.7 = (bf16[1,24,384]{2,1,0:T(8,128)(2,1)S(1)}, bf16[1,24,384]{2,1,0:T(8,128)(2,1)S(1)}, u32[]{:S(2)}, u32[]{:S(2)}) collective-permute-start(bf16[1,24,384]{2,1,0:T(8,128)(2,1)S(1)} %bitcast.6), channel_id=1, source_target_pairs={{0,8},{1,9},{2,10},{3,11},{4,12},{5,13},{6,14},{7,15},{8,0},{9,1},... | collective-permute-start | bytes 55304 | tf_op jit(solution)/shard_map/ppermute | solution.py:354
  77.5 3.8 %collective-permute-start.8 = (bf16[1,24,384]{2,1,0:T(8,128)(2,1)S(1)}, bf16[1,24,384]{2,1,0:T(8,128)(2,1)S(1)}, u32[]{:S(2)}, u32[]{:S(2)}) collective-permute-start(bf16[1,24,384]{2,1,0:T(8,128)(2,1)S(1)} %bitcast.7), channel_id=1, source_target_pairs={{0,4},{1,5},{2,6},{3,7},{4,0},{5,1},{6,2},{7,3},{8,12},{9,13},{10,... | collective-permute-start | bytes 55304 | tf_op jit(solution)/shard_map/ppermute | solution.py:354
  79.0 5.6 %collective-permute-start.9 = (bf16[1,24,384]{2,1,0:T(8,128)(2,1)S(1)}, bf16[1,24,384]{2,1,0:T(8,128)(2,1)S(1)}, u32[]{:S(2)}, u32[]{:S(2)}) collective-permute-start(bf16[1,24,384]{2,1,0:T(8,128)(2,1)S(1)} %bitcast.8), channel_id=1, source_target_pairs={{0,12},{1,13},{2,14},{3,15},{4,8},{5,9},{6,10},{7,11},{8,4},{9,5},... | collective-permute-start | bytes 55304 | tf_op jit(solution)/shard_map/ppermute | solution.py:354
  84.6 4.4 %collective-permute-start.10 = (bf16[4,24,384]{2,1,0:T(8,128)(2,1)S(1)}, bf16[4,24,384]{2,1,0:T(8,128)(2,1)S(1)}, u32[]{:S(2)}, u32[]{:S(2)}) collective-permute-start(bf16[4,24,384]{2,1,0:T(8,128)(2,1)S(1)} %pad_maximum_fusion), channel_id=1, source_target_pairs={{0,2},{1,3},{2,0},{3,1},{4,6},{5,7},{6,4},{7,5},{8,10},{9,11},{10,... | collective-permute-start | bytes 221192 | tf_op jit(solution)/shard_map/ppermute | solution.py:354
  89.0 4.0 %collective-permute-start.11 = (bf16[8,24,384]{2,1,0:T(8,128)(2,1)S(1)}, bf16[8,24,384]{2,1,0:T(8,128)(2,1)S(1)}, u32[]{:S(2)}, u32[]{:S(2)}) collective-permute-start(bf16[8,24,384]{2,1,0:T(8,128)(2,1)S(1)} %constant_dynamic-update-slice_fusion), channel_id=1, source_target_pairs={{0,1},{1,0},{2,3},{3,2},{4,5},{5,4},{6,7},{7,6},{8,9},{9,8},{10,11... | collective-permute-start | bytes 442376 | tf_op jit(solution)/shard_map/ppermute | solution.py:354
  89.1 0.8 copy-start.7
  (4 other events, 3.0 us)

commit v10 on v9

--- a/solution.py
+++ b/solution.py
@@ -34,9 +34,12 @@
     return lax.axis_index("row") * lax.axis_size("node") + lax.axis_index("node")
 
 
-def call(kernel, out_shape, args, scratch=(), smem=(), name=None, vmem=VMEM_BYTES, away=0):
+def call(kernel, out_shape, args, scratch=(), smem=(), name=None, vmem=VMEM_BYTES, far=(), away=0):
     specs = [
-        pl.BlockSpec(memory_space=pltpu.SMEM if n in smem else pltpu.VMEM) for n in range(len(args))
+        pl.BlockSpec(
+            memory_space=pltpu.SMEM if n in smem else pl.ANY if n in far else pltpu.VMEM
+        )
+        for n in range(len(args))
     ]
     single = not isinstance(out_shape, (list, tuple))
     inside = pl.BlockSpec(memory_space=pltpu.VMEM)
@@ -70,34 +73,32 @@
 
 
 def edges_kernel(sz, len_ref, x_ref, ln_ref, w_ref, away_ref, *refs):
-    near = refs[: sz.group]
-    norm_ref, pair_ref, out_ref, sems = refs[sz.group :]
+    near_refs = refs[: sz.group]
+    x_buf, w_buf, norm_ref, pair_ref, out_ref, near_ref, in_sems, out_sems = refs[sz.group :]
     length, me = len_ref[0], position()
     first = me * sz.rows
-    copies = []
-
-    def leave(start, stop):
-        lanes = pl.ds(start * LANES, (stop - start) * LANES)
-        copy = pltpu.make_async_copy(
-            out_ref.at[:, :, lanes], away_ref.at[:, :, lanes], sems.at[len(copies)]
-        )
+    arriving = [
+        pltpu.make_async_copy(x_ref.at[row], x_buf.at[row], in_sems.at[row])
+        for row in range(sz.rows)
+    ]
+    weights_in = pltpu.make_async_copy(w_ref, w_buf, in_sems.at[sz.rows])
+    for copy in arriving:
         copy.start()
-        copies.append(copy)
+    weights_in.start()
+    leaving = []
+
+    def leave(source, target):
+        copy = pltpu.make_async_copy(source, target, out_sems.at[len(leaving)])
+        copy.start()
+        leaving.append(copy)
 
     cd, ch = sz.chans, sz.channels
     mine = me & (sz.group - 1)
-    r = lax.broadcasted_iota(jnp.int32, (ch, ch), 0)
-    e = lax.broadcasted_iota(jnp.int32, (ch, ch), 1)
-    plain = (r == e).astype(BF16)
-    slots = (((r // cd) ^ mine) * cd + r % cd == e).astype(BF16)
-    picks = (plain, plain, slots, slots)
-    weights = [dot(pick, w_ref[p], 1, 1).astype(BF16) for p, pick in enumerate(picks)]
-    gate_w = jnp.concatenate([weights[0], weights[2]], axis=0)
-    value_w = jnp.concatenate([weights[1], weights[3]], axis=0)
     gain = ln_ref[...]
     main = sz.whole * LANES
     for row in range(sz.rows):
-        x = x_ref[row].astype(F32)
+        arriving[row].wait()
+        x = x_buf[row].astype(F32)
         for d in range(sz.devices):
             pair_ref[d, row * sz.rows : (row + 1) * sz.rows, :] = x[d * sz.rows : (d + 1) * sz.rows]
         normed = norm_last(x, gain).astype(BF16)
@@ -105,11 +106,14 @@
         if sz.rest:
             h, q = divmod(row, sz.half)
             norm_ref[pl.ds(sz.rows * main + q * LANES + h * sz.rest, sz.rest), :] = normed[main:]
-    for d in range(sz.devices):
-        for t in range(sz.block_tiles):
-            at = (sz.tiles + t) * LANES
-            out_ref[d, :, at : at + LANES] = pair_ref[d, t * cd : (t + 1) * cd, :].astype(BF16)
-    leave(sz.tiles, sz.tiles + sz.block_tiles)
+    r = lax.broadcasted_iota(jnp.int32, (ch, ch), 0)
+    e = lax.broadcasted_iota(jnp.int32, (ch, ch), 1)
+    plain = (r == e).astype(BF16)
+    slots = (((r // cd) ^ mine) * cd + r % cd == e).astype(BF16)
+    weights_in.wait()
+    weights = [
+        dot(pick, w_buf[p], 1, 1).astype(BF16) for p, pick in enumerate((plain, plain, slots, slots))
+    ]
     lane = lax.broadcasted_iota(jnp.int32, (1, LANES), 1)
 
     def live(tile):
@@ -123,19 +127,35 @@
         return ((row < length) & (k < length)).astype(F32)
 
     step = 2 if sz.tiles % 2 == 0 else 1
-    for tile in range(0, sz.tiles, step):
+
+    def edge(gate_w, value_w, tile):
         n = norm_ref[pl.ds(tile * LANES, step * LANES), :]
         mask = jnp.concatenate([live(tile + s) for s in range(step)], axis=1)
-        edge = sigmoid(dot(gate_w, n, 1, 1)) * dot(value_w, n, 1, 1) * mask
-        edge = edge.astype(BF16)
+        return (sigmoid(dot(gate_w, n, 1, 1)) * (dot(value_w, n, 1, 1) * mask)).astype(BF16)
+
+    for tile in range(0, sz.tiles, step):
         to = slice(tile * LANES, (tile + step) * LANES)
+        right = edge(weights[2], weights[3], tile)
         for g in range(sz.group):
-            left = edge[g * cd : (g + 1) * cd]
-            out_ref[g, :, to] = left
-            out_ref[sz.group + g, :, to] = left
-            near[g][:, to] = edge[ch + g * cd : ch + (g + 1) * cd]
-        leave(tile, tile + step)
-    for copy in copies:
+            near_ref[g, :, to] = right[g * cd : (g + 1) * cd]
+    for g in range(sz.group):
+        leave(near_ref.at[g], near_refs[g])
+    for d in range(sz.devices):
+        for t in range(sz.block_tiles):
+            at = (sz.tiles + t) * LANES
+            out_ref[d, :, at : at + LANES] = pair_ref[d, t * cd : (t + 1) * cd, :].astype(BF16)
+    lanes = pl.ds(sz.tiles * LANES, sz.block_tiles * LANES)
+    leave(out_ref.at[:, :, lanes], away_ref.at[:, :, lanes])
+    for tile in range(0, sz.tiles, step):
+        to = slice(tile * LANES, (tile + step) * LANES)
+        left = edge(weights[0], weights[1], tile)
+        for g in range(sz.group):
+            part = left[g * cd : (g + 1) * cd]
+            out_ref[g, :, to] = part
+            out_ref[sz.group + g, :, to] = part
+        lanes = pl.ds(tile * LANES, step * LANES)
+        leave(out_ref.at[:, :, lanes], away_ref.at[:, :, lanes])
+    for copy in leaving:
         copy.wait()
 
 
@@ -201,25 +221,16 @@
             out_ref[g, :, tile * LANES : (tile + 1) * LANES] = block.astype(BF16)
 
 
-def columns_kernel(sz, pair_ref, lnp_ref, gate_ref, x_ref, gating_ref, cols_ref):
-    cd = sz.chans
+def update_kernel(
+    sz, lnp_ref, gate_ref, lnh_ref, tri_ref, lna_ref, biasw_ref, sums_ref, pair_ref,
+    first_ref, col_ref, bias_ref, cols_ref, brow_ref,
+):
+    n, w, half, ch, cd = sz.crop, sz.whole, sz.half, sz.channels, sz.chans
     for s in range(sz.devices):
         for t in range(sz.block_tiles):
             at = (sz.tiles + t) * LANES
             rows = pl.ds(s * sz.block + t * cd, cd)
             cols_ref[rows, :] = pair_ref[s, :, at : at + LANES].astype(F32)
-    for j in range(sz.rows):
-        x = cols_ref[pl.ds(j, sz.crop, stride=sz.rows), :]
-        x_ref[j] = x.astype(BF16)
-        normed = norm_last(x, lnp_ref[...]).astype(BF16)
-        gating_ref[j] = sigmoid(dot(normed, gate_ref[...], 1, 0))
-
-
-def update_kernel(
-    sz, x_ref, gating_ref, lnh_ref, tri_ref, lna_ref, biasw_ref, sums_ref,
-    first_ref, col_ref, bias_ref, brow_ref,
-):
-    n, w, half, ch = sz.crop, sz.whole, sz.half, sz.channels
     gain_h = jnp.transpose(jnp.broadcast_to(lnh_ref[...], (ch, ch)))
     tri = tri_ref[...]
 
@@ -238,7 +249,10 @@
             h, q = divmod(j, half)
             parts.append(rest[q][h * sz.rest : (h + 1) * sz.rest])
         change = jnp.concatenate(parts, axis=0) if len(parts) > 1 else parts[0]
-        first = (x_ref[j].astype(F32) + gating_ref[j] * change).astype(BF16)
+        x = cols_ref[pl.ds(j, n, stride=sz.rows), :]
+        normed = norm_last(x, lnp_ref[...]).astype(BF16)
+        gating = sigmoid(dot(normed, gate_ref[...], 1, 0))
+        first = (x + gating * change).astype(BF16)
         first_ref[j] = first
         col = norm_last(first.astype(F32), lna_ref[...]).astype(BF16)
         col_ref[j] = col
@@ -314,45 +328,73 @@
     lane = lax.broadcasted_iota(jnp.int32, (1, width), 1)
     head_masks = [((lane >= h * hd) & (lane < (h + 1) * hd)).astype(BF16) for h in range(heads)]
     scale = (hd ** (-0.5)) * LOG2E
-    for j in range(sz.rows):
-        q = q_ref[j]
-        masked = [q * head_masks[h] for h in range(heads)]
-        pieces = [masked[h][: w * LANES] for h in range(heads)]
-        if sz.rest:
-            pieces += [masked[h][w * LANES :] for h in range(heads)]
-        stacked = jnp.concatenate(pieces, axis=0)
-        scores = dot(k_ref[j], stacked, 1, 1) * scale + biasT_ref[...]
-        top = jnp.max(scores, axis=0, keepdims=True)
-        weights = jnp.exp2(scores - top)
+    tiles = [[(h, m * LANES, LANES)] for h in range(heads) for m in range(w)]
+    if sz.rest:
+        tiles += [
+            [(h, w * LANES, sz.rest) for h in range(t * per_tile, (t + 1) * per_tile)]
+            for t in range(heads // per_tile)
+        ]
+    units = [list(range(u, min(u + 2, len(tiles)))) for u in range(0, len(tiles), 2)]
+
+    def score(j, unit):
+        stacked = [
+            q_ref[j, start : start + count, :] * head_masks[h]
+            for t in unit
+            for h, start, count in tiles[t]
+        ]
+        lanes = slice(unit[0] * LANES, (unit[-1] + 1) * LANES)
+        return dot(k_ref[j], jnp.concatenate(stacked, axis=0), 1, 1) * scale + biasT_ref[:, lanes]
+
+    def mix(j, unit, scores, mains, rests):
+        weights = jnp.exp2(scores - jnp.max(scores, axis=0, keepdims=True))
         total = jnp.sum(weights, axis=0, keepdims=True)
-        mixed = dot(v_ref[j], weights.astype(BF16), 1, 0)
+        held = sorted({h for t in unit for h, _, _ in tiles[t]})
+        values = v_ref[j, held[0] * hd : (held[-1] + 1) * hd, :]
+        mixed = dot(values, weights.astype(BF16), 1, 0)
         inverse = 1.0 / total
-        mains, rests = [], []
-        for h in range(heads):
-            sl = slice(h * w * LANES, (h + 1) * w * LANES)
-            mains.append(mixed[h * hd : (h + 1) * hd, sl] * inverse[:, sl])
-            if sz.rest:
-                t, part = divmod(h, per_tile)
-                sl = slice((base + t) * LANES, (base + t + 1) * LANES)
-                piece = mixed[h * hd : (h + 1) * hd, sl] * inverse[:, sl]
-                rests.append(piece[:, part * sz.rest : (part + 1) * sz.rest])
-        attended = jnp.concatenate(mains, axis=0)
-        if sz.rest:
-            attended = jnp.concatenate([attended, jnp.concatenate(rests, axis=0)], axis=1)
-        gated = (attended * g_ref[j]).astype(BF16)
-        total_out = first_ref[j].astype(F32) + dot(gated, aout_ref[...], 0, 0)
-        out_ref[j] = total_out.astype(BF16)
+        for place, t in enumerate(unit):
+            lanes = slice(place * LANES, (place + 1) * LANES)
+            for part, (h, start, count) in enumerate(tiles[t]):
+                rows = slice((h - held[0]) * hd, (h - held[0] + 1) * hd)
+                piece = mixed[rows, lanes] * inverse[:, lanes]
+                if count == LANES:
+                    mains[h].append(piece)
+                else:
+                    rests[h] = piece[:, part * sz.rest : (part + 1) * sz.rest]
+
+    order = [(j, u) for j in range(sz.rows) for u in range(len(units))]
+    scores = score(order[0][0], units[order[0][1]])
+    for at, (j, u) in enumerate(order):
+        if u == 0:
+            mains, rests = [[] for _ in range(heads)], [None] * heads
+        now = scores
+        if at + 1 < len(order):
+            scores = score(order[at + 1][0], units[order[at + 1][1]])
+        mix(j, units[u], now, mains, rests)
+        if u == len(units) - 1:
+            attended = jnp.concatenate(
+                [
+                    jnp.concatenate(mains[h] + ([rests[h]] if sz.rest else []), axis=1)
+                    if w + (sz.rest > 0) > 1
+                    else mains[h][0]
+                    for h in range(heads)
+                ],
+                axis=0,
+            )
+            gated = (attended * g_ref[j]).astype(BF16)
+            total_out = first_ref[j].astype(F32) + dot(gated, aout_ref[...], 0, 0)
+            out_ref[j] = total_out.astype(BF16)
 
 
 def spread(block, devices):
     pieces, offsets = [block[None]], [[0]]
-    first = [devices // 2, devices // 4, devices // 2 + devices // 4]
-    for partners in [first] + [[devices >> s] for s in range(3, devices.bit_length())]:
+    bit = devices // 2
+    while bit:
         held = jnp.concatenate(pieces, axis=0) if len(pieces) > 1 else pieces[0]
         known = [o for part in offsets for o in part]
-        for bit in partners:
-            pieces.append(lax.ppermute(held, AXES, [(d, d ^ bit) for d in range(devices)]))
-            offsets.append([o ^ bit for o in known])
+        pieces.append(lax.ppermute(held, AXES, [(d, d ^ bit) for d in range(devices)]))
+        offsets.append([o ^ bit for o in known])
+        bit //= 2
     return pieces, offsets
 
 
@@ -390,13 +432,18 @@
         [slab(t + bt, devices)] + [slab(t)] * g,
         (length, pair_rep, ln_pair[None], tri_in),
         scratch=[
+            pltpu.VMEM(pair_rep.shape, BF16),
+            pltpu.VMEM(tri_in.shape, BF16),
             pltpu.VMEM((rows * crop, ch), BF16),
             pltpu.VMEM((devices, bt * cd, ch), F32),
             pltpu.VMEM((devices, cd, (t + bt) * LANES), BF16),
-            pltpu.SemaphoreType.DMA((t + 1,)),
+            pltpu.VMEM((g, cd, t * LANES), BF16),
+            pltpu.SemaphoreType.DMA((rows + 1,)),
+            pltpu.SemaphoreType.DMA((t + 1 + g,)),
         ],
         smem=(0,),
-        away=1,
+        far=(1, 3),
+        away=1 + g,
         name="edges",
         vmem=VMEM_MOST,
     )
@@ -430,13 +477,6 @@
         outer, AXES, split_axis=0, concat_axis=0, tiled=True,
         axis_index_groups=[list(range(g)), list(range(g, devices))],
     )
-    columns, gating = call(
-        bound(columns_kernel),
-        [shape((rows, n, ch), BF16), shape((rows, n, ch), F32)],
-        (left, ln_pair[None], tri_gate),
-        scratch=[pltpu.VMEM((devices * sz.block + cd, ch), F32)],
-        name="columns",
-    )
     first, col, bias = call(
         bound(update_kernel),
         [
@@ -444,8 +484,14 @@
             shape((rows, n, ch), BF16),
             shape((rows * heads // 2, 2 * n), BF16),
         ],
-        (columns, gating, ln_hidden[None], tri_out, ln_att[None], att_bias, sums),
-        scratch=[pltpu.VMEM((rows * heads, n), F32)],
+        (
+            ln_pair[None], tri_gate, ln_hidden[None], tri_out, ln_att[None], att_bias,
+            sums, left,
+        ),
+        scratch=[
+            pltpu.VMEM((devices * sz.block + cd, ch), F32),
+            pltpu.VMEM((rows * heads, n), F32),
+        ],
         name="update",
     )
     pieces, steps = spread(bias, devices)

time: 101 us -> 95.6 us (0.947)
  local copies, waits for them, and re-layouts: 8 us -> 0.24 us
  waiting for transfers between devices: 46.1 us -> 48.9 us
    unnamed x49 -> x39, local copies, waits for them, and re-layouts: 7.99 us -> 0.24 us
    all_to_all x1, waiting for transfers between devices: 6.08 us -> 9.36 us  [shards(): lax.all_to_all(outer, AXES, split_axis=0, concat_axis=0, tiled=True, axis...]
    ppermute x5 -> x4, waiting for transfers between devices: 8.59 us -> 8.1 us  [spread(): lax.ppermute(held, AXES, [(d, d ^ bit) for d in range(devices)])]
    ppermute x5 -> x4, starting transfers between devices: 5.08 us -> 5.5 us  [spread(): lax.ppermute(held, AXES, [(d, d ^ bit) for d in range(devices)])]
    pallas_call x7 -> x6, Pallas kernels: 19 us -> 19.2 us  [call(): pl.pallas_call(kernel, out_shape=out_shape, in_specs=specs, out_specs=out...]
  transfers between devices with their start and end apart: 14 -> 13, of which waited for: 11 -> 11; matrix products, arithmetic and copies ran while one was open for 1% -> 0% of each run, Pallas kernels for 3% -> 2%
where the time goes in v10:
time: 95.6 us; the launch traced here: 95.3 us
  waiting for transfers between devices  48.9 us (51%)
  starting transfers between devices  25.9 us (27%)
  Pallas kernels  19.2 us (20%)
    ppermute x7, waiting for transfers between devices, send(): lax.ppermute(block, AXES, [(d, d ^ offset ^ r) for d in range(devices)])  31.4 us
    pallas_call x6, Pallas kernels, call(): pl.pallas_call(kernel, out_shape=out_shape, in_specs=specs, out_specs=out...  19.2 us
    all_to_all x1, waiting for transfers between devices, shards(): lax.all_to_all(outer, AXES, split_axis=0, concat_axis=0, tiled=True, axis...  9.36 us
    ppermute x4, waiting for transfers between devices, spread(): lax.ppermute(held, AXES, [(d, d ^ bit) for d in range(devices)])  8.1 us
    all_to_all x1, starting transfers between devices, shards(): left = lax.all_to_all(left, AXES, split_axis=0, concat_axis=0, tiled=True)  7.53 us
    ppermute x7, starting transfers between devices, send(): lax.ppermute(block, AXES, [(d, d ^ offset ^ r) for d in range(devices)])  6.55 us
    all_to_all x1, starting transfers between devices, shards(): lax.all_to_all(outer, AXES, split_axis=0, concat_axis=0, tiled=True, axis...  6.37 us
    ppermute x4, starting transfers between devices, spread(): lax.ppermute(held, AXES, [(d, d ^ bit) for d in range(devices)])  5.5 us
  transfers between devices with their start and end apart: 13, of which 11 were waited for; matrix products, arithmetic and copies ran while one was open for 0% of the time, Pallas kernels for 2%

profile of v10, /device:TPU:0, one launch (start us, length us, event | category | flops | bytes accessed | tf_op | source)
XLA Modules:
  0.0 95.3 jit_solution(4985143634802636695)
XLA Ops:
  0.7 6.2 %edges.1 = (bf16[16,16,3456]{2,1,0:T(8,128)(2,1)}, bf16[16,2304]{1,0:T(8,128)(2,1)}, bf16[16,2304]{1,0:T(8,128)(2,1)}, bf16[16,2304]{1,0:T(8,128)(2,1)}, bf16[16...) custom-call(s32[1]{0:T(128)S(6)} %copy.16.refs_0_, ...), custom_call_target="tpu_custom_call" | custom-call | tf_op jit(solution)/shard_map/edges/pallas_call | solution.py:50
  6.9 0.0 copy-start
  6.9 7.5 %all-to-all-start = ((bf16[16,16,3456]{2,1,0:T(8,128)(2,1)}), bf16[16,16,3456]{2,1,0:T(8,128)(2,1)S(1)}, u32[]{:S(2)}, u32[]{:S(2)}) async-start(bf16[16,16,3456]{2,1,0:T(8,128)(2,1)} %get-tuple-element.21), calls=%async_computation | async-start | bytes 3538944 | tf_op jit(solution)/shard_map/all_to_all | solution.py:450
  14.5 0.5 collective-permute-start
  14.9 1.7 %collective-permute-start.1 = (bf16[16,2304]{1,0:T(8,128)(2,1)S(1)}, bf16[16,2304]{1,0:T(8,128)(2,1)S(1)}, u32[]{:S(2)}, u32[]{:S(2)}) collective-permute-start(bf16[16,2304]{1,0:T(8,128)(2,1)S(1)} %copy-done.17), channel_id=1, source_target_pairs={{0,2},{1,3},{2,0},{3,1},{4,6},{5,7},{6,4},{7,5},{8,10},{9,11},{10,... | collective-permute-start | bytes 221192 | tf_op jit(solution)/shard_map/ppermute | solution.py:426
  16.6 0.0 collective-permute-start.2
  16.6 1.7 %collective-permute-start.3 = (bf16[16,2304]{1,0:T(8,128)(2,1)S(1)}, bf16[16,2304]{1,0:T(8,128)(2,1)S(1)}, u32[]{:S(2)}, u32[]{:S(2)}) collective-permute-start(bf16[16,2304]{1,0:T(8,128)(2,1)S(1)} %copy-done.15), channel_id=1, source_target_pairs={{0,4},{1,5},{2,6},{3,7},{4,0},{5,1},{6,2},{7,3},{8,12},{9,13},{10,... | collective-permute-start | bytes 221192 | tf_op jit(solution)/shard_map/ppermute | solution.py:426
  18.3 0.1 collective-permute-start.4
  18.4 2.6 %collective-permute-start.5 = (bf16[16,2304]{1,0:T(8,128)(2,1)S(1)}, bf16[16,2304]{1,0:T(8,128)(2,1)S(1)}, u32[]{:S(2)}, u32[]{:S(2)}) collective-permute-start(bf16[16,2304]{1,0:T(8,128)(2,1)S(1)} %copy-done.13), channel_id=1, source_target_pairs={{0,6},{1,7},{2,4},{3,5},{4,2},{5,3},{6,0},{7,1},{8,14},{9,15},{10,... | collective-permute-start | bytes 221192 | tf_op jit(solution)/shard_map/ppermute | solution.py:426
  21.0 9.1 %collective-permute-done.1.refs_2_ = bf16[16,2304]{1,0:T(8,128)(2,1)S(1)} collective-permute-done((bf16[16,2304]{1,0:T(8,128)(2,1)S(1)}, bf16[16,2304]{1,0:T(8,128)(2,1)S(1)}, u32[]{:S(2)}, u32[]{:S(2)}) %collective-permute-start.1) | collective-permute-done | bytes 73760 | tf_op jit(solution)/shard_map/ppermute | solution.py:426
  30.2 0.6 collective-permute-done.2.refs_3_
  30.8 15.1 %collective-permute-done.3.refs_4_ = bf16[16,2304]{1,0:T(8,128)(2,1)S(1)} collective-permute-done((bf16[16,2304]{1,0:T(8,128)(2,1)S(1)}, bf16[16,2304]{1,0:T(8,128)(2,1)S(1)}, u32[]{:S(2)}, u32[]{:S(2)}) %collective-permute-start.3) | collective-permute-done | bytes 73760 | tf_op jit(solution)/shard_map/ppermute | solution.py:426
  45.9 1.6 %collective-permute-done.4.refs_5_ = bf16[16,2304]{1,0:T(8,128)(2,1)S(1)} collective-permute-done((bf16[16,2304]{1,0:T(8,128)(2,1)S(1)}, bf16[16,2304]{1,0:T(8,128)(2,1)S(1)}, u32[]{:S(2)}, u32[]{:S(2)}) %collective-permute-start.4) | collective-permute-done | bytes 73760 | tf_op jit(solution)/shard_map/ppermute | solution.py:426
  47.5 1.6 %collective-permute-done.5.refs_6_ = bf16[16,2304]{1,0:T(8,128)(2,1)S(1)} collective-permute-done((bf16[16,2304]{1,0:T(8,128)(2,1)S(1)}, bf16[16,2304]{1,0:T(8,128)(2,1)S(1)}, u32[]{:S(2)}, u32[]{:S(2)}) %collective-permute-start.5) | collective-permute-done | bytes 73760 | tf_op jit(solution)/shard_map/ppermute | solution.py:426
  49.1 3.4 %collective-permute-done.6.refs_7_ = bf16[16,2304]{1,0:T(8,128)(2,1)S(1)} collective-permute-done((bf16[16,2304]{1,0:T(8,128)(2,1)S(1)}, bf16[16,2304]{1,0:T(8,128)(2,1)S(1)}, u32[]{:S(2)}, u32[]{:S(2)}) %collective-permute-start.6) | collective-permute-done | bytes 73760 | tf_op jit(solution)/shard_map/ppermute | solution.py:426
  52.4 0.7 right.1.refs_1_
  53.2 0.0 copy-start.1
  53.3 2.4 %outer.1 = bf16[8,16,2304]{2,1,0:T(8,128)(2,1)} custom-call(bf16[16,16,3456]{2,1,0:T(8,128)(2,1)S(1)} %all-to-all-done.refs_0_.refs_7_, bf16[16,96,192]{2,1,0:T(8,128)(2,1)S(1)} %right.1.refs_1_), custom_call_target="tpu_custom_call" | custom-call | tf_op jit(solution)/shard_map/outer/pallas_call | solution.py:50
  55.7 6.4 %all-to-all-start.1 = ((bf16[8,16,2304]{2,1,0:T(8,128)(2,1)}), bf16[8,16,2304]{2,1,0:T(8,128)(2,1)S(1)}, u32[]{:S(2)}, u32[]{:S(2)}) async-start(bf16[8,16,2304]{2,1,0:T(8,128)(2,1)} %outer.1), calls=%async_computation.1 | async-start | bytes 1179648 | tf_op jit(solution)/shard_map/all_to_all | solution.py:476
  62.1 0.1 copy.15.refs_5_
  62.3 9.4 %all-to-all-done.1.refs_6_ = bf16[8,16,2304]{2,1,0:T(8,128)(2,1)S(1)} async-done(((bf16[8,16,2304]{2,1,0:T(8,128)(2,1)}), bf16[8,16,2304]{2,1,0:T(8,128)(2,1)S(1)}, u32[]{:S(2)}, u32[]{:S(2)}) %all-to-all-start.1) | async-done | bytes 589856 | tf_op jit(solution)/shard_map/all_to_all | solution.py:476
  71.7 3.3 %update.1 = (bf16[12,192,128]{2,1,0:T(8,128)(2,1)S(1)}, bf16[12,192,128]{2,1,0:T(8,128)(2,1)S(1)}, bf16[24,384]{1,0:T(8,128)(2,1)S(1)}) custom-call(f32[1,128]{1,0:T(1,128)S(1)} %bitcast.11, bf16[128,128]{1,0:T(8,128)(2,1)S(1)} %copy-done.1, f32[1,128]{1,0:T(1,128)S(1)} %bitcast.12, bf16[128,128]{1,0:T(8,128)(2,1)S(1)} %copy-done.2, f32[1,128]{1,0:T(1,128)S(1)} %bitcast.13, ...), custom_call_target="tpu_custom_call" | custom-call | tf_op jit(solution)/shard_map/update/pallas_call | solution.py:50
  74.9 2.2 %collective-permute-start.7 = (bf16[1,24,384]{2,1,0:T(8,128)(2,1)S(1)}, bf16[1,24,384]{2,1,0:T(8,128)(2,1)S(1)}, u32[]{:S(2)}, u32[]{:S(2)}) collective-permute-start(bf16[1,24,384]{2,1,0:T(8,128)(2,1)S(1)} %bitcast.5), channel_id=1, source_target_pairs={{0,8},{1,9},{2,10},{3,11},{4,12},{5,13},{6,14},{7,15},{8,0},{9,1},... | collective-permute-start | bytes 55304 | tf_op jit(solution)/shard_map/ppermute | solution.py:395
  77.1 2.5 %collective-permute-done.7.refs_8_ = bf16[1,24,384]{2,1,0:T(8,128)(2,1)S(1)} collective-permute-done((bf16[1,24,384]{2,1,0:T(8,128)(2,1)S(1)}, bf16[1,24,384]{2,1,0:T(8,128)(2,1)S(1)}, u32[]{:S(2)}, u32[]{:S(2)}) %collective-permute-start.7) | collective-permute-done | bytes 18464 | tf_op jit(solution)/shard_map/ppermute | solution.py:395
  79.6 1.5 %collective-permute-start.8 = (bf16[2,24,384]{2,1,0:T(8,128)(2,1)S(1)}, bf16[2,24,384]{2,1,0:T(8,128)(2,1)S(1)}, u32[]{:S(2)}, u32[]{:S(2)}) collective-permute-start(bf16[2,24,384]{2,1,0:T(8,128)(2,1)S(1)} %pad_maximum_fusion.2), channel_id=1, source_target_pairs={{0,4},{1,5},{2,6},{3,7},{4,0},{5,1},{6,2},{7,3},{8,12},{9,13},{10,... | collective-permute-start | bytes 110600 | tf_op jit(solution)/shard_map/ppermute | solution.py:395
  81.2 2.5 %collective-permute-done.8.refs_9_ = bf16[2,24,384]{2,1,0:T(8,128)(2,1)S(1)} collective-permute-done((bf16[2,24,384]{2,1,0:T(8,128)(2,1)S(1)}, bf16[2,24,384]{2,1,0:T(8,128)(2,1)S(1)}, u32[]{:S(2)}, u32[]{:S(2)}) %collective-permute-start.8) | collective-permute-done | bytes 36896 | tf_op jit(solution)/shard_map/ppermute | solution.py:395
  83.7 1.7 %collective-permute-start.9 = (bf16[4,24,384]{2,1,0:T(8,128)(2,1)S(1)}, bf16[4,24,384]{2,1,0:T(8,128)(2,1)S(1)}, u32[]{:S(2)}, u32[]{:S(2)}) collective-permute-start(bf16[4,24,384]{2,1,0:T(8,128)(2,1)S(1)} %pad_maximum_fusion.1), channel_id=1, source_target_pairs={{0,2},{1,3},{2,0},{3,1},{4,6},{5,7},{6,4},{7,5},{8,10},{9,11},{10,... | collective-permute-start | bytes 221192 | tf_op jit(solution)/shard_map/ppermute | solution.py:395
  85.4 2.7 %collective-permute-done.9.refs_10_ = bf16[4,24,384]{2,1,0:T(8,128)(2,1)S(1)} collective-permute-done((bf16[4,24,384]{2,1,0:T(8,128)(2,1)S(1)}, bf16[4,24,384]{2,1,0:T(8,128)(2,1)S(1)}, u32[]{:S(2)}, u32[]{:S(2)}) %collective-permute-start.9) | collective-permute-done | bytes 73760 | tf_op jit(solution)/shard_map/ppermute | solution.py:395
  88.1 0.1 collective-permute-start.10
  88.2 0.9 project.1
  89.1 0.4 collective-permute-done.10.refs_11_
  89.6 5.7 %attend.1 = bf16[12,192,128]{2,1,0:T(8,128)(2,1)} custom-call(s32[1]{0:T(128)S(6)} %copy.16.refs_0_, bf16[12,192,128]{2,1,0:T(8,128)(2,1)S(1)} %get-tuple-element.31.refs_1_, bf16[12,192,128]{2,1,0:T(8,128)(2,1)S(1)} %get-tuple-element.32.refs_2_, bf16[12,128,192]{2,1,0:T(8,128)(2,1)S(1)} %get-tuple-element.33.refs_3_, ...), custom_call_target="tpu_custom_call" | custom-call | tf_op jit(solution)/shard_map/attend/pallas_call | solution.py:50
  (42 shorter events, 0.2 us)
Async XLA Ops:
  6.8 7.6 %copy-start.18 = (bf16[16,2304]{1,0:T(8,128)(2,1)S(1)}, bf16[16,2304]{1,0:T(8,128)(2,1)}, u32[]{:S(2)}) copy-start(bf16[16,2304]{1,0:T(8,128)(2,1)} %get-tuple-element.23) | copy-start | bytes 221188
  6.8 8.1 %copy-start.17 = (bf16[16,2304]{1,0:T(8,128)(2,1)S(1)}, bf16[16,2304]{1,0:T(8,128)(2,1)}, u32[]{:S(2)}) copy-start(bf16[16,2304]{1,0:T(8,128)(2,1)} %get-tuple-element.24) | copy-start | bytes 221188
  6.9 9.8 %copy-start.16 = (bf16[16,2304]{1,0:T(8,128)(2,1)S(1)}, bf16[16,2304]{1,0:T(8,128)(2,1)}, u32[]{:S(2)}) copy-start(bf16[16,2304]{1,0:T(8,128)(2,1)} %get-tuple-element.25) | copy-start | bytes 221188
  6.9 9.8 %copy-start.15 = (bf16[16,2304]{1,0:T(8,128)(2,1)S(1)}, bf16[16,2304]{1,0:T(8,128)(2,1)}, u32[]{:S(2)}) copy-start(bf16[16,2304]{1,0:T(8,128)(2,1)} %get-tuple-element.26) | copy-start | bytes 221188
  6.9 11.5 %copy-start.14 = (bf16[16,2304]{1,0:T(8,128)(2,1)S(1)}, bf16[16,2304]{1,0:T(8,128)(2,1)}, u32[]{:S(2)}) copy-start(bf16[16,2304]{1,0:T(8,128)(2,1)} %get-tuple-element.27) | copy-start | bytes 221188
  6.9 11.6 %copy-start.13 = (bf16[16,2304]{1,0:T(8,128)(2,1)S(1)}, bf16[16,2304]{1,0:T(8,128)(2,1)}, u32[]{:S(2)}) copy-start(bf16[16,2304]{1,0:T(8,128)(2,1)} %get-tuple-element.28) | copy-start | bytes 221188
  6.9 23.3 %copy-start.12 = (bf16[16,2304]{1,0:T(8,128)(2,1)S(1)}, bf16[16,2304]{1,0:T(8,128)(2,1)}, u32[]{:S(2)}) copy-start(bf16[16,2304]{1,0:T(8,128)(2,1)} %get-tuple-element.29) | copy-start | bytes 221188
  6.9 45.5 %copy-start = (bf16[16,2304]{1,0:T(8,128)(2,1)S(1)}, bf16[16,2304]{1,0:T(8,128)(2,1)}, u32[]{:S(2)}) copy-start(bf16[16,2304]{1,0:T(8,128)(2,1)} %get-tuple-element.22.refs_0_) | copy-start | bytes 221188
  6.9 46.3 %all-to-all-start = ((bf16[16,16,3456]{2,1,0:T(8,128)(2,1)}), bf16[16,16,3456]{2,1,0:T(8,128)(2,1)S(1)}, u32[]{:S(2)}, u32[]{:S(2)}) async-start(bf16[16,16,3456]{2,1,0:T(8,128)(2,1)} %get-tuple-element.21), calls=%async_computation | async-start | bytes 3538944 | tf_op jit(solution)/shard_map/all_to_all | solution.py:450
  14.5 4.0 %collective-permute-start = (bf16[16,2304]{1,0:T(8,128)(2,1)S(1)}, bf16[16,2304]{1,0:T(8,128)(2,1)S(1)}, u32[]{:S(2)}, u32[]{:S(2)}) collective-permute-start(bf16[16,2304]{1,0:T(8,128)(2,1)S(1)} %copy-done.18), channel_id=1, source_target_pairs={{0,1},{1,0},{2,3},{3,2},{4,5},{5,4},{6,7},{7,6},{8,9},{9,8},{10,11... | collective-permute-start | bytes 221192 | tf_op jit(solution)/shard_map/ppermute | solution.py:426
  14.9 15.2 %collective-permute-start.1 = (bf16[16,2304]{1,0:T(8,128)(2,1)S(1)}, bf16[16,2304]{1,0:T(8,128)(2,1)S(1)}, u32[]{:S(2)}, u32[]{:S(2)}) collective-permute-start(bf16[16,2304]{1,0:T(8,128)(2,1)S(1)} %copy-done.17), channel_id=1, source_target_pairs={{0,2},{1,3},{2,0},{3,1},{4,6},{5,7},{6,4},{7,5},{8,10},{9,11},{10,... | collective-permute-start | bytes 221192 | tf_op jit(solution)/shard_map/ppermute | solution.py:426
  16.6 14.2 %collective-permute-start.2 = (bf16[16,2304]{1,0:T(8,128)(2,1)S(1)}, bf16[16,2304]{1,0:T(8,128)(2,1)S(1)}, u32[]{:S(2)}, u32[]{:S(2)}) collective-permute-start(bf16[16,2304]{1,0:T(8,128)(2,1)S(1)} %copy-done.16), channel_id=1, source_target_pairs={{0,3},{1,2},{2,1},{3,0},{4,7},{5,6},{6,5},{7,4},{8,11},{9,10},{10,... | collective-permute-start | bytes 221192 | tf_op jit(solution)/shard_map/ppermute | solution.py:426
  16.6 29.3 %collective-permute-start.3 = (bf16[16,2304]{1,0:T(8,128)(2,1)S(1)}, bf16[16,2304]{1,0:T(8,128)(2,1)S(1)}, u32[]{:S(2)}, u32[]{:S(2)}) collective-permute-start(bf16[16,2304]{1,0:T(8,128)(2,1)S(1)} %copy-done.15), channel_id=1, source_target_pairs={{0,4},{1,5},{2,6},{3,7},{4,0},{5,1},{6,2},{7,3},{8,12},{9,13},{10,... | collective-permute-start | bytes 221192 | tf_op jit(solution)/shard_map/ppermute | solution.py:426
  18.3 29.2 %collective-permute-start.4 = (bf16[16,2304]{1,0:T(8,128)(2,1)S(1)}, bf16[16,2304]{1,0:T(8,128)(2,1)S(1)}, u32[]{:S(2)}, u32[]{:S(2)}) collective-permute-start(bf16[16,2304]{1,0:T(8,128)(2,1)S(1)} %copy-done.14), channel_id=1, source_target_pairs={{0,5},{1,4},{2,7},{3,6},{4,1},{5,0},{6,3},{7,2},{8,13},{9,12},{10,... | collective-permute-start | bytes 221192 | tf_op jit(solution)/shard_map/ppermute | solution.py:426
  18.4 30.6 %collective-permute-start.5 = (bf16[16,2304]{1,0:T(8,128)(2,1)S(1)}, bf16[16,2304]{1,0:T(8,128)(2,1)S(1)}, u32[]{:S(2)}, u32[]{:S(2)}) collective-permute-start(bf16[16,2304]{1,0:T(8,128)(2,1)S(1)} %copy-done.13), channel_id=1, source_target_pairs={{0,6},{1,7},{2,4},{3,5},{4,2},{5,3},{6,0},{7,1},{8,14},{9,15},{10,... | collective-permute-start | bytes 221192 | tf_op jit(solution)/shard_map/ppermute | solution.py:426
  30.2 22.3 %collective-permute-start.6 = (bf16[16,2304]{1,0:T(8,128)(2,1)S(1)}, bf16[16,2304]{1,0:T(8,128)(2,1)S(1)}, u32[]{:S(2)}, u32[]{:S(2)}) collective-permute-start(bf16[16,2304]{1,0:T(8,128)(2,1)S(1)} %copy-done.12), channel_id=1, source_target_pairs={{0,7},{1,6},{2,5},{3,4},{4,3},{5,2},{6,1},{7,0},{8,15},{9,14},{10,... | collective-permute-start | bytes 221192 | tf_op jit(solution)/shard_map/ppermute | solution.py:426
  53.2 8.9 %copy-start.11 = (bf16[128,4]{0,1:T(4,128)(2,1)S(1)}, bf16[128,4]{0,1:T(4,128)(2,1)}, u32[]{:S(2)}) copy-start(bf16[128,4]{0,1:T(4,128)(2,1)} %param.25) | copy-start | bytes 3076
  53.2 18.4 %copy-start.1 = (bf16[128,128]{1,0:T(8,128)(2,1)S(1)}, bf16[128,128]{1,0:T(8,128)(2,1)}, u32[]{:S(2)}) copy-start(bf16[128,128]{1,0:T(8,128)(2,1)} %refs_1_.4) | copy-start | bytes 98308
  53.2 18.4 %copy-start.2 = (bf16[128,128]{1,0:T(8,128)(2,1)S(1)}, bf16[128,128]{1,0:T(8,128)(2,1)}, u32[]{:S(2)}) copy-start(bf16[128,128]{1,0:T(8,128)(2,1)} %refs_3_.4) | copy-start | bytes 98308
  53.2 18.4 %copy-start.8 = (f32[128]{0:T(128)S(1)}, f32[128]{0:T(128)}, u32[]{:S(2)}) copy-start(f32[128]{0:T(128)} %param.16) | copy-start | bytes 1540
  53.2 18.4 %copy-start.9 = (f32[128]{0:T(128)S(1)}, f32[128]{0:T(128)}, u32[]{:S(2)}) copy-start(f32[128]{0:T(128)} %param.19) | copy-start | bytes 1540
  53.2 18.4 %copy-start.10 = (f32[128]{0:T(128)S(1)}, f32[128]{0:T(128)}, u32[]{:S(2)}) copy-start(f32[128]{0:T(128)} %param.21) | copy-start | bytes 1540
  55.7 15.9 %all-to-all-start.1 = ((bf16[8,16,2304]{2,1,0:T(8,128)(2,1)}), bf16[8,16,2304]{2,1,0:T(8,128)(2,1)S(1)}, u32[]{:S(2)}, u32[]{:S(2)}) async-start(bf16[8,16,2304]{2,1,0:T(8,128)(2,1)} %outer.1), calls=%async_computation.1 | async-start | bytes 1179648 | tf_op jit(solution)/shard_map/all_to_all | solution.py:476
  62.1 26.1 %copy-start.4 = (bf16[128,128]{1,0:T(8,128)(2,1)S(1)}, bf16[128,128]{1,0:T(8,128)(2,1)}, u32[]{:S(2)}) copy-start(bf16[128,128]{1,0:T(8,128)(2,1)} %refs_1_.5) | copy-start | bytes 98308
  62.1 26.1 %copy-start.5 = (bf16[128,128]{1,0:T(8,128)(2,1)S(1)}, bf16[128,128]{1,0:T(8,128)(2,1)}, u32[]{:S(2)}) copy-start(bf16[128,128]{1,0:T(8,128)(2,1)} %refs_2_.1) | copy-start | bytes 98308
  62.1 26.1 %copy-start.6 = (bf16[128,128]{1,0:T(8,128)(2,1)S(1)}, bf16[128,128]{1,0:T(8,128)(2,1)}, u32[]{:S(2)}) copy-start(bf16[128,128]{1,0:T(8,128)(2,1)} %refs_3_.5) | copy-start | bytes 98308
  62.1 26.1 %copy-start.7 = (bf16[128,128]{1,0:T(8,128)(2,1)S(1)}, bf16[128,128]{1,0:T(8,128)(2,1)}, u32[]{:S(2)}) copy-start(bf16[128,128]{1,0:T(8,128)(2,1)} %refs_4_.1) | copy-start | bytes 98308
  71.6 17.9 %copy-start.3 = (bf16[128,128]{1,0:T(8,128)(2,1)S(1)}, bf16[128,128]{1,0:T(8,128)(2,1)}, u32[]{:S(2)}) copy-start(bf16[128,128]{1,0:T(8,128)(2,1)} %refs_6_.1) | copy-start | bytes 98308
  74.9 4.7 %collective-permute-start.7 = (bf16[1,24,384]{2,1,0:T(8,128)(2,1)S(1)}, bf16[1,24,384]{2,1,0:T(8,128)(2,1)S(1)}, u32[]{:S(2)}, u32[]{:S(2)}) collective-permute-start(bf16[1,24,384]{2,1,0:T(8,128)(2,1)S(1)} %bitcast.5), channel_id=1, source_target_pairs={{0,8},{1,9},{2,10},{3,11},{4,12},{5,13},{6,14},{7,15},{8,0},{9,1},... | collective-permute-start | bytes 55304 | tf_op jit(solution)/shard_map/ppermute | solution.py:395
  79.6 4.0 %collective-permute-start.8 = (bf16[2,24,384]{2,1,0:T(8,128)(2,1)S(1)}, bf16[2,24,384]{2,1,0:T(8,128)(2,1)S(1)}, u32[]{:S(2)}, u32[]{:S(2)}) collective-permute-start(bf16[2,24,384]{2,1,0:T(8,128)(2,1)S(1)} %pad_maximum_fusion.2), channel_id=1, source_target_pairs={{0,4},{1,5},{2,6},{3,7},{4,0},{5,1},{6,2},{7,3},{8,12},{9,13},{10,... | collective-permute-start | bytes 110600 | tf_op jit(solution)/shard_map/ppermute | solution.py:395
  83.7 4.4 %collective-permute-start.9 = (bf16[4,24,384]{2,1,0:T(8,128)(2,1)S(1)}, bf16[4,24,384]{2,1,0:T(8,128)(2,1)S(1)}, u32[]{:S(2)}, u32[]{:S(2)}) collective-permute-start(bf16[4,24,384]{2,1,0:T(8,128)(2,1)S(1)} %pad_maximum_fusion.1), channel_id=1, source_target_pairs={{0,2},{1,3},{2,0},{3,1},{4,6},{5,7},{6,4},{7,5},{8,10},{9,11},{10,... | collective-permute-start | bytes 221192 | tf_op jit(solution)/shard_map/ppermute | solution.py:395
  88.1 1.4 %collective-permute-start.10 = (bf16[8,24,384]{2,1,0:T(8,128)(2,1)S(1)}, bf16[8,24,384]{2,1,0:T(8,128)(2,1)S(1)}, u32[]{:S(2)}, u32[]{:S(2)}) collective-permute-start(bf16[8,24,384]{2,1,0:T(8,128)(2,1)S(1)} %pad_maximum_fusion), channel_id=1, source_target_pairs={{0,1},{1,0},{2,3},{3,2},{4,5},{5,4},{6,7},{7,6},{8,9},{9,8},{10,11... | collective-permute-start | bytes 442376 | tf_op jit(solution)/shard_map/ppermute | solution.py:395

commit v11 on v9

--- a/solution.py
+++ b/solution.py
@@ -34,21 +34,17 @@
     return lax.axis_index("row") * lax.axis_size("node") + lax.axis_index("node")
 
 
-def call(kernel, out_shape, args, scratch=(), smem=(), name=None, vmem=VMEM_BYTES, away=0):
+def call(kernel, out_shape, args, scratch=(), smem=(), name=None, vmem=VMEM_BYTES):
     specs = [
         pl.BlockSpec(memory_space=pltpu.SMEM if n in smem else pltpu.VMEM) for n in range(len(args))
     ]
     single = not isinstance(out_shape, (list, tuple))
     inside = pl.BlockSpec(memory_space=pltpu.VMEM)
-    if away:
-        outs = [pl.BlockSpec(memory_space=pl.ANY)] * away + [inside] * (len(out_shape) - away)
-    else:
-        outs = inside if single else [inside] * len(out_shape)
     return pl.pallas_call(
         kernel,
         out_shape=out_shape,
         in_specs=specs,
-        out_specs=outs,
+        out_specs=inside if single else [inside] * len(out_shape),
         scratch_shapes=list(scratch),
         compiler_params=pltpu.CompilerParams(vmem_limit_bytes=vmem),
         name=name,
@@ -69,21 +65,11 @@
         self.block_tiles = -(-self.block // self.chans)
 
 
-def edges_kernel(sz, len_ref, x_ref, ln_ref, w_ref, away_ref, *refs):
+def edges_kernel(sz, len_ref, x_ref, ln_ref, w_ref, out_ref, *refs):
     near = refs[: sz.group]
-    norm_ref, pair_ref, out_ref, sems = refs[sz.group :]
+    norm_ref, pair_ref = refs[sz.group :]
     length, me = len_ref[0], position()
     first = me * sz.rows
-    copies = []
-
-    def leave(start, stop):
-        lanes = pl.ds(start * LANES, (stop - start) * LANES)
-        copy = pltpu.make_async_copy(
-            out_ref.at[:, :, lanes], away_ref.at[:, :, lanes], sems.at[len(copies)]
-        )
-        copy.start()
-        copies.append(copy)
-
     cd, ch = sz.chans, sz.channels
     mine = me & (sz.group - 1)
     r = lax.broadcasted_iota(jnp.int32, (ch, ch), 0)
@@ -92,8 +78,7 @@
     slots = (((r // cd) ^ mine) * cd + r % cd == e).astype(BF16)
     picks = (plain, plain, slots, slots)
     weights = [dot(pick, w_ref[p], 1, 1).astype(BF16) for p, pick in enumerate(picks)]
-    gate_w = jnp.concatenate([weights[0], weights[2]], axis=0)
-    value_w = jnp.concatenate([weights[1], weights[3]], axis=0)
+    stacked = jnp.concatenate([weights[p] for p in (0, 2, 1, 3)], axis=0)
     gain = ln_ref[...]
     main = sz.whole * LANES
     for row in range(sz.rows):
@@ -109,7 +94,6 @@
         for t in range(sz.block_tiles):
             at = (sz.tiles + t) * LANES
             out_ref[d, :, at : at + LANES] = pair_ref[d, t * cd : (t + 1) * cd, :].astype(BF16)
-    leave(sz.tiles, sz.tiles + sz.block_tiles)
     lane = lax.broadcasted_iota(jnp.int32, (1, LANES), 1)
 
     def live(tile):
@@ -126,17 +110,14 @@
     for tile in range(0, sz.tiles, step):
         n = norm_ref[pl.ds(tile * LANES, step * LANES), :]
         mask = jnp.concatenate([live(tile + s) for s in range(step)], axis=1)
-        edge = sigmoid(dot(gate_w, n, 1, 1)) * dot(value_w, n, 1, 1) * mask
-        edge = edge.astype(BF16)
+        both = dot(stacked, n, 1, 1)
+        edge = (sigmoid(both[: 2 * ch]) * (both[2 * ch :] * mask)).astype(BF16)
         to = slice(tile * LANES, (tile + step) * LANES)
         for g in range(sz.group):
             left = edge[g * cd : (g + 1) * cd]
             out_ref[g, :, to] = left
             out_ref[sz.group + g, :, to] = left
             near[g][:, to] = edge[ch + g * cd : ch + (g + 1) * cd]
-        leave(tile, tile + step)
-    for copy in copies:
-        copy.wait()
 
 
 def unpack(sz, ref, owner, main_ref, rest_ref):
@@ -201,25 +182,16 @@
             out_ref[g, :, tile * LANES : (tile + 1) * LANES] = block.astype(BF16)
 
 
-def columns_kernel(sz, pair_ref, lnp_ref, gate_ref, x_ref, gating_ref, cols_ref):
-    cd = sz.chans
+def update_kernel(
+    sz, lnp_ref, gate_ref, lnh_ref, tri_ref, lna_ref, biasw_ref, sums_ref, pair_ref,
+    first_ref, col_ref, bias_ref, cols_ref, brow_ref,
+):
+    n, w, half, ch, cd = sz.crop, sz.whole, sz.half, sz.channels, sz.chans
     for s in range(sz.devices):
         for t in range(sz.block_tiles):
             at = (sz.tiles + t) * LANES
             rows = pl.ds(s * sz.block + t * cd, cd)
             cols_ref[rows, :] = pair_ref[s, :, at : at + LANES].astype(F32)
-    for j in range(sz.rows):
-        x = cols_ref[pl.ds(j, sz.crop, stride=sz.rows), :]
-        x_ref[j] = x.astype(BF16)
-        normed = norm_last(x, lnp_ref[...]).astype(BF16)
-        gating_ref[j] = sigmoid(dot(normed, gate_ref[...], 1, 0))
-
-
-def update_kernel(
-    sz, x_ref, gating_ref, lnh_ref, tri_ref, lna_ref, biasw_ref, sums_ref,
-    first_ref, col_ref, bias_ref, brow_ref,
-):
-    n, w, half, ch = sz.crop, sz.whole, sz.half, sz.channels
     gain_h = jnp.transpose(jnp.broadcast_to(lnh_ref[...], (ch, ch)))
     tri = tri_ref[...]
 
@@ -238,7 +210,10 @@
             h, q = divmod(j, half)
             parts.append(rest[q][h * sz.rest : (h + 1) * sz.rest])
         change = jnp.concatenate(parts, axis=0) if len(parts) > 1 else parts[0]
-        first = (x_ref[j].astype(F32) + gating_ref[j] * change).astype(BF16)
+        x = cols_ref[pl.ds(j, n, stride=sz.rows), :]
+        normed = norm_last(x, lnp_ref[...]).astype(BF16)
+        gating = sigmoid(dot(normed, gate_ref[...], 1, 0))
+        first = (x + gating * change).astype(BF16)
         first_ref[j] = first
         col = norm_last(first.astype(F32), lna_ref[...]).astype(BF16)
         col_ref[j] = col
@@ -254,24 +229,20 @@
 
 
 def project_kernel(sz, col_ref, q_ref, k_ref, v_ref, g_ref, qo_ref, ko_ref, vo_ref, go_ref):
-    n, ch = sz.crop, sz.channels
-    qk = jnp.concatenate([q_ref[...], k_ref[...]], axis=1)
-    vg = jnp.transpose(jnp.concatenate([v_ref[...], g_ref[...]], axis=1).astype(F32)).astype(BF16)
+    joined = jnp.concatenate([ref[...] for ref in (q_ref, k_ref, v_ref, g_ref)], axis=1)
     width = q_ref.shape[1]
     for j in range(sz.rows):
-        col = col_ref[j]
-        both = dot(col, qk, 1, 0)
-        qo_ref[j] = both[:, :width].astype(BF16)
-        ko_ref[j] = both[:, width:].astype(BF16)
-        other = dot(vg, col, 1, 1)
-        vo_ref[j] = other[:width].astype(BF16)
-        go_ref[j] = sigmoid(other[width:])
+        made = dot(col_ref[j], joined, 1, 0)
+        qo_ref[j] = made[:, :width].astype(BF16)
+        ko_ref[j] = made[:, width : 2 * width].astype(BF16)
+        vo_ref[j] = made[:, 2 * width : 3 * width].astype(BF16)
+        go_ref[j] = sigmoid(made[:, 3 * width :])
 
 
 def attend_kernel(
     sz, heads, steps, len_ref, q_ref, k_ref, v_ref, g_ref, first_ref, aout_ref, *refs
 ):
-    bias_refs, (out_ref, rows_ref, biasT_ref) = refs[:-3], refs[-3:]
+    bias_refs, (out_ref, rows_ref, bias_ref) = refs[:-3], refs[-3:]
     n, w, ch = sz.crop, sz.whole, sz.channels
     length, me = len_ref[0], position()
     width = q_ref.shape[2]
@@ -287,72 +258,51 @@
                 if sz.rest:
                     tail = block[:, 2 * w * LANES :]
                     rows_ref[w, at, :] = pltpu.roll(tail, sz.rest, 1) if p else tail
-    key = lax.broadcasted_iota(jnp.int32, (n, LANES), 0)
-    dead = jnp.where(key < length, 0.0, -1e9 * LOG2E).astype(F32)
-    halves = []
-    for head in range(heads):
-        b = [
-            jnp.transpose(rows_ref[m, pl.ds(head, n, stride=heads), :])
-            for m in range(w + (sz.rest > 0))
-        ]
-        if sz.rest:
-            b[w] = b[w][: sz.rest]
-        b = jnp.concatenate(b, axis=0) if len(b) > 1 else b[0]
-        for m in range(w):
-            biasT_ref[:, (head * w + m) * LANES : (head * w + m + 1) * LANES] = (
-                b[:, m * LANES : (m + 1) * LANES] + dead
-            )
-        if sz.rest:
-            halves.append(b[:, w * LANES :])
-    per_tile = LANES // sz.rest if sz.rest else 1
-    base = heads * w
-    if sz.rest:
-        for t in range(heads // per_tile):
-            biasT_ref[:, (base + t) * LANES : (base + t + 1) * LANES] = (
-                jnp.concatenate(halves[t * per_tile : (t + 1) * per_tile], axis=1) + dead
-            )
-    lane = lax.broadcasted_iota(jnp.int32, (1, width), 1)
-    head_masks = [((lane >= h * hd) & (lane < (h + 1) * hd)).astype(BF16) for h in range(heads)]
+    lane = lax.broadcasted_iota(jnp.int32, (1, LANES), 1)
+    for m in range(w + (sz.rest > 0)):
+        lanes = slice(m * LANES, min((m + 1) * LANES, n))
+        dead = jnp.where(m * LANES + lane < length, 0.0, -1e9 * LOG2E).astype(F32)
+        for head in range(heads):
+            rows = rows_ref[m, pl.ds(head, n, stride=heads), :] + dead
+            bias_ref[head, :, lanes] = rows[:, : lanes.stop - lanes.start]
+    column = lax.broadcasted_iota(jnp.int32, (1, width), 1)
+    head_masks = [(column >= h * hd) & (column < (h + 1) * hd) for h in range(heads)]
     scale = (hd ** (-0.5)) * LOG2E
-    for j in range(sz.rows):
-        q = q_ref[j]
-        masked = [q * head_masks[h] for h in range(heads)]
-        pieces = [masked[h][: w * LANES] for h in range(heads)]
-        if sz.rest:
-            pieces += [masked[h][w * LANES :] for h in range(heads)]
-        stacked = jnp.concatenate(pieces, axis=0)
-        scores = dot(k_ref[j], stacked, 1, 1) * scale + biasT_ref[...]
-        top = jnp.max(scores, axis=0, keepdims=True)
-        weights = jnp.exp2(scores - top)
-        total = jnp.sum(weights, axis=0, keepdims=True)
-        mixed = dot(v_ref[j], weights.astype(BF16), 1, 0)
-        inverse = 1.0 / total
-        mains, rests = [], []
-        for h in range(heads):
-            sl = slice(h * w * LANES, (h + 1) * w * LANES)
-            mains.append(mixed[h * hd : (h + 1) * hd, sl] * inverse[:, sl])
-            if sz.rest:
-                t, part = divmod(h, per_tile)
-                sl = slice((base + t) * LANES, (base + t + 1) * LANES)
-                piece = mixed[h * hd : (h + 1) * hd, sl] * inverse[:, sl]
-                rests.append(piece[:, part * sz.rest : (part + 1) * sz.rest])
-        attended = jnp.concatenate(mains, axis=0)
-        if sz.rest:
-            attended = jnp.concatenate([attended, jnp.concatenate(rests, axis=0)], axis=1)
-        gated = (attended * g_ref[j]).astype(BF16)
-        total_out = first_ref[j].astype(F32) + dot(gated, aout_ref[...], 0, 0)
-        out_ref[j] = total_out.astype(BF16)
+    ones = jnp.ones((n, width), BF16)
+
+    def score(j, h):
+        query = q_ref[j] * head_masks[h].astype(BF16)
+        return dot(query, k_ref[j], 1, 1) * scale + bias_ref[h]
+
+    order = [(j, h) for j in range(sz.rows) for h in range(heads)]
+    scores = score(*order[0])
+    for at, (j, h) in enumerate(order):
+        now = scores
+        if at + 1 < len(order):
+            scores = score(*order[at + 1])
+        weights = jnp.exp2(now - jnp.max(now, axis=1, keepdims=True)).astype(BF16)
+        if h == 0:
+            values = jnp.concatenate([v_ref[j], ones], axis=1)
+        mixed = dot(weights, values, 1, 0)
+        if h == 0:
+            attended, total = mixed[:, :width], mixed[:, width:]
+        else:
+            attended = jnp.where(head_masks[h], mixed[:, :width], attended)
+            total = jnp.where(head_masks[h], mixed[:, width:], total)
+        if h == heads - 1:
+            gated = (attended / total * g_ref[j]).astype(BF16)
+            out_ref[j] = (first_ref[j].astype(F32) + dot(gated, aout_ref[...], 1, 0)).astype(BF16)
 
 
 def spread(block, devices):
     pieces, offsets = [block[None]], [[0]]
-    first = [devices // 2, devices // 4, devices // 2 + devices // 4]
-    for partners in [first] + [[devices >> s] for s in range(3, devices.bit_length())]:
+    bit = devices // 2
+    while bit:
         held = jnp.concatenate(pieces, axis=0) if len(pieces) > 1 else pieces[0]
         known = [o for part in offsets for o in part]
-        for bit in partners:
-            pieces.append(lax.ppermute(held, AXES, [(d, d ^ bit) for d in range(devices)]))
-            offsets.append([o ^ bit for o in known])
+        pieces.append(lax.ppermute(held, AXES, [(d, d ^ bit) for d in range(devices)]))
+        offsets.append([o ^ bit for o in known])
+        bit //= 2
     return pieces, offsets
 
 
@@ -392,11 +342,8 @@
         scratch=[
             pltpu.VMEM((rows * crop, ch), BF16),
             pltpu.VMEM((devices, bt * cd, ch), F32),
-            pltpu.VMEM((devices, cd, (t + bt) * LANES), BF16),
-            pltpu.SemaphoreType.DMA((t + 1,)),
         ],
         smem=(0,),
-        away=1,
         name="edges",
         vmem=VMEM_MOST,
     )
@@ -430,13 +377,6 @@
         outer, AXES, split_axis=0, concat_axis=0, tiled=True,
         axis_index_groups=[list(range(g)), list(range(g, devices))],
     )
-    columns, gating = call(
-        bound(columns_kernel),
-        [shape((rows, n, ch), BF16), shape((rows, n, ch), F32)],
-        (left, ln_pair[None], tri_gate),
-        scratch=[pltpu.VMEM((devices * sz.block + cd, ch), F32)],
-        name="columns",
-    )
     first, col, bias = call(
         bound(update_kernel),
         [
@@ -444,8 +384,14 @@
             shape((rows, n, ch), BF16),
             shape((rows * heads // 2, 2 * n), BF16),
         ],
-        (columns, gating, ln_hidden[None], tri_out, ln_att[None], att_bias, sums),
-        scratch=[pltpu.VMEM((rows * heads, n), F32)],
+        (
+            ln_pair[None], tri_gate, ln_hidden[None], tri_out, ln_att[None], att_bias,
+            sums, left,
+        ),
+        scratch=[
+            pltpu.VMEM((devices * sz.block + cd, ch), F32),
+            pltpu.VMEM((rows * heads, n), F32),
+        ],
         name="update",
     )
     pieces, steps = spread(bias, devices)
@@ -454,8 +400,8 @@
         [
             shape((rows, n, att_q.shape[1]), BF16),
             shape((rows, n, att_q.shape[1]), BF16),
-            shape((rows, att_q.shape[1], n), BF16),
-            shape((rows, att_q.shape[1], n), F32),
+            shape((rows, n, att_q.shape[1]), BF16),
+            shape((rows, n, att_q.shape[1]), F32),
         ],
         (col, att_q, att_k, att_v, att_gate),
         name="project",
@@ -466,7 +412,7 @@
         (length, query, key, value, gate, first, att_out, *pieces),
         scratch=[
             pltpu.VMEM((-(-n // LANES), n * heads, LANES), F32),
-            pltpu.VMEM((n, heads * n), F32),
+            pltpu.VMEM((heads, n, n), F32),
         ],
         smem=(0,),
         name="attend",

time: 101 us -> 93.3 us (0.924); the launches traced: 99.6 us -> 93 us
  local copies, waits for them, and re-layouts: 8 us -> 0.24 us
  waiting for transfers between devices: 46.1 us -> 49 us
  Pallas kernels: 19 us -> 16.9 us
    unnamed x49 -> x39, local copies, waits for them, and re-layouts: 7.99 us -> 0.24 us
    all_to_all x1, waiting for transfers between devices: 6.08 us -> 9.36 us  [shards(): lax.all_to_all(outer, AXES, split_axis=0, concat_axis=0, tiled=True, axis...]
    pallas_call x7 -> x6, Pallas kernels: 19 us -> 16.9 us  [call(): pl.pallas_call(kernel, out_shape=out_shape, in_specs=specs, out_specs=ins...]
    ppermute x5 -> x4, starting transfers between devices: 5.08 us -> 5.51 us  [spread(): lax.ppermute(held, AXES, [(d, d ^ bit) for d in range(devices)])]
    ppermute x5 -> x4, waiting for transfers between devices: 8.59 us -> 8.21 us  [spread(): lax.ppermute(held, AXES, [(d, d ^ bit) for d in range(devices)])]
  transfers between devices with their start and end apart: 14 -> 13, of which waited for: 11 -> 11; matrix products, arithmetic and copies ran while one was open for 1% -> 0% of each run, Pallas kernels for 3% -> 2%
where the time goes in v11:
time: 93.3 us; the launch traced here: 93 us
  waiting for transfers between devices  49 us (53%)
  starting transfers between devices  26 us (28%)
  Pallas kernels  16.9 us (18%)
    ppermute x7, waiting for transfers between devices, send(): lax.ppermute(block, AXES, [(d, d ^ offset ^ r) for d in range(devices)])  31.4 us
    pallas_call x6, Pallas kernels, call(): pl.pallas_call(kernel, out_shape=out_shape, in_specs=specs, out_specs=ins...  16.9 us
    all_to_all x1, waiting for transfers between devices, shards(): lax.all_to_all(outer, AXES, split_axis=0, concat_axis=0, tiled=True, axis...  9.36 us
    ppermute x4, waiting for transfers between devices, spread(): lax.ppermute(held, AXES, [(d, d ^ bit) for d in range(devices)])  8.21 us
    all_to_all x1, starting transfers between devices, shards(): left = lax.all_to_all(left, AXES, split_axis=0, concat_axis=0, tiled=True)  7.54 us
    ppermute x7, starting transfers between devices, send(): lax.ppermute(block, AXES, [(d, d ^ offset ^ r) for d in range(devices)])  6.55 us
    all_to_all x1, starting transfers between devices, shards(): lax.all_to_all(outer, AXES, split_axis=0, concat_axis=0, tiled=True, axis...  6.36 us
    ppermute x4, starting transfers between devices, spread(): lax.ppermute(held, AXES, [(d, d ^ bit) for d in range(devices)])  5.51 us
  transfers between devices with their start and end apart: 13, of which 11 were waited for; matrix products, arithmetic and copies ran while one was open for 0% of the time, Pallas kernels for 2%

profile of v11, /device:TPU:0, one launch (start us, length us, event | category | flops | bytes accessed | tf_op | source)
XLA Modules:
  0.0 93.0 jit_solution(11036310221144001322)
XLA Ops:
  0.7 3.9 %edges.1 = (bf16[16,16,3456]{2,1,0:T(8,128)(2,1)}, bf16[16,2304]{1,0:T(8,128)(2,1)}, bf16[16,2304]{1,0:T(8,128)(2,1)}, bf16[16,2304]{1,0:T(8,128)(2,1)}, bf16[16...) custom-call(s32[1]{0:T(128)S(6)} %copy.16.refs_0_, ...), custom_call_target="tpu_custom_call" | custom-call | tf_op jit(solution)/shard_map/edges/pallas_call | solution.py:43
  4.6 0.0 copy-start
  4.6 7.5 %all-to-all-start = ((bf16[16,16,3456]{2,1,0:T(8,128)(2,1)}), bf16[16,16,3456]{2,1,0:T(8,128)(2,1)S(1)}, u32[]{:S(2)}, u32[]{:S(2)}) async-start(bf16[16,16,3456]{2,1,0:T(8,128)(2,1)} %get-tuple-element.21), calls=%async_computation | async-start | bytes 3538944 | tf_op jit(solution)/shard_map/all_to_all | solution.py:350
  12.2 0.5 collective-permute-start
  12.7 1.7 %collective-permute-start.1 = (bf16[16,2304]{1,0:T(8,128)(2,1)S(1)}, bf16[16,2304]{1,0:T(8,128)(2,1)S(1)}, u32[]{:S(2)}, u32[]{:S(2)}) collective-permute-start(bf16[16,2304]{1,0:T(8,128)(2,1)S(1)} %copy-done.17), channel_id=1, source_target_pairs={{0,2},{1,3},{2,0},{3,1},{4,6},{5,7},{6,4},{7,5},{8,10},{9,11},{10,... | collective-permute-start | bytes 221192 | tf_op jit(solution)/shard_map/ppermute | solution.py:334
  14.4 0.0 collective-permute-start.2
  14.4 1.7 %collective-permute-start.3 = (bf16[16,2304]{1,0:T(8,128)(2,1)S(1)}, bf16[16,2304]{1,0:T(8,128)(2,1)S(1)}, u32[]{:S(2)}, u32[]{:S(2)}) collective-permute-start(bf16[16,2304]{1,0:T(8,128)(2,1)S(1)} %copy-done.15), channel_id=1, source_target_pairs={{0,4},{1,5},{2,6},{3,7},{4,0},{5,1},{6,2},{7,3},{8,12},{9,13},{10,... | collective-permute-start | bytes 221192 | tf_op jit(solution)/shard_map/ppermute | solution.py:334
  16.1 0.1 collective-permute-start.4
  16.2 2.6 %collective-permute-start.5 = (bf16[16,2304]{1,0:T(8,128)(2,1)S(1)}, bf16[16,2304]{1,0:T(8,128)(2,1)S(1)}, u32[]{:S(2)}, u32[]{:S(2)}) collective-permute-start(bf16[16,2304]{1,0:T(8,128)(2,1)S(1)} %copy-done.13), channel_id=1, source_target_pairs={{0,6},{1,7},{2,4},{3,5},{4,2},{5,3},{6,0},{7,1},{8,14},{9,15},{10,... | collective-permute-start | bytes 221192 | tf_op jit(solution)/shard_map/ppermute | solution.py:334
  18.8 9.1 %collective-permute-done.1.refs_2_ = bf16[16,2304]{1,0:T(8,128)(2,1)S(1)} collective-permute-done((bf16[16,2304]{1,0:T(8,128)(2,1)S(1)}, bf16[16,2304]{1,0:T(8,128)(2,1)S(1)}, u32[]{:S(2)}, u32[]{:S(2)}) %collective-permute-start.1) | collective-permute-done | bytes 73760 | tf_op jit(solution)/shard_map/ppermute | solution.py:334
  27.9 0.6 collective-permute-done.2.refs_3_
  28.5 15.1 %collective-permute-done.3.refs_4_ = bf16[16,2304]{1,0:T(8,128)(2,1)S(1)} collective-permute-done((bf16[16,2304]{1,0:T(8,128)(2,1)S(1)}, bf16[16,2304]{1,0:T(8,128)(2,1)S(1)}, u32[]{:S(2)}, u32[]{:S(2)}) %collective-permute-start.3) | collective-permute-done | bytes 73760 | tf_op jit(solution)/shard_map/ppermute | solution.py:334
  43.7 1.6 %collective-permute-done.4.refs_5_ = bf16[16,2304]{1,0:T(8,128)(2,1)S(1)} collective-permute-done((bf16[16,2304]{1,0:T(8,128)(2,1)S(1)}, bf16[16,2304]{1,0:T(8,128)(2,1)S(1)}, u32[]{:S(2)}, u32[]{:S(2)}) %collective-permute-start.4) | collective-permute-done | bytes 73760 | tf_op jit(solution)/shard_map/ppermute | solution.py:334
  45.3 1.6 %collective-permute-done.5.refs_6_ = bf16[16,2304]{1,0:T(8,128)(2,1)S(1)} collective-permute-done((bf16[16,2304]{1,0:T(8,128)(2,1)S(1)}, bf16[16,2304]{1,0:T(8,128)(2,1)S(1)}, u32[]{:S(2)}, u32[]{:S(2)}) %collective-permute-start.5) | collective-permute-done | bytes 73760 | tf_op jit(solution)/shard_map/ppermute | solution.py:334
  46.8 3.4 %collective-permute-done.6.refs_7_ = bf16[16,2304]{1,0:T(8,128)(2,1)S(1)} collective-permute-done((bf16[16,2304]{1,0:T(8,128)(2,1)S(1)}, bf16[16,2304]{1,0:T(8,128)(2,1)S(1)}, u32[]{:S(2)}, u32[]{:S(2)}) %collective-permute-start.6) | collective-permute-done | bytes 73760 | tf_op jit(solution)/shard_map/ppermute | solution.py:334
  50.2 0.7 right.1.refs_1_
  50.9 0.0 copy-start.11
  51.0 2.5 %outer.1 = bf16[8,16,2304]{2,1,0:T(8,128)(2,1)} custom-call(bf16[16,16,3456]{2,1,0:T(8,128)(2,1)S(1)} %all-to-all-done.refs_0_.refs_7_, bf16[16,96,192]{2,1,0:T(8,128)(2,1)S(1)} %right.1.refs_1_), custom_call_target="tpu_custom_call" | custom-call | tf_op jit(solution)/shard_map/outer/pallas_call | solution.py:43
  53.4 6.4 %all-to-all-start.1 = ((bf16[8,16,2304]{2,1,0:T(8,128)(2,1)}), bf16[8,16,2304]{2,1,0:T(8,128)(2,1)S(1)}, u32[]{:S(2)}, u32[]{:S(2)}) async-start(bf16[8,16,2304]{2,1,0:T(8,128)(2,1)} %outer.1), calls=%async_computation.1 | async-start | bytes 1179648 | tf_op jit(solution)/shard_map/all_to_all | solution.py:376
  59.9 0.1 copy.15.refs_5_
  60.0 9.4 %all-to-all-done.1.refs_6_ = bf16[8,16,2304]{2,1,0:T(8,128)(2,1)S(1)} async-done(((bf16[8,16,2304]{2,1,0:T(8,128)(2,1)}), bf16[8,16,2304]{2,1,0:T(8,128)(2,1)S(1)}, u32[]{:S(2)}, u32[]{:S(2)}) %all-to-all-start.1) | async-done | bytes 589856 | tf_op jit(solution)/shard_map/all_to_all | solution.py:376
  69.4 3.3 %update.1 = (bf16[12,192,128]{2,1,0:T(8,128)(2,1)S(1)}, bf16[12,192,128]{2,1,0:T(8,128)(2,1)S(1)}, bf16[24,384]{1,0:T(8,128)(2,1)S(1)}) custom-call(f32[1,128]{1,0:T(1,128)S(1)} %bitcast.11, bf16[128,128]{1,0:T(8,128)(2,1)S(1)} %copy-done.1, f32[1,128]{1,0:T(1,128)S(1)} %bitcast.12, bf16[128,128]{1,0:T(8,128)(2,1)S(1)} %copy-done.2, f32[1,128]{1,0:T(1,128)S(1)} %bitcast.13, ...), custom_call_target="tpu_custom_call" | custom-call | tf_op jit(solution)/shard_map/update/pallas_call | solution.py:43
  72.7 2.2 %collective-permute-start.7 = (bf16[1,24,384]{2,1,0:T(8,128)(2,1)S(1)}, bf16[1,24,384]{2,1,0:T(8,128)(2,1)S(1)}, u32[]{:S(2)}, u32[]{:S(2)}) collective-permute-start(bf16[1,24,384]{2,1,0:T(8,128)(2,1)S(1)} %bitcast.5), channel_id=1, source_target_pairs={{0,8},{1,9},{2,10},{3,11},{4,12},{5,13},{6,14},{7,15},{8,0},{9,1},... | collective-permute-start | bytes 55304 | tf_op jit(solution)/shard_map/ppermute | solution.py:303
  74.9 2.5 %collective-permute-done.7.refs_8_ = bf16[1,24,384]{2,1,0:T(8,128)(2,1)S(1)} collective-permute-done((bf16[1,24,384]{2,1,0:T(8,128)(2,1)S(1)}, bf16[1,24,384]{2,1,0:T(8,128)(2,1)S(1)}, u32[]{:S(2)}, u32[]{:S(2)}) %collective-permute-start.7) | collective-permute-done | bytes 18464 | tf_op jit(solution)/shard_map/ppermute | solution.py:303
  77.4 1.5 %collective-permute-start.8 = (bf16[2,24,384]{2,1,0:T(8,128)(2,1)S(1)}, bf16[2,24,384]{2,1,0:T(8,128)(2,1)S(1)}, u32[]{:S(2)}, u32[]{:S(2)}) collective-permute-start(bf16[2,24,384]{2,1,0:T(8,128)(2,1)S(1)} %pad_maximum_fusion.2), channel_id=1, source_target_pairs={{0,4},{1,5},{2,6},{3,7},{4,0},{5,1},{6,2},{7,3},{8,12},{9,13},{10,... | collective-permute-start | bytes 110600 | tf_op jit(solution)/shard_map/ppermute | solution.py:303
  78.9 2.5 %collective-permute-done.8.refs_9_ = bf16[2,24,384]{2,1,0:T(8,128)(2,1)S(1)} collective-permute-done((bf16[2,24,384]{2,1,0:T(8,128)(2,1)S(1)}, bf16[2,24,384]{2,1,0:T(8,128)(2,1)S(1)}, u32[]{:S(2)}, u32[]{:S(2)}) %collective-permute-start.8) | collective-permute-done | bytes 36896 | tf_op jit(solution)/shard_map/ppermute | solution.py:303
  81.4 1.7 %collective-permute-start.9 = (bf16[4,24,384]{2,1,0:T(8,128)(2,1)S(1)}, bf16[4,24,384]{2,1,0:T(8,128)(2,1)S(1)}, u32[]{:S(2)}, u32[]{:S(2)}) collective-permute-start(bf16[4,24,384]{2,1,0:T(8,128)(2,1)S(1)} %pad_maximum_fusion.1), channel_id=1, source_target_pairs={{0,2},{1,3},{2,0},{3,1},{4,6},{5,7},{6,4},{7,5},{8,10},{9,11},{10,... | collective-permute-start | bytes 221192 | tf_op jit(solution)/shard_map/ppermute | solution.py:303
  83.1 2.7 %collective-permute-done.9.refs_10_ = bf16[4,24,384]{2,1,0:T(8,128)(2,1)S(1)} collective-permute-done((bf16[4,24,384]{2,1,0:T(8,128)(2,1)S(1)}, bf16[4,24,384]{2,1,0:T(8,128)(2,1)S(1)}, u32[]{:S(2)}, u32[]{:S(2)}) %collective-permute-start.9) | collective-permute-done | bytes 73760 | tf_op jit(solution)/shard_map/ppermute | solution.py:303
  85.9 0.1 collective-permute-start.10
  86.0 0.8 project.1
  86.8 0.5 collective-permute-done.10.refs_11_
  87.3 5.7 %attend.1 = bf16[12,192,128]{2,1,0:T(8,128)(2,1)} custom-call(s32[1]{0:T(128)S(6)} %copy.16.refs_0_, bf16[12,192,128]{2,1,0:T(8,128)(2,1)S(1)} %get-tuple-element.31.refs_1_, bf16[12,192,128]{2,1,0:T(8,128)(2,1)S(1)} %get-tuple-element.32.refs_2_, bf16[12,192,128]{2,1,0:T(8,128)(2,1)S(1)} %get-tuple-element.33.refs_3_, ...), custom_call_target="tpu_custom_call" | custom-call | tf_op jit(solution)/shard_map/attend/pallas_call | solution.py:43
  (42 shorter events, 0.1 us)
Async XLA Ops:
  4.6 7.6 %copy-start.18 = (bf16[16,2304]{1,0:T(8,128)(2,1)S(1)}, bf16[16,2304]{1,0:T(8,128)(2,1)}, u32[]{:S(2)}) copy-start(bf16[16,2304]{1,0:T(8,128)(2,1)} %get-tuple-element.23) | copy-start | bytes 221188
  4.6 8.1 %copy-start.17 = (bf16[16,2304]{1,0:T(8,128)(2,1)S(1)}, bf16[16,2304]{1,0:T(8,128)(2,1)}, u32[]{:S(2)}) copy-start(bf16[16,2304]{1,0:T(8,128)(2,1)} %get-tuple-element.24) | copy-start | bytes 221188
  4.6 9.8 %copy-start.16 = (bf16[16,2304]{1,0:T(8,128)(2,1)S(1)}, bf16[16,2304]{1,0:T(8,128)(2,1)}, u32[]{:S(2)}) copy-start(bf16[16,2304]{1,0:T(8,128)(2,1)} %get-tuple-element.25) | copy-start | bytes 221188
  4.6 9.8 %copy-start.15 = (bf16[16,2304]{1,0:T(8,128)(2,1)S(1)}, bf16[16,2304]{1,0:T(8,128)(2,1)}, u32[]{:S(2)}) copy-start(bf16[16,2304]{1,0:T(8,128)(2,1)} %get-tuple-element.26) | copy-start | bytes 221188
  4.6 11.5 %copy-start.14 = (bf16[16,2304]{1,0:T(8,128)(2,1)S(1)}, bf16[16,2304]{1,0:T(8,128)(2,1)}, u32[]{:S(2)}) copy-start(bf16[16,2304]{1,0:T(8,128)(2,1)} %get-tuple-element.27) | copy-start | bytes 221188
  4.6 11.6 %copy-start.13 = (bf16[16,2304]{1,0:T(8,128)(2,1)S(1)}, bf16[16,2304]{1,0:T(8,128)(2,1)}, u32[]{:S(2)}) copy-start(bf16[16,2304]{1,0:T(8,128)(2,1)} %get-tuple-element.28) | copy-start | bytes 221188
  4.6 23.3 %copy-start.12 = (bf16[16,2304]{1,0:T(8,128)(2,1)S(1)}, bf16[16,2304]{1,0:T(8,128)(2,1)}, u32[]{:S(2)}) copy-start(bf16[16,2304]{1,0:T(8,128)(2,1)} %get-tuple-element.29) | copy-start | bytes 221188
  4.6 45.6 %copy-start = (bf16[16,2304]{1,0:T(8,128)(2,1)S(1)}, bf16[16,2304]{1,0:T(8,128)(2,1)}, u32[]{:S(2)}) copy-start(bf16[16,2304]{1,0:T(8,128)(2,1)} %get-tuple-element.22.refs_0_) | copy-start | bytes 221188
  4.6 46.3 %all-to-all-start = ((bf16[16,16,3456]{2,1,0:T(8,128)(2,1)}), bf16[16,16,3456]{2,1,0:T(8,128)(2,1)S(1)}, u32[]{:S(2)}, u32[]{:S(2)}) async-start(bf16[16,16,3456]{2,1,0:T(8,128)(2,1)} %get-tuple-element.21), calls=%async_computation | async-start | bytes 3538944 | tf_op jit(solution)/shard_map/all_to_all | solution.py:350
  12.2 4.0 %collective-permute-start = (bf16[16,2304]{1,0:T(8,128)(2,1)S(1)}, bf16[16,2304]{1,0:T(8,128)(2,1)S(1)}, u32[]{:S(2)}, u32[]{:S(2)}) collective-permute-start(bf16[16,2304]{1,0:T(8,128)(2,1)S(1)} %copy-done.18), channel_id=1, source_target_pairs={{0,1},{1,0},{2,3},{3,2},{4,5},{5,4},{6,7},{7,6},{8,9},{9,8},{10,11... | collective-permute-start | bytes 221192 | tf_op jit(solution)/shard_map/ppermute | solution.py:334
  12.7 15.2 %collective-permute-start.1 = (bf16[16,2304]{1,0:T(8,128)(2,1)S(1)}, bf16[16,2304]{1,0:T(8,128)(2,1)S(1)}, u32[]{:S(2)}, u32[]{:S(2)}) collective-permute-start(bf16[16,2304]{1,0:T(8,128)(2,1)S(1)} %copy-done.17), channel_id=1, source_target_pairs={{0,2},{1,3},{2,0},{3,1},{4,6},{5,7},{6,4},{7,5},{8,10},{9,11},{10,... | collective-permute-start | bytes 221192 | tf_op jit(solution)/shard_map/ppermute | solution.py:334
  14.4 14.2 %collective-permute-start.2 = (bf16[16,2304]{1,0:T(8,128)(2,1)S(1)}, bf16[16,2304]{1,0:T(8,128)(2,1)S(1)}, u32[]{:S(2)}, u32[]{:S(2)}) collective-permute-start(bf16[16,2304]{1,0:T(8,128)(2,1)S(1)} %copy-done.16), channel_id=1, source_target_pairs={{0,3},{1,2},{2,1},{3,0},{4,7},{5,6},{6,5},{7,4},{8,11},{9,10},{10,... | collective-permute-start | bytes 221192 | tf_op jit(solution)/shard_map/ppermute | solution.py:334
  14.4 29.3 %collective-permute-start.3 = (bf16[16,2304]{1,0:T(8,128)(2,1)S(1)}, bf16[16,2304]{1,0:T(8,128)(2,1)S(1)}, u32[]{:S(2)}, u32[]{:S(2)}) collective-permute-start(bf16[16,2304]{1,0:T(8,128)(2,1)S(1)} %copy-done.15), channel_id=1, source_target_pairs={{0,4},{1,5},{2,6},{3,7},{4,0},{5,1},{6,2},{7,3},{8,12},{9,13},{10,... | collective-permute-start | bytes 221192 | tf_op jit(solution)/shard_map/ppermute | solution.py:334
  16.1 29.2 %collective-permute-start.4 = (bf16[16,2304]{1,0:T(8,128)(2,1)S(1)}, bf16[16,2304]{1,0:T(8,128)(2,1)S(1)}, u32[]{:S(2)}, u32[]{:S(2)}) collective-permute-start(bf16[16,2304]{1,0:T(8,128)(2,1)S(1)} %copy-done.14), channel_id=1, source_target_pairs={{0,5},{1,4},{2,7},{3,6},{4,1},{5,0},{6,3},{7,2},{8,13},{9,12},{10,... | collective-permute-start | bytes 221192 | tf_op jit(solution)/shard_map/ppermute | solution.py:334
  16.2 30.6 %collective-permute-start.5 = (bf16[16,2304]{1,0:T(8,128)(2,1)S(1)}, bf16[16,2304]{1,0:T(8,128)(2,1)S(1)}, u32[]{:S(2)}, u32[]{:S(2)}) collective-permute-start(bf16[16,2304]{1,0:T(8,128)(2,1)S(1)} %copy-done.13), channel_id=1, source_target_pairs={{0,6},{1,7},{2,4},{3,5},{4,2},{5,3},{6,0},{7,1},{8,14},{9,15},{10,... | collective-permute-start | bytes 221192 | tf_op jit(solution)/shard_map/ppermute | solution.py:334
  27.9 22.3 %collective-permute-start.6 = (bf16[16,2304]{1,0:T(8,128)(2,1)S(1)}, bf16[16,2304]{1,0:T(8,128)(2,1)S(1)}, u32[]{:S(2)}, u32[]{:S(2)}) collective-permute-start(bf16[16,2304]{1,0:T(8,128)(2,1)S(1)} %copy-done.12), channel_id=1, source_target_pairs={{0,7},{1,6},{2,5},{3,4},{4,3},{5,2},{6,1},{7,0},{8,15},{9,14},{10,... | collective-permute-start | bytes 221192 | tf_op jit(solution)/shard_map/ppermute | solution.py:334
  50.9 8.9 %copy-start.11 = (bf16[128,4]{0,1:T(4,128)(2,1)S(1)}, bf16[128,4]{0,1:T(4,128)(2,1)}, u32[]{:S(2)}) copy-start(bf16[128,4]{0,1:T(4,128)(2,1)} %param.25) | copy-start | bytes 3076
  50.9 18.4 %copy-start.1 = (bf16[128,128]{1,0:T(8,128)(2,1)S(1)}, bf16[128,128]{1,0:T(8,128)(2,1)}, u32[]{:S(2)}) copy-start(bf16[128,128]{1,0:T(8,128)(2,1)} %refs_1_.4) | copy-start | bytes 98308
  50.9 18.4 %copy-start.2 = (bf16[128,128]{1,0:T(8,128)(2,1)S(1)}, bf16[128,128]{1,0:T(8,128)(2,1)}, u32[]{:S(2)}) copy-start(bf16[128,128]{1,0:T(8,128)(2,1)} %refs_3_.4) | copy-start | bytes 98308
  50.9 18.4 %copy-start.8 = (f32[128]{0:T(128)S(1)}, f32[128]{0:T(128)}, u32[]{:S(2)}) copy-start(f32[128]{0:T(128)} %param.16) | copy-start | bytes 1540
  51.0 18.4 %copy-start.9 = (f32[128]{0:T(128)S(1)}, f32[128]{0:T(128)}, u32[]{:S(2)}) copy-start(f32[128]{0:T(128)} %param.19) | copy-start | bytes 1540
  51.0 18.4 %copy-start.10 = (f32[128]{0:T(128)S(1)}, f32[128]{0:T(128)}, u32[]{:S(2)}) copy-start(f32[128]{0:T(128)} %param.21) | copy-start | bytes 1540
  53.4 15.9 %all-to-all-start.1 = ((bf16[8,16,2304]{2,1,0:T(8,128)(2,1)}), bf16[8,16,2304]{2,1,0:T(8,128)(2,1)S(1)}, u32[]{:S(2)}, u32[]{:S(2)}) async-start(bf16[8,16,2304]{2,1,0:T(8,128)(2,1)} %outer.1), calls=%async_computation.1 | async-start | bytes 1179648 | tf_op jit(solution)/shard_map/all_to_all | solution.py:376
  59.8 26.1 %copy-start.4 = (bf16[128,128]{1,0:T(8,128)(2,1)S(1)}, bf16[128,128]{1,0:T(8,128)(2,1)}, u32[]{:S(2)}) copy-start(bf16[128,128]{1,0:T(8,128)(2,1)} %refs_1_.5) | copy-start | bytes 98308
  59.8 26.1 %copy-start.5 = (bf16[128,128]{1,0:T(8,128)(2,1)S(1)}, bf16[128,128]{1,0:T(8,128)(2,1)}, u32[]{:S(2)}) copy-start(bf16[128,128]{1,0:T(8,128)(2,1)} %refs_2_.1) | copy-start | bytes 98308
  59.8 26.1 %copy-start.6 = (bf16[128,128]{1,0:T(8,128)(2,1)S(1)}, bf16[128,128]{1,0:T(8,128)(2,1)}, u32[]{:S(2)}) copy-start(bf16[128,128]{1,0:T(8,128)(2,1)} %refs_3_.5) | copy-start | bytes 98308
  59.8 26.1 %copy-start.7 = (bf16[128,128]{1,0:T(8,128)(2,1)S(1)}, bf16[128,128]{1,0:T(8,128)(2,1)}, u32[]{:S(2)}) copy-start(bf16[128,128]{1,0:T(8,128)(2,1)} %refs_4_.1) | copy-start | bytes 98308
  69.4 17.9 %copy-start.3 = (bf16[128,128]{1,0:T(8,128)(2,1)S(1)}, bf16[128,128]{1,0:T(8,128)(2,1)}, u32[]{:S(2)}) copy-start(bf16[128,128]{1,0:T(8,128)(2,1)} %refs_6_.1) | copy-start | bytes 98308
  72.7 4.7 %collective-permute-start.7 = (bf16[1,24,384]{2,1,0:T(8,128)(2,1)S(1)}, bf16[1,24,384]{2,1,0:T(8,128)(2,1)S(1)}, u32[]{:S(2)}, u32[]{:S(2)}) collective-permute-start(bf16[1,24,384]{2,1,0:T(8,128)(2,1)S(1)} %bitcast.5), channel_id=1, source_target_pairs={{0,8},{1,9},{2,10},{3,11},{4,12},{5,13},{6,14},{7,15},{8,0},{9,1},... | collective-permute-start | bytes 55304 | tf_op jit(solution)/shard_map/ppermute | solution.py:303
  77.4 4.0 %collective-permute-start.8 = (bf16[2,24,384]{2,1,0:T(8,128)(2,1)S(1)}, bf16[2,24,384]{2,1,0:T(8,128)(2,1)S(1)}, u32[]{:S(2)}, u32[]{:S(2)}) collective-permute-start(bf16[2,24,384]{2,1,0:T(8,128)(2,1)S(1)} %pad_maximum_fusion.2), channel_id=1, source_target_pairs={{0,4},{1,5},{2,6},{3,7},{4,0},{5,1},{6,2},{7,3},{8,12},{9,13},{10,... | collective-permute-start | bytes 110600 | tf_op jit(solution)/shard_map/ppermute | solution.py:303
  81.4 4.4 %collective-permute-start.9 = (bf16[4,24,384]{2,1,0:T(8,128)(2,1)S(1)}, bf16[4,24,384]{2,1,0:T(8,128)(2,1)S(1)}, u32[]{:S(2)}, u32[]{:S(2)}) collective-permute-start(bf16[4,24,384]{2,1,0:T(8,128)(2,1)S(1)} %pad_maximum_fusion.1), channel_id=1, source_target_pairs={{0,2},{1,3},{2,0},{3,1},{4,6},{5,7},{6,4},{7,5},{8,10},{9,11},{10,... | collective-permute-start | bytes 221192 | tf_op jit(solution)/shard_map/ppermute | solution.py:303
  85.9 1.4 %collective-permute-start.10 = (bf16[8,24,384]{2,1,0:T(8,128)(2,1)S(1)}, bf16[8,24,384]{2,1,0:T(8,128)(2,1)S(1)}, u32[]{:S(2)}, u32[]{:S(2)}) collective-permute-start(bf16[8,24,384]{2,1,0:T(8,128)(2,1)S(1)} %pad_maximum_fusion), channel_id=1, source_target_pairs={{0,1},{1,0},{2,3},{3,2},{4,5},{5,4},{6,7},{7,6},{8,9},{9,8},{10,11... | collective-permute-start | bytes 442376 | tf_op jit(solution)/shard_map/ppermute | solution.py:303

commit v12 on v11

--- a/solution.py
+++ b/solution.py
@@ -182,16 +182,25 @@
             out_ref[g, :, tile * LANES : (tile + 1) * LANES] = block.astype(BF16)
 
 
-def update_kernel(
-    sz, lnp_ref, gate_ref, lnh_ref, tri_ref, lna_ref, biasw_ref, sums_ref, pair_ref,
-    first_ref, col_ref, bias_ref, cols_ref, brow_ref,
-):
-    n, w, half, ch, cd = sz.crop, sz.whole, sz.half, sz.channels, sz.chans
+def columns_kernel(sz, pair_ref, lnp_ref, gate_ref, x_ref, gating_ref, cols_ref):
+    cd = sz.chans
     for s in range(sz.devices):
         for t in range(sz.block_tiles):
             at = (sz.tiles + t) * LANES
             rows = pl.ds(s * sz.block + t * cd, cd)
             cols_ref[rows, :] = pair_ref[s, :, at : at + LANES].astype(F32)
+    for j in range(sz.rows):
+        x = cols_ref[pl.ds(j, sz.crop, stride=sz.rows), :]
+        x_ref[j] = x.astype(BF16)
+        normed = norm_last(x, lnp_ref[...]).astype(BF16)
+        gating_ref[j] = sigmoid(dot(normed, gate_ref[...], 1, 0)).astype(BF16)
+
+
+def update_kernel(
+    sz, x_ref, gating_ref, lnh_ref, tri_ref, lna_ref, biasw_ref, sums_ref,
+    first_ref, col_ref, bias_ref, brow_ref,
+):
+    n, w, half, ch = sz.crop, sz.whole, sz.half, sz.channels
     gain_h = jnp.transpose(jnp.broadcast_to(lnh_ref[...], (ch, ch)))
     tri = tri_ref[...]
 
@@ -210,10 +219,7 @@
             h, q = divmod(j, half)
             parts.append(rest[q][h * sz.rest : (h + 1) * sz.rest])
         change = jnp.concatenate(parts, axis=0) if len(parts) > 1 else parts[0]
-        x = cols_ref[pl.ds(j, n, stride=sz.rows), :]
-        normed = norm_last(x, lnp_ref[...]).astype(BF16)
-        gating = sigmoid(dot(normed, gate_ref[...], 1, 0))
-        first = (x + gating * change).astype(BF16)
+        first = (x_ref[j].astype(F32) + gating_ref[j].astype(F32) * change).astype(BF16)
         first_ref[j] = first
         col = norm_last(first.astype(F32), lna_ref[...]).astype(BF16)
         col_ref[j] = col
@@ -270,28 +276,28 @@
     scale = (hd ** (-0.5)) * LOG2E
     ones = jnp.ones((n, width), BF16)
 
-    def score(j, h):
-        query = q_ref[j] * head_masks[h].astype(BF16)
-        return dot(query, k_ref[j], 1, 1) * scale + bias_ref[h]
-
-    order = [(j, h) for j in range(sz.rows) for h in range(heads)]
-    scores = score(*order[0])
-    for at, (j, h) in enumerate(order):
+    def score(j):
+        query = [q_ref[j] * head_masks[h].astype(BF16) for h in range(heads)]
+        return dot(jnp.concatenate(query, axis=0), k_ref[j], 1, 1)
+
+    scores = score(0)
+    for j in range(sz.rows):
         now = scores
-        if at + 1 < len(order):
-            scores = score(*order[at + 1])
-        weights = jnp.exp2(now - jnp.max(now, axis=1, keepdims=True)).astype(BF16)
-        if h == 0:
-            values = jnp.concatenate([v_ref[j], ones], axis=1)
-        mixed = dot(weights, values, 1, 0)
-        if h == 0:
-            attended, total = mixed[:, :width], mixed[:, width:]
-        else:
-            attended = jnp.where(head_masks[h], mixed[:, :width], attended)
-            total = jnp.where(head_masks[h], mixed[:, width:], total)
-        if h == heads - 1:
-            gated = (attended / total * g_ref[j]).astype(BF16)
-            out_ref[j] = (first_ref[j].astype(F32) + dot(gated, aout_ref[...], 1, 0)).astype(BF16)
+        if j + 1 < sz.rows:
+            scores = score(j + 1)
+        weights = []
+        for h in range(heads):
+            part = now[h * n : (h + 1) * n] * scale + bias_ref[h]
+            weights.append(jnp.exp2(part - jnp.max(part, axis=1, keepdims=True)).astype(BF16))
+        values = jnp.concatenate([v_ref[j], ones], axis=1)
+        mixed = dot(jnp.concatenate(weights, axis=0), values, 1, 0)
+        attended, total = mixed[:n, :width], mixed[:n, width:]
+        for h in range(1, heads):
+            rows = slice(h * n, (h + 1) * n)
+            attended = jnp.where(head_masks[h], mixed[rows, :width], attended)
+            total = jnp.where(head_masks[h], mixed[rows, width:], total)
+        gated = (attended / total * g_ref[j]).astype(BF16)
+        out_ref[j] = (first_ref[j].astype(F32) + dot(gated, aout_ref[...], 1, 0)).astype(BF16)
 
 
 def spread(block, devices):
@@ -377,6 +383,13 @@
         outer, AXES, split_axis=0, concat_axis=0, tiled=True,
         axis_index_groups=[list(range(g)), list(range(g, devices))],
     )
+    columns, gating = call(
+        bound(columns_kernel),
+        [shape((rows, n, ch), BF16), shape((rows, n, ch), BF16)],
+        (left, ln_pair[None], tri_gate),
+        scratch=[pltpu.VMEM((devices * sz.block + cd, ch), F32)],
+        name="columns",
+    )
     first, col, bias = call(
         bound(update_kernel),
         [
@@ -384,14 +397,8 @@
             shape((rows, n, ch), BF16),
             shape((rows * heads // 2, 2 * n), BF16),
         ],
-        (
-            ln_pair[None], tri_gate, ln_hidden[None], tri_out, ln_att[None], att_bias,
-            sums, left,
-        ),
-        scratch=[
-            pltpu.VMEM((devices * sz.block + cd, ch), F32),
-            pltpu.VMEM((rows * heads, n), F32),
-        ],
+        (columns, gating, ln_hidden[None], tri_out, ln_att[None], att_bias, sums),
+        scratch=[pltpu.VMEM((rows * heads, n), F32)],
         name="update",
     )
     pieces, steps = spread(bias, devices)

time: 93.3 us -> 97.4 us (1.044)
  local copies, waits for them, and re-layouts: 0.24 us -> 6.84 us
  waiting for transfers between devices: 49 us -> 46 us
    unnamed x39 -> x41, local copies, waits for them, and re-layouts: 0.24 us -> 6.84 us
    all_to_all x1, waiting for transfers between devices: 9.36 us -> 6.89 us  [shards(): lax.all_to_all(outer, AXES, split_axis=0, concat_axis=0, tiled=True, axis...]
    pallas_call x6 -> x7, Pallas kernels: 16.9 us -> 16.6 us  [call(): pl.pallas_call(kernel, out_shape=out_shape, in_specs=specs, out_specs=ins...]
  transfers between devices with their start and end apart: 13 -> 13, of which waited for: 11 -> 10; matrix products, arithmetic and copies ran while one was open for 0% -> 1% of each run, Pallas kernels for 2% -> 3%
where the time goes in v12:
time: 97.4 us; the launch traced here: 96.5 us
  waiting for transfers between devices  46 us (47%)
  starting transfers between devices  26.1 us (27%)
  Pallas kernels  16.6 us (17%)
  local copies, waits for them, and re-layouts  6.84 us (7%)
    ppermute x7, waiting for transfers between devices, send(): lax.ppermute(block, AXES, [(d, d ^ offset ^ r) for d in range(devices)])  31.4 us
    pallas_call x7, Pallas kernels, call(): pl.pallas_call(kernel, out_shape=out_shape, in_specs=specs, out_specs=ins...  16.6 us
    ppermute x4, waiting for transfers between devices, spread(): lax.ppermute(held, AXES, [(d, d ^ bit) for d in range(devices)])  7.68 us
    all_to_all x1, starting transfers between devices, shards(): left = lax.all_to_all(left, AXES, split_axis=0, concat_axis=0, tiled=True)  7.54 us
    all_to_all x1, waiting for transfers between devices, shards(): lax.all_to_all(outer, AXES, split_axis=0, concat_axis=0, tiled=True, axis...  6.89 us
    unnamed x41, local copies, waits for them, and re-layouts  6.84 us
    ppermute x7, starting transfers between devices, send(): lax.ppermute(block, AXES, [(d, d ^ offset ^ r) for d in range(devices)])  6.55 us
    all_to_all x1, starting transfers between devices, shards(): lax.all_to_all(outer, AXES, split_axis=0, concat_axis=0, tiled=True, axis...  6.55 us
  transfers between devices with their start and end apart: 13, of which 10 were waited for; matrix products, arithmetic and copies ran while one was open for 1% of the time, Pallas kernels for 3%

profile of v12, /device:TPU:0, one launch (start us, length us, event | category | flops | bytes accessed | tf_op | source)
XLA Modules:
  0.0 96.5 jit_solution(13935148124744638557)
XLA Ops:
  0.7 3.9 %edges.1 = (bf16[16,16,3456]{2,1,0:T(8,128)(2,1)}, bf16[16,2304]{1,0:T(8,128)(2,1)}, bf16[16,2304]{1,0:T(8,128)(2,1)}, bf16[16,2304]{1,0:T(8,128)(2,1)}, bf16[16...) custom-call(s32[1]{0:T(128)S(6)} %copy.16.refs_0_, ...), custom_call_target="tpu_custom_call" | custom-call | tf_op jit(solution)/shard_map/edges/pallas_call | solution.py:43
  4.6 7.5 %all-to-all-start = ((bf16[16,16,3456]{2,1,0:T(8,128)(2,1)}), bf16[16,16,3456]{2,1,0:T(8,128)(2,1)S(1)}, u32[]{:S(2)}, u32[]{:S(2)}) async-start(bf16[16,16,3456]{2,1,0:T(8,128)(2,1)} %get-tuple-element.23), calls=%async_computation | async-start | bytes 3538944 | tf_op jit(solution)/shard_map/all_to_all | solution.py:356
  12.7 1.7 %collective-permute-start.1 = (bf16[16,2304]{1,0:T(8,128)(2,1)S(1)}, bf16[16,2304]{1,0:T(8,128)(2,1)S(1)}, u32[]{:S(2)}, u32[]{:S(2)}) collective-permute-start(bf16[16,2304]{1,0:T(8,128)(2,1)S(1)} %copy-done.18), channel_id=1, source_target_pairs={{0,2},{1,3},{2,0},{3,1},{4,6},{5,7},{6,4},{7,5},{8,10},{9,11},{10,... | collective-permute-start | bytes 221192 | tf_op jit(solution)/shard_map/ppermute | solution.py:340
  14.4 1.7 %collective-permute-start.3 = (bf16[16,2304]{1,0:T(8,128)(2,1)S(1)}, bf16[16,2304]{1,0:T(8,128)(2,1)S(1)}, u32[]{:S(2)}, u32[]{:S(2)}) collective-permute-start(bf16[16,2304]{1,0:T(8,128)(2,1)S(1)} %copy-done.16), channel_id=1, source_target_pairs={{0,4},{1,5},{2,6},{3,7},{4,0},{5,1},{6,2},{7,3},{8,12},{9,13},{10,... | collective-permute-start | bytes 221192 | tf_op jit(solution)/shard_map/ppermute | solution.py:340
  16.2 2.6 %collective-permute-start.5 = (bf16[16,2304]{1,0:T(8,128)(2,1)S(1)}, bf16[16,2304]{1,0:T(8,128)(2,1)S(1)}, u32[]{:S(2)}, u32[]{:S(2)}) collective-permute-start(bf16[16,2304]{1,0:T(8,128)(2,1)S(1)} %copy-done.14), channel_id=1, source_target_pairs={{0,6},{1,7},{2,4},{3,5},{4,2},{5,3},{6,0},{7,1},{8,14},{9,15},{10,... | collective-permute-start | bytes 221192 | tf_op jit(solution)/shard_map/ppermute | solution.py:340
  18.8 9.1 %collective-permute-done.1.refs_2_ = bf16[16,2304]{1,0:T(8,128)(2,1)S(1)} collective-permute-done((bf16[16,2304]{1,0:T(8,128)(2,1)S(1)}, bf16[16,2304]{1,0:T(8,128)(2,1)S(1)}, u32[]{:S(2)}, u32[]{:S(2)}) %collective-permute-start.1) | collective-permute-done | bytes 73760 | tf_op jit(solution)/shard_map/ppermute | solution.py:340
  28.5 15.1 %collective-permute-done.3.refs_4_ = bf16[16,2304]{1,0:T(8,128)(2,1)S(1)} collective-permute-done((bf16[16,2304]{1,0:T(8,128)(2,1)S(1)}, bf16[16,2304]{1,0:T(8,128)(2,1)S(1)}, u32[]{:S(2)}, u32[]{:S(2)}) %collective-permute-start.3) | collective-permute-done | bytes 73760 | tf_op jit(solution)/shard_map/ppermute | solution.py:340
  43.7 1.6 %collective-permute-done.4.refs_5_ = bf16[16,2304]{1,0:T(8,128)(2,1)S(1)} collective-permute-done((bf16[16,2304]{1,0:T(8,128)(2,1)S(1)}, bf16[16,2304]{1,0:T(8,128)(2,1)S(1)}, u32[]{:S(2)}, u32[]{:S(2)}) %collective-permute-start.4) | collective-permute-done | bytes 73760 | tf_op jit(solution)/shard_map/ppermute | solution.py:340
  45.3 1.6 %collective-permute-done.5.refs_6_ = bf16[16,2304]{1,0:T(8,128)(2,1)S(1)} collective-permute-done((bf16[16,2304]{1,0:T(8,128)(2,1)S(1)}, bf16[16,2304]{1,0:T(8,128)(2,1)S(1)}, u32[]{:S(2)}, u32[]{:S(2)}) %collective-permute-start.5) | collective-permute-done | bytes 73760 | tf_op jit(solution)/shard_map/ppermute | solution.py:340
  46.8 3.4 %collective-permute-done.6.refs_7_ = bf16[16,2304]{1,0:T(8,128)(2,1)S(1)} collective-permute-done((bf16[16,2304]{1,0:T(8,128)(2,1)S(1)}, bf16[16,2304]{1,0:T(8,128)(2,1)S(1)}, u32[]{:S(2)}, u32[]{:S(2)}) %collective-permute-start.6) | collective-permute-done | bytes 73760 | tf_op jit(solution)/shard_map/ppermute | solution.py:340
  50.9 2.5 %outer.1 = bf16[8,16,2304]{2,1,0:T(8,128)(2,1)} custom-call(bf16[16,16,3456]{2,1,0:T(8,128)(2,1)S(1)} %all-to-all-done.refs_0_, bf16[16,96,192]{2,1,0:T(8,128)(2,1)S(1)} %right.1.refs_1_), custom_call_target="tpu_custom_call" | custom-call | tf_op jit(solution)/shard_map/outer/pallas_call | solution.py:43
  53.4 6.5 %all-to-all-start.1 = ((bf16[8,16,2304]{2,1,0:T(8,128)(2,1)}), bf16[8,16,2304]{2,1,0:T(8,128)(2,1)S(1)}, u32[]{:S(2)}, u32[]{:S(2)}) async-start(bf16[8,16,2304]{2,1,0:T(8,128)(2,1)} %outer.1), calls=%async_computation.1 | async-start | bytes 1179648 | tf_op jit(solution)/shard_map/all_to_all | solution.py:382
  60.0 0.7 copy.15.refs_5_
  60.7 0.8 copy-done.2
  61.4 1.2 %columns.1 = (bf16[12,192,128]{2,1,0:T(8,128)(2,1)S(1)}, bf16[12,192,128]{2,1,0:T(8,128)(2,1)S(1)}) custom-call(bf16[16,16,3456]{2,1,0:T(8,128)(2,1)S(1)} %all-to-all-done.refs_0_, f32[1,128]{1,0:T(1,128)S(1)} %bitcast.11, bf16[128,128]{1,0:T(8,128)(2,1)S(1)} %copy-done.2), custom_call_target="tpu_custom_call" | custom-call | tf_op jit(solution)/shard_map/columns/pallas_call | solution.py:43
  62.6 6.9 %all-to-all-done.1.refs_6_ = bf16[8,16,2304]{2,1,0:T(8,128)(2,1)S(1)} async-done(((bf16[8,16,2304]{2,1,0:T(8,128)(2,1)}), bf16[8,16,2304]{2,1,0:T(8,128)(2,1)S(1)}, u32[]{:S(2)}, u32[]{:S(2)}) %all-to-all-start.1) | async-done | bytes 589856 | tf_op jit(solution)/shard_map/all_to_all | solution.py:382
  69.5 0.8 copy-done
  70.3 0.8 copy-done.3
  71.0 2.6 %update.1 = (bf16[12,192,128]{2,1,0:T(8,128)(2,1)S(1)}, bf16[12,192,128]{2,1,0:T(8,128)(2,1)S(1)}, bf16[24,384]{1,0:T(8,128)(2,1)S(1)}) custom-call(bf16[12,192,128]{2,1,0:T(8,128)(2,1)S(1)} %get-tuple-element.24.refs_0_, bf16[12,192,128]{2,1,0:T(8,128)(2,1)S(1)} %get-tuple-element.25.refs_1_, f32[1,128]{1,0:T(1,128)S(1)} %bitcast.12, ...), custom_call_target="tpu_custom_call" | custom-call | tf_op jit(solution)/shard_map/update/pallas_call | solution.py:43
  73.7 2.2 %collective-permute-start.7 = (bf16[1,24,384]{2,1,0:T(8,128)(2,1)S(1)}, bf16[1,24,384]{2,1,0:T(8,128)(2,1)S(1)}, u32[]{:S(2)}, u32[]{:S(2)}) collective-permute-start(bf16[1,24,384]{2,1,0:T(8,128)(2,1)S(1)} %bitcast.5), channel_id=1, source_target_pairs={{0,8},{1,9},{2,10},{3,11},{4,12},{5,13},{6,14},{7,15},{8,0},{9,1},... | collective-permute-start | bytes 55304 | tf_op jit(solution)/shard_map/ppermute | solution.py:309
  75.8 2.5 %collective-permute-done.7.refs_8_ = bf16[1,24,384]{2,1,0:T(8,128)(2,1)S(1)} collective-permute-done((bf16[1,24,384]{2,1,0:T(8,128)(2,1)S(1)}, bf16[1,24,384]{2,1,0:T(8,128)(2,1)S(1)}, u32[]{:S(2)}, u32[]{:S(2)}) %collective-permute-start.7) | collective-permute-done | bytes 18464 | tf_op jit(solution)/shard_map/ppermute | solution.py:309
  78.3 1.5 %collective-permute-start.8 = (bf16[2,24,384]{2,1,0:T(8,128)(2,1)S(1)}, bf16[2,24,384]{2,1,0:T(8,128)(2,1)S(1)}, u32[]{:S(2)}, u32[]{:S(2)}) collective-permute-start(bf16[2,24,384]{2,1,0:T(8,128)(2,1)S(1)} %pad_maximum_fusion.2), channel_id=1, source_target_pairs={{0,4},{1,5},{2,6},{3,7},{4,0},{5,1},{6,2},{7,3},{8,12},{9,13},{10,... | collective-permute-start | bytes 110600 | tf_op jit(solution)/shard_map/ppermute | solution.py:309
  79.9 2.5 %collective-permute-done.8.refs_9_ = bf16[2,24,384]{2,1,0:T(8,128)(2,1)S(1)} collective-permute-done((bf16[2,24,384]{2,1,0:T(8,128)(2,1)S(1)}, bf16[2,24,384]{2,1,0:T(8,128)(2,1)S(1)}, u32[]{:S(2)}, u32[]{:S(2)}) %collective-permute-start.8) | collective-permute-done | bytes 36896 | tf_op jit(solution)/shard_map/ppermute | solution.py:309
  82.4 1.7 %collective-permute-start.9 = (bf16[4,24,384]{2,1,0:T(8,128)(2,1)S(1)}, bf16[4,24,384]{2,1,0:T(8,128)(2,1)S(1)}, u32[]{:S(2)}, u32[]{:S(2)}) collective-permute-start(bf16[4,24,384]{2,1,0:T(8,128)(2,1)S(1)} %pad_maximum_fusion.1), channel_id=1, source_target_pairs={{0,2},{1,3},{2,0},{3,1},{4,6},{5,7},{6,4},{7,5},{8,10},{9,11},{10,... | collective-permute-start | bytes 221192 | tf_op jit(solution)/shard_map/ppermute | solution.py:309
  84.1 2.7 %collective-permute-done.9.refs_10_ = bf16[4,24,384]{2,1,0:T(8,128)(2,1)S(1)} collective-permute-done((bf16[4,24,384]{2,1,0:T(8,128)(2,1)S(1)}, bf16[4,24,384]{2,1,0:T(8,128)(2,1)S(1)}, u32[]{:S(2)}, u32[]{:S(2)}) %collective-permute-start.9) | collective-permute-done | bytes 73760 | tf_op jit(solution)/shard_map/ppermute | solution.py:309
  86.9 0.7 copy-done.5
  87.7 0.8 copy-done.6
  88.4 0.8 copy-done.7
  89.2 0.8 copy-done.8
  90.0 0.8 project.1
  90.7 0.7 copy-done.4
  91.5 5.0 %attend.1 = bf16[12,192,128]{2,1,0:T(8,128)(2,1)} custom-call(s32[1]{0:T(128)S(6)} %copy.16.refs_0_, bf16[12,192,128]{2,1,0:T(8,128)(2,1)S(1)} %get-tuple-element.35.refs_1_, bf16[12,192,128]{2,1,0:T(8,128)(2,1)S(1)} %get-tuple-element.36.refs_2_, bf16[12,192,128]{2,1,0:T(8,128)(2,1)S(1)} %get-tuple-element.37.refs_3_, ...), custom_call_target="tpu_custom_call" | custom-call | tf_op jit(solution)/shard_map/attend/pallas_call | solution.py:43
  (45 shorter events, 2.2 us)
Async XLA Ops:
  4.6 7.6 %copy-start.19 = (bf16[16,2304]{1,0:T(8,128)(2,1)S(1)}, bf16[16,2304]{1,0:T(8,128)(2,1)}, u32[]{:S(2)}) copy-start(bf16[16,2304]{1,0:T(8,128)(2,1)} %get-tuple-element.27) | copy-start | bytes 221188
  4.6 8.1 %copy-start.18 = (bf16[16,2304]{1,0:T(8,128)(2,1)S(1)}, bf16[16,2304]{1,0:T(8,128)(2,1)}, u32[]{:S(2)}) copy-start(bf16[16,2304]{1,0:T(8,128)(2,1)} %get-tuple-element.28) | copy-start | bytes 221188
  4.6 9.8 %copy-start.17 = (bf16[16,2304]{1,0:T(8,128)(2,1)S(1)}, bf16[16,2304]{1,0:T(8,128)(2,1)}, u32[]{:S(2)}) copy-start(bf16[16,2304]{1,0:T(8,128)(2,1)} %get-tuple-element.29) | copy-start | bytes 221188
  4.6 9.8 %copy-start.16 = (bf16[16,2304]{1,0:T(8,128)(2,1)S(1)}, bf16[16,2304]{1,0:T(8,128)(2,1)}, u32[]{:S(2)}) copy-start(bf16[16,2304]{1,0:T(8,128)(2,1)} %get-tuple-element.30) | copy-start | bytes 221188
  4.6 11.5 %copy-start.15 = (bf16[16,2304]{1,0:T(8,128)(2,1)S(1)}, bf16[16,2304]{1,0:T(8,128)(2,1)}, u32[]{:S(2)}) copy-start(bf16[16,2304]{1,0:T(8,128)(2,1)} %get-tuple-element.31) | copy-start | bytes 221188
  4.6 11.6 %copy-start.14 = (bf16[16,2304]{1,0:T(8,128)(2,1)S(1)}, bf16[16,2304]{1,0:T(8,128)(2,1)}, u32[]{:S(2)}) copy-start(bf16[16,2304]{1,0:T(8,128)(2,1)} %get-tuple-element.32) | copy-start | bytes 221188
  4.6 23.3 %copy-start.13 = (bf16[16,2304]{1,0:T(8,128)(2,1)S(1)}, bf16[16,2304]{1,0:T(8,128)(2,1)}, u32[]{:S(2)}) copy-start(bf16[16,2304]{1,0:T(8,128)(2,1)} %get-tuple-element.33) | copy-start | bytes 221188
  4.6 45.6 %copy-start.1 = (bf16[16,2304]{1,0:T(8,128)(2,1)S(1)}, bf16[16,2304]{1,0:T(8,128)(2,1)}, u32[]{:S(2)}) copy-start(bf16[16,2304]{1,0:T(8,128)(2,1)} %get-tuple-element.26.refs_0_) | copy-start | bytes 221188
  4.6 46.3 %all-to-all-start = ((bf16[16,16,3456]{2,1,0:T(8,128)(2,1)}), bf16[16,16,3456]{2,1,0:T(8,128)(2,1)S(1)}, u32[]{:S(2)}, u32[]{:S(2)}) async-start(bf16[16,16,3456]{2,1,0:T(8,128)(2,1)} %get-tuple-element.23), calls=%async_computation | async-start | bytes 3538944 | tf_op jit(solution)/shard_map/all_to_all | solution.py:356
  12.2 4.0 %collective-permute-start = (bf16[16,2304]{1,0:T(8,128)(2,1)S(1)}, bf16[16,2304]{1,0:T(8,128)(2,1)S(1)}, u32[]{:S(2)}, u32[]{:S(2)}) collective-permute-start(bf16[16,2304]{1,0:T(8,128)(2,1)S(1)} %copy-done.19), channel_id=1, source_target_pairs={{0,1},{1,0},{2,3},{3,2},{4,5},{5,4},{6,7},{7,6},{8,9},{9,8},{10,11... | collective-permute-start | bytes 221192 | tf_op jit(solution)/shard_map/ppermute | solution.py:340
  12.7 15.2 %collective-permute-start.1 = (bf16[16,2304]{1,0:T(8,128)(2,1)S(1)}, bf16[16,2304]{1,0:T(8,128)(2,1)S(1)}, u32[]{:S(2)}, u32[]{:S(2)}) collective-permute-start(bf16[16,2304]{1,0:T(8,128)(2,1)S(1)} %copy-done.18), channel_id=1, source_target_pairs={{0,2},{1,3},{2,0},{3,1},{4,6},{5,7},{6,4},{7,5},{8,10},{9,11},{10,... | collective-permute-start | bytes 221192 | tf_op jit(solution)/shard_map/ppermute | solution.py:340
  14.4 14.2 %collective-permute-start.2 = (bf16[16,2304]{1,0:T(8,128)(2,1)S(1)}, bf16[16,2304]{1,0:T(8,128)(2,1)S(1)}, u32[]{:S(2)}, u32[]{:S(2)}) collective-permute-start(bf16[16,2304]{1,0:T(8,128)(2,1)S(1)} %copy-done.17), channel_id=1, source_target_pairs={{0,3},{1,2},{2,1},{3,0},{4,7},{5,6},{6,5},{7,4},{8,11},{9,10},{10,... | collective-permute-start | bytes 221192 | tf_op jit(solution)/shard_map/ppermute | solution.py:340
  14.4 29.3 %collective-permute-start.3 = (bf16[16,2304]{1,0:T(8,128)(2,1)S(1)}, bf16[16,2304]{1,0:T(8,128)(2,1)S(1)}, u32[]{:S(2)}, u32[]{:S(2)}) collective-permute-start(bf16[16,2304]{1,0:T(8,128)(2,1)S(1)} %copy-done.16), channel_id=1, source_target_pairs={{0,4},{1,5},{2,6},{3,7},{4,0},{5,1},{6,2},{7,3},{8,12},{9,13},{10,... | collective-permute-start | bytes 221192 | tf_op jit(solution)/shard_map/ppermute | solution.py:340
  16.1 29.2 %collective-permute-start.4 = (bf16[16,2304]{1,0:T(8,128)(2,1)S(1)}, bf16[16,2304]{1,0:T(8,128)(2,1)S(1)}, u32[]{:S(2)}, u32[]{:S(2)}) collective-permute-start(bf16[16,2304]{1,0:T(8,128)(2,1)S(1)} %copy-done.15), channel_id=1, source_target_pairs={{0,5},{1,4},{2,7},{3,6},{4,1},{5,0},{6,3},{7,2},{8,13},{9,12},{10,... | collective-permute-start | bytes 221192 | tf_op jit(solution)/shard_map/ppermute | solution.py:340
  16.2 30.6 %collective-permute-start.5 = (bf16[16,2304]{1,0:T(8,128)(2,1)S(1)}, bf16[16,2304]{1,0:T(8,128)(2,1)S(1)}, u32[]{:S(2)}, u32[]{:S(2)}) collective-permute-start(bf16[16,2304]{1,0:T(8,128)(2,1)S(1)} %copy-done.14), channel_id=1, source_target_pairs={{0,6},{1,7},{2,4},{3,5},{4,2},{5,3},{6,0},{7,1},{8,14},{9,15},{10,... | collective-permute-start | bytes 221192 | tf_op jit(solution)/shard_map/ppermute | solution.py:340
  27.9 22.3 %collective-permute-start.6 = (bf16[16,2304]{1,0:T(8,128)(2,1)S(1)}, bf16[16,2304]{1,0:T(8,128)(2,1)S(1)}, u32[]{:S(2)}, u32[]{:S(2)}) collective-permute-start(bf16[16,2304]{1,0:T(8,128)(2,1)S(1)} %copy-done.13), channel_id=1, source_target_pairs={{0,7},{1,6},{2,5},{3,4},{4,3},{5,2},{6,1},{7,0},{8,15},{9,14},{10,... | collective-permute-start | bytes 221192 | tf_op jit(solution)/shard_map/ppermute | solution.py:340
  50.9 9.0 %copy-start.12 = (bf16[128,4]{0,1:T(4,128)(2,1)S(1)}, bf16[128,4]{0,1:T(4,128)(2,1)}, u32[]{:S(2)}) copy-start(bf16[128,4]{0,1:T(4,128)(2,1)} %param.25) | copy-start | bytes 3076
  50.9 9.8 %copy-start.9 = (f32[128]{0:T(128)S(1)}, f32[128]{0:T(128)}, u32[]{:S(2)}) copy-start(f32[128]{0:T(128)} %param.16) | copy-start | bytes 1540
  53.4 16.1 %copy-start.10 = (f32[128]{0:T(128)S(1)}, f32[128]{0:T(128)}, u32[]{:S(2)}) copy-start(f32[128]{0:T(128)} %param.19) | copy-start | bytes 1540
  53.4 16.1 %copy-start.11 = (f32[128]{0:T(128)S(1)}, f32[128]{0:T(128)}, u32[]{:S(2)}) copy-start(f32[128]{0:T(128)} %param.21) | copy-start | bytes 1540
  53.4 16.1 %all-to-all-start.1 = ((bf16[8,16,2304]{2,1,0:T(8,128)(2,1)}), bf16[8,16,2304]{2,1,0:T(8,128)(2,1)S(1)}, u32[]{:S(2)}, u32[]{:S(2)}) async-start(bf16[8,16,2304]{2,1,0:T(8,128)(2,1)} %outer.1), calls=%async_computation.1 | async-start | bytes 1179648 | tf_op jit(solution)/shard_map/all_to_all | solution.py:382
  60.7 0.8 copy-start.2
  69.5 0.8 copy-start
  70.3 0.8 copy-start.3
  73.7 4.7 %collective-permute-start.7 = (bf16[1,24,384]{2,1,0:T(8,128)(2,1)S(1)}, bf16[1,24,384]{2,1,0:T(8,128)(2,1)S(1)}, u32[]{:S(2)}, u32[]{:S(2)}) collective-permute-start(bf16[1,24,384]{2,1,0:T(8,128)(2,1)S(1)} %bitcast.5), channel_id=1, source_target_pairs={{0,8},{1,9},{2,10},{3,11},{4,12},{5,13},{6,14},{7,15},{8,0},{9,1},... | collective-permute-start | bytes 55304 | tf_op jit(solution)/shard_map/ppermute | solution.py:309
  78.3 4.0 %collective-permute-start.8 = (bf16[2,24,384]{2,1,0:T(8,128)(2,1)S(1)}, bf16[2,24,384]{2,1,0:T(8,128)(2,1)S(1)}, u32[]{:S(2)}, u32[]{:S(2)}) collective-permute-start(bf16[2,24,384]{2,1,0:T(8,128)(2,1)S(1)} %pad_maximum_fusion.2), channel_id=1, source_target_pairs={{0,4},{1,5},{2,6},{3,7},{4,0},{5,1},{6,2},{7,3},{8,12},{9,13},{10,... | collective-permute-start | bytes 110600 | tf_op jit(solution)/shard_map/ppermute | solution.py:309
  82.4 4.4 %collective-permute-start.9 = (bf16[4,24,384]{2,1,0:T(8,128)(2,1)S(1)}, bf16[4,24,384]{2,1,0:T(8,128)(2,1)S(1)}, u32[]{:S(2)}, u32[]{:S(2)}) collective-permute-start(bf16[4,24,384]{2,1,0:T(8,128)(2,1)S(1)} %pad_maximum_fusion.1), channel_id=1, source_target_pairs={{0,2},{1,3},{2,0},{3,1},{4,6},{5,7},{6,4},{7,5},{8,10},{9,11},{10,... | collective-permute-start | bytes 221192 | tf_op jit(solution)/shard_map/ppermute | solution.py:309
  86.8 3.9 %collective-permute-start.10 = (bf16[8,24,384]{2,1,0:T(8,128)(2,1)S(1)}, bf16[8,24,384]{2,1,0:T(8,128)(2,1)S(1)}, u32[]{:S(2)}, u32[]{:S(2)}) collective-permute-start(bf16[8,24,384]{2,1,0:T(8,128)(2,1)S(1)} %pad_maximum_fusion), channel_id=1, source_target_pairs={{0,1},{1,0},{2,3},{3,2},{4,5},{5,4},{6,7},{7,6},{8,9},{9,8},{10,11... | collective-permute-start | bytes 442376 | tf_op jit(solution)/shard_map/ppermute | solution.py:309
  86.9 0.8 copy-start.5
  87.7 0.8 copy-start.6
  88.4 0.8 copy-start.7
  90.7 0.8 copy-start.4
  (1 other events, 0.8 us)

commit v13 on v12

--- a/solution.py
+++ b/solution.py
@@ -182,25 +182,16 @@
             out_ref[g, :, tile * LANES : (tile + 1) * LANES] = block.astype(BF16)
 
 
-def columns_kernel(sz, pair_ref, lnp_ref, gate_ref, x_ref, gating_ref, cols_ref):
-    cd = sz.chans
+def update_kernel(
+    sz, lnp_ref, gate_ref, lnh_ref, tri_ref, lna_ref, biasw_ref, sums_ref, pair_ref,
+    first_ref, col_ref, bias_ref, cols_ref, brow_ref,
+):
+    n, w, half, ch, cd = sz.crop, sz.whole, sz.half, sz.channels, sz.chans
     for s in range(sz.devices):
         for t in range(sz.block_tiles):
             at = (sz.tiles + t) * LANES
             rows = pl.ds(s * sz.block + t * cd, cd)
             cols_ref[rows, :] = pair_ref[s, :, at : at + LANES].astype(F32)
-    for j in range(sz.rows):
-        x = cols_ref[pl.ds(j, sz.crop, stride=sz.rows), :]
-        x_ref[j] = x.astype(BF16)
-        normed = norm_last(x, lnp_ref[...]).astype(BF16)
-        gating_ref[j] = sigmoid(dot(normed, gate_ref[...], 1, 0)).astype(BF16)
-
-
-def update_kernel(
-    sz, x_ref, gating_ref, lnh_ref, tri_ref, lna_ref, biasw_ref, sums_ref,
-    first_ref, col_ref, bias_ref, brow_ref,
-):
-    n, w, half, ch = sz.crop, sz.whole, sz.half, sz.channels
     gain_h = jnp.transpose(jnp.broadcast_to(lnh_ref[...], (ch, ch)))
     tri = tri_ref[...]
 
@@ -219,7 +210,10 @@
             h, q = divmod(j, half)
             parts.append(rest[q][h * sz.rest : (h + 1) * sz.rest])
         change = jnp.concatenate(parts, axis=0) if len(parts) > 1 else parts[0]
-        first = (x_ref[j].astype(F32) + gating_ref[j].astype(F32) * change).astype(BF16)
+        x = cols_ref[pl.ds(j, n, stride=sz.rows), :]
+        normed = norm_last(x, lnp_ref[...]).astype(BF16)
+        gating = sigmoid(dot(normed, gate_ref[...], 1, 0))
+        first = (x + gating * change).astype(BF16)
         first_ref[j] = first
         col = norm_last(first.astype(F32), lna_ref[...]).astype(BF16)
         col_ref[j] = col
@@ -246,19 +240,20 @@
 
 
 def attend_kernel(
-    sz, heads, steps, len_ref, q_ref, k_ref, v_ref, g_ref, first_ref, aout_ref, *refs
+    sz, heads, len_ref, q_ref, k_ref, v_ref, g_ref, first_ref, aout_ref, *refs
 ):
     bias_refs, (out_ref, rows_ref, bias_ref) = refs[:-3], refs[-3:]
     n, w, ch = sz.crop, sz.whole, sz.channels
-    length, me = len_ref[0], position()
+    length, core = len_ref[0], lax.axis_index("node")
     width = q_ref.shape[2]
     hd = width // heads
     per = sz.rows * heads // 2
-    for ref, offsets in zip(bias_refs, steps):
-        for place, offset in enumerate(offsets):
-            block = ref[place].astype(F32) * LOG2E
+    for other, ref in enumerate(bias_refs):
+        for chip in range(ref.shape[0]):
+            block = ref[chip].astype(F32) * LOG2E
+            owner = 2 * chip + (core ^ other)
             for p in range(2):
-                at = pl.ds(pl.multiple_of(((me ^ offset) * 2 + p) * per, 8), per)
+                at = pl.ds(pl.multiple_of((owner * 2 + p) * per, 8), per)
                 for m in range(w):
                     rows_ref[m, at, :] = block[:, (p * w + m) * LANES : (p * w + m + 1) * LANES]
                 if sz.rest:
@@ -300,18 +295,6 @@
         out_ref[j] = (first_ref[j].astype(F32) + dot(gated, aout_ref[...], 1, 0)).astype(BF16)
 
 
-def spread(block, devices):
-    pieces, offsets = [block[None]], [[0]]
-    bit = devices // 2
-    while bit:
-        held = jnp.concatenate(pieces, axis=0) if len(pieces) > 1 else pieces[0]
-        known = [o for part in offsets for o in part]
-        pieces.append(lax.ppermute(held, AXES, [(d, d ^ bit) for d in range(devices)]))
-        offsets.append([o ^ bit for o in known])
-        bit //= 2
-    return pieces, offsets
-
-
 def shards(
     devices,
     pair_rep, length, ln_pair, tri_in, tri_gate, ln_hidden, tri_out, ln_att,
@@ -383,13 +366,6 @@
         outer, AXES, split_axis=0, concat_axis=0, tiled=True,
         axis_index_groups=[list(range(g)), list(range(g, devices))],
     )
-    columns, gating = call(
-        bound(columns_kernel),
-        [shape((rows, n, ch), BF16), shape((rows, n, ch), BF16)],
-        (left, ln_pair[None], tri_gate),
-        scratch=[pltpu.VMEM((devices * sz.block + cd, ch), F32)],
-        name="columns",
-    )
     first, col, bias = call(
         bound(update_kernel),
         [
@@ -397,11 +373,18 @@
             shape((rows, n, ch), BF16),
             shape((rows * heads // 2, 2 * n), BF16),
         ],
-        (columns, gating, ln_hidden[None], tri_out, ln_att[None], att_bias, sums),
-        scratch=[pltpu.VMEM((rows * heads, n), F32)],
+        (
+            ln_pair[None], tri_gate, ln_hidden[None], tri_out, ln_att[None], att_bias,
+            sums, left,
+        ),
+        scratch=[
+            pltpu.VMEM((devices * sz.block + cd, ch), F32),
+            pltpu.VMEM((rows * heads, n), F32),
+        ],
         name="update",
     )
-    pieces, steps = spread(bias, devices)
+    same = lax.all_gather(bias, "row", axis=0, tiled=False)
+    other = lax.ppermute(same, "node", [(0, 1), (1, 0)])
     query, key, value, gate = call(
         bound(project_kernel),
         [
@@ -414,9 +397,9 @@
         name="project",
     )
     out = call(
-        bound(attend_kernel, heads, steps),
+        bound(attend_kernel, heads),
         shape((rows, n, ch), BF16),
-        (length, query, key, value, gate, first, att_out, *pieces),
+        (length, query, key, value, gate, first, att_out, same, other),
         scratch=[
             pltpu.VMEM((-(-n // LANES), n * heads, LANES), F32),
             pltpu.VMEM((heads, n, n), F32),

time: 97.4 us -> 110 us (1.13)
  blocking collectives: 0 us -> 30.7 us
  local copies, waits for them, and re-layouts: 6.84 us -> 0.23 us
  starting transfers between devices: 26.1 us -> 20.6 us
  waiting for transfers between devices: 46 us -> 41.4 us
    all_gather x0 -> x1, blocking collectives: none -> 30.7 us  [shards(): same = lax.all_gather(bias, 'row', axis=0, tiled=False)]
    ppermute x4 -> x1, waiting for transfers between devices: 7.68 us -> 0.56 us  [shards(): other = lax.ppermute(same, 'node', [(0, 1), (1, 0)])]
    unnamed x41 -> x39, local copies, waits for them, and re-layouts: 6.84 us -> 0.23 us
    ppermute x4 -> x1, starting transfers between devices: 5.51 us -> 0.01 us  [shards(): other = lax.ppermute(same, 'node', [(0, 1), (1, 0)])]
    all_to_all x1, waiting for transfers between devices: 6.89 us -> 9.39 us  [shards(): lax.all_to_all(outer, AXES, split_axis=0, concat_axis=0, tiled=True, axis...]
    pallas_call x7 -> x6, Pallas kernels: 16.6 us -> 16.1 us  [call(): pl.pallas_call(kernel, out_shape=out_shape, in_specs=specs, out_specs=ins...]
  transfers between devices with their start and end apart: 13 -> 10, of which waited for: 10 -> 8; matrix products, arithmetic and copies ran while one was open for 1% -> 0% of each run, Pallas kernels for 3% -> 1%
where the time goes in v13:
time: 110 us
  waiting for transfers between devices  41.4 us (38%)
  blocking collectives  30.7 us (28%)
  starting transfers between devices  20.6 us (19%)
  Pallas kernels  16.1 us (15%)
    ppermute x7, waiting for transfers between devices, send(): lax.ppermute(block, AXES, [(d, d ^ offset ^ r) for d in range(devices)])  31.4 us
    all_gather x1, blocking collectives, shards(): same = lax.all_gather(bias, 'row', axis=0, tiled=False)  30.7 us
    pallas_call x6, Pallas kernels, call(): pl.pallas_call(kernel, out_shape=out_shape, in_specs=specs, out_specs=ins...  16.1 us
    all_to_all x1, waiting for transfers between devices, shards(): lax.all_to_all(outer, AXES, split_axis=0, concat_axis=0, tiled=True, axis...  9.39 us
    all_to_all x1, starting transfers between devices, shards(): left = lax.all_to_all(left, AXES, split_axis=0, concat_axis=0, tiled=True)  7.54 us
    ppermute x7, starting transfers between devices, send(): lax.ppermute(block, AXES, [(d, d ^ offset ^ r) for d in range(devices)])  6.55 us
    all_to_all x1, starting transfers between devices, shards(): lax.all_to_all(outer, AXES, split_axis=0, concat_axis=0, tiled=True, axis...  6.51 us
  transfers between devices with their start and end apart: 10, of which 8 were waited for; matrix products, arithmetic and copies ran while one was open for 0% of the time, Pallas kernels for 1%

profile of v13, /device:TPU:0, one launch (start us, length us, event | category | flops | bytes accessed | tf_op | source)
XLA Modules:
  0.0 109.9 jit_solution(8304721299008092646)
XLA Ops:
  0.7 3.9 %edges.1 = (bf16[16,16,3456]{2,1,0:T(8,128)(2,1)}, bf16[16,2304]{1,0:T(8,128)(2,1)}, bf16[16,2304]{1,0:T(8,128)(2,1)}, bf16[16,2304]{1,0:T(8,128)(2,1)}, bf16[16...) custom-call(s32[1]{0:T(128)S(6)} %copy.16.refs_0_, ...), custom_call_target="tpu_custom_call" | custom-call | tf_op jit(solution)/shard_map/edges/pallas_call | solution.py:43
  4.6 0.0 copy-start
  4.7 7.5 %all-to-all-start = ((bf16[16,16,3456]{2,1,0:T(8,128)(2,1)}), bf16[16,16,3456]{2,1,0:T(8,128)(2,1)S(1)}, u32[]{:S(2)}, u32[]{:S(2)}) async-start(bf16[16,16,3456]{2,1,0:T(8,128)(2,1)} %get-tuple-element.21), calls=%async_computation | async-start | bytes 3538944 | tf_op jit(solution)/shard_map/all_to_all | solution.py:339
  12.2 0.5 collective-permute-start
  12.7 1.7 %collective-permute-start.1 = (bf16[16,2304]{1,0:T(8,128)(2,1)S(1)}, bf16[16,2304]{1,0:T(8,128)(2,1)S(1)}, u32[]{:S(2)}, u32[]{:S(2)}) collective-permute-start(bf16[16,2304]{1,0:T(8,128)(2,1)S(1)} %copy-done.17), channel_id=1, source_target_pairs={{0,2},{1,3},{2,0},{3,1},{4,6},{5,7},{6,4},{7,5},{8,10},{9,11},{10,... | collective-permute-start | bytes 221192 | tf_op jit(solution)/shard_map/ppermute | solution.py:323
  14.4 0.0 collective-permute-start.2
  14.4 1.7 %collective-permute-start.3 = (bf16[16,2304]{1,0:T(8,128)(2,1)S(1)}, bf16[16,2304]{1,0:T(8,128)(2,1)S(1)}, u32[]{:S(2)}, u32[]{:S(2)}) collective-permute-start(bf16[16,2304]{1,0:T(8,128)(2,1)S(1)} %copy-done.15), channel_id=1, source_target_pairs={{0,4},{1,5},{2,6},{3,7},{4,0},{5,1},{6,2},{7,3},{8,12},{9,13},{10,... | collective-permute-start | bytes 221192 | tf_op jit(solution)/shard_map/ppermute | solution.py:323
  16.1 0.1 collective-permute-start.4
  16.2 2.6 %collective-permute-start.5 = (bf16[16,2304]{1,0:T(8,128)(2,1)S(1)}, bf16[16,2304]{1,0:T(8,128)(2,1)S(1)}, u32[]{:S(2)}, u32[]{:S(2)}) collective-permute-start(bf16[16,2304]{1,0:T(8,128)(2,1)S(1)} %copy-done.13), channel_id=1, source_target_pairs={{0,6},{1,7},{2,4},{3,5},{4,2},{5,3},{6,0},{7,1},{8,14},{9,15},{10,... | collective-permute-start | bytes 221192 | tf_op jit(solution)/shard_map/ppermute | solution.py:323
  18.8 9.1 %collective-permute-done.1.refs_2_ = bf16[16,2304]{1,0:T(8,128)(2,1)S(1)} collective-permute-done((bf16[16,2304]{1,0:T(8,128)(2,1)S(1)}, bf16[16,2304]{1,0:T(8,128)(2,1)S(1)}, u32[]{:S(2)}, u32[]{:S(2)}) %collective-permute-start.1) | collective-permute-done | bytes 73760 | tf_op jit(solution)/shard_map/ppermute | solution.py:323
  27.9 0.6 collective-permute-done.2.refs_3_
  28.5 15.1 %collective-permute-done.3.refs_4_ = bf16[16,2304]{1,0:T(8,128)(2,1)S(1)} collective-permute-done((bf16[16,2304]{1,0:T(8,128)(2,1)S(1)}, bf16[16,2304]{1,0:T(8,128)(2,1)S(1)}, u32[]{:S(2)}, u32[]{:S(2)}) %collective-permute-start.3) | collective-permute-done | bytes 73760 | tf_op jit(solution)/shard_map/ppermute | solution.py:323
  43.7 1.6 %collective-permute-done.4.refs_5_ = bf16[16,2304]{1,0:T(8,128)(2,1)S(1)} collective-permute-done((bf16[16,2304]{1,0:T(8,128)(2,1)S(1)}, bf16[16,2304]{1,0:T(8,128)(2,1)S(1)}, u32[]{:S(2)}, u32[]{:S(2)}) %collective-permute-start.4) | collective-permute-done | bytes 73760 | tf_op jit(solution)/shard_map/ppermute | solution.py:323
  45.3 1.6 %collective-permute-done.5.refs_6_ = bf16[16,2304]{1,0:T(8,128)(2,1)S(1)} collective-permute-done((bf16[16,2304]{1,0:T(8,128)(2,1)S(1)}, bf16[16,2304]{1,0:T(8,128)(2,1)S(1)}, u32[]{:S(2)}, u32[]{:S(2)}) %collective-permute-start.5) | collective-permute-done | bytes 73760 | tf_op jit(solution)/shard_map/ppermute | solution.py:323
  46.8 3.4 %collective-permute-done.6.refs_7_ = bf16[16,2304]{1,0:T(8,128)(2,1)S(1)} collective-permute-done((bf16[16,2304]{1,0:T(8,128)(2,1)S(1)}, bf16[16,2304]{1,0:T(8,128)(2,1)S(1)}, u32[]{:S(2)}, u32[]{:S(2)}) %collective-permute-start.6) | collective-permute-done | bytes 73760 | tf_op jit(solution)/shard_map/ppermute | solution.py:323
  50.2 0.7 right.1.refs_1_
  50.9 0.0 copy-start.11
  50.9 0.0 copy-start.1
  51.0 0.0 copy-start.2
  51.0 0.0 copy-start.8
  51.0 0.0 copy-start.9
  51.0 0.0 copy-start.10
  51.0 2.4 %outer.1 = bf16[8,16,2304]{2,1,0:T(8,128)(2,1)} custom-call(bf16[16,16,3456]{2,1,0:T(8,128)(2,1)S(1)} %all-to-all-done.refs_0_.refs_7_, bf16[16,96,192]{2,1,0:T(8,128)(2,1)S(1)} %right.1.refs_1_), custom_call_target="tpu_custom_call" | custom-call | tf_op jit(solution)/shard_map/outer/pallas_call | solution.py:43
  53.5 6.5 %all-to-all-start.1 = ((bf16[8,16,2304]{2,1,0:T(8,128)(2,1)}), bf16[8,16,2304]{2,1,0:T(8,128)(2,1)S(1)}, u32[]{:S(2)}, u32[]{:S(2)}) async-start(bf16[8,16,2304]{2,1,0:T(8,128)(2,1)} %outer.1), calls=%async_computation.1 | async-start | bytes 1179648 | tf_op jit(solution)/shard_map/all_to_all | solution.py:365
  60.0 0.0 copy-start.3
  60.0 0.1 copy.15.refs_5_
  60.1 9.4 %all-to-all-done.1.refs_6_ = bf16[8,16,2304]{2,1,0:T(8,128)(2,1)S(1)} async-done(((bf16[8,16,2304]{2,1,0:T(8,128)(2,1)}), bf16[8,16,2304]{2,1,0:T(8,128)(2,1)S(1)}, u32[]{:S(2)}, u32[]{:S(2)}) %all-to-all-start.1) | async-done | bytes 589856 | tf_op jit(solution)/shard_map/all_to_all | solution.py:365
  69.6 3.3 %update.1 = (bf16[12,192,128]{2,1,0:T(8,128)(2,1)S(1)}, bf16[12,192,128]{2,1,0:T(8,128)(2,1)S(1)}, bf16[24,384]{1,0:T(8,128)(2,1)S(1)}) custom-call(f32[1,128]{1,0:T(1,128)S(1)} %bitcast.8, bf16[128,128]{1,0:T(8,128)(2,1)S(1)} %copy-done.1, f32[1,128]{1,0:T(1,128)S(1)} %bitcast.9, bf16[128,128]{1,0:T(8,128)(2,1)S(1)} %copy-done.2, f32[1,128]{1,0:T(1,128)S(1)} %bitcast.10, ...), custom_call_target="tpu_custom_call" | custom-call | tf_op jit(solution)/shard_map/update/pallas_call | solution.py:43
  72.8 30.7 %all-gather = bf16[192,384]{1,0:T(8,128)(2,1)S(1)} all-gather(bf16[24,384]{1,0:T(8,128)(2,1)S(1)} %get-tuple-element.36), channel_id=2, replica_groups=mesh['grp'=2,'row'=8,'node'=2] {'row'}, dimensions={0}, use_global_device_ids=true | all-gather | bytes 165888 | tf_op jit(solution)/shard_map/all_gather | solution.py:386
  103.6 0.8 project.1
  104.4 0.6 collective-permute-done.7.refs_8_
  105.0 4.9 %attend.1 = bf16[12,192,128]{2,1,0:T(8,128)(2,1)} custom-call(s32[1]{0:T(128)S(6)} %copy.16.refs_0_, bf16[12,192,128]{2,1,0:T(8,128)(2,1)S(1)} %get-tuple-element.31.refs_1_, bf16[12,192,128]{2,1,0:T(8,128)(2,1)S(1)} %get-tuple-element.32.refs_2_, bf16[12,192,128]{2,1,0:T(8,128)(2,1)S(1)} %get-tuple-element.33.refs_3_, ...), custom_call_target="tpu_custom_call" | custom-call | tf_op jit(solution)/shard_map/attend/pallas_call | solution.py:43
  (34 shorter events, 0.1 us)
Async XLA Ops:
  4.6 7.6 %copy-start.18 = (bf16[16,2304]{1,0:T(8,128)(2,1)S(1)}, bf16[16,2304]{1,0:T(8,128)(2,1)}, u32[]{:S(2)}) copy-start(bf16[16,2304]{1,0:T(8,128)(2,1)} %get-tuple-element.23) | copy-start | bytes 221188
  4.6 8.1 %copy-start.17 = (bf16[16,2304]{1,0:T(8,128)(2,1)S(1)}, bf16[16,2304]{1,0:T(8,128)(2,1)}, u32[]{:S(2)}) copy-start(bf16[16,2304]{1,0:T(8,128)(2,1)} %get-tuple-element.24) | copy-start | bytes 221188
  4.6 9.8 %copy-start.16 = (bf16[16,2304]{1,0:T(8,128)(2,1)S(1)}, bf16[16,2304]{1,0:T(8,128)(2,1)}, u32[]{:S(2)}) copy-start(bf16[16,2304]{1,0:T(8,128)(2,1)} %get-tuple-element.25) | copy-start | bytes 221188
  4.6 9.8 %copy-start.15 = (bf16[16,2304]{1,0:T(8,128)(2,1)S(1)}, bf16[16,2304]{1,0:T(8,128)(2,1)}, u32[]{:S(2)}) copy-start(bf16[16,2304]{1,0:T(8,128)(2,1)} %get-tuple-element.26) | copy-start | bytes 221188
  4.6 11.5 %copy-start.14 = (bf16[16,2304]{1,0:T(8,128)(2,1)S(1)}, bf16[16,2304]{1,0:T(8,128)(2,1)}, u32[]{:S(2)}) copy-start(bf16[16,2304]{1,0:T(8,128)(2,1)} %get-tuple-element.27) | copy-start | bytes 221188
  4.6 11.6 %copy-start.13 = (bf16[16,2304]{1,0:T(8,128)(2,1)S(1)}, bf16[16,2304]{1,0:T(8,128)(2,1)}, u32[]{:S(2)}) copy-start(bf16[16,2304]{1,0:T(8,128)(2,1)} %get-tuple-element.28) | copy-start | bytes 221188
  4.6 23.3 %copy-start.12 = (bf16[16,2304]{1,0:T(8,128)(2,1)S(1)}, bf16[16,2304]{1,0:T(8,128)(2,1)}, u32[]{:S(2)}) copy-start(bf16[16,2304]{1,0:T(8,128)(2,1)} %get-tuple-element.29) | copy-start | bytes 221188
  4.6 45.6 %copy-start = (bf16[16,2304]{1,0:T(8,128)(2,1)S(1)}, bf16[16,2304]{1,0:T(8,128)(2,1)}, u32[]{:S(2)}) copy-start(bf16[16,2304]{1,0:T(8,128)(2,1)} %get-tuple-element.22.refs_0_) | copy-start | bytes 221188
  4.7 46.3 %all-to-all-start = ((bf16[16,16,3456]{2,1,0:T(8,128)(2,1)}), bf16[16,16,3456]{2,1,0:T(8,128)(2,1)S(1)}, u32[]{:S(2)}, u32[]{:S(2)}) async-start(bf16[16,16,3456]{2,1,0:T(8,128)(2,1)} %get-tuple-element.21), calls=%async_computation | async-start | bytes 3538944 | tf_op jit(solution)/shard_map/all_to_all | solution.py:339
  12.2 4.0 %collective-permute-start = (bf16[16,2304]{1,0:T(8,128)(2,1)S(1)}, bf16[16,2304]{1,0:T(8,128)(2,1)S(1)}, u32[]{:S(2)}, u32[]{:S(2)}) collective-permute-start(bf16[16,2304]{1,0:T(8,128)(2,1)S(1)} %copy-done.18), channel_id=1, source_target_pairs={{0,1},{1,0},{2,3},{3,2},{4,5},{5,4},{6,7},{7,6},{8,9},{9,8},{10,11... | collective-permute-start | bytes 221192 | tf_op jit(solution)/shard_map/ppermute | solution.py:323
  12.7 15.2 %collective-permute-start.1 = (bf16[16,2304]{1,0:T(8,128)(2,1)S(1)}, bf16[16,2304]{1,0:T(8,128)(2,1)S(1)}, u32[]{:S(2)}, u32[]{:S(2)}) collective-permute-start(bf16[16,2304]{1,0:T(8,128)(2,1)S(1)} %copy-done.17), channel_id=1, source_target_pairs={{0,2},{1,3},{2,0},{3,1},{4,6},{5,7},{6,4},{7,5},{8,10},{9,11},{10,... | collective-permute-start | bytes 221192 | tf_op jit(solution)/shard_map/ppermute | solution.py:323
  14.4 14.2 %collective-permute-start.2 = (bf16[16,2304]{1,0:T(8,128)(2,1)S(1)}, bf16[16,2304]{1,0:T(8,128)(2,1)S(1)}, u32[]{:S(2)}, u32[]{:S(2)}) collective-permute-start(bf16[16,2304]{1,0:T(8,128)(2,1)S(1)} %copy-done.16), channel_id=1, source_target_pairs={{0,3},{1,2},{2,1},{3,0},{4,7},{5,6},{6,5},{7,4},{8,11},{9,10},{10,... | collective-permute-start | bytes 221192 | tf_op jit(solution)/shard_map/ppermute | solution.py:323
  14.4 29.3 %collective-permute-start.3 = (bf16[16,2304]{1,0:T(8,128)(2,1)S(1)}, bf16[16,2304]{1,0:T(8,128)(2,1)S(1)}, u32[]{:S(2)}, u32[]{:S(2)}) collective-permute-start(bf16[16,2304]{1,0:T(8,128)(2,1)S(1)} %copy-done.15), channel_id=1, source_target_pairs={{0,4},{1,5},{2,6},{3,7},{4,0},{5,1},{6,2},{7,3},{8,12},{9,13},{10,... | collective-permute-start | bytes 221192 | tf_op jit(solution)/shard_map/ppermute | solution.py:323
  16.1 29.2 %collective-permute-start.4 = (bf16[16,2304]{1,0:T(8,128)(2,1)S(1)}, bf16[16,2304]{1,0:T(8,128)(2,1)S(1)}, u32[]{:S(2)}, u32[]{:S(2)}) collective-permute-start(bf16[16,2304]{1,0:T(8,128)(2,1)S(1)} %copy-done.14), channel_id=1, source_target_pairs={{0,5},{1,4},{2,7},{3,6},{4,1},{5,0},{6,3},{7,2},{8,13},{9,12},{10,... | collective-permute-start | bytes 221192 | tf_op jit(solution)/shard_map/ppermute | solution.py:323
  16.2 30.6 %collective-permute-start.5 = (bf16[16,2304]{1,0:T(8,128)(2,1)S(1)}, bf16[16,2304]{1,0:T(8,128)(2,1)S(1)}, u32[]{:S(2)}, u32[]{:S(2)}) collective-permute-start(bf16[16,2304]{1,0:T(8,128)(2,1)S(1)} %copy-done.13), channel_id=1, source_target_pairs={{0,6},{1,7},{2,4},{3,5},{4,2},{5,3},{6,0},{7,1},{8,14},{9,15},{10,... | collective-permute-start | bytes 221192 | tf_op jit(solution)/shard_map/ppermute | solution.py:323
  27.9 22.3 %collective-permute-start.6 = (bf16[16,2304]{1,0:T(8,128)(2,1)S(1)}, bf16[16,2304]{1,0:T(8,128)(2,1)S(1)}, u32[]{:S(2)}, u32[]{:S(2)}) collective-permute-start(bf16[16,2304]{1,0:T(8,128)(2,1)S(1)} %copy-done.12), channel_id=1, source_target_pairs={{0,7},{1,6},{2,5},{3,4},{4,3},{5,2},{6,1},{7,0},{8,15},{9,14},{10,... | collective-permute-start | bytes 221192 | tf_op jit(solution)/shard_map/ppermute | solution.py:323
  50.9 9.1 %copy-start.11 = (bf16[128,4]{0,1:T(4,128)(2,1)S(1)}, bf16[128,4]{0,1:T(4,128)(2,1)}, u32[]{:S(2)}) copy-start(bf16[128,4]{0,1:T(4,128)(2,1)} %param.25) | copy-start | bytes 3076
  50.9 18.6 %copy-start.1 = (bf16[128,128]{1,0:T(8,128)(2,1)S(1)}, bf16[128,128]{1,0:T(8,128)(2,1)}, u32[]{:S(2)}) copy-start(bf16[128,128]{1,0:T(8,128)(2,1)} %refs_1_.4) | copy-start | bytes 98308
  51.0 18.6 %copy-start.2 = (bf16[128,128]{1,0:T(8,128)(2,1)S(1)}, bf16[128,128]{1,0:T(8,128)(2,1)}, u32[]{:S(2)}) copy-start(bf16[128,128]{1,0:T(8,128)(2,1)} %refs_3_.4) | copy-start | bytes 98308
  51.0 18.6 %copy-start.8 = (f32[128]{0:T(128)S(1)}, f32[128]{0:T(128)}, u32[]{:S(2)}) copy-start(f32[128]{0:T(128)} %param.16) | copy-start | bytes 1540
  51.0 18.6 %copy-start.9 = (f32[128]{0:T(128)S(1)}, f32[128]{0:T(128)}, u32[]{:S(2)}) copy-start(f32[128]{0:T(128)} %param.19) | copy-start | bytes 1540
  51.0 18.6 %copy-start.10 = (f32[128]{0:T(128)S(1)}, f32[128]{0:T(128)}, u32[]{:S(2)}) copy-start(f32[128]{0:T(128)} %param.21) | copy-start | bytes 1540
  53.5 50.1 %copy-start.4 = (bf16[128,128]{1,0:T(8,128)(2,1)S(1)}, bf16[128,128]{1,0:T(8,128)(2,1)}, u32[]{:S(2)}) copy-start(bf16[128,128]{1,0:T(8,128)(2,1)} %refs_1_.5) | copy-start | bytes 98308
  53.5 50.1 %copy-start.5 = (bf16[128,128]{1,0:T(8,128)(2,1)S(1)}, bf16[128,128]{1,0:T(8,128)(2,1)}, u32[]{:S(2)}) copy-start(bf16[128,128]{1,0:T(8,128)(2,1)} %refs_2_.1) | copy-start | bytes 98308
  53.5 50.1 %copy-start.6 = (bf16[128,128]{1,0:T(8,128)(2,1)S(1)}, bf16[128,128]{1,0:T(8,128)(2,1)}, u32[]{:S(2)}) copy-start(bf16[128,128]{1,0:T(8,128)(2,1)} %refs_3_.5) | copy-start | bytes 98308
  53.5 50.1 %copy-start.7 = (bf16[128,128]{1,0:T(8,128)(2,1)S(1)}, bf16[128,128]{1,0:T(8,128)(2,1)}, u32[]{:S(2)}) copy-start(bf16[128,128]{1,0:T(8,128)(2,1)} %refs_4_.1) | copy-start | bytes 98308
  53.5 16.1 %all-to-all-start.1 = ((bf16[8,16,2304]{2,1,0:T(8,128)(2,1)}), bf16[8,16,2304]{2,1,0:T(8,128)(2,1)S(1)}, u32[]{:S(2)}, u32[]{:S(2)}) async-start(bf16[8,16,2304]{2,1,0:T(8,128)(2,1)} %outer.1), calls=%async_computation.1 | async-start | bytes 1179648 | tf_op jit(solution)/shard_map/all_to_all | solution.py:365
  60.0 45.0 %copy-start.3 = (bf16[128,128]{1,0:T(8,128)(2,1)S(1)}, bf16[128,128]{1,0:T(8,128)(2,1)}, u32[]{:S(2)}) copy-start(bf16[128,128]{1,0:T(8,128)(2,1)} %refs_6_.1) | copy-start | bytes 98308
  103.6 1.4 %collective-permute-start.7 = (bf16[8,24,384]{2,1,0:T(8,128)(2,1)S(1)}, bf16[8,24,384]{2,1,0:T(8,128)(2,1)S(1)}, u32[]{:S(2)}, u32[]{:S(2)}) collective-permute-start(bf16[8,24,384]{2,1,0:T(8,128)(2,1)S(1)} %bitcast.5), channel_id=1, source_target_pairs={{0,1},{1,0},{2,3},{3,2},{4,5},{5,4},{6,7},{7,6},{8,9},{9,8},{10,11... | collective-permute-start | bytes 442376 | tf_op jit(solution)/shard_map/ppermute | solution.py:387

commit v14 on v13

--- a/solution.py
+++ b/solution.py
@@ -65,35 +65,17 @@
         self.block_tiles = -(-self.block // self.chans)
 
 
-def edges_kernel(sz, len_ref, x_ref, ln_ref, w_ref, out_ref, *refs):
-    near = refs[: sz.group]
-    norm_ref, pair_ref = refs[sz.group :]
-    length, me = len_ref[0], position()
-    first = me * sz.rows
-    cd, ch = sz.chans, sz.channels
-    mine = me & (sz.group - 1)
-    r = lax.broadcasted_iota(jnp.int32, (ch, ch), 0)
-    e = lax.broadcasted_iota(jnp.int32, (ch, ch), 1)
-    plain = (r == e).astype(BF16)
-    slots = (((r // cd) ^ mine) * cd + r % cd == e).astype(BF16)
-    picks = (plain, plain, slots, slots)
-    weights = [dot(pick, w_ref[p], 1, 1).astype(BF16) for p, pick in enumerate(picks)]
-    stacked = jnp.concatenate([weights[p] for p in (0, 2, 1, 3)], axis=0)
-    gain = ln_ref[...]
+def normalise(sz, row, x, gain, norm_ref):
     main = sz.whole * LANES
-    for row in range(sz.rows):
-        x = x_ref[row].astype(F32)
-        for d in range(sz.devices):
-            pair_ref[d, row * sz.rows : (row + 1) * sz.rows, :] = x[d * sz.rows : (d + 1) * sz.rows]
-        normed = norm_last(x, gain).astype(BF16)
-        norm_ref[pl.ds(row * main, main), :] = normed[:main]
-        if sz.rest:
-            h, q = divmod(row, sz.half)
-            norm_ref[pl.ds(sz.rows * main + q * LANES + h * sz.rest, sz.rest), :] = normed[main:]
-    for d in range(sz.devices):
-        for t in range(sz.block_tiles):
-            at = (sz.tiles + t) * LANES
-            out_ref[d, :, at : at + LANES] = pair_ref[d, t * cd : (t + 1) * cd, :].astype(BF16)
+    normed = norm_last(x, gain).astype(BF16)
+    norm_ref[pl.ds(row * main, main), :] = normed[:main]
+    if sz.rest:
+        h, q = divmod(row, sz.half)
+        norm_ref[pl.ds(sz.rows * main + q * LANES + h * sz.rest, sz.rest), :] = normed[main:]
+
+
+def project_edges(sz, length, first, gate, value, pick, norm_ref, store):
+    main, ch = sz.whole * LANES, sz.channels
     lane = lax.broadcasted_iota(jnp.int32, (1, LANES), 1)
 
     def live(tile):
@@ -106,18 +88,60 @@
         k = main + lane - jnp.where(second, sz.rest, 0)
         return ((row < length) & (k < length)).astype(F32)
 
+    weights = jnp.concatenate([dot(pick, w, 1, 1).astype(BF16) for w in (gate, value)], axis=0)
     step = 2 if sz.tiles % 2 == 0 else 1
     for tile in range(0, sz.tiles, step):
         n = norm_ref[pl.ds(tile * LANES, step * LANES), :]
         mask = jnp.concatenate([live(tile + s) for s in range(step)], axis=1)
-        both = dot(stacked, n, 1, 1)
-        edge = (sigmoid(both[: 2 * ch]) * (both[2 * ch :] * mask)).astype(BF16)
-        to = slice(tile * LANES, (tile + step) * LANES)
+        both = dot(weights, n, 1, 1)
+        edge = (sigmoid(both[:ch]) * (both[ch:] * mask)).astype(BF16)
         for g in range(sz.group):
-            left = edge[g * cd : (g + 1) * cd]
-            out_ref[g, :, to] = left
-            out_ref[sz.group + g, :, to] = left
-            near[g][:, to] = edge[ch + g * cd : ch + (g + 1) * cd]
+            store(
+                g,
+                slice(tile * LANES, (tile + step) * LANES),
+                edge[g * sz.chans : (g + 1) * sz.chans],
+            )
+
+
+def left_kernel(sz, len_ref, x_ref, ln_ref, w_ref, out_ref, norm_ref, pair_ref):
+    cd, ch = sz.chans, sz.channels
+    gain = ln_ref[...]
+    for row in range(sz.rows):
+        x = x_ref[row].astype(F32)
+        for d in range(sz.devices):
+            pair_ref[d, row * sz.rows : (row + 1) * sz.rows, :] = x[d * sz.rows : (d + 1) * sz.rows]
+        normalise(sz, row, x, gain, norm_ref)
+    for d in range(sz.devices):
+        for t in range(sz.block_tiles):
+            at = (sz.tiles + t) * LANES
+            out_ref[d, :, at : at + LANES] = pair_ref[d, t * cd : (t + 1) * cd, :].astype(BF16)
+    r = lax.broadcasted_iota(jnp.int32, (ch, ch), 0)
+    e = lax.broadcasted_iota(jnp.int32, (ch, ch), 1)
+
+    def store(g, lanes, edge):
+        out_ref[g, :, lanes] = edge
+        out_ref[sz.group + g, :, lanes] = edge
+
+    first = position() * sz.rows
+    pick = (r == e).astype(BF16)
+    project_edges(sz, len_ref[0], first, w_ref[0], w_ref[1], pick, norm_ref, store)
+
+
+def right_kernel(sz, len_ref, x_ref, ln_ref, w_ref, *refs):
+    near, norm_ref = refs[: sz.group], refs[sz.group]
+    cd, ch = sz.chans, sz.channels
+    gain = ln_ref[...]
+    for row in range(sz.rows):
+        normalise(sz, row, x_ref[row].astype(F32), gain, norm_ref)
+    me = position()
+    r = lax.broadcasted_iota(jnp.int32, (ch, ch), 0)
+    e = lax.broadcasted_iota(jnp.int32, (ch, ch), 1)
+    pick = (((r // cd) ^ (me & (sz.group - 1))) * cd + r % cd == e).astype(BF16)
+
+    def store(g, lanes, edge):
+        near[g][:, lanes] = edge
+
+    project_edges(sz, len_ref[0], me * sz.rows, w_ref[2], w_ref[3], pick, norm_ref, store)
 
 
 def unpack(sz, ref, owner, main_ref, rest_ref):
@@ -143,7 +167,7 @@
     return jnp.concatenate(parts, axis=1) if len(parts) > 1 else parts[0]
 
 
-def right_kernel(sz, *refs):
+def arrange_kernel(sz, *refs):
     near, (out_ref, main_ref, rest_ref) = refs[: sz.group], refs[sz.group :]
     mine = position() & (sz.group - 1)
     for r in range(sz.group):
@@ -240,20 +264,19 @@
 
 
 def attend_kernel(
-    sz, heads, len_ref, q_ref, k_ref, v_ref, g_ref, first_ref, aout_ref, *refs
+    sz, heads, steps, len_ref, q_ref, k_ref, v_ref, g_ref, first_ref, aout_ref, *refs
 ):
     bias_refs, (out_ref, rows_ref, bias_ref) = refs[:-3], refs[-3:]
     n, w, ch = sz.crop, sz.whole, sz.channels
-    length, core = len_ref[0], lax.axis_index("node")
+    length, me = len_ref[0], position()
     width = q_ref.shape[2]
     hd = width // heads
     per = sz.rows * heads // 2
-    for other, ref in enumerate(bias_refs):
-        for chip in range(ref.shape[0]):
-            block = ref[chip].astype(F32) * LOG2E
-            owner = 2 * chip + (core ^ other)
+    for ref, offsets in zip(bias_refs, steps):
+        for place, offset in enumerate(offsets):
+            block = ref[place].astype(F32) * LOG2E
             for p in range(2):
-                at = pl.ds(pl.multiple_of((owner * 2 + p) * per, 8), per)
+                at = pl.ds(pl.multiple_of(((me ^ offset) * 2 + p) * per, 8), per)
                 for m in range(w):
                     rows_ref[m, at, :] = block[:, (p * w + m) * LANES : (p * w + m + 1) * LANES]
                 if sz.rest:
@@ -295,6 +318,18 @@
         out_ref[j] = (first_ref[j].astype(F32) + dot(gated, aout_ref[...], 1, 0)).astype(BF16)
 
 
+def spread(block, devices):
+    pieces, offsets = [block[None]], [[0]]
+    bit = devices // 2
+    while bit:
+        held = jnp.concatenate(pieces, axis=0) if len(pieces) > 1 else pieces[0]
+        known = [o for part in offsets for o in part]
+        pieces.append(lax.ppermute(held, AXES, [(d, d ^ bit) for d in range(devices)]))
+        offsets.append([o ^ bit for o in known])
+        bit //= 2
+    return pieces, offsets
+
+
 def shards(
     devices,
     pair_rep, length, ln_pair, tri_in, tri_gate, ln_hidden, tri_out, ln_att,
@@ -324,16 +359,25 @@
             for r, block in enumerate(blocks)
         ]
 
-    left, *others = call(
-        bound(edges_kernel),
-        [slab(t + bt, devices)] + [slab(t)] * g,
+    left = call(
+        bound(left_kernel),
+        slab(t + bt, devices),
         (length, pair_rep, ln_pair[None], tri_in),
         scratch=[
             pltpu.VMEM((rows * crop, ch), BF16),
             pltpu.VMEM((devices, bt * cd, ch), F32),
         ],
         smem=(0,),
-        name="edges",
+        name="left",
+        vmem=VMEM_MOST,
+    )
+    others = call(
+        bound(right_kernel),
+        [slab(t)] * g,
+        (length, pair_rep, ln_pair[None], tri_in),
+        scratch=[pltpu.VMEM((rows * crop, ch), BF16)],
+        smem=(0,),
+        name="right",
         vmem=VMEM_MOST,
     )
     left = lax.all_to_all(left, AXES, split_axis=0, concat_axis=0, tiled=True)
@@ -341,14 +385,14 @@
     rest = sz.rest > 0
     column_rows = sz.columns * cd
     right = call(
-        bound(right_kernel),
+        bound(arrange_kernel),
         shape((cd, sz.columns, n), BF16),
         tuple(near),
         scratch=[
             pltpu.VMEM((sz.whole, column_rows, LANES), F32),
             pltpu.VMEM((column_rows if rest else 8, LANES), F32),
         ],
-        name="right",
+        name="arrange",
     )
     outer = call(
         bound(outer_kernel),
@@ -383,8 +427,7 @@
         ],
         name="update",
     )
-    same = lax.all_gather(bias, "row", axis=0, tiled=False)
-    other = lax.ppermute(same, "node", [(0, 1), (1, 0)])
+    pieces, steps = spread(bias, devices)
     query, key, value, gate = call(
         bound(project_kernel),
         [
@@ -397,9 +440,9 @@
         name="project",
     )
     out = call(
-        bound(attend_kernel, heads),
+        bound(attend_kernel, heads, steps),
         shape((rows, n, ch), BF16),
-        (length, query, key, value, gate, first, att_out, same, other),
+        (length, query, key, value, gate, first, att_out, *pieces),
         scratch=[
             pltpu.VMEM((-(-n // LANES), n * heads, LANES), F32),
             pltpu.VMEM((heads, n, n), F32),

time: 110 us -> 92.1 us (0.84)
  blocking collectives: 30.7 us -> 0 us
  waiting for transfers between devices: 41.4 us -> 46 us
  starting transfers between devices: 20.6 us -> 24.9 us
  Pallas kernels: 16.1 us -> 18.9 us
    all_gather x1 -> x0, blocking collectives: 30.7 us -> none  [shards(): same = lax.all_gather(bias, 'row', axis=0, tiled=False)]
    ppermute x1 -> x4, waiting for transfers between devices: 0.56 us -> 8.22 us  [spread(): lax.ppermute(held, AXES, [(d, d ^ bit) for d in range(devices)])]
    ppermute x1 -> x4, starting transfers between devices: 0.01 us -> 5.5 us  [spread(): lax.ppermute(held, AXES, [(d, d ^ bit) for d in range(devices)])]
    ppermute x7, waiting for transfers between devices: 31.4 us -> 28.4 us  [send(): lax.ppermute(block, AXES, [(d, d ^ offset ^ r) for d in range(devices)])]
    pallas_call x6 -> x7, Pallas kernels: 16.1 us -> 18.9 us  [call(): pl.pallas_call(kernel, out_shape=out_shape, in_specs=specs, out_specs=ins...]
  transfers between devices with their start and end apart: 10 -> 13, of which waited for: 8 -> 11; matrix products, arithmetic and copies ran while one was open for 0% -> 0% of each run, Pallas kernels for 1% -> 5%
where the time goes in v14:
time: 92.1 us; the launch traced here: 91.8 us
  waiting for transfers between devices  46 us (50%)
  starting transfers between devices  24.9 us (27%)
  Pallas kernels  18.9 us (21%)
  local copies, waits for them, and re-layouts  1.09 us (1%)
    ppermute x7, waiting for transfers between devices, send(): lax.ppermute(block, AXES, [(d, d ^ offset ^ r) for d in range(devices)])  28.4 us
    pallas_call x7, Pallas kernels, call(): pl.pallas_call(kernel, out_shape=out_shape, in_specs=specs, out_specs=ins...  18.9 us
    all_to_all x1, waiting for transfers between devices, shards(): lax.all_to_all(outer, AXES, split_axis=0, concat_axis=0, tiled=True, axis...  9.36 us
    ppermute x4, waiting for transfers between devices, spread(): lax.ppermute(held, AXES, [(d, d ^ bit) for d in range(devices)])  8.22 us
    all_to_all x1, starting transfers between devices, shards(): left = lax.all_to_all(left, AXES, split_axis=0, concat_axis=0, tiled=True)  7.38 us
    ppermute x7, starting transfers between devices, send(): lax.ppermute(block, AXES, [(d, d ^ offset ^ r) for d in range(devices)])  6.48 us
    ppermute x4, starting transfers between devices, spread(): lax.ppermute(held, AXES, [(d, d ^ bit) for d in range(devices)])  5.5 us
    all_to_all x1, starting transfers between devices, shards(): lax.all_to_all(outer, AXES, split_axis=0, concat_axis=0, tiled=True, axis...  5.48 us
  transfers between devices with their start and end apart: 13, of which 11 were waited for; matrix products, arithmetic and copies ran while one was open for 0% of the time, Pallas kernels for 5%

profile of v14, /device:TPU:0, one launch (start us, length us, event | category | flops | bytes accessed | tf_op | source)
XLA Modules:
  0.0 91.8 jit_solution(4024719057909738639)
XLA Ops:
  0.7 3.6 %left.1 = bf16[16,16,3456]{2,1,0:T(8,128)(2,1)} custom-call(s32[1]{0:T(128)S(6)} %copy.16.refs_0_, bf16[12,192,128]{2,1,0:T(8,128)(2,1)} %refs_1_.5, f32[1,128]{1,0:T(1,128)} %bitcast.10, bf16[4,128,128]{2,1,0:T(8,128)(2,1)} %refs_3_.5), custom_call_target="tpu_custom_call" | custom-call | tf_op jit(solution)/shard_map/left/pallas_call | solution.py:43
  4.3 7.4 %all-to-all-start = ((bf16[16,16,3456]{2,1,0:T(8,128)(2,1)}), bf16[16,16,3456]{2,1,0:T(8,128)(2,1)S(1)}, u32[]{:S(2)}, u32[]{:S(2)}) async-start(bf16[16,16,3456]{2,1,0:T(8,128)(2,1)} %left.1), calls=%async_computation | async-start | bytes 3538944 | tf_op jit(solution)/shard_map/all_to_all | solution.py:383
  11.7 3.1 %right.1 = (bf16[16,2304]{1,0:T(8,128)(2,1)}, bf16[16,2304]{1,0:T(8,128)(2,1)}, bf16[16,2304]{1,0:T(8,128)(2,1)}, bf16[16,2304]{1,0:T(8,128)(2,1)}, bf16[16,2304...) custom-call(s32[1]{0:T(128)S(6)} %copy.16.refs_0_, ...), custom_call_target="tpu_custom_call" | custom-call | tf_op jit(solution)/shard_map/right/pallas_call | solution.py:43
  14.8 0.4 collective-permute-start
  15.2 1.7 %collective-permute-start.1 = (bf16[16,2304]{1,0:T(8,128)(2,1)}, bf16[16,2304]{1,0:T(8,128)(2,1)S(1)}, u32[]{:S(2)}, u32[]{:S(2)}) collective-permute-start(bf16[16,2304]{1,0:T(8,128)(2,1)} %get-tuple-element.22), channel_id=1, source_target_pairs={{0,2},{1,3},{2,0},{3,1},{4,6},{5,7},{6,4},{7,5},{8,10},{9,11},{10,... | collective-permute-start | bytes 221192 | tf_op jit(solution)/shard_map/ppermute | solution.py:358
  16.9 1.7 %collective-permute-start.3 = (bf16[16,2304]{1,0:T(8,128)(2,1)}, bf16[16,2304]{1,0:T(8,128)(2,1)S(1)}, u32[]{:S(2)}, u32[]{:S(2)}) collective-permute-start(bf16[16,2304]{1,0:T(8,128)(2,1)} %get-tuple-element.24), channel_id=1, source_target_pairs={{0,4},{1,5},{2,6},{3,7},{4,0},{5,1},{6,2},{7,3},{8,12},{9,13},{10,... | collective-permute-start | bytes 221192 | tf_op jit(solution)/shard_map/ppermute | solution.py:358
  18.6 0.1 collective-permute-start.4
  18.7 2.6 %collective-permute-start.5 = (bf16[16,2304]{1,0:T(8,128)(2,1)}, bf16[16,2304]{1,0:T(8,128)(2,1)S(1)}, u32[]{:S(2)}, u32[]{:S(2)}) collective-permute-start(bf16[16,2304]{1,0:T(8,128)(2,1)} %get-tuple-element.26), channel_id=1, source_target_pairs={{0,6},{1,7},{2,4},{3,5},{4,2},{5,3},{6,0},{7,1},{8,14},{9,15},{10,... | collective-permute-start | bytes 221192 | tf_op jit(solution)/shard_map/ppermute | solution.py:358
  21.3 6.1 %collective-permute-done.1.refs_2_ = bf16[16,2304]{1,0:T(8,128)(2,1)S(1)} collective-permute-done((bf16[16,2304]{1,0:T(8,128)(2,1)}, bf16[16,2304]{1,0:T(8,128)(2,1)S(1)}, u32[]{:S(2)}, u32[]{:S(2)}) %collective-permute-start.1) | collective-permute-done | bytes 73760 | tf_op jit(solution)/shard_map/ppermute | solution.py:358
  27.4 0.6 collective-permute-done.2.refs_3_
  28.0 15.2 %collective-permute-done.3.refs_4_ = bf16[16,2304]{1,0:T(8,128)(2,1)S(1)} collective-permute-done((bf16[16,2304]{1,0:T(8,128)(2,1)}, bf16[16,2304]{1,0:T(8,128)(2,1)S(1)}, u32[]{:S(2)}, u32[]{:S(2)}) %collective-permute-start.3) | collective-permute-done | bytes 73760 | tf_op jit(solution)/shard_map/ppermute | solution.py:358
  43.3 1.6 %collective-permute-done.4.refs_5_ = bf16[16,2304]{1,0:T(8,128)(2,1)S(1)} collective-permute-done((bf16[16,2304]{1,0:T(8,128)(2,1)}, bf16[16,2304]{1,0:T(8,128)(2,1)S(1)}, u32[]{:S(2)}, u32[]{:S(2)}) %collective-permute-start.4) | collective-permute-done | bytes 73760 | tf_op jit(solution)/shard_map/ppermute | solution.py:358
  44.8 1.6 %collective-permute-done.5.refs_6_ = bf16[16,2304]{1,0:T(8,128)(2,1)S(1)} collective-permute-done((bf16[16,2304]{1,0:T(8,128)(2,1)}, bf16[16,2304]{1,0:T(8,128)(2,1)S(1)}, u32[]{:S(2)}, u32[]{:S(2)}) %collective-permute-start.5) | collective-permute-done | bytes 73760 | tf_op jit(solution)/shard_map/ppermute | solution.py:358
  46.4 3.2 %collective-permute-done.6.refs_7_ = bf16[16,2304]{1,0:T(8,128)(2,1)S(1)} collective-permute-done((bf16[16,2304]{1,0:T(8,128)(2,1)}, bf16[16,2304]{1,0:T(8,128)(2,1)S(1)}, u32[]{:S(2)}, u32[]{:S(2)}) %collective-permute-start.6) | collective-permute-done | bytes 73760 | tf_op jit(solution)/shard_map/ppermute | solution.py:358
  49.7 0.9 copy-done
  50.5 0.7 arrange.1.refs_1_
  51.3 0.0 copy-start.11
  51.4 2.5 %outer.1 = bf16[8,16,2304]{2,1,0:T(8,128)(2,1)} custom-call(bf16[16,16,3456]{2,1,0:T(8,128)(2,1)S(1)} %all-to-all-done.refs_0_.refs_7_, bf16[16,96,192]{2,1,0:T(8,128)(2,1)S(1)} %arrange.1.refs_1_), custom_call_target="tpu_custom_call" | custom-call | tf_op jit(solution)/shard_map/outer/pallas_call | solution.py:43
  53.8 5.5 %all-to-all-start.1 = ((bf16[8,16,2304]{2,1,0:T(8,128)(2,1)}), bf16[8,16,2304]{2,1,0:T(8,128)(2,1)S(1)}, u32[]{:S(2)}, u32[]{:S(2)}) async-start(bf16[8,16,2304]{2,1,0:T(8,128)(2,1)} %outer.1), calls=%async_computation.1 | async-start | bytes 1179648 | tf_op jit(solution)/shard_map/all_to_all | solution.py:409
  59.3 0.1 copy.15.refs_5_
  59.5 9.4 %all-to-all-done.1.refs_6_ = bf16[8,16,2304]{2,1,0:T(8,128)(2,1)S(1)} async-done(((bf16[8,16,2304]{2,1,0:T(8,128)(2,1)}), bf16[8,16,2304]{2,1,0:T(8,128)(2,1)S(1)}, u32[]{:S(2)}, u32[]{:S(2)}) %all-to-all-start.1) | async-done | bytes 589856 | tf_op jit(solution)/shard_map/all_to_all | solution.py:409
  68.9 3.3 %update.1 = (bf16[12,192,128]{2,1,0:T(8,128)(2,1)S(1)}, bf16[12,192,128]{2,1,0:T(8,128)(2,1)S(1)}, bf16[24,384]{1,0:T(8,128)(2,1)S(1)}) custom-call(f32[1,128]{1,0:T(1,128)S(1)} %bitcast.12, bf16[128,128]{1,0:T(8,128)(2,1)S(1)} %copy-done.1, f32[1,128]{1,0:T(1,128)S(1)} %bitcast.13, bf16[128,128]{1,0:T(8,128)(2,1)S(1)} %copy-done.2, f32[1,128]{1,0:T(1,128)S(1)} %bitcast.14, ...), custom_call_target="tpu_custom_call" | custom-call | tf_op jit(solution)/shard_map/update/pallas_call | solution.py:43
  72.2 2.2 %collective-permute-start.7 = (bf16[1,24,384]{2,1,0:T(8,128)(2,1)S(1)}, bf16[1,24,384]{2,1,0:T(8,128)(2,1)S(1)}, u32[]{:S(2)}, u32[]{:S(2)}) collective-permute-start(bf16[1,24,384]{2,1,0:T(8,128)(2,1)S(1)} %bitcast.5), channel_id=1, source_target_pairs={{0,8},{1,9},{2,10},{3,11},{4,12},{5,13},{6,14},{7,15},{8,0},{9,1},... | collective-permute-start | bytes 55304 | tf_op jit(solution)/shard_map/ppermute | solution.py:327
  74.3 2.5 %collective-permute-done.7.refs_8_ = bf16[1,24,384]{2,1,0:T(8,128)(2,1)S(1)} collective-permute-done((bf16[1,24,384]{2,1,0:T(8,128)(2,1)S(1)}, bf16[1,24,384]{2,1,0:T(8,128)(2,1)S(1)}, u32[]{:S(2)}, u32[]{:S(2)}) %collective-permute-start.7) | collective-permute-done | bytes 18464 | tf_op jit(solution)/shard_map/ppermute | solution.py:327
  76.8 1.5 %collective-permute-start.8 = (bf16[2,24,384]{2,1,0:T(8,128)(2,1)S(1)}, bf16[2,24,384]{2,1,0:T(8,128)(2,1)S(1)}, u32[]{:S(2)}, u32[]{:S(2)}) collective-permute-start(bf16[2,24,384]{2,1,0:T(8,128)(2,1)S(1)} %pad_maximum_fusion.2), channel_id=1, source_target_pairs={{0,4},{1,5},{2,6},{3,7},{4,0},{5,1},{6,2},{7,3},{8,12},{9,13},{10,... | collective-permute-start | bytes 110600 | tf_op jit(solution)/shard_map/ppermute | solution.py:327
  78.4 2.5 %collective-permute-done.8.refs_9_ = bf16[2,24,384]{2,1,0:T(8,128)(2,1)S(1)} collective-permute-done((bf16[2,24,384]{2,1,0:T(8,128)(2,1)S(1)}, bf16[2,24,384]{2,1,0:T(8,128)(2,1)S(1)}, u32[]{:S(2)}, u32[]{:S(2)}) %collective-permute-start.8) | collective-permute-done | bytes 36896 | tf_op jit(solution)/shard_map/ppermute | solution.py:327
  80.9 1.7 %collective-permute-start.9 = (bf16[4,24,384]{2,1,0:T(8,128)(2,1)S(1)}, bf16[4,24,384]{2,1,0:T(8,128)(2,1)S(1)}, u32[]{:S(2)}, u32[]{:S(2)}) collective-permute-start(bf16[4,24,384]{2,1,0:T(8,128)(2,1)S(1)} %pad_maximum_fusion.1), channel_id=1, source_target_pairs={{0,2},{1,3},{2,0},{3,1},{4,6},{5,7},{6,4},{7,5},{8,10},{9,11},{10,... | collective-permute-start | bytes 221192 | tf_op jit(solution)/shard_map/ppermute | solution.py:327
  82.6 2.7 %collective-permute-done.9.refs_10_ = bf16[4,24,384]{2,1,0:T(8,128)(2,1)S(1)} collective-permute-done((bf16[4,24,384]{2,1,0:T(8,128)(2,1)S(1)}, bf16[4,24,384]{2,1,0:T(8,128)(2,1)S(1)}, u32[]{:S(2)}, u32[]{:S(2)}) %collective-permute-start.9) | collective-permute-done | bytes 73760 | tf_op jit(solution)/shard_map/ppermute | solution.py:327
  85.3 0.1 collective-permute-start.10
  85.5 0.8 project.1
  86.2 0.5 collective-permute-done.10.refs_11_
  86.8 5.0 %attend.1 = bf16[12,192,128]{2,1,0:T(8,128)(2,1)} custom-call(s32[1]{0:T(128)S(6)} %copy.16.refs_0_, bf16[12,192,128]{2,1,0:T(8,128)(2,1)S(1)} %get-tuple-element.29.refs_1_, bf16[12,192,128]{2,1,0:T(8,128)(2,1)S(1)} %get-tuple-element.30.refs_2_, bf16[12,192,128]{2,1,0:T(8,128)(2,1)S(1)} %get-tuple-element.31.refs_3_, ...), custom_call_target="tpu_custom_call" | custom-call | tf_op jit(solution)/shard_map/attend/pallas_call | solution.py:43
  (29 shorter events, 0.1 us)
Async XLA Ops:
  4.3 47.1 %all-to-all-start = ((bf16[16,16,3456]{2,1,0:T(8,128)(2,1)}), bf16[16,16,3456]{2,1,0:T(8,128)(2,1)S(1)}, u32[]{:S(2)}, u32[]{:S(2)}) async-start(bf16[16,16,3456]{2,1,0:T(8,128)(2,1)} %left.1), calls=%async_computation | async-start | bytes 3538944 | tf_op jit(solution)/shard_map/all_to_all | solution.py:383
  14.8 3.9 %collective-permute-start = (bf16[16,2304]{1,0:T(8,128)(2,1)}, bf16[16,2304]{1,0:T(8,128)(2,1)S(1)}, u32[]{:S(2)}, u32[]{:S(2)}) collective-permute-start(bf16[16,2304]{1,0:T(8,128)(2,1)} %get-tuple-element.21), channel_id=1, source_target_pairs={{0,1},{1,0},{2,3},{3,2},{4,5},{5,4},{6,7},{7,6},{8,9},{9,8},{10,11... | collective-permute-start | bytes 221192 | tf_op jit(solution)/shard_map/ppermute | solution.py:358
  15.2 12.2 %collective-permute-start.1 = (bf16[16,2304]{1,0:T(8,128)(2,1)}, bf16[16,2304]{1,0:T(8,128)(2,1)S(1)}, u32[]{:S(2)}, u32[]{:S(2)}) collective-permute-start(bf16[16,2304]{1,0:T(8,128)(2,1)} %get-tuple-element.22), channel_id=1, source_target_pairs={{0,2},{1,3},{2,0},{3,1},{4,6},{5,7},{6,4},{7,5},{8,10},{9,11},{10,... | collective-permute-start | bytes 221192 | tf_op jit(solution)/shard_map/ppermute | solution.py:358
  16.9 11.1 %collective-permute-start.2 = (bf16[16,2304]{1,0:T(8,128)(2,1)}, bf16[16,2304]{1,0:T(8,128)(2,1)S(1)}, u32[]{:S(2)}, u32[]{:S(2)}) collective-permute-start(bf16[16,2304]{1,0:T(8,128)(2,1)} %get-tuple-element.23), channel_id=1, source_target_pairs={{0,3},{1,2},{2,1},{3,0},{4,7},{5,6},{6,5},{7,4},{8,11},{9,10},{10,... | collective-permute-start | bytes 221192 | tf_op jit(solution)/shard_map/ppermute | solution.py:358
  16.9 26.4 %collective-permute-start.3 = (bf16[16,2304]{1,0:T(8,128)(2,1)}, bf16[16,2304]{1,0:T(8,128)(2,1)S(1)}, u32[]{:S(2)}, u32[]{:S(2)}) collective-permute-start(bf16[16,2304]{1,0:T(8,128)(2,1)} %get-tuple-element.24), channel_id=1, source_target_pairs={{0,4},{1,5},{2,6},{3,7},{4,0},{5,1},{6,2},{7,3},{8,12},{9,13},{10,... | collective-permute-start | bytes 221192 | tf_op jit(solution)/shard_map/ppermute | solution.py:358
  18.6 26.3 %collective-permute-start.4 = (bf16[16,2304]{1,0:T(8,128)(2,1)}, bf16[16,2304]{1,0:T(8,128)(2,1)S(1)}, u32[]{:S(2)}, u32[]{:S(2)}) collective-permute-start(bf16[16,2304]{1,0:T(8,128)(2,1)} %get-tuple-element.25), channel_id=1, source_target_pairs={{0,5},{1,4},{2,7},{3,6},{4,1},{5,0},{6,3},{7,2},{8,13},{9,12},{10,... | collective-permute-start | bytes 221192 | tf_op jit(solution)/shard_map/ppermute | solution.py:358
  18.7 27.7 %collective-permute-start.5 = (bf16[16,2304]{1,0:T(8,128)(2,1)}, bf16[16,2304]{1,0:T(8,128)(2,1)S(1)}, u32[]{:S(2)}, u32[]{:S(2)}) collective-permute-start(bf16[16,2304]{1,0:T(8,128)(2,1)} %get-tuple-element.26), channel_id=1, source_target_pairs={{0,6},{1,7},{2,4},{3,5},{4,2},{5,3},{6,0},{7,1},{8,14},{9,15},{10,... | collective-permute-start | bytes 221192 | tf_op jit(solution)/shard_map/ppermute | solution.py:358
  27.4 22.3 %collective-permute-start.6 = (bf16[16,2304]{1,0:T(8,128)(2,1)}, bf16[16,2304]{1,0:T(8,128)(2,1)S(1)}, u32[]{:S(2)}, u32[]{:S(2)}) collective-permute-start(bf16[16,2304]{1,0:T(8,128)(2,1)} %get-tuple-element.27), channel_id=1, source_target_pairs={{0,7},{1,6},{2,5},{3,4},{4,3},{5,2},{6,1},{7,0},{8,15},{9,14},{10,... | collective-permute-start | bytes 221192 | tf_op jit(solution)/shard_map/ppermute | solution.py:358
  49.7 0.9 copy-start
  51.3 8.0 %copy-start.11 = (bf16[128,4]{0,1:T(4,128)(2,1)S(1)}, bf16[128,4]{0,1:T(4,128)(2,1)}, u32[]{:S(2)}) copy-start(bf16[128,4]{0,1:T(4,128)(2,1)} %param.25) | copy-start | bytes 3076
  51.3 17.6 %copy-start.1 = (bf16[128,128]{1,0:T(8,128)(2,1)S(1)}, bf16[128,128]{1,0:T(8,128)(2,1)}, u32[]{:S(2)}) copy-start(bf16[128,128]{1,0:T(8,128)(2,1)} %refs_1_.6) | copy-start | bytes 98308
  51.3 17.5 %copy-start.2 = (bf16[128,128]{1,0:T(8,128)(2,1)S(1)}, bf16[128,128]{1,0:T(8,128)(2,1)}, u32[]{:S(2)}) copy-start(bf16[128,128]{1,0:T(8,128)(2,1)} %refs_3_.6) | copy-start | bytes 98308
  51.3 17.5 %copy-start.8 = (f32[128]{0:T(128)S(1)}, f32[128]{0:T(128)}, u32[]{:S(2)}) copy-start(f32[128]{0:T(128)} %param.16) | copy-start | bytes 1540
  51.3 17.5 %copy-start.9 = (f32[128]{0:T(128)S(1)}, f32[128]{0:T(128)}, u32[]{:S(2)}) copy-start(f32[128]{0:T(128)} %param.19) | copy-start | bytes 1540
  51.3 17.5 %copy-start.10 = (f32[128]{0:T(128)S(1)}, f32[128]{0:T(128)}, u32[]{:S(2)}) copy-start(f32[128]{0:T(128)} %param.21) | copy-start | bytes 1540
  53.8 15.0 %all-to-all-start.1 = ((bf16[8,16,2304]{2,1,0:T(8,128)(2,1)}), bf16[8,16,2304]{2,1,0:T(8,128)(2,1)S(1)}, u32[]{:S(2)}, u32[]{:S(2)}) async-start(bf16[8,16,2304]{2,1,0:T(8,128)(2,1)} %outer.1), calls=%async_computation.1 | async-start | bytes 1179648 | tf_op jit(solution)/shard_map/all_to_all | solution.py:409
  59.3 26.1 %copy-start.4 = (bf16[128,128]{1,0:T(8,128)(2,1)S(1)}, bf16[128,128]{1,0:T(8,128)(2,1)}, u32[]{:S(2)}) copy-start(bf16[128,128]{1,0:T(8,128)(2,1)} %refs_1_.7) | copy-start | bytes 98308
  59.3 26.1 %copy-start.5 = (bf16[128,128]{1,0:T(8,128)(2,1)S(1)}, bf16[128,128]{1,0:T(8,128)(2,1)}, u32[]{:S(2)}) copy-start(bf16[128,128]{1,0:T(8,128)(2,1)} %refs_2_.1) | copy-start | bytes 98308
  59.3 26.1 %copy-start.6 = (bf16[128,128]{1,0:T(8,128)(2,1)S(1)}, bf16[128,128]{1,0:T(8,128)(2,1)}, u32[]{:S(2)}) copy-start(bf16[128,128]{1,0:T(8,128)(2,1)} %refs_3_.7) | copy-start | bytes 98308
  59.3 26.1 %copy-start.7 = (bf16[128,128]{1,0:T(8,128)(2,1)S(1)}, bf16[128,128]{1,0:T(8,128)(2,1)}, u32[]{:S(2)}) copy-start(bf16[128,128]{1,0:T(8,128)(2,1)} %refs_4_.1) | copy-start | bytes 98308
  68.9 17.9 %copy-start.3 = (bf16[128,128]{1,0:T(8,128)(2,1)S(1)}, bf16[128,128]{1,0:T(8,128)(2,1)}, u32[]{:S(2)}) copy-start(bf16[128,128]{1,0:T(8,128)(2,1)} %refs_6_.1) | copy-start | bytes 98308
  72.2 4.7 %collective-permute-start.7 = (bf16[1,24,384]{2,1,0:T(8,128)(2,1)S(1)}, bf16[1,24,384]{2,1,0:T(8,128)(2,1)S(1)}, u32[]{:S(2)}, u32[]{:S(2)}) collective-permute-start(bf16[1,24,384]{2,1,0:T(8,128)(2,1)S(1)} %bitcast.5), channel_id=1, source_target_pairs={{0,8},{1,9},{2,10},{3,11},{4,12},{5,13},{6,14},{7,15},{8,0},{9,1},... | collective-permute-start | bytes 55304 | tf_op jit(solution)/shard_map/ppermute | solution.py:327
  76.8 4.0 %collective-permute-start.8 = (bf16[2,24,384]{2,1,0:T(8,128)(2,1)S(1)}, bf16[2,24,384]{2,1,0:T(8,128)(2,1)S(1)}, u32[]{:S(2)}, u32[]{:S(2)}) collective-permute-start(bf16[2,24,384]{2,1,0:T(8,128)(2,1)S(1)} %pad_maximum_fusion.2), channel_id=1, source_target_pairs={{0,4},{1,5},{2,6},{3,7},{4,0},{5,1},{6,2},{7,3},{8,12},{9,13},{10,... | collective-permute-start | bytes 110600 | tf_op jit(solution)/shard_map/ppermute | solution.py:327
  80.9 4.4 %collective-permute-start.9 = (bf16[4,24,384]{2,1,0:T(8,128)(2,1)S(1)}, bf16[4,24,384]{2,1,0:T(8,128)(2,1)S(1)}, u32[]{:S(2)}, u32[]{:S(2)}) collective-permute-start(bf16[4,24,384]{2,1,0:T(8,128)(2,1)S(1)} %pad_maximum_fusion.1), channel_id=1, source_target_pairs={{0,2},{1,3},{2,0},{3,1},{4,6},{5,7},{6,4},{7,5},{8,10},{9,11},{10,... | collective-permute-start | bytes 221192 | tf_op jit(solution)/shard_map/ppermute | solution.py:327
  85.3 1.4 %collective-permute-start.10 = (bf16[8,24,384]{2,1,0:T(8,128)(2,1)S(1)}, bf16[8,24,384]{2,1,0:T(8,128)(2,1)S(1)}, u32[]{:S(2)}, u32[]{:S(2)}) collective-permute-start(bf16[8,24,384]{2,1,0:T(8,128)(2,1)S(1)} %pad_maximum_fusion), channel_id=1, source_target_pairs={{0,1},{1,0},{2,3},{3,2},{4,5},{5,4},{6,7},{7,6},{8,9},{9,8},{10,11... | collective-permute-start | bytes 442376 | tf_op jit(solution)/shard_map/ppermute | solution.py:327

commit v15 on v14

--- a/solution.py
+++ b/solution.py
@@ -34,12 +34,12 @@
     return lax.axis_index("row") * lax.axis_size("node") + lax.axis_index("node")
 
 
-def call(kernel, out_shape, args, scratch=(), smem=(), name=None, vmem=VMEM_BYTES):
+def call(kernel, out_shape, args, scratch=(), smem=(), name=None, vmem=VMEM_BYTES, away=False):
     specs = [
         pl.BlockSpec(memory_space=pltpu.SMEM if n in smem else pltpu.VMEM) for n in range(len(args))
     ]
     single = not isinstance(out_shape, (list, tuple))
-    inside = pl.BlockSpec(memory_space=pltpu.VMEM)
+    inside = pl.BlockSpec(memory_space=pl.ANY if away else pltpu.VMEM)
     return pl.pallas_call(
         kernel,
         out_shape=out_shape,
@@ -103,18 +103,33 @@
             )
 
 
-def left_kernel(sz, len_ref, x_ref, ln_ref, w_ref, out_ref, norm_ref, pair_ref):
+def left_kernel(
+    sz, len_ref, x_ref, ln_ref, w_ref, away_ref, out_ref, norm_ref, wide_ref, pair_ref, sems
+):
     cd, ch = sz.chans, sz.channels
     gain = ln_ref[...]
     for row in range(sz.rows):
         x = x_ref[row].astype(F32)
-        for d in range(sz.devices):
-            pair_ref[d, row * sz.rows : (row + 1) * sz.rows, :] = x[d * sz.rows : (d + 1) * sz.rows]
+        wide_ref[pl.ds(row * sz.crop, sz.crop), :] = x
         normalise(sz, row, x, gain, norm_ref)
     for d in range(sz.devices):
+        for row in range(sz.rows):
+            block = wide_ref[pl.ds(row * sz.crop + d * sz.rows, sz.rows), :]
+            pair_ref[pl.ds(d * sz.block + row * sz.rows, sz.rows), :] = block
         for t in range(sz.block_tiles):
             at = (sz.tiles + t) * LANES
-            out_ref[d, :, at : at + LANES] = pair_ref[d, t * cd : (t + 1) * cd, :].astype(BF16)
+            block = pair_ref[pl.ds(d * sz.block + t * cd, cd), :]
+            out_ref[d, :, at : at + LANES] = block.astype(BF16)
+
+    def leave(start, stop, sem):
+        lanes = pl.ds(start * LANES, (stop - start) * LANES)
+        copy = pltpu.make_async_copy(
+            out_ref.at[:, :, lanes], away_ref.at[:, :, lanes], sems.at[sem]
+        )
+        copy.start()
+        return copy
+
+    pairs_out = leave(sz.tiles, sz.tiles + sz.block_tiles, 0)
     r = lax.broadcasted_iota(jnp.int32, (ch, ch), 0)
     e = lax.broadcasted_iota(jnp.int32, (ch, ch), 1)
 
@@ -125,6 +140,9 @@
     first = position() * sz.rows
     pick = (r == e).astype(BF16)
     project_edges(sz, len_ref[0], first, w_ref[0], w_ref[1], pick, norm_ref, store)
+    edges_out = leave(0, sz.tiles, 1)
+    pairs_out.wait()
+    edges_out.wait()
 
 
 def right_kernel(sz, len_ref, x_ref, ln_ref, w_ref, *refs):
@@ -206,16 +224,29 @@
             out_ref[g, :, tile * LANES : (tile + 1) * LANES] = block.astype(BF16)
 
 
-def update_kernel(
-    sz, lnp_ref, gate_ref, lnh_ref, tri_ref, lna_ref, biasw_ref, sums_ref, pair_ref,
-    first_ref, col_ref, bias_ref, cols_ref, brow_ref,
-):
-    n, w, half, ch, cd = sz.crop, sz.whole, sz.half, sz.channels, sz.chans
+def take_columns(sz, pair_ref, cols_ref):
+    cd = sz.chans
     for s in range(sz.devices):
         for t in range(sz.block_tiles):
             at = (sz.tiles + t) * LANES
             rows = pl.ds(s * sz.block + t * cd, cd)
             cols_ref[rows, :] = pair_ref[s, :, at : at + LANES].astype(F32)
+
+
+def gating_kernel(sz, pair_ref, lnp_ref, gate_ref, gating_ref, cols_ref):
+    take_columns(sz, pair_ref, cols_ref)
+    for j in range(sz.rows):
+        x = cols_ref[pl.ds(j, sz.crop, stride=sz.rows), :]
+        normed = norm_last(x, lnp_ref[...]).astype(BF16)
+        gating_ref[j] = sigmoid(dot(normed, gate_ref[...], 1, 0)).astype(BF16)
+
+
+def update_kernel(
+    sz, gating_ref, lnh_ref, tri_ref, lna_ref, biasw_ref, sums_ref, pair_ref,
+    first_ref, col_ref, bias_ref, cols_ref, brow_ref,
+):
+    n, w, half, ch = sz.crop, sz.whole, sz.half, sz.channels
+    take_columns(sz, pair_ref, cols_ref)
     gain_h = jnp.transpose(jnp.broadcast_to(lnh_ref[...], (ch, ch)))
     tri = tri_ref[...]
 
@@ -235,9 +266,7 @@
             parts.append(rest[q][h * sz.rest : (h + 1) * sz.rest])
         change = jnp.concatenate(parts, axis=0) if len(parts) > 1 else parts[0]
         x = cols_ref[pl.ds(j, n, stride=sz.rows), :]
-        normed = norm_last(x, lnp_ref[...]).astype(BF16)
-        gating = sigmoid(dot(normed, gate_ref[...], 1, 0))
-        first = (x + gating * change).astype(BF16)
+        first = (x + gating_ref[j].astype(F32) * change).astype(BF16)
         first_ref[j] = first
         col = norm_last(first.astype(F32), lna_ref[...]).astype(BF16)
         col_ref[j] = col
@@ -364,10 +393,14 @@
         slab(t + bt, devices),
         (length, pair_rep, ln_pair[None], tri_in),
         scratch=[
+            pltpu.VMEM((devices, cd, (t + bt) * LANES), BF16),
             pltpu.VMEM((rows * crop, ch), BF16),
-            pltpu.VMEM((devices, bt * cd, ch), F32),
+            pltpu.VMEM((rows * crop, ch), F32),
+            pltpu.VMEM((devices * sz.block + cd, ch), F32),
+            pltpu.SemaphoreType.DMA((2,)),
         ],
         smem=(0,),
+        away=True,
         name="left",
         vmem=VMEM_MOST,
     )
@@ -378,7 +411,6 @@
         scratch=[pltpu.VMEM((rows * crop, ch), BF16)],
         smem=(0,),
         name="right",
-        vmem=VMEM_MOST,
     )
     left = lax.all_to_all(left, AXES, split_axis=0, concat_axis=0, tiled=True)
     near = send(others, 0)
@@ -410,6 +442,13 @@
         outer, AXES, split_axis=0, concat_axis=0, tiled=True,
         axis_index_groups=[list(range(g)), list(range(g, devices))],
     )
+    gating = call(
+        bound(gating_kernel),
+        shape((rows, n, ch), BF16),
+        (left, ln_pair[None], tri_gate),
+        scratch=[pltpu.VMEM((devices * sz.block + cd, ch), F32)],
+        name="gating",
+    )
     first, col, bias = call(
         bound(update_kernel),
         [
@@ -418,8 +457,7 @@
             shape((rows * heads // 2, 2 * n), BF16),
         ],
         (
-            ln_pair[None], tri_gate, ln_hidden[None], tri_out, ln_att[None], att_bias,
-            sums, left,
+            gating, ln_hidden[None], tri_out, ln_att[None], att_bias, sums, left,
         ),
         scratch=[
             pltpu.VMEM((devices * sz.block + cd, ch), F32),

time: 92.1 us -> 91.7 us (level)
  Pallas kernels: 18.9 us -> 17.5 us
  starting transfers between devices: 24.9 us -> 26.1 us
    ppermute x7, waiting for transfers between devices: 28.4 us -> 30.2 us  [send(): lax.ppermute(block, AXES, [(d, d ^ offset ^ r) for d in range(devices)])]
    pallas_call x7 -> x8, Pallas kernels: 18.9 us -> 17.5 us  [call(): pl.pallas_call(kernel, out_shape=out_shape, in_specs=specs, out_specs=ins...]
    all_to_all x1, waiting for transfers between devices: 9.36 us -> 8.25 us  [shards(): lax.all_to_all(outer, AXES, split_axis=0, concat_axis=0, tiled=True, axis...]
    all_to_all x1, starting transfers between devices: 5.48 us -> 6.55 us  [shards(): lax.all_to_all(outer, AXES, split_axis=0, concat_axis=0, tiled=True, axis...]
  transfers between devices with their start and end apart: 13 -> 13, of which waited for: 11 -> 11; matrix products, arithmetic and copies ran while one was open for 0% -> 0% of each run, Pallas kernels for 5% -> 4%
where the time goes in v15:
time: 91.7 us; the launch traced here: 91.4 us
  waiting for transfers between devices  46.6 us (51%)
  starting transfers between devices  26.1 us (28%)
  Pallas kernels  17.5 us (19%)
    ppermute x7, waiting for transfers between devices, send(): lax.ppermute(block, AXES, [(d, d ^ offset ^ r) for d in range(devices)])  30.2 us
    pallas_call x8, Pallas kernels, call(): pl.pallas_call(kernel, out_shape=out_shape, in_specs=specs, out_specs=ins...  17.5 us
    all_to_all x1, waiting for transfers between devices, shards(): lax.all_to_all(outer, AXES, split_axis=0, concat_axis=0, tiled=True, axis...  8.25 us
    ppermute x4, waiting for transfers between devices, spread(): lax.ppermute(held, AXES, [(d, d ^ bit) for d in range(devices)])  8.22 us
    all_to_all x1, starting transfers between devices, shards(): left = lax.all_to_all(left, AXES, split_axis=0, concat_axis=0, tiled=True)  7.52 us
    all_to_all x1, starting transfers between devices, shards(): lax.all_to_all(outer, AXES, split_axis=0, concat_axis=0, tiled=True, axis...  6.55 us
    ppermute x7, starting transfers between devices, send(): lax.ppermute(block, AXES, [(d, d ^ offset ^ r) for d in range(devices)])  6.55 us
    ppermute x4, starting transfers between devices, spread(): lax.ppermute(held, AXES, [(d, d ^ bit) for d in range(devices)])  5.51 us
  transfers between devices with their start and end apart: 13, of which 11 were waited for; matrix products, arithmetic and copies ran while one was open for 0% of the time, Pallas kernels for 4%

profile of v15, /device:TPU:0, one launch (start us, length us, event | category | flops | bytes accessed | tf_op | source)
XLA Modules:
  0.0 91.4 jit_solution(6078196793479977866)
XLA Ops:
  0.7 3.6 %left.1 = bf16[16,16,3456]{2,1,0:T(8,128)(2,1)} custom-call(s32[1]{0:T(128)S(6)} %copy.16.refs_0_, bf16[12,192,128]{2,1,0:T(8,128)(2,1)} %refs_1_.4, f32[1,128]{1,0:T(1,128)} %bitcast.10, bf16[4,128,128]{2,1,0:T(8,128)(2,1)} %refs_3_.4), custom_call_target="tpu_custom_call" | custom-call | tf_op jit(solution)/shard_map/left/pallas_call | solution.py:43
  4.2 0.0 copy-start.1
  4.3 7.5 %all-to-all-start = ((bf16[16,16,3456]{2,1,0:T(8,128)(2,1)}), bf16[16,16,3456]{2,1,0:T(8,128)(2,1)S(1)}, u32[]{:S(2)}, u32[]{:S(2)}) async-start(bf16[16,16,3456]{2,1,0:T(8,128)(2,1)} %left.1), calls=%async_computation | async-start | bytes 3538944 | tf_op jit(solution)/shard_map/all_to_all | solution.py:415
  11.8 1.2 %right.1 = (bf16[16,2304]{1,0:T(8,128)(2,1)S(1)}, bf16[16,2304]{1,0:T(8,128)(2,1)S(1)}, bf16[16,2304]{1,0:T(8,128)(2,1)S(1)}, bf16[16,2304]{1,0:T(8,128)(2,1)S(1...) custom-call(s32[1]{0:T(128)S(6)} %copy.16.refs_0_, ...), custom_call_target="tpu_custom_call" | custom-call | tf_op jit(solution)/shard_map/right/pallas_call | solution.py:43
  13.1 0.5 collective-permute-start
  13.5 1.7 %collective-permute-start.1 = (bf16[16,2304]{1,0:T(8,128)(2,1)S(1)}, bf16[16,2304]{1,0:T(8,128)(2,1)S(1)}, u32[]{:S(2)}, u32[]{:S(2)}) collective-permute-start(bf16[16,2304]{1,0:T(8,128)(2,1)S(1)} %get-tuple-element.22), channel_id=1, source_target_pairs={{0,2},{1,3},{2,0},{3,1},{4,6},{5,7},{6,4},{7,5},{8,10},{9,11},{10,... | collective-permute-start | bytes 221192 | tf_op jit(solution)/shard_map/ppermute | solution.py:387
  15.2 1.7 %collective-permute-start.3 = (bf16[16,2304]{1,0:T(8,128)(2,1)S(1)}, bf16[16,2304]{1,0:T(8,128)(2,1)S(1)}, u32[]{:S(2)}, u32[]{:S(2)}) collective-permute-start(bf16[16,2304]{1,0:T(8,128)(2,1)S(1)} %get-tuple-element.24), channel_id=1, source_target_pairs={{0,4},{1,5},{2,6},{3,7},{4,0},{5,1},{6,2},{7,3},{8,12},{9,13},{10,... | collective-permute-start | bytes 221192 | tf_op jit(solution)/shard_map/ppermute | solution.py:387
  16.9 0.1 collective-permute-start.4
  17.0 2.6 %collective-permute-start.5 = (bf16[16,2304]{1,0:T(8,128)(2,1)S(1)}, bf16[16,2304]{1,0:T(8,128)(2,1)S(1)}, u32[]{:S(2)}, u32[]{:S(2)}) collective-permute-start(bf16[16,2304]{1,0:T(8,128)(2,1)S(1)} %get-tuple-element.26), channel_id=1, source_target_pairs={{0,6},{1,7},{2,4},{3,5},{4,2},{5,3},{6,0},{7,1},{8,14},{9,15},{10,... | collective-permute-start | bytes 221192 | tf_op jit(solution)/shard_map/ppermute | solution.py:387
  19.6 7.9 %collective-permute-done.1.refs_2_ = bf16[16,2304]{1,0:T(8,128)(2,1)S(1)} collective-permute-done((bf16[16,2304]{1,0:T(8,128)(2,1)S(1)}, bf16[16,2304]{1,0:T(8,128)(2,1)S(1)}, u32[]{:S(2)}, u32[]{:S(2)}) %collective-permute-start.1) | collective-permute-done | bytes 73760 | tf_op jit(solution)/shard_map/ppermute | solution.py:387
  27.5 0.6 collective-permute-done.2.refs_3_
  28.1 15.1 %collective-permute-done.3.refs_4_ = bf16[16,2304]{1,0:T(8,128)(2,1)S(1)} collective-permute-done((bf16[16,2304]{1,0:T(8,128)(2,1)S(1)}, bf16[16,2304]{1,0:T(8,128)(2,1)S(1)}, u32[]{:S(2)}, u32[]{:S(2)}) %collective-permute-start.3) | collective-permute-done | bytes 73760 | tf_op jit(solution)/shard_map/ppermute | solution.py:387
  43.3 1.6 %collective-permute-done.4.refs_5_ = bf16[16,2304]{1,0:T(8,128)(2,1)S(1)} collective-permute-done((bf16[16,2304]{1,0:T(8,128)(2,1)S(1)}, bf16[16,2304]{1,0:T(8,128)(2,1)S(1)}, u32[]{:S(2)}, u32[]{:S(2)}) %collective-permute-start.4) | collective-permute-done | bytes 73760 | tf_op jit(solution)/shard_map/ppermute | solution.py:387
  44.8 1.6 %collective-permute-done.5.refs_6_ = bf16[16,2304]{1,0:T(8,128)(2,1)S(1)} collective-permute-done((bf16[16,2304]{1,0:T(8,128)(2,1)S(1)}, bf16[16,2304]{1,0:T(8,128)(2,1)S(1)}, u32[]{:S(2)}, u32[]{:S(2)}) %collective-permute-start.5) | collective-permute-done | bytes 73760 | tf_op jit(solution)/shard_map/ppermute | solution.py:387
  46.4 3.4 %collective-permute-done.6.refs_7_ = bf16[16,2304]{1,0:T(8,128)(2,1)S(1)} collective-permute-done((bf16[16,2304]{1,0:T(8,128)(2,1)S(1)}, bf16[16,2304]{1,0:T(8,128)(2,1)S(1)}, u32[]{:S(2)}, u32[]{:S(2)}) %collective-permute-start.6) | collective-permute-done | bytes 73760 | tf_op jit(solution)/shard_map/ppermute | solution.py:387
  49.8 0.7 arrange.1.refs_1_
  50.5 2.4 %outer.1 = bf16[8,16,2304]{2,1,0:T(8,128)(2,1)} custom-call(bf16[16,16,3456]{2,1,0:T(8,128)(2,1)S(1)} %all-to-all-done.refs_0_.refs_6_, bf16[16,96,192]{2,1,0:T(8,128)(2,1)S(1)} %arrange.1.refs_1_), custom_call_target="tpu_custom_call" | custom-call | tf_op jit(solution)/shard_map/outer/pallas_call | solution.py:43
  53.0 6.6 %all-to-all-start.1 = ((bf16[8,16,2304]{2,1,0:T(8,128)(2,1)}), bf16[8,16,2304]{2,1,0:T(8,128)(2,1)S(1)}, u32[]{:S(2)}, u32[]{:S(2)}) async-start(bf16[8,16,2304]{2,1,0:T(8,128)(2,1)} %outer.1), calls=%async_computation.1 | async-start | bytes 1179648 | tf_op jit(solution)/shard_map/all_to_all | solution.py:441
  59.5 0.1 copy.15.refs_4_
  59.7 1.1 %gating.1.refs_0_ = bf16[12,192,128]{2,1,0:T(8,128)(2,1)S(1)} custom-call(bf16[16,16,3456]{2,1,0:T(8,128)(2,1)S(1)} %all-to-all-done.refs_0_.refs_6_, f32[1,128]{1,0:T(1,128)S(1)} %bitcast.12, bf16[128,128]{1,0:T(8,128)(2,1)S(1)} %copy-done.8), custom_call_target="tpu_custom_call" | custom-call | tf_op jit(solution)/shard_map/gating/pallas_call | solution.py:43
  60.8 8.2 %all-to-all-done.1.refs_5_ = bf16[8,16,2304]{2,1,0:T(8,128)(2,1)S(1)} async-done(((bf16[8,16,2304]{2,1,0:T(8,128)(2,1)}), bf16[8,16,2304]{2,1,0:T(8,128)(2,1)S(1)}, u32[]{:S(2)}, u32[]{:S(2)}) %all-to-all-start.1) | async-done | bytes 589856 | tf_op jit(solution)/shard_map/all_to_all | solution.py:441
  69.1 2.7 %update.1 = (bf16[12,192,128]{2,1,0:T(8,128)(2,1)S(1)}, bf16[12,192,128]{2,1,0:T(8,128)(2,1)S(1)}, bf16[24,384]{1,0:T(8,128)(2,1)S(1)}) custom-call(bf16[12,192,128]{2,1,0:T(8,128)(2,1)S(1)} %gating.1.refs_0_, f32[1,128]{1,0:T(1,128)S(1)} %bitcast.13, bf16[128,128]{1,0:T(8,128)(2,1)S(1)} %copy-done.2, f32[1,128]{1,0:T(1,128)S(1)} %bitcast.14, ...), custom_call_target="tpu_custom_call" | custom-call | tf_op jit(solution)/shard_map/update/pallas_call | solution.py:43
  71.8 2.2 %collective-permute-start.7 = (bf16[1,24,384]{2,1,0:T(8,128)(2,1)S(1)}, bf16[1,24,384]{2,1,0:T(8,128)(2,1)S(1)}, u32[]{:S(2)}, u32[]{:S(2)}) collective-permute-start(bf16[1,24,384]{2,1,0:T(8,128)(2,1)S(1)} %bitcast.5), channel_id=1, source_target_pairs={{0,8},{1,9},{2,10},{3,11},{4,12},{5,13},{6,14},{7,15},{8,0},{9,1},... | collective-permute-start | bytes 55304 | tf_op jit(solution)/shard_map/ppermute | solution.py:356
  74.0 2.5 %collective-permute-done.7.refs_8_ = bf16[1,24,384]{2,1,0:T(8,128)(2,1)S(1)} collective-permute-done((bf16[1,24,384]{2,1,0:T(8,128)(2,1)S(1)}, bf16[1,24,384]{2,1,0:T(8,128)(2,1)S(1)}, u32[]{:S(2)}, u32[]{:S(2)}) %collective-permute-start.7) | collective-permute-done | bytes 18464 | tf_op jit(solution)/shard_map/ppermute | solution.py:356
  76.5 1.5 %collective-permute-start.8 = (bf16[2,24,384]{2,1,0:T(8,128)(2,1)S(1)}, bf16[2,24,384]{2,1,0:T(8,128)(2,1)S(1)}, u32[]{:S(2)}, u32[]{:S(2)}) collective-permute-start(bf16[2,24,384]{2,1,0:T(8,128)(2,1)S(1)} %pad_maximum_fusion.2), channel_id=1, source_target_pairs={{0,4},{1,5},{2,6},{3,7},{4,0},{5,1},{6,2},{7,3},{8,12},{9,13},{10,... | collective-permute-start | bytes 110600 | tf_op jit(solution)/shard_map/ppermute | solution.py:356
  78.0 2.5 %collective-permute-done.8.refs_9_ = bf16[2,24,384]{2,1,0:T(8,128)(2,1)S(1)} collective-permute-done((bf16[2,24,384]{2,1,0:T(8,128)(2,1)S(1)}, bf16[2,24,384]{2,1,0:T(8,128)(2,1)S(1)}, u32[]{:S(2)}, u32[]{:S(2)}) %collective-permute-start.8) | collective-permute-done | bytes 36896 | tf_op jit(solution)/shard_map/ppermute | solution.py:356
  80.5 1.7 %collective-permute-start.9 = (bf16[4,24,384]{2,1,0:T(8,128)(2,1)S(1)}, bf16[4,24,384]{2,1,0:T(8,128)(2,1)S(1)}, u32[]{:S(2)}, u32[]{:S(2)}) collective-permute-start(bf16[4,24,384]{2,1,0:T(8,128)(2,1)S(1)} %pad_maximum_fusion.1), channel_id=1, source_target_pairs={{0,2},{1,3},{2,0},{3,1},{4,6},{5,7},{6,4},{7,5},{8,10},{9,11},{10,... | collective-permute-start | bytes 221192 | tf_op jit(solution)/shard_map/ppermute | solution.py:356
  82.2 2.7 %collective-permute-done.9.refs_10_ = bf16[4,24,384]{2,1,0:T(8,128)(2,1)S(1)} collective-permute-done((bf16[4,24,384]{2,1,0:T(8,128)(2,1)S(1)}, bf16[4,24,384]{2,1,0:T(8,128)(2,1)S(1)}, u32[]{:S(2)}, u32[]{:S(2)}) %collective-permute-start.9) | collective-permute-done | bytes 73760 | tf_op jit(solution)/shard_map/ppermute | solution.py:356
  85.0 0.1 collective-permute-start.10
  85.1 0.8 project.1
  85.9 0.5 collective-permute-done.10.refs_11_
  86.4 5.0 %attend.1 = bf16[12,192,128]{2,1,0:T(8,128)(2,1)} custom-call(s32[1]{0:T(128)S(6)} %copy.16.refs_0_, bf16[12,192,128]{2,1,0:T(8,128)(2,1)S(1)} %get-tuple-element.29.refs_1_, bf16[12,192,128]{2,1,0:T(8,128)(2,1)S(1)} %get-tuple-element.30.refs_2_, bf16[12,192,128]{2,1,0:T(8,128)(2,1)S(1)} %get-tuple-element.31.refs_3_, ...), custom_call_target="tpu_custom_call" | custom-call | tf_op jit(solution)/shard_map/attend/pallas_call | solution.py:43
  (32 shorter events, 0.1 us)
Async XLA Ops:
  4.2 7.6 %copy-start = (bf16[12,192,128]{2,1,0:T(8,128)(2,1)S(1)}, bf16[12,192,128]{2,1,0:T(8,128)(2,1)}, u32[]{:S(2)}) copy-start(bf16[12,192,128]{2,1,0:T(8,128)(2,1)} %refs_1_.4) | copy-start | bytes 1769476
  4.2 7.6 %copy-start.1 = (bf16[4,128,128]{2,1,0:T(8,128)(2,1)S(1)}, bf16[4,128,128]{2,1,0:T(8,128)(2,1)}, u32[]{:S(2)}) copy-start(bf16[4,128,128]{2,1,0:T(8,128)(2,1)} %refs_3_.4) | copy-start | bytes 393220
  4.2 7.6 %copy-start.9 = (f32[128]{0:T(128)S(1)}, f32[128]{0:T(128)}, u32[]{:S(2)}) copy-start(f32[128]{0:T(128)} %param.16) | copy-start | bytes 1540
  4.3 46.3 %all-to-all-start = ((bf16[16,16,3456]{2,1,0:T(8,128)(2,1)}), bf16[16,16,3456]{2,1,0:T(8,128)(2,1)S(1)}, u32[]{:S(2)}, u32[]{:S(2)}) async-start(bf16[16,16,3456]{2,1,0:T(8,128)(2,1)} %left.1), calls=%async_computation | async-start | bytes 3538944 | tf_op jit(solution)/shard_map/all_to_all | solution.py:415
  13.1 4.0 %collective-permute-start = (bf16[16,2304]{1,0:T(8,128)(2,1)S(1)}, bf16[16,2304]{1,0:T(8,128)(2,1)S(1)}, u32[]{:S(2)}, u32[]{:S(2)}) collective-permute-start(bf16[16,2304]{1,0:T(8,128)(2,1)S(1)} %get-tuple-element.21), channel_id=1, source_target_pairs={{0,1},{1,0},{2,3},{3,2},{4,5},{5,4},{6,7},{7,6},{8,9},{9,8},{10,11... | collective-permute-start | bytes 221192 | tf_op jit(solution)/shard_map/ppermute | solution.py:387
  13.5 14.0 %collective-permute-start.1 = (bf16[16,2304]{1,0:T(8,128)(2,1)S(1)}, bf16[16,2304]{1,0:T(8,128)(2,1)S(1)}, u32[]{:S(2)}, u32[]{:S(2)}) collective-permute-start(bf16[16,2304]{1,0:T(8,128)(2,1)S(1)} %get-tuple-element.22), channel_id=1, source_target_pairs={{0,2},{1,3},{2,0},{3,1},{4,6},{5,7},{6,4},{7,5},{8,10},{9,11},{10,... | collective-permute-start | bytes 221192 | tf_op jit(solution)/shard_map/ppermute | solution.py:387
  15.2 12.9 %collective-permute-start.2 = (bf16[16,2304]{1,0:T(8,128)(2,1)S(1)}, bf16[16,2304]{1,0:T(8,128)(2,1)S(1)}, u32[]{:S(2)}, u32[]{:S(2)}) collective-permute-start(bf16[16,2304]{1,0:T(8,128)(2,1)S(1)} %get-tuple-element.23), channel_id=1, source_target_pairs={{0,3},{1,2},{2,1},{3,0},{4,7},{5,6},{6,5},{7,4},{8,11},{9,10},{10,... | collective-permute-start | bytes 221192 | tf_op jit(solution)/shard_map/ppermute | solution.py:387
  15.2 28.0 %collective-permute-start.3 = (bf16[16,2304]{1,0:T(8,128)(2,1)S(1)}, bf16[16,2304]{1,0:T(8,128)(2,1)S(1)}, u32[]{:S(2)}, u32[]{:S(2)}) collective-permute-start(bf16[16,2304]{1,0:T(8,128)(2,1)S(1)} %get-tuple-element.24), channel_id=1, source_target_pairs={{0,4},{1,5},{2,6},{3,7},{4,0},{5,1},{6,2},{7,3},{8,12},{9,13},{10,... | collective-permute-start | bytes 221192 | tf_op jit(solution)/shard_map/ppermute | solution.py:387
  16.9 27.9 %collective-permute-start.4 = (bf16[16,2304]{1,0:T(8,128)(2,1)S(1)}, bf16[16,2304]{1,0:T(8,128)(2,1)S(1)}, u32[]{:S(2)}, u32[]{:S(2)}) collective-permute-start(bf16[16,2304]{1,0:T(8,128)(2,1)S(1)} %get-tuple-element.25), channel_id=1, source_target_pairs={{0,5},{1,4},{2,7},{3,6},{4,1},{5,0},{6,3},{7,2},{8,13},{9,12},{10,... | collective-permute-start | bytes 221192 | tf_op jit(solution)/shard_map/ppermute | solution.py:387
  17.0 29.4 %collective-permute-start.5 = (bf16[16,2304]{1,0:T(8,128)(2,1)S(1)}, bf16[16,2304]{1,0:T(8,128)(2,1)S(1)}, u32[]{:S(2)}, u32[]{:S(2)}) collective-permute-start(bf16[16,2304]{1,0:T(8,128)(2,1)S(1)} %get-tuple-element.26), channel_id=1, source_target_pairs={{0,6},{1,7},{2,4},{3,5},{4,2},{5,3},{6,0},{7,1},{8,14},{9,15},{10,... | collective-permute-start | bytes 221192 | tf_op jit(solution)/shard_map/ppermute | solution.py:387
  27.5 22.3 %collective-permute-start.6 = (bf16[16,2304]{1,0:T(8,128)(2,1)S(1)}, bf16[16,2304]{1,0:T(8,128)(2,1)S(1)}, u32[]{:S(2)}, u32[]{:S(2)}) collective-permute-start(bf16[16,2304]{1,0:T(8,128)(2,1)S(1)} %get-tuple-element.27), channel_id=1, source_target_pairs={{0,7},{1,6},{2,5},{3,4},{4,3},{5,2},{6,1},{7,0},{8,15},{9,14},{10,... | collective-permute-start | bytes 221192 | tf_op jit(solution)/shard_map/ppermute | solution.py:387
  50.5 9.0 %copy-start.12 = (bf16[128,4]{0,1:T(4,128)(2,1)S(1)}, bf16[128,4]{0,1:T(4,128)(2,1)}, u32[]{:S(2)}) copy-start(bf16[128,4]{0,1:T(4,128)(2,1)} %param.25) | copy-start | bytes 3076
  50.5 9.2 %copy-start.8 = (bf16[128,128]{1,0:T(8,128)(2,1)S(1)}, bf16[128,128]{1,0:T(8,128)(2,1)}, u32[]{:S(2)}) copy-start(bf16[128,128]{1,0:T(8,128)(2,1)} %refs_2_.3) | copy-start | bytes 98308
  53.0 16.1 %copy-start.2 = (bf16[128,128]{1,0:T(8,128)(2,1)S(1)}, bf16[128,128]{1,0:T(8,128)(2,1)}, u32[]{:S(2)}) copy-start(bf16[128,128]{1,0:T(8,128)(2,1)} %refs_2_.4) | copy-start | bytes 98308
  53.0 16.1 %copy-start.10 = (f32[128]{0:T(128)S(1)}, f32[128]{0:T(128)}, u32[]{:S(2)}) copy-start(f32[128]{0:T(128)} %param.19) | copy-start | bytes 1540
  53.0 16.1 %copy-start.11 = (f32[128]{0:T(128)S(1)}, f32[128]{0:T(128)}, u32[]{:S(2)}) copy-start(f32[128]{0:T(128)} %param.21) | copy-start | bytes 1540
  53.0 16.1 %all-to-all-start.1 = ((bf16[8,16,2304]{2,1,0:T(8,128)(2,1)}), bf16[8,16,2304]{2,1,0:T(8,128)(2,1)S(1)}, u32[]{:S(2)}, u32[]{:S(2)}) async-start(bf16[8,16,2304]{2,1,0:T(8,128)(2,1)} %outer.1), calls=%async_computation.1 | async-start | bytes 1179648 | tf_op jit(solution)/shard_map/all_to_all | solution.py:441
  69.1 16.0 %copy-start.4 = (bf16[128,128]{1,0:T(8,128)(2,1)S(1)}, bf16[128,128]{1,0:T(8,128)(2,1)}, u32[]{:S(2)}) copy-start(bf16[128,128]{1,0:T(8,128)(2,1)} %refs_1_.5) | copy-start | bytes 98308
  69.1 16.0 %copy-start.5 = (bf16[128,128]{1,0:T(8,128)(2,1)S(1)}, bf16[128,128]{1,0:T(8,128)(2,1)}, u32[]{:S(2)}) copy-start(bf16[128,128]{1,0:T(8,128)(2,1)} %refs_2_.5) | copy-start | bytes 98308
  69.1 16.0 %copy-start.6 = (bf16[128,128]{1,0:T(8,128)(2,1)S(1)}, bf16[128,128]{1,0:T(8,128)(2,1)}, u32[]{:S(2)}) copy-start(bf16[128,128]{1,0:T(8,128)(2,1)} %refs_3_.5) | copy-start | bytes 98308
  69.1 16.0 %copy-start.7 = (bf16[128,128]{1,0:T(8,128)(2,1)S(1)}, bf16[128,128]{1,0:T(8,128)(2,1)}, u32[]{:S(2)}) copy-start(bf16[128,128]{1,0:T(8,128)(2,1)} %refs_4_.2) | copy-start | bytes 98308
  69.1 17.3 %copy-start.3 = (bf16[128,128]{1,0:T(8,128)(2,1)S(1)}, bf16[128,128]{1,0:T(8,128)(2,1)}, u32[]{:S(2)}) copy-start(bf16[128,128]{1,0:T(8,128)(2,1)} %refs_6_.1) | copy-start | bytes 98308
  71.8 4.7 %collective-permute-start.7 = (bf16[1,24,384]{2,1,0:T(8,128)(2,1)S(1)}, bf16[1,24,384]{2,1,0:T(8,128)(2,1)S(1)}, u32[]{:S(2)}, u32[]{:S(2)}) collective-permute-start(bf16[1,24,384]{2,1,0:T(8,128)(2,1)S(1)} %bitcast.5), channel_id=1, source_target_pairs={{0,8},{1,9},{2,10},{3,11},{4,12},{5,13},{6,14},{7,15},{8,0},{9,1},... | collective-permute-start | bytes 55304 | tf_op jit(solution)/shard_map/ppermute | solution.py:356
  76.5 4.0 %collective-permute-start.8 = (bf16[2,24,384]{2,1,0:T(8,128)(2,1)S(1)}, bf16[2,24,384]{2,1,0:T(8,128)(2,1)S(1)}, u32[]{:S(2)}, u32[]{:S(2)}) collective-permute-start(bf16[2,24,384]{2,1,0:T(8,128)(2,1)S(1)} %pad_maximum_fusion.2), channel_id=1, source_target_pairs={{0,4},{1,5},{2,6},{3,7},{4,0},{5,1},{6,2},{7,3},{8,12},{9,13},{10,... | collective-permute-start | bytes 110600 | tf_op jit(solution)/shard_map/ppermute | solution.py:356
  80.5 4.4 %collective-permute-start.9 = (bf16[4,24,384]{2,1,0:T(8,128)(2,1)S(1)}, bf16[4,24,384]{2,1,0:T(8,128)(2,1)S(1)}, u32[]{:S(2)}, u32[]{:S(2)}) collective-permute-start(bf16[4,24,384]{2,1,0:T(8,128)(2,1)S(1)} %pad_maximum_fusion.1), channel_id=1, source_target_pairs={{0,2},{1,3},{2,0},{3,1},{4,6},{5,7},{6,4},{7,5},{8,10},{9,11},{10,... | collective-permute-start | bytes 221192 | tf_op jit(solution)/shard_map/ppermute | solution.py:356
  85.0 1.4 %collective-permute-start.10 = (bf16[8,24,384]{2,1,0:T(8,128)(2,1)S(1)}, bf16[8,24,384]{2,1,0:T(8,128)(2,1)S(1)}, u32[]{:S(2)}, u32[]{:S(2)}) collective-permute-start(bf16[8,24,384]{2,1,0:T(8,128)(2,1)S(1)} %pad_maximum_fusion), channel_id=1, source_target_pairs={{0,1},{1,0},{2,3},{3,2},{4,5},{5,4},{6,7},{7,6},{8,9},{9,8},{10,11... | collective-permute-start | bytes 442376 | tf_op jit(solution)/shard_map/ppermute | solution.py:356

commit v16 on v14

--- a/solution.py
+++ b/solution.py
@@ -34,12 +34,12 @@
     return lax.axis_index("row") * lax.axis_size("node") + lax.axis_index("node")
 
 
-def call(kernel, out_shape, args, scratch=(), smem=(), name=None, vmem=VMEM_BYTES):
+def call(kernel, out_shape, args, scratch=(), smem=(), name=None, vmem=VMEM_BYTES, away=False, cost=None):
     specs = [
         pl.BlockSpec(memory_space=pltpu.SMEM if n in smem else pltpu.VMEM) for n in range(len(args))
     ]
     single = not isinstance(out_shape, (list, tuple))
-    inside = pl.BlockSpec(memory_space=pltpu.VMEM)
+    inside = pl.BlockSpec(memory_space=pl.ANY if away else pltpu.VMEM)
     return pl.pallas_call(
         kernel,
         out_shape=out_shape,
@@ -48,6 +48,7 @@
         scratch_shapes=list(scratch),
         compiler_params=pltpu.CompilerParams(vmem_limit_bytes=vmem),
         name=name,
+        cost_estimate=cost,
     )(*args)
 
 
@@ -103,18 +104,11 @@
             )
 
 
-def left_kernel(sz, len_ref, x_ref, ln_ref, w_ref, out_ref, norm_ref, pair_ref):
-    cd, ch = sz.chans, sz.channels
+def left_kernel(sz, len_ref, x_ref, ln_ref, w_ref, out_ref, norm_ref):
+    ch = sz.channels
     gain = ln_ref[...]
     for row in range(sz.rows):
-        x = x_ref[row].astype(F32)
-        for d in range(sz.devices):
-            pair_ref[d, row * sz.rows : (row + 1) * sz.rows, :] = x[d * sz.rows : (d + 1) * sz.rows]
-        normalise(sz, row, x, gain, norm_ref)
-    for d in range(sz.devices):
-        for t in range(sz.block_tiles):
-            at = (sz.tiles + t) * LANES
-            out_ref[d, :, at : at + LANES] = pair_ref[d, t * cd : (t + 1) * cd, :].astype(BF16)
+        normalise(sz, row, x_ref[row].astype(F32), gain, norm_ref)
     r = lax.broadcasted_iota(jnp.int32, (ch, ch), 0)
     e = lax.broadcasted_iota(jnp.int32, (ch, ch), 1)
 
@@ -127,16 +121,33 @@
     project_edges(sz, len_ref[0], first, w_ref[0], w_ref[1], pick, norm_ref, store)
 
 
-def right_kernel(sz, len_ref, x_ref, ln_ref, w_ref, *refs):
-    near, norm_ref = refs[: sz.group], refs[sz.group]
+def right_kernel(sz, len_ref, x_ref, far_ref, ln_ref, w_ref, *refs):
+    near, (norm_ref, own_ref, far_rows_ref, pair_ref) = refs[: sz.group], refs[sz.group :]
     cd, ch = sz.chans, sz.channels
     gain = ln_ref[...]
+    me = position()
+    mine = me & (sz.group - 1)
+    upper = me >= sz.group
     for row in range(sz.rows):
-        normalise(sz, row, x_ref[row].astype(F32), gain, norm_ref)
-    me = position()
+        x = x_ref[row].astype(F32)
+        normalise(sz, row, x, gain, norm_ref)
+        rows = pl.ds(row * sz.columns, sz.columns)
+        own_ref[rows, :] = jnp.where(upper, x[sz.columns :], x[: sz.columns])
+        far_rows_ref[rows, :] = far_ref[row].astype(F32)
+    for base, wide_ref in enumerate((own_ref, far_rows_ref)):
+        for g in range(sz.group):
+            for row in range(sz.rows):
+                block = wide_ref[pl.ds(row * sz.columns + g * sz.rows, sz.rows), :]
+                pair_ref[base, g, row * sz.rows : (row + 1) * sz.rows, :] = block
+    for r in range(sz.group):
+        for base in range(2):
+            for t in range(sz.block_tiles):
+                at = (sz.tiles + base * sz.block_tiles + t) * LANES
+                block = pair_ref[base, mine ^ r, t * cd : (t + 1) * cd, :]
+                near[r][:, at : at + LANES] = block.astype(BF16)
     r = lax.broadcasted_iota(jnp.int32, (ch, ch), 0)
     e = lax.broadcasted_iota(jnp.int32, (ch, ch), 1)
-    pick = (((r // cd) ^ (me & (sz.group - 1))) * cd + r % cd == e).astype(BF16)
+    pick = (((r // cd) ^ mine) * cd + r % cd == e).astype(BF16)
 
     def store(g, lanes, edge):
         near[g][:, lanes] = edge
@@ -206,16 +217,29 @@
             out_ref[g, :, tile * LANES : (tile + 1) * LANES] = block.astype(BF16)
 
 
-def update_kernel(
-    sz, lnp_ref, gate_ref, lnh_ref, tri_ref, lna_ref, biasw_ref, sums_ref, pair_ref,
-    first_ref, col_ref, bias_ref, cols_ref, brow_ref,
-):
-    n, w, half, ch, cd = sz.crop, sz.whole, sz.half, sz.channels, sz.chans
-    for s in range(sz.devices):
-        for t in range(sz.block_tiles):
-            at = (sz.tiles + t) * LANES
-            rows = pl.ds(s * sz.block + t * cd, cd)
-            cols_ref[rows, :] = pair_ref[s, :, at : at + LANES].astype(F32)
+def take_columns(sz, near, cols_ref):
+    cd, me = sz.chans, position()
+    for r in range(sz.group):
+        for base, owner in ((0, me ^ r), (1, me ^ (sz.group + r))):
+            for t in range(sz.block_tiles):
+                at = (sz.tiles + base * sz.block_tiles + t) * LANES
+                rows = pl.ds(pl.multiple_of(owner * sz.block + t * cd, 8), cd)
+                cols_ref[rows, :] = near[r][:, at : at + LANES].astype(F32)
+
+
+def gating_kernel(sz, lnp_ref, gate_ref, *refs):
+    near, (gating_ref, cols_ref) = refs[: sz.group], refs[sz.group :]
+    take_columns(sz, near, cols_ref)
+    for j in range(sz.rows):
+        x = cols_ref[pl.ds(j, sz.crop, stride=sz.rows), :]
+        normed = norm_last(x, lnp_ref[...]).astype(BF16)
+        gating_ref[j] = sigmoid(dot(normed, gate_ref[...], 1, 0)).astype(BF16)
+
+
+def update_kernel(sz, gating_ref, lnh_ref, tri_ref, lna_ref, biasw_ref, sums_ref, *refs):
+    near, (first_ref, col_ref, bias_ref, cols_ref, brow_ref) = refs[: sz.group], refs[sz.group :]
+    n, w, half, ch = sz.crop, sz.whole, sz.half, sz.channels
+    take_columns(sz, near, cols_ref)
     gain_h = jnp.transpose(jnp.broadcast_to(lnh_ref[...], (ch, ch)))
     tri = tri_ref[...]
 
@@ -235,9 +259,7 @@
             parts.append(rest[q][h * sz.rest : (h + 1) * sz.rest])
         change = jnp.concatenate(parts, axis=0) if len(parts) > 1 else parts[0]
         x = cols_ref[pl.ds(j, n, stride=sz.rows), :]
-        normed = norm_last(x, lnp_ref[...]).astype(BF16)
-        gating = sigmoid(dot(normed, gate_ref[...], 1, 0))
-        first = (x + gating * change).astype(BF16)
+        first = (x + gating_ref[j].astype(F32) * change).astype(BF16)
         first_ref[j] = first
         col = norm_last(first.astype(F32), lna_ref[...]).astype(BF16)
         col_ref[j] = col
@@ -359,26 +381,34 @@
             for r, block in enumerate(blocks)
         ]
 
+    upper = (lax.axis_index(AXES) >= g).astype(jnp.int32)
+    far = lax.ppermute(
+        lax.dynamic_slice_in_dim(pair_rep, (1 - upper) * sz.columns, sz.columns, 1),
+        AXES,
+        [(d, d ^ g) for d in range(devices)],
+    )
     left = call(
         bound(left_kernel),
-        slab(t + bt, devices),
+        slab(t, devices),
         (length, pair_rep, ln_pair[None], tri_in),
-        scratch=[
-            pltpu.VMEM((rows * crop, ch), BF16),
-            pltpu.VMEM((devices, bt * cd, ch), F32),
-        ],
+        scratch=[pltpu.VMEM((rows * crop, ch), BF16)],
         smem=(0,),
         name="left",
         vmem=VMEM_MOST,
     )
     others = call(
         bound(right_kernel),
-        [slab(t)] * g,
-        (length, pair_rep, ln_pair[None], tri_in),
-        scratch=[pltpu.VMEM((rows * crop, ch), BF16)],
+        [slab(t + 2 * bt)] * g,
+        (length, pair_rep, far, ln_pair[None], tri_in),
+        scratch=[
+            pltpu.VMEM((rows * crop, ch), BF16),
+            pltpu.VMEM((rows * sz.columns, ch), F32),
+            pltpu.VMEM((rows * sz.columns, ch), F32),
+            pltpu.VMEM((2, g, bt * cd, ch), F32),
+        ],
         smem=(0,),
         name="right",
-        vmem=VMEM_MOST,
+        cost=pl.CostEstimate(flops=10**11, bytes_accessed=10**6, transcendentals=0),
     )
     left = lax.all_to_all(left, AXES, split_axis=0, concat_axis=0, tiled=True)
     near = send(others, 0)
@@ -410,6 +440,13 @@
         outer, AXES, split_axis=0, concat_axis=0, tiled=True,
         axis_index_groups=[list(range(g)), list(range(g, devices))],
     )
+    gating = call(
+        bound(gating_kernel),
+        shape((rows, n, ch), BF16),
+        (ln_pair[None], tri_gate, *near),
+        scratch=[pltpu.VMEM((devices * sz.block + cd, ch), F32)],
+        name="gating",
+    )
     first, col, bias = call(
         bound(update_kernel),
         [
@@ -418,8 +455,7 @@
             shape((rows * heads // 2, 2 * n), BF16),
         ],
         (
-            ln_pair[None], tri_gate, ln_hidden[None], tri_out, ln_att[None], att_bias,
-            sums, left,
+            gating, ln_hidden[None], tri_out, ln_att[None], att_bias, sums, *near,
         ),
         scratch=[
             pltpu.VMEM((devices * sz.block + cd, ch), F32),

time: 92.1 us -> 92 us (level)
  Pallas kernels: 18.9 us -> 17.5 us
  waiting for transfers between devices: 46 us -> 47.2 us
    ppermute x0 -> x1, waiting for transfers between devices: none -> 12.5 us  [shards(): lax.ppermute(lax.dynamic_slice_in_dim(pair_rep, (1 - upper) * sz.columns,...]
    ppermute x7, waiting for transfers between devices: 28.4 us -> 19.3 us  [send(): lax.ppermute(block, AXES, [(d, d ^ offset ^ r) for d in range(devices)])]
    ppermute x0 -> x1, starting transfers between devices: none -> 4.1 us  [shards(): lax.ppermute(lax.dynamic_slice_in_dim(pair_rep, (1 - upper) * sz.columns,...]
    all_to_all x1, starting transfers between devices: 7.38 us -> 4.04 us  [shards(): left = lax.all_to_all(left, AXES, split_axis=0, concat_axis=0, tiled=True)]
    ppermute x4, starting transfers between devices: 5.5 us -> 8.24 us  [spread(): lax.ppermute(held, AXES, [(d, d ^ bit) for d in range(devices)])]
    ppermute x7, starting transfers between devices: 6.48 us -> 4.47 us  [send(): lax.ppermute(block, AXES, [(d, d ^ offset ^ r) for d in range(devices)])]
    all_to_all x1, starting transfers between devices: 5.48 us -> 3.85 us  [shards(): lax.all_to_all(outer, AXES, split_axis=0, concat_axis=0, tiled=True, axis...]
    all_to_all x1, waiting for transfers between devices: 9.36 us -> 7.91 us  [shards(): lax.all_to_all(outer, AXES, split_axis=0, concat_axis=0, tiled=True, axis...]
  transfers between devices with their start and end apart: 13 -> 14, of which waited for: 11 -> 11; matrix products, arithmetic and copies ran while one was open for 0% -> 0% of each run, Pallas kernels for 5% -> 8%
where the time goes in v16:
time: 92 us; the launch traced here: 91.6 us
  waiting for transfers between devices  47.2 us (51%)
  starting transfers between devices  24.7 us (27%)
  Pallas kernels  17.5 us (19%)
  local copies, waits for them, and re-layouts  1.18 us (1%)
    ppermute x7, waiting for transfers between devices, send(): lax.ppermute(block, AXES, [(d, d ^ offset ^ r) for d in range(devices)])  19.3 us
    pallas_call x8, Pallas kernels, call(): pl.pallas_call(kernel, out_shape=out_shape, in_specs=specs, out_specs=ins...  17.5 us
    ppermute x1, waiting for transfers between devices, shards(): lax.ppermute(lax.dynamic_slice_in_dim(pair_rep, (1 - upper) * sz.columns,...  12.5 us
    ppermute x4, starting transfers between devices, spread(): lax.ppermute(held, AXES, [(d, d ^ bit) for d in range(devices)])  8.24 us
    all_to_all x1, waiting for transfers between devices, shards(): lax.all_to_all(outer, AXES, split_axis=0, concat_axis=0, tiled=True, axis...  7.91 us
    ppermute x4, waiting for transfers between devices, spread(): lax.ppermute(held, AXES, [(d, d ^ bit) for d in range(devices)])  7.47 us
    ppermute x7, starting transfers between devices, send(): lax.ppermute(block, AXES, [(d, d ^ offset ^ r) for d in range(devices)])  4.47 us
    ppermute x1, starting transfers between devices, shards(): lax.ppermute(lax.dynamic_slice_in_dim(pair_rep, (1 - upper) * sz.columns,...  4.1 us
  transfers between devices with their start and end apart: 14, of which 11 were waited for; matrix products, arithmetic and copies ran while one was open for 0% of the time, Pallas kernels for 8%

profile of v16, /device:TPU:0, one launch (start us, length us, event | category | flops | bytes accessed | tf_op | source)
XLA Modules:
  0.0 91.6 jit_solution(4683977045302609242)
XLA Ops:
  0.0 1.0 %constant_dynamic-slice_fusion = bf16[12,96,128]{2,1,0:T(8,128)(2,1)S(1)} fusion(bf16[12,192,128]{2,1,0:T(8,128)(2,1)} %refs_1_.6, s32[]{:T(128)S(6)} %select_n.3), kind=kLoop, calls=%fused_computation.3 | loop fusion | bytes 589828 | tf_op jit(solution)/shard_map/dynamic_slice | solution.py:386
  1.0 4.1 %collective-permute-start = (bf16[12,96,128]{2,1,0:T(8,128)(2,1)S(1)}, bf16[12,96,128]{2,1,0:T(8,128)(2,1)S(1)}, u32[]{:S(2)}, u32[]{:S(2)}) collective-permute-start(bf16[12,96,128]{2,1,0:T(8,128)(2,1)S(1)} %constant_dynamic-slice_fusion), channel_id=1, source_target_pairs={{0,8},{1,9},{2,10},{3,11},{4,12},{5,13},{6,14},{7,15},{8,0},{9,1},... | collective-permute-start | bytes 884744 | tf_op jit(solution)/shard_map/ppermute | solution.py:385
  5.7 3.4 %left.1 = bf16[16,16,2304]{2,1,0:T(8,128)(2,1)} custom-call(s32[1]{0:T(128)S(6)} %copy.16.refs_0_, bf16[12,192,128]{2,1,0:T(8,128)(2,1)} %refs_1_.6, f32[1,128]{1,0:T(1,128)} %bitcast.10, bf16[4,128,128]{2,1,0:T(8,128)(2,1)} %refs_3_.2), custom_call_target="tpu_custom_call" | custom-call | tf_op jit(solution)/shard_map/left/pallas_call | solution.py:43
  9.1 4.0 %all-to-all-start = ((bf16[16,16,2304]{2,1,0:T(8,128)(2,1)}), bf16[16,16,2304]{2,1,0:T(8,128)(2,1)S(1)}, u32[]{:S(2)}, u32[]{:S(2)}) async-start(bf16[16,16,2304]{2,1,0:T(8,128)(2,1)} %left.1), calls=%async_computation | async-start | bytes 2359296 | tf_op jit(solution)/shard_map/all_to_all | solution.py:413
  13.2 12.5 %collective-permute-done.refs_2_ = bf16[12,96,128]{2,1,0:T(8,128)(2,1)S(1)} collective-permute-done((bf16[12,96,128]{2,1,0:T(8,128)(2,1)S(1)}, bf16[12,96,128]{2,1,0:T(8,128)(2,1)S(1)}, u32[]{:S(2)}, u32[]{:S(2)}) %collective-permute-start) | collective-permute-done | bytes 294944 | tf_op jit(solution)/shard_map/ppermute | solution.py:385
  25.7 1.4 %right.1 = (bf16[16,4608]{1,0:T(8,128)(2,1)S(1)}, bf16[16,4608]{1,0:T(8,128)(2,1)S(1)}, bf16[16,4608]{1,0:T(8,128)(2,1)S(1)}, bf16[16,4608]{1,0:T(8,128)(2,1)S(1...) custom-call(s32[1]{0:T(128)S(6)} %copy.16.refs_0_, ...), custom_call_target="tpu_custom_call" | custom-call | flops 99999997952 | bytes 1000000 | tf_op jit(solution)/shard_map/right/pallas_call | solution.py:43
  27.2 0.4 collective-permute-start.2
  27.6 1.5 %collective-permute-start.3 = (bf16[16,4608]{1,0:T(8,128)(2,1)S(1)}, bf16[16,4608]{1,0:T(8,128)(2,1)S(1)}, u32[]{:S(2)}, u32[]{:S(2)}) collective-permute-start(bf16[16,4608]{1,0:T(8,128)(2,1)S(1)} %get-tuple-element.23), channel_id=1, source_target_pairs={{0,3},{1,2},{2,1},{3,0},{4,7},{5,6},{6,5},{7,4},{8,11},{9,10},{10,... | collective-permute-start | bytes 442376 | tf_op jit(solution)/shard_map/ppermute | solution.py:380
  29.1 1.7 %collective-permute-start.5 = (bf16[16,4608]{1,0:T(8,128)(2,1)S(1)}, bf16[16,4608]{1,0:T(8,128)(2,1)S(1)}, u32[]{:S(2)}, u32[]{:S(2)}) collective-permute-start(bf16[16,4608]{1,0:T(8,128)(2,1)S(1)} %get-tuple-element.25), channel_id=1, source_target_pairs={{0,5},{1,4},{2,7},{3,6},{4,1},{5,0},{6,3},{7,2},{8,13},{9,12},{10,... | collective-permute-start | bytes 442376 | tf_op jit(solution)/shard_map/ppermute | solution.py:380
  30.8 0.8 collective-permute-start.6
  31.6 3.5 %collective-permute-done.2.refs_4_.refs_2_.refs_8_ = bf16[16,4608]{1,0:T(8,128)(2,1)S(1)} collective-permute-done((bf16[16,4608]{1,0:T(8,128)(2,1)S(1)}, bf16[16,4608]{1,0:T(8,128)(2,1)S(1)}, u32[]{:S(2)}, u32[]{:S(2)}) %collective-permute-start.2) | collective-permute-done | bytes 147488 | tf_op jit(solution)/shard_map/ppermute | solution.py:380
  35.1 4.4 %collective-permute-done.3.refs_5_.refs_3_.refs_9_ = bf16[16,4608]{1,0:T(8,128)(2,1)S(1)} collective-permute-done((bf16[16,4608]{1,0:T(8,128)(2,1)S(1)}, bf16[16,4608]{1,0:T(8,128)(2,1)S(1)}, u32[]{:S(2)}, u32[]{:S(2)}) %collective-permute-start.3) | collective-permute-done | bytes 147488 | tf_op jit(solution)/shard_map/ppermute | solution.py:380
  39.6 4.1 %collective-permute-done.5.refs_7_.refs_5_.refs_11_ = bf16[16,4608]{1,0:T(8,128)(2,1)S(1)} collective-permute-done((bf16[16,4608]{1,0:T(8,128)(2,1)S(1)}, bf16[16,4608]{1,0:T(8,128)(2,1)S(1)}, u32[]{:S(2)}, u32[]{:S(2)}) %collective-permute-start.5) | collective-permute-done | bytes 147488 | tf_op jit(solution)/shard_map/ppermute | solution.py:380
  43.7 4.2 %collective-permute-done.6.refs_8_.refs_6_.refs_12_ = bf16[16,4608]{1,0:T(8,128)(2,1)S(1)} collective-permute-done((bf16[16,4608]{1,0:T(8,128)(2,1)S(1)}, bf16[16,4608]{1,0:T(8,128)(2,1)S(1)}, u32[]{:S(2)}, u32[]{:S(2)}) %collective-permute-start.6) | collective-permute-done | bytes 147488 | tf_op jit(solution)/shard_map/ppermute | solution.py:380
  47.9 3.1 %collective-permute-done.7.refs_9_.refs_7_.refs_13_ = bf16[16,4608]{1,0:T(8,128)(2,1)S(1)} collective-permute-done((bf16[16,4608]{1,0:T(8,128)(2,1)S(1)}, bf16[16,4608]{1,0:T(8,128)(2,1)S(1)}, u32[]{:S(2)}, u32[]{:S(2)}) %collective-permute-start.7) | collective-permute-done | bytes 147488 | tf_op jit(solution)/shard_map/ppermute | solution.py:380
  51.0 0.7 arrange.1.refs_1_
  51.7 2.5 %outer.1 = bf16[8,16,2304]{2,1,0:T(8,128)(2,1)} custom-call(bf16[16,16,2304]{2,1,0:T(8,128)(2,1)S(1)} %all-to-all-done.refs_0_, bf16[16,96,192]{2,1,0:T(8,128)(2,1)S(1)} %arrange.1.refs_1_), custom_call_target="tpu_custom_call" | custom-call | tf_op jit(solution)/shard_map/outer/pallas_call | solution.py:43
  54.2 3.9 %all-to-all-start.1 = ((bf16[8,16,2304]{2,1,0:T(8,128)(2,1)}), bf16[8,16,2304]{2,1,0:T(8,128)(2,1)S(1)}, u32[]{:S(2)}, u32[]{:S(2)}) async-start(bf16[8,16,2304]{2,1,0:T(8,128)(2,1)} %outer.1), calls=%async_computation.1 | async-start | bytes 1179648 | tf_op jit(solution)/shard_map/all_to_all | solution.py:439
  58.1 0.1 copy.15.refs_4_
  58.2 1.2 %gating.1.refs_0_ = bf16[12,192,128]{2,1,0:T(8,128)(2,1)S(1)} custom-call(f32[1,128]{1,0:T(1,128)S(1)} %bitcast.12, bf16[128,128]{1,0:T(8,128)(2,1)S(1)} %copy-done.2, bf16[16,4608]{1,0:T(8,128)(2,1)S(1)} %get-tuple-element.20.refs_2_.refs_0_.refs_6_, bf16[16,4608]{1,0:T(8,128)(2,1)S(1)} %collective-permute-done.1.refs_3_.refs_1_.refs_7_, ...), custom_call_target="tpu_custom_call" | custom-call | tf_op jit(solution)/shard_map/gating/pallas_call | solution.py:43
  59.4 7.9 %all-to-all-done.1.refs_5_ = bf16[8,16,2304]{2,1,0:T(8,128)(2,1)S(1)} async-done(((bf16[8,16,2304]{2,1,0:T(8,128)(2,1)}), bf16[8,16,2304]{2,1,0:T(8,128)(2,1)S(1)}, u32[]{:S(2)}, u32[]{:S(2)}) %all-to-all-start.1) | async-done | bytes 589856 | tf_op jit(solution)/shard_map/all_to_all | solution.py:439
  67.4 2.7 %update.1 = (bf16[12,192,128]{2,1,0:T(8,128)(2,1)S(1)}, bf16[12,192,128]{2,1,0:T(8,128)(2,1)S(1)}, bf16[24,384]{1,0:T(8,128)(2,1)S(1)}) custom-call(bf16[12,192,128]{2,1,0:T(8,128)(2,1)S(1)} %gating.1.refs_0_, f32[1,128]{1,0:T(1,128)S(1)} %bitcast.13, bf16[128,128]{1,0:T(8,128)(2,1)S(1)} %copy-done.3, f32[1,128]{1,0:T(1,128)S(1)} %bitcast.14, ...), custom_call_target="tpu_custom_call" | custom-call | tf_op jit(solution)/shard_map/update/pallas_call | solution.py:43
  70.1 4.9 %collective-permute-start.8 = (bf16[1,24,384]{2,1,0:T(8,128)(2,1)S(1)}, bf16[1,24,384]{2,1,0:T(8,128)(2,1)S(1)}, u32[]{:S(2)}, u32[]{:S(2)}) collective-permute-start(bf16[1,24,384]{2,1,0:T(8,128)(2,1)S(1)} %bitcast.5), channel_id=1, source_target_pairs={{0,8},{1,9},{2,10},{3,11},{4,12},{5,13},{6,14},{7,15},{8,0},{9,1},... | collective-permute-start | bytes 55304 | tf_op jit(solution)/shard_map/ppermute | solution.py:349
  75.0 1.7 %collective-permute-done.8.refs_8_ = bf16[1,24,384]{2,1,0:T(8,128)(2,1)S(1)} collective-permute-done((bf16[1,24,384]{2,1,0:T(8,128)(2,1)S(1)}, bf16[1,24,384]{2,1,0:T(8,128)(2,1)S(1)}, u32[]{:S(2)}, u32[]{:S(2)}) %collective-permute-start.8) | collective-permute-done | bytes 18464 | tf_op jit(solution)/shard_map/ppermute | solution.py:349
  76.7 1.5 %collective-permute-start.9 = (bf16[2,24,384]{2,1,0:T(8,128)(2,1)S(1)}, bf16[2,24,384]{2,1,0:T(8,128)(2,1)S(1)}, u32[]{:S(2)}, u32[]{:S(2)}) collective-permute-start(bf16[2,24,384]{2,1,0:T(8,128)(2,1)S(1)} %pad_maximum_fusion.2), channel_id=1, source_target_pairs={{0,4},{1,5},{2,6},{3,7},{4,0},{5,1},{6,2},{7,3},{8,12},{9,13},{10,... | collective-permute-start | bytes 110600 | tf_op jit(solution)/shard_map/ppermute | solution.py:349
  78.3 2.5 %collective-permute-done.9.refs_9_ = bf16[2,24,384]{2,1,0:T(8,128)(2,1)S(1)} collective-permute-done((bf16[2,24,384]{2,1,0:T(8,128)(2,1)S(1)}, bf16[2,24,384]{2,1,0:T(8,128)(2,1)S(1)}, u32[]{:S(2)}, u32[]{:S(2)}) %collective-permute-start.9) | collective-permute-done | bytes 36896 | tf_op jit(solution)/shard_map/ppermute | solution.py:349
  80.8 1.7 %collective-permute-start.10 = (bf16[4,24,384]{2,1,0:T(8,128)(2,1)S(1)}, bf16[4,24,384]{2,1,0:T(8,128)(2,1)S(1)}, u32[]{:S(2)}, u32[]{:S(2)}) collective-permute-start(bf16[4,24,384]{2,1,0:T(8,128)(2,1)S(1)} %pad_maximum_fusion.1), channel_id=1, source_target_pairs={{0,2},{1,3},{2,0},{3,1},{4,6},{5,7},{6,4},{7,5},{8,10},{9,11},{10,... | collective-permute-start | bytes 221192 | tf_op jit(solution)/shard_map/ppermute | solution.py:349
  82.5 2.7 %collective-permute-done.10.refs_10_ = bf16[4,24,384]{2,1,0:T(8,128)(2,1)S(1)} collective-permute-done((bf16[4,24,384]{2,1,0:T(8,128)(2,1)S(1)}, bf16[4,24,384]{2,1,0:T(8,128)(2,1)S(1)}, u32[]{:S(2)}, u32[]{:S(2)}) %collective-permute-start.10) | collective-permute-done | bytes 73760 | tf_op jit(solution)/shard_map/ppermute | solution.py:349
  85.2 0.1 collective-permute-start.11
  85.3 0.8 project.1
  86.1 0.5 collective-permute-done.11.refs_11_
  86.7 4.9 %attend.1 = bf16[12,192,128]{2,1,0:T(8,128)(2,1)} custom-call(s32[1]{0:T(128)S(6)} %copy.16.refs_0_, bf16[12,192,128]{2,1,0:T(8,128)(2,1)S(1)} %get-tuple-element.29.refs_1_, bf16[12,192,128]{2,1,0:T(8,128)(2,1)S(1)} %get-tuple-element.30.refs_2_, bf16[12,192,128]{2,1,0:T(8,128)(2,1)S(1)} %get-tuple-element.31.refs_3_, ...), custom_call_target="tpu_custom_call" | custom-call | tf_op jit(solution)/shard_map/attend/pallas_call | solution.py:43
  (35 shorter events, 0.2 us)
Async XLA Ops:
  1.0 24.7 %collective-permute-start = (bf16[12,96,128]{2,1,0:T(8,128)(2,1)S(1)}, bf16[12,96,128]{2,1,0:T(8,128)(2,1)S(1)}, u32[]{:S(2)}, u32[]{:S(2)}) collective-permute-start(bf16[12,96,128]{2,1,0:T(8,128)(2,1)S(1)} %constant_dynamic-slice_fusion), channel_id=1, source_target_pairs={{0,8},{1,9},{2,10},{3,11},{4,12},{5,13},{6,14},{7,15},{8,0},{9,1},... | collective-permute-start | bytes 884744 | tf_op jit(solution)/shard_map/ppermute | solution.py:385
  9.1 16.6 %copy-start = (bf16[12,192,128]{2,1,0:T(8,128)(2,1)S(1)}, bf16[12,192,128]{2,1,0:T(8,128)(2,1)}, u32[]{:S(2)}) copy-start(bf16[12,192,128]{2,1,0:T(8,128)(2,1)} %refs_1_.6) | copy-start | bytes 1769476
  9.1 16.6 %copy-start.1 = (bf16[4,128,128]{2,1,0:T(8,128)(2,1)S(1)}, bf16[4,128,128]{2,1,0:T(8,128)(2,1)}, u32[]{:S(2)}) copy-start(bf16[4,128,128]{2,1,0:T(8,128)(2,1)} %refs_3_.2) | copy-start | bytes 393220
  9.1 16.6 %copy-start.9 = (f32[128]{0:T(128)S(1)}, f32[128]{0:T(128)}, u32[]{:S(2)}) copy-start(f32[128]{0:T(128)} %param.16) | copy-start | bytes 1540
  9.1 42.6 %all-to-all-start = ((bf16[16,16,2304]{2,1,0:T(8,128)(2,1)}), bf16[16,16,2304]{2,1,0:T(8,128)(2,1)S(1)}, u32[]{:S(2)}, u32[]{:S(2)}) async-start(bf16[16,16,2304]{2,1,0:T(8,128)(2,1)} %left.1), calls=%async_computation | async-start | bytes 2359296 | tf_op jit(solution)/shard_map/all_to_all | solution.py:413
  27.2 3.6 %collective-permute-start.1 = (bf16[16,4608]{1,0:T(8,128)(2,1)S(1)}, bf16[16,4608]{1,0:T(8,128)(2,1)S(1)}, u32[]{:S(2)}, u32[]{:S(2)}) collective-permute-start(bf16[16,4608]{1,0:T(8,128)(2,1)S(1)} %get-tuple-element.21), channel_id=1, source_target_pairs={{0,1},{1,0},{2,3},{3,2},{4,5},{5,4},{6,7},{7,6},{8,9},{9,8},{10,11... | collective-permute-start | bytes 442376 | tf_op jit(solution)/shard_map/ppermute | solution.py:380
  27.2 7.9 %collective-permute-start.2 = (bf16[16,4608]{1,0:T(8,128)(2,1)S(1)}, bf16[16,4608]{1,0:T(8,128)(2,1)S(1)}, u32[]{:S(2)}, u32[]{:S(2)}) collective-permute-start(bf16[16,4608]{1,0:T(8,128)(2,1)S(1)} %get-tuple-element.22), channel_id=1, source_target_pairs={{0,2},{1,3},{2,0},{3,1},{4,6},{5,7},{6,4},{7,5},{8,10},{9,11},{10,... | collective-permute-start | bytes 442376 | tf_op jit(solution)/shard_map/ppermute | solution.py:380
  27.6 12.0 %collective-permute-start.3 = (bf16[16,4608]{1,0:T(8,128)(2,1)S(1)}, bf16[16,4608]{1,0:T(8,128)(2,1)S(1)}, u32[]{:S(2)}, u32[]{:S(2)}) collective-permute-start(bf16[16,4608]{1,0:T(8,128)(2,1)S(1)} %get-tuple-element.23), channel_id=1, source_target_pairs={{0,3},{1,2},{2,1},{3,0},{4,7},{5,6},{6,5},{7,4},{8,11},{9,10},{10,... | collective-permute-start | bytes 442376 | tf_op jit(solution)/shard_map/ppermute | solution.py:380
  29.1 10.5 %collective-permute-start.4 = (bf16[16,4608]{1,0:T(8,128)(2,1)S(1)}, bf16[16,4608]{1,0:T(8,128)(2,1)S(1)}, u32[]{:S(2)}, u32[]{:S(2)}) collective-permute-start(bf16[16,4608]{1,0:T(8,128)(2,1)S(1)} %get-tuple-element.24), channel_id=1, source_target_pairs={{0,4},{1,5},{2,6},{3,7},{4,0},{5,1},{6,2},{7,3},{8,12},{9,13},{10,... | collective-permute-start | bytes 442376 | tf_op jit(solution)/shard_map/ppermute | solution.py:380
  29.1 14.6 %collective-permute-start.5 = (bf16[16,4608]{1,0:T(8,128)(2,1)S(1)}, bf16[16,4608]{1,0:T(8,128)(2,1)S(1)}, u32[]{:S(2)}, u32[]{:S(2)}) collective-permute-start(bf16[16,4608]{1,0:T(8,128)(2,1)S(1)} %get-tuple-element.25), channel_id=1, source_target_pairs={{0,5},{1,4},{2,7},{3,6},{4,1},{5,0},{6,3},{7,2},{8,13},{9,12},{10,... | collective-permute-start | bytes 442376 | tf_op jit(solution)/shard_map/ppermute | solution.py:380
  30.8 17.1 %collective-permute-start.6 = (bf16[16,4608]{1,0:T(8,128)(2,1)S(1)}, bf16[16,4608]{1,0:T(8,128)(2,1)S(1)}, u32[]{:S(2)}, u32[]{:S(2)}) collective-permute-start(bf16[16,4608]{1,0:T(8,128)(2,1)S(1)} %get-tuple-element.26), channel_id=1, source_target_pairs={{0,6},{1,7},{2,4},{3,5},{4,2},{5,3},{6,0},{7,1},{8,14},{9,15},{10,... | collective-permute-start | bytes 442376 | tf_op jit(solution)/shard_map/ppermute | solution.py:380
  35.1 15.8 %collective-permute-start.7 = (bf16[16,4608]{1,0:T(8,128)(2,1)S(1)}, bf16[16,4608]{1,0:T(8,128)(2,1)S(1)}, u32[]{:S(2)}, u32[]{:S(2)}) collective-permute-start(bf16[16,4608]{1,0:T(8,128)(2,1)S(1)} %get-tuple-element.27), channel_id=1, source_target_pairs={{0,7},{1,6},{2,5},{3,4},{4,3},{5,2},{6,1},{7,0},{8,15},{9,14},{10,... | collective-permute-start | bytes 442376 | tf_op jit(solution)/shard_map/ppermute | solution.py:380
  54.2 3.9 %copy-start.12 = (bf16[128,4]{0,1:T(4,128)(2,1)S(1)}, bf16[128,4]{0,1:T(4,128)(2,1)}, u32[]{:S(2)}) copy-start(bf16[128,4]{0,1:T(4,128)(2,1)} %param.25) | copy-start | bytes 3076
  54.2 4.0 %copy-start.2 = (bf16[128,128]{1,0:T(8,128)(2,1)S(1)}, bf16[128,128]{1,0:T(8,128)(2,1)}, u32[]{:S(2)}) copy-start(bf16[128,128]{1,0:T(8,128)(2,1)} %refs_1_.5) | copy-start | bytes 98308
  54.2 13.1 %all-to-all-start.1 = ((bf16[8,16,2304]{2,1,0:T(8,128)(2,1)}), bf16[8,16,2304]{2,1,0:T(8,128)(2,1)S(1)}, u32[]{:S(2)}, u32[]{:S(2)}) async-start(bf16[8,16,2304]{2,1,0:T(8,128)(2,1)} %outer.1), calls=%async_computation.1 | async-start | bytes 1179648 | tf_op jit(solution)/shard_map/all_to_all | solution.py:439
  58.1 9.3 %copy-start.3 = (bf16[128,128]{1,0:T(8,128)(2,1)S(1)}, bf16[128,128]{1,0:T(8,128)(2,1)}, u32[]{:S(2)}) copy-start(bf16[128,128]{1,0:T(8,128)(2,1)} %refs_2_.2) | copy-start | bytes 98308
  58.1 9.3 %copy-start.10 = (f32[128]{0:T(128)S(1)}, f32[128]{0:T(128)}, u32[]{:S(2)}) copy-start(f32[128]{0:T(128)} %param.19) | copy-start | bytes 1540
  58.1 9.3 %copy-start.11 = (f32[128]{0:T(128)S(1)}, f32[128]{0:T(128)}, u32[]{:S(2)}) copy-start(f32[128]{0:T(128)} %param.21) | copy-start | bytes 1540
  67.3 18.0 %copy-start.5 = (bf16[128,128]{1,0:T(8,128)(2,1)S(1)}, bf16[128,128]{1,0:T(8,128)(2,1)}, u32[]{:S(2)}) copy-start(bf16[128,128]{1,0:T(8,128)(2,1)} %refs_1_.7) | copy-start | bytes 98308
  67.4 18.0 %copy-start.6 = (bf16[128,128]{1,0:T(8,128)(2,1)S(1)}, bf16[128,128]{1,0:T(8,128)(2,1)}, u32[]{:S(2)}) copy-start(bf16[128,128]{1,0:T(8,128)(2,1)} %refs_2_.3) | copy-start | bytes 98308
  67.4 18.0 %copy-start.7 = (bf16[128,128]{1,0:T(8,128)(2,1)S(1)}, bf16[128,128]{1,0:T(8,128)(2,1)}, u32[]{:S(2)}) copy-start(bf16[128,128]{1,0:T(8,128)(2,1)} %refs_3_.3) | copy-start | bytes 98308
  67.4 18.0 %copy-start.8 = (bf16[128,128]{1,0:T(8,128)(2,1)S(1)}, bf16[128,128]{1,0:T(8,128)(2,1)}, u32[]{:S(2)}) copy-start(bf16[128,128]{1,0:T(8,128)(2,1)} %refs_4_.4) | copy-start | bytes 98308
  70.1 16.6 %copy-start.4 = (bf16[128,128]{1,0:T(8,128)(2,1)S(1)}, bf16[128,128]{1,0:T(8,128)(2,1)}, u32[]{:S(2)}) copy-start(bf16[128,128]{1,0:T(8,128)(2,1)} %refs_6_.1) | copy-start | bytes 98308
  70.1 6.7 %collective-permute-start.8 = (bf16[1,24,384]{2,1,0:T(8,128)(2,1)S(1)}, bf16[1,24,384]{2,1,0:T(8,128)(2,1)S(1)}, u32[]{:S(2)}, u32[]{:S(2)}) collective-permute-start(bf16[1,24,384]{2,1,0:T(8,128)(2,1)S(1)} %bitcast.5), channel_id=1, source_target_pairs={{0,8},{1,9},{2,10},{3,11},{4,12},{5,13},{6,14},{7,15},{8,0},{9,1},... | collective-permute-start | bytes 55304 | tf_op jit(solution)/shard_map/ppermute | solution.py:349
  76.7 4.0 %collective-permute-start.9 = (bf16[2,24,384]{2,1,0:T(8,128)(2,1)S(1)}, bf16[2,24,384]{2,1,0:T(8,128)(2,1)S(1)}, u32[]{:S(2)}, u32[]{:S(2)}) collective-permute-start(bf16[2,24,384]{2,1,0:T(8,128)(2,1)S(1)} %pad_maximum_fusion.2), channel_id=1, source_target_pairs={{0,4},{1,5},{2,6},{3,7},{4,0},{5,1},{6,2},{7,3},{8,12},{9,13},{10,... | collective-permute-start | bytes 110600 | tf_op jit(solution)/shard_map/ppermute | solution.py:349
  80.8 4.4 %collective-permute-start.10 = (bf16[4,24,384]{2,1,0:T(8,128)(2,1)S(1)}, bf16[4,24,384]{2,1,0:T(8,128)(2,1)S(1)}, u32[]{:S(2)}, u32[]{:S(2)}) collective-permute-start(bf16[4,24,384]{2,1,0:T(8,128)(2,1)S(1)} %pad_maximum_fusion.1), channel_id=1, source_target_pairs={{0,2},{1,3},{2,0},{3,1},{4,6},{5,7},{6,4},{7,5},{8,10},{9,11},{10,... | collective-permute-start | bytes 221192 | tf_op jit(solution)/shard_map/ppermute | solution.py:349
  85.2 1.4 %collective-permute-start.11 = (bf16[8,24,384]{2,1,0:T(8,128)(2,1)S(1)}, bf16[8,24,384]{2,1,0:T(8,128)(2,1)S(1)}, u32[]{:S(2)}, u32[]{:S(2)}) collective-permute-start(bf16[8,24,384]{2,1,0:T(8,128)(2,1)S(1)} %pad_maximum_fusion), channel_id=1, source_target_pairs={{0,1},{1,0},{2,3},{3,2},{4,5},{5,4},{6,7},{7,6},{8,9},{9,8},{10,11... | collective-permute-start | bytes 442376 | tf_op jit(solution)/shard_map/ppermute | solution.py:349

commit v17 on v16

--- a/solution.py
+++ b/solution.py
@@ -57,6 +57,7 @@
         self.rows, self.crop, self.devices, self.channels = rows, crop, devices, channels
         self.half = rows // 2
         self.group = devices // 2
+        self.partners = [-s % self.group for s in range(self.group)]
         self.columns = rows * self.group
         self.whole = crop // LANES
         self.rest = crop % LANES
@@ -139,15 +140,16 @@
             for row in range(sz.rows):
                 block = wide_ref[pl.ds(row * sz.columns + g * sz.rows, sz.rows), :]
                 pair_ref[base, g, row * sz.rows : (row + 1) * sz.rows, :] = block
-    for r in range(sz.group):
+    for slot, partner in enumerate(sz.partners):
         for base in range(2):
             for t in range(sz.block_tiles):
                 at = (sz.tiles + base * sz.block_tiles + t) * LANES
-                block = pair_ref[base, mine ^ r, t * cd : (t + 1) * cd, :]
-                near[r][:, at : at + LANES] = block.astype(BF16)
+                block = pair_ref[base, mine ^ partner, t * cd : (t + 1) * cd, :]
+                near[slot][:, at : at + LANES] = block.astype(BF16)
     r = lax.broadcasted_iota(jnp.int32, (ch, ch), 0)
     e = lax.broadcasted_iota(jnp.int32, (ch, ch), 1)
-    pick = (((r // cd) ^ mine) * cd + r % cd == e).astype(BF16)
+    partner = (sz.group - r // cd) & (sz.group - 1)
+    pick = ((partner ^ mine) * cd + r % cd == e).astype(BF16)
 
     def store(g, lanes, edge):
         near[g][:, lanes] = edge
@@ -181,8 +183,8 @@
 def arrange_kernel(sz, *refs):
     near, (out_ref, main_ref, rest_ref) = refs[: sz.group], refs[sz.group :]
     mine = position() & (sz.group - 1)
-    for r in range(sz.group):
-        unpack(sz, near[r], mine ^ r, main_ref, rest_ref)
+    for slot, partner in enumerate(sz.partners):
+        unpack(sz, near[slot], mine ^ partner, main_ref, rest_ref)
     for c in range(sz.chans):
         out_ref[c] = matrix(sz, c, sz.columns, main_ref, rest_ref)
 
@@ -219,12 +221,12 @@
 
 def take_columns(sz, near, cols_ref):
     cd, me = sz.chans, position()
-    for r in range(sz.group):
-        for base, owner in ((0, me ^ r), (1, me ^ (sz.group + r))):
+    for slot, partner in enumerate(sz.partners):
+        for base, owner in ((0, me ^ partner), (1, me ^ (sz.group + partner))):
             for t in range(sz.block_tiles):
                 at = (sz.tiles + base * sz.block_tiles + t) * LANES
                 rows = pl.ds(pl.multiple_of(owner * sz.block + t * cd, 8), cd)
-                cols_ref[rows, :] = near[r][:, at : at + LANES].astype(F32)
+                cols_ref[rows, :] = near[slot][:, at : at + LANES].astype(F32)
 
 
 def gating_kernel(sz, lnp_ref, gate_ref, *refs):
@@ -373,12 +375,12 @@
     def slab(tiles, *lead):
         return shape((*lead, cd, tiles * LANES), BF16)
 
-    def send(blocks, offset):
+    def send(blocks):
         return [
-            block
-            if not (offset ^ r)
-            else lax.ppermute(block, AXES, [(d, d ^ offset ^ r) for d in range(devices)])
-            for r, block in enumerate(blocks)
+            lax.ppermute(block, AXES, [(d, d ^ partner) for d in range(devices)])
+            if partner
+            else block
+            for partner, block in zip(sz.partners, blocks)
         ]
 
     upper = (lax.axis_index(AXES) >= g).astype(jnp.int32)
@@ -411,7 +413,7 @@
         cost=pl.CostEstimate(flops=10**11, bytes_accessed=10**6, transcendentals=0),
     )
     left = lax.all_to_all(left, AXES, split_axis=0, concat_axis=0, tiled=True)
-    near = send(others, 0)
+    near = send(others)
     rest = sz.rest > 0
     column_rows = sz.columns * cd
     right = call(

time: 92 us -> 90.8 us (0.987)
    ppermute x7, waiting for transfers between devices: 19.3 us -> 18.2 us  [send(): lax.ppermute(block, AXES, [(d, d ^ partner) for d in range(devices)])]
  transfers between devices with their start and end apart: 14 -> 14, of which waited for: 11 -> 10; matrix products, arithmetic and copies ran while one was open for 0% -> 0% of each run, Pallas kernels for 8% -> 8%
where the time goes in v17:
time: 90.8 us; the launch traced here: 90.4 us
  waiting for transfers between devices  46.7 us (51%)
  starting transfers between devices  24.1 us (27%)
  Pallas kernels  17.5 us (19%)
  local copies, waits for them, and re-layouts  1.18 us (1%)
    ppermute x7, waiting for transfers between devices, send(): lax.ppermute(block, AXES, [(d, d ^ partner) for d in range(devices)])  18.2 us
    pallas_call x8, Pallas kernels, call(): pl.pallas_call(kernel, out_shape=out_shape, in_specs=specs, out_specs=ins...  17.5 us
    ppermute x1, waiting for transfers between devices, shards(): lax.ppermute(lax.dynamic_slice_in_dim(pair_rep, (1 - upper) * sz.columns,...  12.5 us
    ppermute x4, waiting for transfers between devices, spread(): lax.ppermute(held, AXES, [(d, d ^ bit) for d in range(devices)])  8.05 us
    all_to_all x1, waiting for transfers between devices, shards(): lax.all_to_all(outer, AXES, split_axis=0, concat_axis=0, tiled=True, axis...  7.91 us
    ppermute x4, starting transfers between devices, spread(): lax.ppermute(held, AXES, [(d, d ^ bit) for d in range(devices)])  7.37 us
    ppermute x7, starting transfers between devices, send(): lax.ppermute(block, AXES, [(d, d ^ partner) for d in range(devices)])  4.71 us
    ppermute x1, starting transfers between devices, shards(): lax.ppermute(lax.dynamic_slice_in_dim(pair_rep, (1 - upper) * sz.columns,...  4.1 us
  transfers between devices with their start and end apart: 14, of which 10 were waited for; matrix products, arithmetic and copies ran while one was open for 0% of the time, Pallas kernels for 8%

profile of v17, /device:TPU:0, one launch (start us, length us, event | category | flops | bytes accessed | tf_op | source)
XLA Modules:
  0.0 90.4 jit_solution(6278636879418999278)
XLA Ops:
  0.0 1.0 %constant_dynamic-slice_fusion = bf16[12,96,128]{2,1,0:T(8,128)(2,1)S(1)} fusion(bf16[12,192,128]{2,1,0:T(8,128)(2,1)} %refs_1_.6, s32[]{:T(128)S(6)} %select_n.3), kind=kLoop, calls=%fused_computation.3 | loop fusion | bytes 589828 | tf_op jit(solution)/shard_map/dynamic_slice | solution.py:388
  1.0 4.1 %collective-permute-start = (bf16[12,96,128]{2,1,0:T(8,128)(2,1)S(1)}, bf16[12,96,128]{2,1,0:T(8,128)(2,1)S(1)}, u32[]{:S(2)}, u32[]{:S(2)}) collective-permute-start(bf16[12,96,128]{2,1,0:T(8,128)(2,1)S(1)} %constant_dynamic-slice_fusion), channel_id=1, source_target_pairs={{0,8},{1,9},{2,10},{3,11},{4,12},{5,13},{6,14},{7,15},{8,0},{9,1},... | collective-permute-start | bytes 884744 | tf_op jit(solution)/shard_map/ppermute | solution.py:387
  5.7 3.4 %left.1 = bf16[16,16,2304]{2,1,0:T(8,128)(2,1)} custom-call(s32[1]{0:T(128)S(6)} %copy.16.refs_0_, bf16[12,192,128]{2,1,0:T(8,128)(2,1)} %refs_1_.6, f32[1,128]{1,0:T(1,128)} %bitcast.10, bf16[4,128,128]{2,1,0:T(8,128)(2,1)} %refs_3_.2), custom_call_target="tpu_custom_call" | custom-call | tf_op jit(solution)/shard_map/left/pallas_call | solution.py:43
  9.1 4.0 %all-to-all-start = ((bf16[16,16,2304]{2,1,0:T(8,128)(2,1)}), bf16[16,16,2304]{2,1,0:T(8,128)(2,1)S(1)}, u32[]{:S(2)}, u32[]{:S(2)}) async-start(bf16[16,16,2304]{2,1,0:T(8,128)(2,1)} %left.1), calls=%async_computation | async-start | bytes 2359296 | tf_op jit(solution)/shard_map/all_to_all | solution.py:415
  13.2 12.5 %collective-permute-done.refs_2_ = bf16[12,96,128]{2,1,0:T(8,128)(2,1)S(1)} collective-permute-done((bf16[12,96,128]{2,1,0:T(8,128)(2,1)S(1)}, bf16[12,96,128]{2,1,0:T(8,128)(2,1)S(1)}, u32[]{:S(2)}, u32[]{:S(2)}) %collective-permute-start) | collective-permute-done | bytes 294944 | tf_op jit(solution)/shard_map/ppermute | solution.py:387
  25.7 1.4 %right.1 = (bf16[16,4608]{1,0:T(8,128)(2,1)S(1)}, bf16[16,4608]{1,0:T(8,128)(2,1)S(1)}, bf16[16,4608]{1,0:T(8,128)(2,1)S(1)}, bf16[16,4608]{1,0:T(8,128)(2,1)S(1...) custom-call(s32[1]{0:T(128)S(6)} %copy.16.refs_0_, ...), custom_call_target="tpu_custom_call" | custom-call | flops 99999997952 | bytes 1000000 | tf_op jit(solution)/shard_map/right/pallas_call | solution.py:43
  27.2 0.4 collective-permute-start.1
  27.6 0.5 collective-permute-start.2
  28.2 1.2 %collective-permute-start.3 = (bf16[16,4608]{1,0:T(8,128)(2,1)S(1)}, bf16[16,4608]{1,0:T(8,128)(2,1)S(1)}, u32[]{:S(2)}, u32[]{:S(2)}) collective-permute-start(bf16[16,4608]{1,0:T(8,128)(2,1)S(1)} %get-tuple-element.23), channel_id=1, source_target_pairs={{0,5},{1,4},{2,7},{3,6},{4,1},{5,0},{6,3},{7,2},{8,13},{9,12},{10,... | collective-permute-start | bytes 442376 | tf_op jit(solution)/shard_map/ppermute | solution.py:380
  29.4 2.2 %collective-permute-start.4 = (bf16[16,4608]{1,0:T(8,128)(2,1)S(1)}, bf16[16,4608]{1,0:T(8,128)(2,1)S(1)}, u32[]{:S(2)}, u32[]{:S(2)}) collective-permute-start(bf16[16,4608]{1,0:T(8,128)(2,1)S(1)} %get-tuple-element.24), channel_id=1, source_target_pairs={{0,4},{1,5},{2,6},{3,7},{4,0},{5,1},{6,2},{7,3},{8,12},{9,13},{10,... | collective-permute-start | bytes 442376 | tf_op jit(solution)/shard_map/ppermute | solution.py:380
  31.6 7.7 %collective-permute-done.1.refs_3_.refs_1_.refs_7_ = bf16[16,4608]{1,0:T(8,128)(2,1)S(1)} collective-permute-done((bf16[16,4608]{1,0:T(8,128)(2,1)S(1)}, bf16[16,4608]{1,0:T(8,128)(2,1)S(1)}, u32[]{:S(2)}, u32[]{:S(2)}) %collective-permute-start.1) | collective-permute-done | bytes 147488 | tf_op jit(solution)/shard_map/ppermute | solution.py:380
  39.3 0.2 collective-permute-start.6
  39.6 5.2 %collective-permute-done.2.refs_4_.refs_2_.refs_8_ = bf16[16,4608]{1,0:T(8,128)(2,1)S(1)} collective-permute-done((bf16[16,4608]{1,0:T(8,128)(2,1)S(1)}, bf16[16,4608]{1,0:T(8,128)(2,1)S(1)}, u32[]{:S(2)}, u32[]{:S(2)}) %collective-permute-start.2) | collective-permute-done | bytes 147488 | tf_op jit(solution)/shard_map/ppermute | solution.py:380
  44.8 2.1 %collective-permute-done.3.refs_5_.refs_3_.refs_9_ = bf16[16,4608]{1,0:T(8,128)(2,1)S(1)} collective-permute-done((bf16[16,4608]{1,0:T(8,128)(2,1)S(1)}, bf16[16,4608]{1,0:T(8,128)(2,1)S(1)}, u32[]{:S(2)}, u32[]{:S(2)}) %collective-permute-start.3) | collective-permute-done | bytes 147488 | tf_op jit(solution)/shard_map/ppermute | solution.py:380
  46.8 3.2 %collective-permute-done.4.refs_6_.refs_4_.refs_10_ = bf16[16,4608]{1,0:T(8,128)(2,1)S(1)} collective-permute-done((bf16[16,4608]{1,0:T(8,128)(2,1)S(1)}, bf16[16,4608]{1,0:T(8,128)(2,1)S(1)}, u32[]{:S(2)}, u32[]{:S(2)}) %collective-permute-start.4) | collective-permute-done | bytes 147488 | tf_op jit(solution)/shard_map/ppermute | solution.py:380
  50.1 0.7 arrange.1.refs_1_
  50.8 2.5 %outer.1 = bf16[8,16,2304]{2,1,0:T(8,128)(2,1)} custom-call(bf16[16,16,2304]{2,1,0:T(8,128)(2,1)S(1)} %all-to-all-done.refs_0_, bf16[16,96,192]{2,1,0:T(8,128)(2,1)S(1)} %arrange.1.refs_1_), custom_call_target="tpu_custom_call" | custom-call | tf_op jit(solution)/shard_map/outer/pallas_call | solution.py:43
  53.3 3.9 %all-to-all-start.1 = ((bf16[8,16,2304]{2,1,0:T(8,128)(2,1)}), bf16[8,16,2304]{2,1,0:T(8,128)(2,1)S(1)}, u32[]{:S(2)}, u32[]{:S(2)}) async-start(bf16[8,16,2304]{2,1,0:T(8,128)(2,1)} %outer.1), calls=%async_computation.1 | async-start | bytes 1179648 | tf_op jit(solution)/shard_map/all_to_all | solution.py:441
  57.2 0.1 copy.15.refs_4_
  57.3 1.2 %gating.1.refs_0_ = bf16[12,192,128]{2,1,0:T(8,128)(2,1)S(1)} custom-call(f32[1,128]{1,0:T(1,128)S(1)} %bitcast.12, bf16[128,128]{1,0:T(8,128)(2,1)S(1)} %copy-done.2, bf16[16,4608]{1,0:T(8,128)(2,1)S(1)} %get-tuple-element.20.refs_2_.refs_0_.refs_6_, bf16[16,4608]{1,0:T(8,128)(2,1)S(1)} %collective-permute-done.1.refs_3_.refs_1_.refs_7_, ...), custom_call_target="tpu_custom_call" | custom-call | tf_op jit(solution)/shard_map/gating/pallas_call | solution.py:43
  58.5 7.9 %all-to-all-done.1.refs_5_ = bf16[8,16,2304]{2,1,0:T(8,128)(2,1)S(1)} async-done(((bf16[8,16,2304]{2,1,0:T(8,128)(2,1)}), bf16[8,16,2304]{2,1,0:T(8,128)(2,1)S(1)}, u32[]{:S(2)}, u32[]{:S(2)}) %all-to-all-start.1) | async-done | bytes 589856 | tf_op jit(solution)/shard_map/all_to_all | solution.py:441
  66.5 2.7 %update.1 = (bf16[12,192,128]{2,1,0:T(8,128)(2,1)S(1)}, bf16[12,192,128]{2,1,0:T(8,128)(2,1)S(1)}, bf16[24,384]{1,0:T(8,128)(2,1)S(1)}) custom-call(bf16[12,192,128]{2,1,0:T(8,128)(2,1)S(1)} %gating.1.refs_0_, f32[1,128]{1,0:T(1,128)S(1)} %bitcast.13, bf16[128,128]{1,0:T(8,128)(2,1)S(1)} %copy-done.3, f32[1,128]{1,0:T(1,128)S(1)} %bitcast.14, ...), custom_call_target="tpu_custom_call" | custom-call | tf_op jit(solution)/shard_map/update/pallas_call | solution.py:43
  69.2 4.6 %collective-permute-start.8 = (bf16[1,24,384]{2,1,0:T(8,128)(2,1)S(1)}, bf16[1,24,384]{2,1,0:T(8,128)(2,1)S(1)}, u32[]{:S(2)}, u32[]{:S(2)}) collective-permute-start(bf16[1,24,384]{2,1,0:T(8,128)(2,1)S(1)} %bitcast.5), channel_id=1, source_target_pairs={{0,8},{1,9},{2,10},{3,11},{4,12},{5,13},{6,14},{7,15},{8,0},{9,1},... | collective-permute-start | bytes 55304 | tf_op jit(solution)/shard_map/ppermute | solution.py:351
  73.8 1.7 %collective-permute-done.8.refs_8_ = bf16[1,24,384]{2,1,0:T(8,128)(2,1)S(1)} collective-permute-done((bf16[1,24,384]{2,1,0:T(8,128)(2,1)S(1)}, bf16[1,24,384]{2,1,0:T(8,128)(2,1)S(1)}, u32[]{:S(2)}, u32[]{:S(2)}) %collective-permute-start.8) | collective-permute-done | bytes 18464 | tf_op jit(solution)/shard_map/ppermute | solution.py:351
  75.5 1.3 %collective-permute-start.9 = (bf16[2,24,384]{2,1,0:T(8,128)(2,1)S(1)}, bf16[2,24,384]{2,1,0:T(8,128)(2,1)S(1)}, u32[]{:S(2)}, u32[]{:S(2)}) collective-permute-start(bf16[2,24,384]{2,1,0:T(8,128)(2,1)S(1)} %pad_maximum_fusion.2), channel_id=1, source_target_pairs={{0,4},{1,5},{2,6},{3,7},{4,0},{5,1},{6,2},{7,3},{8,12},{9,13},{10,... | collective-permute-start | bytes 110600 | tf_op jit(solution)/shard_map/ppermute | solution.py:351
  76.9 2.7 %collective-permute-done.9.refs_9_ = bf16[2,24,384]{2,1,0:T(8,128)(2,1)S(1)} collective-permute-done((bf16[2,24,384]{2,1,0:T(8,128)(2,1)S(1)}, bf16[2,24,384]{2,1,0:T(8,128)(2,1)S(1)}, u32[]{:S(2)}, u32[]{:S(2)}) %collective-permute-start.9) | collective-permute-done | bytes 36896 | tf_op jit(solution)/shard_map/ppermute | solution.py:351
  79.6 1.3 %collective-permute-start.10 = (bf16[4,24,384]{2,1,0:T(8,128)(2,1)S(1)}, bf16[4,24,384]{2,1,0:T(8,128)(2,1)S(1)}, u32[]{:S(2)}, u32[]{:S(2)}) collective-permute-start(bf16[4,24,384]{2,1,0:T(8,128)(2,1)S(1)} %pad_maximum_fusion.1), channel_id=1, source_target_pairs={{0,2},{1,3},{2,0},{3,1},{4,6},{5,7},{6,4},{7,5},{8,10},{9,11},{10,... | collective-permute-start | bytes 221192 | tf_op jit(solution)/shard_map/ppermute | solution.py:351
  80.9 3.1 %collective-permute-done.10.refs_10_ = bf16[4,24,384]{2,1,0:T(8,128)(2,1)S(1)} collective-permute-done((bf16[4,24,384]{2,1,0:T(8,128)(2,1)S(1)}, bf16[4,24,384]{2,1,0:T(8,128)(2,1)S(1)}, u32[]{:S(2)}, u32[]{:S(2)}) %collective-permute-start.10) | collective-permute-done | bytes 73760 | tf_op jit(solution)/shard_map/ppermute | solution.py:351
  84.0 0.1 collective-permute-start.11
  84.2 0.8 project.1
  84.9 0.5 collective-permute-done.11.refs_11_
  85.5 4.9 %attend.1 = bf16[12,192,128]{2,1,0:T(8,128)(2,1)} custom-call(s32[1]{0:T(128)S(6)} %copy.16.refs_0_, bf16[12,192,128]{2,1,0:T(8,128)(2,1)S(1)} %get-tuple-element.29.refs_1_, bf16[12,192,128]{2,1,0:T(8,128)(2,1)S(1)} %get-tuple-element.30.refs_2_, bf16[12,192,128]{2,1,0:T(8,128)(2,1)S(1)} %get-tuple-element.31.refs_3_, ...), custom_call_target="tpu_custom_call" | custom-call | tf_op jit(solution)/shard_map/attend/pallas_call | solution.py:43
  (35 shorter events, 0.1 us)
Async XLA Ops:
  1.0 24.7 %collective-permute-start = (bf16[12,96,128]{2,1,0:T(8,128)(2,1)S(1)}, bf16[12,96,128]{2,1,0:T(8,128)(2,1)S(1)}, u32[]{:S(2)}, u32[]{:S(2)}) collective-permute-start(bf16[12,96,128]{2,1,0:T(8,128)(2,1)S(1)} %constant_dynamic-slice_fusion), channel_id=1, source_target_pairs={{0,8},{1,9},{2,10},{3,11},{4,12},{5,13},{6,14},{7,15},{8,0},{9,1},... | collective-permute-start | bytes 884744 | tf_op jit(solution)/shard_map/ppermute | solution.py:387
  9.1 16.6 %copy-start = (bf16[12,192,128]{2,1,0:T(8,128)(2,1)S(1)}, bf16[12,192,128]{2,1,0:T(8,128)(2,1)}, u32[]{:S(2)}) copy-start(bf16[12,192,128]{2,1,0:T(8,128)(2,1)} %refs_1_.6) | copy-start | bytes 1769476
  9.1 16.6 %copy-start.1 = (bf16[4,128,128]{2,1,0:T(8,128)(2,1)S(1)}, bf16[4,128,128]{2,1,0:T(8,128)(2,1)}, u32[]{:S(2)}) copy-start(bf16[4,128,128]{2,1,0:T(8,128)(2,1)} %refs_3_.2) | copy-start | bytes 393220
  9.1 16.6 %copy-start.9 = (f32[128]{0:T(128)S(1)}, f32[128]{0:T(128)}, u32[]{:S(2)}) copy-start(f32[128]{0:T(128)} %param.16) | copy-start | bytes 1540
  9.1 41.7 %all-to-all-start = ((bf16[16,16,2304]{2,1,0:T(8,128)(2,1)}), bf16[16,16,2304]{2,1,0:T(8,128)(2,1)S(1)}, u32[]{:S(2)}, u32[]{:S(2)}) async-start(bf16[16,16,2304]{2,1,0:T(8,128)(2,1)} %left.1), calls=%async_computation | async-start | bytes 2359296 | tf_op jit(solution)/shard_map/all_to_all | solution.py:415
  27.2 12.1 %collective-permute-start.1 = (bf16[16,4608]{1,0:T(8,128)(2,1)S(1)}, bf16[16,4608]{1,0:T(8,128)(2,1)S(1)}, u32[]{:S(2)}, u32[]{:S(2)}) collective-permute-start(bf16[16,4608]{1,0:T(8,128)(2,1)S(1)} %get-tuple-element.21), channel_id=1, source_target_pairs={{0,7},{1,6},{2,5},{3,4},{4,3},{5,2},{6,1},{7,0},{8,15},{9,14},{10,... | collective-permute-start | bytes 442376 | tf_op jit(solution)/shard_map/ppermute | solution.py:380
  27.6 17.2 %collective-permute-start.2 = (bf16[16,4608]{1,0:T(8,128)(2,1)S(1)}, bf16[16,4608]{1,0:T(8,128)(2,1)S(1)}, u32[]{:S(2)}, u32[]{:S(2)}) collective-permute-start(bf16[16,4608]{1,0:T(8,128)(2,1)S(1)} %get-tuple-element.22), channel_id=1, source_target_pairs={{0,6},{1,7},{2,4},{3,5},{4,2},{5,3},{6,0},{7,1},{8,14},{9,15},{10,... | collective-permute-start | bytes 442376 | tf_op jit(solution)/shard_map/ppermute | solution.py:380
  28.2 18.7 %collective-permute-start.3 = (bf16[16,4608]{1,0:T(8,128)(2,1)S(1)}, bf16[16,4608]{1,0:T(8,128)(2,1)S(1)}, u32[]{:S(2)}, u32[]{:S(2)}) collective-permute-start(bf16[16,4608]{1,0:T(8,128)(2,1)S(1)} %get-tuple-element.23), channel_id=1, source_target_pairs={{0,5},{1,4},{2,7},{3,6},{4,1},{5,0},{6,3},{7,2},{8,13},{9,12},{10,... | collective-permute-start | bytes 442376 | tf_op jit(solution)/shard_map/ppermute | solution.py:380
  29.4 20.7 %collective-permute-start.4 = (bf16[16,4608]{1,0:T(8,128)(2,1)S(1)}, bf16[16,4608]{1,0:T(8,128)(2,1)S(1)}, u32[]{:S(2)}, u32[]{:S(2)}) collective-permute-start(bf16[16,4608]{1,0:T(8,128)(2,1)S(1)} %get-tuple-element.24), channel_id=1, source_target_pairs={{0,4},{1,5},{2,6},{3,7},{4,0},{5,1},{6,2},{7,3},{8,12},{9,13},{10,... | collective-permute-start | bytes 442376 | tf_op jit(solution)/shard_map/ppermute | solution.py:380
  31.6 18.4 %collective-permute-start.5 = (bf16[16,4608]{1,0:T(8,128)(2,1)S(1)}, bf16[16,4608]{1,0:T(8,128)(2,1)S(1)}, u32[]{:S(2)}, u32[]{:S(2)}) collective-permute-start(bf16[16,4608]{1,0:T(8,128)(2,1)S(1)} %get-tuple-element.25), channel_id=1, source_target_pairs={{0,3},{1,2},{2,1},{3,0},{4,7},{5,6},{6,5},{7,4},{8,11},{9,10},{10,... | collective-permute-start | bytes 442376 | tf_op jit(solution)/shard_map/ppermute | solution.py:380
  39.3 10.7 %collective-permute-start.6 = (bf16[16,4608]{1,0:T(8,128)(2,1)S(1)}, bf16[16,4608]{1,0:T(8,128)(2,1)S(1)}, u32[]{:S(2)}, u32[]{:S(2)}) collective-permute-start(bf16[16,4608]{1,0:T(8,128)(2,1)S(1)} %get-tuple-element.26), channel_id=1, source_target_pairs={{0,2},{1,3},{2,0},{3,1},{4,6},{5,7},{6,4},{7,5},{8,10},{9,11},{10,... | collective-permute-start | bytes 442376 | tf_op jit(solution)/shard_map/ppermute | solution.py:380
  44.8 5.3 %collective-permute-start.7 = (bf16[16,4608]{1,0:T(8,128)(2,1)S(1)}, bf16[16,4608]{1,0:T(8,128)(2,1)S(1)}, u32[]{:S(2)}, u32[]{:S(2)}) collective-permute-start(bf16[16,4608]{1,0:T(8,128)(2,1)S(1)} %get-tuple-element.27), channel_id=1, source_target_pairs={{0,1},{1,0},{2,3},{3,2},{4,5},{5,4},{6,7},{7,6},{8,9},{9,8},{10,11... | collective-permute-start | bytes 442376 | tf_op jit(solution)/shard_map/ppermute | solution.py:380
  53.3 3.9 %copy-start.12 = (bf16[128,4]{0,1:T(4,128)(2,1)S(1)}, bf16[128,4]{0,1:T(4,128)(2,1)}, u32[]{:S(2)}) copy-start(bf16[128,4]{0,1:T(4,128)(2,1)} %param.25) | copy-start | bytes 3076
  53.3 4.0 %copy-start.2 = (bf16[128,128]{1,0:T(8,128)(2,1)S(1)}, bf16[128,128]{1,0:T(8,128)(2,1)}, u32[]{:S(2)}) copy-start(bf16[128,128]{1,0:T(8,128)(2,1)} %refs_1_.5) | copy-start | bytes 98308
  53.3 13.1 %all-to-all-start.1 = ((bf16[8,16,2304]{2,1,0:T(8,128)(2,1)}), bf16[8,16,2304]{2,1,0:T(8,128)(2,1)S(1)}, u32[]{:S(2)}, u32[]{:S(2)}) async-start(bf16[8,16,2304]{2,1,0:T(8,128)(2,1)} %outer.1), calls=%async_computation.1 | async-start | bytes 1179648 | tf_op jit(solution)/shard_map/all_to_all | solution.py:441
  57.2 9.3 %copy-start.3 = (bf16[128,128]{1,0:T(8,128)(2,1)S(1)}, bf16[128,128]{1,0:T(8,128)(2,1)}, u32[]{:S(2)}) copy-start(bf16[128,128]{1,0:T(8,128)(2,1)} %refs_2_.2) | copy-start | bytes 98308
  57.2 9.3 %copy-start.10 = (f32[128]{0:T(128)S(1)}, f32[128]{0:T(128)}, u32[]{:S(2)}) copy-start(f32[128]{0:T(128)} %param.19) | copy-start | bytes 1540
  57.2 9.3 %copy-start.11 = (f32[128]{0:T(128)S(1)}, f32[128]{0:T(128)}, u32[]{:S(2)}) copy-start(f32[128]{0:T(128)} %param.21) | copy-start | bytes 1540
  66.4 17.7 %copy-start.5 = (bf16[128,128]{1,0:T(8,128)(2,1)S(1)}, bf16[128,128]{1,0:T(8,128)(2,1)}, u32[]{:S(2)}) copy-start(bf16[128,128]{1,0:T(8,128)(2,1)} %refs_1_.7) | copy-start | bytes 98308
  66.5 17.7 %copy-start.6 = (bf16[128,128]{1,0:T(8,128)(2,1)S(1)}, bf16[128,128]{1,0:T(8,128)(2,1)}, u32[]{:S(2)}) copy-start(bf16[128,128]{1,0:T(8,128)(2,1)} %refs_2_.3) | copy-start | bytes 98308
  66.5 17.7 %copy-start.7 = (bf16[128,128]{1,0:T(8,128)(2,1)S(1)}, bf16[128,128]{1,0:T(8,128)(2,1)}, u32[]{:S(2)}) copy-start(bf16[128,128]{1,0:T(8,128)(2,1)} %refs_3_.3) | copy-start | bytes 98308
  66.5 17.7 %copy-start.8 = (bf16[128,128]{1,0:T(8,128)(2,1)S(1)}, bf16[128,128]{1,0:T(8,128)(2,1)}, u32[]{:S(2)}) copy-start(bf16[128,128]{1,0:T(8,128)(2,1)} %refs_4_.4) | copy-start | bytes 98308
  69.2 16.3 %copy-start.4 = (bf16[128,128]{1,0:T(8,128)(2,1)S(1)}, bf16[128,128]{1,0:T(8,128)(2,1)}, u32[]{:S(2)}) copy-start(bf16[128,128]{1,0:T(8,128)(2,1)} %refs_6_.1) | copy-start | bytes 98308
  69.2 6.4 %collective-permute-start.8 = (bf16[1,24,384]{2,1,0:T(8,128)(2,1)S(1)}, bf16[1,24,384]{2,1,0:T(8,128)(2,1)S(1)}, u32[]{:S(2)}, u32[]{:S(2)}) collective-permute-start(bf16[1,24,384]{2,1,0:T(8,128)(2,1)S(1)} %bitcast.5), channel_id=1, source_target_pairs={{0,8},{1,9},{2,10},{3,11},{4,12},{5,13},{6,14},{7,15},{8,0},{9,1},... | collective-permute-start | bytes 55304 | tf_op jit(solution)/shard_map/ppermute | solution.py:351
  75.5 4.0 %collective-permute-start.9 = (bf16[2,24,384]{2,1,0:T(8,128)(2,1)S(1)}, bf16[2,24,384]{2,1,0:T(8,128)(2,1)S(1)}, u32[]{:S(2)}, u32[]{:S(2)}) collective-permute-start(bf16[2,24,384]{2,1,0:T(8,128)(2,1)S(1)} %pad_maximum_fusion.2), channel_id=1, source_target_pairs={{0,4},{1,5},{2,6},{3,7},{4,0},{5,1},{6,2},{7,3},{8,12},{9,13},{10,... | collective-permute-start | bytes 110600 | tf_op jit(solution)/shard_map/ppermute | solution.py:351
  79.6 4.4 %collective-permute-start.10 = (bf16[4,24,384]{2,1,0:T(8,128)(2,1)S(1)}, bf16[4,24,384]{2,1,0:T(8,128)(2,1)S(1)}, u32[]{:S(2)}, u32[]{:S(2)}) collective-permute-start(bf16[4,24,384]{2,1,0:T(8,128)(2,1)S(1)} %pad_maximum_fusion.1), channel_id=1, source_target_pairs={{0,2},{1,3},{2,0},{3,1},{4,6},{5,7},{6,4},{7,5},{8,10},{9,11},{10,... | collective-permute-start | bytes 221192 | tf_op jit(solution)/shard_map/ppermute | solution.py:351
  84.0 1.4 %collective-permute-start.11 = (bf16[8,24,384]{2,1,0:T(8,128)(2,1)S(1)}, bf16[8,24,384]{2,1,0:T(8,128)(2,1)S(1)}, u32[]{:S(2)}, u32[]{:S(2)}) collective-permute-start(bf16[8,24,384]{2,1,0:T(8,128)(2,1)S(1)} %pad_maximum_fusion), channel_id=1, source_target_pairs={{0,1},{1,0},{2,3},{3,2},{4,5},{5,4},{6,7},{7,6},{8,9},{9,8},{10,11... | collective-permute-start | bytes 442376 | tf_op jit(solution)/shard_map/ppermute | solution.py:351

commit v18 on v17

--- a/solution.py
+++ b/solution.py
@@ -12,7 +12,6 @@
 BF16 = jnp.bfloat16
 AXES = ("row", "node")
 VMEM_BYTES = 48 * 1024 * 1024
-VMEM_MOST = 60 * 1024 * 1024
 
 
 def norm_last(values, gain):
@@ -230,18 +229,20 @@
 
 
 def gating_kernel(sz, lnp_ref, gate_ref, *refs):
-    near, (gating_ref, cols_ref) = refs[: sz.group], refs[sz.group :]
+    near, (x_ref, gating_ref, cols_ref) = refs[: sz.group], refs[sz.group :]
     take_columns(sz, near, cols_ref)
     for j in range(sz.rows):
         x = cols_ref[pl.ds(j, sz.crop, stride=sz.rows), :]
+        x_ref[j] = x.astype(BF16)
         normed = norm_last(x, lnp_ref[...]).astype(BF16)
         gating_ref[j] = sigmoid(dot(normed, gate_ref[...], 1, 0)).astype(BF16)
 
 
-def update_kernel(sz, gating_ref, lnh_ref, tri_ref, lna_ref, biasw_ref, sums_ref, *refs):
-    near, (first_ref, col_ref, bias_ref, cols_ref, brow_ref) = refs[: sz.group], refs[sz.group :]
+def update_kernel(
+    sz, x_ref, gating_ref, lnh_ref, tri_ref, lna_ref, biasw_ref, sums_ref,
+    first_ref, col_ref, bias_ref, brow_ref,
+):
     n, w, half, ch = sz.crop, sz.whole, sz.half, sz.channels
-    take_columns(sz, near, cols_ref)
     gain_h = jnp.transpose(jnp.broadcast_to(lnh_ref[...], (ch, ch)))
     tri = tri_ref[...]
 
@@ -260,8 +261,7 @@
             h, q = divmod(j, half)
             parts.append(rest[q][h * sz.rest : (h + 1) * sz.rest])
         change = jnp.concatenate(parts, axis=0) if len(parts) > 1 else parts[0]
-        x = cols_ref[pl.ds(j, n, stride=sz.rows), :]
-        first = (x + gating_ref[j].astype(F32) * change).astype(BF16)
+        first = (x_ref[j].astype(F32) + gating_ref[j].astype(F32) * change).astype(BF16)
         first_ref[j] = first
         col = norm_last(first.astype(F32), lna_ref[...]).astype(BF16)
         col_ref[j] = col
@@ -396,7 +396,6 @@
         scratch=[pltpu.VMEM((rows * crop, ch), BF16)],
         smem=(0,),
         name="left",
-        vmem=VMEM_MOST,
     )
     others = call(
         bound(right_kernel),
@@ -442,9 +441,9 @@
         outer, AXES, split_axis=0, concat_axis=0, tiled=True,
         axis_index_groups=[list(range(g)), list(range(g, devices))],
     )
-    gating = call(
+    columns, gating = call(
         bound(gating_kernel),
-        shape((rows, n, ch), BF16),
+        [shape((rows, n, ch), BF16)] * 2,
         (ln_pair[None], tri_gate, *near),
         scratch=[pltpu.VMEM((devices * sz.block + cd, ch), F32)],
         name="gating",
@@ -457,12 +456,9 @@
             shape((rows * heads // 2, 2 * n), BF16),
         ],
         (
-            gating, ln_hidden[None], tri_out, ln_att[None], att_bias, sums, *near,
+            columns, gating, ln_hidden[None], tri_out, ln_att[None], att_bias, sums,
         ),
-        scratch=[
-            pltpu.VMEM((devices * sz.block + cd, ch), F32),
-            pltpu.VMEM((rows * heads, n), F32),
-        ],
+        scratch=[pltpu.VMEM((rows * heads, n), F32)],
         name="update",
     )
     pieces, steps = spread(bias, devices)

time: 90.8 us -> 89.6 us (0.987)
  waiting for transfers between devices: 46.7 us -> 43.4 us
  local copies, waits for them, and re-layouts: 1.18 us -> 3.79 us
  Pallas kernels: 17.5 us -> 16.4 us
    ppermute x1, waiting for transfers between devices: 12.5 us -> 3.78 us  [shards(): lax.ppermute(lax.dynamic_slice_in_dim(pair_rep, (1 - upper) * sz.columns,...]
    ppermute x7, waiting for transfers between devices: 18.2 us -> 24.2 us  [send(): lax.ppermute(block, AXES, [(d, d ^ partner) for d in range(devices)])]
    unnamed x27 -> x33, local copies, waits for them, and re-layouts: 0.2 us -> 2.81 us
    ppermute x7, starting transfers between devices: 4.71 us -> 5.91 us  [send(): lax.ppermute(block, AXES, [(d, d ^ partner) for d in range(devices)])]
    pallas_call x8, Pallas kernels: 17.5 us -> 16.4 us  [call(): pl.pallas_call(kernel, out_shape=out_shape, in_specs=specs, out_specs=ins...]
  transfers between devices with their start and end apart: 14 -> 14, of which waited for: 10 -> 10; matrix products, arithmetic and copies ran while one was open for 0% -> 0% of each run, Pallas kernels for 8% -> 7%
where the time goes in v18:
time: 89.6 us; the launch traced here: 89.2 us
  waiting for transfers between devices  43.4 us (48%)
  starting transfers between devices  24.7 us (28%)
  Pallas kernels  16.4 us (18%)
  local copies, waits for them, and re-layouts  3.79 us (4%)
    ppermute x7, waiting for transfers between devices, send(): lax.ppermute(block, AXES, [(d, d ^ partner) for d in range(devices)])  24.2 us
    pallas_call x8, Pallas kernels, call(): pl.pallas_call(kernel, out_shape=out_shape, in_specs=specs, out_specs=ins...  16.4 us
    all_to_all x1, waiting for transfers between devices, shards(): lax.all_to_all(outer, AXES, split_axis=0, concat_axis=0, tiled=True, axis...  7.95 us
    ppermute x4, waiting for transfers between devices, spread(): lax.ppermute(held, AXES, [(d, d ^ bit) for d in range(devices)])  7.45 us
    ppermute x4, starting transfers between devices, spread(): lax.ppermute(held, AXES, [(d, d ^ bit) for d in range(devices)])  6.79 us
    ppermute x7, starting transfers between devices, send(): lax.ppermute(block, AXES, [(d, d ^ partner) for d in range(devices)])  5.91 us
    ppermute x1, starting transfers between devices, shards(): lax.ppermute(lax.dynamic_slice_in_dim(pair_rep, (1 - upper) * sz.columns,...  4.1 us
    all_to_all x1, starting transfers between devices, shards(): left = lax.all_to_all(left, AXES, split_axis=0, concat_axis=0, tiled=True)  4.04 us
  transfers between devices with their start and end apart: 14, of which 10 were waited for; matrix products, arithmetic and copies ran while one was open for 0% of the time, Pallas kernels for 7%

profile of v18, /device:TPU:0, one launch (start us, length us, event | category | flops | bytes accessed | tf_op | source)
XLA Modules:
  0.0 89.2 jit_solution(6366089463660318593)
XLA Ops:
  0.0 1.0 %constant_dynamic-slice_fusion = bf16[12,96,128]{2,1,0:T(8,128)(2,1)S(1)} fusion(bf16[12,192,128]{2,1,0:T(8,128)(2,1)} %refs_1_.6, s32[]{:T(128)S(6)} %select_n.3), kind=kLoop, calls=%fused_computation.3 | loop fusion | bytes 589828 | tf_op jit(solution)/shard_map/dynamic_slice | solution.py:388
  1.0 4.1 %collective-permute-start = (bf16[12,96,128]{2,1,0:T(8,128)(2,1)S(1)}, bf16[12,96,128]{2,1,0:T(8,128)(2,1)S(1)}, u32[]{:S(2)}, u32[]{:S(2)}) collective-permute-start(bf16[12,96,128]{2,1,0:T(8,128)(2,1)S(1)} %constant_dynamic-slice_fusion), channel_id=1, source_target_pairs={{0,8},{1,9},{2,10},{3,11},{4,12},{5,13},{6,14},{7,15},{8,0},{9,1},... | collective-permute-start | bytes 884744 | tf_op jit(solution)/shard_map/ppermute | solution.py:387
  5.8 1.1 %copy-done = bf16[12,192,128]{2,1,0:T(8,128)(2,1)S(1)} copy-done((bf16[12,192,128]{2,1,0:T(8,128)(2,1)S(1)}, bf16[12,192,128]{2,1,0:T(8,128)(2,1)}, u32[]{:S(2)}) %copy-start) | copy-done | bytes 589848
  6.8 0.9 %copy-done.2 = bf16[4,128,128]{2,1,0:T(8,128)(2,1)S(1)} copy-done((bf16[4,128,128]{2,1,0:T(8,128)(2,1)S(1)}, bf16[4,128,128]{2,1,0:T(8,128)(2,1)}, u32[]{:S(2)}) %copy-start.2) | copy-done | bytes 131096
  7.7 0.7 copy-done.11
  8.4 2.3 %left.1 = bf16[16,16,2304]{2,1,0:T(8,128)(2,1)} custom-call(s32[1]{0:T(128)S(6)} %copy.16.refs_0_, bf16[12,192,128]{2,1,0:T(8,128)(2,1)S(1)} %copy-done, f32[1,128]{1,0:T(1,128)S(1)} %bitcast.10, bf16[4,128,128]{2,1,0:T(8,128)(2,1)S(1)} %copy-done.2), custom_call_target="tpu_custom_call" | custom-call | tf_op jit(solution)/shard_map/left/pallas_call | solution.py:42
  10.6 4.0 %all-to-all-start = ((bf16[16,16,2304]{2,1,0:T(8,128)(2,1)}), bf16[16,16,2304]{2,1,0:T(8,128)(2,1)S(1)}, u32[]{:S(2)}, u32[]{:S(2)}) async-start(bf16[16,16,2304]{2,1,0:T(8,128)(2,1)} %left.1), calls=%async_computation | async-start | bytes 2359296 | tf_op jit(solution)/shard_map/all_to_all | solution.py:414
  14.7 3.8 %collective-permute-done.refs_2_ = bf16[12,96,128]{2,1,0:T(8,128)(2,1)S(1)} collective-permute-done((bf16[12,96,128]{2,1,0:T(8,128)(2,1)S(1)}, bf16[12,96,128]{2,1,0:T(8,128)(2,1)S(1)}, u32[]{:S(2)}, u32[]{:S(2)}) %collective-permute-start) | collective-permute-done | bytes 294944 | tf_op jit(solution)/shard_map/ppermute | solution.py:387
  18.5 1.4 %right.1 = (bf16[16,4608]{1,0:T(8,128)(2,1)S(1)}, bf16[16,4608]{1,0:T(8,128)(2,1)S(1)}, bf16[16,4608]{1,0:T(8,128)(2,1)S(1)}, bf16[16,4608]{1,0:T(8,128)(2,1)S(1...) custom-call(s32[1]{0:T(128)S(6)} %copy.16.refs_0_, ...), custom_call_target="tpu_custom_call" | custom-call | flops 99999997952 | bytes 1000000 | tf_op jit(solution)/shard_map/right/pallas_call | solution.py:42
  19.9 1.4 %collective-permute-start.1 = (bf16[16,4608]{1,0:T(8,128)(2,1)S(1)}, bf16[16,4608]{1,0:T(8,128)(2,1)S(1)}, u32[]{:S(2)}, u32[]{:S(2)}) collective-permute-start(bf16[16,4608]{1,0:T(8,128)(2,1)S(1)} %get-tuple-element.23), channel_id=1, source_target_pairs={{0,7},{1,6},{2,5},{3,4},{4,3},{5,2},{6,1},{7,0},{8,15},{9,14},{10,... | collective-permute-start | bytes 442376 | tf_op jit(solution)/shard_map/ppermute | solution.py:380
  21.4 0.8 collective-permute-start.2
  22.2 0.9 %collective-permute-start.3 = (bf16[16,4608]{1,0:T(8,128)(2,1)S(1)}, bf16[16,4608]{1,0:T(8,128)(2,1)S(1)}, u32[]{:S(2)}, u32[]{:S(2)}) collective-permute-start(bf16[16,4608]{1,0:T(8,128)(2,1)S(1)} %get-tuple-element.25), channel_id=1, source_target_pairs={{0,5},{1,4},{2,7},{3,6},{4,1},{5,0},{6,3},{7,2},{8,13},{9,12},{10,... | collective-permute-start | bytes 442376 | tf_op jit(solution)/shard_map/ppermute | solution.py:380
  23.1 1.3 %collective-permute-start.4 = (bf16[16,4608]{1,0:T(8,128)(2,1)S(1)}, bf16[16,4608]{1,0:T(8,128)(2,1)S(1)}, u32[]{:S(2)}, u32[]{:S(2)}) collective-permute-start(bf16[16,4608]{1,0:T(8,128)(2,1)S(1)} %get-tuple-element.26), channel_id=1, source_target_pairs={{0,4},{1,5},{2,6},{3,7},{4,0},{5,1},{6,2},{7,3},{8,12},{9,13},{10,... | collective-permute-start | bytes 442376 | tf_op jit(solution)/shard_map/ppermute | solution.py:380
  24.8 14.3 %collective-permute-done.1.refs_3_.refs_1_ = bf16[16,4608]{1,0:T(8,128)(2,1)S(1)} collective-permute-done((bf16[16,4608]{1,0:T(8,128)(2,1)S(1)}, bf16[16,4608]{1,0:T(8,128)(2,1)S(1)}, u32[]{:S(2)}, u32[]{:S(2)}) %collective-permute-start.1) | collective-permute-done | bytes 147488 | tf_op jit(solution)/shard_map/ppermute | solution.py:380
  39.1 1.0 %collective-permute-start.6 = (bf16[16,4608]{1,0:T(8,128)(2,1)S(1)}, bf16[16,4608]{1,0:T(8,128)(2,1)S(1)}, u32[]{:S(2)}, u32[]{:S(2)}) collective-permute-start(bf16[16,4608]{1,0:T(8,128)(2,1)S(1)} %get-tuple-element.28), channel_id=1, source_target_pairs={{0,2},{1,3},{2,0},{3,1},{4,6},{5,7},{6,4},{7,5},{8,10},{9,11},{10,... | collective-permute-start | bytes 442376 | tf_op jit(solution)/shard_map/ppermute | solution.py:380
  40.1 4.7 %collective-permute-done.2.refs_4_.refs_2_ = bf16[16,4608]{1,0:T(8,128)(2,1)S(1)} collective-permute-done((bf16[16,4608]{1,0:T(8,128)(2,1)S(1)}, bf16[16,4608]{1,0:T(8,128)(2,1)S(1)}, u32[]{:S(2)}, u32[]{:S(2)}) %collective-permute-start.2) | collective-permute-done | bytes 147488 | tf_op jit(solution)/shard_map/ppermute | solution.py:380
  44.9 2.0 %collective-permute-done.3.refs_5_.refs_3_ = bf16[16,4608]{1,0:T(8,128)(2,1)S(1)} collective-permute-done((bf16[16,4608]{1,0:T(8,128)(2,1)S(1)}, bf16[16,4608]{1,0:T(8,128)(2,1)S(1)}, u32[]{:S(2)}, u32[]{:S(2)}) %collective-permute-start.3) | collective-permute-done | bytes 147488 | tf_op jit(solution)/shard_map/ppermute | solution.py:380
  46.8 3.2 %collective-permute-done.4.refs_6_.refs_4_ = bf16[16,4608]{1,0:T(8,128)(2,1)S(1)} collective-permute-done((bf16[16,4608]{1,0:T(8,128)(2,1)S(1)}, bf16[16,4608]{1,0:T(8,128)(2,1)S(1)}, u32[]{:S(2)}, u32[]{:S(2)}) %collective-permute-start.4) | collective-permute-done | bytes 147488 | tf_op jit(solution)/shard_map/ppermute | solution.py:380
  50.1 0.7 arrange.1.refs_1_
  50.8 2.4 %outer.1 = bf16[8,16,2304]{2,1,0:T(8,128)(2,1)} custom-call(bf16[16,16,2304]{2,1,0:T(8,128)(2,1)S(1)} %all-to-all-done.refs_0_, bf16[16,96,192]{2,1,0:T(8,128)(2,1)S(1)} %arrange.1.refs_1_), custom_call_target="tpu_custom_call" | custom-call | tf_op jit(solution)/shard_map/outer/pallas_call | solution.py:42
  53.3 3.9 %all-to-all-start.1 = ((bf16[8,16,2304]{2,1,0:T(8,128)(2,1)}), bf16[8,16,2304]{2,1,0:T(8,128)(2,1)S(1)}, u32[]{:S(2)}, u32[]{:S(2)}) async-start(bf16[8,16,2304]{2,1,0:T(8,128)(2,1)} %outer.1), calls=%async_computation.1 | async-start | bytes 1179648 | tf_op jit(solution)/shard_map/all_to_all | solution.py:440
  57.3 1.2 %gating.1 = (bf16[12,192,128]{2,1,0:T(8,128)(2,1)S(1)}, bf16[12,192,128]{2,1,0:T(8,128)(2,1)S(1)}) custom-call(f32[1,128]{1,0:T(1,128)S(1)} %bitcast.12, bf16[128,128]{1,0:T(8,128)(2,1)S(1)} %copy-done.6, bf16[16,4608]{1,0:T(8,128)(2,1)S(1)} %get-tuple-element.22.refs_2_.refs_0_, bf16[16,4608]{1,0:T(8,128)(2,1)S(1)} %collective-permute-done.1.refs_3_.refs_1_, ...), custom_call_target="tpu_custom_call" | custom-call | tf_op jit(solution)/shard_map/gating/pallas_call | solution.py:42
  58.5 8.0 %all-to-all-done.1.refs_6_ = bf16[8,16,2304]{2,1,0:T(8,128)(2,1)S(1)} async-done(((bf16[8,16,2304]{2,1,0:T(8,128)(2,1)}), bf16[8,16,2304]{2,1,0:T(8,128)(2,1)S(1)}, u32[]{:S(2)}, u32[]{:S(2)}) %all-to-all-start.1) | async-done | bytes 589856 | tf_op jit(solution)/shard_map/all_to_all | solution.py:440
  66.5 2.6 %update.1 = (bf16[12,192,128]{2,1,0:T(8,128)(2,1)S(1)}, bf16[12,192,128]{2,1,0:T(8,128)(2,1)S(1)}, bf16[24,384]{1,0:T(8,128)(2,1)S(1)}) custom-call(bf16[12,192,128]{2,1,0:T(8,128)(2,1)S(1)} %get-tuple-element.30.refs_0_, bf16[12,192,128]{2,1,0:T(8,128)(2,1)S(1)} %get-tuple-element.31.refs_1_, f32[1,128]{1,0:T(1,128)S(1)} %bitcast.13, ...), custom_call_target="tpu_custom_call" | custom-call | tf_op jit(solution)/shard_map/update/pallas_call | solution.py:42
  69.1 3.5 %collective-permute-start.8 = (bf16[1,24,384]{2,1,0:T(8,128)(2,1)S(1)}, bf16[1,24,384]{2,1,0:T(8,128)(2,1)S(1)}, u32[]{:S(2)}, u32[]{:S(2)}) collective-permute-start(bf16[1,24,384]{2,1,0:T(8,128)(2,1)S(1)} %bitcast.5), channel_id=1, source_target_pairs={{0,8},{1,9},{2,10},{3,11},{4,12},{5,13},{6,14},{7,15},{8,0},{9,1},... | collective-permute-start | bytes 55304 | tf_op jit(solution)/shard_map/ppermute | solution.py:351
  72.6 1.7 %collective-permute-done.8.refs_8_ = bf16[1,24,384]{2,1,0:T(8,128)(2,1)S(1)} collective-permute-done((bf16[1,24,384]{2,1,0:T(8,128)(2,1)S(1)}, bf16[1,24,384]{2,1,0:T(8,128)(2,1)S(1)}, u32[]{:S(2)}, u32[]{:S(2)}) %collective-permute-start.8) | collective-permute-done | bytes 18464 | tf_op jit(solution)/shard_map/ppermute | solution.py:351
  74.3 1.5 %collective-permute-start.9 = (bf16[2,24,384]{2,1,0:T(8,128)(2,1)S(1)}, bf16[2,24,384]{2,1,0:T(8,128)(2,1)S(1)}, u32[]{:S(2)}, u32[]{:S(2)}) collective-permute-start(bf16[2,24,384]{2,1,0:T(8,128)(2,1)S(1)} %pad_maximum_fusion.2), channel_id=1, source_target_pairs={{0,4},{1,5},{2,6},{3,7},{4,0},{5,1},{6,2},{7,3},{8,12},{9,13},{10,... | collective-permute-start | bytes 110600 | tf_op jit(solution)/shard_map/ppermute | solution.py:351
  75.9 2.5 %collective-permute-done.9.refs_9_ = bf16[2,24,384]{2,1,0:T(8,128)(2,1)S(1)} collective-permute-done((bf16[2,24,384]{2,1,0:T(8,128)(2,1)S(1)}, bf16[2,24,384]{2,1,0:T(8,128)(2,1)S(1)}, u32[]{:S(2)}, u32[]{:S(2)}) %collective-permute-start.9) | collective-permute-done | bytes 36896 | tf_op jit(solution)/shard_map/ppermute | solution.py:351
  78.4 1.7 %collective-permute-start.10 = (bf16[4,24,384]{2,1,0:T(8,128)(2,1)S(1)}, bf16[4,24,384]{2,1,0:T(8,128)(2,1)S(1)}, u32[]{:S(2)}, u32[]{:S(2)}) collective-permute-start(bf16[4,24,384]{2,1,0:T(8,128)(2,1)S(1)} %pad_maximum_fusion.1), channel_id=1, source_target_pairs={{0,2},{1,3},{2,0},{3,1},{4,6},{5,7},{6,4},{7,5},{8,10},{9,11},{10,... | collective-permute-start | bytes 221192 | tf_op jit(solution)/shard_map/ppermute | solution.py:351
  80.1 2.7 %collective-permute-done.10.refs_10_ = bf16[4,24,384]{2,1,0:T(8,128)(2,1)S(1)} collective-permute-done((bf16[4,24,384]{2,1,0:T(8,128)(2,1)S(1)}, bf16[4,24,384]{2,1,0:T(8,128)(2,1)S(1)}, u32[]{:S(2)}, u32[]{:S(2)}) %collective-permute-start.10) | collective-permute-done | bytes 73760 | tf_op jit(solution)/shard_map/ppermute | solution.py:351
  82.9 0.8 project.1
  84.2 4.9 %attend.1 = bf16[12,192,128]{2,1,0:T(8,128)(2,1)} custom-call(s32[1]{0:T(128)S(6)} %copy.16.refs_0_, bf16[12,192,128]{2,1,0:T(8,128)(2,1)S(1)} %get-tuple-element.33.refs_1_, bf16[12,192,128]{2,1,0:T(8,128)(2,1)S(1)} %get-tuple-element.34.refs_2_, bf16[12,192,128]{2,1,0:T(8,128)(2,1)S(1)} %get-tuple-element.35.refs_3_, ...), custom_call_target="tpu_custom_call" | custom-call | tf_op jit(solution)/shard_map/attend/pallas_call | solution.py:42
  (41 shorter events, 1.3 us)
Async XLA Ops:
  1.0 17.5 %collective-permute-start = (bf16[12,96,128]{2,1,0:T(8,128)(2,1)S(1)}, bf16[12,96,128]{2,1,0:T(8,128)(2,1)S(1)}, u32[]{:S(2)}, u32[]{:S(2)}) collective-permute-start(bf16[12,96,128]{2,1,0:T(8,128)(2,1)S(1)} %constant_dynamic-slice_fusion), channel_id=1, source_target_pairs={{0,8},{1,9},{2,10},{3,11},{4,12},{5,13},{6,14},{7,15},{8,0},{9,1},... | collective-permute-start | bytes 884744 | tf_op jit(solution)/shard_map/ppermute | solution.py:387
  5.7 1.1 %copy-start = (bf16[12,192,128]{2,1,0:T(8,128)(2,1)S(1)}, bf16[12,192,128]{2,1,0:T(8,128)(2,1)}, u32[]{:S(2)}) copy-start(bf16[12,192,128]{2,1,0:T(8,128)(2,1)} %refs_1_.6) | copy-start | bytes 1769476
  6.8 0.9 %copy-start.2 = (bf16[4,128,128]{2,1,0:T(8,128)(2,1)S(1)}, bf16[4,128,128]{2,1,0:T(8,128)(2,1)}, u32[]{:S(2)}) copy-start(bf16[4,128,128]{2,1,0:T(8,128)(2,1)} %refs_3_.3) | copy-start | bytes 393220
  7.7 0.7 copy-start.11
  10.6 7.8 %copy-start.1 = (bf16[12,192,128]{2,1,0:T(8,128)(2,1)S(1)}, bf16[12,192,128]{2,1,0:T(8,128)(2,1)}, u32[]{:S(2)}) copy-start(bf16[12,192,128]{2,1,0:T(8,128)(2,1)} %refs_1_.6) | copy-start | bytes 1769476
  10.6 7.8 %copy-start.3 = (bf16[4,128,128]{2,1,0:T(8,128)(2,1)S(1)}, bf16[4,128,128]{2,1,0:T(8,128)(2,1)}, u32[]{:S(2)}) copy-start(bf16[4,128,128]{2,1,0:T(8,128)(2,1)} %refs_3_.3) | copy-start | bytes 393220
  10.6 7.8 %copy-start.12 = (f32[128]{0:T(128)S(1)}, f32[128]{0:T(128)}, u32[]{:S(2)}) copy-start(f32[128]{0:T(128)} %param.16) | copy-start | bytes 1540
  10.6 40.2 %all-to-all-start = ((bf16[16,16,2304]{2,1,0:T(8,128)(2,1)}), bf16[16,16,2304]{2,1,0:T(8,128)(2,1)S(1)}, u32[]{:S(2)}, u32[]{:S(2)}) async-start(bf16[16,16,2304]{2,1,0:T(8,128)(2,1)} %left.1), calls=%async_computation | async-start | bytes 2359296 | tf_op jit(solution)/shard_map/all_to_all | solution.py:414
  19.9 19.2 %collective-permute-start.1 = (bf16[16,4608]{1,0:T(8,128)(2,1)S(1)}, bf16[16,4608]{1,0:T(8,128)(2,1)S(1)}, u32[]{:S(2)}, u32[]{:S(2)}) collective-permute-start(bf16[16,4608]{1,0:T(8,128)(2,1)S(1)} %get-tuple-element.23), channel_id=1, source_target_pairs={{0,7},{1,6},{2,5},{3,4},{4,3},{5,2},{6,1},{7,0},{8,15},{9,14},{10,... | collective-permute-start | bytes 442376 | tf_op jit(solution)/shard_map/ppermute | solution.py:380
  21.4 23.5 %collective-permute-start.2 = (bf16[16,4608]{1,0:T(8,128)(2,1)S(1)}, bf16[16,4608]{1,0:T(8,128)(2,1)S(1)}, u32[]{:S(2)}, u32[]{:S(2)}) collective-permute-start(bf16[16,4608]{1,0:T(8,128)(2,1)S(1)} %get-tuple-element.24), channel_id=1, source_target_pairs={{0,6},{1,7},{2,4},{3,5},{4,2},{5,3},{6,0},{7,1},{8,14},{9,15},{10,... | collective-permute-start | bytes 442376 | tf_op jit(solution)/shard_map/ppermute | solution.py:380
  22.2 24.6 %collective-permute-start.3 = (bf16[16,4608]{1,0:T(8,128)(2,1)S(1)}, bf16[16,4608]{1,0:T(8,128)(2,1)S(1)}, u32[]{:S(2)}, u32[]{:S(2)}) collective-permute-start(bf16[16,4608]{1,0:T(8,128)(2,1)S(1)} %get-tuple-element.25), channel_id=1, source_target_pairs={{0,5},{1,4},{2,7},{3,6},{4,1},{5,0},{6,3},{7,2},{8,13},{9,12},{10,... | collective-permute-start | bytes 442376 | tf_op jit(solution)/shard_map/ppermute | solution.py:380
  23.1 26.9 %collective-permute-start.4 = (bf16[16,4608]{1,0:T(8,128)(2,1)S(1)}, bf16[16,4608]{1,0:T(8,128)(2,1)S(1)}, u32[]{:S(2)}, u32[]{:S(2)}) collective-permute-start(bf16[16,4608]{1,0:T(8,128)(2,1)S(1)} %get-tuple-element.26), channel_id=1, source_target_pairs={{0,4},{1,5},{2,6},{3,7},{4,0},{5,1},{6,2},{7,3},{8,12},{9,13},{10,... | collective-permute-start | bytes 442376 | tf_op jit(solution)/shard_map/ppermute | solution.py:380
  24.4 25.7 %collective-permute-start.5 = (bf16[16,4608]{1,0:T(8,128)(2,1)S(1)}, bf16[16,4608]{1,0:T(8,128)(2,1)S(1)}, u32[]{:S(2)}, u32[]{:S(2)}) collective-permute-start(bf16[16,4608]{1,0:T(8,128)(2,1)S(1)} %get-tuple-element.27), channel_id=1, source_target_pairs={{0,3},{1,2},{2,1},{3,0},{4,7},{5,6},{6,5},{7,4},{8,11},{9,10},{10,... | collective-permute-start | bytes 442376 | tf_op jit(solution)/shard_map/ppermute | solution.py:380
  39.1 11.0 %collective-permute-start.6 = (bf16[16,4608]{1,0:T(8,128)(2,1)S(1)}, bf16[16,4608]{1,0:T(8,128)(2,1)S(1)}, u32[]{:S(2)}, u32[]{:S(2)}) collective-permute-start(bf16[16,4608]{1,0:T(8,128)(2,1)S(1)} %get-tuple-element.28), channel_id=1, source_target_pairs={{0,2},{1,3},{2,0},{3,1},{4,6},{5,7},{6,4},{7,5},{8,10},{9,11},{10,... | collective-permute-start | bytes 442376 | tf_op jit(solution)/shard_map/ppermute | solution.py:380
  44.9 5.2 %collective-permute-start.7 = (bf16[16,4608]{1,0:T(8,128)(2,1)S(1)}, bf16[16,4608]{1,0:T(8,128)(2,1)S(1)}, u32[]{:S(2)}, u32[]{:S(2)}) collective-permute-start(bf16[16,4608]{1,0:T(8,128)(2,1)S(1)} %get-tuple-element.29), channel_id=1, source_target_pairs={{0,1},{1,0},{2,3},{3,2},{4,5},{5,4},{6,7},{7,6},{8,9},{9,8},{10,11... | collective-permute-start | bytes 442376 | tf_op jit(solution)/shard_map/ppermute | solution.py:380
  53.2 3.9 %copy-start.15 = (bf16[128,4]{0,1:T(4,128)(2,1)S(1)}, bf16[128,4]{0,1:T(4,128)(2,1)}, u32[]{:S(2)}) copy-start(bf16[128,4]{0,1:T(4,128)(2,1)} %param.25) | copy-start | bytes 3076
  53.2 4.0 %copy-start.6 = (bf16[128,128]{1,0:T(8,128)(2,1)S(1)}, bf16[128,128]{1,0:T(8,128)(2,1)}, u32[]{:S(2)}) copy-start(bf16[128,128]{1,0:T(8,128)(2,1)} %refs_1_.5) | copy-start | bytes 98308
  53.2 13.2 %copy-start.4 = (bf16[128,128]{1,0:T(8,128)(2,1)S(1)}, bf16[128,128]{1,0:T(8,128)(2,1)}, u32[]{:S(2)}) copy-start(bf16[128,128]{1,0:T(8,128)(2,1)} %refs_3_.4) | copy-start | bytes 98308
  53.2 13.2 %copy-start.13 = (f32[128]{0:T(128)S(1)}, f32[128]{0:T(128)}, u32[]{:S(2)}) copy-start(f32[128]{0:T(128)} %param.19) | copy-start | bytes 1540
  53.3 13.2 %copy-start.14 = (f32[128]{0:T(128)S(1)}, f32[128]{0:T(128)}, u32[]{:S(2)}) copy-start(f32[128]{0:T(128)} %param.21) | copy-start | bytes 1540
  53.3 13.2 %all-to-all-start.1 = ((bf16[8,16,2304]{2,1,0:T(8,128)(2,1)}), bf16[8,16,2304]{2,1,0:T(8,128)(2,1)S(1)}, u32[]{:S(2)}, u32[]{:S(2)}) async-start(bf16[8,16,2304]{2,1,0:T(8,128)(2,1)} %outer.1), calls=%async_computation.1 | async-start | bytes 1179648 | tf_op jit(solution)/shard_map/all_to_all | solution.py:440
  66.4 16.5 %copy-start.7 = (bf16[128,128]{1,0:T(8,128)(2,1)S(1)}, bf16[128,128]{1,0:T(8,128)(2,1)}, u32[]{:S(2)}) copy-start(bf16[128,128]{1,0:T(8,128)(2,1)} %refs_1_.7) | copy-start | bytes 98308
  66.4 16.5 %copy-start.8 = (bf16[128,128]{1,0:T(8,128)(2,1)S(1)}, bf16[128,128]{1,0:T(8,128)(2,1)}, u32[]{:S(2)}) copy-start(bf16[128,128]{1,0:T(8,128)(2,1)} %refs_2_.1) | copy-start | bytes 98308
  66.4 16.5 %copy-start.9 = (bf16[128,128]{1,0:T(8,128)(2,1)S(1)}, bf16[128,128]{1,0:T(8,128)(2,1)}, u32[]{:S(2)}) copy-start(bf16[128,128]{1,0:T(8,128)(2,1)} %refs_3_.5) | copy-start | bytes 98308
  66.4 16.5 %copy-start.10 = (bf16[128,128]{1,0:T(8,128)(2,1)S(1)}, bf16[128,128]{1,0:T(8,128)(2,1)}, u32[]{:S(2)}) copy-start(bf16[128,128]{1,0:T(8,128)(2,1)} %refs_4_.3) | copy-start | bytes 98308
  66.5 17.8 %copy-start.5 = (bf16[128,128]{1,0:T(8,128)(2,1)S(1)}, bf16[128,128]{1,0:T(8,128)(2,1)}, u32[]{:S(2)}) copy-start(bf16[128,128]{1,0:T(8,128)(2,1)} %refs_6_.1) | copy-start | bytes 98308
  69.1 5.2 %collective-permute-start.8 = (bf16[1,24,384]{2,1,0:T(8,128)(2,1)S(1)}, bf16[1,24,384]{2,1,0:T(8,128)(2,1)S(1)}, u32[]{:S(2)}, u32[]{:S(2)}) collective-permute-start(bf16[1,24,384]{2,1,0:T(8,128)(2,1)S(1)} %bitcast.5), channel_id=1, source_target_pairs={{0,8},{1,9},{2,10},{3,11},{4,12},{5,13},{6,14},{7,15},{8,0},{9,1},... | collective-permute-start | bytes 55304 | tf_op jit(solution)/shard_map/ppermute | solution.py:351
  74.3 4.0 %collective-permute-start.9 = (bf16[2,24,384]{2,1,0:T(8,128)(2,1)S(1)}, bf16[2,24,384]{2,1,0:T(8,128)(2,1)S(1)}, u32[]{:S(2)}, u32[]{:S(2)}) collective-permute-start(bf16[2,24,384]{2,1,0:T(8,128)(2,1)S(1)} %pad_maximum_fusion.2), channel_id=1, source_target_pairs={{0,4},{1,5},{2,6},{3,7},{4,0},{5,1},{6,2},{7,3},{8,12},{9,13},{10,... | collective-permute-start | bytes 110600 | tf_op jit(solution)/shard_map/ppermute | solution.py:351
  78.4 4.4 %collective-permute-start.10 = (bf16[4,24,384]{2,1,0:T(8,128)(2,1)S(1)}, bf16[4,24,384]{2,1,0:T(8,128)(2,1)S(1)}, u32[]{:S(2)}, u32[]{:S(2)}) collective-permute-start(bf16[4,24,384]{2,1,0:T(8,128)(2,1)S(1)} %pad_maximum_fusion.1), channel_id=1, source_target_pairs={{0,2},{1,3},{2,0},{3,1},{4,6},{5,7},{6,4},{7,5},{8,10},{9,11},{10,... | collective-permute-start | bytes 221192 | tf_op jit(solution)/shard_map/ppermute | solution.py:351
  82.8 1.4 %collective-permute-start.11 = (bf16[8,24,384]{2,1,0:T(8,128)(2,1)S(1)}, bf16[8,24,384]{2,1,0:T(8,128)(2,1)S(1)}, u32[]{:S(2)}, u32[]{:S(2)}) collective-permute-start(bf16[8,24,384]{2,1,0:T(8,128)(2,1)S(1)} %pad_maximum_fusion), channel_id=1, source_target_pairs={{0,1},{1,0},{2,3},{3,2},{4,5},{5,4},{6,7},{7,6},{8,9},{9,8},{10,11... | collective-permute-start | bytes 442376 | tf_op jit(solution)/shard_map/ppermute | solution.py:351

commit v19 on v18

--- a/solution.py
+++ b/solution.py
@@ -189,7 +189,7 @@
 
 
 def outer_kernel(
-    sz, left_ref, right_ref, out_ref, lmain_ref, lrest_ref, omain_ref, orest_ref
+    sz, left_ref, right_ref, away_ref, out_ref, lmain_ref, lrest_ref, omain_ref, orest_ref, sems
 ):
     cd, n, w, half = sz.chans, sz.crop, sz.whole, sz.half
     for d in range(sz.devices):
@@ -202,6 +202,9 @@
             part = outer[:, w * LANES :]
             orest_ref[pl.ds(c, sz.columns, stride=cd), :] = jnp.concatenate([part, part], axis=1)
     low = lax.broadcasted_iota(jnp.int32, (cd, LANES), 1) < sz.rest
+    copies = [
+        pltpu.make_async_copy(out_ref.at[g], away_ref.at[g], sems.at[g]) for g in range(sz.group)
+    ]
     for g in range(sz.group):
         start = g * sz.rows
         for tile in range(sz.tiles):
@@ -216,6 +219,9 @@
                     orest_ref[pl.ds((at + half) * cd, cd), :],
                 )
             out_ref[g, :, tile * LANES : (tile + 1) * LANES] = block.astype(BF16)
+        copies[g].start()
+    for copy in copies:
+        copy.wait()
 
 
 def take_columns(sz, near, cols_ref):
@@ -290,7 +296,7 @@
 def attend_kernel(
     sz, heads, steps, len_ref, q_ref, k_ref, v_ref, g_ref, first_ref, aout_ref, *refs
 ):
-    bias_refs, (out_ref, rows_ref, bias_ref) = refs[:-3], refs[-3:]
+    bias_refs, (away_ref, out_ref, rows_ref, bias_ref, sems) = refs[:-5], refs[-5:]
     n, w, ch = sz.crop, sz.whole, sz.channels
     length, me = len_ref[0], position()
     width = q_ref.shape[2]
@@ -322,6 +328,9 @@
         query = [q_ref[j] * head_masks[h].astype(BF16) for h in range(heads)]
         return dot(jnp.concatenate(query, axis=0), k_ref[j], 1, 1)
 
+    copies = [
+        pltpu.make_async_copy(out_ref.at[j], away_ref.at[j], sems.at[j]) for j in range(sz.rows)
+    ]
     scores = score(0)
     for j in range(sz.rows):
         now = scores
@@ -340,6 +349,9 @@
             total = jnp.where(head_masks[h], mixed[rows, width:], total)
         gated = (attended / total * g_ref[j]).astype(BF16)
         out_ref[j] = (first_ref[j].astype(F32) + dot(gated, aout_ref[...], 1, 0)).astype(BF16)
+        copies[j].start()
+    for copy in copies:
+        copy.wait()
 
 
 def spread(block, devices):
@@ -430,11 +442,14 @@
         slab(t, g),
         (left, right),
         scratch=[
+            pltpu.VMEM((g, cd, t * LANES), BF16),
             pltpu.VMEM((sz.whole, n * cd, LANES), F32),
             pltpu.VMEM((n * cd if rest else 8, LANES), F32),
             pltpu.VMEM((sz.whole, column_rows, LANES), F32),
             pltpu.VMEM((column_rows if rest else 8, LANES), F32),
+            pltpu.SemaphoreType.DMA((g,)),
         ],
+        away=True,
         name="outer",
     )
     sums = lax.all_to_all(
@@ -478,10 +493,13 @@
         shape((rows, n, ch), BF16),
         (length, query, key, value, gate, first, att_out, *pieces),
         scratch=[
+            pltpu.VMEM((rows, n, ch), BF16),
             pltpu.VMEM((-(-n // LANES), n * heads, LANES), F32),
             pltpu.VMEM((heads, n, n), F32),
+            pltpu.SemaphoreType.DMA((rows,)),
         ],
         smem=(0,),
+        away=True,
         name="attend",
     )
     return jnp.swapaxes(out, 0, 1)

time: 89.6 us -> 89.7 us (level)
  no operation moved by 1% of the time
where the time goes in v19:
time: 89.7 us; the launch traced here: 89.3 us
  waiting for transfers between devices  43.4 us (48%)
  starting transfers between devices  24.7 us (28%)
  Pallas kernels  16.3 us (18%)
  local copies, waits for them, and re-layouts  3.8 us (4%)
  between operations  1.04 us (1%)
    ppermute x7, waiting for transfers between devices, send(): lax.ppermute(block, AXES, [(d, d ^ partner) for d in range(devices)])  24.2 us
    pallas_call x8, Pallas kernels, call(): pl.pallas_call(kernel, out_shape=out_shape, in_specs=specs, out_specs=ins...  16.3 us
    all_to_all x1, waiting for transfers between devices, shards(): lax.all_to_all(outer, AXES, split_axis=0, concat_axis=0, tiled=True, axis...  7.95 us
    ppermute x4, waiting for transfers between devices, spread(): lax.ppermute(held, AXES, [(d, d ^ bit) for d in range(devices)])  7.45 us
    ppermute x4, starting transfers between devices, spread(): lax.ppermute(held, AXES, [(d, d ^ bit) for d in range(devices)])  6.79 us
    ppermute x7, starting transfers between devices, send(): lax.ppermute(block, AXES, [(d, d ^ partner) for d in range(devices)])  5.91 us
    ppermute x1, starting transfers between devices, shards(): lax.ppermute(lax.dynamic_slice_in_dim(pair_rep, (1 - upper) * sz.columns,...  4.1 us
    all_to_all x1, starting transfers between devices, shards(): left = lax.all_to_all(left, AXES, split_axis=0, concat_axis=0, tiled=True)  4.04 us
  transfers between devices with their start and end apart: 14, of which 10 were waited for; matrix products, arithmetic and copies ran while one was open for 0% of the time, Pallas kernels for 7%

profile of v19, /device:TPU:0, one launch (start us, length us, event | category | flops | bytes accessed | tf_op | source)
XLA Modules:
  0.0 89.3 jit_solution(16097782585852375618)
XLA Ops:
  0.0 1.0 %constant_dynamic-slice_fusion = bf16[12,96,128]{2,1,0:T(8,128)(2,1)S(1)} fusion(bf16[12,192,128]{2,1,0:T(8,128)(2,1)} %refs_1_.6, s32[]{:T(128)S(6)} %select_n.3), kind=kLoop, calls=%fused_computation.3 | loop fusion | bytes 589828 | tf_op jit(solution)/shard_map/dynamic_slice | solution.py:400
  1.0 4.1 %collective-permute-start = (bf16[12,96,128]{2,1,0:T(8,128)(2,1)S(1)}, bf16[12,96,128]{2,1,0:T(8,128)(2,1)S(1)}, u32[]{:S(2)}, u32[]{:S(2)}) collective-permute-start(bf16[12,96,128]{2,1,0:T(8,128)(2,1)S(1)} %constant_dynamic-slice_fusion), channel_id=1, source_target_pairs={{0,8},{1,9},{2,10},{3,11},{4,12},{5,13},{6,14},{7,15},{8,0},{9,1},... | collective-permute-start | bytes 884744 | tf_op jit(solution)/shard_map/ppermute | solution.py:399
  5.8 1.1 %copy-done = bf16[12,192,128]{2,1,0:T(8,128)(2,1)S(1)} copy-done((bf16[12,192,128]{2,1,0:T(8,128)(2,1)S(1)}, bf16[12,192,128]{2,1,0:T(8,128)(2,1)}, u32[]{:S(2)}) %copy-start) | copy-done | bytes 589848
  6.8 0.9 %copy-done.2 = bf16[4,128,128]{2,1,0:T(8,128)(2,1)S(1)} copy-done((bf16[4,128,128]{2,1,0:T(8,128)(2,1)S(1)}, bf16[4,128,128]{2,1,0:T(8,128)(2,1)}, u32[]{:S(2)}) %copy-start.2) | copy-done | bytes 131096
  7.7 0.7 copy-done.11
  8.4 2.3 %left.1 = bf16[16,16,2304]{2,1,0:T(8,128)(2,1)} custom-call(s32[1]{0:T(128)S(6)} %copy.16.refs_0_, bf16[12,192,128]{2,1,0:T(8,128)(2,1)S(1)} %copy-done, f32[1,128]{1,0:T(1,128)S(1)} %bitcast.10, bf16[4,128,128]{2,1,0:T(8,128)(2,1)S(1)} %copy-done.2), custom_call_target="tpu_custom_call" | custom-call | tf_op jit(solution)/shard_map/left/pallas_call | solution.py:42
  10.6 4.0 %all-to-all-start = ((bf16[16,16,2304]{2,1,0:T(8,128)(2,1)}), bf16[16,16,2304]{2,1,0:T(8,128)(2,1)S(1)}, u32[]{:S(2)}, u32[]{:S(2)}) async-start(bf16[16,16,2304]{2,1,0:T(8,128)(2,1)} %left.1), calls=%async_computation | async-start | bytes 2359296 | tf_op jit(solution)/shard_map/all_to_all | solution.py:426
  14.7 3.8 %collective-permute-done.refs_2_ = bf16[12,96,128]{2,1,0:T(8,128)(2,1)S(1)} collective-permute-done((bf16[12,96,128]{2,1,0:T(8,128)(2,1)S(1)}, bf16[12,96,128]{2,1,0:T(8,128)(2,1)S(1)}, u32[]{:S(2)}, u32[]{:S(2)}) %collective-permute-start) | collective-permute-done | bytes 294944 | tf_op jit(solution)/shard_map/ppermute | solution.py:399
  18.5 1.4 %right.1 = (bf16[16,4608]{1,0:T(8,128)(2,1)S(1)}, bf16[16,4608]{1,0:T(8,128)(2,1)S(1)}, bf16[16,4608]{1,0:T(8,128)(2,1)S(1)}, bf16[16,4608]{1,0:T(8,128)(2,1)S(1...) custom-call(s32[1]{0:T(128)S(6)} %copy.16.refs_0_, ...), custom_call_target="tpu_custom_call" | custom-call | flops 99999997952 | bytes 1000000 | tf_op jit(solution)/shard_map/right/pallas_call | solution.py:42
  19.9 1.4 %collective-permute-start.1 = (bf16[16,4608]{1,0:T(8,128)(2,1)S(1)}, bf16[16,4608]{1,0:T(8,128)(2,1)S(1)}, u32[]{:S(2)}, u32[]{:S(2)}) collective-permute-start(bf16[16,4608]{1,0:T(8,128)(2,1)S(1)} %get-tuple-element.23), channel_id=1, source_target_pairs={{0,7},{1,6},{2,5},{3,4},{4,3},{5,2},{6,1},{7,0},{8,15},{9,14},{10,... | collective-permute-start | bytes 442376 | tf_op jit(solution)/shard_map/ppermute | solution.py:392
  21.4 0.8 collective-permute-start.2
  22.2 0.9 %collective-permute-start.3 = (bf16[16,4608]{1,0:T(8,128)(2,1)S(1)}, bf16[16,4608]{1,0:T(8,128)(2,1)S(1)}, u32[]{:S(2)}, u32[]{:S(2)}) collective-permute-start(bf16[16,4608]{1,0:T(8,128)(2,1)S(1)} %get-tuple-element.25), channel_id=1, source_target_pairs={{0,5},{1,4},{2,7},{3,6},{4,1},{5,0},{6,3},{7,2},{8,13},{9,12},{10,... | collective-permute-start | bytes 442376 | tf_op jit(solution)/shard_map/ppermute | solution.py:392
  23.1 1.3 %collective-permute-start.4 = (bf16[16,4608]{1,0:T(8,128)(2,1)S(1)}, bf16[16,4608]{1,0:T(8,128)(2,1)S(1)}, u32[]{:S(2)}, u32[]{:S(2)}) collective-permute-start(bf16[16,4608]{1,0:T(8,128)(2,1)S(1)} %get-tuple-element.26), channel_id=1, source_target_pairs={{0,4},{1,5},{2,6},{3,7},{4,0},{5,1},{6,2},{7,3},{8,12},{9,13},{10,... | collective-permute-start | bytes 442376 | tf_op jit(solution)/shard_map/ppermute | solution.py:392
  24.8 14.3 %collective-permute-done.1.refs_3_.refs_1_ = bf16[16,4608]{1,0:T(8,128)(2,1)S(1)} collective-permute-done((bf16[16,4608]{1,0:T(8,128)(2,1)S(1)}, bf16[16,4608]{1,0:T(8,128)(2,1)S(1)}, u32[]{:S(2)}, u32[]{:S(2)}) %collective-permute-start.1) | collective-permute-done | bytes 147488 | tf_op jit(solution)/shard_map/ppermute | solution.py:392
  39.1 1.0 %collective-permute-start.6 = (bf16[16,4608]{1,0:T(8,128)(2,1)S(1)}, bf16[16,4608]{1,0:T(8,128)(2,1)S(1)}, u32[]{:S(2)}, u32[]{:S(2)}) collective-permute-start(bf16[16,4608]{1,0:T(8,128)(2,1)S(1)} %get-tuple-element.28), channel_id=1, source_target_pairs={{0,2},{1,3},{2,0},{3,1},{4,6},{5,7},{6,4},{7,5},{8,10},{9,11},{10,... | collective-permute-start | bytes 442376 | tf_op jit(solution)/shard_map/ppermute | solution.py:392
  40.1 4.7 %collective-permute-done.2.refs_4_.refs_2_ = bf16[16,4608]{1,0:T(8,128)(2,1)S(1)} collective-permute-done((bf16[16,4608]{1,0:T(8,128)(2,1)S(1)}, bf16[16,4608]{1,0:T(8,128)(2,1)S(1)}, u32[]{:S(2)}, u32[]{:S(2)}) %collective-permute-start.2) | collective-permute-done | bytes 147488 | tf_op jit(solution)/shard_map/ppermute | solution.py:392
  44.9 2.0 %collective-permute-done.3.refs_5_.refs_3_ = bf16[16,4608]{1,0:T(8,128)(2,1)S(1)} collective-permute-done((bf16[16,4608]{1,0:T(8,128)(2,1)S(1)}, bf16[16,4608]{1,0:T(8,128)(2,1)S(1)}, u32[]{:S(2)}, u32[]{:S(2)}) %collective-permute-start.3) | collective-permute-done | bytes 147488 | tf_op jit(solution)/shard_map/ppermute | solution.py:392
  46.8 3.2 %collective-permute-done.4.refs_6_.refs_4_ = bf16[16,4608]{1,0:T(8,128)(2,1)S(1)} collective-permute-done((bf16[16,4608]{1,0:T(8,128)(2,1)S(1)}, bf16[16,4608]{1,0:T(8,128)(2,1)S(1)}, u32[]{:S(2)}, u32[]{:S(2)}) %collective-permute-start.4) | collective-permute-done | bytes 147488 | tf_op jit(solution)/shard_map/ppermute | solution.py:392
  50.1 0.7 arrange.1.refs_1_
  50.8 2.4 %outer.1 = bf16[8,16,2304]{2,1,0:T(8,128)(2,1)} custom-call(bf16[16,16,2304]{2,1,0:T(8,128)(2,1)S(1)} %all-to-all-done.refs_0_, bf16[16,96,192]{2,1,0:T(8,128)(2,1)S(1)} %arrange.1.refs_1_), custom_call_target="tpu_custom_call" | custom-call | tf_op jit(solution)/shard_map/outer/pallas_call | solution.py:42
  53.3 3.9 %all-to-all-start.1 = ((bf16[8,16,2304]{2,1,0:T(8,128)(2,1)}), bf16[8,16,2304]{2,1,0:T(8,128)(2,1)S(1)}, u32[]{:S(2)}, u32[]{:S(2)}) async-start(bf16[8,16,2304]{2,1,0:T(8,128)(2,1)} %outer.1), calls=%async_computation.1 | async-start | bytes 1179648 | tf_op jit(solution)/shard_map/all_to_all | solution.py:455
  57.3 1.2 %gating.1 = (bf16[12,192,128]{2,1,0:T(8,128)(2,1)S(1)}, bf16[12,192,128]{2,1,0:T(8,128)(2,1)S(1)}) custom-call(f32[1,128]{1,0:T(1,128)S(1)} %bitcast.12, bf16[128,128]{1,0:T(8,128)(2,1)S(1)} %copy-done.6, bf16[16,4608]{1,0:T(8,128)(2,1)S(1)} %get-tuple-element.22.refs_2_.refs_0_, bf16[16,4608]{1,0:T(8,128)(2,1)S(1)} %collective-permute-done.1.refs_3_.refs_1_, ...), custom_call_target="tpu_custom_call" | custom-call | tf_op jit(solution)/shard_map/gating/pallas_call | solution.py:42
  58.5 8.0 %all-to-all-done.1.refs_6_ = bf16[8,16,2304]{2,1,0:T(8,128)(2,1)S(1)} async-done(((bf16[8,16,2304]{2,1,0:T(8,128)(2,1)}), bf16[8,16,2304]{2,1,0:T(8,128)(2,1)S(1)}, u32[]{:S(2)}, u32[]{:S(2)}) %all-to-all-start.1) | async-done | bytes 589856 | tf_op jit(solution)/shard_map/all_to_all | solution.py:455
  66.5 2.6 %update.1 = (bf16[12,192,128]{2,1,0:T(8,128)(2,1)S(1)}, bf16[12,192,128]{2,1,0:T(8,128)(2,1)S(1)}, bf16[24,384]{1,0:T(8,128)(2,1)S(1)}) custom-call(bf16[12,192,128]{2,1,0:T(8,128)(2,1)S(1)} %get-tuple-element.30.refs_0_, bf16[12,192,128]{2,1,0:T(8,128)(2,1)S(1)} %get-tuple-element.31.refs_1_, f32[1,128]{1,0:T(1,128)S(1)} %bitcast.13, ...), custom_call_target="tpu_custom_call" | custom-call | tf_op jit(solution)/shard_map/update/pallas_call | solution.py:42
  69.2 3.5 %collective-permute-start.8 = (bf16[1,24,384]{2,1,0:T(8,128)(2,1)S(1)}, bf16[1,24,384]{2,1,0:T(8,128)(2,1)S(1)}, u32[]{:S(2)}, u32[]{:S(2)}) collective-permute-start(bf16[1,24,384]{2,1,0:T(8,128)(2,1)S(1)} %bitcast.5), channel_id=1, source_target_pairs={{0,8},{1,9},{2,10},{3,11},{4,12},{5,13},{6,14},{7,15},{8,0},{9,1},... | collective-permute-start | bytes 55304 | tf_op jit(solution)/shard_map/ppermute | solution.py:363
  72.6 1.7 %collective-permute-done.8.refs_8_ = bf16[1,24,384]{2,1,0:T(8,128)(2,1)S(1)} collective-permute-done((bf16[1,24,384]{2,1,0:T(8,128)(2,1)S(1)}, bf16[1,24,384]{2,1,0:T(8,128)(2,1)S(1)}, u32[]{:S(2)}, u32[]{:S(2)}) %collective-permute-start.8) | collective-permute-done | bytes 18464 | tf_op jit(solution)/shard_map/ppermute | solution.py:363
  74.4 1.5 %collective-permute-start.9 = (bf16[2,24,384]{2,1,0:T(8,128)(2,1)S(1)}, bf16[2,24,384]{2,1,0:T(8,128)(2,1)S(1)}, u32[]{:S(2)}, u32[]{:S(2)}) collective-permute-start(bf16[2,24,384]{2,1,0:T(8,128)(2,1)S(1)} %pad_maximum_fusion.2), channel_id=1, source_target_pairs={{0,4},{1,5},{2,6},{3,7},{4,0},{5,1},{6,2},{7,3},{8,12},{9,13},{10,... | collective-permute-start | bytes 110600 | tf_op jit(solution)/shard_map/ppermute | solution.py:363
  75.9 2.5 %collective-permute-done.9.refs_9_ = bf16[2,24,384]{2,1,0:T(8,128)(2,1)S(1)} collective-permute-done((bf16[2,24,384]{2,1,0:T(8,128)(2,1)S(1)}, bf16[2,24,384]{2,1,0:T(8,128)(2,1)S(1)}, u32[]{:S(2)}, u32[]{:S(2)}) %collective-permute-start.9) | collective-permute-done | bytes 36896 | tf_op jit(solution)/shard_map/ppermute | solution.py:363
  78.4 1.7 %collective-permute-start.10 = (bf16[4,24,384]{2,1,0:T(8,128)(2,1)S(1)}, bf16[4,24,384]{2,1,0:T(8,128)(2,1)S(1)}, u32[]{:S(2)}, u32[]{:S(2)}) collective-permute-start(bf16[4,24,384]{2,1,0:T(8,128)(2,1)S(1)} %pad_maximum_fusion.1), channel_id=1, source_target_pairs={{0,2},{1,3},{2,0},{3,1},{4,6},{5,7},{6,4},{7,5},{8,10},{9,11},{10,... | collective-permute-start | bytes 221192 | tf_op jit(solution)/shard_map/ppermute | solution.py:363
  80.1 2.7 %collective-permute-done.10.refs_10_ = bf16[4,24,384]{2,1,0:T(8,128)(2,1)S(1)} collective-permute-done((bf16[4,24,384]{2,1,0:T(8,128)(2,1)S(1)}, bf16[4,24,384]{2,1,0:T(8,128)(2,1)S(1)}, u32[]{:S(2)}, u32[]{:S(2)}) %collective-permute-start.10) | collective-permute-done | bytes 73760 | tf_op jit(solution)/shard_map/ppermute | solution.py:363
  83.0 0.8 project.1
  84.3 4.8 %attend.1 = bf16[12,192,128]{2,1,0:T(8,128)(2,1)} custom-call(s32[1]{0:T(128)S(6)} %copy.16.refs_0_, bf16[12,192,128]{2,1,0:T(8,128)(2,1)S(1)} %get-tuple-element.33.refs_1_, bf16[12,192,128]{2,1,0:T(8,128)(2,1)S(1)} %get-tuple-element.34.refs_2_, bf16[12,192,128]{2,1,0:T(8,128)(2,1)S(1)} %get-tuple-element.35.refs_3_, ...), custom_call_target="tpu_custom_call" | custom-call | tf_op jit(solution)/shard_map/attend/pallas_call | solution.py:42
  (41 shorter events, 1.3 us)
Async XLA Ops:
  1.0 17.5 %collective-permute-start = (bf16[12,96,128]{2,1,0:T(8,128)(2,1)S(1)}, bf16[12,96,128]{2,1,0:T(8,128)(2,1)S(1)}, u32[]{:S(2)}, u32[]{:S(2)}) collective-permute-start(bf16[12,96,128]{2,1,0:T(8,128)(2,1)S(1)} %constant_dynamic-slice_fusion), channel_id=1, source_target_pairs={{0,8},{1,9},{2,10},{3,11},{4,12},{5,13},{6,14},{7,15},{8,0},{9,1},... | collective-permute-start | bytes 884744 | tf_op jit(solution)/shard_map/ppermute | solution.py:399
  5.7 1.1 %copy-start = (bf16[12,192,128]{2,1,0:T(8,128)(2,1)S(1)}, bf16[12,192,128]{2,1,0:T(8,128)(2,1)}, u32[]{:S(2)}) copy-start(bf16[12,192,128]{2,1,0:T(8,128)(2,1)} %refs_1_.6) | copy-start | bytes 1769476
  6.8 0.9 %copy-start.2 = (bf16[4,128,128]{2,1,0:T(8,128)(2,1)S(1)}, bf16[4,128,128]{2,1,0:T(8,128)(2,1)}, u32[]{:S(2)}) copy-start(bf16[4,128,128]{2,1,0:T(8,128)(2,1)} %refs_3_.3) | copy-start | bytes 393220
  7.7 0.7 copy-start.11
  10.6 7.8 %copy-start.1 = (bf16[12,192,128]{2,1,0:T(8,128)(2,1)S(1)}, bf16[12,192,128]{2,1,0:T(8,128)(2,1)}, u32[]{:S(2)}) copy-start(bf16[12,192,128]{2,1,0:T(8,128)(2,1)} %refs_1_.6) | copy-start | bytes 1769476
  10.6 7.8 %copy-start.3 = (bf16[4,128,128]{2,1,0:T(8,128)(2,1)S(1)}, bf16[4,128,128]{2,1,0:T(8,128)(2,1)}, u32[]{:S(2)}) copy-start(bf16[4,128,128]{2,1,0:T(8,128)(2,1)} %refs_3_.3) | copy-start | bytes 393220
  10.6 7.8 %copy-start.12 = (f32[128]{0:T(128)S(1)}, f32[128]{0:T(128)}, u32[]{:S(2)}) copy-start(f32[128]{0:T(128)} %param.16) | copy-start | bytes 1540
  10.6 40.2 %all-to-all-start = ((bf16[16,16,2304]{2,1,0:T(8,128)(2,1)}), bf16[16,16,2304]{2,1,0:T(8,128)(2,1)S(1)}, u32[]{:S(2)}, u32[]{:S(2)}) async-start(bf16[16,16,2304]{2,1,0:T(8,128)(2,1)} %left.1), calls=%async_computation | async-start | bytes 2359296 | tf_op jit(solution)/shard_map/all_to_all | solution.py:426
  19.9 19.2 %collective-permute-start.1 = (bf16[16,4608]{1,0:T(8,128)(2,1)S(1)}, bf16[16,4608]{1,0:T(8,128)(2,1)S(1)}, u32[]{:S(2)}, u32[]{:S(2)}) collective-permute-start(bf16[16,4608]{1,0:T(8,128)(2,1)S(1)} %get-tuple-element.23), channel_id=1, source_target_pairs={{0,7},{1,6},{2,5},{3,4},{4,3},{5,2},{6,1},{7,0},{8,15},{9,14},{10,... | collective-permute-start | bytes 442376 | tf_op jit(solution)/shard_map/ppermute | solution.py:392
  21.4 23.5 %collective-permute-start.2 = (bf16[16,4608]{1,0:T(8,128)(2,1)S(1)}, bf16[16,4608]{1,0:T(8,128)(2,1)S(1)}, u32[]{:S(2)}, u32[]{:S(2)}) collective-permute-start(bf16[16,4608]{1,0:T(8,128)(2,1)S(1)} %get-tuple-element.24), channel_id=1, source_target_pairs={{0,6},{1,7},{2,4},{3,5},{4,2},{5,3},{6,0},{7,1},{8,14},{9,15},{10,... | collective-permute-start | bytes 442376 | tf_op jit(solution)/shard_map/ppermute | solution.py:392
  22.2 24.6 %collective-permute-start.3 = (bf16[16,4608]{1,0:T(8,128)(2,1)S(1)}, bf16[16,4608]{1,0:T(8,128)(2,1)S(1)}, u32[]{:S(2)}, u32[]{:S(2)}) collective-permute-start(bf16[16,4608]{1,0:T(8,128)(2,1)S(1)} %get-tuple-element.25), channel_id=1, source_target_pairs={{0,5},{1,4},{2,7},{3,6},{4,1},{5,0},{6,3},{7,2},{8,13},{9,12},{10,... | collective-permute-start | bytes 442376 | tf_op jit(solution)/shard_map/ppermute | solution.py:392
  23.1 26.9 %collective-permute-start.4 = (bf16[16,4608]{1,0:T(8,128)(2,1)S(1)}, bf16[16,4608]{1,0:T(8,128)(2,1)S(1)}, u32[]{:S(2)}, u32[]{:S(2)}) collective-permute-start(bf16[16,4608]{1,0:T(8,128)(2,1)S(1)} %get-tuple-element.26), channel_id=1, source_target_pairs={{0,4},{1,5},{2,6},{3,7},{4,0},{5,1},{6,2},{7,3},{8,12},{9,13},{10,... | collective-permute-start | bytes 442376 | tf_op jit(solution)/shard_map/ppermute | solution.py:392
  24.4 25.7 %collective-permute-start.5 = (bf16[16,4608]{1,0:T(8,128)(2,1)S(1)}, bf16[16,4608]{1,0:T(8,128)(2,1)S(1)}, u32[]{:S(2)}, u32[]{:S(2)}) collective-permute-start(bf16[16,4608]{1,0:T(8,128)(2,1)S(1)} %get-tuple-element.27), channel_id=1, source_target_pairs={{0,3},{1,2},{2,1},{3,0},{4,7},{5,6},{6,5},{7,4},{8,11},{9,10},{10,... | collective-permute-start | bytes 442376 | tf_op jit(solution)/shard_map/ppermute | solution.py:392
  39.1 11.0 %collective-permute-start.6 = (bf16[16,4608]{1,0:T(8,128)(2,1)S(1)}, bf16[16,4608]{1,0:T(8,128)(2,1)S(1)}, u32[]{:S(2)}, u32[]{:S(2)}) collective-permute-start(bf16[16,4608]{1,0:T(8,128)(2,1)S(1)} %get-tuple-element.28), channel_id=1, source_target_pairs={{0,2},{1,3},{2,0},{3,1},{4,6},{5,7},{6,4},{7,5},{8,10},{9,11},{10,... | collective-permute-start | bytes 442376 | tf_op jit(solution)/shard_map/ppermute | solution.py:392
  44.9 5.2 %collective-permute-start.7 = (bf16[16,4608]{1,0:T(8,128)(2,1)S(1)}, bf16[16,4608]{1,0:T(8,128)(2,1)S(1)}, u32[]{:S(2)}, u32[]{:S(2)}) collective-permute-start(bf16[16,4608]{1,0:T(8,128)(2,1)S(1)} %get-tuple-element.29), channel_id=1, source_target_pairs={{0,1},{1,0},{2,3},{3,2},{4,5},{5,4},{6,7},{7,6},{8,9},{9,8},{10,11... | collective-permute-start | bytes 442376 | tf_op jit(solution)/shard_map/ppermute | solution.py:392
  53.2 3.9 %copy-start.15 = (bf16[128,4]{0,1:T(4,128)(2,1)S(1)}, bf16[128,4]{0,1:T(4,128)(2,1)}, u32[]{:S(2)}) copy-start(bf16[128,4]{0,1:T(4,128)(2,1)} %param.25) | copy-start | bytes 3076
  53.3 4.1 %copy-start.6 = (bf16[128,128]{1,0:T(8,128)(2,1)S(1)}, bf16[128,128]{1,0:T(8,128)(2,1)}, u32[]{:S(2)}) copy-start(bf16[128,128]{1,0:T(8,128)(2,1)} %refs_1_.5) | copy-start | bytes 98308
  53.3 13.2 %copy-start.4 = (bf16[128,128]{1,0:T(8,128)(2,1)S(1)}, bf16[128,128]{1,0:T(8,128)(2,1)}, u32[]{:S(2)}) copy-start(bf16[128,128]{1,0:T(8,128)(2,1)} %refs_3_.4) | copy-start | bytes 98308
  53.3 13.2 %copy-start.13 = (f32[128]{0:T(128)S(1)}, f32[128]{0:T(128)}, u32[]{:S(2)}) copy-start(f32[128]{0:T(128)} %param.19) | copy-start | bytes 1540
  53.3 13.2 %copy-start.14 = (f32[128]{0:T(128)S(1)}, f32[128]{0:T(128)}, u32[]{:S(2)}) copy-start(f32[128]{0:T(128)} %param.21) | copy-start | bytes 1540
  53.3 13.2 %all-to-all-start.1 = ((bf16[8,16,2304]{2,1,0:T(8,128)(2,1)}), bf16[8,16,2304]{2,1,0:T(8,128)(2,1)S(1)}, u32[]{:S(2)}, u32[]{:S(2)}) async-start(bf16[8,16,2304]{2,1,0:T(8,128)(2,1)} %outer.1), calls=%async_computation.1 | async-start | bytes 1179648 | tf_op jit(solution)/shard_map/all_to_all | solution.py:455
  66.5 16.5 %copy-start.7 = (bf16[128,128]{1,0:T(8,128)(2,1)S(1)}, bf16[128,128]{1,0:T(8,128)(2,1)}, u32[]{:S(2)}) copy-start(bf16[128,128]{1,0:T(8,128)(2,1)} %refs_1_.7) | copy-start | bytes 98308
  66.5 16.5 %copy-start.8 = (bf16[128,128]{1,0:T(8,128)(2,1)S(1)}, bf16[128,128]{1,0:T(8,128)(2,1)}, u32[]{:S(2)}) copy-start(bf16[128,128]{1,0:T(8,128)(2,1)} %refs_2_.1) | copy-start | bytes 98308
  66.5 16.5 %copy-start.9 = (bf16[128,128]{1,0:T(8,128)(2,1)S(1)}, bf16[128,128]{1,0:T(8,128)(2,1)}, u32[]{:S(2)}) copy-start(bf16[128,128]{1,0:T(8,128)(2,1)} %refs_3_.5) | copy-start | bytes 98308
  66.5 16.5 %copy-start.10 = (bf16[128,128]{1,0:T(8,128)(2,1)S(1)}, bf16[128,128]{1,0:T(8,128)(2,1)}, u32[]{:S(2)}) copy-start(bf16[128,128]{1,0:T(8,128)(2,1)} %refs_4_.3) | copy-start | bytes 98308
  66.5 17.8 %copy-start.5 = (bf16[128,128]{1,0:T(8,128)(2,1)S(1)}, bf16[128,128]{1,0:T(8,128)(2,1)}, u32[]{:S(2)}) copy-start(bf16[128,128]{1,0:T(8,128)(2,1)} %refs_6_.1) | copy-start | bytes 98308
  69.2 5.2 %collective-permute-start.8 = (bf16[1,24,384]{2,1,0:T(8,128)(2,1)S(1)}, bf16[1,24,384]{2,1,0:T(8,128)(2,1)S(1)}, u32[]{:S(2)}, u32[]{:S(2)}) collective-permute-start(bf16[1,24,384]{2,1,0:T(8,128)(2,1)S(1)} %bitcast.5), channel_id=1, source_target_pairs={{0,8},{1,9},{2,10},{3,11},{4,12},{5,13},{6,14},{7,15},{8,0},{9,1},... | collective-permute-start | bytes 55304 | tf_op jit(solution)/shard_map/ppermute | solution.py:363
  74.4 4.0 %collective-permute-start.9 = (bf16[2,24,384]{2,1,0:T(8,128)(2,1)S(1)}, bf16[2,24,384]{2,1,0:T(8,128)(2,1)S(1)}, u32[]{:S(2)}, u32[]{:S(2)}) collective-permute-start(bf16[2,24,384]{2,1,0:T(8,128)(2,1)S(1)} %pad_maximum_fusion.2), channel_id=1, source_target_pairs={{0,4},{1,5},{2,6},{3,7},{4,0},{5,1},{6,2},{7,3},{8,12},{9,13},{10,... | collective-permute-start | bytes 110600 | tf_op jit(solution)/shard_map/ppermute | solution.py:363
  78.4 4.4 %collective-permute-start.10 = (bf16[4,24,384]{2,1,0:T(8,128)(2,1)S(1)}, bf16[4,24,384]{2,1,0:T(8,128)(2,1)S(1)}, u32[]{:S(2)}, u32[]{:S(2)}) collective-permute-start(bf16[4,24,384]{2,1,0:T(8,128)(2,1)S(1)} %pad_maximum_fusion.1), channel_id=1, source_target_pairs={{0,2},{1,3},{2,0},{3,1},{4,6},{5,7},{6,4},{7,5},{8,10},{9,11},{10,... | collective-permute-start | bytes 221192 | tf_op jit(solution)/shard_map/ppermute | solution.py:363
  82.8 1.4 %collective-permute-start.11 = (bf16[8,24,384]{2,1,0:T(8,128)(2,1)S(1)}, bf16[8,24,384]{2,1,0:T(8,128)(2,1)S(1)}, u32[]{:S(2)}, u32[]{:S(2)}) collective-permute-start(bf16[8,24,384]{2,1,0:T(8,128)(2,1)S(1)} %pad_maximum_fusion), channel_id=1, source_target_pairs={{0,1},{1,0},{2,3},{3,2},{4,5},{5,4},{6,7},{7,6},{8,9},{9,8},{10,11... | collective-permute-start | bytes 442376 | tf_op jit(solution)/shard_map/ppermute | solution.py:363

commit v20 on v19

--- a/solution.py
+++ b/solution.py
@@ -121,16 +121,32 @@
     project_edges(sz, len_ref[0], first, w_ref[0], w_ref[1], pick, norm_ref, store)
 
 
-def right_kernel(sz, len_ref, x_ref, far_ref, ln_ref, w_ref, *refs):
-    near, (norm_ref, own_ref, far_rows_ref, pair_ref) = refs[: sz.group], refs[sz.group :]
+def right_kernel(sz, len_ref, x_ref, ln_ref, w_ref, *refs):
+    near, norm_ref = refs[: sz.group], refs[sz.group]
     cd, ch = sz.chans, sz.channels
     gain = ln_ref[...]
+    for row in range(sz.rows):
+        normalise(sz, row, x_ref[row].astype(F32), gain, norm_ref)
     me = position()
+    mine = me & (sz.group - 1)
+    r = lax.broadcasted_iota(jnp.int32, (ch, ch), 0)
+    e = lax.broadcasted_iota(jnp.int32, (ch, ch), 1)
+    partner = (sz.group - r // cd) & (sz.group - 1)
+    pick = ((partner ^ mine) * cd + r % cd == e).astype(BF16)
+
+    def store(g, lanes, edge):
+        near[g][:, lanes] = edge
+
+    project_edges(sz, len_ref[0], me * sz.rows, w_ref[2], w_ref[3], pick, norm_ref, store)
+
+
+def relay_kernel(sz, x_ref, far_ref, *refs):
+    near, (own_ref, far_rows_ref, pair_ref) = refs[: sz.group], refs[sz.group :]
+    cd, me = sz.chans, position()
     mine = me & (sz.group - 1)
     upper = me >= sz.group
     for row in range(sz.rows):
         x = x_ref[row].astype(F32)
-        normalise(sz, row, x, gain, norm_ref)
         rows = pl.ds(row * sz.columns, sz.columns)
         own_ref[rows, :] = jnp.where(upper, x[sz.columns :], x[: sz.columns])
         far_rows_ref[rows, :] = far_ref[row].astype(F32)
@@ -142,18 +158,9 @@
     for slot, partner in enumerate(sz.partners):
         for base in range(2):
             for t in range(sz.block_tiles):
-                at = (sz.tiles + base * sz.block_tiles + t) * LANES
+                at = (base * sz.block_tiles + t) * LANES
                 block = pair_ref[base, mine ^ partner, t * cd : (t + 1) * cd, :]
                 near[slot][:, at : at + LANES] = block.astype(BF16)
-    r = lax.broadcasted_iota(jnp.int32, (ch, ch), 0)
-    e = lax.broadcasted_iota(jnp.int32, (ch, ch), 1)
-    partner = (sz.group - r // cd) & (sz.group - 1)
-    pick = ((partner ^ mine) * cd + r % cd == e).astype(BF16)
-
-    def store(g, lanes, edge):
-        near[g][:, lanes] = edge
-
-    project_edges(sz, len_ref[0], me * sz.rows, w_ref[2], w_ref[3], pick, norm_ref, store)
 
 
 def unpack(sz, ref, owner, main_ref, rest_ref):
@@ -229,7 +236,7 @@
     for slot, partner in enumerate(sz.partners):
         for base, owner in ((0, me ^ partner), (1, me ^ (sz.group + partner))):
             for t in range(sz.block_tiles):
-                at = (sz.tiles + base * sz.block_tiles + t) * LANES
+                at = (base * sz.block_tiles + t) * LANES
                 rows = pl.ds(pl.multiple_of(owner * sz.block + t * cd, 8), cd)
                 cols_ref[rows, :] = near[slot][:, at : at + LANES].astype(F32)
 
@@ -409,23 +416,31 @@
         smem=(0,),
         name="left",
     )
-    others = call(
+    rights = call(
         bound(right_kernel),
-        [slab(t + 2 * bt)] * g,
-        (length, pair_rep, far, ln_pair[None], tri_in),
+        [slab(t)] * g,
+        (length, pair_rep, ln_pair[None], tri_in),
+        scratch=[pltpu.VMEM((rows * crop, ch), BF16)],
+        smem=(0,),
+        name="right",
+    )
+    pairs = call(
+        bound(relay_kernel),
+        [slab(2 * bt)] * g,
+        (pair_rep, far),
         scratch=[
-            pltpu.VMEM((rows * crop, ch), BF16),
             pltpu.VMEM((rows * sz.columns, ch), F32),
             pltpu.VMEM((rows * sz.columns, ch), F32),
             pltpu.VMEM((2, g, bt * cd, ch), F32),
         ],
-        smem=(0,),
-        name="right",
+        name="relay",
         cost=pl.CostEstimate(flops=10**11, bytes_accessed=10**6, transcendentals=0),
     )
     left = lax.all_to_all(left, AXES, split_axis=0, concat_axis=0, tiled=True)
-    near = send(others)
+    near = send(rights)
+    pairs = send(pairs)
     rest = sz.rest > 0
+    left, pairs = lax.optimization_barrier((left, pairs))
     column_rows = sz.columns * cd
     right = call(
         bound(arrange_kernel),
@@ -459,7 +474,7 @@
     columns, gating = call(
         bound(gating_kernel),
         [shape((rows, n, ch), BF16)] * 2,
-        (ln_pair[None], tri_gate, *near),
+        (ln_pair[None], tri_gate, *pairs),
         scratch=[pltpu.VMEM((devices * sz.block + cd, ch), F32)],
         name="gating",
     )

time: 89.7 us -> 92.6 us (1.032)
  starting transfers between devices: 24.7 us -> 32.9 us
  waiting for transfers between devices: 43.4 us -> 38 us
    ppermute x7 -> x14, starting transfers between devices: 5.91 us -> 13.8 us  [send(): lax.ppermute(block, AXES, [(d, d ^ partner) for d in range(devices)])]
    ppermute x1, waiting for transfers between devices: 3.78 us -> 0.01 us  [shards(): lax.ppermute(lax.dynamic_slice_in_dim(pair_rep, (1 - upper) * sz.columns,...]
    ppermute x7 -> x14, waiting for transfers between devices: 24.2 us -> 22.2 us  [send(): lax.ppermute(block, AXES, [(d, d ^ partner) for d in range(devices)])]
    pallas_call x8 -> x9, Pallas kernels: 16.3 us -> 16.3 us  [call(): pl.pallas_call(kernel, out_shape=out_shape, in_specs=specs, out_specs=ins...]
  transfers between devices with their start and end apart: 14 -> 21, of which waited for: 10 -> 12; matrix products, arithmetic and copies ran while one was open for 0% -> 0% of each run, Pallas kernels for 7% -> 7%
where the time goes in v20:
time: 92.6 us; the launch traced here: 92.2 us
  waiting for transfers between devices  38 us (41%)
  starting transfers between devices  32.9 us (36%)
  Pallas kernels  16.3 us (18%)
  local copies, waits for them, and re-layouts  3.8 us (4%)
  between operations  1.07 us (1%)
    ppermute x14, waiting for transfers between devices, send(): lax.ppermute(block, AXES, [(d, d ^ partner) for d in range(devices)])  22.2 us
    pallas_call x9, Pallas kernels, call(): pl.pallas_call(kernel, out_shape=out_shape, in_specs=specs, out_specs=ins...  16.3 us
    ppermute x14, starting transfers between devices, send(): lax.ppermute(block, AXES, [(d, d ^ partner) for d in range(devices)])  13.8 us
    all_to_all x1, waiting for transfers between devices, shards(): lax.all_to_all(outer, AXES, split_axis=0, concat_axis=0, tiled=True, axis...  7.95 us
    ppermute x4, waiting for transfers between devices, spread(): lax.ppermute(held, AXES, [(d, d ^ bit) for d in range(devices)])  7.88 us
    ppermute x4, starting transfers between devices, spread(): lax.ppermute(held, AXES, [(d, d ^ bit) for d in range(devices)])  7.08 us
    ppermute x1, starting transfers between devices, shards(): lax.ppermute(lax.dynamic_slice_in_dim(pair_rep, (1 - upper) * sz.columns,...  4.1 us
    all_to_all x1, starting transfers between devices, shards(): left = lax.all_to_all(left, AXES, split_axis=0, concat_axis=0, tiled=True)  4.04 us
  transfers between devices with their start and end apart: 21, of which 12 were waited for; matrix products, arithmetic and copies ran while one was open for 0% of the time, Pallas kernels for 7%

profile of v20, /device:TPU:0, one launch (start us, length us, event | category | flops | bytes accessed | tf_op | source)
XLA Modules:
  0.0 92.2 jit_solution(16458458805177771900)
XLA Ops:
  0.0 1.0 %constant_dynamic-slice_fusion = bf16[12,96,128]{2,1,0:T(8,128)(2,1)S(1)} fusion(bf16[12,192,128]{2,1,0:T(8,128)(2,1)} %refs_1_.6, s32[]{:T(128)S(6)} %select_n.3), kind=kLoop, calls=%fused_computation.3 | loop fusion | bytes 589828 | tf_op jit(solution)/shard_map/dynamic_slice | solution.py:407
  1.0 4.1 %collective-permute-start = (bf16[12,96,128]{2,1,0:T(8,128)(2,1)S(1)}, bf16[12,96,128]{2,1,0:T(8,128)(2,1)S(1)}, u32[]{:S(2)}, u32[]{:S(2)}) collective-permute-start(bf16[12,96,128]{2,1,0:T(8,128)(2,1)S(1)} %constant_dynamic-slice_fusion), channel_id=1, source_target_pairs={{0,8},{1,9},{2,10},{3,11},{4,12},{5,13},{6,14},{7,15},{8,0},{9,1},... | collective-permute-start | bytes 884744 | tf_op jit(solution)/shard_map/ppermute | solution.py:406
  5.8 1.1 %copy-done = bf16[12,192,128]{2,1,0:T(8,128)(2,1)S(1)} copy-done((bf16[12,192,128]{2,1,0:T(8,128)(2,1)S(1)}, bf16[12,192,128]{2,1,0:T(8,128)(2,1)}, u32[]{:S(2)}) %copy-start) | copy-done | bytes 589848
  6.8 0.9 copy-done.2
  8.4 2.3 %left.1 = bf16[16,16,2304]{2,1,0:T(8,128)(2,1)} custom-call(s32[1]{0:T(128)S(6)} %copy.16.refs_0_, bf16[12,192,128]{2,1,0:T(8,128)(2,1)S(1)} %copy-done, f32[1,128]{1,0:T(1,128)S(1)} %bitcast.10, bf16[4,128,128]{2,1,0:T(8,128)(2,1)S(1)} %copy-done.2), custom_call_target="tpu_custom_call" | custom-call | tf_op jit(solution)/shard_map/left/pallas_call | solution.py:42
  10.6 4.0 %all-to-all-start = ((bf16[16,16,2304]{2,1,0:T(8,128)(2,1)}), bf16[16,16,2304]{2,1,0:T(8,128)(2,1)S(1)}, u32[]{:S(2)}, u32[]{:S(2)}) async-start(bf16[16,16,2304]{2,1,0:T(8,128)(2,1)} %left.1), calls=%async_computation | async-start | bytes 2359296 | tf_op jit(solution)/shard_map/all_to_all | solution.py:439
  14.7 1.2 %right.1 = (bf16[16,2304]{1,0:T(8,128)(2,1)S(1)}, bf16[16,2304]{1,0:T(8,128)(2,1)S(1)}, bf16[16,2304]{1,0:T(8,128)(2,1)S(1)}, bf16[16,2304]{1,0:T(8,128)(2,1)S(1...) custom-call(s32[1]{0:T(128)S(6)} %copy.16.refs_0_, ...), custom_call_target="tpu_custom_call" | custom-call | tf_op jit(solution)/shard_map/right/pallas_call | solution.py:42
  16.0 2.6 %collective-permute-start.8 = (bf16[16,2304]{1,0:T(8,128)(2,1)S(1)}, bf16[16,2304]{1,0:T(8,128)(2,1)S(1)}, u32[]{:S(2)}, u32[]{:S(2)}) collective-permute-start(bf16[16,2304]{1,0:T(8,128)(2,1)S(1)} %get-tuple-element.59), channel_id=1, source_target_pairs={{0,7},{1,6},{2,5},{3,4},{4,3},{5,2},{6,1},{7,0},{8,15},{9,14},{10,... | collective-permute-start | bytes 221192 | tf_op jit(solution)/shard_map/ppermute | solution.py:399
  19.0 1.3 %collective-permute-start.10 = (bf16[16,2304]{1,0:T(8,128)(2,1)S(1)}, bf16[16,2304]{1,0:T(8,128)(2,1)S(1)}, u32[]{:S(2)}, u32[]{:S(2)}) collective-permute-start(bf16[16,2304]{1,0:T(8,128)(2,1)S(1)} %get-tuple-element.61), channel_id=1, source_target_pairs={{0,5},{1,4},{2,7},{3,6},{4,1},{5,0},{6,3},{7,2},{8,13},{9,12},{10,... | collective-permute-start | bytes 221192 | tf_op jit(solution)/shard_map/ppermute | solution.py:399
  20.7 1.4 %collective-permute-start.12 = (bf16[16,2304]{1,0:T(8,128)(2,1)S(1)}, bf16[16,2304]{1,0:T(8,128)(2,1)S(1)}, u32[]{:S(2)}, u32[]{:S(2)}) collective-permute-start(bf16[16,2304]{1,0:T(8,128)(2,1)S(1)} %get-tuple-element.63), channel_id=1, source_target_pairs={{0,3},{1,2},{2,1},{3,0},{4,7},{5,6},{6,5},{7,4},{8,11},{9,10},{10,... | collective-permute-start | bytes 221192 | tf_op jit(solution)/shard_map/ppermute | solution.py:399
  22.4 14.8 %collective-permute-done.8.refs_1_ = bf16[16,2304]{1,0:T(8,128)(2,1)S(1)} collective-permute-done((bf16[16,2304]{1,0:T(8,128)(2,1)S(1)}, bf16[16,2304]{1,0:T(8,128)(2,1)S(1)}, u32[]{:S(2)}, u32[]{:S(2)}) %collective-permute-start.8) | collective-permute-done | bytes 73760 | tf_op jit(solution)/shard_map/ppermute | solution.py:399
  37.2 1.3 %collective-permute-start.13 = (bf16[16,2304]{1,0:T(8,128)(2,1)S(1)}, bf16[16,2304]{1,0:T(8,128)(2,1)S(1)}, u32[]{:S(2)}, u32[]{:S(2)}) collective-permute-start(bf16[16,2304]{1,0:T(8,128)(2,1)S(1)} %get-tuple-element.64), channel_id=1, source_target_pairs={{0,2},{1,3},{2,0},{3,1},{4,6},{5,7},{6,4},{7,5},{8,10},{9,11},{10,... | collective-permute-start | bytes 221192 | tf_op jit(solution)/shard_map/ppermute | solution.py:399
  39.1 3.0 %collective-permute-done.10.refs_3_ = bf16[16,2304]{1,0:T(8,128)(2,1)S(1)} collective-permute-done((bf16[16,2304]{1,0:T(8,128)(2,1)S(1)}, bf16[16,2304]{1,0:T(8,128)(2,1)S(1)}, u32[]{:S(2)}, u32[]{:S(2)}) %collective-permute-start.10) | collective-permute-done | bytes 73760 | tf_op jit(solution)/shard_map/ppermute | solution.py:399
  42.1 1.2 %collective-permute-start.1 = (bf16[16,2304]{1,0:T(8,128)(2,1)S(1)}, bf16[16,2304]{1,0:T(8,128)(2,1)S(1)}, u32[]{:S(2)}, u32[]{:S(2)}) collective-permute-start(bf16[16,2304]{1,0:T(8,128)(2,1)S(1)} %get-tuple-element.40), channel_id=1, source_target_pairs={{0,7},{1,6},{2,5},{3,4},{4,3},{5,2},{6,1},{7,0},{8,15},{9,14},{10,... | collective-permute-start | bytes 221192 | tf_op jit(solution)/shard_map/ppermute | solution.py:399
  43.7 1.0 %collective-permute-start.2 = (bf16[16,2304]{1,0:T(8,128)(2,1)S(1)}, bf16[16,2304]{1,0:T(8,128)(2,1)S(1)}, u32[]{:S(2)}, u32[]{:S(2)}) collective-permute-start(bf16[16,2304]{1,0:T(8,128)(2,1)S(1)} %get-tuple-element.41), channel_id=1, source_target_pairs={{0,6},{1,7},{2,4},{3,5},{4,2},{5,3},{6,0},{7,1},{8,14},{9,15},{10,... | collective-permute-start | bytes 221192 | tf_op jit(solution)/shard_map/ppermute | solution.py:399
  44.8 1.4 %collective-permute-start.3 = (bf16[16,2304]{1,0:T(8,128)(2,1)S(1)}, bf16[16,2304]{1,0:T(8,128)(2,1)S(1)}, u32[]{:S(2)}, u32[]{:S(2)}) collective-permute-start(bf16[16,2304]{1,0:T(8,128)(2,1)S(1)} %get-tuple-element.42), channel_id=1, source_target_pairs={{0,5},{1,4},{2,7},{3,6},{4,1},{5,0},{6,3},{7,2},{8,13},{9,12},{10,... | collective-permute-start | bytes 221192 | tf_op jit(solution)/shard_map/ppermute | solution.py:399
  46.9 1.0 %collective-permute-start.5 = (bf16[16,2304]{1,0:T(8,128)(2,1)S(1)}, bf16[16,2304]{1,0:T(8,128)(2,1)S(1)}, u32[]{:S(2)}, u32[]{:S(2)}) collective-permute-start(bf16[16,2304]{1,0:T(8,128)(2,1)S(1)} %get-tuple-element.44), channel_id=1, source_target_pairs={{0,3},{1,2},{2,1},{3,0},{4,7},{5,6},{6,5},{7,4},{8,11},{9,10},{10,... | collective-permute-start | bytes 221192 | tf_op jit(solution)/shard_map/ppermute | solution.py:399
  47.8 1.0 %collective-permute-start.6 = (bf16[16,2304]{1,0:T(8,128)(2,1)S(1)}, bf16[16,2304]{1,0:T(8,128)(2,1)S(1)}, u32[]{:S(2)}, u32[]{:S(2)}) collective-permute-start(bf16[16,2304]{1,0:T(8,128)(2,1)S(1)} %get-tuple-element.45), channel_id=1, source_target_pairs={{0,2},{1,3},{2,0},{3,1},{4,6},{5,7},{6,4},{7,5},{8,10},{9,11},{10,... | collective-permute-start | bytes 221192 | tf_op jit(solution)/shard_map/ppermute | solution.py:399
  50.4 2.1 %collective-permute-done.4.refs_6_ = bf16[16,2304]{1,0:T(8,128)(2,1)S(1)} collective-permute-done((bf16[16,2304]{1,0:T(8,128)(2,1)S(1)}, bf16[16,2304]{1,0:T(8,128)(2,1)S(1)}, u32[]{:S(2)}, u32[]{:S(2)}) %collective-permute-start.4) | collective-permute-done | bytes 73760 | tf_op jit(solution)/shard_map/ppermute | solution.py:399
  53.0 2.4 %outer.1 = bf16[8,16,2304]{2,1,0:T(8,128)(2,1)} custom-call(bf16[16,16,2304]{2,1,0:T(8,128)(2,1)S(1)} %all-to-all-done.refs_0_, bf16[16,96,192]{2,1,0:T(8,128)(2,1)S(1)} %arrange.1.refs_1_), custom_call_target="tpu_custom_call" | custom-call | tf_op jit(solution)/shard_map/outer/pallas_call | solution.py:42
  55.5 3.9 %all-to-all-start.1 = ((bf16[8,16,2304]{2,1,0:T(8,128)(2,1)}), bf16[8,16,2304]{2,1,0:T(8,128)(2,1)S(1)}, u32[]{:S(2)}, u32[]{:S(2)}) async-start(bf16[8,16,2304]{2,1,0:T(8,128)(2,1)} %outer.1), calls=%async_computation.1 | async-start | bytes 1179648 | tf_op jit(solution)/shard_map/all_to_all | solution.py:470
  59.5 1.2 %gating.1 = (bf16[12,192,128]{2,1,0:T(8,128)(2,1)S(1)}, bf16[12,192,128]{2,1,0:T(8,128)(2,1)S(1)}) custom-call(f32[1,128]{1,0:T(1,128)S(1)} %bitcast.12, bf16[128,128]{1,0:T(8,128)(2,1)S(1)} %copy-done.6, bf16[16,2304]{1,0:T(8,128)(2,1)S(1)} %get-tuple-element.47.refs_2_, bf16[16,2304]{1,0:T(8,128)(2,1)S(1)} %collective-permute-done.1.refs_3_, ...), custom_call_target="tpu_custom_call" | custom-call | tf_op jit(solution)/shard_map/gating/pallas_call | solution.py:42
  60.7 8.0 %all-to-all-done.1.refs_6_ = bf16[8,16,2304]{2,1,0:T(8,128)(2,1)S(1)} async-done(((bf16[8,16,2304]{2,1,0:T(8,128)(2,1)}), bf16[8,16,2304]{2,1,0:T(8,128)(2,1)S(1)}, u32[]{:S(2)}, u32[]{:S(2)}) %all-to-all-start.1) | async-done | bytes 589856 | tf_op jit(solution)/shard_map/all_to_all | solution.py:470
  68.7 2.6 %update.1 = (bf16[12,192,128]{2,1,0:T(8,128)(2,1)S(1)}, bf16[12,192,128]{2,1,0:T(8,128)(2,1)S(1)}, bf16[24,384]{1,0:T(8,128)(2,1)S(1)}) custom-call(bf16[12,192,128]{2,1,0:T(8,128)(2,1)S(1)} %get-tuple-element.55.refs_0_, bf16[12,192,128]{2,1,0:T(8,128)(2,1)S(1)} %get-tuple-element.56.refs_1_, f32[1,128]{1,0:T(1,128)S(1)} %bitcast.13, ...), custom_call_target="tpu_custom_call" | custom-call | tf_op jit(solution)/shard_map/update/pallas_call | solution.py:42
  71.4 4.2 %collective-permute-start.15 = (bf16[1,24,384]{2,1,0:T(8,128)(2,1)S(1)}, bf16[1,24,384]{2,1,0:T(8,128)(2,1)S(1)}, u32[]{:S(2)}, u32[]{:S(2)}) collective-permute-start(bf16[1,24,384]{2,1,0:T(8,128)(2,1)S(1)} %bitcast.5), channel_id=1, source_target_pairs={{0,8},{1,9},{2,10},{3,11},{4,12},{5,13},{6,14},{7,15},{8,0},{9,1},... | collective-permute-start | bytes 55304 | tf_op jit(solution)/shard_map/ppermute | solution.py:370
  75.5 1.7 %collective-permute-done.15.refs_8_ = bf16[1,24,384]{2,1,0:T(8,128)(2,1)S(1)} collective-permute-done((bf16[1,24,384]{2,1,0:T(8,128)(2,1)S(1)}, bf16[1,24,384]{2,1,0:T(8,128)(2,1)S(1)}, u32[]{:S(2)}, u32[]{:S(2)}) %collective-permute-start.15) | collective-permute-done | bytes 18464 | tf_op jit(solution)/shard_map/ppermute | solution.py:370
  77.3 1.4 %collective-permute-start.16 = (bf16[2,24,384]{2,1,0:T(8,128)(2,1)S(1)}, bf16[2,24,384]{2,1,0:T(8,128)(2,1)S(1)}, u32[]{:S(2)}, u32[]{:S(2)}) collective-permute-start(bf16[2,24,384]{2,1,0:T(8,128)(2,1)S(1)} %pad_maximum_fusion.2), channel_id=1, source_target_pairs={{0,4},{1,5},{2,6},{3,7},{4,0},{5,1},{6,2},{7,3},{8,12},{9,13},{10,... | collective-permute-start | bytes 110600 | tf_op jit(solution)/shard_map/ppermute | solution.py:370
  78.7 2.6 %collective-permute-done.16.refs_9_ = bf16[2,24,384]{2,1,0:T(8,128)(2,1)S(1)} collective-permute-done((bf16[2,24,384]{2,1,0:T(8,128)(2,1)S(1)}, bf16[2,24,384]{2,1,0:T(8,128)(2,1)S(1)}, u32[]{:S(2)}, u32[]{:S(2)}) %collective-permute-start.16) | collective-permute-done | bytes 36896 | tf_op jit(solution)/shard_map/ppermute | solution.py:370
  81.3 1.4 %collective-permute-start.17 = (bf16[4,24,384]{2,1,0:T(8,128)(2,1)S(1)}, bf16[4,24,384]{2,1,0:T(8,128)(2,1)S(1)}, u32[]{:S(2)}, u32[]{:S(2)}) collective-permute-start(bf16[4,24,384]{2,1,0:T(8,128)(2,1)S(1)} %pad_maximum_fusion.1), channel_id=1, source_target_pairs={{0,2},{1,3},{2,0},{3,1},{4,6},{5,7},{6,4},{7,5},{8,10},{9,11},{10,... | collective-permute-start | bytes 221192 | tf_op jit(solution)/shard_map/ppermute | solution.py:370
  82.7 3.0 %collective-permute-done.17.refs_10_ = bf16[4,24,384]{2,1,0:T(8,128)(2,1)S(1)} collective-permute-done((bf16[4,24,384]{2,1,0:T(8,128)(2,1)S(1)}, bf16[4,24,384]{2,1,0:T(8,128)(2,1)S(1)}, u32[]{:S(2)}, u32[]{:S(2)}) %collective-permute-start.17) | collective-permute-done | bytes 73760 | tf_op jit(solution)/shard_map/ppermute | solution.py:370
  85.9 0.8 project.1
  87.2 4.8 %attend.1 = bf16[12,192,128]{2,1,0:T(8,128)(2,1)} custom-call(s32[1]{0:T(128)S(6)} %copy.16.refs_0_, bf16[12,192,128]{2,1,0:T(8,128)(2,1)S(1)} %get-tuple-element.67.refs_1_, bf16[12,192,128]{2,1,0:T(8,128)(2,1)S(1)} %get-tuple-element.68.refs_2_, bf16[12,192,128]{2,1,0:T(8,128)(2,1)S(1)} %get-tuple-element.69.refs_3_, ...), custom_call_target="tpu_custom_call" | custom-call | tf_op jit(solution)/shard_map/attend/pallas_call | solution.py:42
  (56 shorter events, 6.2 us)
Async XLA Ops:
  1.0 19.7 %collective-permute-start = (bf16[12,96,128]{2,1,0:T(8,128)(2,1)S(1)}, bf16[12,96,128]{2,1,0:T(8,128)(2,1)S(1)}, u32[]{:S(2)}, u32[]{:S(2)}) collective-permute-start(bf16[12,96,128]{2,1,0:T(8,128)(2,1)S(1)} %constant_dynamic-slice_fusion), channel_id=1, source_target_pairs={{0,8},{1,9},{2,10},{3,11},{4,12},{5,13},{6,14},{7,15},{8,0},{9,1},... | collective-permute-start | bytes 884744 | tf_op jit(solution)/shard_map/ppermute | solution.py:406
  10.6 4.1 %copy-start.3 = (bf16[4,128,128]{2,1,0:T(8,128)(2,1)S(1)}, bf16[4,128,128]{2,1,0:T(8,128)(2,1)}, u32[]{:S(2)}) copy-start(bf16[4,128,128]{2,1,0:T(8,128)(2,1)} %refs_3_.5) | copy-start | bytes 393220
  10.6 4.1 %copy-start.12 = (f32[128]{0:T(128)S(1)}, f32[128]{0:T(128)}, u32[]{:S(2)}) copy-start(f32[128]{0:T(128)} %param.16) | copy-start | bytes 1540
  10.6 42.4 %all-to-all-start = ((bf16[16,16,2304]{2,1,0:T(8,128)(2,1)}), bf16[16,16,2304]{2,1,0:T(8,128)(2,1)S(1)}, u32[]{:S(2)}, u32[]{:S(2)}) async-start(bf16[16,16,2304]{2,1,0:T(8,128)(2,1)} %left.1), calls=%async_computation | async-start | bytes 2359296 | tf_op jit(solution)/shard_map/all_to_all | solution.py:439
  16.0 21.3 %collective-permute-start.8 = (bf16[16,2304]{1,0:T(8,128)(2,1)S(1)}, bf16[16,2304]{1,0:T(8,128)(2,1)S(1)}, u32[]{:S(2)}, u32[]{:S(2)}) collective-permute-start(bf16[16,2304]{1,0:T(8,128)(2,1)S(1)} %get-tuple-element.59), channel_id=1, source_target_pairs={{0,7},{1,6},{2,5},{3,4},{4,3},{5,2},{6,1},{7,0},{8,15},{9,14},{10,... | collective-permute-start | bytes 221192 | tf_op jit(solution)/shard_map/ppermute | solution.py:399
  18.6 20.5 %collective-permute-start.9 = (bf16[16,2304]{1,0:T(8,128)(2,1)S(1)}, bf16[16,2304]{1,0:T(8,128)(2,1)S(1)}, u32[]{:S(2)}, u32[]{:S(2)}) collective-permute-start(bf16[16,2304]{1,0:T(8,128)(2,1)S(1)} %get-tuple-element.60), channel_id=1, source_target_pairs={{0,6},{1,7},{2,4},{3,5},{4,2},{5,3},{6,0},{7,1},{8,14},{9,15},{10,... | collective-permute-start | bytes 221192 | tf_op jit(solution)/shard_map/ppermute | solution.py:399
  19.0 23.1 %collective-permute-start.10 = (bf16[16,2304]{1,0:T(8,128)(2,1)S(1)}, bf16[16,2304]{1,0:T(8,128)(2,1)S(1)}, u32[]{:S(2)}, u32[]{:S(2)}) collective-permute-start(bf16[16,2304]{1,0:T(8,128)(2,1)S(1)} %get-tuple-element.61), channel_id=1, source_target_pairs={{0,5},{1,4},{2,7},{3,6},{4,1},{5,0},{6,3},{7,2},{8,13},{9,12},{10,... | collective-permute-start | bytes 221192 | tf_op jit(solution)/shard_map/ppermute | solution.py:399
  20.3 23.4 %collective-permute-start.11 = (bf16[16,2304]{1,0:T(8,128)(2,1)S(1)}, bf16[16,2304]{1,0:T(8,128)(2,1)S(1)}, u32[]{:S(2)}, u32[]{:S(2)}) collective-permute-start(bf16[16,2304]{1,0:T(8,128)(2,1)S(1)} %get-tuple-element.62), channel_id=1, source_target_pairs={{0,4},{1,5},{2,6},{3,7},{4,0},{5,1},{6,2},{7,3},{8,12},{9,13},{10,... | collective-permute-start | bytes 221192 | tf_op jit(solution)/shard_map/ppermute | solution.py:399
  20.7 24.1 %collective-permute-start.12 = (bf16[16,2304]{1,0:T(8,128)(2,1)S(1)}, bf16[16,2304]{1,0:T(8,128)(2,1)S(1)}, u32[]{:S(2)}, u32[]{:S(2)}) collective-permute-start(bf16[16,2304]{1,0:T(8,128)(2,1)S(1)} %get-tuple-element.63), channel_id=1, source_target_pairs={{0,3},{1,2},{2,1},{3,0},{4,7},{5,6},{6,5},{7,4},{8,11},{9,10},{10,... | collective-permute-start | bytes 221192 | tf_op jit(solution)/shard_map/ppermute | solution.py:399
  37.2 8.9 %collective-permute-start.13 = (bf16[16,2304]{1,0:T(8,128)(2,1)S(1)}, bf16[16,2304]{1,0:T(8,128)(2,1)S(1)}, u32[]{:S(2)}, u32[]{:S(2)}) collective-permute-start(bf16[16,2304]{1,0:T(8,128)(2,1)S(1)} %get-tuple-element.64), channel_id=1, source_target_pairs={{0,2},{1,3},{2,0},{3,1},{4,6},{5,7},{6,4},{7,5},{8,10},{9,11},{10,... | collective-permute-start | bytes 221192 | tf_op jit(solution)/shard_map/ppermute | solution.py:399
  39.1 7.8 %collective-permute-start.14 = (bf16[16,2304]{1,0:T(8,128)(2,1)S(1)}, bf16[16,2304]{1,0:T(8,128)(2,1)S(1)}, u32[]{:S(2)}, u32[]{:S(2)}) collective-permute-start(bf16[16,2304]{1,0:T(8,128)(2,1)S(1)} %get-tuple-element.65), channel_id=1, source_target_pairs={{0,1},{1,0},{2,3},{3,2},{4,5},{5,4},{6,7},{7,6},{8,9},{9,8},{10,11... | collective-permute-start | bytes 221192 | tf_op jit(solution)/shard_map/ppermute | solution.py:399
  42.1 5.7 %collective-permute-start.1 = (bf16[16,2304]{1,0:T(8,128)(2,1)S(1)}, bf16[16,2304]{1,0:T(8,128)(2,1)S(1)}, u32[]{:S(2)}, u32[]{:S(2)}) collective-permute-start(bf16[16,2304]{1,0:T(8,128)(2,1)S(1)} %get-tuple-element.40), channel_id=1, source_target_pairs={{0,7},{1,6},{2,5},{3,4},{4,3},{5,2},{6,1},{7,0},{8,15},{9,14},{10,... | collective-permute-start | bytes 221192 | tf_op jit(solution)/shard_map/ppermute | solution.py:399
  43.7 5.9 %collective-permute-start.2 = (bf16[16,2304]{1,0:T(8,128)(2,1)S(1)}, bf16[16,2304]{1,0:T(8,128)(2,1)S(1)}, u32[]{:S(2)}, u32[]{:S(2)}) collective-permute-start(bf16[16,2304]{1,0:T(8,128)(2,1)S(1)} %get-tuple-element.41), channel_id=1, source_target_pairs={{0,6},{1,7},{2,4},{3,5},{4,2},{5,3},{6,0},{7,1},{8,14},{9,15},{10,... | collective-permute-start | bytes 221192 | tf_op jit(solution)/shard_map/ppermute | solution.py:399
  44.8 5.6 %collective-permute-start.3 = (bf16[16,2304]{1,0:T(8,128)(2,1)S(1)}, bf16[16,2304]{1,0:T(8,128)(2,1)S(1)}, u32[]{:S(2)}, u32[]{:S(2)}) collective-permute-start(bf16[16,2304]{1,0:T(8,128)(2,1)S(1)} %get-tuple-element.42), channel_id=1, source_target_pairs={{0,5},{1,4},{2,7},{3,6},{4,1},{5,0},{6,3},{7,2},{8,13},{9,12},{10,... | collective-permute-start | bytes 221192 | tf_op jit(solution)/shard_map/ppermute | solution.py:399
  46.2 6.3 %collective-permute-start.4 = (bf16[16,2304]{1,0:T(8,128)(2,1)S(1)}, bf16[16,2304]{1,0:T(8,128)(2,1)S(1)}, u32[]{:S(2)}, u32[]{:S(2)}) collective-permute-start(bf16[16,2304]{1,0:T(8,128)(2,1)S(1)} %get-tuple-element.43), channel_id=1, source_target_pairs={{0,4},{1,5},{2,6},{3,7},{4,0},{5,1},{6,2},{7,3},{8,12},{9,13},{10,... | collective-permute-start | bytes 221192 | tf_op jit(solution)/shard_map/ppermute | solution.py:399
  46.9 5.6 %collective-permute-start.5 = (bf16[16,2304]{1,0:T(8,128)(2,1)S(1)}, bf16[16,2304]{1,0:T(8,128)(2,1)S(1)}, u32[]{:S(2)}, u32[]{:S(2)}) collective-permute-start(bf16[16,2304]{1,0:T(8,128)(2,1)S(1)} %get-tuple-element.44), channel_id=1, source_target_pairs={{0,3},{1,2},{2,1},{3,0},{4,7},{5,6},{6,5},{7,4},{8,11},{9,10},{10,... | collective-permute-start | bytes 221192 | tf_op jit(solution)/shard_map/ppermute | solution.py:399
  47.8 5.2 %collective-permute-start.6 = (bf16[16,2304]{1,0:T(8,128)(2,1)S(1)}, bf16[16,2304]{1,0:T(8,128)(2,1)S(1)}, u32[]{:S(2)}, u32[]{:S(2)}) collective-permute-start(bf16[16,2304]{1,0:T(8,128)(2,1)S(1)} %get-tuple-element.45), channel_id=1, source_target_pairs={{0,2},{1,3},{2,0},{3,1},{4,6},{5,7},{6,4},{7,5},{8,10},{9,11},{10,... | collective-permute-start | bytes 221192 | tf_op jit(solution)/shard_map/ppermute | solution.py:399
  49.6 3.4 %collective-permute-start.7 = (bf16[16,2304]{1,0:T(8,128)(2,1)S(1)}, bf16[16,2304]{1,0:T(8,128)(2,1)S(1)}, u32[]{:S(2)}, u32[]{:S(2)}) collective-permute-start(bf16[16,2304]{1,0:T(8,128)(2,1)S(1)} %get-tuple-element.46), channel_id=1, source_target_pairs={{0,1},{1,0},{2,3},{3,2},{4,5},{5,4},{6,7},{7,6},{8,9},{9,8},{10,11... | collective-permute-start | bytes 221192 | tf_op jit(solution)/shard_map/ppermute | solution.py:399
  55.5 4.1 %copy-start.6 = (bf16[128,128]{1,0:T(8,128)(2,1)S(1)}, bf16[128,128]{1,0:T(8,128)(2,1)}, u32[]{:S(2)}) copy-start(bf16[128,128]{1,0:T(8,128)(2,1)} %refs_1_.5) | copy-start | bytes 98308
  55.5 13.2 %copy-start.4 = (bf16[128,128]{1,0:T(8,128)(2,1)S(1)}, bf16[128,128]{1,0:T(8,128)(2,1)}, u32[]{:S(2)}) copy-start(bf16[128,128]{1,0:T(8,128)(2,1)} %refs_3_.6) | copy-start | bytes 98308
  55.5 13.2 %copy-start.13 = (f32[128]{0:T(128)S(1)}, f32[128]{0:T(128)}, u32[]{:S(2)}) copy-start(f32[128]{0:T(128)} %param.19) | copy-start | bytes 1540
  55.5 13.2 %copy-start.14 = (f32[128]{0:T(128)S(1)}, f32[128]{0:T(128)}, u32[]{:S(2)}) copy-start(f32[128]{0:T(128)} %param.21) | copy-start | bytes 1540
  55.5 13.2 %all-to-all-start.1 = ((bf16[8,16,2304]{2,1,0:T(8,128)(2,1)}), bf16[8,16,2304]{2,1,0:T(8,128)(2,1)S(1)}, u32[]{:S(2)}, u32[]{:S(2)}) async-start(bf16[8,16,2304]{2,1,0:T(8,128)(2,1)} %outer.1), calls=%async_computation.1 | async-start | bytes 1179648 | tf_op jit(solution)/shard_map/all_to_all | solution.py:470
  68.7 17.2 %copy-start.7 = (bf16[128,128]{1,0:T(8,128)(2,1)S(1)}, bf16[128,128]{1,0:T(8,128)(2,1)}, u32[]{:S(2)}) copy-start(bf16[128,128]{1,0:T(8,128)(2,1)} %refs_1_.7) | copy-start | bytes 98308
  68.7 17.2 %copy-start.8 = (bf16[128,128]{1,0:T(8,128)(2,1)S(1)}, bf16[128,128]{1,0:T(8,128)(2,1)}, u32[]{:S(2)}) copy-start(bf16[128,128]{1,0:T(8,128)(2,1)} %refs_2_.1) | copy-start | bytes 98308
  68.7 17.2 %copy-start.9 = (bf16[128,128]{1,0:T(8,128)(2,1)S(1)}, bf16[128,128]{1,0:T(8,128)(2,1)}, u32[]{:S(2)}) copy-start(bf16[128,128]{1,0:T(8,128)(2,1)} %refs_3_.7) | copy-start | bytes 98308
  68.7 17.2 %copy-start.10 = (bf16[128,128]{1,0:T(8,128)(2,1)S(1)}, bf16[128,128]{1,0:T(8,128)(2,1)}, u32[]{:S(2)}) copy-start(bf16[128,128]{1,0:T(8,128)(2,1)} %refs_4_.1) | copy-start | bytes 98308
  68.7 18.5 %copy-start.5 = (bf16[128,128]{1,0:T(8,128)(2,1)S(1)}, bf16[128,128]{1,0:T(8,128)(2,1)}, u32[]{:S(2)}) copy-start(bf16[128,128]{1,0:T(8,128)(2,1)} %refs_6_.1) | copy-start | bytes 98308
  71.4 5.9 %collective-permute-start.15 = (bf16[1,24,384]{2,1,0:T(8,128)(2,1)S(1)}, bf16[1,24,384]{2,1,0:T(8,128)(2,1)S(1)}, u32[]{:S(2)}, u32[]{:S(2)}) collective-permute-start(bf16[1,24,384]{2,1,0:T(8,128)(2,1)S(1)} %bitcast.5), channel_id=1, source_target_pairs={{0,8},{1,9},{2,10},{3,11},{4,12},{5,13},{6,14},{7,15},{8,0},{9,1},... | collective-permute-start | bytes 55304 | tf_op jit(solution)/shard_map/ppermute | solution.py:370
  77.3 4.0 %collective-permute-start.16 = (bf16[2,24,384]{2,1,0:T(8,128)(2,1)S(1)}, bf16[2,24,384]{2,1,0:T(8,128)(2,1)S(1)}, u32[]{:S(2)}, u32[]{:S(2)}) collective-permute-start(bf16[2,24,384]{2,1,0:T(8,128)(2,1)S(1)} %pad_maximum_fusion.2), channel_id=1, source_target_pairs={{0,4},{1,5},{2,6},{3,7},{4,0},{5,1},{6,2},{7,3},{8,12},{9,13},{10,... | collective-permute-start | bytes 110600 | tf_op jit(solution)/shard_map/ppermute | solution.py:370
  81.3 4.4 %collective-permute-start.17 = (bf16[4,24,384]{2,1,0:T(8,128)(2,1)S(1)}, bf16[4,24,384]{2,1,0:T(8,128)(2,1)S(1)}, u32[]{:S(2)}, u32[]{:S(2)}) collective-permute-start(bf16[4,24,384]{2,1,0:T(8,128)(2,1)S(1)} %pad_maximum_fusion.1), channel_id=1, source_target_pairs={{0,2},{1,3},{2,0},{3,1},{4,6},{5,7},{6,4},{7,5},{8,10},{9,11},{10,... | collective-permute-start | bytes 221192 | tf_op jit(solution)/shard_map/ppermute | solution.py:370
  85.8 1.4 %collective-permute-start.18 = (bf16[8,24,384]{2,1,0:T(8,128)(2,1)S(1)}, bf16[8,24,384]{2,1,0:T(8,128)(2,1)S(1)}, u32[]{:S(2)}, u32[]{:S(2)}) collective-permute-start(bf16[8,24,384]{2,1,0:T(8,128)(2,1)S(1)} %pad_maximum_fusion), channel_id=1, source_target_pairs={{0,1},{1,0},{2,3},{3,2},{4,5},{5,4},{6,7},{7,6},{8,9},{9,8},{10,11... | collective-permute-start | bytes 442376 | tf_op jit(solution)/shard_map/ppermute | solution.py:370
  (5 other events, 10.6 us)

commit v21 on v20

--- a/solution.py
+++ b/solution.py
@@ -438,7 +438,6 @@
     )
     left = lax.all_to_all(left, AXES, split_axis=0, concat_axis=0, tiled=True)
     near = send(rights)
-    pairs = send(pairs)
     rest = sz.rest > 0
     left, pairs = lax.optimization_barrier((left, pairs))
     column_rows = sz.columns * cd
@@ -471,6 +470,7 @@
         outer, AXES, split_axis=0, concat_axis=0, tiled=True,
         axis_index_groups=[list(range(g)), list(range(g, devices))],
     )
+    pairs = send(pairs)
     columns, gating = call(
         bound(gating_kernel),
         [shape((rows, n, ch), BF16)] * 2,

time: 92.6 us -> 105 us (1.13)
  waiting for transfers between devices: 38 us -> 49.5 us
    all_to_all x1, waiting for transfers between devices: 0.01 us -> 23.8 us  [shards(): left = lax.all_to_all(left, AXES, split_axis=0, concat_axis=0, tiled=True)]
    all_to_all x1, waiting for transfers between devices: 7.95 us -> 0.01 us  [shards(): lax.all_to_all(outer, AXES, split_axis=0, concat_axis=0, tiled=True, axis...]
    ppermute x14, waiting for transfers between devices: 22.2 us -> 16.5 us  [send(): lax.ppermute(block, AXES, [(d, d ^ partner) for d in range(devices)])]
    all_to_all x1, starting transfers between devices: 3.86 us -> 6.72 us  [shards(): lax.all_to_all(outer, AXES, split_axis=0, concat_axis=0, tiled=True, axis...]
    ppermute x4, starting transfers between devices: 7.08 us -> 4.53 us  [spread(): lax.ppermute(held, AXES, [(d, d ^ bit) for d in range(devices)])]
    ppermute x4, waiting for transfers between devices: 7.88 us -> 9.21 us  [spread(): lax.ppermute(held, AXES, [(d, d ^ bit) for d in range(devices)])]
    unnamed x33 -> x31, local copies, waits for them, and re-layouts: 2.82 us -> 3.1 us
  transfers between devices with their start and end apart: 21 -> 21, of which waited for: 12 -> 12; matrix products, arithmetic and copies ran while one was open for 0% -> 0% of each run, Pallas kernels for 7% -> 6%
where the time goes in v21:
time: 105 us; the launch traced here: 104 us
  waiting for transfers between devices  49.5 us (47%)
  starting transfers between devices  33.1 us (32%)
  Pallas kernels  16.4 us (16%)
  local copies, waits for them, and re-layouts  4.08 us (4%)
  between operations  1.11 us (1%)
    all_to_all x1, waiting for transfers between devices, shards(): left = lax.all_to_all(left, AXES, split_axis=0, concat_axis=0, tiled=True)  23.8 us
    ppermute x14, waiting for transfers between devices, send(): lax.ppermute(block, AXES, [(d, d ^ partner) for d in range(devices)])  16.5 us
    pallas_call x9, Pallas kernels, call(): pl.pallas_call(kernel, out_shape=out_shape, in_specs=specs, out_specs=ins...  16.4 us
    ppermute x14, starting transfers between devices, send(): lax.ppermute(block, AXES, [(d, d ^ partner) for d in range(devices)])  13.6 us
    ppermute x4, waiting for transfers between devices, spread(): lax.ppermute(held, AXES, [(d, d ^ bit) for d in range(devices)])  9.21 us
    all_to_all x1, starting transfers between devices, shards(): lax.all_to_all(outer, AXES, split_axis=0, concat_axis=0, tiled=True, axis...  6.72 us
    ppermute x4, starting transfers between devices, spread(): lax.ppermute(held, AXES, [(d, d ^ bit) for d in range(devices)])  4.53 us
    all_to_all x1, starting transfers between devices, shards(): left = lax.all_to_all(left, AXES, split_axis=0, concat_axis=0, tiled=True)  4.17 us
  transfers between devices with their start and end apart: 21, of which 12 were waited for; matrix products, arithmetic and copies ran while one was open for 0% of the time, Pallas kernels for 6%

profile of v21, /device:TPU:0, one launch (start us, length us, event | category | flops | bytes accessed | tf_op | source)
XLA Modules:
  0.0 104.2 jit_solution(11353672932749857191)
XLA Ops:
  0.0 1.0 constant_dynamic-slice_fusion
  1.0 4.1 %collective-permute-start = (bf16[12,96,128]{2,1,0:T(8,128)(2,1)S(1)}, bf16[12,96,128]{2,1,0:T(8,128)(2,1)S(1)}, u32[]{:S(2)}, u32[]{:S(2)}) collective-permute-start(bf16[12,96,128]{2,1,0:T(8,128)(2,1)S(1)} %constant_dynamic-slice_fusion), channel_id=1, source_target_pairs={{0,8},{1,9},{2,10},{3,11},{4,12},{5,13},{6,14},{7,15},{8,0},{9,1},... | collective-permute-start | bytes 884744 | tf_op jit(solution)/shard_map/ppermute | solution.py:406
  5.8 1.1 %copy-done = bf16[12,192,128]{2,1,0:T(8,128)(2,1)S(1)} copy-done((bf16[12,192,128]{2,1,0:T(8,128)(2,1)S(1)}, bf16[12,192,128]{2,1,0:T(8,128)(2,1)}, u32[]{:S(2)}) %copy-start) | copy-done | bytes 589848
  6.8 0.9 copy-done.2
  8.4 1.2 %right.1 = (bf16[16,2304]{1,0:T(8,128)(2,1)S(1)}, bf16[16,2304]{1,0:T(8,128)(2,1)S(1)}, bf16[16,2304]{1,0:T(8,128)(2,1)S(1)}, bf16[16,2304]{1,0:T(8,128)(2,1)S(1...) custom-call(s32[1]{0:T(128)S(6)} %copy.16.refs_0_, ...), custom_call_target="tpu_custom_call" | custom-call | tf_op jit(solution)/shard_map/right/pallas_call | solution.py:42
  9.6 1.7 %collective-permute-start.8 = (bf16[16,2304]{1,0:T(8,128)(2,1)S(1)}, bf16[16,2304]{1,0:T(8,128)(2,1)S(1)}, u32[]{:S(2)}, u32[]{:S(2)}) collective-permute-start(bf16[16,2304]{1,0:T(8,128)(2,1)S(1)} %get-tuple-element.59), channel_id=1, source_target_pairs={{0,7},{1,6},{2,5},{3,4},{4,3},{5,2},{6,1},{7,0},{8,15},{9,14},{10,... | collective-permute-start | bytes 221192 | tf_op jit(solution)/shard_map/ppermute | solution.py:399
  11.4 0.9 collective-permute-start.9
  12.3 1.3 %collective-permute-start.10 = (bf16[16,2304]{1,0:T(8,128)(2,1)S(1)}, bf16[16,2304]{1,0:T(8,128)(2,1)S(1)}, u32[]{:S(2)}, u32[]{:S(2)}) collective-permute-start(bf16[16,2304]{1,0:T(8,128)(2,1)S(1)} %get-tuple-element.61), channel_id=1, source_target_pairs={{0,5},{1,4},{2,7},{3,6},{4,1},{5,0},{6,3},{7,2},{8,13},{9,12},{10,... | collective-permute-start | bytes 221192 | tf_op jit(solution)/shard_map/ppermute | solution.py:399
  14.1 6.0 %collective-permute-done.8.refs_1_ = bf16[16,2304]{1,0:T(8,128)(2,1)S(1)} collective-permute-done((bf16[16,2304]{1,0:T(8,128)(2,1)S(1)}, bf16[16,2304]{1,0:T(8,128)(2,1)S(1)}, u32[]{:S(2)}, u32[]{:S(2)}) %collective-permute-start.8) | collective-permute-done | bytes 73760 | tf_op jit(solution)/shard_map/ppermute | solution.py:399
  20.1 1.1 %collective-permute-start.12 = (bf16[16,2304]{1,0:T(8,128)(2,1)S(1)}, bf16[16,2304]{1,0:T(8,128)(2,1)S(1)}, u32[]{:S(2)}, u32[]{:S(2)}) collective-permute-start(bf16[16,2304]{1,0:T(8,128)(2,1)S(1)} %get-tuple-element.63), channel_id=1, source_target_pairs={{0,3},{1,2},{2,1},{3,0},{4,7},{5,6},{6,5},{7,4},{8,11},{9,10},{10,... | collective-permute-start | bytes 221192 | tf_op jit(solution)/shard_map/ppermute | solution.py:399
  21.8 1.2 %collective-permute-start.13 = (bf16[16,2304]{1,0:T(8,128)(2,1)S(1)}, bf16[16,2304]{1,0:T(8,128)(2,1)S(1)}, u32[]{:S(2)}, u32[]{:S(2)}) collective-permute-start(bf16[16,2304]{1,0:T(8,128)(2,1)S(1)} %get-tuple-element.64), channel_id=1, source_target_pairs={{0,2},{1,3},{2,0},{3,1},{4,6},{5,7},{6,4},{7,5},{8,10},{9,11},{10,... | collective-permute-start | bytes 221192 | tf_op jit(solution)/shard_map/ppermute | solution.py:399
  23.2 2.3 %left.1 = bf16[16,16,2304]{2,1,0:T(8,128)(2,1)} custom-call(s32[1]{0:T(128)S(6)} %copy.16.refs_0_, bf16[12,192,128]{2,1,0:T(8,128)(2,1)S(1)} %copy-done, f32[1,128]{1,0:T(1,128)S(1)} %bitcast.11, bf16[4,128,128]{2,1,0:T(8,128)(2,1)S(1)} %copy-done.2), custom_call_target="tpu_custom_call" | custom-call | tf_op jit(solution)/shard_map/left/pallas_call | solution.py:42
  25.5 4.2 %all-to-all-start = ((bf16[16,16,2304]{2,1,0:T(8,128)(2,1)}), bf16[16,16,2304]{2,1,0:T(8,128)(2,1)S(1)}, u32[]{:S(2)}, u32[]{:S(2)}) async-start(bf16[16,16,2304]{2,1,0:T(8,128)(2,1)} %left.1), calls=%async_computation | async-start | bytes 2359296 | tf_op jit(solution)/shard_map/all_to_all | solution.py:439
  31.1 23.8 %all-to-all-done.refs_0_ = bf16[16,16,2304]{2,1,0:T(8,128)(2,1)S(1)} async-done(((bf16[16,16,2304]{2,1,0:T(8,128)(2,1)}), bf16[16,16,2304]{2,1,0:T(8,128)(2,1)S(1)}, u32[]{:S(2)}, u32[]{:S(2)}) %all-to-all-start) | async-done | bytes 1179680 | tf_op jit(solution)/shard_map/all_to_all | solution.py:439
  54.8 2.4 %outer.1 = bf16[8,16,2304]{2,1,0:T(8,128)(2,1)} custom-call(bf16[16,16,2304]{2,1,0:T(8,128)(2,1)S(1)} %all-to-all-done.refs_0_, bf16[16,96,192]{2,1,0:T(8,128)(2,1)S(1)} %arrange.1.refs_1_), custom_call_target="tpu_custom_call" | custom-call | tf_op jit(solution)/shard_map/outer/pallas_call | solution.py:42
  57.3 6.7 %all-to-all-start.1 = ((bf16[8,16,2304]{2,1,0:T(8,128)(2,1)}), bf16[8,16,2304]{2,1,0:T(8,128)(2,1)S(1)}, u32[]{:S(2)}, u32[]{:S(2)}) async-start(bf16[8,16,2304]{2,1,0:T(8,128)(2,1)} %outer.1), calls=%async_computation.1 | async-start | bytes 1179648 | tf_op jit(solution)/shard_map/all_to_all | solution.py:469
  64.1 2.7 %collective-permute-start.1 = (bf16[16,2304]{1,0:T(8,128)(2,1)S(1)}, bf16[16,2304]{1,0:T(8,128)(2,1)S(1)}, u32[]{:S(2)}, u32[]{:S(2)}) collective-permute-start(bf16[16,2304]{1,0:T(8,128)(2,1)S(1)} %get-tuple-element.48), channel_id=1, source_target_pairs={{0,7},{1,6},{2,5},{3,4},{4,3},{5,2},{6,1},{7,0},{8,15},{9,14},{10,... | collective-permute-start | bytes 221192 | tf_op jit(solution)/shard_map/ppermute | solution.py:399
  67.1 1.4 %collective-permute-start.3 = (bf16[16,2304]{1,0:T(8,128)(2,1)S(1)}, bf16[16,2304]{1,0:T(8,128)(2,1)S(1)}, u32[]{:S(2)}, u32[]{:S(2)}) collective-permute-start(bf16[16,2304]{1,0:T(8,128)(2,1)S(1)} %get-tuple-element.50), channel_id=1, source_target_pairs={{0,5},{1,4},{2,7},{3,6},{4,1},{5,0},{6,3},{7,2},{8,13},{9,12},{10,... | collective-permute-start | bytes 221192 | tf_op jit(solution)/shard_map/ppermute | solution.py:399
  68.8 1.4 %collective-permute-start.5 = (bf16[16,2304]{1,0:T(8,128)(2,1)S(1)}, bf16[16,2304]{1,0:T(8,128)(2,1)S(1)}, u32[]{:S(2)}, u32[]{:S(2)}) collective-permute-start(bf16[16,2304]{1,0:T(8,128)(2,1)S(1)} %get-tuple-element.52), channel_id=1, source_target_pairs={{0,3},{1,2},{2,1},{3,0},{4,7},{5,6},{6,5},{7,4},{8,11},{9,10},{10,... | collective-permute-start | bytes 221192 | tf_op jit(solution)/shard_map/ppermute | solution.py:399
  70.2 5.5 %collective-permute-done.1.refs_3_ = bf16[16,2304]{1,0:T(8,128)(2,1)S(1)} collective-permute-done((bf16[16,2304]{1,0:T(8,128)(2,1)S(1)}, bf16[16,2304]{1,0:T(8,128)(2,1)S(1)}, u32[]{:S(2)}, u32[]{:S(2)}) %collective-permute-start.1) | collective-permute-done | bytes 73760 | tf_op jit(solution)/shard_map/ppermute | solution.py:399
  76.3 1.9 %collective-permute-done.2.refs_4_ = bf16[16,2304]{1,0:T(8,128)(2,1)S(1)} collective-permute-done((bf16[16,2304]{1,0:T(8,128)(2,1)S(1)}, bf16[16,2304]{1,0:T(8,128)(2,1)S(1)}, u32[]{:S(2)}, u32[]{:S(2)}) %collective-permute-start.2) | collective-permute-done | bytes 73760 | tf_op jit(solution)/shard_map/ppermute | solution.py:399
  78.3 1.6 %collective-permute-done.4.refs_6_ = bf16[16,2304]{1,0:T(8,128)(2,1)S(1)} collective-permute-done((bf16[16,2304]{1,0:T(8,128)(2,1)S(1)}, bf16[16,2304]{1,0:T(8,128)(2,1)S(1)}, u32[]{:S(2)}, u32[]{:S(2)}) %collective-permute-start.4) | collective-permute-done | bytes 73760 | tf_op jit(solution)/shard_map/ppermute | solution.py:399
  80.7 1.2 %gating.1 = (bf16[12,192,128]{2,1,0:T(8,128)(2,1)S(1)}, bf16[12,192,128]{2,1,0:T(8,128)(2,1)S(1)}) custom-call(f32[1,128]{1,0:T(1,128)S(1)} %bitcast.12, bf16[128,128]{1,0:T(8,128)(2,1)S(1)} %copy-done.5, bf16[16,2304]{1,0:T(8,128)(2,1)S(1)} %get-tuple-element.47.refs_2_, bf16[16,2304]{1,0:T(8,128)(2,1)S(1)} %collective-permute-done.1.refs_3_, ...), custom_call_target="tpu_custom_call" | custom-call | tf_op jit(solution)/shard_map/gating/pallas_call | solution.py:42
  82.0 2.6 %update.1 = (bf16[12,192,128]{2,1,0:T(8,128)(2,1)S(1)}, bf16[12,192,128]{2,1,0:T(8,128)(2,1)S(1)}, bf16[24,384]{1,0:T(8,128)(2,1)S(1)}) custom-call(bf16[12,192,128]{2,1,0:T(8,128)(2,1)S(1)} %get-tuple-element.55.refs_0_, bf16[12,192,128]{2,1,0:T(8,128)(2,1)S(1)} %get-tuple-element.56.refs_1_, f32[1,128]{1,0:T(1,128)S(1)} %bitcast.13, ...), custom_call_target="tpu_custom_call" | custom-call | tf_op jit(solution)/shard_map/update/pallas_call | solution.py:42
  84.6 2.6 %collective-permute-start.15 = (bf16[1,24,384]{2,1,0:T(8,128)(2,1)S(1)}, bf16[1,24,384]{2,1,0:T(8,128)(2,1)S(1)}, u32[]{:S(2)}, u32[]{:S(2)}) collective-permute-start(bf16[1,24,384]{2,1,0:T(8,128)(2,1)S(1)} %bitcast.5), channel_id=1, source_target_pairs={{0,8},{1,9},{2,10},{3,11},{4,12},{5,13},{6,14},{7,15},{8,0},{9,1},... | collective-permute-start | bytes 55304 | tf_op jit(solution)/shard_map/ppermute | solution.py:370
  87.2 2.1 %collective-permute-done.15.refs_8_ = bf16[1,24,384]{2,1,0:T(8,128)(2,1)S(1)} collective-permute-done((bf16[1,24,384]{2,1,0:T(8,128)(2,1)S(1)}, bf16[1,24,384]{2,1,0:T(8,128)(2,1)S(1)}, u32[]{:S(2)}, u32[]{:S(2)}) %collective-permute-start.15) | collective-permute-done | bytes 18464 | tf_op jit(solution)/shard_map/ppermute | solution.py:370
  89.3 0.8 collective-permute-start.16
  90.1 3.2 %collective-permute-done.16.refs_9_ = bf16[2,24,384]{2,1,0:T(8,128)(2,1)S(1)} collective-permute-done((bf16[2,24,384]{2,1,0:T(8,128)(2,1)S(1)}, bf16[2,24,384]{2,1,0:T(8,128)(2,1)S(1)}, u32[]{:S(2)}, u32[]{:S(2)}) %collective-permute-start.16) | collective-permute-done | bytes 36896 | tf_op jit(solution)/shard_map/ppermute | solution.py:370
  93.3 1.1 %collective-permute-start.17 = (bf16[4,24,384]{2,1,0:T(8,128)(2,1)S(1)}, bf16[4,24,384]{2,1,0:T(8,128)(2,1)S(1)}, u32[]{:S(2)}, u32[]{:S(2)}) collective-permute-start(bf16[4,24,384]{2,1,0:T(8,128)(2,1)S(1)} %pad_maximum_fusion.1), channel_id=1, source_target_pairs={{0,2},{1,3},{2,0},{3,1},{4,6},{5,7},{6,4},{7,5},{8,10},{9,11},{10,... | collective-permute-start | bytes 221192 | tf_op jit(solution)/shard_map/ppermute | solution.py:370
  94.4 3.4 %collective-permute-done.17.refs_10_ = bf16[4,24,384]{2,1,0:T(8,128)(2,1)S(1)} collective-permute-done((bf16[4,24,384]{2,1,0:T(8,128)(2,1)S(1)}, bf16[4,24,384]{2,1,0:T(8,128)(2,1)S(1)}, u32[]{:S(2)}, u32[]{:S(2)}) %collective-permute-start.17) | collective-permute-done | bytes 73760 | tf_op jit(solution)/shard_map/ppermute | solution.py:370
  97.9 0.8 project.1
  99.2 4.8 %attend.1 = bf16[12,192,128]{2,1,0:T(8,128)(2,1)} custom-call(s32[1]{0:T(128)S(6)} %copy.16.refs_0_, bf16[12,192,128]{2,1,0:T(8,128)(2,1)S(1)} %get-tuple-element.67.refs_1_, bf16[12,192,128]{2,1,0:T(8,128)(2,1)S(1)} %get-tuple-element.68.refs_2_, bf16[12,192,128]{2,1,0:T(8,128)(2,1)S(1)} %get-tuple-element.69.refs_3_, ...), custom_call_target="tpu_custom_call" | custom-call | tf_op jit(solution)/shard_map/attend/pallas_call | solution.py:42
  (54 shorter events, 6.2 us)
Async XLA Ops:
  1.0 29.5 %collective-permute-start = (bf16[12,96,128]{2,1,0:T(8,128)(2,1)S(1)}, bf16[12,96,128]{2,1,0:T(8,128)(2,1)S(1)}, u32[]{:S(2)}, u32[]{:S(2)}) collective-permute-start(bf16[12,96,128]{2,1,0:T(8,128)(2,1)S(1)} %constant_dynamic-slice_fusion), channel_id=1, source_target_pairs={{0,8},{1,9},{2,10},{3,11},{4,12},{5,13},{6,14},{7,15},{8,0},{9,1},... | collective-permute-start | bytes 884744 | tf_op jit(solution)/shard_map/ppermute | solution.py:406
  9.6 10.4 %collective-permute-start.8 = (bf16[16,2304]{1,0:T(8,128)(2,1)S(1)}, bf16[16,2304]{1,0:T(8,128)(2,1)S(1)}, u32[]{:S(2)}, u32[]{:S(2)}) collective-permute-start(bf16[16,2304]{1,0:T(8,128)(2,1)S(1)} %get-tuple-element.59), channel_id=1, source_target_pairs={{0,7},{1,6},{2,5},{3,4},{4,3},{5,2},{6,1},{7,0},{8,15},{9,14},{10,... | collective-permute-start | bytes 221192 | tf_op jit(solution)/shard_map/ppermute | solution.py:399
  11.4 10.5 %collective-permute-start.9 = (bf16[16,2304]{1,0:T(8,128)(2,1)S(1)}, bf16[16,2304]{1,0:T(8,128)(2,1)S(1)}, u32[]{:S(2)}, u32[]{:S(2)}) collective-permute-start(bf16[16,2304]{1,0:T(8,128)(2,1)S(1)} %get-tuple-element.60), channel_id=1, source_target_pairs={{0,6},{1,7},{2,4},{3,5},{4,2},{5,3},{6,0},{7,1},{8,14},{9,15},{10,... | collective-permute-start | bytes 221192 | tf_op jit(solution)/shard_map/ppermute | solution.py:399
  12.3 10.9 %collective-permute-start.10 = (bf16[16,2304]{1,0:T(8,128)(2,1)S(1)}, bf16[16,2304]{1,0:T(8,128)(2,1)S(1)}, u32[]{:S(2)}, u32[]{:S(2)}) collective-permute-start(bf16[16,2304]{1,0:T(8,128)(2,1)S(1)} %get-tuple-element.61), channel_id=1, source_target_pairs={{0,5},{1,4},{2,7},{3,6},{4,1},{5,0},{6,3},{7,2},{8,13},{9,12},{10,... | collective-permute-start | bytes 221192 | tf_op jit(solution)/shard_map/ppermute | solution.py:399
  13.6 16.1 %collective-permute-start.11 = (bf16[16,2304]{1,0:T(8,128)(2,1)S(1)}, bf16[16,2304]{1,0:T(8,128)(2,1)S(1)}, u32[]{:S(2)}, u32[]{:S(2)}) collective-permute-start(bf16[16,2304]{1,0:T(8,128)(2,1)S(1)} %get-tuple-element.62), channel_id=1, source_target_pairs={{0,4},{1,5},{2,6},{3,7},{4,0},{5,1},{6,2},{7,3},{8,12},{9,13},{10,... | collective-permute-start | bytes 221192 | tf_op jit(solution)/shard_map/ppermute | solution.py:399
  20.1 9.7 %collective-permute-start.12 = (bf16[16,2304]{1,0:T(8,128)(2,1)S(1)}, bf16[16,2304]{1,0:T(8,128)(2,1)S(1)}, u32[]{:S(2)}, u32[]{:S(2)}) collective-permute-start(bf16[16,2304]{1,0:T(8,128)(2,1)S(1)} %get-tuple-element.63), channel_id=1, source_target_pairs={{0,3},{1,2},{2,1},{3,0},{4,7},{5,6},{6,5},{7,4},{8,11},{9,10},{10,... | collective-permute-start | bytes 221192 | tf_op jit(solution)/shard_map/ppermute | solution.py:399
  21.8 7.9 %collective-permute-start.13 = (bf16[16,2304]{1,0:T(8,128)(2,1)S(1)}, bf16[16,2304]{1,0:T(8,128)(2,1)S(1)}, u32[]{:S(2)}, u32[]{:S(2)}) collective-permute-start(bf16[16,2304]{1,0:T(8,128)(2,1)S(1)} %get-tuple-element.64), channel_id=1, source_target_pairs={{0,2},{1,3},{2,0},{3,1},{4,6},{5,7},{6,4},{7,5},{8,10},{9,11},{10,... | collective-permute-start | bytes 221192 | tf_op jit(solution)/shard_map/ppermute | solution.py:399
  23.2 6.6 %collective-permute-start.14 = (bf16[16,2304]{1,0:T(8,128)(2,1)S(1)}, bf16[16,2304]{1,0:T(8,128)(2,1)S(1)}, u32[]{:S(2)}, u32[]{:S(2)}) collective-permute-start(bf16[16,2304]{1,0:T(8,128)(2,1)S(1)} %get-tuple-element.65), channel_id=1, source_target_pairs={{0,1},{1,0},{2,3},{3,2},{4,5},{5,4},{6,7},{7,6},{8,9},{9,8},{10,11... | collective-permute-start | bytes 221192 | tf_op jit(solution)/shard_map/ppermute | solution.py:399
  25.5 29.3 %all-to-all-start = ((bf16[16,16,2304]{2,1,0:T(8,128)(2,1)}), bf16[16,16,2304]{2,1,0:T(8,128)(2,1)S(1)}, u32[]{:S(2)}, u32[]{:S(2)}) async-start(bf16[16,16,2304]{2,1,0:T(8,128)(2,1)} %left.1), calls=%async_computation | async-start | bytes 2359296 | tf_op jit(solution)/shard_map/all_to_all | solution.py:439
  57.3 20.9 %copy-start.14 = (bf16[128,4]{0,1:T(4,128)(2,1)S(1)}, bf16[128,4]{0,1:T(4,128)(2,1)}, u32[]{:S(2)}) copy-start(bf16[128,4]{0,1:T(4,128)(2,1)} %param.25) | copy-start | bytes 3076
  57.3 23.4 %copy-start.5 = (bf16[128,128]{1,0:T(8,128)(2,1)S(1)}, bf16[128,128]{1,0:T(8,128)(2,1)}, u32[]{:S(2)}) copy-start(bf16[128,128]{1,0:T(8,128)(2,1)} %refs_1_.5) | copy-start | bytes 98308
  57.3 23.4 %copy-start.11 = (f32[128]{0:T(128)S(1)}, f32[128]{0:T(128)}, u32[]{:S(2)}) copy-start(f32[128]{0:T(128)} %param.16) | copy-start | bytes 1540
  57.3 24.6 %copy-start.3 = (bf16[128,128]{1,0:T(8,128)(2,1)S(1)}, bf16[128,128]{1,0:T(8,128)(2,1)}, u32[]{:S(2)}) copy-start(bf16[128,128]{1,0:T(8,128)(2,1)} %refs_3_.6) | copy-start | bytes 98308
  57.3 24.6 %copy-start.12 = (f32[128]{0:T(128)S(1)}, f32[128]{0:T(128)}, u32[]{:S(2)}) copy-start(f32[128]{0:T(128)} %param.19) | copy-start | bytes 1540
  57.3 24.6 %copy-start.13 = (f32[128]{0:T(128)S(1)}, f32[128]{0:T(128)}, u32[]{:S(2)}) copy-start(f32[128]{0:T(128)} %param.21) | copy-start | bytes 1540
  57.3 24.5 %all-to-all-start.1 = ((bf16[8,16,2304]{2,1,0:T(8,128)(2,1)}), bf16[8,16,2304]{2,1,0:T(8,128)(2,1)S(1)}, u32[]{:S(2)}, u32[]{:S(2)}) async-start(bf16[8,16,2304]{2,1,0:T(8,128)(2,1)} %outer.1), calls=%async_computation.1 | async-start | bytes 1179648 | tf_op jit(solution)/shard_map/all_to_all | solution.py:469
  64.1 11.7 %collective-permute-start.1 = (bf16[16,2304]{1,0:T(8,128)(2,1)S(1)}, bf16[16,2304]{1,0:T(8,128)(2,1)S(1)}, u32[]{:S(2)}, u32[]{:S(2)}) collective-permute-start(bf16[16,2304]{1,0:T(8,128)(2,1)S(1)} %get-tuple-element.48), channel_id=1, source_target_pairs={{0,7},{1,6},{2,5},{3,4},{4,3},{5,2},{6,1},{7,0},{8,15},{9,14},{10,... | collective-permute-start | bytes 221192 | tf_op jit(solution)/shard_map/ppermute | solution.py:399
  66.7 11.4 %collective-permute-start.2 = (bf16[16,2304]{1,0:T(8,128)(2,1)S(1)}, bf16[16,2304]{1,0:T(8,128)(2,1)S(1)}, u32[]{:S(2)}, u32[]{:S(2)}) collective-permute-start(bf16[16,2304]{1,0:T(8,128)(2,1)S(1)} %get-tuple-element.49), channel_id=1, source_target_pairs={{0,6},{1,7},{2,4},{3,5},{4,2},{5,3},{6,0},{7,1},{8,14},{9,15},{10,... | collective-permute-start | bytes 221192 | tf_op jit(solution)/shard_map/ppermute | solution.py:399
  67.1 11.2 %collective-permute-start.3 = (bf16[16,2304]{1,0:T(8,128)(2,1)S(1)}, bf16[16,2304]{1,0:T(8,128)(2,1)S(1)}, u32[]{:S(2)}, u32[]{:S(2)}) collective-permute-start(bf16[16,2304]{1,0:T(8,128)(2,1)S(1)} %get-tuple-element.50), channel_id=1, source_target_pairs={{0,5},{1,4},{2,7},{3,6},{4,1},{5,0},{6,3},{7,2},{8,13},{9,12},{10,... | collective-permute-start | bytes 221192 | tf_op jit(solution)/shard_map/ppermute | solution.py:399
  68.5 11.5 %collective-permute-start.4 = (bf16[16,2304]{1,0:T(8,128)(2,1)S(1)}, bf16[16,2304]{1,0:T(8,128)(2,1)S(1)}, u32[]{:S(2)}, u32[]{:S(2)}) collective-permute-start(bf16[16,2304]{1,0:T(8,128)(2,1)S(1)} %get-tuple-element.51), channel_id=1, source_target_pairs={{0,4},{1,5},{2,6},{3,7},{4,0},{5,1},{6,2},{7,3},{8,12},{9,13},{10,... | collective-permute-start | bytes 221192 | tf_op jit(solution)/shard_map/ppermute | solution.py:399
  68.8 11.2 %collective-permute-start.5 = (bf16[16,2304]{1,0:T(8,128)(2,1)S(1)}, bf16[16,2304]{1,0:T(8,128)(2,1)S(1)}, u32[]{:S(2)}, u32[]{:S(2)}) collective-permute-start(bf16[16,2304]{1,0:T(8,128)(2,1)S(1)} %get-tuple-element.52), channel_id=1, source_target_pairs={{0,3},{1,2},{2,1},{3,0},{4,7},{5,6},{6,5},{7,4},{8,11},{9,10},{10,... | collective-permute-start | bytes 221192 | tf_op jit(solution)/shard_map/ppermute | solution.py:399
  75.7 4.9 %collective-permute-start.6 = (bf16[16,2304]{1,0:T(8,128)(2,1)S(1)}, bf16[16,2304]{1,0:T(8,128)(2,1)S(1)}, u32[]{:S(2)}, u32[]{:S(2)}) collective-permute-start(bf16[16,2304]{1,0:T(8,128)(2,1)S(1)} %get-tuple-element.53), channel_id=1, source_target_pairs={{0,2},{1,3},{2,0},{3,1},{4,6},{5,7},{6,4},{7,5},{8,10},{9,11},{10,... | collective-permute-start | bytes 221192 | tf_op jit(solution)/shard_map/ppermute | solution.py:399
  78.2 2.5 %collective-permute-start.7 = (bf16[16,2304]{1,0:T(8,128)(2,1)S(1)}, bf16[16,2304]{1,0:T(8,128)(2,1)S(1)}, u32[]{:S(2)}, u32[]{:S(2)}) collective-permute-start(bf16[16,2304]{1,0:T(8,128)(2,1)S(1)} %get-tuple-element.54), channel_id=1, source_target_pairs={{0,1},{1,0},{2,3},{3,2},{4,5},{5,4},{6,7},{7,6},{8,9},{9,8},{10,11... | collective-permute-start | bytes 221192 | tf_op jit(solution)/shard_map/ppermute | solution.py:399
  81.9 16.0 %copy-start.6 = (bf16[128,128]{1,0:T(8,128)(2,1)S(1)}, bf16[128,128]{1,0:T(8,128)(2,1)}, u32[]{:S(2)}) copy-start(bf16[128,128]{1,0:T(8,128)(2,1)} %refs_1_.7) | copy-start | bytes 98308
  81.9 16.0 %copy-start.7 = (bf16[128,128]{1,0:T(8,128)(2,1)S(1)}, bf16[128,128]{1,0:T(8,128)(2,1)}, u32[]{:S(2)}) copy-start(bf16[128,128]{1,0:T(8,128)(2,1)} %refs_2_.1) | copy-start | bytes 98308
  81.9 16.0 %copy-start.8 = (bf16[128,128]{1,0:T(8,128)(2,1)S(1)}, bf16[128,128]{1,0:T(8,128)(2,1)}, u32[]{:S(2)}) copy-start(bf16[128,128]{1,0:T(8,128)(2,1)} %refs_3_.7) | copy-start | bytes 98308
  81.9 16.0 %copy-start.9 = (bf16[128,128]{1,0:T(8,128)(2,1)S(1)}, bf16[128,128]{1,0:T(8,128)(2,1)}, u32[]{:S(2)}) copy-start(bf16[128,128]{1,0:T(8,128)(2,1)} %refs_4_.1) | copy-start | bytes 98308
  81.9 17.3 %copy-start.4 = (bf16[128,128]{1,0:T(8,128)(2,1)S(1)}, bf16[128,128]{1,0:T(8,128)(2,1)}, u32[]{:S(2)}) copy-start(bf16[128,128]{1,0:T(8,128)(2,1)} %refs_6_.1) | copy-start | bytes 98308
  84.6 4.7 %collective-permute-start.15 = (bf16[1,24,384]{2,1,0:T(8,128)(2,1)S(1)}, bf16[1,24,384]{2,1,0:T(8,128)(2,1)S(1)}, u32[]{:S(2)}, u32[]{:S(2)}) collective-permute-start(bf16[1,24,384]{2,1,0:T(8,128)(2,1)S(1)} %bitcast.5), channel_id=1, source_target_pairs={{0,8},{1,9},{2,10},{3,11},{4,12},{5,13},{6,14},{7,15},{8,0},{9,1},... | collective-permute-start | bytes 55304 | tf_op jit(solution)/shard_map/ppermute | solution.py:370
  89.3 4.0 %collective-permute-start.16 = (bf16[2,24,384]{2,1,0:T(8,128)(2,1)S(1)}, bf16[2,24,384]{2,1,0:T(8,128)(2,1)S(1)}, u32[]{:S(2)}, u32[]{:S(2)}) collective-permute-start(bf16[2,24,384]{2,1,0:T(8,128)(2,1)S(1)} %pad_maximum_fusion.2), channel_id=1, source_target_pairs={{0,4},{1,5},{2,6},{3,7},{4,0},{5,1},{6,2},{7,3},{8,12},{9,13},{10,... | collective-permute-start | bytes 110600 | tf_op jit(solution)/shard_map/ppermute | solution.py:370
  93.3 4.4 %collective-permute-start.17 = (bf16[4,24,384]{2,1,0:T(8,128)(2,1)S(1)}, bf16[4,24,384]{2,1,0:T(8,128)(2,1)S(1)}, u32[]{:S(2)}, u32[]{:S(2)}) collective-permute-start(bf16[4,24,384]{2,1,0:T(8,128)(2,1)S(1)} %pad_maximum_fusion.1), channel_id=1, source_target_pairs={{0,2},{1,3},{2,0},{3,1},{4,6},{5,7},{6,4},{7,5},{8,10},{9,11},{10,... | collective-permute-start | bytes 221192 | tf_op jit(solution)/shard_map/ppermute | solution.py:370
  97.8 1.4 %collective-permute-start.18 = (bf16[8,24,384]{2,1,0:T(8,128)(2,1)S(1)}, bf16[8,24,384]{2,1,0:T(8,128)(2,1)S(1)}, u32[]{:S(2)}, u32[]{:S(2)}) collective-permute-start(bf16[8,24,384]{2,1,0:T(8,128)(2,1)S(1)} %pad_maximum_fusion), channel_id=1, source_target_pairs={{0,1},{1,0},{2,3},{3,2},{4,5},{5,4},{6,7},{7,6},{8,9},{9,8},{10,11... | collective-permute-start | bytes 442376 | tf_op jit(solution)/shard_map/ppermute | solution.py:370
  (4 other events, 3.7 us)
